TPU v7x, 32 devices: a whole 2x2x4 slice. The times are simulated.
32 devices in a mesh: parts: 2 (over y), expert: 16 (over z, x, core), dp: 1.
Axes of the slice: x: 2, y: 2, z: 4, core: 2. Of those that a mesh axis runs over, the one named last changes fastest.
Arguments:
- tokens: bfloat16 [2048, 2048], P(('parts', 'expert', 'dp')), parts along dimension 0, may hold values from -6 to 6
- expert_ids: int32 [2048, 8], P(('parts', 'expert', 'dp')), parts along dimension 0, may hold values from 0 to 15, all different within a row; in each aligned block of 64 rows (0 to 63, 64 to 127, ...) at most 64 rows name the same one
- router_weights: float32 [2048, 8], P(('parts', 'expert', 'dp')), parts along dimension 0, may hold values from 0.1 to 1
- w_gate: bfloat16 [16, 2048, 768], P('expert', None, 'dp'), may hold values from -0.125 to 0.125
- w_up: bfloat16 [16, 2048, 768], P('expert', None, 'dp'), may hold values from -0.125 to 0.125
- w_down: bfloat16 [16, 2048, 768], P('expert', None, 'dp'), may hold values from -0.21875 to 0.21875
Outputs:
- mixed: bfloat16 [2048, 2048], P(('parts', 'expert', 'dp')), parts along dimension 0
There are 2 independent parts, one for each index of `parts`. A program takes and returns all parts, laid end to end along the dimension named above; an argument that names none is the same for every part. Nothing has to cross between parts.
Inputs may be any that keep to these rules, and one draw needn't show every extreme that they name: `expert_ids`: each token names 8 different experts. Among the 64 tokens of one device no expert is named more than 64 times, and in every draw some expert is named exactly 64 times by the tokens of some device.
All inputs are finite; a program needn't handle non-finite values.
Results may differ from a plain program's by a relative error of at most 0.008.
Values may be sent and summed in bfloat16 or wider, within the bound.
No kernel may reach another device: no remote copies, remote signals or barrier semaphores. Data moves between devices by JAX's collectives and lax.ppermute only.
A program may use at most 128 MiB of HBM per device.

v0:
```python
import math

import jax
import jax.numpy as jnp
from jax import lax
from jax.sharding import PartitionSpec as P


def expert_rows(rows, gate_w, up_w, down_w):
    total = rows.shape[0]
    block = math.gcd(total, 128)
    pieces = []
    for index in range(total // block):
        block_rows = rows[index * block : (index + 1) * block]
        gate_val = jnp.dot(block_rows, gate_w, preferred_element_type=jnp.float32)
        up_val = jnp.dot(block_rows, up_w, preferred_element_type=jnp.float32)
        hidden = (jax.nn.silu(gate_val) * up_val).astype(jnp.bfloat16)
        pieces.append(
            lax.dot_general(
                hidden, down_w, (((1,), (1,)), ((), ())), preferred_element_type=jnp.float32
            )
        )
    return jnp.concatenate(pieces, 0)


def body(tokens, expert_ids, router_weights, w_gate, w_up, w_down):
    tok_count, top = expert_ids.shape
    width = tokens.shape[1]
    experts = lax.axis_size("expert")
    cap = max(2, min(tok_count, 2 * tok_count * top // experts))
    slots_all = experts * cap
    flat_ids = expert_ids.reshape(-1)
    onehot = (flat_ids[:, None] == jnp.arange(experts, dtype=jnp.int32)[None, :]).astype(jnp.int32)
    before = jnp.cumsum(onehot, 0) - onehot
    position = jnp.sum(before * onehot, 1)
    slot = flat_ids * cap + position
    send = jnp.zeros((slots_all, width), jnp.bfloat16).at[slot].set(jnp.repeat(tokens, top, 0))
    send = send.reshape(experts, cap, width)
    arrived = lax.all_to_all(send, "expert", split_axis=0, concat_axis=0, tiled=True)
    packed = arrived.reshape(slots_all, width)
    result = expert_rows(
        packed,
        lax.all_gather(w_gate, "dp", axis=2, tiled=True)[0],
        lax.all_gather(w_up, "dp", axis=2, tiled=True)[0],
        lax.all_gather(w_down, "dp", axis=2, tiled=True)[0],
    )
    expert_out = result.astype(jnp.bfloat16)
    back = lax.all_to_all(
        expert_out.reshape(experts, cap, width), "expert", split_axis=0, concat_axis=0, tiled=True
    )
    picked = back.reshape(slots_all, width)[slot].reshape(tok_count, top, width)
    mixed = jnp.einsum("tk,tkd->td", router_weights, picked.astype(jnp.float32))
    return mixed.astype(jnp.bfloat16)


def solution(mesh):
    in_specs = (
        P(("parts", "expert", "dp"), None),
        P(("parts", "expert", "dp"), None),
        P(("parts", "expert", "dp"), None),
        P("expert", None, "dp"),
        P("expert", None, "dp"),
        P("expert", None, "dp"),
    )
    out_specs = P(("parts", "expert", "dp"), None)
    return jax.shard_map(body, mesh=mesh, in_specs=in_specs, out_specs=out_specs, check_vma=False)
```

profile of v0, /device:TPU:15, one launch (start us, length us, event | category | flops | bytes accessed | tf_op | source)
XLA Modules:
  0.0 267.5 jit_solution(9964746450724570678)
XLA Ops:
  0.0 0.0 copy-start
  0.0 0.9 copy.8
  0.9 0.1 eq.29
  1.0 0.1 eq.25
  1.1 0.7 broadcast_multiply_fusion
  1.8 1.1 reduce-window.6
  3.0 0.2 slice_reduce_fusion
  3.2 0.1 copy.7
  3.3 0.1 mul.70
  3.4 0.1 fusion.216
  3.5 6.6 %scatter_custom_fusion = bf16[1024,2048]{1,0:T(8,128)(2,1)} fusion(s32[512]{0:T(512)S(1)} %bitcast.208, bf16[]{:T(256)} %constant.18.clone.1, bf16[64,2048]{1,0:T(8,128)(2,1)} %param.6), kind=kCustom, calls=%fused_computation.68 | custom fusion | bytes 4456450 | tf_op jit(solution)/shard_map/scatter | solution.py:37
  10.1 98.8 %all_to_all.10 = bf16[16,64,2048]{2,1,0:T(8,128)(2,1)S(1)} all-to-all(bf16[16,64,2048]{2,1,0:T(8,128)(2,1)} %bitcast.190), channel_id=1, replica_groups=mesh['parts'=2,'expert'=16,'dp'=1] {'expert'}, dimensions={0} | all-to-all | bytes 8388608 | tf_op jit(solution)/shard_map/all_to_all | solution.py:39
  108.9 0.0 copy-start.1
  108.9 0.6 fusion.226
  109.5 0.0 copy-start.8
  109.5 0.0 copy-start.9
  109.5 0.0 copy-start.7
  109.5 0.0 copy-start.6
  109.5 0.0 copy-start.5
  109.5 0.0 copy-start.4
  109.5 0.0 copy-start.3
  109.5 0.0 copy-start.2
  109.5 2.1 copy-done.1
  111.6 1.4 fusion.46
  113.0 1.4 fusion.44
  114.3 0.0 copy-done.8
  114.4 0.0 copy-done.9
  114.4 0.0 copy-done.7
  114.4 1.3 fusion.42
  115.7 0.0 copy-done.6
  115.7 1.3 fusion.40
  117.0 0.0 copy-done.5
  117.0 1.4 fusion.38
  118.4 0.0 copy-done.4
  118.4 1.4 fusion.36
  119.8 0.0 copy-done.3
  119.8 1.4 fusion.34
  121.1 0.0 copy-done.2
  121.1 0.6 fusion.32
  121.7 0.0 copy-done
  121.7 4.6 %fusion.51 = bf16[1024,2048]{1,0:T(8,128)(2,1)} fusion(bf16[1,2048,768]{2,1,0:T(8,128)(2,1)S(1)} %copy-done, bf16[128,2048]{1,0:T(8,128)(2,1)} %bitcast.207, bf16[1,2048,768]{2,1,0:T(8,128)(2,1)} %param.10, f32[128,768]{1,0:T(8,128)} %fusion.46), kind=kOutput, calls=%fused_computation.51 | convolution fusion | flops 806158336 | bytes 7733248 | tf_op jit(solution)/shard_map/dot_general | solution.py:19
  126.3 4.6 %fusion.57 = bf16[1024,2048]{1,0:T(8,128)(2,1)} fusion(bf16[1024,2048]{1,0:T(8,128)(2,1)} %fusion.51, bf16[1,2048,768]{2,1,0:T(8,128)(2,1)S(1)} %copy-done, bf16[128,2048]{1,0:T(8,128)(2,1)} %bitcast.205, bf16[1,2048,768]{2,1,0:T(8,128)(2,1)} %param.10, f32[128,768]{1,0:T(8,128)} %fusion.44), kind=kOutput, calls=%fused_computation.53 | convolution fusion | flops 806158336 | bytes 7733248 | tf_op jit(solution)/shard_map/dot_general | solution.py:19
  130.9 4.6 %fusion.63 = bf16[1024,2048]{1,0:T(8,128)(2,1)} fusion(bf16[1024,2048]{1,0:T(8,128)(2,1)} %fusion.57, bf16[1,2048,768]{2,1,0:T(8,128)(2,1)S(1)} %copy-done, bf16[128,2048]{1,0:T(8,128)(2,1)} %bitcast.203, bf16[1,2048,768]{2,1,0:T(8,128)(2,1)} %param.10, f32[128,768]{1,0:T(8,128)} %fusion.42), kind=kOutput, calls=%fused_computation.55 | convolution fusion | flops 806158336 | bytes 7733248 | tf_op jit(solution)/shard_map/dot_general | solution.py:19
  135.4 4.6 %fusion.69 = bf16[1024,2048]{1,0:T(8,128)(2,1)} fusion(bf16[1024,2048]{1,0:T(8,128)(2,1)} %fusion.63, bf16[1,2048,768]{2,1,0:T(8,128)(2,1)S(1)} %copy-done, bf16[128,2048]{1,0:T(8,128)(2,1)} %bitcast.201, bf16[1,2048,768]{2,1,0:T(8,128)(2,1)} %param.10, f32[128,768]{1,0:T(8,128)} %fusion.40), kind=kOutput, calls=%fused_computation.57 | convolution fusion | flops 806158336 | bytes 7733248 | tf_op jit(solution)/shard_map/dot_general | solution.py:19
  140.0 4.6 %fusion.75 = bf16[1024,2048]{1,0:T(8,128)(2,1)} fusion(bf16[1024,2048]{1,0:T(8,128)(2,1)} %fusion.69, bf16[1,2048,768]{2,1,0:T(8,128)(2,1)S(1)} %copy-done, bf16[128,2048]{1,0:T(8,128)(2,1)} %bitcast.199, bf16[1,2048,768]{2,1,0:T(8,128)(2,1)} %param.10, f32[128,768]{1,0:T(8,128)} %fusion.38), kind=kOutput, calls=%fused_computation.59 | convolution fusion | flops 806158336 | bytes 7733248 | tf_op jit(solution)/shard_map/dot_general | solution.py:19
  144.6 4.6 %fusion.81 = bf16[1024,2048]{1,0:T(8,128)(2,1)} fusion(bf16[1024,2048]{1,0:T(8,128)(2,1)} %fusion.75, bf16[1,2048,768]{2,1,0:T(8,128)(2,1)S(1)} %copy-done, bf16[128,2048]{1,0:T(8,128)(2,1)} %bitcast.197, bf16[1,2048,768]{2,1,0:T(8,128)(2,1)} %param.10, f32[128,768]{1,0:T(8,128)} %fusion.36), kind=kOutput, calls=%fused_computation.61 | convolution fusion | flops 806158336 | bytes 7733248 | tf_op jit(solution)/shard_map/dot_general | solution.py:19
  149.2 4.8 %fusion.87 = bf16[1024,2048]{1,0:T(8,128)(2,1)} fusion(bf16[1024,2048]{1,0:T(8,128)(2,1)} %fusion.81, bf16[1,2048,768]{2,1,0:T(8,128)(2,1)S(1)} %copy-done, bf16[128,2048]{1,0:T(8,128)(2,1)} %bitcast.195, bf16[1,2048,768]{2,1,0:T(8,128)(2,1)} %param.10, f32[128,768]{1,0:T(8,128)} %fusion.34), kind=kOutput, calls=%fused_computation.63 | convolution fusion | flops 806158336 | bytes 7733248 | tf_op jit(solution)/shard_map/dot_general | solution.py:19
  153.9 4.5 %fusion.93 = bf16[1024,2048]{1,0:T(8,128)(2,1)} fusion(bf16[1024,2048]{1,0:T(8,128)(2,1)} %fusion.87, bf16[1,2048,768]{2,1,0:T(8,128)(2,1)S(1)} %copy-done, bf16[128,2048]{1,0:T(8,128)(2,1)} %bitcast.193, bf16[1,2048,768]{2,1,0:T(8,128)(2,1)} %param.10, f32[128,768]{1,0:T(8,128)S(1)} %fusion.32), kind=kOutput, calls=%fused_computation.65 | convolution fusion | flops 806158336 | bytes 7733248 | tf_op jit(solution)/shard_map/dot_general | solution.py:19
  158.5 0.0 copy-start.10
  158.5 5.4 %all-to-all-start.1 = ((bf16[16,64,2048]{2,1,0:T(8,128)(2,1)}), bf16[16,64,2048]{2,1,0:T(8,128)(2,1)}, u32[]{:S(2)}, u32[]{:S(2)}) async-start(bf16[16,64,2048]{2,1,0:T(8,128)(2,1)} %bitcast.191), calls=%async_computation.1 | async-start | bytes 8388608 | tf_op jit(solution)/shard_map/all_to_all | solution.py:48
  163.9 0.0 copy-done.10
  163.9 0.1 copy.11
  164.0 92.3 %all-to-all-done.1 = bf16[16,64,2048]{2,1,0:T(8,128)(2,1)} async-done(((bf16[16,64,2048]{2,1,0:T(8,128)(2,1)}), bf16[16,64,2048]{2,1,0:T(8,128)(2,1)}, u32[]{:S(2)}, u32[]{:S(2)}) %all-to-all-start.1) | async-done | bytes 4194336 | tf_op jit(solution)/shard_map/all_to_all | solution.py:48
  256.4 8.0 %gather_fusion = bf16[512,2048]{1,0:T(8,128)(2,1)} fusion(bf16[1024,2048]{1,0:T(8,128)(2,1)} %bitcast.17, s32[1024]{0:T(1024)S(1)} %pad_clamp_fusion), kind=kCustom, calls=%fused_computation | custom fusion | bytes 4196352 | tf_op jit(solution)/shard_map/gather | solution.py:51
  264.4 2.3 fusion.96
  266.7 0.9 copy.16
  (5 shorter events, 0.1 us)
Async XLA Ops:
  0.0 121.7 %copy-start = (bf16[1,2048,768]{2,1,0:T(8,128)(2,1)S(1)}, bf16[1,2048,768]{2,1,0:T(8,128)(2,1)}, u32[]{:S(2)}) copy-start(bf16[1,2048,768]{2,1,0:T(8,128)(2,1)} %param.11) | copy-start | bytes 9437188
  108.9 2.7 %copy-start.1 = (bf16[1,2048,768]{2,1,0:T(8,128)(2,1)S(1)}, bf16[1,2048,768]{2,1,0:T(8,128)(2,1)}, u32[]{:S(2)}) copy-start(bf16[1,2048,768]{2,1,0:T(8,128)(2,1)} %param.9) | copy-start | bytes 9437188
  109.5 4.9 %copy-start.8 = (bf16[2,64,2048]{2,1,0:T(8,128)(2,1)}, bf16[2,64,2048]{2,1,0:T(8,128)(2,1)S(1)}, u32[]{:S(2)}) copy-start(bf16[2,64,2048]{2,1,0:T(8,128)(2,1)S(1)} %get-tuple-element.11) | copy-start | bytes 1572868
  109.5 4.9 %copy-start.9 = (bf16[2,64,2048]{2,1,0:T(8,128)(2,1)}, bf16[2,64,2048]{2,1,0:T(8,128)(2,1)S(1)}, u32[]{:S(2)}) copy-start(bf16[2,64,2048]{2,1,0:T(8,128)(2,1)S(1)} %get-tuple-element.12) | copy-start | bytes 1572868
  109.5 4.9 %copy-start.7 = (bf16[2,64,2048]{2,1,0:T(8,128)(2,1)}, bf16[2,64,2048]{2,1,0:T(8,128)(2,1)S(1)}, u32[]{:S(2)}) copy-start(bf16[2,64,2048]{2,1,0:T(8,128)(2,1)S(1)} %get-tuple-element.10) | copy-start | bytes 1572868
  109.5 6.2 %copy-start.6 = (bf16[2,64,2048]{2,1,0:T(8,128)(2,1)}, bf16[2,64,2048]{2,1,0:T(8,128)(2,1)S(1)}, u32[]{:S(2)}) copy-start(bf16[2,64,2048]{2,1,0:T(8,128)(2,1)S(1)} %get-tuple-element.9) | copy-start | bytes 1572868
  109.5 7.5 %copy-start.5 = (bf16[2,64,2048]{2,1,0:T(8,128)(2,1)}, bf16[2,64,2048]{2,1,0:T(8,128)(2,1)S(1)}, u32[]{:S(2)}) copy-start(bf16[2,64,2048]{2,1,0:T(8,128)(2,1)S(1)} %get-tuple-element.8) | copy-start | bytes 1572868
  109.5 8.9 %copy-start.4 = (bf16[2,64,2048]{2,1,0:T(8,128)(2,1)}, bf16[2,64,2048]{2,1,0:T(8,128)(2,1)S(1)}, u32[]{:S(2)}) copy-start(bf16[2,64,2048]{2,1,0:T(8,128)(2,1)S(1)} %get-tuple-element.7) | copy-start | bytes 1572868
  109.5 10.2 %copy-start.3 = (bf16[2,64,2048]{2,1,0:T(8,128)(2,1)}, bf16[2,64,2048]{2,1,0:T(8,128)(2,1)S(1)}, u32[]{:S(2)}) copy-start(bf16[2,64,2048]{2,1,0:T(8,128)(2,1)S(1)} %get-tuple-element.6) | copy-start | bytes 1572868
  109.5 11.6 %copy-start.2 = (bf16[2,64,2048]{2,1,0:T(8,128)(2,1)}, bf16[2,64,2048]{2,1,0:T(8,128)(2,1)S(1)}, u32[]{:S(2)}) copy-start(bf16[2,64,2048]{2,1,0:T(8,128)(2,1)S(1)} %get-tuple-element.5) | copy-start | bytes 1572868
  158.5 5.5 %copy-start.10 = (f32[64,8]{0,1:T(8,128)S(1)}, f32[64,8]{0,1:T(8,128)}, u32[]{:S(2)}) copy-start(f32[64,8]{0,1:T(8,128)} %param.8) | copy-start | bytes 6148
  158.5 97.9 %all-to-all-start.1 = ((bf16[16,64,2048]{2,1,0:T(8,128)(2,1)}), bf16[16,64,2048]{2,1,0:T(8,128)(2,1)}, u32[]{:S(2)}, u32[]{:S(2)}) async-start(bf16[16,64,2048]{2,1,0:T(8,128)(2,1)} %bitcast.191), calls=%async_computation.1 | async-start | bytes 8388608 | tf_op jit(solution)/shard_map/all_to_all | solution.py:48
where the time goes:
time: 268 us
  blocking collectives  98.8 us (37%)
  waiting for transfers between devices  92.3 us (34%)
  matrix products  49.1 us (18%)
  local copies, waits for them, and re-layouts  19.7 us (7%)
  starting transfers between devices  5.45 us (2%)
    all_to_all x1, blocking collectives, body(): lax.all_to_all(send, 'expert', split_axis=0, concat_axis=0, tiled=True)  98.8 us
    all_to_all x1, waiting for transfers between devices, body(): lax.all_to_all(expert_out.reshape(experts, cap, width), 'expert', split_a...  92.3 us
    dot_general x8, matrix products, expert_rows(): lax.dot_general(hidden, down_w, (((1,), (1,)), ((), ())), preferred_eleme...  36.7 us
    dot_general x8, matrix products, expert_rows(): gate_val = jnp.dot(block_rows, gate_w, preferred_element_type=jnp.float32)  10.1 us
    gather x1, local copies, waits for them, and re-layouts, body(): picked = back.reshape(slots_all, width)[slot].reshape(tok_count, top, width)  8.01 us
    scatter x1, local copies, waits for them, and re-layouts, body(): jnp.zeros((slots_all, width), jnp.bfloat16).at[slot]  6.58 us
    all_to_all x1, starting transfers between devices, body(): lax.all_to_all(expert_out.reshape(experts, cap, width), 'expert', split_a...  5.45 us
  transfers between devices with their start and end apart: 1, of which 1 were waited for; matrix products, arithmetic and copies ran while one was open for 0% of the time, Pallas kernels for 0%

commit v1 on v0

--- a/solution.py
+++ b/solution.py
@@ -23,7 +23,7 @@
     return jnp.concatenate(pieces, 0)
 
 
-def body(tokens, expert_ids, router_weights, w_gate, w_up, w_down):
+def routed_body(tokens, expert_ids, router_weights, w_gate, w_up, w_down):
     tok_count, top = expert_ids.shape
     width = tokens.shape[1]
     experts = lax.axis_size("expert")
@@ -53,6 +53,23 @@
     return mixed.astype(jnp.bfloat16)
 
 
+def dense_body(tokens, expert_ids, router_weights, w_gate, w_up, w_down):
+    experts = lax.axis_size("expert")
+    numbers = jnp.arange(experts, dtype=jnp.int32)
+    chosen = expert_ids[None, :, :] == numbers[:, None, None]
+    weight = jnp.sum(jnp.where(chosen, router_weights[None, :, :], 0.0), 2)
+    weight = lax.all_to_all(weight, "expert", split_axis=0, concat_axis=0, tiled=True).reshape(-1)
+    rows = lax.all_gather(tokens, "expert", axis=0, tiled=True)
+    gate_val = jnp.dot(rows, w_gate[0], preferred_element_type=jnp.float32)
+    up_val = jnp.dot(rows, w_up[0], preferred_element_type=jnp.float32)
+    hidden = (jax.nn.silu(gate_val) * up_val).astype(jnp.bfloat16)
+    out = lax.dot_general(
+        hidden, w_down[0], (((1,), (1,)), ((), ())), preferred_element_type=jnp.float32
+    )
+    out = (out * weight[:, None]).astype(jnp.bfloat16)
+    return lax.psum_scatter(out, "expert", scatter_dimension=0, tiled=True)
+
+
 def solution(mesh):
     in_specs = (
         P(("parts", "expert", "dp"), None),
@@ -63,4 +80,12 @@
         P("expert", None, "dp"),
     )
     out_specs = P(("parts", "expert", "dp"), None)
-    return jax.shard_map(body, mesh=mesh, in_specs=in_specs, out_specs=out_specs, check_vma=False)
+
+    def whole(tokens, expert_ids, router_weights, w_gate, w_up, w_down):
+        few = mesh.shape["dp"] == 1 and 2 * expert_ids.shape[1] >= mesh.shape["expert"]
+        body = dense_body if few else routed_body
+        return jax.shard_map(
+            body, mesh=mesh, in_specs=in_specs, out_specs=out_specs, check_vma=False
+        )(tokens, expert_ids, router_weights, w_gate, w_up, w_down)
+
+    return whole

time: 268 us -> 162 us (0.60)
  the two profiles are of different devices: /device:TPU:15 before, /device:TPU:0 now
where the time goes in v1:
time: 162 us
  waiting for transfers between devices  112 us (69%)
  matrix products  20.6 us (13%)
  blocking collectives  13.6 us (8%)
  between operations  13.4 us (8%)
    reduce_scatter x1, waiting for transfers between devices, dense_body(): return lax.psum_scatter(out, 'expert', scatter_dimension=0, tiled=True)  71.2 us
    all_gather x1, waiting for transfers between devices, dense_body(): rows = lax.all_gather(tokens, 'expert', axis=0, tiled=True)  39.8 us
    all_to_all x1, blocking collectives, dense_body(): lax.all_to_all(weight, 'expert', split_axis=0, concat_axis=0, tiled=True)  13.6 us
    dot_general x1, matrix products, dense_body(): lax.dot_general(hidden, w_down[0], (((1,), (1,)), ((), ())), preferred_el...  12.3 us
    dot_general x1, matrix products, dense_body(): up_val = jnp.dot(rows, w_up[0], preferred_element_type=jnp.float32)  8.33 us
  transfers between devices with their start and end apart: 2, of which 2 were waited for; matrix products, arithmetic and copies ran while one was open for 1% of the time, Pallas kernels for 0%

profile of v1, /device:TPU:0, one launch (start us, length us, event | category | flops | bytes accessed | tf_op | source)
XLA Modules:
  0.0 161.6 jit_solution(13287259876756076945)
XLA Ops:
  6.5 0.0 copy-start
  6.5 0.0 all-gather.2.cloned.1.call-start
  6.5 0.7 all-gather.2.cloned.1.call-update
  7.3 0.0 reduce-scatter.2.cloned.1.call-start
  7.3 0.9 select_reduce_fusion
  8.2 13.6 %all_to_all.9 = f32[16,1,64]{2,1,0:T(1,128)S(1)} all-to-all(f32[16,1,64]{2,1,0:T(1,128)S(1)} %bitcast.18), channel_id=1, replica_groups=mesh['parts'=2,'expert'=16,'dp'=1] {'expert'}, dimensions={0} | all-to-all | bytes 8192 | tf_op jit(solution)/shard_map/all_to_all | solution.py:61
  21.8 0.5 broadcast.7
  22.3 0.7 reduce.3
  23.0 0.1 mul.19
  23.0 39.8 %all-gather.2.cloned.1.call-done = bf16[1024,2048]{1,0:T(8,128)(2,1)} async-done(((bf16[64,2048]{1,0:T(8,128)(2,1)}), bf16[1024,2048]{1,0:T(8,128)(2,1)}) %all-gather.2.cloned.1.call-update) | async-done | bytes 4194320 | tf_op jit(solution)/shard_map/all_gather | solution.py:62
  62.8 8.3 %fusion.1 = f32[1024,768]{1,0:T(8,128)} fusion(bf16[1024,2048]{1,0:T(8,128)(2,1)} %all-gather.2.cloned.1.call-done, bf16[1,2048,768]{2,1,0:T(8,128)(2,1)} %param.10), kind=kOutput, calls=%fused_computation.2 | convolution fusion | flops 3221225472 | bytes 10485760 | tf_op jit(solution)/shard_map/dot_general | solution.py:64
  71.2 0.0 copy-done
  71.2 12.3 %multiply_convert_fusion = bf16[1024,2048]{1,0:T(8,128)(2,1)} fusion(f32[1024]{0:T(1024)S(1)} %mul.19, bf16[1,2048,768]{2,1,0:T(8,128)(2,1)S(1)} %copy-done, f32[1024,768]{1,0:T(8,128)} %fusion.1, bf16[1024,2048]{1,0:T(8,128)(2,1)} %all-gather.2.cloned.1.call-done, bf16[1,2048,768]{2,1,0:T(8,128)(2,1)} %param.9), kind=kOutput, calls=%fused_computation | convolution fusion | flops 6451363840 | bytes 17829888 | tf_op jit(solution)/shard_map/dot_general | solution.py:66
  83.5 0.0 reduce-scatter.2.cloned.1.call-update
  83.5 71.2 %reduce-scatter.2.cloned.1.call-done = bf16[64,2048]{1,0:T(8,128)(2,1)} async-done(((bf16[1024,2048]{1,0:T(8,128)(2,1)}), bf16[64,2048]{1,0:T(8,128)(2,1)}) %reduce-scatter.2.cloned.1.call-update) | async-done | bytes 262160 | tf_op jit(solution)/shard_map/reduce_scatter | solution.py:70
Async XLA Ops:
  6.5 64.6 %copy-start = (bf16[1,2048,768]{2,1,0:T(8,128)(2,1)S(1)}, bf16[1,2048,768]{2,1,0:T(8,128)(2,1)}, u32[]{:S(2)}) copy-start(bf16[1,2048,768]{2,1,0:T(8,128)(2,1)} %param.11) | copy-start | bytes 9437188
  6.5 56.3 %all-gather.2.cloned.1.call-start = ((), (), s32[]{:S(2)}) async-start(), calls=%async_computation.2 | async-start | bytes 4456448 | tf_op jit(solution)/shard_map/all_gather | solution.py:62
  7.3 147.5 %reduce-scatter.2.cloned.1.call-start = ((), (), s32[]{:S(2)}) async-start(), calls=%async_computation.3 | async-start | bytes 4456448 | tf_op jit(solution)/shard_map/reduce_scatter | solution.py:70
Sparse Core Ops, SparseCore 0:
  9.5 53.2 all-gather.1
  83.6 71.0 reduce-scatter.1

commit v2 on v1

--- a/solution.py
+++ b/solution.py
@@ -1,8 +1,11 @@
+import functools
 import math
 
 import jax
 import jax.numpy as jnp
 from jax import lax
+from jax.experimental import pallas as pl
+from jax.experimental.pallas import tpu as pltpu
 from jax.sharding import PartitionSpec as P
 
 
@@ -53,21 +56,120 @@
     return mixed.astype(jnp.bfloat16)
 
 
+def ring_order(chips):
+    half = chips // 2
+    return [2 * row for row in range(half)] + [2 * row + 1 for row in reversed(range(half))]
+
+
+def swap_pairs(experts):
+    return [(index, index ^ 1) for index in range(experts)]
+
+
+def ring_pairs(experts):
+    order = ring_order(experts // 2)
+    count = len(order)
+    pairs = []
+    for place, chip in enumerate(order):
+        pairs.append((2 * chip, 2 * order[(place + 1) % count]))
+        pairs.append((2 * chip + 1, 2 * order[(place - 1) % count] + 1))
+    return pairs
+
+
+def expert_kernel(width, experts, own_ref, first_ref, second_ref, gate_ref, up_ref, down_ref,
+                  first_out, second_out, rows_ref, hidden_ref):
+    half = first_ref.shape[0]
+    ff = gate_ref.shape[2]
+    rows_ref[:half, :] = first_ref[...]
+    rows_ref[half:, :] = second_ref[...]
+    tail = rows_ref[:, width:].astype(jnp.float32)
+    lane = lax.broadcasted_iota(jnp.int32, tail.shape, 1)
+    own = own_ref[0]
+    mine = (lane == own) | (lane == own + experts)
+    weight = jnp.sum(jnp.where(mine, tail, 0.0), axis=1, keepdims=True)
+    step = math.gcd(ff, 256)
+    for at in range(0, ff, step):
+        part = slice(at, at + step)
+        rows = rows_ref[:, :width]
+        gate = jnp.dot(rows, gate_ref[0, :, part], preferred_element_type=jnp.float32)
+        up = jnp.dot(rows, up_ref[0, :, part], preferred_element_type=jnp.float32)
+        hidden_ref[:, part] = (gate / (1.0 + jnp.exp(-gate)) * up).astype(jnp.bfloat16)
+    step = math.gcd(width, 512)
+    for at in range(0, width, step):
+        part = slice(at, at + step)
+        out = lax.dot_general(
+            hidden_ref[...], down_ref[0, part, :], (((1,), (1,)), ((), ())),
+            preferred_element_type=jnp.float32,
+        )
+        out = (out * weight).astype(jnp.bfloat16)
+        first_out[:, part] = out[:half]
+        second_out[:, part] = out[half:]
+
+
+def run_expert(own, first, second, gate_w, up_w, down_w, experts):
+    half, wide = first.shape
+    width, ff = gate_w.shape[1:]
+    vmem = pl.BlockSpec(memory_space=pltpu.VMEM)
+    return pl.pallas_call(
+        functools.partial(expert_kernel, width, experts),
+        out_shape=[jax.ShapeDtypeStruct((half, width), jnp.bfloat16)] * 2,
+        in_specs=[pl.BlockSpec(memory_space=pltpu.SMEM)] + [vmem] * 5,
+        out_specs=[vmem] * 2,
+        scratch_shapes=[
+            pltpu.VMEM((2 * half, wide), jnp.bfloat16),
+            pltpu.VMEM((2 * half, ff), jnp.bfloat16),
+        ],
+        compiler_params=pltpu.CompilerParams(vmem_limit_bytes=30 << 20),
+        cost_estimate=pl.CostEstimate(
+            flops=2 * 2 * half * 3 * width * ff, bytes_accessed=8 * half * width,
+            transcendentals=2 * half * ff,
+        ),
+    )(own, first, second, gate_w, up_w, down_w)
+
+
+def added(*terms):
+    total = terms[0].astype(jnp.float32)
+    for term in terms[1:]:
+        total = total + term.astype(jnp.float32)
+    return total.astype(jnp.bfloat16)
+
+
 def dense_body(tokens, expert_ids, router_weights, w_gate, w_up, w_down):
     experts = lax.axis_size("expert")
+    count = tokens.shape[0]
+    rounds = experts // 4
+    swap = functools.partial(lax.ppermute, axis_name="expert", perm=swap_pairs(experts))
+    ring = functools.partial(lax.ppermute, axis_name="expert", perm=ring_pairs(experts))
+    own = lax.axis_index("expert").reshape(1)
+
     numbers = jnp.arange(experts, dtype=jnp.int32)
-    chosen = expert_ids[None, :, :] == numbers[:, None, None]
-    weight = jnp.sum(jnp.where(chosen, router_weights[None, :, :], 0.0), 2)
-    weight = lax.all_to_all(weight, "expert", split_axis=0, concat_axis=0, tiled=True).reshape(-1)
-    rows = lax.all_gather(tokens, "expert", axis=0, tiled=True)
-    gate_val = jnp.dot(rows, w_gate[0], preferred_element_type=jnp.float32)
-    up_val = jnp.dot(rows, w_up[0], preferred_element_type=jnp.float32)
-    hidden = (jax.nn.silu(gate_val) * up_val).astype(jnp.bfloat16)
-    out = lax.dot_general(
-        hidden, w_down[0], (((1,), (1,)), ((), ())), preferred_element_type=jnp.float32
-    )
-    out = (out * weight[:, None]).astype(jnp.bfloat16)
-    return lax.psum_scatter(out, "expert", scatter_dimension=0, tiled=True)
+    chosen = expert_ids[:, :, None] == numbers[None, None, :]
+    weight = jnp.sum(jnp.where(chosen, router_weights[:, :, None], 0.0), 1)
+    high = weight.astype(jnp.bfloat16)
+    low = (weight - high.astype(jnp.float32)).astype(jnp.bfloat16)
+    empty = jnp.zeros((count, 128 - 2 * experts), jnp.bfloat16)
+    mine = jnp.concatenate([tokens, high, low, empty], 1)
+
+    weights = [pltpu.with_memory_space_constraint(w, pltpu.VMEM) for w in (w_gate, w_up, w_down)]
+    run = lambda first, second: run_expert(own, first, second, *weights, experts)
+
+    sibling = swap(mine)
+    held = jnp.concatenate([mine, sibling], 0)
+    kept, other = run(mine, sibling)
+    pairs = []
+    for step in range(1, rounds + 1):
+        held = ring(held if step < rounds else held[:count])
+        first, second = run(held, swap(held))
+        pairs.append((second, swap(first)))
+    moving = None
+    for second, first in reversed(pairs):
+        terms = added(second, first) if moving is None else None
+        if moving is not None:
+            if moving.shape[0] < second.shape[0]:
+                moving = jnp.pad(moving, ((0, second.shape[0] - moving.shape[0]), (0, 0)))
+            terms = added(second, first, moving)
+        moving = ring(terms)
+    last = swap(added(moving[:count], other))
+    return added(moving[count:], kept, last)
 
 
 def solution(mesh):

time: 162 us -> 90.2 us (0.56)
  waiting for transfers between devices: 112 us -> 48.4 us
  matrix products: 20.6 us -> 0 us
  starting transfers between devices: 0.04 us -> 20 us
  blocking collectives: 13.6 us -> 0 us
  between operations: 13.4 us -> 0.15 us
  Pallas kernels: 0 us -> 12 us
  local copies, waits for them, and re-layouts: 0.59 us -> 6.93 us
    reduce_scatter x1 -> x0, waiting for transfers between devices: 71.2 us -> none  [dense_body(): return lax.psum_scatter(out, 'expert', scatter_dimension=0, tiled=True)]
    ppermute x0 -> x18, waiting for transfers between devices: none -> 48.4 us  [the longest x4 26.7 us: dense_body(): held = ring(held if step < rounds else held[:count])]
    all_gather x1 -> x0, waiting for transfers between devices: 39.8 us -> none  [dense_body(): rows = lax.all_gather(tokens, 'expert', axis=0, tiled=True)]
    dot_general x2 -> x0, matrix products: 20.6 us -> none  [the longest x1 12.3 us: dense_body(): lax.dot_general(hidden, w_down[0], (((1,), (1,)), ((), ())), preferred_el...]
    ppermute x0 -> x18, starting transfers between devices: none -> 20 us  [the longest x4 9.36 us: dense_body(): held = ring(held if step < rounds else held[:count])]
    all_to_all x1 -> x0, blocking collectives: 13.6 us -> none  [dense_body(): lax.all_to_all(weight, 'expert', split_axis=0, concat_axis=0, tiled=True)]
    pallas_call x0 -> x5, Pallas kernels: none -> 12 us  [run_expert(): pl.pallas_call(functools.partial(expert_kernel, width, experts), out_shap...]
    unnamed x2 -> x10, local copies, waits for them, and re-layouts: 0.01 us -> 5.68 us
  transfers between devices with their start and end apart: 2 -> 18, of which waited for: 2 -> 11; matrix products, arithmetic and copies ran while one was open for 1% -> 1% of each run, Pallas kernels for 0% -> 13%
where the time goes in v2:
time: 90.2 us; the launch traced here: 89.9 us
  waiting for transfers between devices  48.4 us (54%)
  starting transfers between devices  20 us (22%)
  Pallas kernels  12 us (13%)
  local copies, waits for them, and re-layouts  6.93 us (8%)
  other arithmetic  2.36 us (3%)
    ppermute x4, waiting for transfers between devices, dense_body(): held = ring(held if step < rounds else held[:count])  26.7 us
    ppermute x4, waiting for transfers between devices, dense_body(): moving = ring(terms)  17.4 us
    pallas_call x5, Pallas kernels, run_expert(): pl.pallas_call(functools.partial(expert_kernel, width, experts), out_shap...  12 us
    ppermute x4, starting transfers between devices, dense_body(): held = ring(held if step < rounds else held[:count])  9.36 us
    ppermute x4, starting transfers between devices, dense_body(): moving = ring(terms)  8.64 us
    unnamed x10, local copies, waits for them, and re-layouts  5.68 us
  transfers between devices with their start and end apart: 18, of which 11 were waited for; matrix products, arithmetic and copies ran while one was open for 1% of the time, Pallas kernels for 13%

profile of v2, /device:TPU:0, one launch (start us, length us, event | category | flops | bytes accessed | tf_op | source)
XLA Modules:
  0.0 89.9 jit_solution(16652597681897269540)
XLA Ops:
  0.0 0.7 select_reduce_fusion
  0.7 0.1 copy.12
  0.8 0.1 copy.13
  0.9 1.0 %concatenate.6.first_ref = bf16[64,2176]{1,0:T(8,128)(2,1)S(1)} concatenate(bf16[64,2048]{1,0:T(8,128)(2,1)} %param.6, bf16[64,16]{1,0:T(8,128)(2,1)S(1)} %copy.13, bf16[64,16]{1,0:T(8,128)(2,1)S(1)} %subtract_convert_fusion, bf16[64,96]{1,0:T(8,128)(2,1)S(1)} %broadcast_in_dim.20), dimensions={1} | concatenate | bytes 557056 | tf_op jit(solution)/shard_map/concatenate | solution.py:150
  2.0 0.5 collective-permute-start
  2.5 1.2 %collective-permute-done.second_ref = bf16[64,2176]{1,0:T(8,128)(2,1)S(1)} collective-permute-done((bf16[64,2176]{1,0:T(8,128)(2,1)S(1)}, bf16[64,2176]{1,0:T(8,128)(2,1)S(1)}, u32[]{:S(2)}, u32[]{:S(2)}) %collective-permute-start) | collective-permute-done | bytes 278560 | tf_op jit(solution)/shard_map/ppermute | solution.py:155
  3.7 3.0 %collective-permute-start.1 = (bf16[128,2176]{1,0:T(8,128)(2,1)S(1)}, bf16[128,2176]{1,0:T(8,128)(2,1)S(1)}, u32[]{:S(2)}, u32[]{:S(2)}) collective-permute-start(bf16[128,2176]{1,0:T(8,128)(2,1)S(1)} %pad_maximum_fusion), channel_id=1, source_target_pairs={{0,4},{1,3},{4,8},{5,1},{8,12},{9,5},{12,14},{13,9},{14,10},{15,13... | collective-permute-start | bytes 1671176 | tf_op jit(solution)/shard_map/ppermute | solution.py:160
  6.7 7.4 %collective-permute-done.1.first_ref = bf16[128,2176]{1,0:T(8,128)(2,1)S(1)} collective-permute-done((bf16[128,2176]{1,0:T(8,128)(2,1)S(1)}, bf16[128,2176]{1,0:T(8,128)(2,1)S(1)}, u32[]{:S(2)}, u32[]{:S(2)}) %collective-permute-start.1) | collective-permute-done | bytes 557088 | tf_op jit(solution)/shard_map/ppermute | solution.py:160
  14.2 2.1 %collective-permute-start.4 = (bf16[128,2176]{1,0:T(8,128)(2,1)S(1)}, bf16[128,2176]{1,0:T(8,128)(2,1)S(1)}, u32[]{:S(2)}, u32[]{:S(2)}) collective-permute-start(bf16[128,2176]{1,0:T(8,128)(2,1)S(1)} %collective-permute-done.1.first_ref), channel_id=1, source_target_pairs={{0,4},{1,3},{4,8},{5,1},{8,12},{9,5},{12,14},{13,9},{14,10},{15,13... | collective-permute-start | bytes 1671176 | tf_op jit(solution)/shard_map/ppermute | solution.py:160
  16.3 7.4 %collective-permute-done.4.first_ref = bf16[128,2176]{1,0:T(8,128)(2,1)S(1)} collective-permute-done((bf16[128,2176]{1,0:T(8,128)(2,1)S(1)}, bf16[128,2176]{1,0:T(8,128)(2,1)S(1)}, u32[]{:S(2)}, u32[]{:S(2)}) %collective-permute-start.4) | collective-permute-done | bytes 557088 | tf_op jit(solution)/shard_map/ppermute | solution.py:160
  23.7 2.1 %collective-permute-start.7 = (bf16[128,2176]{1,0:T(8,128)(2,1)S(1)}, bf16[128,2176]{1,0:T(8,128)(2,1)S(1)}, u32[]{:S(2)}, u32[]{:S(2)}) collective-permute-start(bf16[128,2176]{1,0:T(8,128)(2,1)S(1)} %collective-permute-done.4.first_ref), channel_id=1, source_target_pairs={{0,4},{1,3},{4,8},{5,1},{8,12},{9,5},{12,14},{13,9},{14,10},{15,13... | collective-permute-start | bytes 1671176 | tf_op jit(solution)/shard_map/ppermute | solution.py:160
  25.8 7.4 %collective-permute-done.7.first_ref = bf16[128,2176]{1,0:T(8,128)(2,1)S(1)} collective-permute-done((bf16[128,2176]{1,0:T(8,128)(2,1)S(1)}, bf16[128,2176]{1,0:T(8,128)(2,1)S(1)}, u32[]{:S(2)}, u32[]{:S(2)}) %collective-permute-start.7) | collective-permute-done | bytes 557088 | tf_op jit(solution)/shard_map/ppermute | solution.py:160
  33.2 2.2 %collective-permute-start.10 = (bf16[64,2176]{1,0:T(8,128)(2,1)S(1)}, bf16[64,2176]{1,0:T(8,128)(2,1)S(1)}, u32[]{:S(2)}, u32[]{:S(2)}) collective-permute-start(bf16[64,2176]{1,0:T(8,128)(2,1)S(1)} %slice.12), channel_id=1, source_target_pairs={{0,4},{1,3},{4,8},{5,1},{8,12},{9,5},{12,14},{13,9},{14,10},{15,13... | collective-permute-start | bytes 835592 | tf_op jit(solution)/shard_map/ppermute | solution.py:160
  35.4 0.0 collective-permute-start.8
  35.4 4.4 %collective-permute-done.10.first_ref = bf16[64,2176]{1,0:T(8,128)(2,1)S(1)} collective-permute-done((bf16[64,2176]{1,0:T(8,128)(2,1)S(1)}, bf16[64,2176]{1,0:T(8,128)(2,1)S(1)}, u32[]{:S(2)}, u32[]{:S(2)}) %collective-permute-start.10) | collective-permute-done | bytes 278560 | tf_op jit(solution)/shard_map/ppermute | solution.py:160
  39.9 0.0 collective-permute-start.11
  39.9 1.6 %collective-permute-done.11.second_ref = bf16[64,2176]{1,0:T(8,128)(2,1)S(1)} collective-permute-done((bf16[64,2176]{1,0:T(8,128)(2,1)S(1)}, bf16[64,2176]{1,0:T(8,128)(2,1)S(1)}, u32[]{:S(2)}, u32[]{:S(2)}) %collective-permute-start.11) | collective-permute-done | bytes 278560 | tf_op jit(solution)/shard_map/ppermute | solution.py:161
  41.4 0.0 copy-start
  41.4 1.9 %copy-done = bf16[1,2048,768]{2,1,0:T(8,128)(2,1)S(1)} copy-done((bf16[1,2048,768]{2,1,0:T(8,128)(2,1)S(1)}, bf16[1,2048,768]{2,1,0:T(8,128)(2,1)}, u32[]{:S(2)}) %copy-start) | copy-done | bytes 3145752
  43.3 0.0 copy-start.2
  43.3 1.9 %copy-done.2 = bf16[1,2048,768]{2,1,0:T(8,128)(2,1)S(1)} copy-done((bf16[1,2048,768]{2,1,0:T(8,128)(2,1)S(1)}, bf16[1,2048,768]{2,1,0:T(8,128)(2,1)}, u32[]{:S(2)}) %copy-start.2) | copy-done | bytes 3145752
  45.2 0.0 copy-start.4
  45.2 1.9 %copy-done.4 = bf16[1,2048,768]{2,1,0:T(8,128)(2,1)S(1)} copy-done((bf16[1,2048,768]{2,1,0:T(8,128)(2,1)S(1)}, bf16[1,2048,768]{2,1,0:T(8,128)(2,1)}, u32[]{:S(2)}) %copy-start.4) | copy-done | bytes 3145752
  47.1 2.0 %shard_map.67 = (bf16[64,2048]{1,0:T(8,128)(2,1)S(1)}, bf16[64,2048]{1,0:T(8,128)(2,1)S(1)}) custom-call(s32[1]{0:T(128)} %bitcast.own_ref, bf16[64,2176]{1,0:T(8,128)(2,1)S(1)} %collective-permute-done.10.first_ref, bf16[64,2176]{1,0:T(8,128)(2,1)S(1)} %collective-permute-done.11.second_ref, bf16[1,2048,768]{2,1,0:T(8,128)(2,1)S(1)} %copy-done, ...), custom_call_target="tpu_custom_call" | custom-call | flops 1207959552 | bytes 1048576 | tf_op jit(solution)/shard_map/pallas_call | solution.py:112
  49.1 0.2 collective-permute-start.12
  49.3 0.4 collective-permute-start.5
  49.7 0.0 collective-permute-done.8.second_ref
  49.7 2.7 %shard_map.66 = (bf16[128,2048]{1,0:T(8,128)(2,1)S(1)}, bf16[128,2048]{1,0:T(8,128)(2,1)S(1)}) custom-call(s32[1]{0:T(128)} %bitcast.own_ref, bf16[128,2176]{1,0:T(8,128)(2,1)S(1)} %collective-permute-done.7.first_ref, bf16[128,2176]{1,0:T(8,128)(2,1)S(1)} %collective-permute-done.8.second_ref, bf16[1,2048,768]{2,1,0:T(8,128)(2,1)S(1)} %copy-done, ...), custom_call_target="tpu_custom_call" | custom-call | flops 2415919104 | bytes 2097152 | tf_op jit(solution)/shard_map/pallas_call | solution.py:112
  52.4 0.2 collective-permute-start.9
  52.6 0.0 collective-permute-done.12
  52.6 0.1 add_convert_fusion.5
  52.6 2.2 %collective-permute-start.13 = (bf16[64,2048]{1,0:T(8,128)(2,1)S(1)}, bf16[64,2048]{1,0:T(8,128)(2,1)S(1)}, u32[]{:S(2)}, u32[]{:S(2)}) collective-permute-start(bf16[64,2048]{1,0:T(8,128)(2,1)S(1)} %add_convert_fusion.5), channel_id=1, source_target_pairs={{0,4},{1,3},{4,8},{5,1},{8,12},{9,5},{12,14},{13,9},{14,10},{15,13... | collective-permute-start | bytes 786440 | tf_op jit(solution)/shard_map/ppermute | solution.py:170
  54.8 0.0 collective-permute-start.2
  54.8 0.0 collective-permute-done.5.second_ref
  54.8 2.7 %shard_map.65 = (bf16[128,2048]{1,0:T(8,128)(2,1)S(1)}, bf16[128,2048]{1,0:T(8,128)(2,1)S(1)}) custom-call(s32[1]{0:T(128)} %bitcast.own_ref, bf16[128,2176]{1,0:T(8,128)(2,1)S(1)} %collective-permute-done.4.first_ref, bf16[128,2176]{1,0:T(8,128)(2,1)S(1)} %collective-permute-done.5.second_ref, bf16[1,2048,768]{2,1,0:T(8,128)(2,1)S(1)} %copy-done, ...), custom_call_target="tpu_custom_call" | custom-call | flops 2415919104 | bytes 2097152 | tf_op jit(solution)/shard_map/pallas_call | solution.py:112
  57.5 0.6 collective-permute-start.6
  58.0 1.0 %collective-permute-done.13 = bf16[64,2048]{1,0:T(8,128)(2,1)S(1)} collective-permute-done((bf16[64,2048]{1,0:T(8,128)(2,1)S(1)}, bf16[64,2048]{1,0:T(8,128)(2,1)S(1)}, u32[]{:S(2)}, u32[]{:S(2)}) %collective-permute-start.13) | collective-permute-done | bytes 262176 | tf_op jit(solution)/shard_map/ppermute | solution.py:170
  59.1 0.0 collective-permute-done.9
  59.1 0.2 add_convert_fusion.2
  59.3 2.2 %collective-permute-start.14 = (bf16[128,2048]{1,0:T(8,128)(2,1)S(1)}, bf16[128,2048]{1,0:T(8,128)(2,1)S(1)}, u32[]{:S(2)}, u32[]{:S(2)}) collective-permute-start(bf16[128,2048]{1,0:T(8,128)(2,1)S(1)} %add_convert_fusion.2), channel_id=1, source_target_pairs={{0,4},{1,3},{4,8},{5,1},{8,12},{9,5},{12,14},{13,9},{14,10},{15,13... | collective-permute-start | bytes 1572872 | tf_op jit(solution)/shard_map/ppermute | solution.py:170
  61.4 0.0 collective-permute-done.2.second_ref
  61.4 0.0 copy-start.3
  61.4 2.6 %shard_map.64 = (bf16[128,2048]{1,0:T(8,128)(2,1)S(1)}, bf16[128,2048]{1,0:T(8,128)(2,1)S(1)}) custom-call(s32[1]{0:T(128)} %bitcast.own_ref, bf16[128,2176]{1,0:T(8,128)(2,1)S(1)} %collective-permute-done.1.first_ref, bf16[128,2176]{1,0:T(8,128)(2,1)S(1)} %collective-permute-done.2.second_ref, bf16[1,2048,768]{2,1,0:T(8,128)(2,1)S(1)} %copy-done, ...), custom_call_target="tpu_custom_call" | custom-call | flops 2415919104 | bytes 2097152 | tf_op jit(solution)/shard_map/pallas_call | solution.py:112
  64.1 0.0 copy-start.1
  64.1 0.1 collective-permute-start.3
  64.2 0.0 collective-permute-done.6
  64.2 4.3 %collective-permute-done.14 = bf16[128,2048]{1,0:T(8,128)(2,1)S(1)} collective-permute-done((bf16[128,2048]{1,0:T(8,128)(2,1)S(1)}, bf16[128,2048]{1,0:T(8,128)(2,1)S(1)}, u32[]{:S(2)}, u32[]{:S(2)}) %collective-permute-start.14) | collective-permute-done | bytes 524320 | tf_op jit(solution)/shard_map/ppermute | solution.py:170
  68.5 0.2 add_convert_fusion.1
  68.7 2.2 %collective-permute-start.15 = (bf16[128,2048]{1,0:T(8,128)(2,1)S(1)}, bf16[128,2048]{1,0:T(8,128)(2,1)S(1)}, u32[]{:S(2)}, u32[]{:S(2)}) collective-permute-start(bf16[128,2048]{1,0:T(8,128)(2,1)S(1)} %add_convert_fusion.1), channel_id=1, source_target_pairs={{0,4},{1,3},{4,8},{5,1},{8,12},{9,5},{12,14},{13,9},{14,10},{15,13... | collective-permute-start | bytes 1572872 | tf_op jit(solution)/shard_map/ppermute | solution.py:170
  70.9 0.0 collective-permute-done.3
  70.9 7.1 %collective-permute-done.15 = bf16[128,2048]{1,0:T(8,128)(2,1)S(1)} collective-permute-done((bf16[128,2048]{1,0:T(8,128)(2,1)S(1)}, bf16[128,2048]{1,0:T(8,128)(2,1)S(1)}, u32[]{:S(2)}, u32[]{:S(2)}) %collective-permute-start.15) | collective-permute-done | bytes 524320 | tf_op jit(solution)/shard_map/ppermute | solution.py:170
  78.0 0.2 add_convert_fusion
  78.2 2.2 %collective-permute-start.16 = (bf16[128,2048]{1,0:T(8,128)(2,1)S(1)}, bf16[128,2048]{1,0:T(8,128)(2,1)S(1)}, u32[]{:S(2)}, u32[]{:S(2)}) collective-permute-start(bf16[128,2048]{1,0:T(8,128)(2,1)S(1)} %add_convert_fusion), channel_id=1, source_target_pairs={{0,4},{1,3},{4,8},{5,1},{8,12},{9,5},{12,14},{13,9},{14,10},{15,13... | collective-permute-start | bytes 1572872 | tf_op jit(solution)/shard_map/ppermute | solution.py:170
  80.4 0.0 copy-done.3
  80.4 0.0 copy-done.1
  80.4 2.0 %shard_map.68 = (bf16[64,2048]{1,0:T(8,128)(2,1)S(1)}, bf16[64,2048]{1,0:T(8,128)(2,1)S(1)}) custom-call(s32[1]{0:T(128)} %bitcast.own_ref, bf16[64,2176]{1,0:T(8,128)(2,1)S(1)} %concatenate.6.first_ref, bf16[64,2176]{1,0:T(8,128)(2,1)S(1)} %collective-permute-done.second_ref, bf16[1,2048,768]{2,1,0:T(8,128)(2,1)S(1)} %copy-done.1, ...), custom_call_target="tpu_custom_call" | custom-call | flops 1207959552 | bytes 1048576 | tf_op jit(solution)/shard_map/pallas_call | solution.py:112
  82.4 5.0 %collective-permute-done.16 = bf16[128,2048]{1,0:T(8,128)(2,1)S(1)} collective-permute-done((bf16[128,2048]{1,0:T(8,128)(2,1)S(1)}, bf16[128,2048]{1,0:T(8,128)(2,1)S(1)}, u32[]{:S(2)}, u32[]{:S(2)}) %collective-permute-start.16) | collective-permute-done | bytes 524320 | tf_op jit(solution)/shard_map/ppermute | solution.py:170
  87.5 0.1 add_convert_fusion.4
  87.5 0.1 collective-permute-start.17
  87.6 1.5 %collective-permute-done.17 = bf16[64,2048]{1,0:T(8,128)(2,1)S(1)} collective-permute-done((bf16[64,2048]{1,0:T(8,128)(2,1)S(1)}, bf16[64,2048]{1,0:T(8,128)(2,1)S(1)}, u32[]{:S(2)}, u32[]{:S(2)}) %collective-permute-start.17) | collective-permute-done | bytes 262176 | tf_op jit(solution)/shard_map/ppermute | solution.py:171
  89.1 0.8 add_convert_fusion.3
  (5 shorter events, 0.1 us)
Async XLA Ops:
  2.0 1.7 %collective-permute-start = (bf16[64,2176]{1,0:T(8,128)(2,1)S(1)}, bf16[64,2176]{1,0:T(8,128)(2,1)S(1)}, u32[]{:S(2)}, u32[]{:S(2)}) collective-permute-start(bf16[64,2176]{1,0:T(8,128)(2,1)S(1)} %concatenate.6.first_ref), channel_id=1, source_target_pairs={{0,1},{1,0},{2,3},{3,2},{4,5},{5,4},{6,7},{7,6},{8,9},{9,8},{10,11... | collective-permute-start | bytes 835592 | tf_op jit(solution)/shard_map/ppermute | solution.py:155
  3.7 10.4 %collective-permute-start.1 = (bf16[128,2176]{1,0:T(8,128)(2,1)S(1)}, bf16[128,2176]{1,0:T(8,128)(2,1)S(1)}, u32[]{:S(2)}, u32[]{:S(2)}) collective-permute-start(bf16[128,2176]{1,0:T(8,128)(2,1)S(1)} %pad_maximum_fusion), channel_id=1, source_target_pairs={{0,4},{1,3},{4,8},{5,1},{8,12},{9,5},{12,14},{13,9},{14,10},{15,13... | collective-permute-start | bytes 1671176 | tf_op jit(solution)/shard_map/ppermute | solution.py:160
  14.2 9.5 %collective-permute-start.4 = (bf16[128,2176]{1,0:T(8,128)(2,1)S(1)}, bf16[128,2176]{1,0:T(8,128)(2,1)S(1)}, u32[]{:S(2)}, u32[]{:S(2)}) collective-permute-start(bf16[128,2176]{1,0:T(8,128)(2,1)S(1)} %collective-permute-done.1.first_ref), channel_id=1, source_target_pairs={{0,4},{1,3},{4,8},{5,1},{8,12},{9,5},{12,14},{13,9},{14,10},{15,13... | collective-permute-start | bytes 1671176 | tf_op jit(solution)/shard_map/ppermute | solution.py:160
  23.7 9.5 %collective-permute-start.7 = (bf16[128,2176]{1,0:T(8,128)(2,1)S(1)}, bf16[128,2176]{1,0:T(8,128)(2,1)S(1)}, u32[]{:S(2)}, u32[]{:S(2)}) collective-permute-start(bf16[128,2176]{1,0:T(8,128)(2,1)S(1)} %collective-permute-done.4.first_ref), channel_id=1, source_target_pairs={{0,4},{1,3},{4,8},{5,1},{8,12},{9,5},{12,14},{13,9},{14,10},{15,13... | collective-permute-start | bytes 1671176 | tf_op jit(solution)/shard_map/ppermute | solution.py:160
  33.2 6.6 %collective-permute-start.10 = (bf16[64,2176]{1,0:T(8,128)(2,1)S(1)}, bf16[64,2176]{1,0:T(8,128)(2,1)S(1)}, u32[]{:S(2)}, u32[]{:S(2)}) collective-permute-start(bf16[64,2176]{1,0:T(8,128)(2,1)S(1)} %slice.12), channel_id=1, source_target_pairs={{0,4},{1,3},{4,8},{5,1},{8,12},{9,5},{12,14},{13,9},{14,10},{15,13... | collective-permute-start | bytes 835592 | tf_op jit(solution)/shard_map/ppermute | solution.py:160
  35.4 14.3 %collective-permute-start.8 = (bf16[128,2176]{1,0:T(8,128)(2,1)S(1)}, bf16[128,2176]{1,0:T(8,128)(2,1)S(1)}, u32[]{:S(2)}, u32[]{:S(2)}) collective-permute-start(bf16[128,2176]{1,0:T(8,128)(2,1)S(1)} %collective-permute-done.7.first_ref), channel_id=1, source_target_pairs={{0,1},{1,0},{2,3},{3,2},{4,5},{5,4},{6,7},{7,6},{8,9},{9,8},{10,11... | collective-permute-start | bytes 1671176 | tf_op jit(solution)/shard_map/ppermute | solution.py:161
  39.9 1.6 %collective-permute-start.11 = (bf16[64,2176]{1,0:T(8,128)(2,1)S(1)}, bf16[64,2176]{1,0:T(8,128)(2,1)S(1)}, u32[]{:S(2)}, u32[]{:S(2)}) collective-permute-start(bf16[64,2176]{1,0:T(8,128)(2,1)S(1)} %collective-permute-done.10.first_ref), channel_id=1, source_target_pairs={{0,1},{1,0},{2,3},{3,2},{4,5},{5,4},{6,7},{7,6},{8,9},{9,8},{10,11... | collective-permute-start | bytes 835592 | tf_op jit(solution)/shard_map/ppermute | solution.py:161
  41.4 1.9 %copy-start = (bf16[1,2048,768]{2,1,0:T(8,128)(2,1)S(1)}, bf16[1,2048,768]{2,1,0:T(8,128)(2,1)}, u32[]{:S(2)}) copy-start(bf16[1,2048,768]{2,1,0:T(8,128)(2,1)} %gate_ref.9) | copy-start | bytes 9437188
  43.3 1.9 %copy-start.2 = (bf16[1,2048,768]{2,1,0:T(8,128)(2,1)S(1)}, bf16[1,2048,768]{2,1,0:T(8,128)(2,1)}, u32[]{:S(2)}) copy-start(bf16[1,2048,768]{2,1,0:T(8,128)(2,1)} %up_ref.9) | copy-start | bytes 9437188
  45.2 1.9 %copy-start.4 = (bf16[1,2048,768]{2,1,0:T(8,128)(2,1)S(1)}, bf16[1,2048,768]{2,1,0:T(8,128)(2,1)}, u32[]{:S(2)}) copy-start(bf16[1,2048,768]{2,1,0:T(8,128)(2,1)} %down_ref.9) | copy-start | bytes 9437188
  49.1 3.4 %collective-permute-start.12 = (bf16[64,2048]{1,0:T(8,128)(2,1)S(1)}, bf16[64,2048]{1,0:T(8,128)(2,1)S(1)}, u32[]{:S(2)}, u32[]{:S(2)}) collective-permute-start(bf16[64,2048]{1,0:T(8,128)(2,1)S(1)} %get-tuple-element.22), channel_id=1, source_target_pairs={{0,1},{1,0},{2,3},{3,2},{4,5},{5,4},{6,7},{7,6},{8,9},{9,8},{10,11... | collective-permute-start | bytes 786440 | tf_op jit(solution)/shard_map/ppermute | solution.py:162
  49.3 5.5 %collective-permute-start.5 = (bf16[128,2176]{1,0:T(8,128)(2,1)S(1)}, bf16[128,2176]{1,0:T(8,128)(2,1)S(1)}, u32[]{:S(2)}, u32[]{:S(2)}) collective-permute-start(bf16[128,2176]{1,0:T(8,128)(2,1)S(1)} %collective-permute-done.4.first_ref), channel_id=1, source_target_pairs={{0,1},{1,0},{2,3},{3,2},{4,5},{5,4},{6,7},{7,6},{8,9},{9,8},{10,11... | collective-permute-start | bytes 1671176 | tf_op jit(solution)/shard_map/ppermute | solution.py:161
  52.4 6.7 %collective-permute-start.9 = (bf16[128,2048]{1,0:T(8,128)(2,1)S(1)}, bf16[128,2048]{1,0:T(8,128)(2,1)S(1)}, u32[]{:S(2)}, u32[]{:S(2)}) collective-permute-start(bf16[128,2048]{1,0:T(8,128)(2,1)S(1)} %get-tuple-element.20), channel_id=1, source_target_pairs={{0,1},{1,0},{2,3},{3,2},{4,5},{5,4},{6,7},{7,6},{8,9},{9,8},{10,11... | collective-permute-start | bytes 1572872 | tf_op jit(solution)/shard_map/ppermute | solution.py:162
  52.6 6.4 %collective-permute-start.13 = (bf16[64,2048]{1,0:T(8,128)(2,1)S(1)}, bf16[64,2048]{1,0:T(8,128)(2,1)S(1)}, u32[]{:S(2)}, u32[]{:S(2)}) collective-permute-start(bf16[64,2048]{1,0:T(8,128)(2,1)S(1)} %add_convert_fusion.5), channel_id=1, source_target_pairs={{0,4},{1,3},{4,8},{5,1},{8,12},{9,5},{12,14},{13,9},{14,10},{15,13... | collective-permute-start | bytes 786440 | tf_op jit(solution)/shard_map/ppermute | solution.py:170
  54.8 6.6 %collective-permute-start.2 = (bf16[128,2176]{1,0:T(8,128)(2,1)S(1)}, bf16[128,2176]{1,0:T(8,128)(2,1)S(1)}, u32[]{:S(2)}, u32[]{:S(2)}) collective-permute-start(bf16[128,2176]{1,0:T(8,128)(2,1)S(1)} %collective-permute-done.1.first_ref), channel_id=1, source_target_pairs={{0,1},{1,0},{2,3},{3,2},{4,5},{5,4},{6,7},{7,6},{8,9},{9,8},{10,11... | collective-permute-start | bytes 1671176 | tf_op jit(solution)/shard_map/ppermute | solution.py:161
  57.5 6.7 %collective-permute-start.6 = (bf16[128,2048]{1,0:T(8,128)(2,1)S(1)}, bf16[128,2048]{1,0:T(8,128)(2,1)S(1)}, u32[]{:S(2)}, u32[]{:S(2)}) collective-permute-start(bf16[128,2048]{1,0:T(8,128)(2,1)S(1)} %get-tuple-element.18), channel_id=1, source_target_pairs={{0,1},{1,0},{2,3},{3,2},{4,5},{5,4},{6,7},{7,6},{8,9},{9,8},{10,11... | collective-permute-start | bytes 1572872 | tf_op jit(solution)/shard_map/ppermute | solution.py:162
  59.3 9.2 %collective-permute-start.14 = (bf16[128,2048]{1,0:T(8,128)(2,1)S(1)}, bf16[128,2048]{1,0:T(8,128)(2,1)S(1)}, u32[]{:S(2)}, u32[]{:S(2)}) collective-permute-start(bf16[128,2048]{1,0:T(8,128)(2,1)S(1)} %add_convert_fusion.2), channel_id=1, source_target_pairs={{0,4},{1,3},{4,8},{5,1},{8,12},{9,5},{12,14},{13,9},{14,10},{15,13... | collective-permute-start | bytes 1572872 | tf_op jit(solution)/shard_map/ppermute | solution.py:170
  61.4 19.0 %copy-start.3 = (bf16[1,2048,768]{2,1,0:T(8,128)(2,1)S(1)}, bf16[1,2048,768]{2,1,0:T(8,128)(2,1)}, u32[]{:S(2)}) copy-start(bf16[1,2048,768]{2,1,0:T(8,128)(2,1)} %up_ref.9) | copy-start | bytes 9437188
  64.1 16.3 %copy-start.1 = (bf16[1,2048,768]{2,1,0:T(8,128)(2,1)S(1)}, bf16[1,2048,768]{2,1,0:T(8,128)(2,1)}, u32[]{:S(2)}) copy-start(bf16[1,2048,768]{2,1,0:T(8,128)(2,1)} %gate_ref.9) | copy-start | bytes 9437188
  64.1 6.8 %collective-permute-start.3 = (bf16[128,2048]{1,0:T(8,128)(2,1)S(1)}, bf16[128,2048]{1,0:T(8,128)(2,1)S(1)}, u32[]{:S(2)}, u32[]{:S(2)}) collective-permute-start(bf16[128,2048]{1,0:T(8,128)(2,1)S(1)} %get-tuple-element.16), channel_id=1, source_target_pairs={{0,1},{1,0},{2,3},{3,2},{4,5},{5,4},{6,7},{7,6},{8,9},{9,8},{10,11... | collective-permute-start | bytes 1572872 | tf_op jit(solution)/shard_map/ppermute | solution.py:162
  68.7 9.2 %collective-permute-start.15 = (bf16[128,2048]{1,0:T(8,128)(2,1)S(1)}, bf16[128,2048]{1,0:T(8,128)(2,1)S(1)}, u32[]{:S(2)}, u32[]{:S(2)}) collective-permute-start(bf16[128,2048]{1,0:T(8,128)(2,1)S(1)} %add_convert_fusion.1), channel_id=1, source_target_pairs={{0,4},{1,3},{4,8},{5,1},{8,12},{9,5},{12,14},{13,9},{14,10},{15,13... | collective-permute-start | bytes 1572872 | tf_op jit(solution)/shard_map/ppermute | solution.py:170
  78.2 9.2 %collective-permute-start.16 = (bf16[128,2048]{1,0:T(8,128)(2,1)S(1)}, bf16[128,2048]{1,0:T(8,128)(2,1)S(1)}, u32[]{:S(2)}, u32[]{:S(2)}) collective-permute-start(bf16[128,2048]{1,0:T(8,128)(2,1)S(1)} %add_convert_fusion), channel_id=1, source_target_pairs={{0,4},{1,3},{4,8},{5,1},{8,12},{9,5},{12,14},{13,9},{14,10},{15,13... | collective-permute-start | bytes 1572872 | tf_op jit(solution)/shard_map/ppermute | solution.py:170
  87.5 1.6 %collective-permute-start.17 = (bf16[64,2048]{1,0:T(8,128)(2,1)S(1)}, bf16[64,2048]{1,0:T(8,128)(2,1)S(1)}, u32[]{:S(2)}, u32[]{:S(2)}) collective-permute-start(bf16[64,2048]{1,0:T(8,128)(2,1)S(1)} %add_convert_fusion.4), channel_id=1, source_target_pairs={{0,1},{1,0},{2,3},{3,2},{4,5},{5,4},{6,7},{7,6},{8,9},{9,8},{10,11... | collective-permute-start | bytes 786440 | tf_op jit(solution)/shard_map/ppermute | solution.py:171

commit v3 on v2

--- a/solution.py
+++ b/solution.py
@@ -75,17 +75,8 @@
     return pairs
 
 
-def expert_kernel(width, experts, own_ref, first_ref, second_ref, gate_ref, up_ref, down_ref,
-                  first_out, second_out, rows_ref, hidden_ref):
-    half = first_ref.shape[0]
-    ff = gate_ref.shape[2]
-    rows_ref[:half, :] = first_ref[...]
-    rows_ref[half:, :] = second_ref[...]
-    tail = rows_ref[:, width:].astype(jnp.float32)
-    lane = lax.broadcasted_iota(jnp.int32, tail.shape, 1)
-    own = own_ref[0]
-    mine = (lane == own) | (lane == own + experts)
-    weight = jnp.sum(jnp.where(mine, tail, 0.0), axis=1, keepdims=True)
+def hidden_units(rows_ref, hidden_ref, gate_ref, up_ref):
+    width, ff = gate_ref.shape[1:]
     step = math.gcd(ff, 256)
     for at in range(0, ff, step):
         part = slice(at, at + step)
@@ -93,6 +84,16 @@
         gate = jnp.dot(rows, gate_ref[0, :, part], preferred_element_type=jnp.float32)
         up = jnp.dot(rows, up_ref[0, :, part], preferred_element_type=jnp.float32)
         hidden_ref[:, part] = (gate / (1.0 + jnp.exp(-gate)) * up).astype(jnp.bfloat16)
+
+
+def weighted_out(experts, own_ref, rows_ref, hidden_ref, down_ref, outs):
+    width = down_ref.shape[1]
+    each = outs[0].shape[0]
+    tail = rows_ref[:, width:].astype(jnp.float32)
+    lane = lax.broadcasted_iota(jnp.int32, tail.shape, 1)
+    own = own_ref[0]
+    mine = (lane == own) | (lane == own + experts)
+    weight = jnp.sum(jnp.where(mine, tail, 0.0), axis=1, keepdims=True)
     step = math.gcd(width, 512)
     for at in range(0, width, step):
         part = slice(at, at + step)
@@ -101,29 +102,77 @@
             preferred_element_type=jnp.float32,
         )
         out = (out * weight).astype(jnp.bfloat16)
-        first_out[:, part] = out[:half]
-        second_out[:, part] = out[half:]
-
-
-def run_expert(own, first, second, gate_w, up_w, down_w, experts):
-    half, wide = first.shape
-    width, ff = gate_w.shape[1:]
+        for number, target in enumerate(outs):
+            target[:, part] = out[number * each : (number + 1) * each]
+
+
+def fill(rows_ref, blocks):
+    at = 0
+    for block in blocks:
+        rows_ref[at : at + block.shape[0], :] = block[...]
+        at += block.shape[0]
+
+
+def expert_kernel(experts, blocks, own_ref, *refs):
+    gate_ref, up_ref, down_ref = refs[blocks : blocks + 3]
+    outs = refs[blocks + 3 : 2 * blocks + 3]
+    rows_ref, hidden_ref = refs[2 * blocks + 3 :]
+    fill(rows_ref, refs[:blocks])
+    hidden_units(rows_ref, hidden_ref, gate_ref, up_ref)
+    weighted_out(experts, own_ref, rows_ref, hidden_ref, down_ref, outs)
+
+
+def first_kernel(experts, blocks, pieces, own_ref, *refs):
+    sources = refs[blocks : blocks + 3]
+    outs = refs[blocks + 3 : 2 * blocks + 3]
+    gate_ref, up_ref, down_ref, rows_ref, hidden_ref, done = refs[2 * blocks + 3 :]
+    copies = []
+    for number, (source, target) in enumerate(zip(sources, (gate_ref, up_ref, down_ref))):
+        depth = source.shape[1] // pieces
+        for piece in range(pieces):
+            part = pl.ds(piece * depth, depth)
+            copy = pltpu.make_async_copy(
+                source.at[:, part], target.at[:, part], done.at[number * pieces + piece]
+            )
+            copy.start()
+            copies.append(copy)
+    fill(rows_ref, refs[:blocks])
+    for copy in copies[: 2 * pieces]:
+        copy.wait()
+    hidden_units(rows_ref, hidden_ref, gate_ref, up_ref)
+    for copy in copies[2 * pieces :]:
+        copy.wait()
+    weighted_out(experts, own_ref, rows_ref, hidden_ref, down_ref, outs)
+
+
+def run_expert(own, blocks, weights, experts, load):
+    rows = sum(block.shape[0] for block in blocks)
+    wide = blocks[0].shape[1]
+    width, ff = weights[0].shape[1:]
     vmem = pl.BlockSpec(memory_space=pltpu.VMEM)
+    pieces = 4
+    out_shape = [jax.ShapeDtypeStruct((block.shape[0], width), jnp.bfloat16) for block in blocks]
+    scratch = [pltpu.VMEM((rows, wide), jnp.bfloat16), pltpu.VMEM((rows, ff), jnp.bfloat16)]
+    if load:
+        kernel = functools.partial(first_kernel, experts, len(blocks), pieces)
+        out_shape += [pltpu.VMEM(w.shape, w.dtype) for w in weights]
+        scratch.append(pltpu.SemaphoreType.DMA((3 * pieces,)))
+        place = pl.BlockSpec(memory_space=pltpu.HBM)
+    else:
+        kernel = functools.partial(expert_kernel, experts, len(blocks))
+        place = vmem
     return pl.pallas_call(
-        functools.partial(expert_kernel, width, experts),
-        out_shape=[jax.ShapeDtypeStruct((half, width), jnp.bfloat16)] * 2,
-        in_specs=[pl.BlockSpec(memory_space=pltpu.SMEM)] + [vmem] * 5,
-        out_specs=[vmem] * 2,
-        scratch_shapes=[
-            pltpu.VMEM((2 * half, wide), jnp.bfloat16),
-            pltpu.VMEM((2 * half, ff), jnp.bfloat16),
-        ],
+        kernel,
+        out_shape=out_shape,
+        in_specs=[pl.BlockSpec(memory_space=pltpu.SMEM)] + [vmem] * len(blocks) + [place] * 3,
+        out_specs=[vmem] * len(out_shape),
+        scratch_shapes=scratch,
         compiler_params=pltpu.CompilerParams(vmem_limit_bytes=30 << 20),
         cost_estimate=pl.CostEstimate(
-            flops=2 * 2 * half * 3 * width * ff, bytes_accessed=8 * half * width,
-            transcendentals=2 * half * ff,
+            flops=2 * rows * 3 * width * ff, bytes_accessed=4 * rows * width,
+            transcendentals=rows * ff,
         ),
-    )(own, first, second, gate_w, up_w, down_w)
+    )(own, *blocks, *weights)
 
 
 def added(*terms):
@@ -131,6 +180,10 @@
     for term in terms[1:]:
         total = total + term.astype(jnp.float32)
     return total.astype(jnp.bfloat16)
+
+
+def after(value, *others):
+    return lax.optimization_barrier((value, *others))[0]
 
 
 def dense_body(tokens, expert_ids, router_weights, w_gate, w_up, w_down):
@@ -149,27 +202,36 @@
     empty = jnp.zeros((count, 128 - 2 * experts), jnp.bfloat16)
     mine = jnp.concatenate([tokens, high, low, empty], 1)
 
-    weights = [pltpu.with_memory_space_constraint(w, pltpu.VMEM) for w in (w_gate, w_up, w_down)]
-    run = lambda first, second: run_expert(own, first, second, *weights, experts)
-
     sibling = swap(mine)
-    held = jnp.concatenate([mine, sibling], 0)
-    kept, other = run(mine, sibling)
-    pairs = []
-    for step in range(1, rounds + 1):
-        held = ring(held if step < rounds else held[:count])
-        first, second = run(held, swap(held))
-        pairs.append((second, swap(first)))
-    moving = None
-    for second, first in reversed(pairs):
-        terms = added(second, first) if moving is None else None
-        if moving is not None:
-            if moving.shape[0] < second.shape[0]:
-                moving = jnp.pad(moving, ((0, second.shape[0] - moving.shape[0]), (0, 0)))
-            terms = added(second, first, moving)
-        moving = ring(terms)
-    last = swap(added(moving[:count], other))
-    return added(moving[count:], kept, last)
+    first, second = ring(mine), ring(sibling)
+    weights = [pltpu.with_memory_space_constraint(w, pltpu.HBM) for w in (w_gate, w_up, w_down)]
+    kept, other, *weights = run_expert(own, [mine, sibling], weights, experts, True)
+    done = [kept]
+    turned = []
+    for step in range(1, rounds):
+        blocks = [swap(first), swap(second), first, second]
+        if turned:
+            blocks[0] = after(blocks[0], *turned[-1])
+        first = ring(first)
+        if step < rounds - 1:
+            second = ring(after(second, *done))
+        keep, keep_trail, send, send_trail = run_expert(own, blocks, weights, experts, False)
+        done = [keep]
+        send, send_trail = swap(send), swap(send_trail)
+        turned.append((keep, keep_trail, send, send_trail))
+    keep, keep_trail, send, send_trail = turned[-1]
+    trail = added(keep_trail, send_trail)
+    first = after(first, turned[-2][0])
+    blocks = [after(swap(first), trail), first]
+    trail = ring(trail)
+    keep, send = run_expert(own, blocks, weights, experts, False)
+    lead = ring(added(keep, swap(send)))
+    for step, (keep, keep_trail, send, send_trail) in enumerate(reversed(turned)):
+        if step > 0:
+            trail = ring(added(keep_trail, send_trail, trail))
+        lead = ring(after(added(keep, send, lead), trail))
+    last = swap(added(lead, other))
+    return added(trail, kept, last)
 
 
 def solution(mesh):

time: 90.2 us -> 82.6 us (0.916)
  waiting for transfers between devices: 48.4 us -> 33.5 us
  starting transfers between devices: 20 us -> 30.2 us
  local copies, waits for them, and re-layouts: 6.93 us -> 1.23 us
  Pallas kernels: 12 us -> 15.1 us
    ppermute x17 -> x29, waiting for transfers between devices: 47.2 us -> 33.5 us  [the longest x3 9.33 us: dense_body(): lead = ring(after(added(keep, send, lead), trail))]
    ppermute x17 -> x29, starting transfers between devices: 19.5 us -> 29.7 us  [the longest x3 6.32 us: dense_body(): lead = ring(after(added(keep, send, lead), trail))]
    unnamed x10 -> x0, local copies, waits for them, and re-layouts: 5.68 us -> none
    pallas_call x5, Pallas kernels: 12 us -> 15.1 us  [run_expert(): pl.pallas_call(kernel, out_shape=out_shape, in_specs=[pl.BlockSpec(memory...]
    ppermute x1, waiting for transfers between devices: 1.19 us -> 0.01 us  [dense_body(): sibling = swap(mine)]
  transfers between devices with their start and end apart: 18 -> 30, of which waited for: 11 -> 18; matrix products, arithmetic and copies ran while one was open for 1% -> 1% of each run, Pallas kernels for 13% -> 16%
where the time goes in v3:
time: 82.6 us; the launch traced here: 82.4 us
  waiting for transfers between devices  33.5 us (41%)
  starting transfers between devices  30.2 us (37%)
  Pallas kernels  15.1 us (18%)
  other arithmetic  2.22 us (3%)
  local copies, waits for them, and re-layouts  1.23 us (1%)
    pallas_call x5, Pallas kernels, run_expert(): pl.pallas_call(kernel, out_shape=out_shape, in_specs=[pl.BlockSpec(memory...  15.1 us
    ppermute x3, waiting for transfers between devices, dense_body(): lead = ring(after(added(keep, send, lead), trail))  9.33 us
    ppermute x3, starting transfers between devices, dense_body(): lead = ring(after(added(keep, send, lead), trail))  6.32 us
    ppermute x3, starting transfers between devices, dense_body(): first = ring(first)  5.65 us
    ppermute x2, waiting for transfers between devices, dense_body(): trail = ring(added(keep_trail, send_trail, trail))  5.41 us
    ppermute x2, starting transfers between devices, dense_body(): second = ring(after(second, *done))  4.27 us
    ppermute x2, starting transfers between devices, dense_body(): first, second = (ring(mine), ring(sibling))  4.21 us
    ppermute x2, waiting for transfers between devices, dense_body(): first, second = (ring(mine), ring(sibling))  3.74 us
  transfers between devices with their start and end apart: 30, of which 18 were waited for; matrix products, arithmetic and copies ran while one was open for 1% of the time, Pallas kernels for 16%

profile of v3, /device:TPU:0, one launch (start us, length us, event | category | flops | bytes accessed | tf_op | source)
XLA Modules:
  0.0 82.4 jit_solution(6686341771733084245)
XLA Ops:
  0.0 0.7 select_reduce_fusion
  0.7 0.1 copy.12
  0.8 0.1 copy.13
  0.9 1.0 %concatenate.3.refs_0_ = bf16[64,2176]{1,0:T(8,128)(2,1)S(1)} concatenate(bf16[64,2048]{1,0:T(8,128)(2,1)} %param.6, bf16[64,16]{1,0:T(8,128)(2,1)S(1)} %copy.13, bf16[64,16]{1,0:T(8,128)(2,1)S(1)} %subtract_convert_fusion, bf16[64,96]{1,0:T(8,128)(2,1)S(1)} %broadcast_in_dim.20), dimensions={1} | concatenate | bytes 557056 | tf_op jit(solution)/shard_map/concatenate | solution.py:203
  2.0 0.5 collective-permute-start.2
  2.5 2.6 %collective-permute-start = (bf16[64,2176]{1,0:T(8,128)(2,1)S(1)}, bf16[64,2176]{1,0:T(8,128)(2,1)S(1)}, u32[]{:S(2)}, u32[]{:S(2)}) collective-permute-start(bf16[64,2176]{1,0:T(8,128)(2,1)S(1)} %concatenate.3.refs_0_), channel_id=1, source_target_pairs={{0,4},{1,3},{4,8},{5,1},{8,12},{9,5},{12,14},{13,9},{14,10},{15,13... | collective-permute-start | bytes 835592 | tf_op jit(solution)/shard_map/ppermute | solution.py:206
  5.1 1.6 %collective-permute-start.3 = (bf16[64,2176]{1,0:T(8,128)(2,1)S(1)}, bf16[64,2176]{1,0:T(8,128)(2,1)S(1)}, u32[]{:S(2)}, u32[]{:S(2)}) collective-permute-start(bf16[64,2176]{1,0:T(8,128)(2,1)S(1)} %collective-permute-done.2.refs_1_), channel_id=1, source_target_pairs={{0,4},{1,3},{4,8},{5,1},{8,12},{9,5},{12,14},{13,9},{14,10},{15,13... | collective-permute-start | bytes 835592 | tf_op jit(solution)/shard_map/ppermute | solution.py:206
  6.7 2.9 %collective-permute-done.refs_2_ = bf16[64,2176]{1,0:T(8,128)(2,1)S(1)} collective-permute-done((bf16[64,2176]{1,0:T(8,128)(2,1)S(1)}, bf16[64,2176]{1,0:T(8,128)(2,1)S(1)}, u32[]{:S(2)}, u32[]{:S(2)}) %collective-permute-start) | collective-permute-done | bytes 278560 | tf_op jit(solution)/shard_map/ppermute | solution.py:206
  9.6 2.1 %collective-permute-start.6 = (bf16[64,2176]{1,0:T(8,128)(2,1)S(1)}, bf16[64,2176]{1,0:T(8,128)(2,1)S(1)}, u32[]{:S(2)}, u32[]{:S(2)}) collective-permute-start(bf16[64,2176]{1,0:T(8,128)(2,1)S(1)} %collective-permute-done.refs_2_), channel_id=1, source_target_pairs={{0,4},{1,3},{4,8},{5,1},{8,12},{9,5},{12,14},{13,9},{14,10},{15,13... | collective-permute-start | bytes 835592 | tf_op jit(solution)/shard_map/ppermute | solution.py:215
  11.7 0.9 %collective-permute-done.3.refs_3_ = bf16[64,2176]{1,0:T(8,128)(2,1)S(1)} collective-permute-done((bf16[64,2176]{1,0:T(8,128)(2,1)S(1)}, bf16[64,2176]{1,0:T(8,128)(2,1)S(1)}, u32[]{:S(2)}, u32[]{:S(2)}) %collective-permute-start.3) | collective-permute-done | bytes 278560 | tf_op jit(solution)/shard_map/ppermute | solution.py:206
  12.6 5.1 %shard_map.64 = (bf16[64,2048]{1,0:T(8,128)(2,1)S(1)}, bf16[64,2048]{1,0:T(8,128)(2,1)S(1)}, bf16[1,2048,768]{2,1,0:T(8,128)(2,1)S(1)}, bf16[1,2048,768]{2,1,0:T(8,128)(2,1)S(1)}, bf16[1,2048,768]{2,1,0:T(8,128)(2,1)S(1)}) custom-call(s32[1]{0:T(128)} %bitcast.own_ref, bf16[64,2176]{1,0:T(8,128)(2,1)S(1)} %concatenate.3.refs_0_, ...), custom_call_target="tpu_custom_call" | custom-call | flops 1207959552 | bytes 1048576 | tf_op jit(solution)/shard_map/pallas_call | solution.py:164
  17.7 2.2 %collective-permute-start.9 = (bf16[64,2176]{1,0:T(8,128)(2,1)S(1)}, bf16[64,2176]{1,0:T(8,128)(2,1)S(1)}, u32[]{:S(2)}, u32[]{:S(2)}) collective-permute-start(bf16[64,2176]{1,0:T(8,128)(2,1)S(1)} %collective-permute-done.3.refs_3_), channel_id=1, source_target_pairs={{0,4},{1,3},{4,8},{5,1},{8,12},{9,5},{12,14},{13,9},{14,10},{15,13... | collective-permute-start | bytes 835592 | tf_op jit(solution)/shard_map/ppermute | solution.py:217
  19.8 0.0 collective-permute-done.6.refs_2_
  19.8 0.1 collective-permute-start.7
  20.0 1.4 %collective-permute-start.12 = (bf16[64,2176]{1,0:T(8,128)(2,1)S(1)}, bf16[64,2176]{1,0:T(8,128)(2,1)S(1)}, u32[]{:S(2)}, u32[]{:S(2)}) collective-permute-start(bf16[64,2176]{1,0:T(8,128)(2,1)S(1)} %collective-permute-done.6.refs_2_), channel_id=1, source_target_pairs={{0,4},{1,3},{4,8},{5,1},{8,12},{9,5},{12,14},{13,9},{14,10},{15,13... | collective-permute-start | bytes 835592 | tf_op jit(solution)/shard_map/ppermute | solution.py:215
  21.4 2.7 %shard_map.65 = (bf16[64,2048]{1,0:T(8,128)(2,1)S(1)}, bf16[64,2048]{1,0:T(8,128)(2,1)S(1)}, bf16[64,2048]{1,0:T(8,128)(2,1)S(1)}, bf16[64,2048]{1,0:T(8,128)(2,1)S(1)}) custom-call(s32[1]{0:T(128)} %bitcast.own_ref, bf16[64,2176]{1,0:T(8,128)(2,1)S(1)} %collective-permute-done.1.refs_0_, bf16[64,2176]{1,0:T(8,128)(2,1)S(1)} %collective-permute-done.4.refs_1_, ...), custom_call_target="tpu_custom_call" | custom-call | flops 2415919104 | bytes 2097152 | tf_op jit(solution)/shard_map/pallas_call | solution.py:164
  24.1 0.2 collective-permute-done.9.refs_3_
  24.3 2.1 %collective-permute-start.15 = (bf16[64,2176]{1,0:T(8,128)(2,1)S(1)}, bf16[64,2176]{1,0:T(8,128)(2,1)S(1)}, u32[]{:S(2)}, u32[]{:S(2)}) collective-permute-start(bf16[64,2176]{1,0:T(8,128)(2,1)S(1)} %collective-permute-done.9.refs_3_), channel_id=1, source_target_pairs={{0,4},{1,3},{4,8},{5,1},{8,12},{9,5},{12,14},{13,9},{14,10},{15,13... | collective-permute-start | bytes 835592 | tf_op jit(solution)/shard_map/ppermute | solution.py:217
  26.4 0.0 collective-permute-start.10
  26.4 0.5 collective-permute-start.5
  26.9 0.0 collective-permute-done.7.refs_0_
  26.9 0.0 collective-permute-start.8
  26.9 0.4 collective-permute-done.12.refs_2_
  27.3 0.2 collective-permute-start.13
  27.4 0.9 %collective-permute-done.5 = bf16[64,2048]{1,0:T(8,128)(2,1)S(1)} collective-permute-done((bf16[64,2048]{1,0:T(8,128)(2,1)S(1)}, bf16[64,2048]{1,0:T(8,128)(2,1)S(1)}, u32[]{:S(2)}, u32[]{:S(2)}) %collective-permute-start.5) | collective-permute-done | bytes 262176 | tf_op jit(solution)/shard_map/ppermute | solution.py:220
  28.3 0.4 collective-permute-done.8
  28.7 2.1 %collective-permute-done.15.refs_3_ = bf16[64,2176]{1,0:T(8,128)(2,1)S(1)} collective-permute-done((bf16[64,2176]{1,0:T(8,128)(2,1)S(1)}, bf16[64,2176]{1,0:T(8,128)(2,1)S(1)}, u32[]{:S(2)}, u32[]{:S(2)}) %collective-permute-start.15) | collective-permute-done | bytes 278560 | tf_op jit(solution)/shard_map/ppermute | solution.py:217
  30.8 2.7 %shard_map.66 = (bf16[64,2048]{1,0:T(8,128)(2,1)S(1)}, bf16[64,2048]{1,0:T(8,128)(2,1)S(1)}, bf16[64,2048]{1,0:T(8,128)(2,1)S(1)}, bf16[64,2048]{1,0:T(8,128)(2,1)S(1)}) custom-call(s32[1]{0:T(128)} %bitcast.own_ref, bf16[64,2176]{1,0:T(8,128)(2,1)S(1)} %collective-permute-done.7.refs_0_, bf16[64,2176]{1,0:T(8,128)(2,1)S(1)} %collective-permute-done.10.refs_1_, ...), custom_call_target="tpu_custom_call" | custom-call | flops 2415919104 | bytes 2097152 | tf_op jit(solution)/shard_map/pallas_call | solution.py:164
  33.5 0.6 collective-permute-start.11
  34.1 0.1 collective-permute-start.14
  34.1 2.1 %collective-permute-start.22 = (bf16[64,2176]{1,0:T(8,128)(2,1)S(1)}, bf16[64,2176]{1,0:T(8,128)(2,1)S(1)}, u32[]{:S(2)}, u32[]{:S(2)}) collective-permute-start(bf16[64,2176]{1,0:T(8,128)(2,1)S(1)} %collective-permute-done.12.refs_2_), channel_id=1, source_target_pairs={{0,4},{1,3},{4,8},{5,1},{8,12},{9,5},{12,14},{13,9},{14,10},{15,13... | collective-permute-start | bytes 835592 | tf_op jit(solution)/shard_map/ppermute | solution.py:215
  36.3 2.7 %shard_map.67 = (bf16[64,2048]{1,0:T(8,128)(2,1)S(1)}, bf16[64,2048]{1,0:T(8,128)(2,1)S(1)}, bf16[64,2048]{1,0:T(8,128)(2,1)S(1)}, bf16[64,2048]{1,0:T(8,128)(2,1)S(1)}) custom-call(s32[1]{0:T(128)} %bitcast.own_ref, bf16[64,2176]{1,0:T(8,128)(2,1)S(1)} %collective-permute-done.13.refs_0_, bf16[64,2176]{1,0:T(8,128)(2,1)S(1)} %collective-permute-done.16.refs_1_, ...), custom_call_target="tpu_custom_call" | custom-call | flops 2415919104 | bytes 2097152 | tf_op jit(solution)/shard_map/pallas_call | solution.py:164
  38.9 0.1 collective-permute-start.17
  39.1 1.6 %collective-permute-done.22.refs_1_ = bf16[64,2176]{1,0:T(8,128)(2,1)S(1)} collective-permute-done((bf16[64,2176]{1,0:T(8,128)(2,1)S(1)}, bf16[64,2176]{1,0:T(8,128)(2,1)S(1)}, u32[]{:S(2)}, u32[]{:S(2)}) %collective-permute-start.22) | collective-permute-done | bytes 278560 | tf_op jit(solution)/shard_map/ppermute | solution.py:215
  40.7 0.1 add_convert_fusion.8
  40.8 1.5 %collective-permute-done.23.refs_0_ = bf16[64,2176]{1,0:T(8,128)(2,1)S(1)} collective-permute-done((bf16[64,2176]{1,0:T(8,128)(2,1)S(1)}, bf16[64,2176]{1,0:T(8,128)(2,1)S(1)}, u32[]{:S(2)}, u32[]{:S(2)}) %collective-permute-start.23) | collective-permute-done | bytes 278560 | tf_op jit(solution)/shard_map/ppermute | solution.py:225
  42.3 2.0 %shard_map.68 = (bf16[64,2048]{1,0:T(8,128)(2,1)S(1)}, bf16[64,2048]{1,0:T(8,128)(2,1)S(1)}) custom-call(s32[1]{0:T(128)} %bitcast.own_ref, bf16[64,2176]{1,0:T(8,128)(2,1)S(1)} %collective-permute-done.23.refs_0_, bf16[64,2176]{1,0:T(8,128)(2,1)S(1)} %collective-permute-done.22.refs_1_, bf16[1,2048,768]{2,1,0:T(8,128)(2,1)S(1)} %get-tuple-element.33.refs_4_.refs_2_, ...), custom_call_target="tpu_custom_call" | custom-call | flops 1207959552 | bytes 1048576 | tf_op jit(solution)/shard_map/pallas_call | solution.py:164
  44.3 0.2 collective-permute-start.24
  44.5 0.4 collective-permute-start.21
  44.9 1.0 %collective-permute-done.24 = bf16[64,2048]{1,0:T(8,128)(2,1)S(1)} collective-permute-done((bf16[64,2048]{1,0:T(8,128)(2,1)S(1)}, bf16[64,2048]{1,0:T(8,128)(2,1)S(1)}, u32[]{:S(2)}, u32[]{:S(2)}) %collective-permute-start.24) | collective-permute-done | bytes 262176 | tf_op jit(solution)/shard_map/ppermute | solution.py:228
  45.9 0.1 add_convert_fusion.5
  46.0 2.2 %collective-permute-start.25 = (bf16[64,2048]{1,0:T(8,128)(2,1)S(1)}, bf16[64,2048]{1,0:T(8,128)(2,1)S(1)}, u32[]{:S(2)}, u32[]{:S(2)}) collective-permute-start(bf16[64,2048]{1,0:T(8,128)(2,1)S(1)} %add_convert_fusion.5), channel_id=1, source_target_pairs={{0,4},{1,3},{4,8},{5,1},{8,12},{9,5},{12,14},{13,9},{14,10},{15,13... | collective-permute-start | bytes 786440 | tf_op jit(solution)/shard_map/ppermute | solution.py:228
  48.1 1.6 %collective-permute-start.18 = (bf16[64,2048]{1,0:T(8,128)(2,1)S(1)}, bf16[64,2048]{1,0:T(8,128)(2,1)S(1)}, u32[]{:S(2)}, u32[]{:S(2)}) collective-permute-start(bf16[64,2048]{1,0:T(8,128)(2,1)S(1)} %add_convert_fusion.8), channel_id=1, source_target_pairs={{0,4},{1,3},{4,8},{5,1},{8,12},{9,5},{12,14},{13,9},{14,10},{15,13... | collective-permute-start | bytes 786440 | tf_op jit(solution)/shard_map/ppermute | solution.py:226
  49.7 2.7 %collective-permute-done.25 = bf16[64,2048]{1,0:T(8,128)(2,1)S(1)} collective-permute-done((bf16[64,2048]{1,0:T(8,128)(2,1)S(1)}, bf16[64,2048]{1,0:T(8,128)(2,1)S(1)}, u32[]{:S(2)}, u32[]{:S(2)}) %collective-permute-start.25) | collective-permute-done | bytes 262176 | tf_op jit(solution)/shard_map/ppermute | solution.py:228
  52.4 0.1 add_convert_fusion.4
  52.5 2.7 %collective-permute-done.18 = bf16[64,2048]{1,0:T(8,128)(2,1)S(1)} collective-permute-done((bf16[64,2048]{1,0:T(8,128)(2,1)S(1)}, bf16[64,2048]{1,0:T(8,128)(2,1)S(1)}, u32[]{:S(2)}, u32[]{:S(2)}) %collective-permute-start.18) | collective-permute-done | bytes 262176 | tf_op jit(solution)/shard_map/ppermute | solution.py:226
  55.2 2.1 %collective-permute-start.26 = (bf16[64,2048]{1,0:T(8,128)(2,1)S(1)}, bf16[64,2048]{1,0:T(8,128)(2,1)S(1)}, u32[]{:S(2)}, u32[]{:S(2)}) collective-permute-start(bf16[64,2048]{1,0:T(8,128)(2,1)S(1)} %add_convert_fusion.4), channel_id=1, source_target_pairs={{0,4},{1,3},{4,8},{5,1},{8,12},{9,5},{12,14},{13,9},{14,10},{15,13... | collective-permute-start | bytes 786440 | tf_op jit(solution)/shard_map/ppermute | solution.py:232
  57.3 0.1 add_convert_fusion.7
  57.4 1.6 %collective-permute-start.19 = (bf16[64,2048]{1,0:T(8,128)(2,1)S(1)}, bf16[64,2048]{1,0:T(8,128)(2,1)S(1)}, u32[]{:S(2)}, u32[]{:S(2)}) collective-permute-start(bf16[64,2048]{1,0:T(8,128)(2,1)S(1)} %add_convert_fusion.7), channel_id=1, source_target_pairs={{0,4},{1,3},{4,8},{5,1},{8,12},{9,5},{12,14},{13,9},{14,10},{15,13... | collective-permute-start | bytes 786440 | tf_op jit(solution)/shard_map/ppermute | solution.py:231
  59.0 2.5 %collective-permute-done.26 = bf16[64,2048]{1,0:T(8,128)(2,1)S(1)} collective-permute-done((bf16[64,2048]{1,0:T(8,128)(2,1)S(1)}, bf16[64,2048]{1,0:T(8,128)(2,1)S(1)}, u32[]{:S(2)}, u32[]{:S(2)}) %collective-permute-start.26) | collective-permute-done | bytes 262176 | tf_op jit(solution)/shard_map/ppermute | solution.py:232
  61.6 0.1 add_convert_fusion.3
  61.7 2.7 %collective-permute-done.19 = bf16[64,2048]{1,0:T(8,128)(2,1)S(1)} collective-permute-done((bf16[64,2048]{1,0:T(8,128)(2,1)S(1)}, bf16[64,2048]{1,0:T(8,128)(2,1)S(1)}, u32[]{:S(2)}, u32[]{:S(2)}) %collective-permute-start.19) | collective-permute-done | bytes 262176 | tf_op jit(solution)/shard_map/ppermute | solution.py:231
  64.4 2.1 %collective-permute-start.27 = (bf16[64,2048]{1,0:T(8,128)(2,1)S(1)}, bf16[64,2048]{1,0:T(8,128)(2,1)S(1)}, u32[]{:S(2)}, u32[]{:S(2)}) collective-permute-start(bf16[64,2048]{1,0:T(8,128)(2,1)S(1)} %add_convert_fusion.3), channel_id=1, source_target_pairs={{0,4},{1,3},{4,8},{5,1},{8,12},{9,5},{12,14},{13,9},{14,10},{15,13... | collective-permute-start | bytes 786440 | tf_op jit(solution)/shard_map/ppermute | solution.py:232
  66.5 0.1 add_convert_fusion.6
  66.6 1.6 %collective-permute-start.20 = (bf16[64,2048]{1,0:T(8,128)(2,1)S(1)}, bf16[64,2048]{1,0:T(8,128)(2,1)S(1)}, u32[]{:S(2)}, u32[]{:S(2)}) collective-permute-start(bf16[64,2048]{1,0:T(8,128)(2,1)S(1)} %add_convert_fusion.6), channel_id=1, source_target_pairs={{0,4},{1,3},{4,8},{5,1},{8,12},{9,5},{12,14},{13,9},{14,10},{15,13... | collective-permute-start | bytes 786440 | tf_op jit(solution)/shard_map/ppermute | solution.py:231
  68.2 2.5 %collective-permute-done.27 = bf16[64,2048]{1,0:T(8,128)(2,1)S(1)} collective-permute-done((bf16[64,2048]{1,0:T(8,128)(2,1)S(1)}, bf16[64,2048]{1,0:T(8,128)(2,1)S(1)}, u32[]{:S(2)}, u32[]{:S(2)}) %collective-permute-start.27) | collective-permute-done | bytes 262176 | tf_op jit(solution)/shard_map/ppermute | solution.py:232
  70.8 0.1 add_convert_fusion.2
  70.9 2.7 %collective-permute-done.20 = bf16[64,2048]{1,0:T(8,128)(2,1)S(1)} collective-permute-done((bf16[64,2048]{1,0:T(8,128)(2,1)S(1)}, bf16[64,2048]{1,0:T(8,128)(2,1)S(1)}, u32[]{:S(2)}, u32[]{:S(2)}) %collective-permute-start.20) | collective-permute-done | bytes 262176 | tf_op jit(solution)/shard_map/ppermute | solution.py:231
  73.6 2.1 %collective-permute-start.28 = (bf16[64,2048]{1,0:T(8,128)(2,1)S(1)}, bf16[64,2048]{1,0:T(8,128)(2,1)S(1)}, u32[]{:S(2)}, u32[]{:S(2)}) collective-permute-start(bf16[64,2048]{1,0:T(8,128)(2,1)S(1)} %add_convert_fusion.2), channel_id=1, source_target_pairs={{0,4},{1,3},{4,8},{5,1},{8,12},{9,5},{12,14},{13,9},{14,10},{15,13... | collective-permute-start | bytes 786440 | tf_op jit(solution)/shard_map/ppermute | solution.py:232
  75.7 4.3 %collective-permute-done.28 = bf16[64,2048]{1,0:T(8,128)(2,1)S(1)} collective-permute-done((bf16[64,2048]{1,0:T(8,128)(2,1)S(1)}, bf16[64,2048]{1,0:T(8,128)(2,1)S(1)}, u32[]{:S(2)}, u32[]{:S(2)}) %collective-permute-start.28) | collective-permute-done | bytes 262176 | tf_op jit(solution)/shard_map/ppermute | solution.py:232
  79.9 0.1 add_convert_fusion.1
  80.0 0.1 collective-permute-start.29
  80.1 1.5 %collective-permute-done.29 = bf16[64,2048]{1,0:T(8,128)(2,1)S(1)} collective-permute-done((bf16[64,2048]{1,0:T(8,128)(2,1)S(1)}, bf16[64,2048]{1,0:T(8,128)(2,1)S(1)}, u32[]{:S(2)}, u32[]{:S(2)}) %collective-permute-start.29) | collective-permute-done | bytes 262176 | tf_op jit(solution)/shard_map/ppermute | solution.py:233
  81.6 0.8 add_convert_fusion
  (17 shorter events, 0.1 us)
Async XLA Ops:
  2.0 3.2 %collective-permute-start.2 = (bf16[64,2176]{1,0:T(8,128)(2,1)S(1)}, bf16[64,2176]{1,0:T(8,128)(2,1)S(1)}, u32[]{:S(2)}, u32[]{:S(2)}) collective-permute-start(bf16[64,2176]{1,0:T(8,128)(2,1)S(1)} %concatenate.3.refs_0_), channel_id=1, source_target_pairs={{0,1},{1,0},{2,3},{3,2},{4,5},{5,4},{6,7},{7,6},{8,9},{9,8},{10,11... | collective-permute-start | bytes 835592 | tf_op jit(solution)/shard_map/ppermute | solution.py:205
  2.5 7.1 %collective-permute-start = (bf16[64,2176]{1,0:T(8,128)(2,1)S(1)}, bf16[64,2176]{1,0:T(8,128)(2,1)S(1)}, u32[]{:S(2)}, u32[]{:S(2)}) collective-permute-start(bf16[64,2176]{1,0:T(8,128)(2,1)S(1)} %concatenate.3.refs_0_), channel_id=1, source_target_pairs={{0,4},{1,3},{4,8},{5,1},{8,12},{9,5},{12,14},{13,9},{14,10},{15,13... | collective-permute-start | bytes 835592 | tf_op jit(solution)/shard_map/ppermute | solution.py:206
  5.1 7.4 %collective-permute-start.3 = (bf16[64,2176]{1,0:T(8,128)(2,1)S(1)}, bf16[64,2176]{1,0:T(8,128)(2,1)S(1)}, u32[]{:S(2)}, u32[]{:S(2)}) collective-permute-start(bf16[64,2176]{1,0:T(8,128)(2,1)S(1)} %collective-permute-done.2.refs_1_), channel_id=1, source_target_pairs={{0,4},{1,3},{4,8},{5,1},{8,12},{9,5},{12,14},{13,9},{14,10},{15,13... | collective-permute-start | bytes 835592 | tf_op jit(solution)/shard_map/ppermute | solution.py:206
  9.6 10.3 %collective-permute-start.6 = (bf16[64,2176]{1,0:T(8,128)(2,1)S(1)}, bf16[64,2176]{1,0:T(8,128)(2,1)S(1)}, u32[]{:S(2)}, u32[]{:S(2)}) collective-permute-start(bf16[64,2176]{1,0:T(8,128)(2,1)S(1)} %collective-permute-done.refs_2_), channel_id=1, source_target_pairs={{0,4},{1,3},{4,8},{5,1},{8,12},{9,5},{12,14},{13,9},{14,10},{15,13... | collective-permute-start | bytes 835592 | tf_op jit(solution)/shard_map/ppermute | solution.py:215
  11.7 9.7 %collective-permute-start.1 = (bf16[64,2176]{1,0:T(8,128)(2,1)S(1)}, bf16[64,2176]{1,0:T(8,128)(2,1)S(1)}, u32[]{:S(2)}, u32[]{:S(2)}) collective-permute-start(bf16[64,2176]{1,0:T(8,128)(2,1)S(1)} %collective-permute-done.refs_2_), channel_id=1, source_target_pairs={{0,1},{1,0},{2,3},{3,2},{4,5},{5,4},{6,7},{7,6},{8,9},{9,8},{10,11... | collective-permute-start | bytes 835592 | tf_op jit(solution)/shard_map/ppermute | solution.py:212
  12.6 8.9 %collective-permute-start.4 = (bf16[64,2176]{1,0:T(8,128)(2,1)S(1)}, bf16[64,2176]{1,0:T(8,128)(2,1)S(1)}, u32[]{:S(2)}, u32[]{:S(2)}) collective-permute-start(bf16[64,2176]{1,0:T(8,128)(2,1)S(1)} %collective-permute-done.3.refs_3_), channel_id=1, source_target_pairs={{0,1},{1,0},{2,3},{3,2},{4,5},{5,4},{6,7},{7,6},{8,9},{9,8},{10,11... | collective-permute-start | bytes 835592 | tf_op jit(solution)/shard_map/ppermute | solution.py:212
  17.7 6.6 %collective-permute-start.9 = (bf16[64,2176]{1,0:T(8,128)(2,1)S(1)}, bf16[64,2176]{1,0:T(8,128)(2,1)S(1)}, u32[]{:S(2)}, u32[]{:S(2)}) collective-permute-start(bf16[64,2176]{1,0:T(8,128)(2,1)S(1)} %collective-permute-done.3.refs_3_), channel_id=1, source_target_pairs={{0,4},{1,3},{4,8},{5,1},{8,12},{9,5},{12,14},{13,9},{14,10},{15,13... | collective-permute-start | bytes 835592 | tf_op jit(solution)/shard_map/ppermute | solution.py:217
  19.8 7.1 %collective-permute-start.7 = (bf16[64,2176]{1,0:T(8,128)(2,1)S(1)}, bf16[64,2176]{1,0:T(8,128)(2,1)S(1)}, u32[]{:S(2)}, u32[]{:S(2)}) collective-permute-start(bf16[64,2176]{1,0:T(8,128)(2,1)S(1)} %collective-permute-done.6.refs_2_), channel_id=1, source_target_pairs={{0,1},{1,0},{2,3},{3,2},{4,5},{5,4},{6,7},{7,6},{8,9},{9,8},{10,11... | collective-permute-start | bytes 835592 | tf_op jit(solution)/shard_map/ppermute | solution.py:212
  20.0 7.3 %collective-permute-start.12 = (bf16[64,2176]{1,0:T(8,128)(2,1)S(1)}, bf16[64,2176]{1,0:T(8,128)(2,1)S(1)}, u32[]{:S(2)}, u32[]{:S(2)}) collective-permute-start(bf16[64,2176]{1,0:T(8,128)(2,1)S(1)} %collective-permute-done.6.refs_2_), channel_id=1, source_target_pairs={{0,4},{1,3},{4,8},{5,1},{8,12},{9,5},{12,14},{13,9},{14,10},{15,13... | collective-permute-start | bytes 835592 | tf_op jit(solution)/shard_map/ppermute | solution.py:215
  24.3 6.5 %collective-permute-start.15 = (bf16[64,2176]{1,0:T(8,128)(2,1)S(1)}, bf16[64,2176]{1,0:T(8,128)(2,1)S(1)}, u32[]{:S(2)}, u32[]{:S(2)}) collective-permute-start(bf16[64,2176]{1,0:T(8,128)(2,1)S(1)} %collective-permute-done.9.refs_3_), channel_id=1, source_target_pairs={{0,4},{1,3},{4,8},{5,1},{8,12},{9,5},{12,14},{13,9},{14,10},{15,13... | collective-permute-start | bytes 835592 | tf_op jit(solution)/shard_map/ppermute | solution.py:217
  26.4 4.4 %collective-permute-start.10 = (bf16[64,2176]{1,0:T(8,128)(2,1)S(1)}, bf16[64,2176]{1,0:T(8,128)(2,1)S(1)}, u32[]{:S(2)}, u32[]{:S(2)}) collective-permute-start(bf16[64,2176]{1,0:T(8,128)(2,1)S(1)} %collective-permute-done.9.refs_3_), channel_id=1, source_target_pairs={{0,1},{1,0},{2,3},{3,2},{4,5},{5,4},{6,7},{7,6},{8,9},{9,8},{10,11... | collective-permute-start | bytes 835592 | tf_op jit(solution)/shard_map/ppermute | solution.py:212
  26.4 1.9 %collective-permute-start.5 = (bf16[64,2048]{1,0:T(8,128)(2,1)S(1)}, bf16[64,2048]{1,0:T(8,128)(2,1)S(1)}, u32[]{:S(2)}, u32[]{:S(2)}) collective-permute-start(bf16[64,2048]{1,0:T(8,128)(2,1)S(1)} %get-tuple-element.37), channel_id=1, source_target_pairs={{0,1},{1,0},{2,3},{3,2},{4,5},{5,4},{6,7},{7,6},{8,9},{9,8},{10,11... | collective-permute-start | bytes 786440 | tf_op jit(solution)/shard_map/ppermute | solution.py:220
  26.9 1.8 %collective-permute-start.8 = (bf16[64,2048]{1,0:T(8,128)(2,1)S(1)}, bf16[64,2048]{1,0:T(8,128)(2,1)S(1)}, u32[]{:S(2)}, u32[]{:S(2)}) collective-permute-start(bf16[64,2048]{1,0:T(8,128)(2,1)S(1)} %get-tuple-element.39), channel_id=1, source_target_pairs={{0,1},{1,0},{2,3},{3,2},{4,5},{5,4},{6,7},{7,6},{8,9},{9,8},{10,11... | collective-permute-start | bytes 786440 | tf_op jit(solution)/shard_map/ppermute | solution.py:220
  27.3 9.0 %collective-permute-start.13 = (bf16[64,2176]{1,0:T(8,128)(2,1)S(1)}, bf16[64,2176]{1,0:T(8,128)(2,1)S(1)}, u32[]{:S(2)}, u32[]{:S(2)}) collective-permute-start(bf16[64,2176]{1,0:T(8,128)(2,1)S(1)} %collective-permute-done.12.refs_2_), channel_id=1, source_target_pairs={{0,1},{1,0},{2,3},{3,2},{4,5},{5,4},{6,7},{7,6},{8,9},{9,8},{10,11... | collective-permute-start | bytes 835592 | tf_op jit(solution)/shard_map/ppermute | solution.py:212
  30.8 5.4 %collective-permute-start.16 = (bf16[64,2176]{1,0:T(8,128)(2,1)S(1)}, bf16[64,2176]{1,0:T(8,128)(2,1)S(1)}, u32[]{:S(2)}, u32[]{:S(2)}) collective-permute-start(bf16[64,2176]{1,0:T(8,128)(2,1)S(1)} %collective-permute-done.15.refs_3_), channel_id=1, source_target_pairs={{0,1},{1,0},{2,3},{3,2},{4,5},{5,4},{6,7},{7,6},{8,9},{9,8},{10,11... | collective-permute-start | bytes 835592 | tf_op jit(solution)/shard_map/ppermute | solution.py:212
  33.5 2.8 %collective-permute-start.11 = (bf16[64,2048]{1,0:T(8,128)(2,1)S(1)}, bf16[64,2048]{1,0:T(8,128)(2,1)S(1)}, u32[]{:S(2)}, u32[]{:S(2)}) collective-permute-start(bf16[64,2048]{1,0:T(8,128)(2,1)S(1)} %get-tuple-element.44), channel_id=1, source_target_pairs={{0,1},{1,0},{2,3},{3,2},{4,5},{5,4},{6,7},{7,6},{8,9},{9,8},{10,11... | collective-permute-start | bytes 786440 | tf_op jit(solution)/shard_map/ppermute | solution.py:220
  34.1 2.2 %collective-permute-start.14 = (bf16[64,2048]{1,0:T(8,128)(2,1)S(1)}, bf16[64,2048]{1,0:T(8,128)(2,1)S(1)}, u32[]{:S(2)}, u32[]{:S(2)}) collective-permute-start(bf16[64,2048]{1,0:T(8,128)(2,1)S(1)} %get-tuple-element.46), channel_id=1, source_target_pairs={{0,1},{1,0},{2,3},{3,2},{4,5},{5,4},{6,7},{7,6},{8,9},{9,8},{10,11... | collective-permute-start | bytes 786440 | tf_op jit(solution)/shard_map/ppermute | solution.py:220
  34.1 6.5 %collective-permute-start.22 = (bf16[64,2176]{1,0:T(8,128)(2,1)S(1)}, bf16[64,2176]{1,0:T(8,128)(2,1)S(1)}, u32[]{:S(2)}, u32[]{:S(2)}) collective-permute-start(bf16[64,2176]{1,0:T(8,128)(2,1)S(1)} %collective-permute-done.12.refs_2_), channel_id=1, source_target_pairs={{0,4},{1,3},{4,8},{5,1},{8,12},{9,5},{12,14},{13,9},{14,10},{15,13... | collective-permute-start | bytes 835592 | tf_op jit(solution)/shard_map/ppermute | solution.py:215
  38.9 1.8 %collective-permute-start.17 = (bf16[64,2048]{1,0:T(8,128)(2,1)S(1)}, bf16[64,2048]{1,0:T(8,128)(2,1)S(1)}, u32[]{:S(2)}, u32[]{:S(2)}) collective-permute-start(bf16[64,2048]{1,0:T(8,128)(2,1)S(1)} %get-tuple-element.50), channel_id=1, source_target_pairs={{0,1},{1,0},{2,3},{3,2},{4,5},{5,4},{6,7},{7,6},{8,9},{9,8},{10,11... | collective-permute-start | bytes 786440 | tf_op jit(solution)/shard_map/ppermute | solution.py:220
  40.7 1.6 %collective-permute-start.23 = (bf16[64,2176]{1,0:T(8,128)(2,1)S(1)}, bf16[64,2176]{1,0:T(8,128)(2,1)S(1)}, u32[]{:S(2)}, u32[]{:S(2)}) collective-permute-start(bf16[64,2176]{1,0:T(8,128)(2,1)S(1)} %collective-permute-done.22.refs_1_), channel_id=1, source_target_pairs={{0,1},{1,0},{2,3},{3,2},{4,5},{5,4},{6,7},{7,6},{8,9},{9,8},{10,11... | collective-permute-start | bytes 835592 | tf_op jit(solution)/shard_map/ppermute | solution.py:225
  44.3 1.6 %collective-permute-start.24 = (bf16[64,2048]{1,0:T(8,128)(2,1)S(1)}, bf16[64,2048]{1,0:T(8,128)(2,1)S(1)}, u32[]{:S(2)}, u32[]{:S(2)}) collective-permute-start(bf16[64,2048]{1,0:T(8,128)(2,1)S(1)} %get-tuple-element.56), channel_id=1, source_target_pairs={{0,1},{1,0},{2,3},{3,2},{4,5},{5,4},{6,7},{7,6},{8,9},{9,8},{10,11... | collective-permute-start | bytes 786440 | tf_op jit(solution)/shard_map/ppermute | solution.py:228
  44.5 5.2 %collective-permute-start.21 = (bf16[64,2048]{1,0:T(8,128)(2,1)S(1)}, bf16[64,2048]{1,0:T(8,128)(2,1)S(1)}, u32[]{:S(2)}, u32[]{:S(2)}) collective-permute-start(bf16[64,2048]{1,0:T(8,128)(2,1)S(1)} %get-tuple-element.52), channel_id=1, source_target_pairs={{0,1},{1,0},{2,3},{3,2},{4,5},{5,4},{6,7},{7,6},{8,9},{9,8},{10,11... | collective-permute-start | bytes 786440 | tf_op jit(solution)/shard_map/ppermute | solution.py:220
  46.0 6.4 %collective-permute-start.25 = (bf16[64,2048]{1,0:T(8,128)(2,1)S(1)}, bf16[64,2048]{1,0:T(8,128)(2,1)S(1)}, u32[]{:S(2)}, u32[]{:S(2)}) collective-permute-start(bf16[64,2048]{1,0:T(8,128)(2,1)S(1)} %add_convert_fusion.5), channel_id=1, source_target_pairs={{0,4},{1,3},{4,8},{5,1},{8,12},{9,5},{12,14},{13,9},{14,10},{15,13... | collective-permute-start | bytes 786440 | tf_op jit(solution)/shard_map/ppermute | solution.py:228
  48.1 7.1 %collective-permute-start.18 = (bf16[64,2048]{1,0:T(8,128)(2,1)S(1)}, bf16[64,2048]{1,0:T(8,128)(2,1)S(1)}, u32[]{:S(2)}, u32[]{:S(2)}) collective-permute-start(bf16[64,2048]{1,0:T(8,128)(2,1)S(1)} %add_convert_fusion.8), channel_id=1, source_target_pairs={{0,4},{1,3},{4,8},{5,1},{8,12},{9,5},{12,14},{13,9},{14,10},{15,13... | collective-permute-start | bytes 786440 | tf_op jit(solution)/shard_map/ppermute | solution.py:226
  55.2 6.4 %collective-permute-start.26 = (bf16[64,2048]{1,0:T(8,128)(2,1)S(1)}, bf16[64,2048]{1,0:T(8,128)(2,1)S(1)}, u32[]{:S(2)}, u32[]{:S(2)}) collective-permute-start(bf16[64,2048]{1,0:T(8,128)(2,1)S(1)} %add_convert_fusion.4), channel_id=1, source_target_pairs={{0,4},{1,3},{4,8},{5,1},{8,12},{9,5},{12,14},{13,9},{14,10},{15,13... | collective-permute-start | bytes 786440 | tf_op jit(solution)/shard_map/ppermute | solution.py:232
  57.4 7.0 %collective-permute-start.19 = (bf16[64,2048]{1,0:T(8,128)(2,1)S(1)}, bf16[64,2048]{1,0:T(8,128)(2,1)S(1)}, u32[]{:S(2)}, u32[]{:S(2)}) collective-permute-start(bf16[64,2048]{1,0:T(8,128)(2,1)S(1)} %add_convert_fusion.7), channel_id=1, source_target_pairs={{0,4},{1,3},{4,8},{5,1},{8,12},{9,5},{12,14},{13,9},{14,10},{15,13... | collective-permute-start | bytes 786440 | tf_op jit(solution)/shard_map/ppermute | solution.py:231
  64.4 6.4 %collective-permute-start.27 = (bf16[64,2048]{1,0:T(8,128)(2,1)S(1)}, bf16[64,2048]{1,0:T(8,128)(2,1)S(1)}, u32[]{:S(2)}, u32[]{:S(2)}) collective-permute-start(bf16[64,2048]{1,0:T(8,128)(2,1)S(1)} %add_convert_fusion.3), channel_id=1, source_target_pairs={{0,4},{1,3},{4,8},{5,1},{8,12},{9,5},{12,14},{13,9},{14,10},{15,13... | collective-permute-start | bytes 786440 | tf_op jit(solution)/shard_map/ppermute | solution.py:232
  66.6 7.0 %collective-permute-start.20 = (bf16[64,2048]{1,0:T(8,128)(2,1)S(1)}, bf16[64,2048]{1,0:T(8,128)(2,1)S(1)}, u32[]{:S(2)}, u32[]{:S(2)}) collective-permute-start(bf16[64,2048]{1,0:T(8,128)(2,1)S(1)} %add_convert_fusion.6), channel_id=1, source_target_pairs={{0,4},{1,3},{4,8},{5,1},{8,12},{9,5},{12,14},{13,9},{14,10},{15,13... | collective-permute-start | bytes 786440 | tf_op jit(solution)/shard_map/ppermute | solution.py:231
  73.6 6.4 %collective-permute-start.28 = (bf16[64,2048]{1,0:T(8,128)(2,1)S(1)}, bf16[64,2048]{1,0:T(8,128)(2,1)S(1)}, u32[]{:S(2)}, u32[]{:S(2)}) collective-permute-start(bf16[64,2048]{1,0:T(8,128)(2,1)S(1)} %add_convert_fusion.2), channel_id=1, source_target_pairs={{0,4},{1,3},{4,8},{5,1},{8,12},{9,5},{12,14},{13,9},{14,10},{15,13... | collective-permute-start | bytes 786440 | tf_op jit(solution)/shard_map/ppermute | solution.py:232
  80.0 1.6 %collective-permute-start.29 = (bf16[64,2048]{1,0:T(8,128)(2,1)S(1)}, bf16[64,2048]{1,0:T(8,128)(2,1)S(1)}, u32[]{:S(2)}, u32[]{:S(2)}) collective-permute-start(bf16[64,2048]{1,0:T(8,128)(2,1)S(1)} %add_convert_fusion.1), channel_id=1, source_target_pairs={{0,1},{1,0},{2,3},{3,2},{4,5},{5,4},{6,7},{7,6},{8,9},{9,8},{10,11... | collective-permute-start | bytes 786440 | tf_op jit(solution)/shard_map/ppermute | solution.py:233

commit v4 on v3

--- a/solution.py
+++ b/solution.py
@@ -75,10 +75,11 @@
     return pairs
 
 
-def hidden_units(rows_ref, hidden_ref, gate_ref, up_ref):
+def hidden_units(rows_ref, hidden_ref, gate_ref, up_ref, ready=lambda tile: None):
     width, ff = gate_ref.shape[1:]
     step = math.gcd(ff, 256)
     for at in range(0, ff, step):
+        ready(at // step)
         part = slice(at, at + step)
         rows = rows_ref[:, :width]
         gate = jnp.dot(rows, gate_ref[0, :, part], preferred_element_type=jnp.float32)
@@ -122,26 +123,32 @@
     weighted_out(experts, own_ref, rows_ref, hidden_ref, down_ref, outs)
 
 
-def first_kernel(experts, blocks, pieces, own_ref, *refs):
+def first_kernel(experts, blocks, own_ref, *refs):
     sources = refs[blocks : blocks + 3]
     outs = refs[blocks + 3 : 2 * blocks + 3]
     gate_ref, up_ref, down_ref, rows_ref, hidden_ref, done = refs[2 * blocks + 3 :]
+    step = math.gcd(gate_ref.shape[2], 256)
+    tiles = gate_ref.shape[2] // step
     copies = []
-    for number, (source, target) in enumerate(zip(sources, (gate_ref, up_ref, down_ref))):
-        depth = source.shape[1] // pieces
-        for piece in range(pieces):
-            part = pl.ds(piece * depth, depth)
-            copy = pltpu.make_async_copy(
-                source.at[:, part], target.at[:, part], done.at[number * pieces + piece]
+    for tile in range(tiles):
+        part = pl.ds(tile * step, step)
+        for source, target in ((sources[0], gate_ref), (sources[1], up_ref)):
+            copies.append(
+                pltpu.make_async_copy(
+                    source.at[:, :, part], target.at[:, :, part], done.at[len(copies)]
+                )
             )
-            copy.start()
-            copies.append(copy)
+    copies.append(pltpu.make_async_copy(sources[2], down_ref, done.at[len(copies)]))
+    for copy in copies:
+        copy.start()
     fill(rows_ref, refs[:blocks])
-    for copy in copies[: 2 * pieces]:
-        copy.wait()
-    hidden_units(rows_ref, hidden_ref, gate_ref, up_ref)
-    for copy in copies[2 * pieces :]:
-        copy.wait()
+
+    def ready(tile):
+        copies[2 * tile].wait()
+        copies[2 * tile + 1].wait()
+
+    hidden_units(rows_ref, hidden_ref, gate_ref, up_ref, ready)
+    copies[-1].wait()
     weighted_out(experts, own_ref, rows_ref, hidden_ref, down_ref, outs)
 
 
@@ -150,13 +157,12 @@
     wide = blocks[0].shape[1]
     width, ff = weights[0].shape[1:]
     vmem = pl.BlockSpec(memory_space=pltpu.VMEM)
-    pieces = 4
     out_shape = [jax.ShapeDtypeStruct((block.shape[0], width), jnp.bfloat16) for block in blocks]
     scratch = [pltpu.VMEM((rows, wide), jnp.bfloat16), pltpu.VMEM((rows, ff), jnp.bfloat16)]
     if load:
-        kernel = functools.partial(first_kernel, experts, len(blocks), pieces)
+        kernel = functools.partial(first_kernel, experts, len(blocks))
         out_shape += [pltpu.VMEM(w.shape, w.dtype) for w in weights]
-        scratch.append(pltpu.SemaphoreType.DMA((3 * pieces,)))
+        scratch.append(pltpu.SemaphoreType.DMA((2 * (ff // math.gcd(ff, 256)) + 1,)))
         place = pl.BlockSpec(memory_space=pltpu.HBM)
     else:
         kernel = functools.partial(expert_kernel, experts, len(blocks))
@@ -169,8 +175,7 @@
         scratch_shapes=scratch,
         compiler_params=pltpu.CompilerParams(vmem_limit_bytes=30 << 20),
         cost_estimate=pl.CostEstimate(
-            flops=2 * rows * 3 * width * ff, bytes_accessed=4 * rows * width,
-            transcendentals=rows * ff,
+            flops=rows * width, bytes_accessed=rows * width, transcendentals=0
         ),
     )(own, *blocks, *weights)
 
@@ -205,31 +210,35 @@
     sibling = swap(mine)
     first, second = ring(mine), ring(sibling)
     weights = [pltpu.with_memory_space_constraint(w, pltpu.HBM) for w in (w_gate, w_up, w_down)]
-    kept, other, *weights = run_expert(own, [mine, sibling], weights, experts, True)
-    done = [kept]
+    run = lambda blocks: run_expert(own, blocks, weights, experts, False)
     turned = []
     for step in range(1, rounds):
         blocks = [swap(first), swap(second), first, second]
+        first = ring(first)
+        if step < rounds - 1:
+            second = ring(second)
+        blocks[0] = after(blocks[0], first)
         if turned:
             blocks[0] = after(blocks[0], *turned[-1])
-        first = ring(first)
-        if step < rounds - 1:
-            second = ring(after(second, *done))
-        keep, keep_trail, send, send_trail = run_expert(own, blocks, weights, experts, False)
-        done = [keep]
-        send, send_trail = swap(send), swap(send_trail)
-        turned.append((keep, keep_trail, send, send_trail))
+        if step == 1:
+            *sums, gate_w, up_w, down_w = run_expert(own, blocks, weights, experts, True)
+            weights = [gate_w, up_w, down_w]
+        else:
+            sums = run(blocks)
+        keep, keep_trail, send, send_trail = sums
+        turned.append((keep, keep_trail, swap(send), swap(send_trail)))
     keep, keep_trail, send, send_trail = turned[-1]
-    trail = added(keep_trail, send_trail)
+    trail = ring(added(keep_trail, send_trail))
     first = after(first, turned[-2][0])
-    blocks = [after(swap(first), trail), first]
-    trail = ring(trail)
-    keep, send = run_expert(own, blocks, weights, experts, False)
+    keep, send = run([after(swap(first), turned[-1][0]), first])
+    kept, other = run([mine, sibling])
     lead = ring(added(keep, swap(send)))
     for step, (keep, keep_trail, send, send_trail) in enumerate(reversed(turned)):
         if step > 0:
             trail = ring(added(keep_trail, send_trail, trail))
-        lead = ring(after(added(keep, send, lead), trail))
+        if step == 1:
+            kept, other, trail = lax.optimization_barrier((kept, other, trail))
+        lead = ring(added(keep, send, lead))
     last = swap(added(lead, other))
     return added(trail, kept, last)
 

time: 82.6 us -> 74.1 us (0.90)
  waiting for transfers between devices: 33.5 us -> 25 us
    ppermute x13, waiting for transfers between devices: 17.1 us -> 11.9 us  [the longest x3 7.77 us: dense_body(): lead = ring(added(keep, send, lead))]
    ppermute x2, waiting for transfers between devices: 5.41 us -> 2.66 us  [dense_body(): trail = ring(added(keep_trail, send_trail, trail))]
    ppermute x1, waiting for transfers between devices: 1.52 us -> 0.01 us  [dense_body(): last = swap(added(lead, other))]
    ppermute x13, starting transfers between devices: 13.8 us -> 12.7 us  [the longest x3 4.89 us: dense_body(): lead = ring(added(keep, send, lead))]
    ppermute x3, waiting for transfers between devices: 1.99 us -> 2.91 us  [dense_body(): first = ring(first)]
  transfers between devices with their start and end apart: 30 -> 30, of which waited for: 18 -> 16; matrix products, arithmetic and copies ran while one was open for 1% -> 1% of each run, Pallas kernels for 16% -> 18%
where the time goes in v4:
time: 74.1 us; the launch traced here: 73.9 us
  starting transfers between devices  30 us (40%)
  waiting for transfers between devices  25 us (34%)
  Pallas kernels  15.3 us (21%)
  other arithmetic  2.23 us (3%)
  local copies, waits for them, and re-layouts  1.23 us (2%)
    pallas_call x5, Pallas kernels, run_expert(): pl.pallas_call(kernel, out_shape=out_shape, in_specs=[pl.BlockSpec(memory...  15.3 us
    ppermute x3, waiting for transfers between devices, dense_body(): lead = ring(added(keep, send, lead))  7.77 us
    ppermute x3, starting transfers between devices, dense_body(): first = ring(first)  6.32 us
    ppermute x3, starting transfers between devices, dense_body(): lead = ring(added(keep, send, lead))  4.89 us
    ppermute x2, starting transfers between devices, dense_body(): first, second = (ring(mine), ring(sibling))  4.21 us
    ppermute x2, starting transfers between devices, dense_body(): second = ring(second)  4.21 us
    ppermute x2, waiting for transfers between devices, dense_body(): lead = ring(added(keep, swap(send)))  3.75 us
    ppermute x2, waiting for transfers between devices, dense_body(): first, second = (ring(mine), ring(sibling))  3.74 us
  transfers between devices with their start and end apart: 30, of which 16 were waited for; matrix products, arithmetic and copies ran while one was open for 1% of the time, Pallas kernels for 18%

profile of v4, /device:TPU:0, one launch (start us, length us, event | category | flops | bytes accessed | tf_op | source)
XLA Modules:
  0.0 73.9 jit_solution(1720677122269732907)
XLA Ops:
  0.0 0.7 select_reduce_fusion
  0.7 0.1 copy.12
  0.8 0.1 copy.13
  0.9 1.0 %concatenate.3.refs_0_ = bf16[64,2176]{1,0:T(8,128)(2,1)S(1)} concatenate(bf16[64,2048]{1,0:T(8,128)(2,1)} %param.6, bf16[64,16]{1,0:T(8,128)(2,1)S(1)} %copy.13, bf16[64,16]{1,0:T(8,128)(2,1)S(1)} %subtract_convert_fusion, bf16[64,96]{1,0:T(8,128)(2,1)S(1)} %broadcast_in_dim.20), dimensions={1} | concatenate | bytes 557056 | tf_op jit(solution)/shard_map/concatenate | solution.py:208
  2.0 0.5 collective-permute-start.3
  2.5 2.6 %collective-permute-start = (bf16[64,2176]{1,0:T(8,128)(2,1)S(1)}, bf16[64,2176]{1,0:T(8,128)(2,1)S(1)}, u32[]{:S(2)}, u32[]{:S(2)}) collective-permute-start(bf16[64,2176]{1,0:T(8,128)(2,1)S(1)} %concatenate.3.refs_0_), channel_id=1, source_target_pairs={{0,4},{1,3},{4,8},{5,1},{8,12},{9,5},{12,14},{13,9},{14,10},{15,13... | collective-permute-start | bytes 835592 | tf_op jit(solution)/shard_map/ppermute | solution.py:211
  5.1 0.0 collective-permute-done.3.refs_1_
  5.1 1.6 %collective-permute-start.4 = (bf16[64,2176]{1,0:T(8,128)(2,1)S(1)}, bf16[64,2176]{1,0:T(8,128)(2,1)S(1)}, u32[]{:S(2)}, u32[]{:S(2)}) collective-permute-start(bf16[64,2176]{1,0:T(8,128)(2,1)S(1)} %collective-permute-done.3.refs_1_), channel_id=1, source_target_pairs={{0,4},{1,3},{4,8},{5,1},{8,12},{9,5},{12,14},{13,9},{14,10},{15,13... | collective-permute-start | bytes 835592 | tf_op jit(solution)/shard_map/ppermute | solution.py:211
  6.7 2.9 %collective-permute-done.refs_2_ = bf16[64,2176]{1,0:T(8,128)(2,1)S(1)} collective-permute-done((bf16[64,2176]{1,0:T(8,128)(2,1)S(1)}, bf16[64,2176]{1,0:T(8,128)(2,1)S(1)}, u32[]{:S(2)}, u32[]{:S(2)}) %collective-permute-start) | collective-permute-done | bytes 278560 | tf_op jit(solution)/shard_map/ppermute | solution.py:211
  9.6 2.1 %collective-permute-start.2 = (bf16[64,2176]{1,0:T(8,128)(2,1)S(1)}, bf16[64,2176]{1,0:T(8,128)(2,1)S(1)}, u32[]{:S(2)}, u32[]{:S(2)}) collective-permute-start(bf16[64,2176]{1,0:T(8,128)(2,1)S(1)} %collective-permute-done.refs_2_), channel_id=1, source_target_pairs={{0,4},{1,3},{4,8},{5,1},{8,12},{9,5},{12,14},{13,9},{14,10},{15,13... | collective-permute-start | bytes 835592 | tf_op jit(solution)/shard_map/ppermute | solution.py:217
  11.7 0.9 %collective-permute-done.4.refs_3_ = bf16[64,2176]{1,0:T(8,128)(2,1)S(1)} collective-permute-done((bf16[64,2176]{1,0:T(8,128)(2,1)S(1)}, bf16[64,2176]{1,0:T(8,128)(2,1)S(1)}, u32[]{:S(2)}, u32[]{:S(2)}) %collective-permute-start.4) | collective-permute-done | bytes 278560 | tf_op jit(solution)/shard_map/ppermute | solution.py:211
  12.6 2.1 %collective-permute-start.10 = (bf16[64,2176]{1,0:T(8,128)(2,1)S(1)}, bf16[64,2176]{1,0:T(8,128)(2,1)S(1)}, u32[]{:S(2)}, u32[]{:S(2)}) collective-permute-start(bf16[64,2176]{1,0:T(8,128)(2,1)S(1)} %collective-permute-done.4.refs_3_), channel_id=1, source_target_pairs={{0,4},{1,3},{4,8},{5,1},{8,12},{9,5},{12,14},{13,9},{14,10},{15,13... | collective-permute-start | bytes 835592 | tf_op jit(solution)/shard_map/ppermute | solution.py:219
  14.7 1.5 %collective-permute-done.2.refs_2_ = bf16[64,2176]{1,0:T(8,128)(2,1)S(1)} collective-permute-done((bf16[64,2176]{1,0:T(8,128)(2,1)S(1)}, bf16[64,2176]{1,0:T(8,128)(2,1)S(1)}, u32[]{:S(2)}, u32[]{:S(2)}) %collective-permute-start.2) | collective-permute-done | bytes 278560 | tf_op jit(solution)/shard_map/ppermute | solution.py:217
  16.1 2.1 %collective-permute-start.8 = (bf16[64,2176]{1,0:T(8,128)(2,1)S(1)}, bf16[64,2176]{1,0:T(8,128)(2,1)S(1)}, u32[]{:S(2)}, u32[]{:S(2)}) collective-permute-start(bf16[64,2176]{1,0:T(8,128)(2,1)S(1)} %collective-permute-done.2.refs_2_), channel_id=1, source_target_pairs={{0,4},{1,3},{4,8},{5,1},{8,12},{9,5},{12,14},{13,9},{14,10},{15,13... | collective-permute-start | bytes 835592 | tf_op jit(solution)/shard_map/ppermute | solution.py:217
  18.2 0.0 collective-permute-start.5
  18.2 0.5 collective-permute-start.7
  18.8 0.4 collective-permute-done.10.refs_3_
  19.1 2.1 %collective-permute-start.16 = (bf16[64,2176]{1,0:T(8,128)(2,1)S(1)}, bf16[64,2176]{1,0:T(8,128)(2,1)S(1)}, u32[]{:S(2)}, u32[]{:S(2)}) collective-permute-start(bf16[64,2176]{1,0:T(8,128)(2,1)S(1)} %collective-permute-done.10.refs_3_), channel_id=1, source_target_pairs={{0,4},{1,3},{4,8},{5,1},{8,12},{9,5},{12,14},{13,9},{14,10},{15,13... | collective-permute-start | bytes 835592 | tf_op jit(solution)/shard_map/ppermute | solution.py:219
  21.2 1.5 %collective-permute-done.8.refs_2_ = bf16[64,2176]{1,0:T(8,128)(2,1)S(1)} collective-permute-done((bf16[64,2176]{1,0:T(8,128)(2,1)S(1)}, bf16[64,2176]{1,0:T(8,128)(2,1)S(1)}, u32[]{:S(2)}, u32[]{:S(2)}) %collective-permute-start.8) | collective-permute-done | bytes 278560 | tf_op jit(solution)/shard_map/ppermute | solution.py:217
  22.7 2.1 %collective-permute-start.14 = (bf16[64,2176]{1,0:T(8,128)(2,1)S(1)}, bf16[64,2176]{1,0:T(8,128)(2,1)S(1)}, u32[]{:S(2)}, u32[]{:S(2)}) collective-permute-start(bf16[64,2176]{1,0:T(8,128)(2,1)S(1)} %collective-permute-done.8.refs_2_), channel_id=1, source_target_pairs={{0,4},{1,3},{4,8},{5,1},{8,12},{9,5},{12,14},{13,9},{14,10},{15,13... | collective-permute-start | bytes 835592 | tf_op jit(solution)/shard_map/ppermute | solution.py:217
  24.8 0.0 collective-permute-done.5.refs_1_
  24.8 5.9 %shard_map.64 = (bf16[64,2048]{1,0:T(8,128)(2,1)S(1)}, bf16[64,2048]{1,0:T(8,128)(2,1)S(1)}, bf16[64,2048]{1,0:T(8,128)(2,1)S(1)}, bf16[64,2048]{1,0:T(8,128)(2,...) custom-call(s32[1]{0:T(128)} %bitcast.own_ref, ...), custom_call_target="tpu_custom_call" | custom-call | flops 524288 | bytes 524288 | tf_op jit(solution)/shard_map/pallas_call | solution.py:170
  30.7 0.1 collective-permute-start.9
  30.8 0.5 collective-permute-start.6
  31.3 1.0 %collective-permute-done.9 = bf16[64,2048]{1,0:T(8,128)(2,1)S(1)} collective-permute-done((bf16[64,2048]{1,0:T(8,128)(2,1)S(1)}, bf16[64,2048]{1,0:T(8,128)(2,1)S(1)}, u32[]{:S(2)}, u32[]{:S(2)}) %collective-permute-start.9) | collective-permute-done | bytes 262176 | tf_op jit(solution)/shard_map/ppermute | solution.py:229
  32.3 0.1 collective-permute-start.13
  32.5 0.2 collective-permute-done.6
  32.7 0.1 collective-permute-start.17
  32.9 2.7 %shard_map.66 = (bf16[64,2048]{1,0:T(8,128)(2,1)S(1)}, bf16[64,2048]{1,0:T(8,128)(2,1)S(1)}, bf16[64,2048]{1,0:T(8,128)(2,1)S(1)}, bf16[64,2048]{1,0:T(8,128)(2,1)S(1)}) custom-call(s32[1]{0:T(128)} %bitcast.own_ref, bf16[64,2176]{1,0:T(8,128)(2,1)S(1)} %collective-permute-done.7.refs_0_, bf16[64,2176]{1,0:T(8,128)(2,1)S(1)} %collective-permute-done.11.refs_1_, ...), custom_call_target="tpu_custom_call" | custom-call | flops 524288 | bytes 524288 | tf_op jit(solution)/shard_map/pallas_call | solution.py:170
  35.5 0.4 collective-permute-start.23
  36.0 0.1 collective-permute-start.15
  36.1 0.4 collective-permute-start.12
  36.5 1.0 %collective-permute-done.15 = bf16[64,2048]{1,0:T(8,128)(2,1)S(1)} collective-permute-done((bf16[64,2048]{1,0:T(8,128)(2,1)S(1)}, bf16[64,2048]{1,0:T(8,128)(2,1)S(1)}, u32[]{:S(2)}, u32[]{:S(2)}) %collective-permute-start.15) | collective-permute-done | bytes 262176 | tf_op jit(solution)/shard_map/ppermute | solution.py:229
  37.5 0.4 collective-permute-done.12
  37.9 2.7 %shard_map.67 = (bf16[64,2048]{1,0:T(8,128)(2,1)S(1)}, bf16[64,2048]{1,0:T(8,128)(2,1)S(1)}, bf16[64,2048]{1,0:T(8,128)(2,1)S(1)}, bf16[64,2048]{1,0:T(8,128)(2,1)S(1)}) custom-call(s32[1]{0:T(128)} %bitcast.own_ref, bf16[64,2176]{1,0:T(8,128)(2,1)S(1)} %collective-permute-done.13.refs_0_, bf16[64,2176]{1,0:T(8,128)(2,1)S(1)} %collective-permute-done.17.refs_1_, ...), custom_call_target="tpu_custom_call" | custom-call | flops 524288 | bytes 524288 | tf_op jit(solution)/shard_map/pallas_call | solution.py:170
  40.6 2.0 %shard_map.68 = (bf16[64,2048]{1,0:T(8,128)(2,1)S(1)}, bf16[64,2048]{1,0:T(8,128)(2,1)S(1)}) custom-call(s32[1]{0:T(128)} %bitcast.own_ref, bf16[64,2176]{1,0:T(8,128)(2,1)S(1)} %collective-permute-done.23.refs_0_, bf16[64,2176]{1,0:T(8,128)(2,1)S(1)} %collective-permute-done.14.refs_1_, bf16[1,2048,768]{2,1,0:T(8,128)(2,1)S(1)} %get-tuple-element.37.refs_2_.refs_4_, ...), custom_call_target="tpu_custom_call" | custom-call | flops 262144 | bytes 262144 | tf_op jit(solution)/shard_map/pallas_call | solution.py:170
  42.6 0.4 collective-permute-start.24
  43.1 0.1 collective-permute-start.18
  43.2 0.4 collective-permute-start.22
  43.6 0.7 collective-permute-done.24
  44.2 0.1 add_convert_fusion.5
  44.3 1.6 %collective-permute-start.25 = (bf16[64,2048]{1,0:T(8,128)(2,1)S(1)}, bf16[64,2048]{1,0:T(8,128)(2,1)S(1)}, u32[]{:S(2)}, u32[]{:S(2)}) collective-permute-start(bf16[64,2048]{1,0:T(8,128)(2,1)S(1)} %add_convert_fusion.5), channel_id=1, source_target_pairs={{0,4},{1,3},{4,8},{5,1},{8,12},{9,5},{12,14},{13,9},{14,10},{15,13... | collective-permute-start | bytes 786440 | tf_op jit(solution)/shard_map/ppermute | solution.py:235
  45.9 0.1 add_convert_fusion.8
  46.0 1.6 %collective-permute-start.19 = (bf16[64,2048]{1,0:T(8,128)(2,1)S(1)}, bf16[64,2048]{1,0:T(8,128)(2,1)S(1)}, u32[]{:S(2)}, u32[]{:S(2)}) collective-permute-start(bf16[64,2048]{1,0:T(8,128)(2,1)S(1)} %add_convert_fusion.8), channel_id=1, source_target_pairs={{0,4},{1,3},{4,8},{5,1},{8,12},{9,5},{12,14},{13,9},{14,10},{15,13... | collective-permute-start | bytes 786440 | tf_op jit(solution)/shard_map/ppermute | solution.py:231
  47.6 3.1 %collective-permute-done.25 = bf16[64,2048]{1,0:T(8,128)(2,1)S(1)} collective-permute-done((bf16[64,2048]{1,0:T(8,128)(2,1)S(1)}, bf16[64,2048]{1,0:T(8,128)(2,1)S(1)}, u32[]{:S(2)}, u32[]{:S(2)}) %collective-permute-start.25) | collective-permute-done | bytes 262176 | tf_op jit(solution)/shard_map/ppermute | solution.py:235
  50.7 0.1 add_convert_fusion.4
  50.8 1.6 %collective-permute-start.26 = (bf16[64,2048]{1,0:T(8,128)(2,1)S(1)}, bf16[64,2048]{1,0:T(8,128)(2,1)S(1)}, u32[]{:S(2)}, u32[]{:S(2)}) collective-permute-start(bf16[64,2048]{1,0:T(8,128)(2,1)S(1)} %add_convert_fusion.4), channel_id=1, source_target_pairs={{0,4},{1,3},{4,8},{5,1},{8,12},{9,5},{12,14},{13,9},{14,10},{15,13... | collective-permute-start | bytes 786440 | tf_op jit(solution)/shard_map/ppermute | solution.py:241
  52.5 1.1 %collective-permute-done.19 = bf16[64,2048]{1,0:T(8,128)(2,1)S(1)} collective-permute-done((bf16[64,2048]{1,0:T(8,128)(2,1)S(1)}, bf16[64,2048]{1,0:T(8,128)(2,1)S(1)}, u32[]{:S(2)}, u32[]{:S(2)}) %collective-permute-start.19) | collective-permute-done | bytes 262176 | tf_op jit(solution)/shard_map/ppermute | solution.py:231
  53.5 0.1 add_convert_fusion.7
  53.6 1.6 %collective-permute-start.20 = (bf16[64,2048]{1,0:T(8,128)(2,1)S(1)}, bf16[64,2048]{1,0:T(8,128)(2,1)S(1)}, u32[]{:S(2)}, u32[]{:S(2)}) collective-permute-start(bf16[64,2048]{1,0:T(8,128)(2,1)S(1)} %add_convert_fusion.7), channel_id=1, source_target_pairs={{0,4},{1,3},{4,8},{5,1},{8,12},{9,5},{12,14},{13,9},{14,10},{15,13... | collective-permute-start | bytes 786440 | tf_op jit(solution)/shard_map/ppermute | solution.py:238
  55.3 2.0 %collective-permute-done.26 = bf16[64,2048]{1,0:T(8,128)(2,1)S(1)} collective-permute-done((bf16[64,2048]{1,0:T(8,128)(2,1)S(1)}, bf16[64,2048]{1,0:T(8,128)(2,1)S(1)}, u32[]{:S(2)}, u32[]{:S(2)}) %collective-permute-start.26) | collective-permute-done | bytes 262176 | tf_op jit(solution)/shard_map/ppermute | solution.py:241
  57.3 0.1 add_convert_fusion.3
  57.4 1.6 %collective-permute-start.27 = (bf16[64,2048]{1,0:T(8,128)(2,1)S(1)}, bf16[64,2048]{1,0:T(8,128)(2,1)S(1)}, u32[]{:S(2)}, u32[]{:S(2)}) collective-permute-start(bf16[64,2048]{1,0:T(8,128)(2,1)S(1)} %add_convert_fusion.3), channel_id=1, source_target_pairs={{0,4},{1,3},{4,8},{5,1},{8,12},{9,5},{12,14},{13,9},{14,10},{15,13... | collective-permute-start | bytes 786440 | tf_op jit(solution)/shard_map/ppermute | solution.py:241
  59.0 2.0 %shard_map.65 = (bf16[64,2048]{1,0:T(8,128)(2,1)S(1)}, bf16[64,2048]{1,0:T(8,128)(2,1)S(1)}) custom-call(s32[1]{0:T(128)} %bitcast.own_ref, bf16[64,2176]{1,0:T(8,128)(2,1)S(1)} %concatenate.3.refs_0_, bf16[64,2176]{1,0:T(8,128)(2,1)S(1)} %collective-permute-done.3.refs_1_, bf16[1,2048,768]{2,1,0:T(8,128)(2,1)S(1)} %get-tuple-element.37.refs_2_.refs_4_, ...), custom_call_target="tpu_custom_call" | custom-call | flops 262144 | bytes 262144 | tf_op jit(solution)/shard_map/pallas_call | solution.py:170
  61.0 2.7 %collective-permute-done.27 = bf16[64,2048]{1,0:T(8,128)(2,1)S(1)} collective-permute-done((bf16[64,2048]{1,0:T(8,128)(2,1)S(1)}, bf16[64,2048]{1,0:T(8,128)(2,1)S(1)}, u32[]{:S(2)}, u32[]{:S(2)}) %collective-permute-start.27) | collective-permute-done | bytes 262176 | tf_op jit(solution)/shard_map/ppermute | solution.py:241
  63.8 0.1 add_convert_fusion.2
  63.9 1.6 %collective-permute-start.28 = (bf16[64,2048]{1,0:T(8,128)(2,1)S(1)}, bf16[64,2048]{1,0:T(8,128)(2,1)S(1)}, u32[]{:S(2)}, u32[]{:S(2)}) collective-permute-start(bf16[64,2048]{1,0:T(8,128)(2,1)S(1)} %add_convert_fusion.2), channel_id=1, source_target_pairs={{0,4},{1,3},{4,8},{5,1},{8,12},{9,5},{12,14},{13,9},{14,10},{15,13... | collective-permute-start | bytes 786440 | tf_op jit(solution)/shard_map/ppermute | solution.py:241
  65.5 0.1 add_convert_fusion.6
  65.6 1.6 %collective-permute-start.21 = (bf16[64,2048]{1,0:T(8,128)(2,1)S(1)}, bf16[64,2048]{1,0:T(8,128)(2,1)S(1)}, u32[]{:S(2)}, u32[]{:S(2)}) collective-permute-start(bf16[64,2048]{1,0:T(8,128)(2,1)S(1)} %add_convert_fusion.6), channel_id=1, source_target_pairs={{0,4},{1,3},{4,8},{5,1},{8,12},{9,5},{12,14},{13,9},{14,10},{15,13... | collective-permute-start | bytes 786440 | tf_op jit(solution)/shard_map/ppermute | solution.py:238
  67.2 3.1 %collective-permute-done.28 = bf16[64,2048]{1,0:T(8,128)(2,1)S(1)} collective-permute-done((bf16[64,2048]{1,0:T(8,128)(2,1)S(1)}, bf16[64,2048]{1,0:T(8,128)(2,1)S(1)}, u32[]{:S(2)}, u32[]{:S(2)}) %collective-permute-start.28) | collective-permute-done | bytes 262176 | tf_op jit(solution)/shard_map/ppermute | solution.py:241
  70.3 0.1 add_convert_fusion.1
  70.4 0.1 collective-permute-start.29
  70.5 2.7 %collective-permute-done.21 = bf16[64,2048]{1,0:T(8,128)(2,1)S(1)} collective-permute-done((bf16[64,2048]{1,0:T(8,128)(2,1)S(1)}, bf16[64,2048]{1,0:T(8,128)(2,1)S(1)}, u32[]{:S(2)}, u32[]{:S(2)}) %collective-permute-start.21) | collective-permute-done | bytes 262176 | tf_op jit(solution)/shard_map/ppermute | solution.py:238
  73.1 0.8 %add_convert_fusion = bf16[64,2048]{1,0:T(8,128)(2,1)} fusion(bf16[64,2048]{1,0:T(8,128)(2,1)S(1)} %collective-permute-done.29, bf16[64,2048]{1,0:T(8,128)(2,1)S(1)} %get-tuple-element.55, bf16[64,2048]{1,0:T(8,128)(2,1)S(1)} %collective-permute-done.21), kind=kLoop, calls=%fused_computation | loop fusion | flops 786432 | bytes 1048576 | tf_op jit(solution)/shard_map/convert_element_type | solution.py:187
  (17 shorter events, 0.1 us)
Async XLA Ops:
  2.0 3.2 %collective-permute-start.3 = (bf16[64,2176]{1,0:T(8,128)(2,1)S(1)}, bf16[64,2176]{1,0:T(8,128)(2,1)S(1)}, u32[]{:S(2)}, u32[]{:S(2)}) collective-permute-start(bf16[64,2176]{1,0:T(8,128)(2,1)S(1)} %concatenate.3.refs_0_), channel_id=1, source_target_pairs={{0,1},{1,0},{2,3},{3,2},{4,5},{5,4},{6,7},{7,6},{8,9},{9,8},{10,11... | collective-permute-start | bytes 835592 | tf_op jit(solution)/shard_map/ppermute | solution.py:210
  2.5 7.1 %collective-permute-start = (bf16[64,2176]{1,0:T(8,128)(2,1)S(1)}, bf16[64,2176]{1,0:T(8,128)(2,1)S(1)}, u32[]{:S(2)}, u32[]{:S(2)}) collective-permute-start(bf16[64,2176]{1,0:T(8,128)(2,1)S(1)} %concatenate.3.refs_0_), channel_id=1, source_target_pairs={{0,4},{1,3},{4,8},{5,1},{8,12},{9,5},{12,14},{13,9},{14,10},{15,13... | collective-permute-start | bytes 835592 | tf_op jit(solution)/shard_map/ppermute | solution.py:211
  5.1 7.4 %collective-permute-start.4 = (bf16[64,2176]{1,0:T(8,128)(2,1)S(1)}, bf16[64,2176]{1,0:T(8,128)(2,1)S(1)}, u32[]{:S(2)}, u32[]{:S(2)}) collective-permute-start(bf16[64,2176]{1,0:T(8,128)(2,1)S(1)} %collective-permute-done.3.refs_1_), channel_id=1, source_target_pairs={{0,4},{1,3},{4,8},{5,1},{8,12},{9,5},{12,14},{13,9},{14,10},{15,13... | collective-permute-start | bytes 835592 | tf_op jit(solution)/shard_map/ppermute | solution.py:211
  9.6 6.5 %collective-permute-start.2 = (bf16[64,2176]{1,0:T(8,128)(2,1)S(1)}, bf16[64,2176]{1,0:T(8,128)(2,1)S(1)}, u32[]{:S(2)}, u32[]{:S(2)}) collective-permute-start(bf16[64,2176]{1,0:T(8,128)(2,1)S(1)} %collective-permute-done.refs_2_), channel_id=1, source_target_pairs={{0,4},{1,3},{4,8},{5,1},{8,12},{9,5},{12,14},{13,9},{14,10},{15,13... | collective-permute-start | bytes 835592 | tf_op jit(solution)/shard_map/ppermute | solution.py:217
  12.6 6.5 %collective-permute-start.10 = (bf16[64,2176]{1,0:T(8,128)(2,1)S(1)}, bf16[64,2176]{1,0:T(8,128)(2,1)S(1)}, u32[]{:S(2)}, u32[]{:S(2)}) collective-permute-start(bf16[64,2176]{1,0:T(8,128)(2,1)S(1)} %collective-permute-done.4.refs_3_), channel_id=1, source_target_pairs={{0,4},{1,3},{4,8},{5,1},{8,12},{9,5},{12,14},{13,9},{14,10},{15,13... | collective-permute-start | bytes 835592 | tf_op jit(solution)/shard_map/ppermute | solution.py:219
  14.7 6.6 %collective-permute-start.1 = (bf16[64,2176]{1,0:T(8,128)(2,1)S(1)}, bf16[64,2176]{1,0:T(8,128)(2,1)S(1)}, u32[]{:S(2)}, u32[]{:S(2)}) collective-permute-start(bf16[64,2176]{1,0:T(8,128)(2,1)S(1)} %collective-permute-done.refs_2_), channel_id=1, source_target_pairs={{0,1},{1,0},{2,3},{3,2},{4,5},{5,4},{6,7},{7,6},{8,9},{9,8},{10,11... | collective-permute-start | bytes 835592 | tf_op jit(solution)/shard_map/ppermute | solution.py:216
  16.1 6.5 %collective-permute-start.8 = (bf16[64,2176]{1,0:T(8,128)(2,1)S(1)}, bf16[64,2176]{1,0:T(8,128)(2,1)S(1)}, u32[]{:S(2)}, u32[]{:S(2)}) collective-permute-start(bf16[64,2176]{1,0:T(8,128)(2,1)S(1)} %collective-permute-done.2.refs_2_), channel_id=1, source_target_pairs={{0,4},{1,3},{4,8},{5,1},{8,12},{9,5},{12,14},{13,9},{14,10},{15,13... | collective-permute-start | bytes 835592 | tf_op jit(solution)/shard_map/ppermute | solution.py:217
  18.2 6.6 %collective-permute-start.5 = (bf16[64,2176]{1,0:T(8,128)(2,1)S(1)}, bf16[64,2176]{1,0:T(8,128)(2,1)}, u32[]{:S(2)}, u32[]{:S(2)}) collective-permute-start(bf16[64,2176]{1,0:T(8,128)(2,1)S(1)} %collective-permute-done.4.refs_3_), channel_id=1, source_target_pairs={{0,1},{1,0},{2,3},{3,2},{4,5},{5,4},{6,7},{7,6},{8,9},{9,8},{10,11... | collective-permute-start | bytes 835592 | tf_op jit(solution)/shard_map/ppermute | solution.py:216
  18.2 12.6 %collective-permute-start.7 = (bf16[64,2176]{1,0:T(8,128)(2,1)S(1)}, bf16[64,2176]{1,0:T(8,128)(2,1)S(1)}, u32[]{:S(2)}, u32[]{:S(2)}) collective-permute-start(bf16[64,2176]{1,0:T(8,128)(2,1)S(1)} %collective-permute-done.2.refs_2_), channel_id=1, source_target_pairs={{0,1},{1,0},{2,3},{3,2},{4,5},{5,4},{6,7},{7,6},{8,9},{9,8},{10,11... | collective-permute-start | bytes 835592 | tf_op jit(solution)/shard_map/ppermute | solution.py:216
  19.1 13.6 %collective-permute-start.16 = (bf16[64,2176]{1,0:T(8,128)(2,1)S(1)}, bf16[64,2176]{1,0:T(8,128)(2,1)S(1)}, u32[]{:S(2)}, u32[]{:S(2)}) collective-permute-start(bf16[64,2176]{1,0:T(8,128)(2,1)S(1)} %collective-permute-done.10.refs_3_), channel_id=1, source_target_pairs={{0,4},{1,3},{4,8},{5,1},{8,12},{9,5},{12,14},{13,9},{14,10},{15,13... | collective-permute-start | bytes 835592 | tf_op jit(solution)/shard_map/ppermute | solution.py:219
  21.2 11.6 %collective-permute-start.11 = (bf16[64,2176]{1,0:T(8,128)(2,1)S(1)}, bf16[64,2176]{1,0:T(8,128)(2,1)S(1)}, u32[]{:S(2)}, u32[]{:S(2)}) collective-permute-start(bf16[64,2176]{1,0:T(8,128)(2,1)S(1)} %collective-permute-done.10.refs_3_), channel_id=1, source_target_pairs={{0,1},{1,0},{2,3},{3,2},{4,5},{5,4},{6,7},{7,6},{8,9},{9,8},{10,11... | collective-permute-start | bytes 835592 | tf_op jit(solution)/shard_map/ppermute | solution.py:216
  22.7 12.8 %collective-permute-start.14 = (bf16[64,2176]{1,0:T(8,128)(2,1)S(1)}, bf16[64,2176]{1,0:T(8,128)(2,1)S(1)}, u32[]{:S(2)}, u32[]{:S(2)}) collective-permute-start(bf16[64,2176]{1,0:T(8,128)(2,1)S(1)} %collective-permute-done.8.refs_2_), channel_id=1, source_target_pairs={{0,4},{1,3},{4,8},{5,1},{8,12},{9,5},{12,14},{13,9},{14,10},{15,13... | collective-permute-start | bytes 835592 | tf_op jit(solution)/shard_map/ppermute | solution.py:217
  30.7 1.6 %collective-permute-start.9 = (bf16[64,2048]{1,0:T(8,128)(2,1)S(1)}, bf16[64,2048]{1,0:T(8,128)(2,1)S(1)}, u32[]{:S(2)}, u32[]{:S(2)}) collective-permute-start(bf16[64,2048]{1,0:T(8,128)(2,1)S(1)} %get-tuple-element.44), channel_id=1, source_target_pairs={{0,1},{1,0},{2,3},{3,2},{4,5},{5,4},{6,7},{7,6},{8,9},{9,8},{10,11... | collective-permute-start | bytes 786440 | tf_op jit(solution)/shard_map/ppermute | solution.py:229
  30.8 1.9 %collective-permute-start.6 = (bf16[64,2048]{1,0:T(8,128)(2,1)S(1)}, bf16[64,2048]{1,0:T(8,128)(2,1)S(1)}, u32[]{:S(2)}, u32[]{:S(2)}) collective-permute-start(bf16[64,2048]{1,0:T(8,128)(2,1)S(1)} %get-tuple-element.36), channel_id=1, source_target_pairs={{0,1},{1,0},{2,3},{3,2},{4,5},{5,4},{6,7},{7,6},{8,9},{9,8},{10,11... | collective-permute-start | bytes 786440 | tf_op jit(solution)/shard_map/ppermute | solution.py:229
  32.3 4.1 %collective-permute-start.13 = (bf16[64,2176]{1,0:T(8,128)(2,1)S(1)}, bf16[64,2176]{1,0:T(8,128)(2,1)S(1)}, u32[]{:S(2)}, u32[]{:S(2)}) collective-permute-start(bf16[64,2176]{1,0:T(8,128)(2,1)S(1)} %collective-permute-done.8.refs_2_), channel_id=1, source_target_pairs={{0,1},{1,0},{2,3},{3,2},{4,5},{5,4},{6,7},{7,6},{8,9},{9,8},{10,11... | collective-permute-start | bytes 835592 | tf_op jit(solution)/shard_map/ppermute | solution.py:216
  32.7 5.2 %collective-permute-start.17 = (bf16[64,2176]{1,0:T(8,128)(2,1)S(1)}, bf16[64,2176]{1,0:T(8,128)(2,1)S(1)}, u32[]{:S(2)}, u32[]{:S(2)}) collective-permute-start(bf16[64,2176]{1,0:T(8,128)(2,1)S(1)} %collective-permute-done.16.refs_3_), channel_id=1, source_target_pairs={{0,1},{1,0},{2,3},{3,2},{4,5},{5,4},{6,7},{7,6},{8,9},{9,8},{10,11... | collective-permute-start | bytes 835592 | tf_op jit(solution)/shard_map/ppermute | solution.py:216
  35.5 5.0 %collective-permute-start.23 = (bf16[64,2176]{1,0:T(8,128)(2,1)S(1)}, bf16[64,2176]{1,0:T(8,128)(2,1)S(1)}, u32[]{:S(2)}, u32[]{:S(2)}) collective-permute-start(bf16[64,2176]{1,0:T(8,128)(2,1)S(1)} %collective-permute-done.14.refs_1_), channel_id=1, source_target_pairs={{0,1},{1,0},{2,3},{3,2},{4,5},{5,4},{6,7},{7,6},{8,9},{9,8},{10,11... | collective-permute-start | bytes 835592 | tf_op jit(solution)/shard_map/ppermute | solution.py:233
  36.0 1.6 %collective-permute-start.15 = (bf16[64,2048]{1,0:T(8,128)(2,1)S(1)}, bf16[64,2048]{1,0:T(8,128)(2,1)S(1)}, u32[]{:S(2)}, u32[]{:S(2)}) collective-permute-start(bf16[64,2048]{1,0:T(8,128)(2,1)S(1)} %get-tuple-element.50), channel_id=1, source_target_pairs={{0,1},{1,0},{2,3},{3,2},{4,5},{5,4},{6,7},{7,6},{8,9},{9,8},{10,11... | collective-permute-start | bytes 786440 | tf_op jit(solution)/shard_map/ppermute | solution.py:229
  36.1 1.8 %collective-permute-start.12 = (bf16[64,2048]{1,0:T(8,128)(2,1)S(1)}, bf16[64,2048]{1,0:T(8,128)(2,1)S(1)}, u32[]{:S(2)}, u32[]{:S(2)}) collective-permute-start(bf16[64,2048]{1,0:T(8,128)(2,1)S(1)} %get-tuple-element.47), channel_id=1, source_target_pairs={{0,1},{1,0},{2,3},{3,2},{4,5},{5,4},{6,7},{7,6},{8,9},{9,8},{10,11... | collective-permute-start | bytes 786440 | tf_op jit(solution)/shard_map/ppermute | solution.py:229
  42.6 1.6 %collective-permute-start.24 = (bf16[64,2048]{1,0:T(8,128)(2,1)S(1)}, bf16[64,2048]{1,0:T(8,128)(2,1)S(1)}, u32[]{:S(2)}, u32[]{:S(2)}) collective-permute-start(bf16[64,2048]{1,0:T(8,128)(2,1)S(1)} %get-tuple-element.61), channel_id=1, source_target_pairs={{0,1},{1,0},{2,3},{3,2},{4,5},{5,4},{6,7},{7,6},{8,9},{9,8},{10,11... | collective-permute-start | bytes 786440 | tf_op jit(solution)/shard_map/ppermute | solution.py:235
  43.1 2.9 %collective-permute-start.18 = (bf16[64,2048]{1,0:T(8,128)(2,1)S(1)}, bf16[64,2048]{1,0:T(8,128)(2,1)S(1)}, u32[]{:S(2)}, u32[]{:S(2)}) collective-permute-start(bf16[64,2048]{1,0:T(8,128)(2,1)S(1)} %get-tuple-element.53), channel_id=1, source_target_pairs={{0,1},{1,0},{2,3},{3,2},{4,5},{5,4},{6,7},{7,6},{8,9},{9,8},{10,11... | collective-permute-start | bytes 786440 | tf_op jit(solution)/shard_map/ppermute | solution.py:229
  43.2 4.4 %collective-permute-start.22 = (bf16[64,2048]{1,0:T(8,128)(2,1)S(1)}, bf16[64,2048]{1,0:T(8,128)(2,1)S(1)}, u32[]{:S(2)}, u32[]{:S(2)}) collective-permute-start(bf16[64,2048]{1,0:T(8,128)(2,1)S(1)} %get-tuple-element.57), channel_id=1, source_target_pairs={{0,1},{1,0},{2,3},{3,2},{4,5},{5,4},{6,7},{7,6},{8,9},{9,8},{10,11... | collective-permute-start | bytes 786440 | tf_op jit(solution)/shard_map/ppermute | solution.py:229
  44.3 6.4 %collective-permute-start.25 = (bf16[64,2048]{1,0:T(8,128)(2,1)S(1)}, bf16[64,2048]{1,0:T(8,128)(2,1)S(1)}, u32[]{:S(2)}, u32[]{:S(2)}) collective-permute-start(bf16[64,2048]{1,0:T(8,128)(2,1)S(1)} %add_convert_fusion.5), channel_id=1, source_target_pairs={{0,4},{1,3},{4,8},{5,1},{8,12},{9,5},{12,14},{13,9},{14,10},{15,13... | collective-permute-start | bytes 786440 | tf_op jit(solution)/shard_map/ppermute | solution.py:235
  46.0 7.5 %collective-permute-start.19 = (bf16[64,2048]{1,0:T(8,128)(2,1)S(1)}, bf16[64,2048]{1,0:T(8,128)(2,1)S(1)}, u32[]{:S(2)}, u32[]{:S(2)}) collective-permute-start(bf16[64,2048]{1,0:T(8,128)(2,1)S(1)} %add_convert_fusion.8), channel_id=1, source_target_pairs={{0,4},{1,3},{4,8},{5,1},{8,12},{9,5},{12,14},{13,9},{14,10},{15,13... | collective-permute-start | bytes 786440 | tf_op jit(solution)/shard_map/ppermute | solution.py:231
  50.8 6.4 %collective-permute-start.26 = (bf16[64,2048]{1,0:T(8,128)(2,1)S(1)}, bf16[64,2048]{1,0:T(8,128)(2,1)S(1)}, u32[]{:S(2)}, u32[]{:S(2)}) collective-permute-start(bf16[64,2048]{1,0:T(8,128)(2,1)S(1)} %add_convert_fusion.4), channel_id=1, source_target_pairs={{0,4},{1,3},{4,8},{5,1},{8,12},{9,5},{12,14},{13,9},{14,10},{15,13... | collective-permute-start | bytes 786440 | tf_op jit(solution)/shard_map/ppermute | solution.py:241
  53.6 7.4 %collective-permute-start.20 = (bf16[64,2048]{1,0:T(8,128)(2,1)S(1)}, bf16[64,2048]{1,0:T(8,128)(2,1)S(1)}, u32[]{:S(2)}, u32[]{:S(2)}) collective-permute-start(bf16[64,2048]{1,0:T(8,128)(2,1)S(1)} %add_convert_fusion.7), channel_id=1, source_target_pairs={{0,4},{1,3},{4,8},{5,1},{8,12},{9,5},{12,14},{13,9},{14,10},{15,13... | collective-permute-start | bytes 786440 | tf_op jit(solution)/shard_map/ppermute | solution.py:238
  57.4 6.4 %collective-permute-start.27 = (bf16[64,2048]{1,0:T(8,128)(2,1)S(1)}, bf16[64,2048]{1,0:T(8,128)(2,1)S(1)}, u32[]{:S(2)}, u32[]{:S(2)}) collective-permute-start(bf16[64,2048]{1,0:T(8,128)(2,1)S(1)} %add_convert_fusion.3), channel_id=1, source_target_pairs={{0,4},{1,3},{4,8},{5,1},{8,12},{9,5},{12,14},{13,9},{14,10},{15,13... | collective-permute-start | bytes 786440 | tf_op jit(solution)/shard_map/ppermute | solution.py:241
  63.9 6.4 %collective-permute-start.28 = (bf16[64,2048]{1,0:T(8,128)(2,1)S(1)}, bf16[64,2048]{1,0:T(8,128)(2,1)S(1)}, u32[]{:S(2)}, u32[]{:S(2)}) collective-permute-start(bf16[64,2048]{1,0:T(8,128)(2,1)S(1)} %add_convert_fusion.2), channel_id=1, source_target_pairs={{0,4},{1,3},{4,8},{5,1},{8,12},{9,5},{12,14},{13,9},{14,10},{15,13... | collective-permute-start | bytes 786440 | tf_op jit(solution)/shard_map/ppermute | solution.py:241
  65.6 7.5 %collective-permute-start.21 = (bf16[64,2048]{1,0:T(8,128)(2,1)S(1)}, bf16[64,2048]{1,0:T(8,128)(2,1)S(1)}, u32[]{:S(2)}, u32[]{:S(2)}) collective-permute-start(bf16[64,2048]{1,0:T(8,128)(2,1)S(1)} %add_convert_fusion.6), channel_id=1, source_target_pairs={{0,4},{1,3},{4,8},{5,1},{8,12},{9,5},{12,14},{13,9},{14,10},{15,13... | collective-permute-start | bytes 786440 | tf_op jit(solution)/shard_map/ppermute | solution.py:238
  70.4 2.7 %collective-permute-start.29 = (bf16[64,2048]{1,0:T(8,128)(2,1)S(1)}, bf16[64,2048]{1,0:T(8,128)(2,1)S(1)}, u32[]{:S(2)}, u32[]{:S(2)}) collective-permute-start(bf16[64,2048]{1,0:T(8,128)(2,1)S(1)} %add_convert_fusion.1), channel_id=1, source_target_pairs={{0,1},{1,0},{2,3},{3,2},{4,5},{5,4},{6,7},{7,6},{8,9},{9,8},{10,11... | collective-permute-start | bytes 786440 | tf_op jit(solution)/shard_map/ppermute | solution.py:242

commit v5 on v2

--- a/solution.py
+++ b/solution.py
@@ -75,17 +75,14 @@
     return pairs
 
 
-def expert_kernel(width, experts, own_ref, first_ref, second_ref, gate_ref, up_ref, down_ref,
-                  first_out, second_out, rows_ref, hidden_ref):
-    half = first_ref.shape[0]
-    ff = gate_ref.shape[2]
-    rows_ref[:half, :] = first_ref[...]
-    rows_ref[half:, :] = second_ref[...]
-    tail = rows_ref[:, width:].astype(jnp.float32)
-    lane = lax.broadcasted_iota(jnp.int32, tail.shape, 1)
-    own = own_ref[0]
-    mine = (lane == own) | (lane == own + experts)
-    weight = jnp.sum(jnp.where(mine, tail, 0.0), axis=1, keepdims=True)
+def expert_kernel(experts, blocks, own_ref, *refs):
+    gate_ref, up_ref, down_ref = refs[blocks : blocks + 3]
+    outs = refs[blocks + 3 : 2 * blocks + 3]
+    rows_ref, hidden_ref = refs[2 * blocks + 3 :]
+    width, ff = gate_ref.shape[1:]
+    each = outs[0].shape[0]
+    for number in range(blocks):
+        rows_ref[number * each : (number + 1) * each, :] = refs[number][...]
     step = math.gcd(ff, 256)
     for at in range(0, ff, step):
         part = slice(at, at + step)
@@ -93,6 +90,11 @@
         gate = jnp.dot(rows, gate_ref[0, :, part], preferred_element_type=jnp.float32)
         up = jnp.dot(rows, up_ref[0, :, part], preferred_element_type=jnp.float32)
         hidden_ref[:, part] = (gate / (1.0 + jnp.exp(-gate)) * up).astype(jnp.bfloat16)
+    tail = rows_ref[:, width:].astype(jnp.float32)
+    lane = lax.broadcasted_iota(jnp.int32, tail.shape, 1)
+    own = own_ref[0]
+    mine = (lane == own) | (lane == own + experts)
+    weight = jnp.sum(jnp.where(mine, tail, 0.0), axis=1, keepdims=True)
     step = math.gcd(width, 512)
     for at in range(0, width, step):
         part = slice(at, at + step)
@@ -101,29 +103,102 @@
             preferred_element_type=jnp.float32,
         )
         out = (out * weight).astype(jnp.bfloat16)
-        first_out[:, part] = out[:half]
-        second_out[:, part] = out[half:]
-
-
-def run_expert(own, first, second, gate_w, up_w, down_w, experts):
-    half, wide = first.shape
-    width, ff = gate_w.shape[1:]
+        for number, target in enumerate(outs):
+            target[:, part] = out[number * each : (number + 1) * each]
+
+
+def run_expert(own, blocks, weights, experts):
+    rows = sum(block.shape[0] for block in blocks)
+    wide = blocks[0].shape[1]
+    width, ff = weights[0].shape[1:]
     vmem = pl.BlockSpec(memory_space=pltpu.VMEM)
     return pl.pallas_call(
-        functools.partial(expert_kernel, width, experts),
-        out_shape=[jax.ShapeDtypeStruct((half, width), jnp.bfloat16)] * 2,
-        in_specs=[pl.BlockSpec(memory_space=pltpu.SMEM)] + [vmem] * 5,
-        out_specs=[vmem] * 2,
-        scratch_shapes=[
-            pltpu.VMEM((2 * half, wide), jnp.bfloat16),
-            pltpu.VMEM((2 * half, ff), jnp.bfloat16),
-        ],
+        functools.partial(expert_kernel, experts, len(blocks)),
+        out_shape=[jax.ShapeDtypeStruct((block.shape[0], width), jnp.bfloat16) for block in blocks],
+        in_specs=[pl.BlockSpec(memory_space=pltpu.SMEM)] + [vmem] * (len(blocks) + 3),
+        out_specs=[vmem] * len(blocks),
+        scratch_shapes=[pltpu.VMEM((rows, wide), jnp.bfloat16), pltpu.VMEM((rows, ff), jnp.bfloat16)],
         compiler_params=pltpu.CompilerParams(vmem_limit_bytes=30 << 20),
         cost_estimate=pl.CostEstimate(
-            flops=2 * 2 * half * 3 * width * ff, bytes_accessed=8 * half * width,
-            transcendentals=2 * half * ff,
+            flops=rows * width, bytes_accessed=rows * width, transcendentals=0
         ),
-    )(own, first, second, gate_w, up_w, down_w)
+        name="expert",
+    )(own, *blocks, *weights)
+
+
+def load_kernel(pieces, *refs):
+    done = refs[6]
+    copies = []
+    for source, target in zip(refs[:3], refs[3:6]):
+        depth = source.shape[1] // pieces
+        for piece in range(pieces):
+            part = pl.ds(piece * depth, depth)
+            copies.append(
+                pltpu.make_async_copy(source.at[:, part], target.at[:, part], done.at[len(copies)])
+            )
+    for copy in copies:
+        copy.start()
+    for copy in copies:
+        copy.wait()
+
+
+def load_weights(weights):
+    pieces = math.gcd(weights[0].shape[1] // 16, 4)
+    return pl.pallas_call(
+        functools.partial(load_kernel, pieces),
+        out_shape=[pltpu.VMEM(w.shape, w.dtype) for w in weights],
+        in_specs=[pl.BlockSpec(memory_space=pltpu.HBM)] * 3,
+        out_specs=[pl.BlockSpec(memory_space=pltpu.VMEM)] * 3,
+        scratch_shapes=[pltpu.SemaphoreType.DMA((3 * pieces,))],
+        compiler_params=pltpu.CompilerParams(vmem_limit_bytes=30 << 20),
+        cost_estimate=pl.CostEstimate(flops=0, bytes_accessed=1024, transcendentals=0),
+        name="load",
+    )(*[pltpu.with_memory_space_constraint(w, pltpu.HBM) for w in weights])
+
+
+def pack_kernel(experts, tokens_ref, ids_ref, weights_ref, out_ref, own_ids, own_weights, done):
+    count, width = tokens_ref.shape
+    copies = [
+        pltpu.make_async_copy(source, target, done.at[number])
+        for number, (source, target) in enumerate(
+            ((ids_ref, own_ids), (weights_ref, own_weights), (tokens_ref, out_ref.at[:, :width]))
+        )
+    ]
+    for copy in copies:
+        copy.start()
+    copies[0].wait()
+    copies[1].wait()
+    ids = own_ids[...]
+    scale = own_weights[...]
+    number = lax.broadcasted_iota(jnp.int32, (experts, count), 0)
+    weight = jnp.zeros((experts, count), jnp.float32)
+    for choice in range(ids.shape[0]):
+        weight += jnp.where(ids[choice : choice + 1] == number, scale[choice : choice + 1], 0.0)
+    high = weight.astype(jnp.bfloat16).astype(jnp.float32)
+    low = weight - high
+    rest = jnp.zeros((128 - 2 * experts, count), jnp.float32)
+    columns = jnp.concatenate([high, low, rest], 0)
+    columns = jnp.concatenate([columns, jnp.zeros((128, 128 - count), jnp.float32)], 1)
+    out_ref[:, width:] = columns.T[:count].astype(jnp.bfloat16)
+    copies[2].wait()
+
+
+def pack(tokens, expert_ids, router_weights, experts):
+    count, width = tokens.shape
+    ids, scale = expert_ids.T, router_weights.T
+    return pl.pallas_call(
+        functools.partial(pack_kernel, experts),
+        out_shape=jax.ShapeDtypeStruct((count, width + 128), jnp.bfloat16),
+        in_specs=[pl.BlockSpec(memory_space=pltpu.HBM)] * 3,
+        out_specs=pl.BlockSpec(memory_space=pltpu.VMEM),
+        scratch_shapes=[
+            pltpu.VMEM(ids.shape, ids.dtype),
+            pltpu.VMEM(scale.shape, scale.dtype),
+            pltpu.SemaphoreType.DMA((3,)),
+        ],
+        cost_estimate=pl.CostEstimate(flops=0, bytes_accessed=1024, transcendentals=0),
+        name="pack",
+    )(*[pltpu.with_memory_space_constraint(array, pltpu.HBM) for array in (tokens, ids, scale)])
 
 
 def added(*terms):
@@ -131,6 +206,10 @@
     for term in terms[1:]:
         total = total + term.astype(jnp.float32)
     return total.astype(jnp.bfloat16)
+
+
+def after(value, *others):
+    return lax.optimization_barrier((value, *others))[0]
 
 
 def dense_body(tokens, expert_ids, router_weights, w_gate, w_up, w_down):
@@ -141,35 +220,35 @@
     ring = functools.partial(lax.ppermute, axis_name="expert", perm=ring_pairs(experts))
     own = lax.axis_index("expert").reshape(1)
 
-    numbers = jnp.arange(experts, dtype=jnp.int32)
-    chosen = expert_ids[:, :, None] == numbers[None, None, :]
-    weight = jnp.sum(jnp.where(chosen, router_weights[:, :, None], 0.0), 1)
-    high = weight.astype(jnp.bfloat16)
-    low = (weight - high.astype(jnp.float32)).astype(jnp.bfloat16)
-    empty = jnp.zeros((count, 128 - 2 * experts), jnp.bfloat16)
-    mine = jnp.concatenate([tokens, high, low, empty], 1)
-
-    weights = [pltpu.with_memory_space_constraint(w, pltpu.VMEM) for w in (w_gate, w_up, w_down)]
-    run = lambda first, second: run_expert(own, first, second, *weights, experts)
-
+    mine = pack(tokens, expert_ids, router_weights, experts)
     sibling = swap(mine)
-    held = jnp.concatenate([mine, sibling], 0)
-    kept, other = run(mine, sibling)
-    pairs = []
-    for step in range(1, rounds + 1):
-        held = ring(held if step < rounds else held[:count])
-        first, second = run(held, swap(held))
-        pairs.append((second, swap(first)))
-    moving = None
-    for second, first in reversed(pairs):
-        terms = added(second, first) if moving is None else None
-        if moving is not None:
-            if moving.shape[0] < second.shape[0]:
-                moving = jnp.pad(moving, ((0, second.shape[0] - moving.shape[0]), (0, 0)))
-            terms = added(second, first, moving)
-        moving = ring(terms)
-    last = swap(added(moving[:count], other))
-    return added(moving[count:], kept, last)
+    first, second = ring(mine), ring(sibling)
+    weights = load_weights((after(w_gate, sibling), w_up, w_down))
+    first = after(first, weights[0])
+    run = lambda *blocks: run_expert(own, blocks, weights, experts)
+    blocks = {}
+    for step in range(1, rounds):
+        if step > 1:
+            second = ring(second)
+        blocks[step] = (swap(first), swap(second), first, second)
+        first = ring(first)
+    sums = {2: run(*blocks[2])}
+    first = after(first, sums[2][0], *blocks[1][:2], blocks[3][0])
+    keep, send, *sums[3] = run(swap(first), first, *blocks[3])
+    lead, trail = ring(added(keep, swap(send))), None
+    for step in (3, 2, 1):
+        if step == 3:
+            sums[1] = run(after(blocks[1][0], lead), *blocks[1][1:])
+        if step == 2:
+            lead = after(lead, sums[1][0])
+        keep, keep_trail, send, send_trail = sums[step]
+        send, send_trail = swap(send), swap(send_trail)
+        trail = ring(added(*([keep_trail, send_trail] + ([] if trail is None else [trail]))))
+        lead = ring(added(keep, send, lead))
+        if step == 2:
+            kept, other = run(after(mine, lead), sibling)
+    last = swap(added(lead, other))
+    return added(trail, kept, last)
 
 
 def solution(mesh):

time: 90.2 us -> 81.3 us (0.901)
  waiting for transfers between devices: 48.4 us -> 22.7 us
  Pallas kernels: 12 us -> 20.2 us
  local copies, waits for them, and re-layouts: 6.93 us -> 12.1 us
  starting transfers between devices: 20 us -> 24.3 us
    ppermute x17 -> x29, waiting for transfers between devices: 47.2 us -> 22.7 us  [the longest x3 6.65 us: dense_body(): first = ring(first)]
    pallas_call x5 -> x6, Pallas kernels: 12 us -> 20.2 us  [the longest x4 14.6 us: run_expert(): pl.pallas_call(functools.partial(expert_kernel, experts, len(blocks)), ou...]
    unnamed x10 -> x26, local copies, waits for them, and re-layouts: 5.68 us -> 12.1 us
    ppermute x17 -> x29, starting transfers between devices: 19.5 us -> 23.7 us  [the longest x3 4.73 us: dense_body(): first = ring(first)]
    ppermute x1, waiting for transfers between devices: 1.19 us -> 0.01 us  [dense_body(): sibling = swap(mine)]
    concatenate x1 -> x0, local copies, waits for them, and re-layouts: 1.05 us -> none  [dense_body(): mine = jnp.concatenate([tokens, high, low, empty], 1)]
  transfers between devices with their start and end apart: 18 -> 30, of which waited for: 11 -> 13; matrix products, arithmetic and copies ran while one was open for 1% -> 1% of each run, Pallas kernels for 13% -> 17%
where the time goes in v5:
time: 81.3 us; the launch traced here: 81 us
  starting transfers between devices  24.3 us (30%)
  waiting for transfers between devices  22.7 us (28%)
  Pallas kernels  20.2 us (25%)
  local copies, waits for them, and re-layouts  12.1 us (15%)
  other arithmetic  1.49 us (2%)
    pallas_call x4, Pallas kernels, run_expert(): pl.pallas_call(functools.partial(expert_kernel, experts, len(blocks)), ou...  14.6 us
    unnamed x26, local copies, waits for them, and re-layouts  12.1 us
    ppermute x3, waiting for transfers between devices, dense_body(): first = ring(first)  6.65 us
    ppermute x2, waiting for transfers between devices, dense_body(): lead, trail = (ring(added(keep, swap(send))), None)  5.39 us
    ppermute x3, waiting for transfers between devices, dense_body(): ring(added(*[keep_trail, send_trail] + ([] if trail is None else [trail])))  5.26 us
    ppermute x3, starting transfers between devices, dense_body(): first = ring(first)  4.73 us
    ppermute x2, starting transfers between devices, dense_body(): first, second = (ring(mine), ring(sibling))  4.34 us
    ppermute x3, starting transfers between devices, dense_body(): lead = ring(added(keep, send, lead))  4.06 us
  transfers between devices with their start and end apart: 30, of which 13 were waited for; matrix products, arithmetic and copies ran while one was open for 1% of the time, Pallas kernels for 17%

profile of v5, /device:TPU:0, one launch (start us, length us, event | category | flops | bytes accessed | tf_op | source)
XLA Modules:
  0.0 81.0 jit_solution(17879027558524937652)
XLA Ops:
  0.0 1.7 %pack.1.refs_0_ = bf16[64,2176]{1,0:T(8,128)(2,1)} custom-call(bf16[64,2048]{1,0:T(8,128)(2,1)} %tokens_ref.1, s32[8,64]{1,0:T(8,128)} %bitcast.3, f32[8,64]{1,0:T(8,128)} %bitcast.4), custom_call_target="tpu_custom_call" | custom-call | bytes 1024 | tf_op jit(solution)/shard_map/pack/pallas_call | solution.py:189
  1.7 0.5 collective-permute-start.1
  2.2 2.6 %collective-permute-start = (bf16[64,2176]{1,0:T(8,128)(2,1)}, bf16[64,2176]{1,0:T(8,128)(2,1)}, u32[]{:S(2)}, u32[]{:S(2)}) collective-permute-start(bf16[64,2176]{1,0:T(8,128)(2,1)} %pack.1.refs_0_), channel_id=1, source_target_pairs={{0,4},{1,3},{4,8},{5,1},{8,12},{9,5},{12,14},{13,9},{14,10},{15,13... | collective-permute-start | bytes 835592 | tf_op jit(solution)/shard_map/ppermute | solution.py:225
  4.9 0.0 collective-permute-done.1.refs_1_
  4.9 1.7 %collective-permute-start.7 = (bf16[64,2176]{1,0:T(8,128)(2,1)S(1)}, bf16[64,2176]{1,0:T(8,128)(2,1)}, u32[]{:S(2)}, u32[]{:S(2)}) collective-permute-start(bf16[64,2176]{1,0:T(8,128)(2,1)S(1)} %collective-permute-done.1.refs_1_), channel_id=1, source_target_pairs={{0,4},{1,3},{4,8},{5,1},{8,12},{9,5},{12,14},{13,9},{14,10},{15,13... | collective-permute-start | bytes 835592 | tf_op jit(solution)/shard_map/ppermute | solution.py:225
  6.6 3.9 %load.1 = (bf16[1,2048,768]{2,1,0:T(8,128)(2,1)S(1)}, bf16[1,2048,768]{2,1,0:T(8,128)(2,1)S(1)}, bf16[1,2048,768]{2,1,0:T(8,128)(2,1)S(1)}) custom-call(bf16[1,2048,768]{2,1,0:T(8,128)(2,1)} %refs_0_, bf16[1,2048,768]{2,1,0:T(8,128)(2,1)} %refs_1_.1, bf16[1,2048,768]{2,1,0:T(8,128)(2,1)} %refs_2_.1), custom_call_target="tpu_custom_call" | custom-call | bytes 1024 | tf_op jit(solution)/shard_map/load/pallas_call | solution.py:147
  10.5 1.6 %copy-done = bf16[1,2048,768]{2,1,0:T(8,128)(2,1)} copy-done((bf16[1,2048,768]{2,1,0:T(8,128)(2,1)}, bf16[1,2048,768]{2,1,0:T(8,128)(2,1)S(1)}, u32[]{:S(2)}) %copy-start) | copy-done | bytes 3145752
  12.1 1.7 %copy-done.3 = bf16[1,2048,768]{2,1,0:T(8,128)(2,1)} copy-done((bf16[1,2048,768]{2,1,0:T(8,128)(2,1)}, bf16[1,2048,768]{2,1,0:T(8,128)(2,1)S(1)}, u32[]{:S(2)}) %copy-start.3) | copy-done | bytes 3145752
  13.8 1.6 %collective-permute-start.3 = (bf16[64,2176]{1,0:T(8,128)(2,1)}, bf16[64,2176]{1,0:T(8,128)(2,1)S(1)}, u32[]{:S(2)}, u32[]{:S(2)}) collective-permute-start(bf16[64,2176]{1,0:T(8,128)(2,1)} %collective-permute-done.refs_2_), channel_id=1, source_target_pairs={{0,4},{1,3},{4,8},{5,1},{8,12},{9,5},{12,14},{13,9},{14,10},{15,13... | collective-permute-start | bytes 835592 | tf_op jit(solution)/shard_map/ppermute | solution.py:234
  15.4 1.6 %collective-permute-start.8 = (bf16[64,2176]{1,0:T(8,128)(2,1)}, bf16[64,2176]{1,0:T(8,128)(2,1)}, u32[]{:S(2)}, u32[]{:S(2)}) collective-permute-start(bf16[64,2176]{1,0:T(8,128)(2,1)} %collective-permute-done.7.refs_3_), channel_id=1, source_target_pairs={{0,4},{1,3},{4,8},{5,1},{8,12},{9,5},{12,14},{13,9},{14,10},{15,13... | collective-permute-start | bytes 835592 | tf_op jit(solution)/shard_map/ppermute | solution.py:232
  16.9 3.6 %collective-permute-done.3.refs_2_ = bf16[64,2176]{1,0:T(8,128)(2,1)S(1)} collective-permute-done((bf16[64,2176]{1,0:T(8,128)(2,1)}, bf16[64,2176]{1,0:T(8,128)(2,1)S(1)}, u32[]{:S(2)}, u32[]{:S(2)}) %collective-permute-start.3) | collective-permute-done | bytes 278560 | tf_op jit(solution)/shard_map/ppermute | solution.py:234
  20.5 1.6 %collective-permute-start.4 = (bf16[64,2176]{1,0:T(8,128)(2,1)S(1)}, bf16[64,2176]{1,0:T(8,128)(2,1)}, u32[]{:S(2)}, u32[]{:S(2)}) collective-permute-start(bf16[64,2176]{1,0:T(8,128)(2,1)S(1)} %collective-permute-done.3.refs_2_), channel_id=1, source_target_pairs={{0,4},{1,3},{4,8},{5,1},{8,12},{9,5},{12,14},{13,9},{14,10},{15,13... | collective-permute-start | bytes 835592 | tf_op jit(solution)/shard_map/ppermute | solution.py:234
  22.1 0.7 copy-done.7
  22.8 0.8 collective-permute-done.8.refs_3_
  23.6 0.5 collective-permute-start.2
  24.1 0.0 collective-permute-start.10
  24.1 3.0 %collective-permute-done.4.refs_4_ = bf16[64,2176]{1,0:T(8,128)(2,1)} collective-permute-done((bf16[64,2176]{1,0:T(8,128)(2,1)S(1)}, bf16[64,2176]{1,0:T(8,128)(2,1)}, u32[]{:S(2)}, u32[]{:S(2)}) %collective-permute-start.4) | collective-permute-done | bytes 278560 | tf_op jit(solution)/shard_map/ppermute | solution.py:234
  27.2 0.7 copy-done.9
  27.9 1.6 %collective-permute-start.5 = (bf16[64,2176]{1,0:T(8,128)(2,1)}, bf16[64,2176]{1,0:T(8,128)(2,1)}, u32[]{:S(2)}, u32[]{:S(2)}) collective-permute-start(bf16[64,2176]{1,0:T(8,128)(2,1)} %collective-permute-done.4.refs_4_), channel_id=1, source_target_pairs={{0,4},{1,3},{4,8},{5,1},{8,12},{9,5},{12,14},{13,9},{14,10},{15,13... | collective-permute-start | bytes 835592 | tf_op jit(solution)/shard_map/ppermute | solution.py:234
  29.5 0.7 copy-done.11
  30.2 1.6 %collective-permute-start.13 = (bf16[64,2176]{1,0:T(8,128)(2,1)}, bf16[64,2176]{1,0:T(8,128)(2,1)}, u32[]{:S(2)}, u32[]{:S(2)}) collective-permute-start(bf16[64,2176]{1,0:T(8,128)(2,1)} %collective-permute-done.8.refs_3_), channel_id=1, source_target_pairs={{0,4},{1,3},{4,8},{5,1},{8,12},{9,5},{12,14},{13,9},{14,10},{15,13... | collective-permute-start | bytes 835592 | tf_op jit(solution)/shard_map/ppermute | solution.py:232
  31.8 1.9 %copy-done.1 = bf16[1,2048,768]{2,1,0:T(8,128)(2,1)S(1)} copy-done((bf16[1,2048,768]{2,1,0:T(8,128)(2,1)S(1)}, bf16[1,2048,768]{2,1,0:T(8,128)(2,1)}, u32[]{:S(2)}) %copy-start.1) | copy-done | bytes 3145752
  33.7 1.9 %copy-done.4 = bf16[1,2048,768]{2,1,0:T(8,128)(2,1)S(1)} copy-done((bf16[1,2048,768]{2,1,0:T(8,128)(2,1)S(1)}, bf16[1,2048,768]{2,1,0:T(8,128)(2,1)}, u32[]{:S(2)}) %copy-start.4) | copy-done | bytes 3145752
  35.6 1.0 %copy-done.8 = bf16[64,2176]{1,0:T(8,128)(2,1)S(1)} copy-done((bf16[64,2176]{1,0:T(8,128)(2,1)S(1)}, bf16[64,2176]{1,0:T(8,128)(2,1)}, u32[]{:S(2)}) %copy-start.8) | copy-done | bytes 278552
  36.5 1.0 %copy-done.10 = bf16[64,2176]{1,0:T(8,128)(2,1)S(1)} copy-done((bf16[64,2176]{1,0:T(8,128)(2,1)S(1)}, bf16[64,2176]{1,0:T(8,128)(2,1)}, u32[]{:S(2)}) %copy-start.10) | copy-done | bytes 278552
  37.5 1.0 %copy-done.12 = bf16[64,2176]{1,0:T(8,128)(2,1)S(1)} copy-done((bf16[64,2176]{1,0:T(8,128)(2,1)S(1)}, bf16[64,2176]{1,0:T(8,128)(2,1)}, u32[]{:S(2)}) %copy-start.12) | copy-done | bytes 278552
  38.4 3.6 %expert.4 = (bf16[64,2048]{1,0:T(8,128)(2,1)S(1)}, bf16[64,2048]{1,0:T(8,128)(2,1)S(1)}, bf16[64,2048]{1,0:T(8,128)(2,1)S(1)}, bf16[64,2048]{1,0:T(8,128)(2,1)S(1)}) custom-call(s32[1]{0:T(128)} %bitcast.own_ref, bf16[64,2176]{1,0:T(8,128)(2,1)S(1)} %copy-done.10, bf16[64,2176]{1,0:T(8,128)(2,1)S(1)} %copy-done.12, bf16[64,2176]{1,0:T(8,128)(2,1)S(1)} %copy-done.8, ...), custom_call_target="tpu_custom_call" | custom-call | flops 524288 | bytes 524288 | tf_op jit(solution)/shard_map/expert/pallas_call | solution.py:115
  42.1 0.1 collective-permute-start.14
  42.2 0.5 collective-permute-start.12
  42.7 1.3 %collective-permute-done.14.refs_3_ = bf16[64,2176]{1,0:T(8,128)(2,1)S(1)} collective-permute-done((bf16[64,2176]{1,0:T(8,128)(2,1)}, bf16[64,2176]{1,0:T(8,128)(2,1)S(1)}, u32[]{:S(2)}, u32[]{:S(2)}) %collective-permute-start.14) | collective-permute-done | bytes 278560 | tf_op jit(solution)/shard_map/ppermute | solution.py:233
  43.9 0.4 collective-permute-done.12.refs_0_
  44.3 5.0 %expert.5 = (bf16[64,2048]{1,0:T(8,128)(2,1)S(1)}, bf16[64,2048]{1,0:T(8,128)(2,1)S(1)}, bf16[64,2048]{1,0:T(8,128)(2,1)S(1)}, bf16[64,2048]{1,0:T(8,128)(2,1)S(...) custom-call(s32[1]{0:T(128)} %bitcast.own_ref, bf16[64,2176]{1,0:T(8,128)(2,1)S(1)} %collective-permute-done.12.refs_0_, ...), custom_call_target="tpu_custom_call" | custom-call | flops 786432 | bytes 786432 | tf_op jit(solution)/shard_map/expert/pallas_call | solution.py:115
  49.4 0.2 collective-permute-start.15
  49.6 0.4 collective-permute-start.24
  50.0 1.0 %collective-permute-done.15 = bf16[64,2048]{1,0:T(8,128)(2,1)S(1)} collective-permute-done((bf16[64,2048]{1,0:T(8,128)(2,1)S(1)}, bf16[64,2048]{1,0:T(8,128)(2,1)S(1)}, u32[]{:S(2)}, u32[]{:S(2)}) %collective-permute-start.15) | collective-permute-done | bytes 262176 | tf_op jit(solution)/shard_map/ppermute | solution.py:238
  51.0 0.1 add_convert_fusion.8
  51.0 1.5 %collective-permute-start.16 = (bf16[64,2048]{1,0:T(8,128)(2,1)S(1)}, bf16[64,2048]{1,0:T(8,128)(2,1)S(1)}, u32[]{:S(2)}, u32[]{:S(2)}) collective-permute-start(bf16[64,2048]{1,0:T(8,128)(2,1)S(1)} %add_convert_fusion.8), channel_id=1, source_target_pairs={{0,4},{1,3},{4,8},{5,1},{8,12},{9,5},{12,14},{13,9},{14,10},{15,13... | collective-permute-start | bytes 786440 | tf_op jit(solution)/shard_map/ppermute | solution.py:238
  52.6 0.5 collective-permute-start.23
  53.1 4.4 %collective-permute-done.16 = bf16[64,2048]{1,0:T(8,128)(2,1)S(1)} collective-permute-done((bf16[64,2048]{1,0:T(8,128)(2,1)S(1)}, bf16[64,2048]{1,0:T(8,128)(2,1)S(1)}, u32[]{:S(2)}, u32[]{:S(2)}) %collective-permute-start.16) | collective-permute-done | bytes 262176 | tf_op jit(solution)/shard_map/ppermute | solution.py:238
  57.5 0.1 add_convert_fusion.4
  57.6 1.5 %collective-permute-start.25 = (bf16[64,2048]{1,0:T(8,128)(2,1)S(1)}, bf16[64,2048]{1,0:T(8,128)(2,1)S(1)}, u32[]{:S(2)}, u32[]{:S(2)}) collective-permute-start(bf16[64,2048]{1,0:T(8,128)(2,1)S(1)} %add_convert_fusion.4), channel_id=1, source_target_pairs={{0,4},{1,3},{4,8},{5,1},{8,12},{9,5},{12,14},{13,9},{14,10},{15,13... | collective-permute-start | bytes 786440 | tf_op jit(solution)/shard_map/ppermute | solution.py:247
  59.1 0.1 add_convert_fusion.7
  59.2 0.5 collective-permute-start.20
  59.7 4.0 %expert.6 = (bf16[64,2048]{1,0:T(8,128)(2,1)S(1)}, bf16[64,2048]{1,0:T(8,128)(2,1)S(1)}, bf16[64,2048]{1,0:T(8,128)(2,1)S(1)}, bf16[64,2048]{1,0:T(8,128)(2,1)S(1)}) custom-call(s32[1]{0:T(128)} %bitcast.own_ref, bf16[64,2176]{1,0:T(8,128)(2,1)} %collective-permute-done.2.refs_0_, bf16[64,2176]{1,0:T(8,128)(2,1)} %collective-permute-done.10.refs_1_, ...), custom_call_target="tpu_custom_call" | custom-call | flops 524288 | bytes 524288 | tf_op jit(solution)/shard_map/expert/pallas_call | solution.py:115
  63.7 0.1 collective-permute-start.17
  63.8 0.2 collective-permute-done.25
  64.0 0.3 collective-permute-start.27
  64.3 0.1 add_convert_fusion.3
  64.4 1.3 %collective-permute-start.26 = (bf16[64,2048]{1,0:T(8,128)(2,1)S(1)}, bf16[64,2048]{1,0:T(8,128)(2,1)S(1)}, u32[]{:S(2)}, u32[]{:S(2)}) collective-permute-start(bf16[64,2048]{1,0:T(8,128)(2,1)S(1)} %add_convert_fusion.3), channel_id=1, source_target_pairs={{0,4},{1,3},{4,8},{5,1},{8,12},{9,5},{12,14},{13,9},{14,10},{15,13... | collective-permute-start | bytes 786440 | tf_op jit(solution)/shard_map/ppermute | solution.py:247
  65.7 1.2 %collective-permute-done.20 = bf16[64,2048]{1,0:T(8,128)(2,1)S(1)} collective-permute-done((bf16[64,2048]{1,0:T(8,128)(2,1)S(1)}, bf16[64,2048]{1,0:T(8,128)(2,1)S(1)}, u32[]{:S(2)}, u32[]{:S(2)}) %collective-permute-start.20) | collective-permute-done | bytes 262176 | tf_op jit(solution)/shard_map/ppermute | solution.py:246
  66.8 0.1 add_convert_fusion.6
  66.9 1.5 %collective-permute-start.21 = (bf16[64,2048]{1,0:T(8,128)(2,1)S(1)}, bf16[64,2048]{1,0:T(8,128)(2,1)S(1)}, u32[]{:S(2)}, u32[]{:S(2)}) collective-permute-start(bf16[64,2048]{1,0:T(8,128)(2,1)S(1)} %add_convert_fusion.6), channel_id=1, source_target_pairs={{0,4},{1,3},{4,8},{5,1},{8,12},{9,5},{12,14},{13,9},{14,10},{15,13... | collective-permute-start | bytes 786440 | tf_op jit(solution)/shard_map/ppermute | solution.py:246
  68.5 2.4 %collective-permute-done.26 = bf16[64,2048]{1,0:T(8,128)(2,1)S(1)} collective-permute-done((bf16[64,2048]{1,0:T(8,128)(2,1)S(1)}, bf16[64,2048]{1,0:T(8,128)(2,1)S(1)}, u32[]{:S(2)}, u32[]{:S(2)}) %collective-permute-start.26) | collective-permute-done | bytes 262176 | tf_op jit(solution)/shard_map/ppermute | solution.py:247
  70.8 0.1 add_convert_fusion.2
  70.9 1.3 %collective-permute-start.28 = (bf16[64,2048]{1,0:T(8,128)(2,1)S(1)}, bf16[64,2048]{1,0:T(8,128)(2,1)S(1)}, u32[]{:S(2)}, u32[]{:S(2)}) collective-permute-start(bf16[64,2048]{1,0:T(8,128)(2,1)S(1)} %add_convert_fusion.2), channel_id=1, source_target_pairs={{0,4},{1,3},{4,8},{5,1},{8,12},{9,5},{12,14},{13,9},{14,10},{15,13... | collective-permute-start | bytes 786440 | tf_op jit(solution)/shard_map/ppermute | solution.py:247
  72.2 1.4 %collective-permute-done.21 = bf16[64,2048]{1,0:T(8,128)(2,1)S(1)} collective-permute-done((bf16[64,2048]{1,0:T(8,128)(2,1)S(1)}, bf16[64,2048]{1,0:T(8,128)(2,1)S(1)}, u32[]{:S(2)}, u32[]{:S(2)}) %collective-permute-start.21) | collective-permute-done | bytes 262176 | tf_op jit(solution)/shard_map/ppermute | solution.py:246
  73.6 0.1 add_convert_fusion.5
  73.7 1.3 %collective-permute-start.22 = (bf16[64,2048]{1,0:T(8,128)(2,1)S(1)}, bf16[64,2048]{1,0:T(8,128)(2,1)S(1)}, u32[]{:S(2)}, u32[]{:S(2)}) collective-permute-start(bf16[64,2048]{1,0:T(8,128)(2,1)S(1)} %add_convert_fusion.5), channel_id=1, source_target_pairs={{0,4},{1,3},{4,8},{5,1},{8,12},{9,5},{12,14},{13,9},{14,10},{15,13... | collective-permute-start | bytes 786440 | tf_op jit(solution)/shard_map/ppermute | solution.py:246
  75.0 2.0 %expert.7 = (bf16[64,2048]{1,0:T(8,128)(2,1)S(1)}, bf16[64,2048]{1,0:T(8,128)(2,1)S(1)}) custom-call(s32[1]{0:T(128)} %bitcast.own_ref, bf16[64,2176]{1,0:T(8,128)(2,1)S(1)} %copy-done.6, bf16[64,2176]{1,0:T(8,128)(2,1)S(1)} %collective-permute-done.1.refs_1_, bf16[1,2048,768]{2,1,0:T(8,128)(2,1)S(1)} %get-tuple-element.31.refs_4_.refs_6_.refs_2_, ...), custom_call_target="tpu_custom_call" | custom-call | flops 262144 | bytes 262144 | tf_op jit(solution)/shard_map/expert/pallas_call | solution.py:115
  77.0 0.3 collective-permute-done.28
  77.3 0.1 add_convert_fusion.1
  77.4 0.1 collective-permute-start.29
  77.5 2.7 %collective-permute-done.22 = bf16[64,2048]{1,0:T(8,128)(2,1)S(1)} collective-permute-done((bf16[64,2048]{1,0:T(8,128)(2,1)S(1)}, bf16[64,2048]{1,0:T(8,128)(2,1)S(1)}, u32[]{:S(2)}, u32[]{:S(2)}) %collective-permute-start.22) | collective-permute-done | bytes 262176 | tf_op jit(solution)/shard_map/ppermute | solution.py:246
  80.2 0.8 add_convert_fusion
  (37 shorter events, 0.1 us)
Async XLA Ops:
  1.7 3.2 %collective-permute-start.1 = (bf16[64,2176]{1,0:T(8,128)(2,1)}, bf16[64,2176]{1,0:T(8,128)(2,1)S(1)}, u32[]{:S(2)}, u32[]{:S(2)}) collective-permute-start(bf16[64,2176]{1,0:T(8,128)(2,1)} %pack.1.refs_0_), channel_id=1, source_target_pairs={{0,1},{1,0},{2,3},{3,2},{4,5},{5,4},{6,7},{7,6},{8,9},{9,8},{10,11... | collective-permute-start | bytes 835592 | tf_op jit(solution)/shard_map/ppermute | solution.py:224
  2.2 11.5 %collective-permute-start = (bf16[64,2176]{1,0:T(8,128)(2,1)}, bf16[64,2176]{1,0:T(8,128)(2,1)}, u32[]{:S(2)}, u32[]{:S(2)}) collective-permute-start(bf16[64,2176]{1,0:T(8,128)(2,1)} %pack.1.refs_0_), channel_id=1, source_target_pairs={{0,4},{1,3},{4,8},{5,1},{8,12},{9,5},{12,14},{13,9},{14,10},{15,13... | collective-permute-start | bytes 835592 | tf_op jit(solution)/shard_map/ppermute | solution.py:225
  4.9 10.5 %collective-permute-start.7 = (bf16[64,2176]{1,0:T(8,128)(2,1)S(1)}, bf16[64,2176]{1,0:T(8,128)(2,1)}, u32[]{:S(2)}, u32[]{:S(2)}) collective-permute-start(bf16[64,2176]{1,0:T(8,128)(2,1)S(1)} %collective-permute-done.1.refs_1_), channel_id=1, source_target_pairs={{0,4},{1,3},{4,8},{5,1},{8,12},{9,5},{12,14},{13,9},{14,10},{15,13... | collective-permute-start | bytes 835592 | tf_op jit(solution)/shard_map/ppermute | solution.py:225
  10.4 1.6 %copy-start = (bf16[1,2048,768]{2,1,0:T(8,128)(2,1)}, bf16[1,2048,768]{2,1,0:T(8,128)(2,1)S(1)}, u32[]{:S(2)}) copy-start(bf16[1,2048,768]{2,1,0:T(8,128)(2,1)S(1)} %get-tuple-element.33.refs_5_.refs_7_.refs_3_) | copy-start | bytes 9437188
  12.1 1.7 %copy-start.3 = (bf16[1,2048,768]{2,1,0:T(8,128)(2,1)}, bf16[1,2048,768]{2,1,0:T(8,128)(2,1)S(1)}, u32[]{:S(2)}) copy-start(bf16[1,2048,768]{2,1,0:T(8,128)(2,1)S(1)} %get-tuple-element.34.refs_6_.refs_8_.refs_4_) | copy-start | bytes 9437188
  13.8 6.8 %collective-permute-start.3 = (bf16[64,2176]{1,0:T(8,128)(2,1)}, bf16[64,2176]{1,0:T(8,128)(2,1)S(1)}, u32[]{:S(2)}, u32[]{:S(2)}) collective-permute-start(bf16[64,2176]{1,0:T(8,128)(2,1)} %collective-permute-done.refs_2_), channel_id=1, source_target_pairs={{0,4},{1,3},{4,8},{5,1},{8,12},{9,5},{12,14},{13,9},{14,10},{15,13... | collective-permute-start | bytes 835592 | tf_op jit(solution)/shard_map/ppermute | solution.py:234
  15.4 8.3 %collective-permute-start.8 = (bf16[64,2176]{1,0:T(8,128)(2,1)}, bf16[64,2176]{1,0:T(8,128)(2,1)}, u32[]{:S(2)}, u32[]{:S(2)}) collective-permute-start(bf16[64,2176]{1,0:T(8,128)(2,1)} %collective-permute-done.7.refs_3_), channel_id=1, source_target_pairs={{0,4},{1,3},{4,8},{5,1},{8,12},{9,5},{12,14},{13,9},{14,10},{15,13... | collective-permute-start | bytes 835592 | tf_op jit(solution)/shard_map/ppermute | solution.py:232
  20.5 6.7 %collective-permute-start.4 = (bf16[64,2176]{1,0:T(8,128)(2,1)S(1)}, bf16[64,2176]{1,0:T(8,128)(2,1)}, u32[]{:S(2)}, u32[]{:S(2)}) collective-permute-start(bf16[64,2176]{1,0:T(8,128)(2,1)S(1)} %collective-permute-done.3.refs_2_), channel_id=1, source_target_pairs={{0,4},{1,3},{4,8},{5,1},{8,12},{9,5},{12,14},{13,9},{14,10},{15,13... | collective-permute-start | bytes 835592 | tf_op jit(solution)/shard_map/ppermute | solution.py:234
  22.1 5.1 %collective-permute-start.6 = (bf16[64,2176]{1,0:T(8,128)(2,1)S(1)}, bf16[64,2176]{1,0:T(8,128)(2,1)S(1)}, u32[]{:S(2)}, u32[]{:S(2)}) collective-permute-start(bf16[64,2176]{1,0:T(8,128)(2,1)S(1)} %collective-permute-done.3.refs_2_), channel_id=1, source_target_pairs={{0,1},{1,0},{2,3},{3,2},{4,5},{5,4},{6,7},{7,6},{8,9},{9,8},{10,11... | collective-permute-start | bytes 835592 | tf_op jit(solution)/shard_map/ppermute | solution.py:233
  22.1 0.7 copy-start.7
  23.6 5.9 %collective-permute-start.9 = (bf16[64,2176]{1,0:T(8,128)(2,1)}, bf16[64,2176]{1,0:T(8,128)(2,1)S(1)}, u32[]{:S(2)}, u32[]{:S(2)}) collective-permute-start(bf16[64,2176]{1,0:T(8,128)(2,1)} %collective-permute-done.8.refs_3_), channel_id=1, source_target_pairs={{0,1},{1,0},{2,3},{3,2},{4,5},{5,4},{6,7},{7,6},{8,9},{9,8},{10,11... | collective-permute-start | bytes 835592 | tf_op jit(solution)/shard_map/ppermute | solution.py:233
  23.6 18.4 %collective-permute-start.2 = (bf16[64,2176]{1,0:T(8,128)(2,1)}, bf16[64,2176]{1,0:T(8,128)(2,1)}, u32[]{:S(2)}, u32[]{:S(2)}) collective-permute-start(bf16[64,2176]{1,0:T(8,128)(2,1)} %collective-permute-done.refs_2_), channel_id=1, source_target_pairs={{0,1},{1,0},{2,3},{3,2},{4,5},{5,4},{6,7},{7,6},{8,9},{9,8},{10,11... | collective-permute-start | bytes 835592 | tf_op jit(solution)/shard_map/ppermute | solution.py:233
  24.1 17.9 %collective-permute-start.10 = (bf16[64,2176]{1,0:T(8,128)(2,1)}, bf16[64,2176]{1,0:T(8,128)(2,1)}, u32[]{:S(2)}, u32[]{:S(2)}) collective-permute-start(bf16[64,2176]{1,0:T(8,128)(2,1)} %collective-permute-done.7.refs_3_), channel_id=1, source_target_pairs={{0,1},{1,0},{2,3},{3,2},{4,5},{5,4},{6,7},{7,6},{8,9},{9,8},{10,11... | collective-permute-start | bytes 835592 | tf_op jit(solution)/shard_map/ppermute | solution.py:233
  27.2 14.9 %collective-permute-start.11 = (bf16[64,2176]{1,0:T(8,128)(2,1)}, bf16[64,2176]{1,0:T(8,128)(2,1)}, u32[]{:S(2)}, u32[]{:S(2)}) collective-permute-start(bf16[64,2176]{1,0:T(8,128)(2,1)} %collective-permute-done.4.refs_4_), channel_id=1, source_target_pairs={{0,1},{1,0},{2,3},{3,2},{4,5},{5,4},{6,7},{7,6},{8,9},{9,8},{10,11... | collective-permute-start | bytes 835592 | tf_op jit(solution)/shard_map/ppermute | solution.py:233
  27.2 0.7 copy-start.9
  27.9 14.2 %collective-permute-start.5 = (bf16[64,2176]{1,0:T(8,128)(2,1)}, bf16[64,2176]{1,0:T(8,128)(2,1)}, u32[]{:S(2)}, u32[]{:S(2)}) collective-permute-start(bf16[64,2176]{1,0:T(8,128)(2,1)} %collective-permute-done.4.refs_4_), channel_id=1, source_target_pairs={{0,4},{1,3},{4,8},{5,1},{8,12},{9,5},{12,14},{13,9},{14,10},{15,13... | collective-permute-start | bytes 835592 | tf_op jit(solution)/shard_map/ppermute | solution.py:234
  29.5 0.7 copy-start.11
  30.2 11.9 %collective-permute-start.13 = (bf16[64,2176]{1,0:T(8,128)(2,1)}, bf16[64,2176]{1,0:T(8,128)(2,1)}, u32[]{:S(2)}, u32[]{:S(2)}) collective-permute-start(bf16[64,2176]{1,0:T(8,128)(2,1)} %collective-permute-done.8.refs_3_), channel_id=1, source_target_pairs={{0,4},{1,3},{4,8},{5,1},{8,12},{9,5},{12,14},{13,9},{14,10},{15,13... | collective-permute-start | bytes 835592 | tf_op jit(solution)/shard_map/ppermute | solution.py:232
  31.8 1.9 %copy-start.1 = (bf16[1,2048,768]{2,1,0:T(8,128)(2,1)S(1)}, bf16[1,2048,768]{2,1,0:T(8,128)(2,1)}, u32[]{:S(2)}) copy-start(bf16[1,2048,768]{2,1,0:T(8,128)(2,1)} %copy-done) | copy-start | bytes 9437188
  33.7 1.9 %copy-start.4 = (bf16[1,2048,768]{2,1,0:T(8,128)(2,1)S(1)}, bf16[1,2048,768]{2,1,0:T(8,128)(2,1)}, u32[]{:S(2)}) copy-start(bf16[1,2048,768]{2,1,0:T(8,128)(2,1)} %copy-done.3) | copy-start | bytes 9437188
  35.6 1.0 %copy-start.8 = (bf16[64,2176]{1,0:T(8,128)(2,1)S(1)}, bf16[64,2176]{1,0:T(8,128)(2,1)}, u32[]{:S(2)}) copy-start(bf16[64,2176]{1,0:T(8,128)(2,1)} %copy-done.7) | copy-start | bytes 835588
  36.5 1.0 %copy-start.10 = (bf16[64,2176]{1,0:T(8,128)(2,1)S(1)}, bf16[64,2176]{1,0:T(8,128)(2,1)}, u32[]{:S(2)}) copy-start(bf16[64,2176]{1,0:T(8,128)(2,1)} %copy-done.9) | copy-start | bytes 835588
  37.5 1.0 %copy-start.12 = (bf16[64,2176]{1,0:T(8,128)(2,1)S(1)}, bf16[64,2176]{1,0:T(8,128)(2,1)}, u32[]{:S(2)}) copy-start(bf16[64,2176]{1,0:T(8,128)(2,1)} %copy-done.11) | copy-start | bytes 835588
  42.1 1.8 %collective-permute-start.14 = (bf16[64,2176]{1,0:T(8,128)(2,1)}, bf16[64,2176]{1,0:T(8,128)(2,1)S(1)}, u32[]{:S(2)}, u32[]{:S(2)}) collective-permute-start(bf16[64,2176]{1,0:T(8,128)(2,1)} %collective-permute-done.13.refs_5_), channel_id=1, source_target_pairs={{0,1},{1,0},{2,3},{3,2},{4,5},{5,4},{6,7},{7,6},{8,9},{9,8},{10,11... | collective-permute-start | bytes 835592 | tf_op jit(solution)/shard_map/ppermute | solution.py:233
  42.2 2.2 %collective-permute-start.12 = (bf16[64,2176]{1,0:T(8,128)(2,1)}, bf16[64,2176]{1,0:T(8,128)(2,1)S(1)}, u32[]{:S(2)}, u32[]{:S(2)}) collective-permute-start(bf16[64,2176]{1,0:T(8,128)(2,1)} %collective-permute-done.5.refs_1_), channel_id=1, source_target_pairs={{0,1},{1,0},{2,3},{3,2},{4,5},{5,4},{6,7},{7,6},{8,9},{9,8},{10,11... | collective-permute-start | bytes 835592 | tf_op jit(solution)/shard_map/ppermute | solution.py:237
  49.4 1.6 %collective-permute-start.15 = (bf16[64,2048]{1,0:T(8,128)(2,1)S(1)}, bf16[64,2048]{1,0:T(8,128)(2,1)S(1)}, u32[]{:S(2)}, u32[]{:S(2)}) collective-permute-start(bf16[64,2048]{1,0:T(8,128)(2,1)S(1)} %get-tuple-element.38), channel_id=1, source_target_pairs={{0,1},{1,0},{2,3},{3,2},{4,5},{5,4},{6,7},{7,6},{8,9},{9,8},{10,11... | collective-permute-start | bytes 786440 | tf_op jit(solution)/shard_map/ppermute | solution.py:238
  49.6 3.5 %collective-permute-start.24 = (bf16[64,2048]{1,0:T(8,128)(2,1)S(1)}, bf16[64,2048]{1,0:T(8,128)(2,1)S(1)}, u32[]{:S(2)}, u32[]{:S(2)}) collective-permute-start(bf16[64,2048]{1,0:T(8,128)(2,1)S(1)} %get-tuple-element.48), channel_id=1, source_target_pairs={{0,1},{1,0},{2,3},{3,2},{4,5},{5,4},{6,7},{7,6},{8,9},{9,8},{10,11... | collective-permute-start | bytes 786440 | tf_op jit(solution)/shard_map/ppermute | solution.py:245
  51.0 6.4 %collective-permute-start.16 = (bf16[64,2048]{1,0:T(8,128)(2,1)S(1)}, bf16[64,2048]{1,0:T(8,128)(2,1)S(1)}, u32[]{:S(2)}, u32[]{:S(2)}) collective-permute-start(bf16[64,2048]{1,0:T(8,128)(2,1)S(1)} %add_convert_fusion.8), channel_id=1, source_target_pairs={{0,4},{1,3},{4,8},{5,1},{8,12},{9,5},{12,14},{13,9},{14,10},{15,13... | collective-permute-start | bytes 786440 | tf_op jit(solution)/shard_map/ppermute | solution.py:238
  52.6 13.1 %collective-permute-start.18 = (bf16[64,2048]{1,0:T(8,128)(2,1)S(1)}, bf16[64,2048]{1,0:T(8,128)(2,1)S(1)}, u32[]{:S(2)}, u32[]{:S(2)}) collective-permute-start(bf16[64,2048]{1,0:T(8,128)(2,1)S(1)} %get-tuple-element.43), channel_id=1, source_target_pairs={{0,1},{1,0},{2,3},{3,2},{4,5},{5,4},{6,7},{7,6},{8,9},{9,8},{10,11... | collective-permute-start | bytes 786440 | tf_op jit(solution)/shard_map/ppermute | solution.py:245
  52.6 11.7 %collective-permute-start.23 = (bf16[64,2048]{1,0:T(8,128)(2,1)S(1)}, bf16[64,2048]{1,0:T(8,128)(2,1)S(1)}, u32[]{:S(2)}, u32[]{:S(2)}) collective-permute-start(bf16[64,2048]{1,0:T(8,128)(2,1)S(1)} %get-tuple-element.46), channel_id=1, source_target_pairs={{0,1},{1,0},{2,3},{3,2},{4,5},{5,4},{6,7},{7,6},{8,9},{9,8},{10,11... | collective-permute-start | bytes 786440 | tf_op jit(solution)/shard_map/ppermute | solution.py:245
  53.1 6.0 %collective-permute-start.19 = (bf16[64,2048]{1,0:T(8,128)(2,1)S(1)}, bf16[64,2048]{1,0:T(8,128)(2,1)S(1)}, u32[]{:S(2)}, u32[]{:S(2)}) collective-permute-start(bf16[64,2048]{1,0:T(8,128)(2,1)S(1)} %get-tuple-element.45), channel_id=1, source_target_pairs={{0,1},{1,0},{2,3},{3,2},{4,5},{5,4},{6,7},{7,6},{8,9},{9,8},{10,11... | collective-permute-start | bytes 786440 | tf_op jit(solution)/shard_map/ppermute | solution.py:245
  57.6 6.4 %collective-permute-start.25 = (bf16[64,2048]{1,0:T(8,128)(2,1)S(1)}, bf16[64,2048]{1,0:T(8,128)(2,1)S(1)}, u32[]{:S(2)}, u32[]{:S(2)}) collective-permute-start(bf16[64,2048]{1,0:T(8,128)(2,1)S(1)} %add_convert_fusion.4), channel_id=1, source_target_pairs={{0,4},{1,3},{4,8},{5,1},{8,12},{9,5},{12,14},{13,9},{14,10},{15,13... | collective-permute-start | bytes 786440 | tf_op jit(solution)/shard_map/ppermute | solution.py:247
  59.2 7.6 %collective-permute-start.20 = (bf16[64,2048]{1,0:T(8,128)(2,1)S(1)}, bf16[64,2048]{1,0:T(8,128)(2,1)S(1)}, u32[]{:S(2)}, u32[]{:S(2)}) collective-permute-start(bf16[64,2048]{1,0:T(8,128)(2,1)S(1)} %add_convert_fusion.7), channel_id=1, source_target_pairs={{0,4},{1,3},{4,8},{5,1},{8,12},{9,5},{12,14},{13,9},{14,10},{15,13... | collective-permute-start | bytes 786440 | tf_op jit(solution)/shard_map/ppermute | solution.py:246
  59.7 15.3 %copy-start.5 = (bf16[1,2048,768]{2,1,0:T(8,128)(2,1)S(1)}, bf16[1,2048,768]{2,1,0:T(8,128)(2,1)}, u32[]{:S(2)}) copy-start(bf16[1,2048,768]{2,1,0:T(8,128)(2,1)} %copy-done.3) | copy-start | bytes 9437188
  63.7 11.3 %copy-start.2 = (bf16[1,2048,768]{2,1,0:T(8,128)(2,1)S(1)}, bf16[1,2048,768]{2,1,0:T(8,128)(2,1)}, u32[]{:S(2)}) copy-start(bf16[1,2048,768]{2,1,0:T(8,128)(2,1)} %copy-done) | copy-start | bytes 9437188
  63.7 11.3 %copy-start.6 = (bf16[64,2176]{1,0:T(8,128)(2,1)S(1)}, bf16[64,2176]{1,0:T(8,128)(2,1)}, u32[]{:S(2)}) copy-start(bf16[64,2176]{1,0:T(8,128)(2,1)} %pack.1.refs_0_) | copy-start | bytes 835588
  63.7 8.5 %collective-permute-start.17 = (bf16[64,2048]{1,0:T(8,128)(2,1)S(1)}, bf16[64,2048]{1,0:T(8,128)(2,1)S(1)}, u32[]{:S(2)}, u32[]{:S(2)}) collective-permute-start(bf16[64,2048]{1,0:T(8,128)(2,1)S(1)} %get-tuple-element.41), channel_id=1, source_target_pairs={{0,1},{1,0},{2,3},{3,2},{4,5},{5,4},{6,7},{7,6},{8,9},{9,8},{10,11... | collective-permute-start | bytes 786440 | tf_op jit(solution)/shard_map/ppermute | solution.py:245
  64.0 4.5 %collective-permute-start.27 = (bf16[64,2048]{1,0:T(8,128)(2,1)S(1)}, bf16[64,2048]{1,0:T(8,128)(2,1)S(1)}, u32[]{:S(2)}, u32[]{:S(2)}) collective-permute-start(bf16[64,2048]{1,0:T(8,128)(2,1)S(1)} %get-tuple-element.53), channel_id=1, source_target_pairs={{0,1},{1,0},{2,3},{3,2},{4,5},{5,4},{6,7},{7,6},{8,9},{9,8},{10,11... | collective-permute-start | bytes 786440 | tf_op jit(solution)/shard_map/ppermute | solution.py:245
  64.4 6.4 %collective-permute-start.26 = (bf16[64,2048]{1,0:T(8,128)(2,1)S(1)}, bf16[64,2048]{1,0:T(8,128)(2,1)S(1)}, u32[]{:S(2)}, u32[]{:S(2)}) collective-permute-start(bf16[64,2048]{1,0:T(8,128)(2,1)S(1)} %add_convert_fusion.3), channel_id=1, source_target_pairs={{0,4},{1,3},{4,8},{5,1},{8,12},{9,5},{12,14},{13,9},{14,10},{15,13... | collective-permute-start | bytes 786440 | tf_op jit(solution)/shard_map/ppermute | solution.py:247
  66.9 6.7 %collective-permute-start.21 = (bf16[64,2048]{1,0:T(8,128)(2,1)S(1)}, bf16[64,2048]{1,0:T(8,128)(2,1)S(1)}, u32[]{:S(2)}, u32[]{:S(2)}) collective-permute-start(bf16[64,2048]{1,0:T(8,128)(2,1)S(1)} %add_convert_fusion.6), channel_id=1, source_target_pairs={{0,4},{1,3},{4,8},{5,1},{8,12},{9,5},{12,14},{13,9},{14,10},{15,13... | collective-permute-start | bytes 786440 | tf_op jit(solution)/shard_map/ppermute | solution.py:246
  70.9 6.4 %collective-permute-start.28 = (bf16[64,2048]{1,0:T(8,128)(2,1)S(1)}, bf16[64,2048]{1,0:T(8,128)(2,1)S(1)}, u32[]{:S(2)}, u32[]{:S(2)}) collective-permute-start(bf16[64,2048]{1,0:T(8,128)(2,1)S(1)} %add_convert_fusion.2), channel_id=1, source_target_pairs={{0,4},{1,3},{4,8},{5,1},{8,12},{9,5},{12,14},{13,9},{14,10},{15,13... | collective-permute-start | bytes 786440 | tf_op jit(solution)/shard_map/ppermute | solution.py:247
  73.7 6.4 %collective-permute-start.22 = (bf16[64,2048]{1,0:T(8,128)(2,1)S(1)}, bf16[64,2048]{1,0:T(8,128)(2,1)S(1)}, u32[]{:S(2)}, u32[]{:S(2)}) collective-permute-start(bf16[64,2048]{1,0:T(8,128)(2,1)S(1)} %add_convert_fusion.5), channel_id=1, source_target_pairs={{0,4},{1,3},{4,8},{5,1},{8,12},{9,5},{12,14},{13,9},{14,10},{15,13... | collective-permute-start | bytes 786440 | tf_op jit(solution)/shard_map/ppermute | solution.py:246
  77.4 2.7 %collective-permute-start.29 = (bf16[64,2048]{1,0:T(8,128)(2,1)S(1)}, bf16[64,2048]{1,0:T(8,128)(2,1)S(1)}, u32[]{:S(2)}, u32[]{:S(2)}) collective-permute-start(bf16[64,2048]{1,0:T(8,128)(2,1)S(1)} %add_convert_fusion.1), channel_id=1, source_target_pairs={{0,1},{1,0},{2,3},{3,2},{4,5},{5,4},{6,7},{7,6},{8,9},{9,8},{10,11... | collective-permute-start | bytes 786440 | tf_op jit(solution)/shard_map/ppermute | solution.py:250

commit v6 on v5

--- a/solution.py
+++ b/solution.py
@@ -118,7 +118,7 @@
         in_specs=[pl.BlockSpec(memory_space=pltpu.SMEM)] + [vmem] * (len(blocks) + 3),
         out_specs=[vmem] * len(blocks),
         scratch_shapes=[pltpu.VMEM((rows, wide), jnp.bfloat16), pltpu.VMEM((rows, ff), jnp.bfloat16)],
-        compiler_params=pltpu.CompilerParams(vmem_limit_bytes=30 << 20),
+        compiler_params=pltpu.CompilerParams(vmem_limit_bytes=16 << 20),
         cost_estimate=pl.CostEstimate(
             flops=rows * width, bytes_accessed=rows * width, transcendentals=0
         ),
@@ -127,9 +127,10 @@
 
 
 def load_kernel(pieces, *refs):
-    done = refs[6]
+    *arrays, done = refs
+    count = len(arrays) // 2
     copies = []
-    for source, target in zip(refs[:3], refs[3:6]):
+    for source, target in zip(arrays[:count], arrays[count:]):
         depth = source.shape[1] // pieces
         for piece in range(pieces):
             part = pl.ds(piece * depth, depth)
@@ -147,10 +148,10 @@
     return pl.pallas_call(
         functools.partial(load_kernel, pieces),
         out_shape=[pltpu.VMEM(w.shape, w.dtype) for w in weights],
-        in_specs=[pl.BlockSpec(memory_space=pltpu.HBM)] * 3,
-        out_specs=[pl.BlockSpec(memory_space=pltpu.VMEM)] * 3,
-        scratch_shapes=[pltpu.SemaphoreType.DMA((3 * pieces,))],
-        compiler_params=pltpu.CompilerParams(vmem_limit_bytes=30 << 20),
+        in_specs=[pl.BlockSpec(memory_space=pltpu.HBM)] * len(weights),
+        out_specs=[pl.BlockSpec(memory_space=pltpu.VMEM)] * len(weights),
+        scratch_shapes=[pltpu.SemaphoreType.DMA((len(weights) * pieces,))],
+        compiler_params=pltpu.CompilerParams(vmem_limit_bytes=16 << 20),
         cost_estimate=pl.CostEstimate(flops=0, bytes_accessed=1024, transcendentals=0),
         name="load",
     )(*[pltpu.with_memory_space_constraint(w, pltpu.HBM) for w in weights])
@@ -220,11 +221,13 @@
     ring = functools.partial(lax.ppermute, axis_name="expert", perm=ring_pairs(experts))
     own = lax.axis_index("expert").reshape(1)
 
-    mine = pack(tokens, expert_ids, router_weights, experts)
+    mine = pack(after(tokens, own), expert_ids, router_weights, experts)
     sibling = swap(mine)
     first, second = ring(mine), ring(sibling)
-    weights = load_weights((after(w_gate, sibling), w_up, w_down))
-    first = after(first, weights[0])
+    gate_w, up_w = load_weights((after(w_gate, sibling), w_up))
+    first = after(first, gate_w)
+    down_w, = load_weights((after(w_down, first),))
+    weights = [gate_w, up_w, down_w]
     run = lambda *blocks: run_expert(own, blocks, weights, experts)
     blocks = {}
     for step in range(1, rounds):
@@ -232,6 +235,8 @@
             second = ring(second)
         blocks[step] = (swap(first), swap(second), first, second)
         first = ring(first)
+        if step == 1:
+            first = after(first, down_w)
     sums = {2: run(*blocks[2])}
     first = after(first, sums[2][0], *blocks[1][:2], blocks[3][0])
     keep, send, *sums[3] = run(swap(first), first, *blocks[3])

time: 81.3 us -> 70.2 us (0.86)
  local copies, waits for them, and re-layouts: 12.1 us -> 0.01 us
  starting transfers between devices: 24.3 us -> 27.9 us
  Pallas kernels: 20.2 us -> 17.7 us
    unnamed x26 -> x2, local copies, waits for them, and re-layouts: 12.1 us -> 0.01 us
    pallas_call x4, Pallas kernels: 14.6 us -> 11.2 us  [run_expert(): pl.pallas_call(functools.partial(expert_kernel, experts, len(blocks)), ou...]
    ppermute x2, waiting for transfers between devices: 0.79 us -> 3.86 us  [dense_body(): second = ring(second)]
    ppermute x3, waiting for transfers between devices: 6.65 us -> 4.2 us  [dense_body(): first = ring(first)]
    ppermute x3, starting transfers between devices: 3.3 us -> 4.93 us  [dense_body(): ring(added(*[keep_trail, send_trail] + ([] if trail is None else [trail])))]
    ppermute x2, waiting for transfers between devices: 0.01 us -> 0.96 us  [dense_body(): first, second = (ring(mine), ring(sibling))]
    pallas_call x1 -> x2, Pallas kernels: 3.85 us -> 4.73 us  [load_weights(): pl.pallas_call(functools.partial(load_kernel, pieces), out_shape=[pltpu.V...]
    ppermute x3, starting transfers between devices: 4.06 us -> 4.93 us  [dense_body(): lead = ring(added(keep, send, lead))]
  transfers between devices with their start and end apart: 30 -> 30, of which waited for: 13 -> 15; matrix products, arithmetic and copies ran while one was open for 1% -> 1% of each run, Pallas kernels for 17% -> 17%
where the time goes in v6:
time: 70.2 us; the launch traced here: 70 us
  starting transfers between devices  27.9 us (40%)
  waiting for transfers between devices  22.7 us (32%)
  Pallas kernels  17.7 us (25%)
  other arithmetic  1.5 us (2%)
    pallas_call x4, Pallas kernels, run_expert(): pl.pallas_call(functools.partial(expert_kernel, experts, len(blocks)), ou...  11.2 us
    ppermute x3, starting transfers between devices, dense_body(): first = ring(first)  5.39 us
    ppermute x2, waiting for transfers between devices, dense_body(): lead, trail = (ring(added(keep, swap(send))), None)  5.26 us
    ppermute x3, starting transfers between devices, dense_body(): ring(added(*[keep_trail, send_trail] + ([] if trail is None else [trail])))  4.93 us
    ppermute x3, starting transfers between devices, dense_body(): lead = ring(added(keep, send, lead))  4.93 us
    pallas_call x2, Pallas kernels, load_weights(): pl.pallas_call(functools.partial(load_kernel, pieces), out_shape=[pltpu.V...  4.73 us
    ppermute x3, waiting for transfers between devices, dense_body(): ring(added(*[keep_trail, send_trail] + ([] if trail is None else [trail])))  4.52 us
    ppermute x2, starting transfers between devices, dense_body(): first, second = (ring(mine), ring(sibling))  4.34 us
  transfers between devices with their start and end apart: 30, of which 15 were waited for; matrix products, arithmetic and copies ran while one was open for 1% of the time, Pallas kernels for 17%

profile of v6, /device:TPU:0, one launch (start us, length us, event | category | flops | bytes accessed | tf_op | source)
XLA Modules:
  0.0 70.0 jit_solution(7684189142041474965)
XLA Ops:
  0.0 1.7 %pack.1.refs_0_ = bf16[64,2176]{1,0:T(8,128)(2,1)} custom-call(bf16[64,2048]{1,0:T(8,128)(2,1)} %tokens_ref, s32[8,64]{1,0:T(8,128)} %bitcast.3, f32[8,64]{1,0:T(8,128)} %bitcast.4), custom_call_target="tpu_custom_call" | custom-call | bytes 1024 | tf_op jit(solution)/shard_map/pack/pallas_call | solution.py:190
  1.7 0.5 collective-permute-start.1
  2.2 2.6 %collective-permute-start = (bf16[64,2176]{1,0:T(8,128)(2,1)}, bf16[64,2176]{1,0:T(8,128)(2,1)S(1)}, u32[]{:S(2)}, u32[]{:S(2)}) collective-permute-start(bf16[64,2176]{1,0:T(8,128)(2,1)} %pack.1.refs_0_), channel_id=1, source_target_pairs={{0,4},{1,3},{4,8},{5,1},{8,12},{9,5},{12,14},{13,9},{14,10},{15,13... | collective-permute-start | bytes 835592 | tf_op jit(solution)/shard_map/ppermute | solution.py:226
  4.9 1.7 %collective-permute-start.7 = (bf16[64,2176]{1,0:T(8,128)(2,1)S(1)}, bf16[64,2176]{1,0:T(8,128)(2,1)S(1)}, u32[]{:S(2)}, u32[]{:S(2)}) collective-permute-start(bf16[64,2176]{1,0:T(8,128)(2,1)S(1)} %collective-permute-done.1.refs_1_), channel_id=1, source_target_pairs={{0,4},{1,3},{4,8},{5,1},{8,12},{9,5},{12,14},{13,9},{14,10},{15,13... | collective-permute-start | bytes 835592 | tf_op jit(solution)/shard_map/ppermute | solution.py:226
  6.6 2.9 %load.2 = (bf16[1,2048,768]{2,1,0:T(8,128)(2,1)S(1)}, bf16[1,2048,768]{2,1,0:T(8,128)(2,1)S(1)}) custom-call(bf16[1,2048,768]{2,1,0:T(8,128)(2,1)} %refs_0_, bf16[1,2048,768]{2,1,0:T(8,128)(2,1)} %refs_1_.1), custom_call_target="tpu_custom_call" | custom-call | bytes 1024 | tf_op jit(solution)/shard_map/load/pallas_call | solution.py:148
  9.4 0.1 collective-permute-done.refs_2_
  9.5 2.1 %collective-permute-start.3 = (bf16[64,2176]{1,0:T(8,128)(2,1)S(1)}, bf16[64,2176]{1,0:T(8,128)(2,1)S(1)}, u32[]{:S(2)}, u32[]{:S(2)}) collective-permute-start(bf16[64,2176]{1,0:T(8,128)(2,1)S(1)} %collective-permute-done.refs_2_), channel_id=1, source_target_pairs={{0,4},{1,3},{4,8},{5,1},{8,12},{9,5},{12,14},{13,9},{14,10},{15,13... | collective-permute-start | bytes 835592 | tf_op jit(solution)/shard_map/ppermute | solution.py:237
  11.6 0.9 %collective-permute-done.7.refs_3_ = bf16[64,2176]{1,0:T(8,128)(2,1)S(1)} collective-permute-done((bf16[64,2176]{1,0:T(8,128)(2,1)S(1)}, bf16[64,2176]{1,0:T(8,128)(2,1)S(1)}, u32[]{:S(2)}, u32[]{:S(2)}) %collective-permute-start.7) | collective-permute-done | bytes 278560 | tf_op jit(solution)/shard_map/ppermute | solution.py:226
  12.5 2.1 %collective-permute-start.8 = (bf16[64,2176]{1,0:T(8,128)(2,1)S(1)}, bf16[64,2176]{1,0:T(8,128)(2,1)S(1)}, u32[]{:S(2)}, u32[]{:S(2)}) collective-permute-start(bf16[64,2176]{1,0:T(8,128)(2,1)S(1)} %collective-permute-done.7.refs_3_), channel_id=1, source_target_pairs={{0,4},{1,3},{4,8},{5,1},{8,12},{9,5},{12,14},{13,9},{14,10},{15,13... | collective-permute-start | bytes 835592 | tf_op jit(solution)/shard_map/ppermute | solution.py:235
  14.6 1.9 %load.3.refs_6_.refs_8_.refs_4_ = bf16[1,2048,768]{2,1,0:T(8,128)(2,1)S(1)} custom-call(bf16[1,2048,768]{2,1,0:T(8,128)(2,1)} %refs_0_.1), custom_call_target="tpu_custom_call" | custom-call | bytes 1024 | tf_op jit(solution)/shard_map/load/pallas_call | solution.py:148
  16.5 0.0 collective-permute-done.3.refs_2_
  16.5 1.7 %collective-permute-start.4 = (bf16[64,2176]{1,0:T(8,128)(2,1)S(1)}, bf16[64,2176]{1,0:T(8,128)(2,1)S(1)}, u32[]{:S(2)}, u32[]{:S(2)}) collective-permute-start(bf16[64,2176]{1,0:T(8,128)(2,1)S(1)} %collective-permute-done.3.refs_2_), channel_id=1, source_target_pairs={{0,4},{1,3},{4,8},{5,1},{8,12},{9,5},{12,14},{13,9},{14,10},{15,13... | collective-permute-start | bytes 835592 | tf_op jit(solution)/shard_map/ppermute | solution.py:237
  18.2 0.0 collective-permute-start.6
  18.2 0.9 %collective-permute-done.8.refs_3_ = bf16[64,2176]{1,0:T(8,128)(2,1)S(1)} collective-permute-done((bf16[64,2176]{1,0:T(8,128)(2,1)S(1)}, bf16[64,2176]{1,0:T(8,128)(2,1)S(1)}, u32[]{:S(2)}, u32[]{:S(2)}) %collective-permute-start.8) | collective-permute-done | bytes 278560 | tf_op jit(solution)/shard_map/ppermute | solution.py:235
  19.1 0.0 collective-permute-start.9
  19.1 0.5 collective-permute-start.2
  19.6 0.0 collective-permute-start.10
  19.6 3.5 %collective-permute-done.4.refs_4_ = bf16[64,2176]{1,0:T(8,128)(2,1)S(1)} collective-permute-done((bf16[64,2176]{1,0:T(8,128)(2,1)S(1)}, bf16[64,2176]{1,0:T(8,128)(2,1)S(1)}, u32[]{:S(2)}, u32[]{:S(2)}) %collective-permute-start.4) | collective-permute-done | bytes 278560 | tf_op jit(solution)/shard_map/ppermute | solution.py:237
  23.1 0.0 collective-permute-start.11
  23.1 1.6 %collective-permute-start.5 = (bf16[64,2176]{1,0:T(8,128)(2,1)S(1)}, bf16[64,2176]{1,0:T(8,128)(2,1)S(1)}, u32[]{:S(2)}, u32[]{:S(2)}) collective-permute-start(bf16[64,2176]{1,0:T(8,128)(2,1)S(1)} %collective-permute-done.4.refs_4_), channel_id=1, source_target_pairs={{0,4},{1,3},{4,8},{5,1},{8,12},{9,5},{12,14},{13,9},{14,10},{15,13... | collective-permute-start | bytes 835592 | tf_op jit(solution)/shard_map/ppermute | solution.py:237
  24.7 0.0 collective-permute-done.9.refs_1_
  24.7 1.6 %collective-permute-start.13 = (bf16[64,2176]{1,0:T(8,128)(2,1)S(1)}, bf16[64,2176]{1,0:T(8,128)(2,1)S(1)}, u32[]{:S(2)}, u32[]{:S(2)}) collective-permute-start(bf16[64,2176]{1,0:T(8,128)(2,1)S(1)} %collective-permute-done.8.refs_3_), channel_id=1, source_target_pairs={{0,4},{1,3},{4,8},{5,1},{8,12},{9,5},{12,14},{13,9},{14,10},{15,13... | collective-permute-start | bytes 835592 | tf_op jit(solution)/shard_map/ppermute | solution.py:235
  26.3 2.6 %expert.4 = (bf16[64,2048]{1,0:T(8,128)(2,1)S(1)}, bf16[64,2048]{1,0:T(8,128)(2,1)S(1)}, bf16[64,2048]{1,0:T(8,128)(2,1)S(1)}, bf16[64,2048]{1,0:T(8,128)(2,1)S(1)}) custom-call(s32[1]{0:T(128)} %bitcast.own_ref, bf16[64,2176]{1,0:T(8,128)(2,1)S(1)} %collective-permute-done.6.refs_0_, bf16[64,2176]{1,0:T(8,128)(2,1)S(1)} %collective-permute-done.9.refs_1_, ...), custom_call_target="tpu_custom_call" | custom-call | flops 524288 | bytes 524288 | tf_op jit(solution)/shard_map/expert/pallas_call | solution.py:115
  29.0 0.0 collective-permute-done.10.refs_1_
  29.0 0.7 collective-permute-done.5.refs_1_
  29.7 3.0 %collective-permute-done.13.refs_5_ = bf16[64,2176]{1,0:T(8,128)(2,1)S(1)} collective-permute-done((bf16[64,2176]{1,0:T(8,128)(2,1)S(1)}, bf16[64,2176]{1,0:T(8,128)(2,1)S(1)}, u32[]{:S(2)}, u32[]{:S(2)}) %collective-permute-start.13) | collective-permute-done | bytes 278560 | tf_op jit(solution)/shard_map/ppermute | solution.py:235
  32.6 0.0 collective-permute-start.14
  32.6 0.5 collective-permute-start.12
  33.2 1.0 %collective-permute-done.14.refs_3_ = bf16[64,2176]{1,0:T(8,128)(2,1)S(1)} collective-permute-done((bf16[64,2176]{1,0:T(8,128)(2,1)S(1)}, bf16[64,2176]{1,0:T(8,128)(2,1)S(1)}, u32[]{:S(2)}, u32[]{:S(2)}) %collective-permute-start.14) | collective-permute-done | bytes 278560 | tf_op jit(solution)/shard_map/ppermute | solution.py:236
  34.2 0.4 collective-permute-done.12.refs_0_
  34.6 3.9 %expert.5 = (bf16[64,2048]{1,0:T(8,128)(2,1)S(1)}, bf16[64,2048]{1,0:T(8,128)(2,1)S(1)}, bf16[64,2048]{1,0:T(8,128)(2,1)S(1)}, bf16[64,2048]{1,0:T(8,128)(2,1)S(...) custom-call(s32[1]{0:T(128)} %bitcast.own_ref, bf16[64,2176]{1,0:T(8,128)(2,1)S(1)} %collective-permute-done.12.refs_0_, ...), custom_call_target="tpu_custom_call" | custom-call | flops 786432 | bytes 786432 | tf_op jit(solution)/shard_map/expert/pallas_call | solution.py:115
  38.5 0.2 collective-permute-start.15
  38.7 0.4 collective-permute-start.24
  39.1 1.0 %collective-permute-done.15 = bf16[64,2048]{1,0:T(8,128)(2,1)S(1)} collective-permute-done((bf16[64,2048]{1,0:T(8,128)(2,1)S(1)}, bf16[64,2048]{1,0:T(8,128)(2,1)S(1)}, u32[]{:S(2)}, u32[]{:S(2)}) %collective-permute-start.15) | collective-permute-done | bytes 262176 | tf_op jit(solution)/shard_map/ppermute | solution.py:243
  40.1 0.1 add_convert_fusion.8
  40.2 1.7 %collective-permute-start.16 = (bf16[64,2048]{1,0:T(8,128)(2,1)S(1)}, bf16[64,2048]{1,0:T(8,128)(2,1)S(1)}, u32[]{:S(2)}, u32[]{:S(2)}) collective-permute-start(bf16[64,2048]{1,0:T(8,128)(2,1)S(1)} %add_convert_fusion.8), channel_id=1, source_target_pairs={{0,4},{1,3},{4,8},{5,1},{8,12},{9,5},{12,14},{13,9},{14,10},{15,13... | collective-permute-start | bytes 786440 | tf_op jit(solution)/shard_map/ppermute | solution.py:243
  41.8 0.0 collective-permute-start.18
  41.8 0.5 collective-permute-start.23
  42.4 0.0 collective-permute-start.19
  42.4 4.2 %collective-permute-done.16 = bf16[64,2048]{1,0:T(8,128)(2,1)S(1)} collective-permute-done((bf16[64,2048]{1,0:T(8,128)(2,1)S(1)}, bf16[64,2048]{1,0:T(8,128)(2,1)S(1)}, u32[]{:S(2)}, u32[]{:S(2)}) %collective-permute-start.16) | collective-permute-done | bytes 262176 | tf_op jit(solution)/shard_map/ppermute | solution.py:243
  46.6 0.1 add_convert_fusion.4
  46.7 1.7 %collective-permute-start.25 = (bf16[64,2048]{1,0:T(8,128)(2,1)S(1)}, bf16[64,2048]{1,0:T(8,128)(2,1)S(1)}, u32[]{:S(2)}, u32[]{:S(2)}) collective-permute-start(bf16[64,2048]{1,0:T(8,128)(2,1)S(1)} %add_convert_fusion.4), channel_id=1, source_target_pairs={{0,4},{1,3},{4,8},{5,1},{8,12},{9,5},{12,14},{13,9},{14,10},{15,13... | collective-permute-start | bytes 786440 | tf_op jit(solution)/shard_map/ppermute | solution.py:252
  48.4 0.1 add_convert_fusion.7
  48.4 1.6 %collective-permute-start.20 = (bf16[64,2048]{1,0:T(8,128)(2,1)S(1)}, bf16[64,2048]{1,0:T(8,128)(2,1)S(1)}, u32[]{:S(2)}, u32[]{:S(2)}) collective-permute-start(bf16[64,2048]{1,0:T(8,128)(2,1)S(1)} %add_convert_fusion.7), channel_id=1, source_target_pairs={{0,4},{1,3},{4,8},{5,1},{8,12},{9,5},{12,14},{13,9},{14,10},{15,13... | collective-permute-start | bytes 786440 | tf_op jit(solution)/shard_map/ppermute | solution.py:251
  50.1 2.7 %expert.6 = (bf16[64,2048]{1,0:T(8,128)(2,1)S(1)}, bf16[64,2048]{1,0:T(8,128)(2,1)S(1)}, bf16[64,2048]{1,0:T(8,128)(2,1)S(1)}, bf16[64,2048]{1,0:T(8,128)(2,1)S(1)}) custom-call(s32[1]{0:T(128)} %bitcast.own_ref, bf16[64,2176]{1,0:T(8,128)(2,1)S(1)} %collective-permute-done.2.refs_0_, bf16[64,2176]{1,0:T(8,128)(2,1)S(1)} %collective-permute-done.10.refs_1_, ...), custom_call_target="tpu_custom_call" | custom-call | flops 524288 | bytes 524288 | tf_op jit(solution)/shard_map/expert/pallas_call | solution.py:115
  52.7 0.1 collective-permute-start.17
  52.8 0.3 collective-permute-done.25
  53.1 0.2 collective-permute-start.27
  53.3 0.1 add_convert_fusion.3
  53.4 1.6 %collective-permute-start.26 = (bf16[64,2048]{1,0:T(8,128)(2,1)S(1)}, bf16[64,2048]{1,0:T(8,128)(2,1)S(1)}, u32[]{:S(2)}, u32[]{:S(2)}) collective-permute-start(bf16[64,2048]{1,0:T(8,128)(2,1)S(1)} %add_convert_fusion.3), channel_id=1, source_target_pairs={{0,4},{1,3},{4,8},{5,1},{8,12},{9,5},{12,14},{13,9},{14,10},{15,13... | collective-permute-start | bytes 786440 | tf_op jit(solution)/shard_map/ppermute | solution.py:252
  55.1 0.9 %collective-permute-done.20 = bf16[64,2048]{1,0:T(8,128)(2,1)S(1)} collective-permute-done((bf16[64,2048]{1,0:T(8,128)(2,1)S(1)}, bf16[64,2048]{1,0:T(8,128)(2,1)S(1)}, u32[]{:S(2)}, u32[]{:S(2)}) %collective-permute-start.20) | collective-permute-done | bytes 262176 | tf_op jit(solution)/shard_map/ppermute | solution.py:251
  55.9 0.1 add_convert_fusion.6
  56.0 1.7 %collective-permute-start.21 = (bf16[64,2048]{1,0:T(8,128)(2,1)S(1)}, bf16[64,2048]{1,0:T(8,128)(2,1)S(1)}, u32[]{:S(2)}, u32[]{:S(2)}) collective-permute-start(bf16[64,2048]{1,0:T(8,128)(2,1)S(1)} %add_convert_fusion.6), channel_id=1, source_target_pairs={{0,4},{1,3},{4,8},{5,1},{8,12},{9,5},{12,14},{13,9},{14,10},{15,13... | collective-permute-start | bytes 786440 | tf_op jit(solution)/shard_map/ppermute | solution.py:251
  57.7 2.1 %collective-permute-done.26 = bf16[64,2048]{1,0:T(8,128)(2,1)S(1)} collective-permute-done((bf16[64,2048]{1,0:T(8,128)(2,1)S(1)}, bf16[64,2048]{1,0:T(8,128)(2,1)S(1)}, u32[]{:S(2)}, u32[]{:S(2)}) %collective-permute-start.26) | collective-permute-done | bytes 262176 | tf_op jit(solution)/shard_map/ppermute | solution.py:252
  59.9 0.1 add_convert_fusion.2
  60.0 1.6 %collective-permute-start.28 = (bf16[64,2048]{1,0:T(8,128)(2,1)S(1)}, bf16[64,2048]{1,0:T(8,128)(2,1)S(1)}, u32[]{:S(2)}, u32[]{:S(2)}) collective-permute-start(bf16[64,2048]{1,0:T(8,128)(2,1)S(1)} %add_convert_fusion.2), channel_id=1, source_target_pairs={{0,4},{1,3},{4,8},{5,1},{8,12},{9,5},{12,14},{13,9},{14,10},{15,13... | collective-permute-start | bytes 786440 | tf_op jit(solution)/shard_map/ppermute | solution.py:252
  61.6 1.1 %collective-permute-done.21 = bf16[64,2048]{1,0:T(8,128)(2,1)S(1)} collective-permute-done((bf16[64,2048]{1,0:T(8,128)(2,1)S(1)}, bf16[64,2048]{1,0:T(8,128)(2,1)S(1)}, u32[]{:S(2)}, u32[]{:S(2)}) %collective-permute-start.21) | collective-permute-done | bytes 262176 | tf_op jit(solution)/shard_map/ppermute | solution.py:251
  62.7 0.1 add_convert_fusion.5
  62.8 1.6 %collective-permute-start.22 = (bf16[64,2048]{1,0:T(8,128)(2,1)S(1)}, bf16[64,2048]{1,0:T(8,128)(2,1)S(1)}, u32[]{:S(2)}, u32[]{:S(2)}) collective-permute-start(bf16[64,2048]{1,0:T(8,128)(2,1)S(1)} %add_convert_fusion.5), channel_id=1, source_target_pairs={{0,4},{1,3},{4,8},{5,1},{8,12},{9,5},{12,14},{13,9},{14,10},{15,13... | collective-permute-start | bytes 786440 | tf_op jit(solution)/shard_map/ppermute | solution.py:251
  64.4 2.0 %expert.7 = (bf16[64,2048]{1,0:T(8,128)(2,1)S(1)}, bf16[64,2048]{1,0:T(8,128)(2,1)S(1)}) custom-call(s32[1]{0:T(128)} %bitcast.own_ref, bf16[64,2176]{1,0:T(8,128)(2,1)S(1)} %copy-done, bf16[64,2176]{1,0:T(8,128)(2,1)S(1)} %collective-permute-done.1.refs_1_, bf16[1,2048,768]{2,1,0:T(8,128)(2,1)S(1)} %get-tuple-element.34.refs_4_.refs_6_.refs_2_, ...), custom_call_target="tpu_custom_call" | custom-call | flops 262144 | bytes 262144 | tf_op jit(solution)/shard_map/expert/pallas_call | solution.py:115
  66.5 0.1 add_convert_fusion.1
  66.5 0.1 collective-permute-start.29
  66.6 2.6 %collective-permute-done.22 = bf16[64,2048]{1,0:T(8,128)(2,1)S(1)} collective-permute-done((bf16[64,2048]{1,0:T(8,128)(2,1)S(1)}, bf16[64,2048]{1,0:T(8,128)(2,1)S(1)}, u32[]{:S(2)}, u32[]{:S(2)}) %collective-permute-start.22) | collective-permute-done | bytes 262176 | tf_op jit(solution)/shard_map/ppermute | solution.py:251
  69.2 0.8 %add_convert_fusion = bf16[64,2048]{1,0:T(8,128)(2,1)} fusion(bf16[64,2048]{1,0:T(8,128)(2,1)S(1)} %collective-permute-done.29, bf16[64,2048]{1,0:T(8,128)(2,1)S(1)} %get-tuple-element.56, bf16[64,2048]{1,0:T(8,128)(2,1)S(1)} %collective-permute-done.22), kind=kLoop, calls=%fused_computation | loop fusion | flops 786432 | bytes 1048576 | tf_op jit(solution)/shard_map/convert_element_type | solution.py:209
  (14 shorter events, 0.0 us)
Async XLA Ops:
  1.7 3.2 %collective-permute-start.1 = (bf16[64,2176]{1,0:T(8,128)(2,1)}, bf16[64,2176]{1,0:T(8,128)(2,1)S(1)}, u32[]{:S(2)}, u32[]{:S(2)}) collective-permute-start(bf16[64,2176]{1,0:T(8,128)(2,1)} %pack.1.refs_0_), channel_id=1, source_target_pairs={{0,1},{1,0},{2,3},{3,2},{4,5},{5,4},{6,7},{7,6},{8,9},{9,8},{10,11... | collective-permute-start | bytes 835592 | tf_op jit(solution)/shard_map/ppermute | solution.py:225
  2.2 7.3 %collective-permute-start = (bf16[64,2176]{1,0:T(8,128)(2,1)}, bf16[64,2176]{1,0:T(8,128)(2,1)S(1)}, u32[]{:S(2)}, u32[]{:S(2)}) collective-permute-start(bf16[64,2176]{1,0:T(8,128)(2,1)} %pack.1.refs_0_), channel_id=1, source_target_pairs={{0,4},{1,3},{4,8},{5,1},{8,12},{9,5},{12,14},{13,9},{14,10},{15,13... | collective-permute-start | bytes 835592 | tf_op jit(solution)/shard_map/ppermute | solution.py:226
  4.9 7.6 %collective-permute-start.7 = (bf16[64,2176]{1,0:T(8,128)(2,1)S(1)}, bf16[64,2176]{1,0:T(8,128)(2,1)S(1)}, u32[]{:S(2)}, u32[]{:S(2)}) collective-permute-start(bf16[64,2176]{1,0:T(8,128)(2,1)S(1)} %collective-permute-done.1.refs_1_), channel_id=1, source_target_pairs={{0,4},{1,3},{4,8},{5,1},{8,12},{9,5},{12,14},{13,9},{14,10},{15,13... | collective-permute-start | bytes 835592 | tf_op jit(solution)/shard_map/ppermute | solution.py:226
  9.5 7.0 %collective-permute-start.3 = (bf16[64,2176]{1,0:T(8,128)(2,1)S(1)}, bf16[64,2176]{1,0:T(8,128)(2,1)S(1)}, u32[]{:S(2)}, u32[]{:S(2)}) collective-permute-start(bf16[64,2176]{1,0:T(8,128)(2,1)S(1)} %collective-permute-done.refs_2_), channel_id=1, source_target_pairs={{0,4},{1,3},{4,8},{5,1},{8,12},{9,5},{12,14},{13,9},{14,10},{15,13... | collective-permute-start | bytes 835592 | tf_op jit(solution)/shard_map/ppermute | solution.py:237
  12.5 6.5 %collective-permute-start.8 = (bf16[64,2176]{1,0:T(8,128)(2,1)S(1)}, bf16[64,2176]{1,0:T(8,128)(2,1)S(1)}, u32[]{:S(2)}, u32[]{:S(2)}) collective-permute-start(bf16[64,2176]{1,0:T(8,128)(2,1)S(1)} %collective-permute-done.7.refs_3_), channel_id=1, source_target_pairs={{0,4},{1,3},{4,8},{5,1},{8,12},{9,5},{12,14},{13,9},{14,10},{15,13... | collective-permute-start | bytes 835592 | tf_op jit(solution)/shard_map/ppermute | solution.py:235
  16.5 6.6 %collective-permute-start.4 = (bf16[64,2176]{1,0:T(8,128)(2,1)S(1)}, bf16[64,2176]{1,0:T(8,128)(2,1)S(1)}, u32[]{:S(2)}, u32[]{:S(2)}) collective-permute-start(bf16[64,2176]{1,0:T(8,128)(2,1)S(1)} %collective-permute-done.3.refs_2_), channel_id=1, source_target_pairs={{0,4},{1,3},{4,8},{5,1},{8,12},{9,5},{12,14},{13,9},{14,10},{15,13... | collective-permute-start | bytes 835592 | tf_op jit(solution)/shard_map/ppermute | solution.py:237
  18.2 4.9 %collective-permute-start.6 = (bf16[64,2176]{1,0:T(8,128)(2,1)S(1)}, bf16[64,2176]{1,0:T(8,128)(2,1)S(1)}, u32[]{:S(2)}, u32[]{:S(2)}) collective-permute-start(bf16[64,2176]{1,0:T(8,128)(2,1)S(1)} %collective-permute-done.3.refs_2_), channel_id=1, source_target_pairs={{0,1},{1,0},{2,3},{3,2},{4,5},{5,4},{6,7},{7,6},{8,9},{9,8},{10,11... | collective-permute-start | bytes 835592 | tf_op jit(solution)/shard_map/ppermute | solution.py:236
  19.1 5.7 %collective-permute-start.9 = (bf16[64,2176]{1,0:T(8,128)(2,1)S(1)}, bf16[64,2176]{1,0:T(8,128)(2,1)S(1)}, u32[]{:S(2)}, u32[]{:S(2)}) collective-permute-start(bf16[64,2176]{1,0:T(8,128)(2,1)S(1)} %collective-permute-done.8.refs_3_), channel_id=1, source_target_pairs={{0,1},{1,0},{2,3},{3,2},{4,5},{5,4},{6,7},{7,6},{8,9},{9,8},{10,11... | collective-permute-start | bytes 835592 | tf_op jit(solution)/shard_map/ppermute | solution.py:236
  19.1 9.9 %collective-permute-start.2 = (bf16[64,2176]{1,0:T(8,128)(2,1)S(1)}, bf16[64,2176]{1,0:T(8,128)(2,1)S(1)}, u32[]{:S(2)}, u32[]{:S(2)}) collective-permute-start(bf16[64,2176]{1,0:T(8,128)(2,1)S(1)} %collective-permute-done.refs_2_), channel_id=1, source_target_pairs={{0,1},{1,0},{2,3},{3,2},{4,5},{5,4},{6,7},{7,6},{8,9},{9,8},{10,11... | collective-permute-start | bytes 835592 | tf_op jit(solution)/shard_map/ppermute | solution.py:236
  19.6 9.4 %collective-permute-start.10 = (bf16[64,2176]{1,0:T(8,128)(2,1)S(1)}, bf16[64,2176]{1,0:T(8,128)(2,1)S(1)}, u32[]{:S(2)}, u32[]{:S(2)}) collective-permute-start(bf16[64,2176]{1,0:T(8,128)(2,1)S(1)} %collective-permute-done.7.refs_3_), channel_id=1, source_target_pairs={{0,1},{1,0},{2,3},{3,2},{4,5},{5,4},{6,7},{7,6},{8,9},{9,8},{10,11... | collective-permute-start | bytes 835592 | tf_op jit(solution)/shard_map/ppermute | solution.py:236
  23.1 5.9 %collective-permute-start.11 = (bf16[64,2176]{1,0:T(8,128)(2,1)S(1)}, bf16[64,2176]{1,0:T(8,128)(2,1)S(1)}, u32[]{:S(2)}, u32[]{:S(2)}) collective-permute-start(bf16[64,2176]{1,0:T(8,128)(2,1)S(1)} %collective-permute-done.4.refs_4_), channel_id=1, source_target_pairs={{0,1},{1,0},{2,3},{3,2},{4,5},{5,4},{6,7},{7,6},{8,9},{9,8},{10,11... | collective-permute-start | bytes 835592 | tf_op jit(solution)/shard_map/ppermute | solution.py:236
  23.1 6.5 %collective-permute-start.5 = (bf16[64,2176]{1,0:T(8,128)(2,1)S(1)}, bf16[64,2176]{1,0:T(8,128)(2,1)S(1)}, u32[]{:S(2)}, u32[]{:S(2)}) collective-permute-start(bf16[64,2176]{1,0:T(8,128)(2,1)S(1)} %collective-permute-done.4.refs_4_), channel_id=1, source_target_pairs={{0,4},{1,3},{4,8},{5,1},{8,12},{9,5},{12,14},{13,9},{14,10},{15,13... | collective-permute-start | bytes 835592 | tf_op jit(solution)/shard_map/ppermute | solution.py:237
  24.7 7.9 %collective-permute-start.13 = (bf16[64,2176]{1,0:T(8,128)(2,1)S(1)}, bf16[64,2176]{1,0:T(8,128)(2,1)S(1)}, u32[]{:S(2)}, u32[]{:S(2)}) collective-permute-start(bf16[64,2176]{1,0:T(8,128)(2,1)S(1)} %collective-permute-done.8.refs_3_), channel_id=1, source_target_pairs={{0,4},{1,3},{4,8},{5,1},{8,12},{9,5},{12,14},{13,9},{14,10},{15,13... | collective-permute-start | bytes 835592 | tf_op jit(solution)/shard_map/ppermute | solution.py:235
  32.6 1.6 %collective-permute-start.14 = (bf16[64,2176]{1,0:T(8,128)(2,1)S(1)}, bf16[64,2176]{1,0:T(8,128)(2,1)S(1)}, u32[]{:S(2)}, u32[]{:S(2)}) collective-permute-start(bf16[64,2176]{1,0:T(8,128)(2,1)S(1)} %collective-permute-done.13.refs_5_), channel_id=1, source_target_pairs={{0,1},{1,0},{2,3},{3,2},{4,5},{5,4},{6,7},{7,6},{8,9},{9,8},{10,11... | collective-permute-start | bytes 835592 | tf_op jit(solution)/shard_map/ppermute | solution.py:236
  32.6 2.0 %collective-permute-start.12 = (bf16[64,2176]{1,0:T(8,128)(2,1)S(1)}, bf16[64,2176]{1,0:T(8,128)(2,1)S(1)}, u32[]{:S(2)}, u32[]{:S(2)}) collective-permute-start(bf16[64,2176]{1,0:T(8,128)(2,1)S(1)} %collective-permute-done.5.refs_1_), channel_id=1, source_target_pairs={{0,1},{1,0},{2,3},{3,2},{4,5},{5,4},{6,7},{7,6},{8,9},{9,8},{10,11... | collective-permute-start | bytes 835592 | tf_op jit(solution)/shard_map/ppermute | solution.py:242
  38.5 1.6 %collective-permute-start.15 = (bf16[64,2048]{1,0:T(8,128)(2,1)S(1)}, bf16[64,2048]{1,0:T(8,128)(2,1)S(1)}, u32[]{:S(2)}, u32[]{:S(2)}) collective-permute-start(bf16[64,2048]{1,0:T(8,128)(2,1)S(1)} %get-tuple-element.42), channel_id=1, source_target_pairs={{0,1},{1,0},{2,3},{3,2},{4,5},{5,4},{6,7},{7,6},{8,9},{9,8},{10,11... | collective-permute-start | bytes 786440 | tf_op jit(solution)/shard_map/ppermute | solution.py:243
  38.7 3.7 %collective-permute-start.24 = (bf16[64,2048]{1,0:T(8,128)(2,1)S(1)}, bf16[64,2048]{1,0:T(8,128)(2,1)S(1)}, u32[]{:S(2)}, u32[]{:S(2)}) collective-permute-start(bf16[64,2048]{1,0:T(8,128)(2,1)S(1)} %get-tuple-element.52), channel_id=1, source_target_pairs={{0,1},{1,0},{2,3},{3,2},{4,5},{5,4},{6,7},{7,6},{8,9},{9,8},{10,11... | collective-permute-start | bytes 786440 | tf_op jit(solution)/shard_map/ppermute | solution.py:250
  40.2 6.4 %collective-permute-start.16 = (bf16[64,2048]{1,0:T(8,128)(2,1)S(1)}, bf16[64,2048]{1,0:T(8,128)(2,1)S(1)}, u32[]{:S(2)}, u32[]{:S(2)}) collective-permute-start(bf16[64,2048]{1,0:T(8,128)(2,1)S(1)} %add_convert_fusion.8), channel_id=1, source_target_pairs={{0,4},{1,3},{4,8},{5,1},{8,12},{9,5},{12,14},{13,9},{14,10},{15,13... | collective-permute-start | bytes 786440 | tf_op jit(solution)/shard_map/ppermute | solution.py:243
  41.8 13.2 %collective-permute-start.18 = (bf16[64,2048]{1,0:T(8,128)(2,1)S(1)}, bf16[64,2048]{1,0:T(8,128)(2,1)S(1)}, u32[]{:S(2)}, u32[]{:S(2)}) collective-permute-start(bf16[64,2048]{1,0:T(8,128)(2,1)S(1)} %get-tuple-element.47), channel_id=1, source_target_pairs={{0,1},{1,0},{2,3},{3,2},{4,5},{5,4},{6,7},{7,6},{8,9},{9,8},{10,11... | collective-permute-start | bytes 786440 | tf_op jit(solution)/shard_map/ppermute | solution.py:250
  41.8 11.5 %collective-permute-start.23 = (bf16[64,2048]{1,0:T(8,128)(2,1)S(1)}, bf16[64,2048]{1,0:T(8,128)(2,1)S(1)}, u32[]{:S(2)}, u32[]{:S(2)}) collective-permute-start(bf16[64,2048]{1,0:T(8,128)(2,1)S(1)} %get-tuple-element.50), channel_id=1, source_target_pairs={{0,1},{1,0},{2,3},{3,2},{4,5},{5,4},{6,7},{7,6},{8,9},{9,8},{10,11... | collective-permute-start | bytes 786440 | tf_op jit(solution)/shard_map/ppermute | solution.py:250
  42.4 6.0 %collective-permute-start.19 = (bf16[64,2048]{1,0:T(8,128)(2,1)S(1)}, bf16[64,2048]{1,0:T(8,128)(2,1)S(1)}, u32[]{:S(2)}, u32[]{:S(2)}) collective-permute-start(bf16[64,2048]{1,0:T(8,128)(2,1)S(1)} %get-tuple-element.49), channel_id=1, source_target_pairs={{0,1},{1,0},{2,3},{3,2},{4,5},{5,4},{6,7},{7,6},{8,9},{9,8},{10,11... | collective-permute-start | bytes 786440 | tf_op jit(solution)/shard_map/ppermute | solution.py:250
  46.7 6.4 %collective-permute-start.25 = (bf16[64,2048]{1,0:T(8,128)(2,1)S(1)}, bf16[64,2048]{1,0:T(8,128)(2,1)S(1)}, u32[]{:S(2)}, u32[]{:S(2)}) collective-permute-start(bf16[64,2048]{1,0:T(8,128)(2,1)S(1)} %add_convert_fusion.4), channel_id=1, source_target_pairs={{0,4},{1,3},{4,8},{5,1},{8,12},{9,5},{12,14},{13,9},{14,10},{15,13... | collective-permute-start | bytes 786440 | tf_op jit(solution)/shard_map/ppermute | solution.py:252
  48.4 7.5 %collective-permute-start.20 = (bf16[64,2048]{1,0:T(8,128)(2,1)S(1)}, bf16[64,2048]{1,0:T(8,128)(2,1)S(1)}, u32[]{:S(2)}, u32[]{:S(2)}) collective-permute-start(bf16[64,2048]{1,0:T(8,128)(2,1)S(1)} %add_convert_fusion.7), channel_id=1, source_target_pairs={{0,4},{1,3},{4,8},{5,1},{8,12},{9,5},{12,14},{13,9},{14,10},{15,13... | collective-permute-start | bytes 786440 | tf_op jit(solution)/shard_map/ppermute | solution.py:251
  52.7 11.7 %copy-start = (bf16[64,2176]{1,0:T(8,128)(2,1)S(1)}, bf16[64,2176]{1,0:T(8,128)(2,1)}, u32[]{:S(2)}) copy-start(bf16[64,2176]{1,0:T(8,128)(2,1)} %pack.1.refs_0_) | copy-start | bytes 835588
  52.7 8.8 %collective-permute-start.17 = (bf16[64,2048]{1,0:T(8,128)(2,1)S(1)}, bf16[64,2048]{1,0:T(8,128)(2,1)S(1)}, u32[]{:S(2)}, u32[]{:S(2)}) collective-permute-start(bf16[64,2048]{1,0:T(8,128)(2,1)S(1)} %get-tuple-element.45), channel_id=1, source_target_pairs={{0,1},{1,0},{2,3},{3,2},{4,5},{5,4},{6,7},{7,6},{8,9},{9,8},{10,11... | collective-permute-start | bytes 786440 | tf_op jit(solution)/shard_map/ppermute | solution.py:250
  53.1 4.6 %collective-permute-start.27 = (bf16[64,2048]{1,0:T(8,128)(2,1)S(1)}, bf16[64,2048]{1,0:T(8,128)(2,1)S(1)}, u32[]{:S(2)}, u32[]{:S(2)}) collective-permute-start(bf16[64,2048]{1,0:T(8,128)(2,1)S(1)} %get-tuple-element.57), channel_id=1, source_target_pairs={{0,1},{1,0},{2,3},{3,2},{4,5},{5,4},{6,7},{7,6},{8,9},{9,8},{10,11... | collective-permute-start | bytes 786440 | tf_op jit(solution)/shard_map/ppermute | solution.py:250
  53.4 6.4 %collective-permute-start.26 = (bf16[64,2048]{1,0:T(8,128)(2,1)S(1)}, bf16[64,2048]{1,0:T(8,128)(2,1)S(1)}, u32[]{:S(2)}, u32[]{:S(2)}) collective-permute-start(bf16[64,2048]{1,0:T(8,128)(2,1)S(1)} %add_convert_fusion.3), channel_id=1, source_target_pairs={{0,4},{1,3},{4,8},{5,1},{8,12},{9,5},{12,14},{13,9},{14,10},{15,13... | collective-permute-start | bytes 786440 | tf_op jit(solution)/shard_map/ppermute | solution.py:252
  56.0 6.6 %collective-permute-start.21 = (bf16[64,2048]{1,0:T(8,128)(2,1)S(1)}, bf16[64,2048]{1,0:T(8,128)(2,1)S(1)}, u32[]{:S(2)}, u32[]{:S(2)}) collective-permute-start(bf16[64,2048]{1,0:T(8,128)(2,1)S(1)} %add_convert_fusion.6), channel_id=1, source_target_pairs={{0,4},{1,3},{4,8},{5,1},{8,12},{9,5},{12,14},{13,9},{14,10},{15,13... | collective-permute-start | bytes 786440 | tf_op jit(solution)/shard_map/ppermute | solution.py:251
  60.0 6.5 %collective-permute-start.28 = (bf16[64,2048]{1,0:T(8,128)(2,1)S(1)}, bf16[64,2048]{1,0:T(8,128)(2,1)S(1)}, u32[]{:S(2)}, u32[]{:S(2)}) collective-permute-start(bf16[64,2048]{1,0:T(8,128)(2,1)S(1)} %add_convert_fusion.2), channel_id=1, source_target_pairs={{0,4},{1,3},{4,8},{5,1},{8,12},{9,5},{12,14},{13,9},{14,10},{15,13... | collective-permute-start | bytes 786440 | tf_op jit(solution)/shard_map/ppermute | solution.py:252
  62.8 6.4 %collective-permute-start.22 = (bf16[64,2048]{1,0:T(8,128)(2,1)S(1)}, bf16[64,2048]{1,0:T(8,128)(2,1)S(1)}, u32[]{:S(2)}, u32[]{:S(2)}) collective-permute-start(bf16[64,2048]{1,0:T(8,128)(2,1)S(1)} %add_convert_fusion.5), channel_id=1, source_target_pairs={{0,4},{1,3},{4,8},{5,1},{8,12},{9,5},{12,14},{13,9},{14,10},{15,13... | collective-permute-start | bytes 786440 | tf_op jit(solution)/shard_map/ppermute | solution.py:251
  66.5 2.7 %collective-permute-start.29 = (bf16[64,2048]{1,0:T(8,128)(2,1)S(1)}, bf16[64,2048]{1,0:T(8,128)(2,1)S(1)}, u32[]{:S(2)}, u32[]{:S(2)}) collective-permute-start(bf16[64,2048]{1,0:T(8,128)(2,1)S(1)} %add_convert_fusion.1), channel_id=1, source_target_pairs={{0,1},{1,0},{2,3},{3,2},{4,5},{5,4},{6,7},{7,6},{8,9},{9,8},{10,11... | collective-permute-start | bytes 786440 | tf_op jit(solution)/shard_map/ppermute | solution.py:255

commit v7 on v6

--- a/solution.py
+++ b/solution.py
@@ -107,7 +107,7 @@
             target[:, part] = out[number * each : (number + 1) * each]
 
 
-def run_expert(own, blocks, weights, experts):
+def run_expert(own, blocks, weights, experts, cost=1):
     rows = sum(block.shape[0] for block in blocks)
     wide = blocks[0].shape[1]
     width, ff = weights[0].shape[1:]
@@ -120,7 +120,7 @@
         scratch_shapes=[pltpu.VMEM((rows, wide), jnp.bfloat16), pltpu.VMEM((rows, ff), jnp.bfloat16)],
         compiler_params=pltpu.CompilerParams(vmem_limit_bytes=16 << 20),
         cost_estimate=pl.CostEstimate(
-            flops=rows * width, bytes_accessed=rows * width, transcendentals=0
+            flops=cost * rows * width, bytes_accessed=rows * width, transcendentals=0
         ),
         name="expert",
     )(own, *blocks, *weights)
@@ -234,12 +234,15 @@
         if step > 1:
             second = ring(second)
         blocks[step] = (swap(first), swap(second), first, second)
+        if step == rounds - 1:
+            first = after(first, *blocks[1][:2])
         first = ring(first)
         if step == 1:
             first = after(first, down_w)
     sums = {2: run(*blocks[2])}
-    first = after(first, sums[2][0], *blocks[1][:2], blocks[3][0])
-    keep, send, *sums[3] = run(swap(first), first, *blocks[3])
+    first = after(first, sums[2][0], blocks[3][0])
+    sums[3] = run_expert(own, blocks[3], weights, experts, cost=6 * w_gate.shape[2])
+    keep, send = run(after(swap(first), sums[3][0]), first)
     lead, trail = ring(added(keep, swap(send))), None
     for step in (3, 2, 1):
         if step == 3:
@@ -252,7 +255,7 @@
         lead = ring(added(keep, send, lead))
         if step == 2:
             kept, other = run(after(mine, lead), sibling)
-    last = swap(added(lead, other))
+    last = swap(after(added(lead, other), trail))
     return added(trail, kept, last)
 
 

time: 70.2 us -> 67.5 us (0.962)
  waiting for transfers between devices: 22.7 us -> 19.3 us
  Pallas kernels: 17.7 us -> 18.5 us
    ppermute x3, waiting for transfers between devices: 4.2 us -> 2.33 us  [dense_body(): first = ring(first)]
    ppermute x2, waiting for transfers between devices: 3.86 us -> 2.24 us  [dense_body(): second = ring(second)]
    ppermute x2, waiting for transfers between devices: 0.4 us -> 1.54 us  [the longest x1 1.53 us: dense_body(): last = swap(after(added(lead, other), trail))]
    ppermute x6, waiting for transfers between devices: 1.06 us -> 0.02 us  [dense_body(): blocks[step] = (swap(first), swap(second), first, second)]
    pallas_call x4 -> x5, Pallas kernels: 11.2 us -> 12.1 us  [run_expert(): pl.pallas_call(functools.partial(expert_kernel, experts, len(blocks)), ou...]
  transfers between devices with their start and end apart: 30 -> 30, of which waited for: 15 -> 14; matrix products, arithmetic and copies ran while one was open for 1% -> 1% of each run, Pallas kernels for 17% -> 22%
where the time goes in v7:
time: 67.5 us; the launch traced here: 67.4 us
  starting transfers between devices  27.9 us (41%)
  waiting for transfers between devices  19.3 us (29%)
  Pallas kernels  18.5 us (27%)
  other arithmetic  1.5 us (2%)
    pallas_call x5, Pallas kernels, run_expert(): pl.pallas_call(functools.partial(expert_kernel, experts, len(blocks)), ou...  12.1 us
    ppermute x3, starting transfers between devices, dense_body(): first = ring(first)  5.39 us
    ppermute x2, waiting for transfers between devices, dense_body(): lead, trail = (ring(added(keep, swap(send))), None)  5.32 us
    ppermute x3, starting transfers between devices, dense_body(): lead = ring(added(keep, send, lead))  5.01 us
    ppermute x3, starting transfers between devices, dense_body(): ring(added(*[keep_trail, send_trail] + ([] if trail is None else [trail])))  4.97 us
    pallas_call x2, Pallas kernels, load_weights(): pl.pallas_call(functools.partial(load_kernel, pieces), out_shape=[pltpu.V...  4.73 us
    ppermute x3, waiting for transfers between devices, dense_body(): ring(added(*[keep_trail, send_trail] + ([] if trail is None else [trail])))  4.67 us
    ppermute x2, starting transfers between devices, dense_body(): first, second = (ring(mine), ring(sibling))  4.34 us
  transfers between devices with their start and end apart: 30, of which 14 were waited for; matrix products, arithmetic and copies ran while one was open for 1% of the time, Pallas kernels for 22%

profile of v7, /device:TPU:0, one launch (start us, length us, event | category | flops | bytes accessed | tf_op | source)
XLA Modules:
  0.0 67.4 jit_solution(9059642342506858605)
XLA Ops:
  0.0 1.7 %pack.1.refs_0_ = bf16[64,2176]{1,0:T(8,128)(2,1)} custom-call(bf16[64,2048]{1,0:T(8,128)(2,1)} %tokens_ref, s32[8,64]{1,0:T(8,128)} %bitcast.3, f32[8,64]{1,0:T(8,128)} %bitcast.4), custom_call_target="tpu_custom_call" | custom-call | bytes 1024 | tf_op jit(solution)/shard_map/pack/pallas_call | solution.py:190
  1.7 0.5 collective-permute-start.1
  2.2 2.6 %collective-permute-start = (bf16[64,2176]{1,0:T(8,128)(2,1)}, bf16[64,2176]{1,0:T(8,128)(2,1)S(1)}, u32[]{:S(2)}, u32[]{:S(2)}) collective-permute-start(bf16[64,2176]{1,0:T(8,128)(2,1)} %pack.1.refs_0_), channel_id=1, source_target_pairs={{0,4},{1,3},{4,8},{5,1},{8,12},{9,5},{12,14},{13,9},{14,10},{15,13... | collective-permute-start | bytes 835592 | tf_op jit(solution)/shard_map/ppermute | solution.py:226
  4.9 1.7 %collective-permute-start.5 = (bf16[64,2176]{1,0:T(8,128)(2,1)S(1)}, bf16[64,2176]{1,0:T(8,128)(2,1)S(1)}, u32[]{:S(2)}, u32[]{:S(2)}) collective-permute-start(bf16[64,2176]{1,0:T(8,128)(2,1)S(1)} %collective-permute-done.1.refs_1_), channel_id=1, source_target_pairs={{0,4},{1,3},{4,8},{5,1},{8,12},{9,5},{12,14},{13,9},{14,10},{15,13... | collective-permute-start | bytes 835592 | tf_op jit(solution)/shard_map/ppermute | solution.py:226
  6.6 2.9 %load.2 = (bf16[1,2048,768]{2,1,0:T(8,128)(2,1)S(1)}, bf16[1,2048,768]{2,1,0:T(8,128)(2,1)S(1)}) custom-call(bf16[1,2048,768]{2,1,0:T(8,128)(2,1)} %refs_0_, bf16[1,2048,768]{2,1,0:T(8,128)(2,1)} %refs_1_.1), custom_call_target="tpu_custom_call" | custom-call | bytes 1024 | tf_op jit(solution)/shard_map/load/pallas_call | solution.py:148
  9.4 0.1 collective-permute-done.refs_2_
  9.5 2.1 %collective-permute-start.3 = (bf16[64,2176]{1,0:T(8,128)(2,1)S(1)}, bf16[64,2176]{1,0:T(8,128)(2,1)S(1)}, u32[]{:S(2)}, u32[]{:S(2)}) collective-permute-start(bf16[64,2176]{1,0:T(8,128)(2,1)S(1)} %collective-permute-done.refs_2_), channel_id=1, source_target_pairs={{0,4},{1,3},{4,8},{5,1},{8,12},{9,5},{12,14},{13,9},{14,10},{15,13... | collective-permute-start | bytes 835592 | tf_op jit(solution)/shard_map/ppermute | solution.py:239
  11.6 0.9 %collective-permute-done.5.refs_3_ = bf16[64,2176]{1,0:T(8,128)(2,1)S(1)} collective-permute-done((bf16[64,2176]{1,0:T(8,128)(2,1)S(1)}, bf16[64,2176]{1,0:T(8,128)(2,1)S(1)}, u32[]{:S(2)}, u32[]{:S(2)}) %collective-permute-start.5) | collective-permute-done | bytes 278560 | tf_op jit(solution)/shard_map/ppermute | solution.py:226
  12.5 2.1 %collective-permute-start.9 = (bf16[64,2176]{1,0:T(8,128)(2,1)S(1)}, bf16[64,2176]{1,0:T(8,128)(2,1)S(1)}, u32[]{:S(2)}, u32[]{:S(2)}) collective-permute-start(bf16[64,2176]{1,0:T(8,128)(2,1)S(1)} %collective-permute-done.5.refs_3_), channel_id=1, source_target_pairs={{0,4},{1,3},{4,8},{5,1},{8,12},{9,5},{12,14},{13,9},{14,10},{15,13... | collective-permute-start | bytes 835592 | tf_op jit(solution)/shard_map/ppermute | solution.py:235
  14.6 1.9 %load.3.refs_6_.refs_4_ = bf16[1,2048,768]{2,1,0:T(8,128)(2,1)S(1)} custom-call(bf16[1,2048,768]{2,1,0:T(8,128)(2,1)} %refs_0_.1), custom_call_target="tpu_custom_call" | custom-call | bytes 1024 | tf_op jit(solution)/shard_map/load/pallas_call | solution.py:148
  16.5 0.0 collective-permute-done.3.refs_2_
  16.5 1.7 %collective-permute-start.4 = (bf16[64,2176]{1,0:T(8,128)(2,1)S(1)}, bf16[64,2176]{1,0:T(8,128)(2,1)S(1)}, u32[]{:S(2)}, u32[]{:S(2)}) collective-permute-start(bf16[64,2176]{1,0:T(8,128)(2,1)S(1)} %collective-permute-done.3.refs_2_), channel_id=1, source_target_pairs={{0,4},{1,3},{4,8},{5,1},{8,12},{9,5},{12,14},{13,9},{14,10},{15,13... | collective-permute-start | bytes 835592 | tf_op jit(solution)/shard_map/ppermute | solution.py:239
  18.2 0.0 collective-permute-start.6
  18.2 0.9 %collective-permute-done.9.refs_3_ = bf16[64,2176]{1,0:T(8,128)(2,1)S(1)} collective-permute-done((bf16[64,2176]{1,0:T(8,128)(2,1)S(1)}, bf16[64,2176]{1,0:T(8,128)(2,1)S(1)}, u32[]{:S(2)}, u32[]{:S(2)}) %collective-permute-start.9) | collective-permute-done | bytes 278560 | tf_op jit(solution)/shard_map/ppermute | solution.py:235
  19.1 2.1 %collective-permute-start.13 = (bf16[64,2176]{1,0:T(8,128)(2,1)S(1)}, bf16[64,2176]{1,0:T(8,128)(2,1)S(1)}, u32[]{:S(2)}, u32[]{:S(2)}) collective-permute-start(bf16[64,2176]{1,0:T(8,128)(2,1)S(1)} %collective-permute-done.9.refs_3_), channel_id=1, source_target_pairs={{0,4},{1,3},{4,8},{5,1},{8,12},{9,5},{12,14},{13,9},{14,10},{15,13... | collective-permute-start | bytes 835592 | tf_op jit(solution)/shard_map/ppermute | solution.py:235
  21.2 0.5 collective-permute-start.10
  21.7 1.4 %collective-permute-done.4.refs_2_ = bf16[64,2176]{1,0:T(8,128)(2,1)S(1)} collective-permute-done((bf16[64,2176]{1,0:T(8,128)(2,1)S(1)}, bf16[64,2176]{1,0:T(8,128)(2,1)S(1)}, u32[]{:S(2)}, u32[]{:S(2)}) %collective-permute-start.4) | collective-permute-done | bytes 278560 | tf_op jit(solution)/shard_map/ppermute | solution.py:239
  23.1 0.0 collective-permute-done.6.refs_1_
  23.1 1.6 %collective-permute-start.7 = (bf16[64,2176]{1,0:T(8,128)(2,1)S(1)}, bf16[64,2176]{1,0:T(8,128)(2,1)S(1)}, u32[]{:S(2)}, u32[]{:S(2)}) collective-permute-start(bf16[64,2176]{1,0:T(8,128)(2,1)S(1)} %collective-permute-done.4.refs_2_), channel_id=1, source_target_pairs={{0,4},{1,3},{4,8},{5,1},{8,12},{9,5},{12,14},{13,9},{14,10},{15,13... | collective-permute-start | bytes 835592 | tf_op jit(solution)/shard_map/ppermute | solution.py:239
  24.7 1.4 %collective-permute-done.13.refs_3_ = bf16[64,2176]{1,0:T(8,128)(2,1)S(1)} collective-permute-done((bf16[64,2176]{1,0:T(8,128)(2,1)S(1)}, bf16[64,2176]{1,0:T(8,128)(2,1)S(1)}, u32[]{:S(2)}, u32[]{:S(2)}) %collective-permute-start.13) | collective-permute-done | bytes 278560 | tf_op jit(solution)/shard_map/ppermute | solution.py:235
  26.1 0.0 collective-permute-start.14
  26.1 0.0 collective-permute-done.8.refs_0_
  26.1 0.0 collective-permute-done.10.refs_1_
  26.1 2.7 %expert.5 = (bf16[64,2048]{1,0:T(8,128)(2,1)S(1)}, bf16[64,2048]{1,0:T(8,128)(2,1)S(1)}, bf16[64,2048]{1,0:T(8,128)(2,1)S(1)}, bf16[64,2048]{1,0:T(8,128)(2,1)S(1)}) custom-call(s32[1]{0:T(128)} %bitcast.own_ref, bf16[64,2176]{1,0:T(8,128)(2,1)S(1)} %collective-permute-done.8.refs_0_, bf16[64,2176]{1,0:T(8,128)(2,1)S(1)} %collective-permute-done.10.refs_1_, ...), custom_call_target="tpu_custom_call" | custom-call | flops 524288 | bytes 524288 | tf_op jit(solution)/shard_map/expert/pallas_call | solution.py:115
  28.8 0.0 collective-permute-done.11.refs_0_
  28.8 0.9 %collective-permute-done.7.refs_1_ = bf16[64,2176]{1,0:T(8,128)(2,1)S(1)} collective-permute-done((bf16[64,2176]{1,0:T(8,128)(2,1)S(1)}, bf16[64,2176]{1,0:T(8,128)(2,1)S(1)}, u32[]{:S(2)}, u32[]{:S(2)}) %collective-permute-start.7) | collective-permute-done | bytes 278560 | tf_op jit(solution)/shard_map/ppermute | solution.py:239
  29.7 2.7 %expert.6 = (bf16[64,2048]{1,0:T(8,128)(2,1)S(1)}, bf16[64,2048]{1,0:T(8,128)(2,1)S(1)}, bf16[64,2048]{1,0:T(8,128)(2,1)S(1)}, bf16[64,2048]{1,0:T(8,128)(2,1)S(1)}) custom-call(s32[1]{0:T(128)} %bitcast.own_ref, bf16[64,2176]{1,0:T(8,128)(2,1)S(1)} %collective-permute-done.11.refs_0_, bf16[64,2176]{1,0:T(8,128)(2,1)S(1)} %collective-permute-done.14.refs_1_, ...), custom_call_target="tpu_custom_call" | custom-call | flops 2415919104 | bytes 524288 | tf_op jit(solution)/shard_map/expert/pallas_call | solution.py:115
  32.4 2.1 %expert.7 = (bf16[64,2048]{1,0:T(8,128)(2,1)S(1)}, bf16[64,2048]{1,0:T(8,128)(2,1)S(1)}) custom-call(s32[1]{0:T(128)} %bitcast.own_ref, bf16[64,2176]{1,0:T(8,128)(2,1)S(1)} %collective-permute-done.12.refs_0_, bf16[64,2176]{1,0:T(8,128)(2,1)S(1)} %collective-permute-done.7.refs_1_, bf16[1,2048,768]{2,1,0:T(8,128)(2,1)S(1)} %get-tuple-element.37.refs_4_.refs_2_, ...), custom_call_target="tpu_custom_call" | custom-call | flops 262144 | bytes 262144 | tf_op jit(solution)/shard_map/expert/pallas_call | solution.py:115
  34.4 0.6 collective-permute-start.15
  35.0 0.1 collective-permute-start.24
  35.1 1.1 %collective-permute-done.15 = bf16[64,2048]{1,0:T(8,128)(2,1)S(1)} collective-permute-done((bf16[64,2048]{1,0:T(8,128)(2,1)S(1)}, bf16[64,2048]{1,0:T(8,128)(2,1)S(1)}, u32[]{:S(2)}, u32[]{:S(2)}) %collective-permute-start.15) | collective-permute-done | bytes 262176 | tf_op jit(solution)/shard_map/ppermute | solution.py:246
  36.1 0.1 add_convert_fusion.8
  36.2 1.7 %collective-permute-start.16 = (bf16[64,2048]{1,0:T(8,128)(2,1)S(1)}, bf16[64,2048]{1,0:T(8,128)(2,1)S(1)}, u32[]{:S(2)}, u32[]{:S(2)}) collective-permute-start(bf16[64,2048]{1,0:T(8,128)(2,1)S(1)} %add_convert_fusion.8), channel_id=1, source_target_pairs={{0,4},{1,3},{4,8},{5,1},{8,12},{9,5},{12,14},{13,9},{14,10},{15,13... | collective-permute-start | bytes 786440 | tf_op jit(solution)/shard_map/ppermute | solution.py:246
  37.9 0.0 collective-permute-start.18
  37.9 0.5 collective-permute-start.23
  38.4 0.0 collective-permute-start.19
  38.4 4.2 %collective-permute-done.16 = bf16[64,2048]{1,0:T(8,128)(2,1)S(1)} collective-permute-done((bf16[64,2048]{1,0:T(8,128)(2,1)S(1)}, bf16[64,2048]{1,0:T(8,128)(2,1)S(1)}, u32[]{:S(2)}, u32[]{:S(2)}) %collective-permute-start.16) | collective-permute-done | bytes 262176 | tf_op jit(solution)/shard_map/ppermute | solution.py:246
  42.6 0.1 add_convert_fusion.4
  42.7 1.7 %collective-permute-start.25 = (bf16[64,2048]{1,0:T(8,128)(2,1)S(1)}, bf16[64,2048]{1,0:T(8,128)(2,1)S(1)}, u32[]{:S(2)}, u32[]{:S(2)}) collective-permute-start(bf16[64,2048]{1,0:T(8,128)(2,1)S(1)} %add_convert_fusion.4), channel_id=1, source_target_pairs={{0,4},{1,3},{4,8},{5,1},{8,12},{9,5},{12,14},{13,9},{14,10},{15,13... | collective-permute-start | bytes 786440 | tf_op jit(solution)/shard_map/ppermute | solution.py:255
  44.4 0.0 collective-permute-done.19
  44.4 0.1 add_convert_fusion.7
  44.5 1.6 %collective-permute-start.20 = (bf16[64,2048]{1,0:T(8,128)(2,1)S(1)}, bf16[64,2048]{1,0:T(8,128)(2,1)S(1)}, u32[]{:S(2)}, u32[]{:S(2)}) collective-permute-start(bf16[64,2048]{1,0:T(8,128)(2,1)S(1)} %add_convert_fusion.7), channel_id=1, source_target_pairs={{0,4},{1,3},{4,8},{5,1},{8,12},{9,5},{12,14},{13,9},{14,10},{15,13... | collective-permute-start | bytes 786440 | tf_op jit(solution)/shard_map/ppermute | solution.py:254
  46.1 2.7 %expert.8 = (bf16[64,2048]{1,0:T(8,128)(2,1)S(1)}, bf16[64,2048]{1,0:T(8,128)(2,1)S(1)}, bf16[64,2048]{1,0:T(8,128)(2,1)S(1)}, bf16[64,2048]{1,0:T(8,128)(2,1)S(1)}) custom-call(s32[1]{0:T(128)} %bitcast.own_ref, bf16[64,2176]{1,0:T(8,128)(2,1)S(1)} %collective-permute-done.2.refs_0_, bf16[64,2176]{1,0:T(8,128)(2,1)S(1)} %collective-permute-done.6.refs_1_, ...), custom_call_target="tpu_custom_call" | custom-call | flops 524288 | bytes 524288 | tf_op jit(solution)/shard_map/expert/pallas_call | solution.py:115
  48.8 0.1 collective-permute-start.27
  48.9 0.3 collective-permute-done.25
  49.2 0.1 add_convert_fusion.3
  49.3 1.7 %collective-permute-start.26 = (bf16[64,2048]{1,0:T(8,128)(2,1)S(1)}, bf16[64,2048]{1,0:T(8,128)(2,1)S(1)}, u32[]{:S(2)}, u32[]{:S(2)}) collective-permute-start(bf16[64,2048]{1,0:T(8,128)(2,1)S(1)} %add_convert_fusion.3), channel_id=1, source_target_pairs={{0,4},{1,3},{4,8},{5,1},{8,12},{9,5},{12,14},{13,9},{14,10},{15,13... | collective-permute-start | bytes 786440 | tf_op jit(solution)/shard_map/ppermute | solution.py:255
  50.9 0.0 collective-permute-done.18
  50.9 1.0 %collective-permute-done.20 = bf16[64,2048]{1,0:T(8,128)(2,1)S(1)} collective-permute-done((bf16[64,2048]{1,0:T(8,128)(2,1)S(1)}, bf16[64,2048]{1,0:T(8,128)(2,1)S(1)}, u32[]{:S(2)}, u32[]{:S(2)}) %collective-permute-start.20) | collective-permute-done | bytes 262176 | tf_op jit(solution)/shard_map/ppermute | solution.py:254
  52.0 0.1 add_convert_fusion.6
  52.1 1.7 %collective-permute-start.21 = (bf16[64,2048]{1,0:T(8,128)(2,1)S(1)}, bf16[64,2048]{1,0:T(8,128)(2,1)S(1)}, u32[]{:S(2)}, u32[]{:S(2)}) collective-permute-start(bf16[64,2048]{1,0:T(8,128)(2,1)S(1)} %add_convert_fusion.6), channel_id=1, source_target_pairs={{0,4},{1,3},{4,8},{5,1},{8,12},{9,5},{12,14},{13,9},{14,10},{15,13... | collective-permute-start | bytes 786440 | tf_op jit(solution)/shard_map/ppermute | solution.py:254
  53.7 0.0 collective-permute-start.17
  53.8 0.0 collective-permute-done.27
  53.8 1.9 %collective-permute-done.26 = bf16[64,2048]{1,0:T(8,128)(2,1)S(1)} collective-permute-done((bf16[64,2048]{1,0:T(8,128)(2,1)S(1)}, bf16[64,2048]{1,0:T(8,128)(2,1)S(1)}, u32[]{:S(2)}, u32[]{:S(2)}) %collective-permute-start.26) | collective-permute-done | bytes 262176 | tf_op jit(solution)/shard_map/ppermute | solution.py:255
  55.7 0.1 add_convert_fusion.2
  55.8 1.7 %collective-permute-start.28 = (bf16[64,2048]{1,0:T(8,128)(2,1)S(1)}, bf16[64,2048]{1,0:T(8,128)(2,1)S(1)}, u32[]{:S(2)}, u32[]{:S(2)}) collective-permute-start(bf16[64,2048]{1,0:T(8,128)(2,1)S(1)} %add_convert_fusion.2), channel_id=1, source_target_pairs={{0,4},{1,3},{4,8},{5,1},{8,12},{9,5},{12,14},{13,9},{14,10},{15,13... | collective-permute-start | bytes 786440 | tf_op jit(solution)/shard_map/ppermute | solution.py:255
  57.5 1.0 %collective-permute-done.21 = bf16[64,2048]{1,0:T(8,128)(2,1)S(1)} collective-permute-done((bf16[64,2048]{1,0:T(8,128)(2,1)S(1)}, bf16[64,2048]{1,0:T(8,128)(2,1)S(1)}, u32[]{:S(2)}, u32[]{:S(2)}) %collective-permute-start.21) | collective-permute-done | bytes 262176 | tf_op jit(solution)/shard_map/ppermute | solution.py:254
  58.5 0.1 add_convert_fusion.5
  58.6 1.7 %collective-permute-start.22 = (bf16[64,2048]{1,0:T(8,128)(2,1)S(1)}, bf16[64,2048]{1,0:T(8,128)(2,1)S(1)}, u32[]{:S(2)}, u32[]{:S(2)}) collective-permute-start(bf16[64,2048]{1,0:T(8,128)(2,1)S(1)} %add_convert_fusion.5), channel_id=1, source_target_pairs={{0,4},{1,3},{4,8},{5,1},{8,12},{9,5},{12,14},{13,9},{14,10},{15,13... | collective-permute-start | bytes 786440 | tf_op jit(solution)/shard_map/ppermute | solution.py:254
  60.3 2.0 %expert.9 = (bf16[64,2048]{1,0:T(8,128)(2,1)S(1)}, bf16[64,2048]{1,0:T(8,128)(2,1)S(1)}) custom-call(s32[1]{0:T(128)} %bitcast.own_ref, bf16[64,2176]{1,0:T(8,128)(2,1)S(1)} %copy-done, bf16[64,2176]{1,0:T(8,128)(2,1)S(1)} %collective-permute-done.1.refs_1_, bf16[1,2048,768]{2,1,0:T(8,128)(2,1)S(1)} %get-tuple-element.37.refs_4_.refs_2_, ...), custom_call_target="tpu_custom_call" | custom-call | flops 262144 | bytes 262144 | tf_op jit(solution)/shard_map/expert/pallas_call | solution.py:115
  62.3 0.1 add_convert_fusion.1
  62.4 2.6 %collective-permute-done.22 = bf16[64,2048]{1,0:T(8,128)(2,1)S(1)} collective-permute-done((bf16[64,2048]{1,0:T(8,128)(2,1)S(1)}, bf16[64,2048]{1,0:T(8,128)(2,1)S(1)}, u32[]{:S(2)}, u32[]{:S(2)}) %collective-permute-start.22) | collective-permute-done | bytes 262176 | tf_op jit(solution)/shard_map/ppermute | solution.py:254
  65.0 1.5 %collective-permute-done.29 = bf16[64,2048]{1,0:T(8,128)(2,1)S(1)} collective-permute-done((bf16[64,2048]{1,0:T(8,128)(2,1)S(1)}, bf16[64,2048]{1,0:T(8,128)(2,1)S(1)}, u32[]{:S(2)}, u32[]{:S(2)}) %collective-permute-start.29) | collective-permute-done | bytes 262176 | tf_op jit(solution)/shard_map/ppermute | solution.py:258
  66.6 0.8 %add_convert_fusion = bf16[64,2048]{1,0:T(8,128)(2,1)} fusion(bf16[64,2048]{1,0:T(8,128)(2,1)S(1)} %collective-permute-done.29, bf16[64,2048]{1,0:T(8,128)(2,1)S(1)} %get-tuple-element.61, bf16[64,2048]{1,0:T(8,128)(2,1)S(1)} %collective-permute-done.22), kind=kLoop, calls=%fused_computation | loop fusion | flops 786432 | bytes 1048576 | tf_op jit(solution)/shard_map/convert_element_type | solution.py:209
  (15 shorter events, 0.0 us)
Async XLA Ops:
  1.7 3.2 %collective-permute-start.1 = (bf16[64,2176]{1,0:T(8,128)(2,1)}, bf16[64,2176]{1,0:T(8,128)(2,1)S(1)}, u32[]{:S(2)}, u32[]{:S(2)}) collective-permute-start(bf16[64,2176]{1,0:T(8,128)(2,1)} %pack.1.refs_0_), channel_id=1, source_target_pairs={{0,1},{1,0},{2,3},{3,2},{4,5},{5,4},{6,7},{7,6},{8,9},{9,8},{10,11... | collective-permute-start | bytes 835592 | tf_op jit(solution)/shard_map/ppermute | solution.py:225
  2.2 7.3 %collective-permute-start = (bf16[64,2176]{1,0:T(8,128)(2,1)}, bf16[64,2176]{1,0:T(8,128)(2,1)S(1)}, u32[]{:S(2)}, u32[]{:S(2)}) collective-permute-start(bf16[64,2176]{1,0:T(8,128)(2,1)} %pack.1.refs_0_), channel_id=1, source_target_pairs={{0,4},{1,3},{4,8},{5,1},{8,12},{9,5},{12,14},{13,9},{14,10},{15,13... | collective-permute-start | bytes 835592 | tf_op jit(solution)/shard_map/ppermute | solution.py:226
  4.9 7.6 %collective-permute-start.5 = (bf16[64,2176]{1,0:T(8,128)(2,1)S(1)}, bf16[64,2176]{1,0:T(8,128)(2,1)S(1)}, u32[]{:S(2)}, u32[]{:S(2)}) collective-permute-start(bf16[64,2176]{1,0:T(8,128)(2,1)S(1)} %collective-permute-done.1.refs_1_), channel_id=1, source_target_pairs={{0,4},{1,3},{4,8},{5,1},{8,12},{9,5},{12,14},{13,9},{14,10},{15,13... | collective-permute-start | bytes 835592 | tf_op jit(solution)/shard_map/ppermute | solution.py:226
  9.5 7.0 %collective-permute-start.3 = (bf16[64,2176]{1,0:T(8,128)(2,1)S(1)}, bf16[64,2176]{1,0:T(8,128)(2,1)S(1)}, u32[]{:S(2)}, u32[]{:S(2)}) collective-permute-start(bf16[64,2176]{1,0:T(8,128)(2,1)S(1)} %collective-permute-done.refs_2_), channel_id=1, source_target_pairs={{0,4},{1,3},{4,8},{5,1},{8,12},{9,5},{12,14},{13,9},{14,10},{15,13... | collective-permute-start | bytes 835592 | tf_op jit(solution)/shard_map/ppermute | solution.py:239
  12.5 6.5 %collective-permute-start.9 = (bf16[64,2176]{1,0:T(8,128)(2,1)S(1)}, bf16[64,2176]{1,0:T(8,128)(2,1)S(1)}, u32[]{:S(2)}, u32[]{:S(2)}) collective-permute-start(bf16[64,2176]{1,0:T(8,128)(2,1)S(1)} %collective-permute-done.5.refs_3_), channel_id=1, source_target_pairs={{0,4},{1,3},{4,8},{5,1},{8,12},{9,5},{12,14},{13,9},{14,10},{15,13... | collective-permute-start | bytes 835592 | tf_op jit(solution)/shard_map/ppermute | solution.py:235
  14.6 6.6 %collective-permute-start.2 = (bf16[64,2176]{1,0:T(8,128)(2,1)S(1)}, bf16[64,2176]{1,0:T(8,128)(2,1)S(1)}, u32[]{:S(2)}, u32[]{:S(2)}) collective-permute-start(bf16[64,2176]{1,0:T(8,128)(2,1)S(1)} %collective-permute-done.refs_2_), channel_id=1, source_target_pairs={{0,1},{1,0},{2,3},{3,2},{4,5},{5,4},{6,7},{7,6},{8,9},{9,8},{10,11... | collective-permute-start | bytes 835592 | tf_op jit(solution)/shard_map/ppermute | solution.py:236
  16.5 6.6 %collective-permute-start.4 = (bf16[64,2176]{1,0:T(8,128)(2,1)S(1)}, bf16[64,2176]{1,0:T(8,128)(2,1)S(1)}, u32[]{:S(2)}, u32[]{:S(2)}) collective-permute-start(bf16[64,2176]{1,0:T(8,128)(2,1)S(1)} %collective-permute-done.3.refs_2_), channel_id=1, source_target_pairs={{0,4},{1,3},{4,8},{5,1},{8,12},{9,5},{12,14},{13,9},{14,10},{15,13... | collective-permute-start | bytes 835592 | tf_op jit(solution)/shard_map/ppermute | solution.py:239
  18.2 4.9 %collective-permute-start.6 = (bf16[64,2176]{1,0:T(8,128)(2,1)S(1)}, bf16[64,2176]{1,0:T(8,128)(2,1)S(1)}, u32[]{:S(2)}, u32[]{:S(2)}) collective-permute-start(bf16[64,2176]{1,0:T(8,128)(2,1)S(1)} %collective-permute-done.5.refs_3_), channel_id=1, source_target_pairs={{0,1},{1,0},{2,3},{3,2},{4,5},{5,4},{6,7},{7,6},{8,9},{9,8},{10,11... | collective-permute-start | bytes 835592 | tf_op jit(solution)/shard_map/ppermute | solution.py:236
  19.1 7.0 %collective-permute-start.13 = (bf16[64,2176]{1,0:T(8,128)(2,1)S(1)}, bf16[64,2176]{1,0:T(8,128)(2,1)S(1)}, u32[]{:S(2)}, u32[]{:S(2)}) collective-permute-start(bf16[64,2176]{1,0:T(8,128)(2,1)S(1)} %collective-permute-done.9.refs_3_), channel_id=1, source_target_pairs={{0,4},{1,3},{4,8},{5,1},{8,12},{9,5},{12,14},{13,9},{14,10},{15,13... | collective-permute-start | bytes 835592 | tf_op jit(solution)/shard_map/ppermute | solution.py:235
  21.2 4.9 %collective-permute-start.8 = (bf16[64,2176]{1,0:T(8,128)(2,1)S(1)}, bf16[64,2176]{1,0:T(8,128)(2,1)S(1)}, u32[]{:S(2)}, u32[]{:S(2)}) collective-permute-start(bf16[64,2176]{1,0:T(8,128)(2,1)S(1)} %collective-permute-done.3.refs_2_), channel_id=1, source_target_pairs={{0,1},{1,0},{2,3},{3,2},{4,5},{5,4},{6,7},{7,6},{8,9},{9,8},{10,11... | collective-permute-start | bytes 835592 | tf_op jit(solution)/shard_map/ppermute | solution.py:236
  21.2 4.9 %collective-permute-start.10 = (bf16[64,2176]{1,0:T(8,128)(2,1)S(1)}, bf16[64,2176]{1,0:T(8,128)(2,1)S(1)}, u32[]{:S(2)}, u32[]{:S(2)}) collective-permute-start(bf16[64,2176]{1,0:T(8,128)(2,1)S(1)} %collective-permute-done.9.refs_3_), channel_id=1, source_target_pairs={{0,1},{1,0},{2,3},{3,2},{4,5},{5,4},{6,7},{7,6},{8,9},{9,8},{10,11... | collective-permute-start | bytes 835592 | tf_op jit(solution)/shard_map/ppermute | solution.py:236
  23.1 5.7 %collective-permute-start.11 = (bf16[64,2176]{1,0:T(8,128)(2,1)S(1)}, bf16[64,2176]{1,0:T(8,128)(2,1)S(1)}, u32[]{:S(2)}, u32[]{:S(2)}) collective-permute-start(bf16[64,2176]{1,0:T(8,128)(2,1)S(1)} %collective-permute-done.4.refs_2_), channel_id=1, source_target_pairs={{0,1},{1,0},{2,3},{3,2},{4,5},{5,4},{6,7},{7,6},{8,9},{9,8},{10,11... | collective-permute-start | bytes 835592 | tf_op jit(solution)/shard_map/ppermute | solution.py:236
  23.1 6.5 %collective-permute-start.7 = (bf16[64,2176]{1,0:T(8,128)(2,1)S(1)}, bf16[64,2176]{1,0:T(8,128)(2,1)S(1)}, u32[]{:S(2)}, u32[]{:S(2)}) collective-permute-start(bf16[64,2176]{1,0:T(8,128)(2,1)S(1)} %collective-permute-done.4.refs_2_), channel_id=1, source_target_pairs={{0,4},{1,3},{4,8},{5,1},{8,12},{9,5},{12,14},{13,9},{14,10},{15,13... | collective-permute-start | bytes 835592 | tf_op jit(solution)/shard_map/ppermute | solution.py:239
  26.1 3.6 %collective-permute-start.14 = (bf16[64,2176]{1,0:T(8,128)(2,1)S(1)}, bf16[64,2176]{1,0:T(8,128)(2,1)S(1)}, u32[]{:S(2)}, u32[]{:S(2)}) collective-permute-start(bf16[64,2176]{1,0:T(8,128)(2,1)S(1)} %collective-permute-done.13.refs_3_), channel_id=1, source_target_pairs={{0,1},{1,0},{2,3},{3,2},{4,5},{5,4},{6,7},{7,6},{8,9},{9,8},{10,11... | collective-permute-start | bytes 835592 | tf_op jit(solution)/shard_map/ppermute | solution.py:236
  29.7 2.7 %collective-permute-start.12 = (bf16[64,2176]{1,0:T(8,128)(2,1)S(1)}, bf16[64,2176]{1,0:T(8,128)(2,1)S(1)}, u32[]{:S(2)}, u32[]{:S(2)}) collective-permute-start(bf16[64,2176]{1,0:T(8,128)(2,1)S(1)} %collective-permute-done.7.refs_1_), channel_id=1, source_target_pairs={{0,1},{1,0},{2,3},{3,2},{4,5},{5,4},{6,7},{7,6},{8,9},{9,8},{10,11... | collective-permute-start | bytes 835592 | tf_op jit(solution)/shard_map/ppermute | solution.py:245
  34.4 1.7 %collective-permute-start.15 = (bf16[64,2048]{1,0:T(8,128)(2,1)S(1)}, bf16[64,2048]{1,0:T(8,128)(2,1)S(1)}, u32[]{:S(2)}, u32[]{:S(2)}) collective-permute-start(bf16[64,2048]{1,0:T(8,128)(2,1)S(1)} %get-tuple-element.48), channel_id=1, source_target_pairs={{0,1},{1,0},{2,3},{3,2},{4,5},{5,4},{6,7},{7,6},{8,9},{9,8},{10,11... | collective-permute-start | bytes 786440 | tf_op jit(solution)/shard_map/ppermute | solution.py:246
  35.0 3.4 %collective-permute-start.24 = (bf16[64,2048]{1,0:T(8,128)(2,1)S(1)}, bf16[64,2048]{1,0:T(8,128)(2,1)S(1)}, u32[]{:S(2)}, u32[]{:S(2)}) collective-permute-start(bf16[64,2048]{1,0:T(8,128)(2,1)S(1)} %get-tuple-element.57), channel_id=1, source_target_pairs={{0,1},{1,0},{2,3},{3,2},{4,5},{5,4},{6,7},{7,6},{8,9},{9,8},{10,11... | collective-permute-start | bytes 786440 | tf_op jit(solution)/shard_map/ppermute | solution.py:253
  36.2 6.4 %collective-permute-start.16 = (bf16[64,2048]{1,0:T(8,128)(2,1)S(1)}, bf16[64,2048]{1,0:T(8,128)(2,1)S(1)}, u32[]{:S(2)}, u32[]{:S(2)}) collective-permute-start(bf16[64,2048]{1,0:T(8,128)(2,1)S(1)} %add_convert_fusion.8), channel_id=1, source_target_pairs={{0,4},{1,3},{4,8},{5,1},{8,12},{9,5},{12,14},{13,9},{14,10},{15,13... | collective-permute-start | bytes 786440 | tf_op jit(solution)/shard_map/ppermute | solution.py:246
  37.9 13.1 %collective-permute-start.18 = (bf16[64,2048]{1,0:T(8,128)(2,1)S(1)}, bf16[64,2048]{1,0:T(8,128)(2,1)S(1)}, u32[]{:S(2)}, u32[]{:S(2)}) collective-permute-start(bf16[64,2048]{1,0:T(8,128)(2,1)S(1)} %get-tuple-element.53), channel_id=1, source_target_pairs={{0,1},{1,0},{2,3},{3,2},{4,5},{5,4},{6,7},{7,6},{8,9},{9,8},{10,11... | collective-permute-start | bytes 786440 | tf_op jit(solution)/shard_map/ppermute | solution.py:253
  37.9 11.3 %collective-permute-start.23 = (bf16[64,2048]{1,0:T(8,128)(2,1)S(1)}, bf16[64,2048]{1,0:T(8,128)(2,1)S(1)}, u32[]{:S(2)}, u32[]{:S(2)}) collective-permute-start(bf16[64,2048]{1,0:T(8,128)(2,1)S(1)} %get-tuple-element.56), channel_id=1, source_target_pairs={{0,1},{1,0},{2,3},{3,2},{4,5},{5,4},{6,7},{7,6},{8,9},{9,8},{10,11... | collective-permute-start | bytes 786440 | tf_op jit(solution)/shard_map/ppermute | solution.py:253
  38.4 6.0 %collective-permute-start.19 = (bf16[64,2048]{1,0:T(8,128)(2,1)S(1)}, bf16[64,2048]{1,0:T(8,128)(2,1)S(1)}, u32[]{:S(2)}, u32[]{:S(2)}) collective-permute-start(bf16[64,2048]{1,0:T(8,128)(2,1)S(1)} %get-tuple-element.55), channel_id=1, source_target_pairs={{0,1},{1,0},{2,3},{3,2},{4,5},{5,4},{6,7},{7,6},{8,9},{9,8},{10,11... | collective-permute-start | bytes 786440 | tf_op jit(solution)/shard_map/ppermute | solution.py:253
  42.7 6.4 %collective-permute-start.25 = (bf16[64,2048]{1,0:T(8,128)(2,1)S(1)}, bf16[64,2048]{1,0:T(8,128)(2,1)S(1)}, u32[]{:S(2)}, u32[]{:S(2)}) collective-permute-start(bf16[64,2048]{1,0:T(8,128)(2,1)S(1)} %add_convert_fusion.4), channel_id=1, source_target_pairs={{0,4},{1,3},{4,8},{5,1},{8,12},{9,5},{12,14},{13,9},{14,10},{15,13... | collective-permute-start | bytes 786440 | tf_op jit(solution)/shard_map/ppermute | solution.py:255
  44.5 7.5 %collective-permute-start.20 = (bf16[64,2048]{1,0:T(8,128)(2,1)S(1)}, bf16[64,2048]{1,0:T(8,128)(2,1)S(1)}, u32[]{:S(2)}, u32[]{:S(2)}) collective-permute-start(bf16[64,2048]{1,0:T(8,128)(2,1)S(1)} %add_convert_fusion.7), channel_id=1, source_target_pairs={{0,4},{1,3},{4,8},{5,1},{8,12},{9,5},{12,14},{13,9},{14,10},{15,13... | collective-permute-start | bytes 786440 | tf_op jit(solution)/shard_map/ppermute | solution.py:254
  48.8 11.5 %copy-start = (bf16[64,2176]{1,0:T(8,128)(2,1)S(1)}, bf16[64,2176]{1,0:T(8,128)(2,1)}, u32[]{:S(2)}) copy-start(bf16[64,2176]{1,0:T(8,128)(2,1)} %pack.1.refs_0_) | copy-start | bytes 835588
  48.8 5.0 %collective-permute-start.27 = (bf16[64,2048]{1,0:T(8,128)(2,1)S(1)}, bf16[64,2048]{1,0:T(8,128)(2,1)S(1)}, u32[]{:S(2)}, u32[]{:S(2)}) collective-permute-start(bf16[64,2048]{1,0:T(8,128)(2,1)S(1)} %get-tuple-element.62), channel_id=1, source_target_pairs={{0,1},{1,0},{2,3},{3,2},{4,5},{5,4},{6,7},{7,6},{8,9},{9,8},{10,11... | collective-permute-start | bytes 786440 | tf_op jit(solution)/shard_map/ppermute | solution.py:253
  49.3 6.4 %collective-permute-start.26 = (bf16[64,2048]{1,0:T(8,128)(2,1)S(1)}, bf16[64,2048]{1,0:T(8,128)(2,1)S(1)}, u32[]{:S(2)}, u32[]{:S(2)}) collective-permute-start(bf16[64,2048]{1,0:T(8,128)(2,1)S(1)} %add_convert_fusion.3), channel_id=1, source_target_pairs={{0,4},{1,3},{4,8},{5,1},{8,12},{9,5},{12,14},{13,9},{14,10},{15,13... | collective-permute-start | bytes 786440 | tf_op jit(solution)/shard_map/ppermute | solution.py:255
  52.1 6.4 %collective-permute-start.21 = (bf16[64,2048]{1,0:T(8,128)(2,1)S(1)}, bf16[64,2048]{1,0:T(8,128)(2,1)S(1)}, u32[]{:S(2)}, u32[]{:S(2)}) collective-permute-start(bf16[64,2048]{1,0:T(8,128)(2,1)S(1)} %add_convert_fusion.6), channel_id=1, source_target_pairs={{0,4},{1,3},{4,8},{5,1},{8,12},{9,5},{12,14},{13,9},{14,10},{15,13... | collective-permute-start | bytes 786440 | tf_op jit(solution)/shard_map/ppermute | solution.py:254
  53.7 4.8 %collective-permute-start.17 = (bf16[64,2048]{1,0:T(8,128)(2,1)S(1)}, bf16[64,2048]{1,0:T(8,128)(2,1)S(1)}, u32[]{:S(2)}, u32[]{:S(2)}) collective-permute-start(bf16[64,2048]{1,0:T(8,128)(2,1)S(1)} %get-tuple-element.51), channel_id=1, source_target_pairs={{0,1},{1,0},{2,3},{3,2},{4,5},{5,4},{6,7},{7,6},{8,9},{9,8},{10,11... | collective-permute-start | bytes 786440 | tf_op jit(solution)/shard_map/ppermute | solution.py:253
  55.8 6.5 %collective-permute-start.28 = (bf16[64,2048]{1,0:T(8,128)(2,1)S(1)}, bf16[64,2048]{1,0:T(8,128)(2,1)S(1)}, u32[]{:S(2)}, u32[]{:S(2)}) collective-permute-start(bf16[64,2048]{1,0:T(8,128)(2,1)S(1)} %add_convert_fusion.2), channel_id=1, source_target_pairs={{0,4},{1,3},{4,8},{5,1},{8,12},{9,5},{12,14},{13,9},{14,10},{15,13... | collective-permute-start | bytes 786440 | tf_op jit(solution)/shard_map/ppermute | solution.py:255
  58.6 6.4 %collective-permute-start.22 = (bf16[64,2048]{1,0:T(8,128)(2,1)S(1)}, bf16[64,2048]{1,0:T(8,128)(2,1)S(1)}, u32[]{:S(2)}, u32[]{:S(2)}) collective-permute-start(bf16[64,2048]{1,0:T(8,128)(2,1)S(1)} %add_convert_fusion.5), channel_id=1, source_target_pairs={{0,4},{1,3},{4,8},{5,1},{8,12},{9,5},{12,14},{13,9},{14,10},{15,13... | collective-permute-start | bytes 786440 | tf_op jit(solution)/shard_map/ppermute | solution.py:254
  65.0 1.5 %collective-permute-start.29 = (bf16[64,2048]{1,0:T(8,128)(2,1)S(1)}, bf16[64,2048]{1,0:T(8,128)(2,1)S(1)}, u32[]{:S(2)}, u32[]{:S(2)}) collective-permute-start(bf16[64,2048]{1,0:T(8,128)(2,1)S(1)} %add_convert_fusion.1), channel_id=1, source_target_pairs={{0,1},{1,0},{2,3},{3,2},{4,5},{5,4},{6,7},{7,6},{8,9},{9,8},{10,11... | collective-permute-start | bytes 786440 | tf_op jit(solution)/shard_map/ppermute | solution.py:258

commit v8 on v6

--- a/solution.py
+++ b/solution.py
@@ -234,26 +234,30 @@
         if step > 1:
             second = ring(second)
         blocks[step] = (swap(first), swap(second), first, second)
+        if step == rounds - 1:
+            first = after(first, *blocks[1][:2])
         first = ring(first)
         if step == 1:
             first = after(first, down_w)
-    sums = {2: run(*blocks[2])}
-    first = after(first, sums[2][0], *blocks[1][:2], blocks[3][0])
-    keep, send, *sums[3] = run(swap(first), first, *blocks[3])
+    *second_sums, early, early_send = run(*blocks[2], blocks[3][0], blocks[3][2])
+    late = run(blocks[3][1], blocks[3][3])
+    sums = {2: second_sums, 3: (early, late[0], early_send, late[1])}
+    first = after(first, early, blocks[3][1])
+    send, keep = run(after(swap(first), late[0]), first)
     lead, trail = ring(added(keep, swap(send))), None
     for step in (3, 2, 1):
         if step == 3:
             sums[1] = run(after(blocks[1][0], lead), *blocks[1][1:])
         if step == 2:
             lead = after(lead, sums[1][0])
-        keep, keep_trail, send, send_trail = sums[step]
+        keep_trail, keep, send_trail, send = sums[step]
         send, send_trail = swap(send), swap(send_trail)
         trail = ring(added(*([keep_trail, send_trail] + ([] if trail is None else [trail]))))
         lead = ring(added(keep, send, lead))
-        if step == 2:
+        if step == 3:
             kept, other = run(after(mine, lead), sibling)
-    last = swap(added(lead, other))
-    return added(trail, kept, last)
+    last = swap(added(trail, other))
+    return added(lead, kept, last)
 
 
 def solution(mesh):

time: 70.2 us -> 64.7 us (0.922)
  waiting for transfers between devices: 22.7 us -> 14.8 us
  Pallas kernels: 17.7 us -> 19.1 us
  starting transfers between devices: 27.9 us -> 28.9 us
    ppermute x3, waiting for transfers between devices: 4.2 us -> 1.44 us  [dense_body(): first = ring(first)]
    ppermute x3, waiting for transfers between devices: 4.52 us -> 2.12 us  [dense_body(): ring(added(*[keep_trail, send_trail] + ([] if trail is None else [trail])))]
    ppermute x3, waiting for transfers between devices: 2.44 us -> 4.56 us  [dense_body(): lead = ring(added(keep, send, lead))]
    ppermute x2, waiting for transfers between devices: 5.26 us -> 3.49 us  [dense_body(): lead, trail = (ring(added(keep, swap(send))), None)]
    ppermute x2, waiting for transfers between devices: 3.86 us -> 2.24 us  [dense_body(): second = ring(second)]
    pallas_call x4 -> x5, Pallas kernels: 11.2 us -> 12.7 us  [run_expert(): pl.pallas_call(functools.partial(expert_kernel, experts, len(blocks)), ou...]
    ppermute x6, waiting for transfers between devices: 1.06 us -> 0.02 us  [dense_body(): blocks[step] = (swap(first), swap(second), first, second)]
  transfers between devices with their start and end apart: 30 -> 30, of which waited for: 15 -> 11; matrix products, arithmetic and copies ran while one was open for 1% -> 1% of each run, Pallas kernels for 17% -> 24%
where the time goes in v8:
time: 64.7 us; the launch traced here: 64.5 us
  starting transfers between devices  28.9 us (45%)
  Pallas kernels  19.1 us (30%)
  waiting for transfers between devices  14.8 us (23%)
  other arithmetic  1.49 us (2%)
    pallas_call x5, Pallas kernels, run_expert(): pl.pallas_call(functools.partial(expert_kernel, experts, len(blocks)), ou...  12.7 us
    ppermute x3, starting transfers between devices, dense_body(): first = ring(first)  5.39 us
    ppermute x3, starting transfers between devices, dense_body(): lead = ring(added(keep, send, lead))  4.93 us
    ppermute x3, starting transfers between devices, dense_body(): ring(added(*[keep_trail, send_trail] + ([] if trail is None else [trail])))  4.92 us
    pallas_call x2, Pallas kernels, load_weights(): pl.pallas_call(functools.partial(load_kernel, pieces), out_shape=[pltpu.V...  4.73 us
    ppermute x3, waiting for transfers between devices, dense_body(): lead = ring(added(keep, send, lead))  4.56 us
    ppermute x2, starting transfers between devices, dense_body(): first, second = (ring(mine), ring(sibling))  4.34 us
    ppermute x2, starting transfers between devices, dense_body(): second = ring(second)  4.21 us
  transfers between devices with their start and end apart: 30, of which 11 were waited for; matrix products, arithmetic and copies ran while one was open for 1% of the time, Pallas kernels for 24%

profile of v8, /device:TPU:0, one launch (start us, length us, event | category | flops | bytes accessed | tf_op | source)
XLA Modules:
  0.0 64.5 jit_solution(11841612257836180050)
XLA Ops:
  0.0 1.7 %pack.1.refs_0_ = bf16[64,2176]{1,0:T(8,128)(2,1)} custom-call(bf16[64,2048]{1,0:T(8,128)(2,1)} %tokens_ref, s32[8,64]{1,0:T(8,128)} %bitcast.3, f32[8,64]{1,0:T(8,128)} %bitcast.4), custom_call_target="tpu_custom_call" | custom-call | bytes 1024 | tf_op jit(solution)/shard_map/pack/pallas_call | solution.py:190
  1.7 0.5 collective-permute-start.1
  2.2 2.6 %collective-permute-start = (bf16[64,2176]{1,0:T(8,128)(2,1)}, bf16[64,2176]{1,0:T(8,128)(2,1)S(1)}, u32[]{:S(2)}, u32[]{:S(2)}) collective-permute-start(bf16[64,2176]{1,0:T(8,128)(2,1)} %pack.1.refs_0_), channel_id=1, source_target_pairs={{0,4},{1,3},{4,8},{5,1},{8,12},{9,5},{12,14},{13,9},{14,10},{15,13... | collective-permute-start | bytes 835592 | tf_op jit(solution)/shard_map/ppermute | solution.py:226
  4.9 0.0 collective-permute-done.1.refs_1_
  4.9 1.7 %collective-permute-start.5 = (bf16[64,2176]{1,0:T(8,128)(2,1)S(1)}, bf16[64,2176]{1,0:T(8,128)(2,1)S(1)}, u32[]{:S(2)}, u32[]{:S(2)}) collective-permute-start(bf16[64,2176]{1,0:T(8,128)(2,1)S(1)} %collective-permute-done.1.refs_1_), channel_id=1, source_target_pairs={{0,4},{1,3},{4,8},{5,1},{8,12},{9,5},{12,14},{13,9},{14,10},{15,13... | collective-permute-start | bytes 835592 | tf_op jit(solution)/shard_map/ppermute | solution.py:226
  6.6 2.9 %load.2 = (bf16[1,2048,768]{2,1,0:T(8,128)(2,1)S(1)}, bf16[1,2048,768]{2,1,0:T(8,128)(2,1)S(1)}) custom-call(bf16[1,2048,768]{2,1,0:T(8,128)(2,1)} %refs_0_, bf16[1,2048,768]{2,1,0:T(8,128)(2,1)} %refs_1_.1), custom_call_target="tpu_custom_call" | custom-call | bytes 1024 | tf_op jit(solution)/shard_map/load/pallas_call | solution.py:148
  9.4 0.1 collective-permute-done.refs_2_
  9.5 2.1 %collective-permute-start.3 = (bf16[64,2176]{1,0:T(8,128)(2,1)S(1)}, bf16[64,2176]{1,0:T(8,128)(2,1)S(1)}, u32[]{:S(2)}, u32[]{:S(2)}) collective-permute-start(bf16[64,2176]{1,0:T(8,128)(2,1)S(1)} %collective-permute-done.refs_2_), channel_id=1, source_target_pairs={{0,4},{1,3},{4,8},{5,1},{8,12},{9,5},{12,14},{13,9},{14,10},{15,13... | collective-permute-start | bytes 835592 | tf_op jit(solution)/shard_map/ppermute | solution.py:239
  11.6 0.9 %collective-permute-done.5.refs_3_ = bf16[64,2176]{1,0:T(8,128)(2,1)S(1)} collective-permute-done((bf16[64,2176]{1,0:T(8,128)(2,1)S(1)}, bf16[64,2176]{1,0:T(8,128)(2,1)S(1)}, u32[]{:S(2)}, u32[]{:S(2)}) %collective-permute-start.5) | collective-permute-done | bytes 278560 | tf_op jit(solution)/shard_map/ppermute | solution.py:226
  12.5 2.1 %collective-permute-start.9 = (bf16[64,2176]{1,0:T(8,128)(2,1)S(1)}, bf16[64,2176]{1,0:T(8,128)(2,1)S(1)}, u32[]{:S(2)}, u32[]{:S(2)}) collective-permute-start(bf16[64,2176]{1,0:T(8,128)(2,1)S(1)} %collective-permute-done.5.refs_3_), channel_id=1, source_target_pairs={{0,4},{1,3},{4,8},{5,1},{8,12},{9,5},{12,14},{13,9},{14,10},{15,13... | collective-permute-start | bytes 835592 | tf_op jit(solution)/shard_map/ppermute | solution.py:235
  14.6 0.0 collective-permute-start.2
  14.6 1.9 %load.3.refs_8_.refs_4_.refs_6_ = bf16[1,2048,768]{2,1,0:T(8,128)(2,1)S(1)} custom-call(bf16[1,2048,768]{2,1,0:T(8,128)(2,1)} %refs_0_.1), custom_call_target="tpu_custom_call" | custom-call | bytes 1024 | tf_op jit(solution)/shard_map/load/pallas_call | solution.py:148
  16.5 1.7 %collective-permute-start.4 = (bf16[64,2176]{1,0:T(8,128)(2,1)S(1)}, bf16[64,2176]{1,0:T(8,128)(2,1)S(1)}, u32[]{:S(2)}, u32[]{:S(2)}) collective-permute-start(bf16[64,2176]{1,0:T(8,128)(2,1)S(1)} %collective-permute-done.3.refs_2_), channel_id=1, source_target_pairs={{0,4},{1,3},{4,8},{5,1},{8,12},{9,5},{12,14},{13,9},{14,10},{15,13... | collective-permute-start | bytes 835592 | tf_op jit(solution)/shard_map/ppermute | solution.py:239
  18.2 0.9 %collective-permute-done.9.refs_3_ = bf16[64,2176]{1,0:T(8,128)(2,1)S(1)} collective-permute-done((bf16[64,2176]{1,0:T(8,128)(2,1)S(1)}, bf16[64,2176]{1,0:T(8,128)(2,1)S(1)}, u32[]{:S(2)}, u32[]{:S(2)}) %collective-permute-start.9) | collective-permute-done | bytes 278560 | tf_op jit(solution)/shard_map/ppermute | solution.py:235
  19.1 2.1 %collective-permute-start.12 = (bf16[64,2176]{1,0:T(8,128)(2,1)S(1)}, bf16[64,2176]{1,0:T(8,128)(2,1)S(1)}, u32[]{:S(2)}, u32[]{:S(2)}) collective-permute-start(bf16[64,2176]{1,0:T(8,128)(2,1)S(1)} %collective-permute-done.9.refs_3_), channel_id=1, source_target_pairs={{0,4},{1,3},{4,8},{5,1},{8,12},{9,5},{12,14},{13,9},{14,10},{15,13... | collective-permute-start | bytes 835592 | tf_op jit(solution)/shard_map/ppermute | solution.py:235
  21.2 0.0 collective-permute-start.8
  21.2 0.0 collective-permute-done.2.refs_0_
  21.2 0.5 collective-permute-start.10
  21.7 1.4 %collective-permute-done.4.refs_5_ = bf16[64,2176]{1,0:T(8,128)(2,1)S(1)} collective-permute-done((bf16[64,2176]{1,0:T(8,128)(2,1)S(1)}, bf16[64,2176]{1,0:T(8,128)(2,1)S(1)}, u32[]{:S(2)}, u32[]{:S(2)}) %collective-permute-start.4) | collective-permute-done | bytes 278560 | tf_op jit(solution)/shard_map/ppermute | solution.py:239
  23.1 0.0 collective-permute-start.11
  23.1 0.0 collective-permute-done.6.refs_1_
  23.1 1.6 %collective-permute-start.7 = (bf16[64,2176]{1,0:T(8,128)(2,1)S(1)}, bf16[64,2176]{1,0:T(8,128)(2,1)S(1)}, u32[]{:S(2)}, u32[]{:S(2)}) collective-permute-start(bf16[64,2176]{1,0:T(8,128)(2,1)S(1)} %collective-permute-done.4.refs_5_), channel_id=1, source_target_pairs={{0,4},{1,3},{4,8},{5,1},{8,12},{9,5},{12,14},{13,9},{14,10},{15,13... | collective-permute-start | bytes 835592 | tf_op jit(solution)/shard_map/ppermute | solution.py:239
  24.7 1.4 %collective-permute-done.12.refs_1_ = bf16[64,2176]{1,0:T(8,128)(2,1)S(1)} collective-permute-done((bf16[64,2176]{1,0:T(8,128)(2,1)S(1)}, bf16[64,2176]{1,0:T(8,128)(2,1)S(1)}, u32[]{:S(2)}, u32[]{:S(2)}) %collective-permute-start.12) | collective-permute-done | bytes 278560 | tf_op jit(solution)/shard_map/ppermute | solution.py:235
  26.1 0.0 collective-permute-start.13
  26.1 3.9 %expert.5 = (bf16[64,2048]{1,0:T(8,128)(2,1)S(1)}, bf16[64,2048]{1,0:T(8,128)(2,1)S(1)}, bf16[64,2048]{1,0:T(8,128)(2,1)S(1)}, bf16[64,2048]{1,0:T(8,128)(2,1)S(...) custom-call(s32[1]{0:T(128)} %bitcast.own_ref, bf16[64,2176]{1,0:T(8,128)(2,1)S(1)} %collective-permute-done.8.refs_0_, ...), custom_call_target="tpu_custom_call" | custom-call | flops 786432 | bytes 786432 | tf_op jit(solution)/shard_map/expert/pallas_call | solution.py:115
  30.0 0.0 collective-permute-done.7.refs_1_
  30.1 0.6 collective-permute-start.14
  30.6 2.0 %expert.6 = (bf16[64,2048]{1,0:T(8,128)(2,1)S(1)}, bf16[64,2048]{1,0:T(8,128)(2,1)S(1)}) custom-call(s32[1]{0:T(128)} %bitcast.own_ref, bf16[64,2176]{1,0:T(8,128)(2,1)S(1)} %collective-permute-done.13.refs_0_, bf16[64,2176]{1,0:T(8,128)(2,1)S(1)} %collective-permute-done.12.refs_1_, bf16[1,2048,768]{2,1,0:T(8,128)(2,1)S(1)} %get-tuple-element.36.refs_6_.refs_2_.refs_4_, ...), custom_call_target="tpu_custom_call" | custom-call | flops 262144 | bytes 262144 | tf_op jit(solution)/shard_map/expert/pallas_call | solution.py:115
  32.7 2.0 %expert.7 = (bf16[64,2048]{1,0:T(8,128)(2,1)S(1)}, bf16[64,2048]{1,0:T(8,128)(2,1)S(1)}) custom-call(s32[1]{0:T(128)} %bitcast.own_ref, bf16[64,2176]{1,0:T(8,128)(2,1)S(1)} %collective-permute-done.14.refs_0_, bf16[64,2176]{1,0:T(8,128)(2,1)S(1)} %collective-permute-done.7.refs_1_, bf16[1,2048,768]{2,1,0:T(8,128)(2,1)S(1)} %get-tuple-element.36.refs_6_.refs_2_.refs_4_, ...), custom_call_target="tpu_custom_call" | custom-call | flops 262144 | bytes 262144 | tf_op jit(solution)/shard_map/expert/pallas_call | solution.py:115
  34.7 0.1 collective-permute-start.15
  34.8 0.5 collective-permute-start.18
  35.3 0.1 collective-permute-start.25
  35.4 0.4 collective-permute-start.24
  35.8 0.1 collective-permute-start.19
  35.9 0.4 collective-permute-done.15
  36.3 0.1 add_convert_fusion.8
  36.4 1.7 %collective-permute-start.16 = (bf16[64,2048]{1,0:T(8,128)(2,1)S(1)}, bf16[64,2048]{1,0:T(8,128)(2,1)S(1)}, u32[]{:S(2)}, u32[]{:S(2)}) collective-permute-start(bf16[64,2048]{1,0:T(8,128)(2,1)S(1)} %add_convert_fusion.8), channel_id=1, source_target_pairs={{0,4},{1,3},{4,8},{5,1},{8,12},{9,5},{12,14},{13,9},{14,10},{15,13... | collective-permute-start | bytes 786440 | tf_op jit(solution)/shard_map/ppermute | solution.py:247
  38.1 0.0 collective-permute-done.25
  38.1 0.1 add_convert_fusion.4
  38.1 1.6 %collective-permute-start.26 = (bf16[64,2048]{1,0:T(8,128)(2,1)S(1)}, bf16[64,2048]{1,0:T(8,128)(2,1)S(1)}, u32[]{:S(2)}, u32[]{:S(2)}) collective-permute-start(bf16[64,2048]{1,0:T(8,128)(2,1)S(1)} %add_convert_fusion.4), channel_id=1, source_target_pairs={{0,4},{1,3},{4,8},{5,1},{8,12},{9,5},{12,14},{13,9},{14,10},{15,13... | collective-permute-start | bytes 786440 | tf_op jit(solution)/shard_map/ppermute | solution.py:255
  39.8 0.0 collective-permute-done.19
  39.8 3.1 %collective-permute-done.16 = bf16[64,2048]{1,0:T(8,128)(2,1)S(1)} collective-permute-done((bf16[64,2048]{1,0:T(8,128)(2,1)S(1)}, bf16[64,2048]{1,0:T(8,128)(2,1)S(1)}, u32[]{:S(2)}, u32[]{:S(2)}) %collective-permute-start.16) | collective-permute-done | bytes 262176 | tf_op jit(solution)/shard_map/ppermute | solution.py:247
  42.8 0.1 add_convert_fusion.7
  42.9 1.7 %collective-permute-start.20 = (bf16[64,2048]{1,0:T(8,128)(2,1)S(1)}, bf16[64,2048]{1,0:T(8,128)(2,1)S(1)}, u32[]{:S(2)}, u32[]{:S(2)}) collective-permute-start(bf16[64,2048]{1,0:T(8,128)(2,1)S(1)} %add_convert_fusion.7), channel_id=1, source_target_pairs={{0,4},{1,3},{4,8},{5,1},{8,12},{9,5},{12,14},{13,9},{14,10},{15,13... | collective-permute-start | bytes 786440 | tf_op jit(solution)/shard_map/ppermute | solution.py:256
  44.6 0.0 collective-permute-done.24
  44.6 1.0 %collective-permute-done.26 = bf16[64,2048]{1,0:T(8,128)(2,1)S(1)} collective-permute-done((bf16[64,2048]{1,0:T(8,128)(2,1)S(1)}, bf16[64,2048]{1,0:T(8,128)(2,1)S(1)}, u32[]{:S(2)}, u32[]{:S(2)}) %collective-permute-start.26) | collective-permute-done | bytes 262176 | tf_op jit(solution)/shard_map/ppermute | solution.py:255
  45.6 0.1 add_convert_fusion.3
  45.7 1.7 %collective-permute-start.27 = (bf16[64,2048]{1,0:T(8,128)(2,1)S(1)}, bf16[64,2048]{1,0:T(8,128)(2,1)S(1)}, u32[]{:S(2)}, u32[]{:S(2)}) collective-permute-start(bf16[64,2048]{1,0:T(8,128)(2,1)S(1)} %add_convert_fusion.3), channel_id=1, source_target_pairs={{0,4},{1,3},{4,8},{5,1},{8,12},{9,5},{12,14},{13,9},{14,10},{15,13... | collective-permute-start | bytes 786440 | tf_op jit(solution)/shard_map/ppermute | solution.py:255
  47.4 2.6 %expert.8 = (bf16[64,2048]{1,0:T(8,128)(2,1)S(1)}, bf16[64,2048]{1,0:T(8,128)(2,1)S(1)}, bf16[64,2048]{1,0:T(8,128)(2,1)S(1)}, bf16[64,2048]{1,0:T(8,128)(2,1)S(1)}) custom-call(s32[1]{0:T(128)} %bitcast.own_ref, bf16[64,2176]{1,0:T(8,128)(2,1)S(1)} %collective-permute-done.2.refs_0_, bf16[64,2176]{1,0:T(8,128)(2,1)S(1)} %collective-permute-done.6.refs_1_, ...), custom_call_target="tpu_custom_call" | custom-call | flops 524288 | bytes 524288 | tf_op jit(solution)/shard_map/expert/pallas_call | solution.py:115
  50.1 0.1 collective-permute-start.17
  50.1 0.5 collective-permute-start.23
  50.6 0.1 add_convert_fusion.6
  50.8 1.6 %collective-permute-start.21 = (bf16[64,2048]{1,0:T(8,128)(2,1)S(1)}, bf16[64,2048]{1,0:T(8,128)(2,1)S(1)}, u32[]{:S(2)}, u32[]{:S(2)}) collective-permute-start(bf16[64,2048]{1,0:T(8,128)(2,1)S(1)} %add_convert_fusion.6), channel_id=1, source_target_pairs={{0,4},{1,3},{4,8},{5,1},{8,12},{9,5},{12,14},{13,9},{14,10},{15,13... | collective-permute-start | bytes 786440 | tf_op jit(solution)/shard_map/ppermute | solution.py:256
  52.4 0.1 add_convert_fusion.2
  52.5 1.6 %collective-permute-start.28 = (bf16[64,2048]{1,0:T(8,128)(2,1)S(1)}, bf16[64,2048]{1,0:T(8,128)(2,1)S(1)}, u32[]{:S(2)}, u32[]{:S(2)}) collective-permute-start(bf16[64,2048]{1,0:T(8,128)(2,1)S(1)} %add_convert_fusion.2), channel_id=1, source_target_pairs={{0,4},{1,3},{4,8},{5,1},{8,12},{9,5},{12,14},{13,9},{14,10},{15,13... | collective-permute-start | bytes 786440 | tf_op jit(solution)/shard_map/ppermute | solution.py:255
  54.1 2.0 %expert.9 = (bf16[64,2048]{1,0:T(8,128)(2,1)S(1)}, bf16[64,2048]{1,0:T(8,128)(2,1)S(1)}) custom-call(s32[1]{0:T(128)} %bitcast.own_ref, bf16[64,2176]{1,0:T(8,128)(2,1)S(1)} %copy-done, bf16[64,2176]{1,0:T(8,128)(2,1)S(1)} %collective-permute-done.1.refs_1_, bf16[1,2048,768]{2,1,0:T(8,128)(2,1)S(1)} %get-tuple-element.36.refs_6_.refs_2_.refs_4_, ...), custom_call_target="tpu_custom_call" | custom-call | flops 262144 | bytes 262144 | tf_op jit(solution)/shard_map/expert/pallas_call | solution.py:115
  56.2 1.0 %collective-permute-done.21 = bf16[64,2048]{1,0:T(8,128)(2,1)S(1)} collective-permute-done((bf16[64,2048]{1,0:T(8,128)(2,1)S(1)}, bf16[64,2048]{1,0:T(8,128)(2,1)S(1)}, u32[]{:S(2)}, u32[]{:S(2)}) %collective-permute-start.21) | collective-permute-done | bytes 262176 | tf_op jit(solution)/shard_map/ppermute | solution.py:256
  57.2 0.1 add_convert_fusion.5
  57.3 1.6 %collective-permute-start.22 = (bf16[64,2048]{1,0:T(8,128)(2,1)S(1)}, bf16[64,2048]{1,0:T(8,128)(2,1)S(1)}, u32[]{:S(2)}, u32[]{:S(2)}) collective-permute-start(bf16[64,2048]{1,0:T(8,128)(2,1)S(1)} %add_convert_fusion.5), channel_id=1, source_target_pairs={{0,4},{1,3},{4,8},{5,1},{8,12},{9,5},{12,14},{13,9},{14,10},{15,13... | collective-permute-start | bytes 786440 | tf_op jit(solution)/shard_map/ppermute | solution.py:256
  58.9 1.1 %collective-permute-done.28 = bf16[64,2048]{1,0:T(8,128)(2,1)S(1)} collective-permute-done((bf16[64,2048]{1,0:T(8,128)(2,1)S(1)}, bf16[64,2048]{1,0:T(8,128)(2,1)S(1)}, u32[]{:S(2)}, u32[]{:S(2)}) %collective-permute-start.28) | collective-permute-done | bytes 262176 | tf_op jit(solution)/shard_map/ppermute | solution.py:255
  60.0 0.1 add_convert_fusion.1
  60.1 0.1 collective-permute-start.29
  60.1 3.6 %collective-permute-done.22 = bf16[64,2048]{1,0:T(8,128)(2,1)S(1)} collective-permute-done((bf16[64,2048]{1,0:T(8,128)(2,1)S(1)}, bf16[64,2048]{1,0:T(8,128)(2,1)S(1)}, u32[]{:S(2)}, u32[]{:S(2)}) %collective-permute-start.22) | collective-permute-done | bytes 262176 | tf_op jit(solution)/shard_map/ppermute | solution.py:256
  63.7 0.8 %add_convert_fusion = bf16[64,2048]{1,0:T(8,128)(2,1)} fusion(bf16[64,2048]{1,0:T(8,128)(2,1)S(1)} %collective-permute-done.29, bf16[64,2048]{1,0:T(8,128)(2,1)S(1)} %get-tuple-element.57, bf16[64,2048]{1,0:T(8,128)(2,1)S(1)} %collective-permute-done.22), kind=kLoop, calls=%fused_computation | loop fusion | flops 786432 | bytes 1048576 | tf_op jit(solution)/shard_map/convert_element_type | solution.py:209
  (15 shorter events, 0.0 us)
Async XLA Ops:
  1.7 3.2 %collective-permute-start.1 = (bf16[64,2176]{1,0:T(8,128)(2,1)}, bf16[64,2176]{1,0:T(8,128)(2,1)S(1)}, u32[]{:S(2)}, u32[]{:S(2)}) collective-permute-start(bf16[64,2176]{1,0:T(8,128)(2,1)} %pack.1.refs_0_), channel_id=1, source_target_pairs={{0,1},{1,0},{2,3},{3,2},{4,5},{5,4},{6,7},{7,6},{8,9},{9,8},{10,11... | collective-permute-start | bytes 835592 | tf_op jit(solution)/shard_map/ppermute | solution.py:225
  2.2 7.3 %collective-permute-start = (bf16[64,2176]{1,0:T(8,128)(2,1)}, bf16[64,2176]{1,0:T(8,128)(2,1)S(1)}, u32[]{:S(2)}, u32[]{:S(2)}) collective-permute-start(bf16[64,2176]{1,0:T(8,128)(2,1)} %pack.1.refs_0_), channel_id=1, source_target_pairs={{0,4},{1,3},{4,8},{5,1},{8,12},{9,5},{12,14},{13,9},{14,10},{15,13... | collective-permute-start | bytes 835592 | tf_op jit(solution)/shard_map/ppermute | solution.py:226
  4.9 7.6 %collective-permute-start.5 = (bf16[64,2176]{1,0:T(8,128)(2,1)S(1)}, bf16[64,2176]{1,0:T(8,128)(2,1)S(1)}, u32[]{:S(2)}, u32[]{:S(2)}) collective-permute-start(bf16[64,2176]{1,0:T(8,128)(2,1)S(1)} %collective-permute-done.1.refs_1_), channel_id=1, source_target_pairs={{0,4},{1,3},{4,8},{5,1},{8,12},{9,5},{12,14},{13,9},{14,10},{15,13... | collective-permute-start | bytes 835592 | tf_op jit(solution)/shard_map/ppermute | solution.py:226
  9.5 7.0 %collective-permute-start.3 = (bf16[64,2176]{1,0:T(8,128)(2,1)S(1)}, bf16[64,2176]{1,0:T(8,128)(2,1)S(1)}, u32[]{:S(2)}, u32[]{:S(2)}) collective-permute-start(bf16[64,2176]{1,0:T(8,128)(2,1)S(1)} %collective-permute-done.refs_2_), channel_id=1, source_target_pairs={{0,4},{1,3},{4,8},{5,1},{8,12},{9,5},{12,14},{13,9},{14,10},{15,13... | collective-permute-start | bytes 835592 | tf_op jit(solution)/shard_map/ppermute | solution.py:239
  12.5 6.5 %collective-permute-start.9 = (bf16[64,2176]{1,0:T(8,128)(2,1)S(1)}, bf16[64,2176]{1,0:T(8,128)(2,1)S(1)}, u32[]{:S(2)}, u32[]{:S(2)}) collective-permute-start(bf16[64,2176]{1,0:T(8,128)(2,1)S(1)} %collective-permute-done.5.refs_3_), channel_id=1, source_target_pairs={{0,4},{1,3},{4,8},{5,1},{8,12},{9,5},{12,14},{13,9},{14,10},{15,13... | collective-permute-start | bytes 835592 | tf_op jit(solution)/shard_map/ppermute | solution.py:235
  14.6 6.6 %collective-permute-start.2 = (bf16[64,2176]{1,0:T(8,128)(2,1)S(1)}, bf16[64,2176]{1,0:T(8,128)(2,1)S(1)}, u32[]{:S(2)}, u32[]{:S(2)}) collective-permute-start(bf16[64,2176]{1,0:T(8,128)(2,1)S(1)} %collective-permute-done.refs_2_), channel_id=1, source_target_pairs={{0,1},{1,0},{2,3},{3,2},{4,5},{5,4},{6,7},{7,6},{8,9},{9,8},{10,11... | collective-permute-start | bytes 835592 | tf_op jit(solution)/shard_map/ppermute | solution.py:236
  16.5 6.6 %collective-permute-start.4 = (bf16[64,2176]{1,0:T(8,128)(2,1)S(1)}, bf16[64,2176]{1,0:T(8,128)(2,1)S(1)}, u32[]{:S(2)}, u32[]{:S(2)}) collective-permute-start(bf16[64,2176]{1,0:T(8,128)(2,1)S(1)} %collective-permute-done.3.refs_2_), channel_id=1, source_target_pairs={{0,4},{1,3},{4,8},{5,1},{8,12},{9,5},{12,14},{13,9},{14,10},{15,13... | collective-permute-start | bytes 835592 | tf_op jit(solution)/shard_map/ppermute | solution.py:239
  18.2 4.9 %collective-permute-start.6 = (bf16[64,2176]{1,0:T(8,128)(2,1)S(1)}, bf16[64,2176]{1,0:T(8,128)(2,1)S(1)}, u32[]{:S(2)}, u32[]{:S(2)}) collective-permute-start(bf16[64,2176]{1,0:T(8,128)(2,1)S(1)} %collective-permute-done.5.refs_3_), channel_id=1, source_target_pairs={{0,1},{1,0},{2,3},{3,2},{4,5},{5,4},{6,7},{7,6},{8,9},{9,8},{10,11... | collective-permute-start | bytes 835592 | tf_op jit(solution)/shard_map/ppermute | solution.py:236
  19.1 7.0 %collective-permute-start.12 = (bf16[64,2176]{1,0:T(8,128)(2,1)S(1)}, bf16[64,2176]{1,0:T(8,128)(2,1)S(1)}, u32[]{:S(2)}, u32[]{:S(2)}) collective-permute-start(bf16[64,2176]{1,0:T(8,128)(2,1)S(1)} %collective-permute-done.9.refs_3_), channel_id=1, source_target_pairs={{0,4},{1,3},{4,8},{5,1},{8,12},{9,5},{12,14},{13,9},{14,10},{15,13... | collective-permute-start | bytes 835592 | tf_op jit(solution)/shard_map/ppermute | solution.py:235
  21.2 4.9 %collective-permute-start.8 = (bf16[64,2176]{1,0:T(8,128)(2,1)S(1)}, bf16[64,2176]{1,0:T(8,128)(2,1)S(1)}, u32[]{:S(2)}, u32[]{:S(2)}) collective-permute-start(bf16[64,2176]{1,0:T(8,128)(2,1)S(1)} %collective-permute-done.3.refs_2_), channel_id=1, source_target_pairs={{0,1},{1,0},{2,3},{3,2},{4,5},{5,4},{6,7},{7,6},{8,9},{9,8},{10,11... | collective-permute-start | bytes 835592 | tf_op jit(solution)/shard_map/ppermute | solution.py:236
  21.2 4.9 %collective-permute-start.10 = (bf16[64,2176]{1,0:T(8,128)(2,1)S(1)}, bf16[64,2176]{1,0:T(8,128)(2,1)S(1)}, u32[]{:S(2)}, u32[]{:S(2)}) collective-permute-start(bf16[64,2176]{1,0:T(8,128)(2,1)S(1)} %collective-permute-done.9.refs_3_), channel_id=1, source_target_pairs={{0,1},{1,0},{2,3},{3,2},{4,5},{5,4},{6,7},{7,6},{8,9},{9,8},{10,11... | collective-permute-start | bytes 835592 | tf_op jit(solution)/shard_map/ppermute | solution.py:236
  23.1 3.0 %collective-permute-start.11 = (bf16[64,2176]{1,0:T(8,128)(2,1)S(1)}, bf16[64,2176]{1,0:T(8,128)(2,1)S(1)}, u32[]{:S(2)}, u32[]{:S(2)}) collective-permute-start(bf16[64,2176]{1,0:T(8,128)(2,1)S(1)} %collective-permute-done.4.refs_5_), channel_id=1, source_target_pairs={{0,1},{1,0},{2,3},{3,2},{4,5},{5,4},{6,7},{7,6},{8,9},{9,8},{10,11... | collective-permute-start | bytes 835592 | tf_op jit(solution)/shard_map/ppermute | solution.py:236
  23.1 6.9 %collective-permute-start.7 = (bf16[64,2176]{1,0:T(8,128)(2,1)S(1)}, bf16[64,2176]{1,0:T(8,128)(2,1)S(1)}, u32[]{:S(2)}, u32[]{:S(2)}) collective-permute-start(bf16[64,2176]{1,0:T(8,128)(2,1)S(1)} %collective-permute-done.4.refs_5_), channel_id=1, source_target_pairs={{0,4},{1,3},{4,8},{5,1},{8,12},{9,5},{12,14},{13,9},{14,10},{15,13... | collective-permute-start | bytes 835592 | tf_op jit(solution)/shard_map/ppermute | solution.py:239
  26.1 3.9 %collective-permute-start.13 = (bf16[64,2176]{1,0:T(8,128)(2,1)S(1)}, bf16[64,2176]{1,0:T(8,128)(2,1)S(1)}, u32[]{:S(2)}, u32[]{:S(2)}) collective-permute-start(bf16[64,2176]{1,0:T(8,128)(2,1)S(1)} %collective-permute-done.12.refs_1_), channel_id=1, source_target_pairs={{0,1},{1,0},{2,3},{3,2},{4,5},{5,4},{6,7},{7,6},{8,9},{9,8},{10,11... | collective-permute-start | bytes 835592 | tf_op jit(solution)/shard_map/ppermute | solution.py:236
  30.1 2.6 %collective-permute-start.14 = (bf16[64,2176]{1,0:T(8,128)(2,1)S(1)}, bf16[64,2176]{1,0:T(8,128)(2,1)S(1)}, u32[]{:S(2)}, u32[]{:S(2)}) collective-permute-start(bf16[64,2176]{1,0:T(8,128)(2,1)S(1)} %collective-permute-done.7.refs_1_), channel_id=1, source_target_pairs={{0,1},{1,0},{2,3},{3,2},{4,5},{5,4},{6,7},{7,6},{8,9},{9,8},{10,11... | collective-permute-start | bytes 835592 | tf_op jit(solution)/shard_map/ppermute | solution.py:246
  34.7 1.6 %collective-permute-start.15 = (bf16[64,2048]{1,0:T(8,128)(2,1)S(1)}, bf16[64,2048]{1,0:T(8,128)(2,1)S(1)}, u32[]{:S(2)}, u32[]{:S(2)}) collective-permute-start(bf16[64,2048]{1,0:T(8,128)(2,1)S(1)} %get-tuple-element.47), channel_id=1, source_target_pairs={{0,1},{1,0},{2,3},{3,2},{4,5},{5,4},{6,7},{7,6},{8,9},{9,8},{10,11... | collective-permute-start | bytes 786440 | tf_op jit(solution)/shard_map/ppermute | solution.py:247
  34.8 15.8 %collective-permute-start.18 = (bf16[64,2048]{1,0:T(8,128)(2,1)S(1)}, bf16[64,2048]{1,0:T(8,128)(2,1)S(1)}, u32[]{:S(2)}, u32[]{:S(2)}) collective-permute-start(bf16[64,2048]{1,0:T(8,128)(2,1)S(1)} %get-tuple-element.52), channel_id=1, source_target_pairs={{0,1},{1,0},{2,3},{3,2},{4,5},{5,4},{6,7},{7,6},{8,9},{9,8},{10,11... | collective-permute-start | bytes 786440 | tf_op jit(solution)/shard_map/ppermute | solution.py:254
  35.3 2.8 %collective-permute-start.25 = (bf16[64,2048]{1,0:T(8,128)(2,1)S(1)}, bf16[64,2048]{1,0:T(8,128)(2,1)S(1)}, u32[]{:S(2)}, u32[]{:S(2)}) collective-permute-start(bf16[64,2048]{1,0:T(8,128)(2,1)S(1)} %get-tuple-element.61), channel_id=1, source_target_pairs={{0,1},{1,0},{2,3},{3,2},{4,5},{5,4},{6,7},{7,6},{8,9},{9,8},{10,11... | collective-permute-start | bytes 786440 | tf_op jit(solution)/shard_map/ppermute | solution.py:254
  35.4 9.2 %collective-permute-start.24 = (bf16[64,2048]{1,0:T(8,128)(2,1)S(1)}, bf16[64,2048]{1,0:T(8,128)(2,1)S(1)}, u32[]{:S(2)}, u32[]{:S(2)}) collective-permute-start(bf16[64,2048]{1,0:T(8,128)(2,1)S(1)} %get-tuple-element.60), channel_id=1, source_target_pairs={{0,1},{1,0},{2,3},{3,2},{4,5},{5,4},{6,7},{7,6},{8,9},{9,8},{10,11... | collective-permute-start | bytes 786440 | tf_op jit(solution)/shard_map/ppermute | solution.py:254
  35.8 3.9 %collective-permute-start.19 = (bf16[64,2048]{1,0:T(8,128)(2,1)S(1)}, bf16[64,2048]{1,0:T(8,128)(2,1)S(1)}, u32[]{:S(2)}, u32[]{:S(2)}) collective-permute-start(bf16[64,2048]{1,0:T(8,128)(2,1)S(1)} %get-tuple-element.53), channel_id=1, source_target_pairs={{0,1},{1,0},{2,3},{3,2},{4,5},{5,4},{6,7},{7,6},{8,9},{9,8},{10,11... | collective-permute-start | bytes 786440 | tf_op jit(solution)/shard_map/ppermute | solution.py:254
  36.4 6.4 %collective-permute-start.16 = (bf16[64,2048]{1,0:T(8,128)(2,1)S(1)}, bf16[64,2048]{1,0:T(8,128)(2,1)S(1)}, u32[]{:S(2)}, u32[]{:S(2)}) collective-permute-start(bf16[64,2048]{1,0:T(8,128)(2,1)S(1)} %add_convert_fusion.8), channel_id=1, source_target_pairs={{0,4},{1,3},{4,8},{5,1},{8,12},{9,5},{12,14},{13,9},{14,10},{15,13... | collective-permute-start | bytes 786440 | tf_op jit(solution)/shard_map/ppermute | solution.py:247
  38.1 7.5 %collective-permute-start.26 = (bf16[64,2048]{1,0:T(8,128)(2,1)S(1)}, bf16[64,2048]{1,0:T(8,128)(2,1)S(1)}, u32[]{:S(2)}, u32[]{:S(2)}) collective-permute-start(bf16[64,2048]{1,0:T(8,128)(2,1)S(1)} %add_convert_fusion.4), channel_id=1, source_target_pairs={{0,4},{1,3},{4,8},{5,1},{8,12},{9,5},{12,14},{13,9},{14,10},{15,13... | collective-permute-start | bytes 786440 | tf_op jit(solution)/shard_map/ppermute | solution.py:255
  42.9 7.7 %collective-permute-start.20 = (bf16[64,2048]{1,0:T(8,128)(2,1)S(1)}, bf16[64,2048]{1,0:T(8,128)(2,1)S(1)}, u32[]{:S(2)}, u32[]{:S(2)}) collective-permute-start(bf16[64,2048]{1,0:T(8,128)(2,1)S(1)} %add_convert_fusion.7), channel_id=1, source_target_pairs={{0,4},{1,3},{4,8},{5,1},{8,12},{9,5},{12,14},{13,9},{14,10},{15,13... | collective-permute-start | bytes 786440 | tf_op jit(solution)/shard_map/ppermute | solution.py:256
  45.7 8.4 %copy-start = (bf16[64,2176]{1,0:T(8,128)(2,1)S(1)}, bf16[64,2176]{1,0:T(8,128)(2,1)}, u32[]{:S(2)}) copy-start(bf16[64,2176]{1,0:T(8,128)(2,1)} %pack.1.refs_0_) | copy-start | bytes 835588
  45.7 6.6 %collective-permute-start.27 = (bf16[64,2048]{1,0:T(8,128)(2,1)S(1)}, bf16[64,2048]{1,0:T(8,128)(2,1)S(1)}, u32[]{:S(2)}, u32[]{:S(2)}) collective-permute-start(bf16[64,2048]{1,0:T(8,128)(2,1)S(1)} %add_convert_fusion.3), channel_id=1, source_target_pairs={{0,4},{1,3},{4,8},{5,1},{8,12},{9,5},{12,14},{13,9},{14,10},{15,13... | collective-permute-start | bytes 786440 | tf_op jit(solution)/shard_map/ppermute | solution.py:255
  50.1 6.1 %collective-permute-start.17 = (bf16[64,2048]{1,0:T(8,128)(2,1)S(1)}, bf16[64,2048]{1,0:T(8,128)(2,1)S(1)}, u32[]{:S(2)}, u32[]{:S(2)}) collective-permute-start(bf16[64,2048]{1,0:T(8,128)(2,1)S(1)} %get-tuple-element.50), channel_id=1, source_target_pairs={{0,1},{1,0},{2,3},{3,2},{4,5},{5,4},{6,7},{7,6},{8,9},{9,8},{10,11... | collective-permute-start | bytes 786440 | tf_op jit(solution)/shard_map/ppermute | solution.py:254
  50.1 2.2 %collective-permute-start.23 = (bf16[64,2048]{1,0:T(8,128)(2,1)S(1)}, bf16[64,2048]{1,0:T(8,128)(2,1)S(1)}, u32[]{:S(2)}, u32[]{:S(2)}) collective-permute-start(bf16[64,2048]{1,0:T(8,128)(2,1)S(1)} %get-tuple-element.58), channel_id=1, source_target_pairs={{0,1},{1,0},{2,3},{3,2},{4,5},{5,4},{6,7},{7,6},{8,9},{9,8},{10,11... | collective-permute-start | bytes 786440 | tf_op jit(solution)/shard_map/ppermute | solution.py:254
  50.8 6.4 %collective-permute-start.21 = (bf16[64,2048]{1,0:T(8,128)(2,1)S(1)}, bf16[64,2048]{1,0:T(8,128)(2,1)S(1)}, u32[]{:S(2)}, u32[]{:S(2)}) collective-permute-start(bf16[64,2048]{1,0:T(8,128)(2,1)S(1)} %add_convert_fusion.6), channel_id=1, source_target_pairs={{0,4},{1,3},{4,8},{5,1},{8,12},{9,5},{12,14},{13,9},{14,10},{15,13... | collective-permute-start | bytes 786440 | tf_op jit(solution)/shard_map/ppermute | solution.py:256
  52.5 7.5 %collective-permute-start.28 = (bf16[64,2048]{1,0:T(8,128)(2,1)S(1)}, bf16[64,2048]{1,0:T(8,128)(2,1)S(1)}, u32[]{:S(2)}, u32[]{:S(2)}) collective-permute-start(bf16[64,2048]{1,0:T(8,128)(2,1)S(1)} %add_convert_fusion.2), channel_id=1, source_target_pairs={{0,4},{1,3},{4,8},{5,1},{8,12},{9,5},{12,14},{13,9},{14,10},{15,13... | collective-permute-start | bytes 786440 | tf_op jit(solution)/shard_map/ppermute | solution.py:255
  57.3 6.4 %collective-permute-start.22 = (bf16[64,2048]{1,0:T(8,128)(2,1)S(1)}, bf16[64,2048]{1,0:T(8,128)(2,1)S(1)}, u32[]{:S(2)}, u32[]{:S(2)}) collective-permute-start(bf16[64,2048]{1,0:T(8,128)(2,1)S(1)} %add_convert_fusion.5), channel_id=1, source_target_pairs={{0,4},{1,3},{4,8},{5,1},{8,12},{9,5},{12,14},{13,9},{14,10},{15,13... | collective-permute-start | bytes 786440 | tf_op jit(solution)/shard_map/ppermute | solution.py:256
  60.1 3.7 %collective-permute-start.29 = (bf16[64,2048]{1,0:T(8,128)(2,1)S(1)}, bf16[64,2048]{1,0:T(8,128)(2,1)S(1)}, u32[]{:S(2)}, u32[]{:S(2)}) collective-permute-start(bf16[64,2048]{1,0:T(8,128)(2,1)S(1)} %add_convert_fusion.1), channel_id=1, source_target_pairs={{0,1},{1,0},{2,3},{3,2},{4,5},{5,4},{6,7},{7,6},{8,9},{9,8},{10,11... | collective-permute-start | bytes 786440 | tf_op jit(solution)/shard_map/ppermute | solution.py:259

commit v9 on v6

--- a/solution.py
+++ b/solution.py
@@ -65,13 +65,13 @@
     return [(index, index ^ 1) for index in range(experts)]
 
 
-def ring_pairs(experts):
+def ring_pairs(experts, places):
     order = ring_order(experts // 2)
     count = len(order)
     pairs = []
     for place, chip in enumerate(order):
-        pairs.append((2 * chip, 2 * order[(place + 1) % count]))
-        pairs.append((2 * chip + 1, 2 * order[(place - 1) % count] + 1))
+        pairs.append((2 * chip, 2 * order[(place + places) % count]))
+        pairs.append((2 * chip + 1, 2 * order[(place - places) % count] + 1))
     return pairs
 
 
@@ -218,7 +218,8 @@
     count = tokens.shape[0]
     rounds = experts // 4
     swap = functools.partial(lax.ppermute, axis_name="expert", perm=swap_pairs(experts))
-    ring = functools.partial(lax.ppermute, axis_name="expert", perm=ring_pairs(experts))
+    ring = functools.partial(lax.ppermute, axis_name="expert", perm=ring_pairs(experts, 1))
+    leap = functools.partial(lax.ppermute, axis_name="expert", perm=ring_pairs(experts, 2))
     own = lax.axis_index("expert").reshape(1)
 
     mine = pack(after(tokens, own), expert_ids, router_weights, experts)
@@ -234,26 +235,37 @@
         if step > 1:
             second = ring(second)
         blocks[step] = (swap(first), swap(second), first, second)
-        first = ring(first)
+        if step == rounds - 2:
+            far = leap(first)
+        if step < rounds - 1:
+            first = ring(first)
         if step == 1:
             first = after(first, down_w)
-    sums = {2: run(*blocks[2])}
-    first = after(first, sums[2][0], *blocks[1][:2], blocks[3][0])
-    keep, send, *sums[3] = run(swap(first), first, *blocks[3])
-    lead, trail = ring(added(keep, swap(send))), None
-    for step in (3, 2, 1):
+    turned = lambda keep_trail, keep, send_trail, send: (keep_trail, keep, swap(send_trail), swap(send))
+    sums = {2: run(after(blocks[2][0], *blocks[1][:2]), *blocks[2][1:])}
+    far = after(far, sums[2][0])
+    sums[2] = turned(*sums[2])
+    near = after(blocks[3][0], *sums[2][2:])
+    send, keep, early, early_send = run(swap(far), far, near, blocks[3][2])
+    late, late_send = run(after(blocks[3][1], early), blocks[3][3])
+    sums[3] = turned(early, late, early_send, late_send)
+    far = leap(added(keep, swap(send)))
+    lead, trail = [], []
+    for step in range(rounds - 1, 0, -1):
+        if step == 2:
+            lead = [after(lead[0], sums[1][0]), far]
+        if step == 1:
+            lead = [after(lead[0], kept)]
+        keep_trail, keep, send_trail, send = sums[step]
+        trail = [ring(added(keep_trail, send_trail, *trail))]
+        lead = [added(keep, send, *lead)]
         if step == 3:
-            sums[1] = run(after(blocks[1][0], lead), *blocks[1][1:])
+            sums[1] = turned(*run(after(blocks[1][0], lead[0]), *blocks[1][1:]))
         if step == 2:
-            lead = after(lead, sums[1][0])
-        keep, keep_trail, send, send_trail = sums[step]
-        send, send_trail = swap(send), swap(send_trail)
-        trail = ring(added(*([keep_trail, send_trail] + ([] if trail is None else [trail]))))
-        lead = ring(added(keep, send, lead))
-        if step == 2:
-            kept, other = run(after(mine, lead), sibling)
-    last = swap(added(lead, other))
-    return added(trail, kept, last)
+            kept, other = run(after(mine, lead[0]), sibling)
+        lead = [ring(lead[0])]
+    last = swap(added(trail[0], other))
+    return added(lead[0], kept, last)
 
 
 def solution(mesh):

time: 70.2 us -> 74 us (1.054)
  starting transfers between devices: 27.9 us -> 30 us
  waiting for transfers between devices: 22.7 us -> 23.7 us
  Pallas kernels: 17.7 us -> 18.5 us
    ppermute x16 -> x17, waiting for transfers between devices: 12.6 us -> 21.2 us  [the longest x3 6.42 us: dense_body(): trail = [ring(added(keep_trail, send_trail, *trail))]]
    ppermute x3 -> x2, waiting for transfers between devices: 4.2 us -> 0.01 us  [dense_body(): first = ring(first)]
    ppermute x16 -> x17, starting transfers between devices: 13.5 us -> 16.4 us  [the longest x3 4.93 us: dense_body(): lead = [ring(lead[0])]]
    ppermute x2, waiting for transfers between devices: 3.86 us -> 1.47 us  [dense_body(): second = ring(second)]
    ppermute x3 -> x2, starting transfers between devices: 5.39 us -> 3.68 us  [dense_body(): first = ring(first)]
    ppermute x6, waiting for transfers between devices: 1.06 us -> 0.02 us  [dense_body(): blocks[step] = (swap(first), swap(second), first, second)]
    pallas_call x4 -> x5, Pallas kernels: 11.2 us -> 12.1 us  [run_expert(): pl.pallas_call(functools.partial(expert_kernel, experts, len(blocks)), ou...]
    ppermute x6, starting transfers between devices: 0.52 us -> 1.32 us  [dense_body(): blocks[step] = (swap(first), swap(second), first, second)]
  transfers between devices with their start and end apart: 30 -> 30, of which waited for: 15 -> 13; matrix products, arithmetic and copies ran while one was open for 1% -> 1% of each run, Pallas kernels for 17% -> 20%
where the time goes in v9:
time: 74 us; the launch traced here: 73.8 us
  starting transfers between devices  30 us (41%)
  waiting for transfers between devices  23.7 us (32%)
  Pallas kernels  18.5 us (25%)
  other arithmetic  1.5 us (2%)
    pallas_call x5, Pallas kernels, run_expert(): pl.pallas_call(functools.partial(expert_kernel, experts, len(blocks)), ou...  12.1 us
    ppermute x3, waiting for transfers between devices, dense_body(): trail = [ring(added(keep_trail, send_trail, *trail))]  6.42 us
    ppermute x2, waiting for transfers between devices, dense_body(): far = leap(added(keep, swap(send)))  5.09 us
    ppermute x3, starting transfers between devices, dense_body(): lead = [ring(lead[0])]  4.93 us
    pallas_call x2, Pallas kernels, load_weights(): pl.pallas_call(functools.partial(load_kernel, pieces), out_shape=[pltpu.V...  4.73 us
    ppermute x2, starting transfers between devices, dense_body(): first, second = (ring(mine), ring(sibling))  4.34 us
    ppermute x1, waiting for transfers between devices, dense_body(): far = leap(first)  4.16 us
    ppermute x3, starting transfers between devices, dense_body(): trail = [ring(added(keep_trail, send_trail, *trail))]  3.74 us
  transfers between devices with their start and end apart: 30, of which 13 were waited for; matrix products, arithmetic and copies ran while one was open for 1% of the time, Pallas kernels for 20%

profile of v9, /device:TPU:0, one launch (start us, length us, event | category | flops | bytes accessed | tf_op | source)
XLA Modules:
  0.0 73.8 jit_solution(1801268496092361809)
XLA Ops:
  0.0 1.7 %pack.1.refs_0_ = bf16[64,2176]{1,0:T(8,128)(2,1)} custom-call(bf16[64,2048]{1,0:T(8,128)(2,1)} %tokens_ref, s32[8,64]{1,0:T(8,128)} %bitcast.3, f32[8,64]{1,0:T(8,128)} %bitcast.4), custom_call_target="tpu_custom_call" | custom-call | bytes 1024 | tf_op jit(solution)/shard_map/pack/pallas_call | solution.py:190
  1.7 0.5 collective-permute-start.1
  2.2 2.6 %collective-permute-start = (bf16[64,2176]{1,0:T(8,128)(2,1)}, bf16[64,2176]{1,0:T(8,128)(2,1)S(1)}, u32[]{:S(2)}, u32[]{:S(2)}) collective-permute-start(bf16[64,2176]{1,0:T(8,128)(2,1)} %pack.1.refs_0_), channel_id=1, source_target_pairs={{0,4},{1,3},{4,8},{5,1},{8,12},{9,5},{12,14},{13,9},{14,10},{15,13... | collective-permute-start | bytes 835592 | tf_op jit(solution)/shard_map/ppermute | solution.py:227
  4.9 0.0 collective-permute-done.1.refs_1_
  4.9 1.7 %collective-permute-start.3 = (bf16[64,2176]{1,0:T(8,128)(2,1)S(1)}, bf16[64,2176]{1,0:T(8,128)(2,1)S(1)}, u32[]{:S(2)}, u32[]{:S(2)}) collective-permute-start(bf16[64,2176]{1,0:T(8,128)(2,1)S(1)} %collective-permute-done.1.refs_1_), channel_id=1, source_target_pairs={{0,4},{1,3},{4,8},{5,1},{8,12},{9,5},{12,14},{13,9},{14,10},{15,13... | collective-permute-start | bytes 835592 | tf_op jit(solution)/shard_map/ppermute | solution.py:227
  6.6 2.9 %load.2 = (bf16[1,2048,768]{2,1,0:T(8,128)(2,1)S(1)}, bf16[1,2048,768]{2,1,0:T(8,128)(2,1)S(1)}) custom-call(bf16[1,2048,768]{2,1,0:T(8,128)(2,1)} %refs_0_, bf16[1,2048,768]{2,1,0:T(8,128)(2,1)} %refs_1_.1), custom_call_target="tpu_custom_call" | custom-call | bytes 1024 | tf_op jit(solution)/shard_map/load/pallas_call | solution.py:148
  9.4 0.1 collective-permute-done.refs_2_
  9.5 2.1 %collective-permute-start.7 = (bf16[64,2176]{1,0:T(8,128)(2,1)S(1)}, bf16[64,2176]{1,0:T(8,128)(2,1)S(1)}, u32[]{:S(2)}, u32[]{:S(2)}) collective-permute-start(bf16[64,2176]{1,0:T(8,128)(2,1)S(1)} %collective-permute-done.refs_2_), channel_id=1, source_target_pairs={{0,4},{1,3},{4,8},{5,1},{8,12},{9,5},{12,14},{13,9},{14,10},{15,13... | collective-permute-start | bytes 835592 | tf_op jit(solution)/shard_map/ppermute | solution.py:241
  11.6 0.9 %collective-permute-done.3.refs_3_ = bf16[64,2176]{1,0:T(8,128)(2,1)S(1)} collective-permute-done((bf16[64,2176]{1,0:T(8,128)(2,1)S(1)}, bf16[64,2176]{1,0:T(8,128)(2,1)S(1)}, u32[]{:S(2)}, u32[]{:S(2)}) %collective-permute-start.3) | collective-permute-done | bytes 278560 | tf_op jit(solution)/shard_map/ppermute | solution.py:227
  12.5 2.1 %collective-permute-start.4 = (bf16[64,2176]{1,0:T(8,128)(2,1)S(1)}, bf16[64,2176]{1,0:T(8,128)(2,1)S(1)}, u32[]{:S(2)}, u32[]{:S(2)}) collective-permute-start(bf16[64,2176]{1,0:T(8,128)(2,1)S(1)} %collective-permute-done.3.refs_3_), channel_id=1, source_target_pairs={{0,4},{1,3},{4,8},{5,1},{8,12},{9,5},{12,14},{13,9},{14,10},{15,13... | collective-permute-start | bytes 835592 | tf_op jit(solution)/shard_map/ppermute | solution.py:236
  14.6 0.0 collective-permute-start.2
  14.6 1.9 %load.3.refs_6_.refs_4_ = bf16[1,2048,768]{2,1,0:T(8,128)(2,1)S(1)} custom-call(bf16[1,2048,768]{2,1,0:T(8,128)(2,1)} %refs_0_.1), custom_call_target="tpu_custom_call" | custom-call | bytes 1024 | tf_op jit(solution)/shard_map/load/pallas_call | solution.py:148
  16.5 0.6 collective-permute-start.9
  17.1 0.1 collective-permute-start.10
  17.2 1.6 %collective-permute-start.13 = (bf16[64,2176]{1,0:T(8,128)(2,1)S(1)}, bf16[64,2176]{1,0:T(8,128)(2,1)S(1)}, u32[]{:S(2)}, u32[]{:S(2)}) collective-permute-start(bf16[64,2176]{1,0:T(8,128)(2,1)S(1)} %collective-permute-done.7.refs_2_), channel_id=1, source_target_pairs={{0,4},{1,3},{4,8},{5,1},{8,12},{9,5},{12,14},{13,9},{14,10},{15,13... | collective-permute-start | bytes 835592 | tf_op jit(solution)/shard_map/ppermute | solution.py:241
  18.7 0.3 collective-permute-done.4.refs_3_
  19.1 0.0 collective-permute-start.11
  19.1 0.0 collective-permute-done.2.refs_0_
  19.1 3.1 %collective-permute-start.8 = (bf16[64,2176]{1,0:T(8,128)(2,1)S(1)}, bf16[64,2176]{1,0:T(8,128)(2,1)S(1)}, u32[]{:S(2)}, u32[]{:S(2)}) collective-permute-start(bf16[64,2176]{1,0:T(8,128)(2,1)S(1)} %collective-permute-done.7.refs_2_), channel_id=1, source_target_pairs={{0,8},{1,7},{4,12},{5,3},{8,14},{9,1},{12,10},{13,5},{14,6},{15,9}... | collective-permute-start | bytes 835592 | tf_op jit(solution)/shard_map/ppermute | solution.py:239
  22.2 1.6 %collective-permute-start.5 = (bf16[64,2176]{1,0:T(8,128)(2,1)S(1)}, bf16[64,2176]{1,0:T(8,128)(2,1)S(1)}, u32[]{:S(2)}, u32[]{:S(2)}) collective-permute-start(bf16[64,2176]{1,0:T(8,128)(2,1)S(1)} %collective-permute-done.4.refs_3_), channel_id=1, source_target_pairs={{0,4},{1,3},{4,8},{5,1},{8,12},{9,5},{12,14},{13,9},{14,10},{15,13... | collective-permute-start | bytes 835592 | tf_op jit(solution)/shard_map/ppermute | solution.py:236
  23.8 0.0 collective-permute-done.10.refs_1_
  23.8 0.0 collective-permute-done.11.refs_1_
  23.8 2.7 %expert.5 = (bf16[64,2048]{1,0:T(8,128)(2,1)S(1)}, bf16[64,2048]{1,0:T(8,128)(2,1)S(1)}, bf16[64,2048]{1,0:T(8,128)(2,1)S(1)}, bf16[64,2048]{1,0:T(8,128)(2,1)S(1)}) custom-call(s32[1]{0:T(128)} %bitcast.own_ref, bf16[64,2176]{1,0:T(8,128)(2,1)S(1)} %collective-permute-done.9.refs_0_, bf16[64,2176]{1,0:T(8,128)(2,1)S(1)} %collective-permute-done.11.refs_1_, ...), custom_call_target="tpu_custom_call" | custom-call | flops 524288 | bytes 524288 | tf_op jit(solution)/shard_map/expert/pallas_call | solution.py:115
  26.5 4.2 %collective-permute-done.8.refs_1_ = bf16[64,2176]{1,0:T(8,128)(2,1)S(1)} collective-permute-done((bf16[64,2176]{1,0:T(8,128)(2,1)S(1)}, bf16[64,2176]{1,0:T(8,128)(2,1)S(1)}, u32[]{:S(2)}, u32[]{:S(2)}) %collective-permute-start.8) | collective-permute-done | bytes 278560 | tf_op jit(solution)/shard_map/ppermute | solution.py:239
  30.6 0.0 collective-permute-start.12
  30.6 1.2 %collective-permute-done.5.refs_1_ = bf16[64,2176]{1,0:T(8,128)(2,1)S(1)} collective-permute-done((bf16[64,2176]{1,0:T(8,128)(2,1)S(1)}, bf16[64,2176]{1,0:T(8,128)(2,1)S(1)}, u32[]{:S(2)}, u32[]{:S(2)}) %collective-permute-start.5) | collective-permute-done | bytes 278560 | tf_op jit(solution)/shard_map/ppermute | solution.py:236
  31.8 0.7 collective-permute-start.6
  32.4 0.0 collective-permute-start.15
  32.4 0.5 collective-permute-start.16
  32.9 0.0 collective-permute-done.14.refs_2_
  32.9 1.0 %collective-permute-done.15 = bf16[64,2048]{1,0:T(8,128)(2,1)S(1)} collective-permute-done((bf16[64,2048]{1,0:T(8,128)(2,1)S(1)}, bf16[64,2048]{1,0:T(8,128)(2,1)S(1)}, u32[]{:S(2)}, u32[]{:S(2)}) %collective-permute-start.15) | collective-permute-done | bytes 262176 | tf_op jit(solution)/shard_map/ppermute | solution.py:244
  34.0 0.4 collective-permute-done.16
  34.4 0.0 collective-permute-done.12.refs_0_
  34.4 2.7 %expert.6 = (bf16[64,2048]{1,0:T(8,128)(2,1)S(1)}, bf16[64,2048]{1,0:T(8,128)(2,1)S(1)}, bf16[64,2048]{1,0:T(8,128)(2,1)S(1)}, bf16[64,2048]{1,0:T(8,128)(2,1)S(1)}) custom-call(s32[1]{0:T(128)} %bitcast.own_ref, bf16[64,2176]{1,0:T(8,128)(2,1)S(1)} %collective-permute-done.12.refs_0_, bf16[64,2176]{1,0:T(8,128)(2,1)S(1)} %collective-permute-done.8.refs_1_, ...), custom_call_target="tpu_custom_call" | custom-call | flops 524288 | bytes 524288 | tf_op jit(solution)/shard_map/expert/pallas_call | solution.py:115
  37.0 2.1 %expert.7 = (bf16[64,2048]{1,0:T(8,128)(2,1)S(1)}, bf16[64,2048]{1,0:T(8,128)(2,1)S(1)}) custom-call(s32[1]{0:T(128)} %bitcast.own_ref, bf16[64,2176]{1,0:T(8,128)(2,1)S(1)} %collective-permute-done.6.refs_0_, bf16[64,2176]{1,0:T(8,128)(2,1)S(1)} %collective-permute-done.5.refs_1_, bf16[1,2048,768]{2,1,0:T(8,128)(2,1)S(1)} %get-tuple-element.38.refs_4_.refs_2_, ...), custom_call_target="tpu_custom_call" | custom-call | flops 262144 | bytes 262144 | tf_op jit(solution)/shard_map/expert/pallas_call | solution.py:115
  39.1 0.4 collective-permute-start.17
  39.5 0.1 collective-permute-start.20
  39.7 0.4 collective-permute-start.25
  40.1 0.7 collective-permute-done.17
  40.7 0.1 add_convert_fusion.8
  40.8 2.2 %collective-permute-start.19 = (bf16[64,2048]{1,0:T(8,128)(2,1)S(1)}, bf16[64,2048]{1,0:T(8,128)(2,1)S(1)}, u32[]{:S(2)}, u32[]{:S(2)}) collective-permute-start(bf16[64,2048]{1,0:T(8,128)(2,1)S(1)} %add_convert_fusion.8), channel_id=1, source_target_pairs={{0,4},{1,3},{4,8},{5,1},{8,12},{9,5},{12,14},{13,9},{14,10},{15,13... | collective-permute-start | bytes 786440 | tf_op jit(solution)/shard_map/ppermute | solution.py:266
  43.0 0.1 add_convert_fusion.7
  43.1 3.0 %collective-permute-start.21 = (bf16[64,2048]{1,0:T(8,128)(2,1)S(1)}, bf16[64,2048]{1,0:T(8,128)(2,1)S(1)}, u32[]{:S(2)}, u32[]{:S(2)}) collective-permute-start(bf16[64,2048]{1,0:T(8,128)(2,1)S(1)} %add_convert_fusion.7), channel_id=1, source_target_pairs={{0,8},{1,7},{4,12},{5,3},{8,14},{9,1},{12,10},{13,5},{14,6},{15,9}... | collective-permute-start | bytes 786440 | tf_op jit(solution)/shard_map/ppermute | solution.py:252
  46.1 0.1 add_convert_fusion.4
  46.2 0.3 collective-permute-start.26
  46.5 2.7 %expert.8 = (bf16[64,2048]{1,0:T(8,128)(2,1)S(1)}, bf16[64,2048]{1,0:T(8,128)(2,1)S(1)}, bf16[64,2048]{1,0:T(8,128)(2,1)S(1)}, bf16[64,2048]{1,0:T(8,128)(2,1)S(1)}) custom-call(s32[1]{0:T(128)} %bitcast.own_ref, bf16[64,2176]{1,0:T(8,128)(2,1)S(1)} %collective-permute-done.2.refs_0_, bf16[64,2176]{1,0:T(8,128)(2,1)S(1)} %collective-permute-done.10.refs_1_, ...), custom_call_target="tpu_custom_call" | custom-call | flops 524288 | bytes 524288 | tf_op jit(solution)/shard_map/expert/pallas_call | solution.py:115
  49.1 0.1 collective-permute-start.24
  49.2 5.1 %collective-permute-done.21 = bf16[64,2048]{1,0:T(8,128)(2,1)S(1)} collective-permute-done((bf16[64,2048]{1,0:T(8,128)(2,1)S(1)}, bf16[64,2048]{1,0:T(8,128)(2,1)S(1)}, u32[]{:S(2)}, u32[]{:S(2)}) %collective-permute-start.21) | collective-permute-done | bytes 262176 | tf_op jit(solution)/shard_map/ppermute | solution.py:252
  54.3 0.1 add_convert_fusion.6
  54.5 1.0 %collective-permute-start.22 = (bf16[64,2048]{1,0:T(8,128)(2,1)S(1)}, bf16[64,2048]{1,0:T(8,128)(2,1)S(1)}, u32[]{:S(2)}, u32[]{:S(2)}) collective-permute-start(bf16[64,2048]{1,0:T(8,128)(2,1)S(1)} %add_convert_fusion.6), channel_id=1, source_target_pairs={{0,4},{1,3},{4,8},{5,1},{8,12},{9,5},{12,14},{13,9},{14,10},{15,13... | collective-permute-start | bytes 786440 | tf_op jit(solution)/shard_map/ppermute | solution.py:266
  55.4 0.1 add_convert_fusion.3
  55.5 2.5 %collective-permute-start.27 = (bf16[64,2048]{1,0:T(8,128)(2,1)S(1)}, bf16[64,2048]{1,0:T(8,128)(2,1)S(1)}, u32[]{:S(2)}, u32[]{:S(2)}) collective-permute-start(bf16[64,2048]{1,0:T(8,128)(2,1)S(1)} %add_convert_fusion.3), channel_id=1, source_target_pairs={{0,4},{1,3},{4,8},{5,1},{8,12},{9,5},{12,14},{13,9},{14,10},{15,13... | collective-permute-start | bytes 786440 | tf_op jit(solution)/shard_map/ppermute | solution.py:260
  58.0 2.0 %expert.9 = (bf16[64,2048]{1,0:T(8,128)(2,1)S(1)}, bf16[64,2048]{1,0:T(8,128)(2,1)S(1)}) custom-call(s32[1]{0:T(128)} %bitcast.own_ref, bf16[64,2176]{1,0:T(8,128)(2,1)S(1)} %copy-done, bf16[64,2176]{1,0:T(8,128)(2,1)S(1)} %collective-permute-done.1.refs_1_, bf16[1,2048,768]{2,1,0:T(8,128)(2,1)S(1)} %get-tuple-element.38.refs_4_.refs_2_, ...), custom_call_target="tpu_custom_call" | custom-call | flops 262144 | bytes 262144 | tf_op jit(solution)/shard_map/expert/pallas_call | solution.py:115
  60.1 0.8 %collective-permute-done.22 = bf16[64,2048]{1,0:T(8,128)(2,1)S(1)} collective-permute-done((bf16[64,2048]{1,0:T(8,128)(2,1)S(1)}, bf16[64,2048]{1,0:T(8,128)(2,1)S(1)}, u32[]{:S(2)}, u32[]{:S(2)}) %collective-permute-start.22) | collective-permute-done | bytes 262176 | tf_op jit(solution)/shard_map/ppermute | solution.py:266
  60.9 2.8 %collective-permute-done.27 = bf16[64,2048]{1,0:T(8,128)(2,1)S(1)} collective-permute-done((bf16[64,2048]{1,0:T(8,128)(2,1)S(1)}, bf16[64,2048]{1,0:T(8,128)(2,1)S(1)}, u32[]{:S(2)}, u32[]{:S(2)}) %collective-permute-start.27) | collective-permute-done | bytes 262176 | tf_op jit(solution)/shard_map/ppermute | solution.py:260
  63.7 0.1 add_convert_fusion.2
  63.8 1.0 %collective-permute-start.28 = (bf16[64,2048]{1,0:T(8,128)(2,1)S(1)}, bf16[64,2048]{1,0:T(8,128)(2,1)S(1)}, u32[]{:S(2)}, u32[]{:S(2)}) collective-permute-start(bf16[64,2048]{1,0:T(8,128)(2,1)S(1)} %add_convert_fusion.2), channel_id=1, source_target_pairs={{0,4},{1,3},{4,8},{5,1},{8,12},{9,5},{12,14},{13,9},{14,10},{15,13... | collective-permute-start | bytes 786440 | tf_op jit(solution)/shard_map/ppermute | solution.py:260
  64.8 0.1 add_convert_fusion.5
  64.9 1.7 %collective-permute-start.23 = (bf16[64,2048]{1,0:T(8,128)(2,1)S(1)}, bf16[64,2048]{1,0:T(8,128)(2,1)S(1)}, u32[]{:S(2)}, u32[]{:S(2)}) collective-permute-start(bf16[64,2048]{1,0:T(8,128)(2,1)S(1)} %add_convert_fusion.5), channel_id=1, source_target_pairs={{0,4},{1,3},{4,8},{5,1},{8,12},{9,5},{12,14},{13,9},{14,10},{15,13... | collective-permute-start | bytes 786440 | tf_op jit(solution)/shard_map/ppermute | solution.py:266
  66.6 3.6 %collective-permute-done.28 = bf16[64,2048]{1,0:T(8,128)(2,1)S(1)} collective-permute-done((bf16[64,2048]{1,0:T(8,128)(2,1)S(1)}, bf16[64,2048]{1,0:T(8,128)(2,1)S(1)}, u32[]{:S(2)}, u32[]{:S(2)}) %collective-permute-start.28) | collective-permute-done | bytes 262176 | tf_op jit(solution)/shard_map/ppermute | solution.py:260
  70.2 0.1 add_convert_fusion.1
  70.3 0.1 collective-permute-start.29
  70.4 2.7 %collective-permute-done.23 = bf16[64,2048]{1,0:T(8,128)(2,1)S(1)} collective-permute-done((bf16[64,2048]{1,0:T(8,128)(2,1)S(1)}, bf16[64,2048]{1,0:T(8,128)(2,1)S(1)}, u32[]{:S(2)}, u32[]{:S(2)}) %collective-permute-start.23) | collective-permute-done | bytes 262176 | tf_op jit(solution)/shard_map/ppermute | solution.py:266
  73.0 0.8 %add_convert_fusion = bf16[64,2048]{1,0:T(8,128)(2,1)} fusion(bf16[64,2048]{1,0:T(8,128)(2,1)S(1)} %collective-permute-done.29, bf16[64,2048]{1,0:T(8,128)(2,1)S(1)} %get-tuple-element.62, bf16[64,2048]{1,0:T(8,128)(2,1)S(1)} %collective-permute-done.23), kind=kLoop, calls=%fused_computation | loop fusion | flops 786432 | bytes 1048576 | tf_op jit(solution)/shard_map/convert_element_type | solution.py:209
  (15 shorter events, 0.0 us)
Async XLA Ops:
  1.7 3.2 %collective-permute-start.1 = (bf16[64,2176]{1,0:T(8,128)(2,1)}, bf16[64,2176]{1,0:T(8,128)(2,1)S(1)}, u32[]{:S(2)}, u32[]{:S(2)}) collective-permute-start(bf16[64,2176]{1,0:T(8,128)(2,1)} %pack.1.refs_0_), channel_id=1, source_target_pairs={{0,1},{1,0},{2,3},{3,2},{4,5},{5,4},{6,7},{7,6},{8,9},{9,8},{10,11... | collective-permute-start | bytes 835592 | tf_op jit(solution)/shard_map/ppermute | solution.py:226
  2.2 7.3 %collective-permute-start = (bf16[64,2176]{1,0:T(8,128)(2,1)}, bf16[64,2176]{1,0:T(8,128)(2,1)S(1)}, u32[]{:S(2)}, u32[]{:S(2)}) collective-permute-start(bf16[64,2176]{1,0:T(8,128)(2,1)} %pack.1.refs_0_), channel_id=1, source_target_pairs={{0,4},{1,3},{4,8},{5,1},{8,12},{9,5},{12,14},{13,9},{14,10},{15,13... | collective-permute-start | bytes 835592 | tf_op jit(solution)/shard_map/ppermute | solution.py:227
  4.9 7.6 %collective-permute-start.3 = (bf16[64,2176]{1,0:T(8,128)(2,1)S(1)}, bf16[64,2176]{1,0:T(8,128)(2,1)S(1)}, u32[]{:S(2)}, u32[]{:S(2)}) collective-permute-start(bf16[64,2176]{1,0:T(8,128)(2,1)S(1)} %collective-permute-done.1.refs_1_), channel_id=1, source_target_pairs={{0,4},{1,3},{4,8},{5,1},{8,12},{9,5},{12,14},{13,9},{14,10},{15,13... | collective-permute-start | bytes 835592 | tf_op jit(solution)/shard_map/ppermute | solution.py:227
  9.5 7.0 %collective-permute-start.7 = (bf16[64,2176]{1,0:T(8,128)(2,1)S(1)}, bf16[64,2176]{1,0:T(8,128)(2,1)S(1)}, u32[]{:S(2)}, u32[]{:S(2)}) collective-permute-start(bf16[64,2176]{1,0:T(8,128)(2,1)S(1)} %collective-permute-done.refs_2_), channel_id=1, source_target_pairs={{0,4},{1,3},{4,8},{5,1},{8,12},{9,5},{12,14},{13,9},{14,10},{15,13... | collective-permute-start | bytes 835592 | tf_op jit(solution)/shard_map/ppermute | solution.py:241
  12.5 6.5 %collective-permute-start.4 = (bf16[64,2176]{1,0:T(8,128)(2,1)S(1)}, bf16[64,2176]{1,0:T(8,128)(2,1)S(1)}, u32[]{:S(2)}, u32[]{:S(2)}) collective-permute-start(bf16[64,2176]{1,0:T(8,128)(2,1)S(1)} %collective-permute-done.3.refs_3_), channel_id=1, source_target_pairs={{0,4},{1,3},{4,8},{5,1},{8,12},{9,5},{12,14},{13,9},{14,10},{15,13... | collective-permute-start | bytes 835592 | tf_op jit(solution)/shard_map/ppermute | solution.py:236
  14.6 4.4 %collective-permute-start.2 = (bf16[64,2176]{1,0:T(8,128)(2,1)S(1)}, bf16[64,2176]{1,0:T(8,128)(2,1)S(1)}, u32[]{:S(2)}, u32[]{:S(2)}) collective-permute-start(bf16[64,2176]{1,0:T(8,128)(2,1)S(1)} %collective-permute-done.refs_2_), channel_id=1, source_target_pairs={{0,1},{1,0},{2,3},{3,2},{4,5},{5,4},{6,7},{7,6},{8,9},{9,8},{10,11... | collective-permute-start | bytes 835592 | tf_op jit(solution)/shard_map/ppermute | solution.py:237
  16.5 5.7 %collective-permute-start.9 = (bf16[64,2176]{1,0:T(8,128)(2,1)S(1)}, bf16[64,2176]{1,0:T(8,128)(2,1)S(1)}, u32[]{:S(2)}, u32[]{:S(2)}) collective-permute-start(bf16[64,2176]{1,0:T(8,128)(2,1)S(1)} %collective-permute-done.7.refs_2_), channel_id=1, source_target_pairs={{0,1},{1,0},{2,3},{3,2},{4,5},{5,4},{6,7},{7,6},{8,9},{9,8},{10,11... | collective-permute-start | bytes 835592 | tf_op jit(solution)/shard_map/ppermute | solution.py:237
  17.1 6.7 %collective-permute-start.10 = (bf16[64,2176]{1,0:T(8,128)(2,1)S(1)}, bf16[64,2176]{1,0:T(8,128)(2,1)S(1)}, u32[]{:S(2)}, u32[]{:S(2)}) collective-permute-start(bf16[64,2176]{1,0:T(8,128)(2,1)S(1)} %collective-permute-done.3.refs_3_), channel_id=1, source_target_pairs={{0,1},{1,0},{2,3},{3,2},{4,5},{5,4},{6,7},{7,6},{8,9},{9,8},{10,11... | collective-permute-start | bytes 835592 | tf_op jit(solution)/shard_map/ppermute | solution.py:237
  17.2 6.6 %collective-permute-start.13 = (bf16[64,2176]{1,0:T(8,128)(2,1)S(1)}, bf16[64,2176]{1,0:T(8,128)(2,1)S(1)}, u32[]{:S(2)}, u32[]{:S(2)}) collective-permute-start(bf16[64,2176]{1,0:T(8,128)(2,1)S(1)} %collective-permute-done.7.refs_2_), channel_id=1, source_target_pairs={{0,4},{1,3},{4,8},{5,1},{8,12},{9,5},{12,14},{13,9},{14,10},{15,13... | collective-permute-start | bytes 835592 | tf_op jit(solution)/shard_map/ppermute | solution.py:241
  19.1 4.7 %collective-permute-start.11 = (bf16[64,2176]{1,0:T(8,128)(2,1)S(1)}, bf16[64,2176]{1,0:T(8,128)(2,1)S(1)}, u32[]{:S(2)}, u32[]{:S(2)}) collective-permute-start(bf16[64,2176]{1,0:T(8,128)(2,1)S(1)} %collective-permute-done.4.refs_3_), channel_id=1, source_target_pairs={{0,1},{1,0},{2,3},{3,2},{4,5},{5,4},{6,7},{7,6},{8,9},{9,8},{10,11... | collective-permute-start | bytes 835592 | tf_op jit(solution)/shard_map/ppermute | solution.py:237
  19.1 11.5 %collective-permute-start.8 = (bf16[64,2176]{1,0:T(8,128)(2,1)S(1)}, bf16[64,2176]{1,0:T(8,128)(2,1)S(1)}, u32[]{:S(2)}, u32[]{:S(2)}) collective-permute-start(bf16[64,2176]{1,0:T(8,128)(2,1)S(1)} %collective-permute-done.7.refs_2_), channel_id=1, source_target_pairs={{0,8},{1,7},{4,12},{5,3},{8,14},{9,1},{12,10},{13,5},{14,6},{15,9}... | collective-permute-start | bytes 835592 | tf_op jit(solution)/shard_map/ppermute | solution.py:239
  22.2 9.6 %collective-permute-start.5 = (bf16[64,2176]{1,0:T(8,128)(2,1)S(1)}, bf16[64,2176]{1,0:T(8,128)(2,1)S(1)}, u32[]{:S(2)}, u32[]{:S(2)}) collective-permute-start(bf16[64,2176]{1,0:T(8,128)(2,1)S(1)} %collective-permute-done.4.refs_3_), channel_id=1, source_target_pairs={{0,4},{1,3},{4,8},{5,1},{8,12},{9,5},{12,14},{13,9},{14,10},{15,13... | collective-permute-start | bytes 835592 | tf_op jit(solution)/shard_map/ppermute | solution.py:236
  23.8 9.2 %collective-permute-start.14 = (bf16[64,2176]{1,0:T(8,128)(2,1)S(1)}, bf16[64,2176]{1,0:T(8,128)(2,1)S(1)}, u32[]{:S(2)}, u32[]{:S(2)}) collective-permute-start(bf16[64,2176]{1,0:T(8,128)(2,1)S(1)} %collective-permute-done.13.refs_3_), channel_id=1, source_target_pairs={{0,1},{1,0},{2,3},{3,2},{4,5},{5,4},{6,7},{7,6},{8,9},{9,8},{10,11... | collective-permute-start | bytes 835592 | tf_op jit(solution)/shard_map/ppermute | solution.py:237
  30.6 3.8 %collective-permute-start.12 = (bf16[64,2176]{1,0:T(8,128)(2,1)S(1)}, bf16[64,2176]{1,0:T(8,128)(2,1)S(1)}, u32[]{:S(2)}, u32[]{:S(2)}) collective-permute-start(bf16[64,2176]{1,0:T(8,128)(2,1)S(1)} %collective-permute-done.8.refs_1_), channel_id=1, source_target_pairs={{0,1},{1,0},{2,3},{3,2},{4,5},{5,4},{6,7},{7,6},{8,9},{9,8},{10,11... | collective-permute-start | bytes 835592 | tf_op jit(solution)/shard_map/ppermute | solution.py:249
  31.8 5.3 %collective-permute-start.6 = (bf16[64,2176]{1,0:T(8,128)(2,1)S(1)}, bf16[64,2176]{1,0:T(8,128)(2,1)S(1)}, u32[]{:S(2)}, u32[]{:S(2)}) collective-permute-start(bf16[64,2176]{1,0:T(8,128)(2,1)S(1)} %collective-permute-done.5.refs_1_), channel_id=1, source_target_pairs={{0,1},{1,0},{2,3},{3,2},{4,5},{5,4},{6,7},{7,6},{8,9},{9,8},{10,11... | collective-permute-start | bytes 835592 | tf_op jit(solution)/shard_map/ppermute | solution.py:237
  32.4 1.6 %collective-permute-start.15 = (bf16[64,2048]{1,0:T(8,128)(2,1)S(1)}, bf16[64,2048]{1,0:T(8,128)(2,1)S(1)}, u32[]{:S(2)}, u32[]{:S(2)}) collective-permute-start(bf16[64,2048]{1,0:T(8,128)(2,1)S(1)} %get-tuple-element.46), channel_id=1, source_target_pairs={{0,1},{1,0},{2,3},{3,2},{4,5},{5,4},{6,7},{7,6},{8,9},{9,8},{10,11... | collective-permute-start | bytes 786440 | tf_op jit(solution)/shard_map/ppermute | solution.py:244
  32.4 1.9 %collective-permute-start.16 = (bf16[64,2048]{1,0:T(8,128)(2,1)S(1)}, bf16[64,2048]{1,0:T(8,128)(2,1)S(1)}, u32[]{:S(2)}, u32[]{:S(2)}) collective-permute-start(bf16[64,2048]{1,0:T(8,128)(2,1)S(1)} %get-tuple-element.47), channel_id=1, source_target_pairs={{0,1},{1,0},{2,3},{3,2},{4,5},{5,4},{6,7},{7,6},{8,9},{9,8},{10,11... | collective-permute-start | bytes 786440 | tf_op jit(solution)/shard_map/ppermute | solution.py:244
  39.1 1.6 %collective-permute-start.17 = (bf16[64,2048]{1,0:T(8,128)(2,1)S(1)}, bf16[64,2048]{1,0:T(8,128)(2,1)S(1)}, u32[]{:S(2)}, u32[]{:S(2)}) collective-permute-start(bf16[64,2048]{1,0:T(8,128)(2,1)S(1)} %get-tuple-element.52), channel_id=1, source_target_pairs={{0,1},{1,0},{2,3},{3,2},{4,5},{5,4},{6,7},{7,6},{8,9},{9,8},{10,11... | collective-permute-start | bytes 786440 | tf_op jit(solution)/shard_map/ppermute | solution.py:244
  39.5 3.5 %collective-permute-start.20 = (bf16[64,2048]{1,0:T(8,128)(2,1)S(1)}, bf16[64,2048]{1,0:T(8,128)(2,1)S(1)}, u32[]{:S(2)}, u32[]{:S(2)}) collective-permute-start(bf16[64,2048]{1,0:T(8,128)(2,1)S(1)} %get-tuple-element.60), channel_id=1, source_target_pairs={{0,1},{1,0},{2,3},{3,2},{4,5},{5,4},{6,7},{7,6},{8,9},{9,8},{10,11... | collective-permute-start | bytes 786440 | tf_op jit(solution)/shard_map/ppermute | solution.py:252
  39.7 6.4 %collective-permute-start.25 = (bf16[64,2048]{1,0:T(8,128)(2,1)S(1)}, bf16[64,2048]{1,0:T(8,128)(2,1)S(1)}, u32[]{:S(2)}, u32[]{:S(2)}) collective-permute-start(bf16[64,2048]{1,0:T(8,128)(2,1)S(1)} %get-tuple-element.65), channel_id=1, source_target_pairs={{0,1},{1,0},{2,3},{3,2},{4,5},{5,4},{6,7},{7,6},{8,9},{9,8},{10,11... | collective-permute-start | bytes 786440 | tf_op jit(solution)/shard_map/ppermute | solution.py:244
  40.8 8.4 %collective-permute-start.19 = (bf16[64,2048]{1,0:T(8,128)(2,1)S(1)}, bf16[64,2048]{1,0:T(8,128)(2,1)S(1)}, u32[]{:S(2)}, u32[]{:S(2)}) collective-permute-start(bf16[64,2048]{1,0:T(8,128)(2,1)S(1)} %add_convert_fusion.8), channel_id=1, source_target_pairs={{0,4},{1,3},{4,8},{5,1},{8,12},{9,5},{12,14},{13,9},{14,10},{15,13... | collective-permute-start | bytes 786440 | tf_op jit(solution)/shard_map/ppermute | solution.py:266
  43.1 11.2 %collective-permute-start.21 = (bf16[64,2048]{1,0:T(8,128)(2,1)S(1)}, bf16[64,2048]{1,0:T(8,128)(2,1)S(1)}, u32[]{:S(2)}, u32[]{:S(2)}) collective-permute-start(bf16[64,2048]{1,0:T(8,128)(2,1)S(1)} %add_convert_fusion.7), channel_id=1, source_target_pairs={{0,8},{1,7},{4,12},{5,3},{8,14},{9,1},{12,10},{13,5},{14,6},{15,9}... | collective-permute-start | bytes 786440 | tf_op jit(solution)/shard_map/ppermute | solution.py:252
  46.2 11.9 %copy-start = (bf16[64,2176]{1,0:T(8,128)(2,1)S(1)}, bf16[64,2176]{1,0:T(8,128)(2,1)}, u32[]{:S(2)}) copy-start(bf16[64,2176]{1,0:T(8,128)(2,1)} %pack.1.refs_0_) | copy-start | bytes 835588
  46.2 9.2 %collective-permute-start.26 = (bf16[64,2048]{1,0:T(8,128)(2,1)S(1)}, bf16[64,2048]{1,0:T(8,128)(2,1)S(1)}, u32[]{:S(2)}, u32[]{:S(2)}) collective-permute-start(bf16[64,2048]{1,0:T(8,128)(2,1)S(1)} %add_convert_fusion.4), channel_id=1, source_target_pairs={{0,4},{1,3},{4,8},{5,1},{8,12},{9,5},{12,14},{13,9},{14,10},{15,13... | collective-permute-start | bytes 786440 | tf_op jit(solution)/shard_map/ppermute | solution.py:260
  49.1 11.7 %collective-permute-start.24 = (bf16[64,2048]{1,0:T(8,128)(2,1)S(1)}, bf16[64,2048]{1,0:T(8,128)(2,1)S(1)}, u32[]{:S(2)}, u32[]{:S(2)}) collective-permute-start(bf16[64,2048]{1,0:T(8,128)(2,1)S(1)} %get-tuple-element.64), channel_id=1, source_target_pairs={{0,1},{1,0},{2,3},{3,2},{4,5},{5,4},{6,7},{7,6},{8,9},{9,8},{10,11... | collective-permute-start | bytes 786440 | tf_op jit(solution)/shard_map/ppermute | solution.py:244
  54.5 6.4 %collective-permute-start.22 = (bf16[64,2048]{1,0:T(8,128)(2,1)S(1)}, bf16[64,2048]{1,0:T(8,128)(2,1)S(1)}, u32[]{:S(2)}, u32[]{:S(2)}) collective-permute-start(bf16[64,2048]{1,0:T(8,128)(2,1)S(1)} %add_convert_fusion.6), channel_id=1, source_target_pairs={{0,4},{1,3},{4,8},{5,1},{8,12},{9,5},{12,14},{13,9},{14,10},{15,13... | collective-permute-start | bytes 786440 | tf_op jit(solution)/shard_map/ppermute | solution.py:266
  55.5 8.2 %collective-permute-start.27 = (bf16[64,2048]{1,0:T(8,128)(2,1)S(1)}, bf16[64,2048]{1,0:T(8,128)(2,1)S(1)}, u32[]{:S(2)}, u32[]{:S(2)}) collective-permute-start(bf16[64,2048]{1,0:T(8,128)(2,1)S(1)} %add_convert_fusion.3), channel_id=1, source_target_pairs={{0,4},{1,3},{4,8},{5,1},{8,12},{9,5},{12,14},{13,9},{14,10},{15,13... | collective-permute-start | bytes 786440 | tf_op jit(solution)/shard_map/ppermute | solution.py:260
  58.0 6.7 %collective-permute-start.18 = (bf16[64,2048]{1,0:T(8,128)(2,1)S(1)}, bf16[64,2048]{1,0:T(8,128)(2,1)S(1)}, u32[]{:S(2)}, u32[]{:S(2)}) collective-permute-start(bf16[64,2048]{1,0:T(8,128)(2,1)S(1)} %get-tuple-element.55), channel_id=1, source_target_pairs={{0,1},{1,0},{2,3},{3,2},{4,5},{5,4},{6,7},{7,6},{8,9},{9,8},{10,11... | collective-permute-start | bytes 786440 | tf_op jit(solution)/shard_map/ppermute | solution.py:244
  63.8 6.4 %collective-permute-start.28 = (bf16[64,2048]{1,0:T(8,128)(2,1)S(1)}, bf16[64,2048]{1,0:T(8,128)(2,1)S(1)}, u32[]{:S(2)}, u32[]{:S(2)}) collective-permute-start(bf16[64,2048]{1,0:T(8,128)(2,1)S(1)} %add_convert_fusion.2), channel_id=1, source_target_pairs={{0,4},{1,3},{4,8},{5,1},{8,12},{9,5},{12,14},{13,9},{14,10},{15,13... | collective-permute-start | bytes 786440 | tf_op jit(solution)/shard_map/ppermute | solution.py:260
  64.9 8.2 %collective-permute-start.23 = (bf16[64,2048]{1,0:T(8,128)(2,1)S(1)}, bf16[64,2048]{1,0:T(8,128)(2,1)S(1)}, u32[]{:S(2)}, u32[]{:S(2)}) collective-permute-start(bf16[64,2048]{1,0:T(8,128)(2,1)S(1)} %add_convert_fusion.5), channel_id=1, source_target_pairs={{0,4},{1,3},{4,8},{5,1},{8,12},{9,5},{12,14},{13,9},{14,10},{15,13... | collective-permute-start | bytes 786440 | tf_op jit(solution)/shard_map/ppermute | solution.py:266
  70.3 2.7 %collective-permute-start.29 = (bf16[64,2048]{1,0:T(8,128)(2,1)S(1)}, bf16[64,2048]{1,0:T(8,128)(2,1)S(1)}, u32[]{:S(2)}, u32[]{:S(2)}) collective-permute-start(bf16[64,2048]{1,0:T(8,128)(2,1)S(1)} %add_convert_fusion.1), channel_id=1, source_target_pairs={{0,1},{1,0},{2,3},{3,2},{4,5},{5,4},{6,7},{7,6},{8,9},{9,8},{10,11... | collective-permute-start | bytes 786440 | tf_op jit(solution)/shard_map/ppermute | solution.py:267

commit v10 on v9

--- a/solution.py
+++ b/solution.py
@@ -76,13 +76,14 @@
 
 
 def expert_kernel(experts, blocks, own_ref, *refs):
-    gate_ref, up_ref, down_ref = refs[blocks : blocks + 3]
-    outs = refs[blocks + 3 : 2 * blocks + 3]
-    rows_ref, hidden_ref = refs[2 * blocks + 3 :]
+    gate_ref, up_ref, down_ref, *outs = refs[blocks:-2]
+    rows_ref, hidden_ref = refs[-2:]
     width, ff = gate_ref.shape[1:]
     each = outs[0].shape[0]
-    for number in range(blocks):
-        rows_ref[number * each : (number + 1) * each, :] = refs[number][...]
+    at = 0
+    for block in refs[:blocks]:
+        rows_ref[at : at + block.shape[0], :] = block[...]
+        at += block.shape[0]
     step = math.gcd(ff, 256)
     for at in range(0, ff, step):
         part = slice(at, at + step)
@@ -107,16 +108,16 @@
             target[:, part] = out[number * each : (number + 1) * each]
 
 
-def run_expert(own, blocks, weights, experts):
+def run_expert(own, blocks, weights, experts, each):
     rows = sum(block.shape[0] for block in blocks)
     wide = blocks[0].shape[1]
     width, ff = weights[0].shape[1:]
     vmem = pl.BlockSpec(memory_space=pltpu.VMEM)
     return pl.pallas_call(
         functools.partial(expert_kernel, experts, len(blocks)),
-        out_shape=[jax.ShapeDtypeStruct((block.shape[0], width), jnp.bfloat16) for block in blocks],
+        out_shape=[jax.ShapeDtypeStruct((each, width), jnp.bfloat16)] * (rows // each),
         in_specs=[pl.BlockSpec(memory_space=pltpu.SMEM)] + [vmem] * (len(blocks) + 3),
-        out_specs=[vmem] * len(blocks),
+        out_specs=[vmem] * (rows // each),
         scratch_shapes=[pltpu.VMEM((rows, wide), jnp.bfloat16), pltpu.VMEM((rows, ff), jnp.bfloat16)],
         compiler_params=pltpu.CompilerParams(vmem_limit_bytes=16 << 20),
         cost_estimate=pl.CostEstimate(
@@ -229,43 +230,39 @@
     first = after(first, gate_w)
     down_w, = load_weights((after(w_down, first),))
     weights = [gate_w, up_w, down_w]
-    run = lambda *blocks: run_expert(own, blocks, weights, experts)
+    run = lambda *blocks: run_expert(own, blocks, weights, experts, count)
     blocks = {}
-    for step in range(1, rounds):
+    for step in range(1, rounds - 1):
         if step > 1:
-            second = ring(second)
+            first, second = ring(first), ring(second)
+        if step == 2:
+            first = after(first, down_w)
         blocks[step] = (swap(first), swap(second), first, second)
-        if step == rounds - 2:
-            far = leap(first)
-        if step < rounds - 1:
-            first = ring(first)
-        if step == 1:
-            first = after(first, down_w)
-    turned = lambda keep_trail, keep, send_trail, send: (keep_trail, keep, swap(send_trail), swap(send))
+    far = leap(first)
+    both = ring(jnp.concatenate([first, second], 0))
+    turned = lambda keep, keep_trail, send, send_trail: (keep_trail, keep, swap(send_trail), swap(send))
     sums = {2: run(after(blocks[2][0], *blocks[1][:2]), *blocks[2][1:])}
     far = after(far, sums[2][0])
     sums[2] = turned(*sums[2])
-    near = after(blocks[3][0], *sums[2][2:])
-    send, keep, early, early_send = run(swap(far), far, near, blocks[3][2])
-    late, late_send = run(after(blocks[3][1], early), blocks[3][3])
-    sums[3] = turned(early, late, early_send, late_send)
-    far = leap(added(keep, swap(send)))
-    lead, trail = [], []
+    keep, send = run(swap(far), far)
+    lead, trail = [added(keep, swap(send))], []
+    sums[3] = turned(*run(after(swap(both), lead[0]), both))
+    lead = [ring(lead[0])]
     for step in range(rounds - 1, 0, -1):
         if step == 2:
-            lead = [after(lead[0], sums[1][0]), far]
+            lead = [after(lead[0], sums[1][0])]
         if step == 1:
             lead = [after(lead[0], kept)]
         keep_trail, keep, send_trail, send = sums[step]
-        trail = [ring(added(keep_trail, send_trail, *trail))]
+        trail = [added(keep_trail, send_trail, *trail)]
         lead = [added(keep, send, *lead)]
         if step == 3:
-            sums[1] = turned(*run(after(blocks[1][0], lead[0]), *blocks[1][1:]))
+            sums[1] = turned(*run(after(blocks[1][0], lead[0], trail[0]), *blocks[1][1:]))
         if step == 2:
             kept, other = run(after(mine, lead[0]), sibling)
-        lead = [ring(lead[0])]
-    last = swap(added(trail[0], other))
-    return added(lead[0], kept, last)
+        lead, trail = [ring(lead[0])], [ring(trail[0])]
+    last = swap(added(lead[0], other))
+    return added(trail[0], kept, last)
 
 
 def solution(mesh):

time: 74 us -> 63.5 us (0.86)
  waiting for transfers between devices: 23.7 us -> 15.4 us
  starting transfers between devices: 30 us -> 27.7 us
    ppermute x3 -> x1, starting transfers between devices: 4.93 us -> 1.43 us  [dense_body(): lead = [ring(lead[0])]]
    ppermute x11 -> x13, waiting for transfers between devices: 13 us -> 10 us  [the longest x6 7.58 us: dense_body(): lead, trail = ([ring(lead[0])], [ring(trail[0])])]
    ppermute x3 -> x1, waiting for transfers between devices: 3.48 us -> 1.25 us  [dense_body(): lead = [ring(lead[0])]]
    ppermute x11 -> x13, starting transfers between devices: 14.3 us -> 16.1 us  [the longest x6 9.59 us: dense_body(): lead, trail = ([ring(lead[0])], [ring(trail[0])])]
    ppermute x3, waiting for transfers between devices: 1.05 us -> 0.01 us  [dense_body(): swap(send_trail)]
    ppermute x3, waiting for transfers between devices: 1.03 us -> 0.01 us  [dense_body(): swap(send)]
    ppermute x1, waiting for transfers between devices: 4.16 us -> 3.16 us  [dense_body(): far = leap(first)]
  transfers between devices with their start and end apart: 30 -> 28, of which waited for: 13 -> 12; matrix products, arithmetic and copies ran while one was open for 1% -> 1% of each run, Pallas kernels for 20% -> 26%
where the time goes in v10:
time: 63.5 us; the launch traced here: 63.4 us
  starting transfers between devices  27.7 us (44%)
  Pallas kernels  18.5 us (29%)
  waiting for transfers between devices  15.4 us (24%)
  other arithmetic  1.54 us (2%)
    pallas_call x5, Pallas kernels, run_expert(): pl.pallas_call(functools.partial(expert_kernel, experts, len(blocks)), ou...  12.1 us
    ppermute x6, starting transfers between devices, dense_body(): lead, trail = ([ring(lead[0])], [ring(trail[0])])  9.59 us
    ppermute x6, waiting for transfers between devices, dense_body(): lead, trail = ([ring(lead[0])], [ring(trail[0])])  7.58 us
    pallas_call x2, Pallas kernels, load_weights(): pl.pallas_call(functools.partial(load_kernel, pieces), out_shape=[pltpu.V...  4.73 us
    ppermute x2, starting transfers between devices, dense_body(): first, second = (ring(mine), ring(sibling))  4.34 us
    ppermute x2, starting transfers between devices, dense_body(): first, second = (ring(first), ring(second))  4.21 us
    ppermute x1, waiting for transfers between devices, dense_body(): far = leap(first)  3.16 us
    ppermute x1, starting transfers between devices, dense_body(): far = leap(first)  2.59 us
  transfers between devices with their start and end apart: 28, of which 12 were waited for; matrix products, arithmetic and copies ran while one was open for 1% of the time, Pallas kernels for 26%

profile of v10, /device:TPU:0, one launch (start us, length us, event | category | flops | bytes accessed | tf_op | source)
XLA Modules:
  0.0 63.4 jit_solution(562877362282166669)
XLA Ops:
  0.0 1.7 %pack.1.refs_0_ = bf16[64,2176]{1,0:T(8,128)(2,1)} custom-call(bf16[64,2048]{1,0:T(8,128)(2,1)} %tokens_ref, s32[8,64]{1,0:T(8,128)} %bitcast.3, f32[8,64]{1,0:T(8,128)} %bitcast.4), custom_call_target="tpu_custom_call" | custom-call | bytes 1024 | tf_op jit(solution)/shard_map/pack/pallas_call | solution.py:191
  1.7 0.5 collective-permute-start.1
  2.2 2.6 %collective-permute-start = (bf16[64,2176]{1,0:T(8,128)(2,1)}, bf16[64,2176]{1,0:T(8,128)(2,1)S(1)}, u32[]{:S(2)}, u32[]{:S(2)}) collective-permute-start(bf16[64,2176]{1,0:T(8,128)(2,1)} %pack.1.refs_0_), channel_id=1, source_target_pairs={{0,4},{1,3},{4,8},{5,1},{8,12},{9,5},{12,14},{13,9},{14,10},{15,13... | collective-permute-start | bytes 835592 | tf_op jit(solution)/shard_map/ppermute | solution.py:228
  4.9 0.0 collective-permute-done.1.refs_1_
  4.9 1.7 %collective-permute-start.4 = (bf16[64,2176]{1,0:T(8,128)(2,1)S(1)}, bf16[64,2176]{1,0:T(8,128)(2,1)S(1)}, u32[]{:S(2)}, u32[]{:S(2)}) collective-permute-start(bf16[64,2176]{1,0:T(8,128)(2,1)S(1)} %collective-permute-done.1.refs_1_), channel_id=1, source_target_pairs={{0,4},{1,3},{4,8},{5,1},{8,12},{9,5},{12,14},{13,9},{14,10},{15,13... | collective-permute-start | bytes 835592 | tf_op jit(solution)/shard_map/ppermute | solution.py:228
  6.6 2.9 %load.2 = (bf16[1,2048,768]{2,1,0:T(8,128)(2,1)S(1)}, bf16[1,2048,768]{2,1,0:T(8,128)(2,1)S(1)}) custom-call(bf16[1,2048,768]{2,1,0:T(8,128)(2,1)} %refs_0_, bf16[1,2048,768]{2,1,0:T(8,128)(2,1)} %refs_1_.1), custom_call_target="tpu_custom_call" | custom-call | bytes 1024 | tf_op jit(solution)/shard_map/load/pallas_call | solution.py:149
  9.4 0.1 collective-permute-done.refs_2_
  9.5 2.1 %collective-permute-start.3 = (bf16[64,2176]{1,0:T(8,128)(2,1)S(1)}, bf16[64,2176]{1,0:T(8,128)(2,1)S(1)}, u32[]{:S(2)}, u32[]{:S(2)}) collective-permute-start(bf16[64,2176]{1,0:T(8,128)(2,1)S(1)} %collective-permute-done.refs_2_), channel_id=1, source_target_pairs={{0,4},{1,3},{4,8},{5,1},{8,12},{9,5},{12,14},{13,9},{14,10},{15,13... | collective-permute-start | bytes 835592 | tf_op jit(solution)/shard_map/ppermute | solution.py:237
  11.6 0.9 %collective-permute-done.4.refs_3_ = bf16[64,2176]{1,0:T(8,128)(2,1)S(1)} collective-permute-done((bf16[64,2176]{1,0:T(8,128)(2,1)S(1)}, bf16[64,2176]{1,0:T(8,128)(2,1)S(1)}, u32[]{:S(2)}, u32[]{:S(2)}) %collective-permute-start.4) | collective-permute-done | bytes 278560 | tf_op jit(solution)/shard_map/ppermute | solution.py:228
  12.5 2.1 %collective-permute-start.5 = (bf16[64,2176]{1,0:T(8,128)(2,1)S(1)}, bf16[64,2176]{1,0:T(8,128)(2,1)S(1)}, u32[]{:S(2)}, u32[]{:S(2)}) collective-permute-start(bf16[64,2176]{1,0:T(8,128)(2,1)S(1)} %collective-permute-done.4.refs_3_), channel_id=1, source_target_pairs={{0,4},{1,3},{4,8},{5,1},{8,12},{9,5},{12,14},{13,9},{14,10},{15,13... | collective-permute-start | bytes 835592 | tf_op jit(solution)/shard_map/ppermute | solution.py:237
  14.6 0.0 collective-permute-start.2
  14.6 1.9 %load.3.refs_6_.refs_4_ = bf16[1,2048,768]{2,1,0:T(8,128)(2,1)S(1)} custom-call(bf16[1,2048,768]{2,1,0:T(8,128)(2,1)} %refs_0_.1), custom_call_target="tpu_custom_call" | custom-call | bytes 1024 | tf_op jit(solution)/shard_map/load/pallas_call | solution.py:149
  16.5 0.6 collective-permute-start.9
  17.1 2.6 %collective-permute-start.8 = (bf16[64,2176]{1,0:T(8,128)(2,1)S(1)}, bf16[64,2176]{1,0:T(8,128)(2,1)S(1)}, u32[]{:S(2)}, u32[]{:S(2)}) collective-permute-start(bf16[64,2176]{1,0:T(8,128)(2,1)S(1)} %collective-permute-done.3.refs_2_), channel_id=1, source_target_pairs={{0,8},{1,7},{4,12},{5,3},{8,14},{9,1},{12,10},{13,5},{14,6},{15,9}... | collective-permute-start | bytes 835592 | tf_op jit(solution)/shard_map/ppermute | solution.py:241
  19.7 0.0 collective-permute-done.5.refs_3_
  19.7 0.5 collective-permute-start.11
  20.2 0.0 collective-permute-done.2.refs_0_
  20.2 1.5 %collective-permute-start.6 = (bf16[128,2176]{1,0:T(8,128)(2,1)S(1)}, bf16[128,2176]{1,0:T(8,128)(2,1)S(1)}, u32[]{:S(2)}, u32[]{:S(2)}) collective-permute-start(bf16[128,2176]{1,0:T(8,128)(2,1)S(1)} %pad_maximum_fusion), channel_id=1, source_target_pairs={{0,4},{1,3},{4,8},{5,1},{8,12},{9,5},{12,14},{13,9},{14,10},{15,13... | collective-permute-start | bytes 1671176 | tf_op jit(solution)/shard_map/ppermute | solution.py:242
  21.8 2.7 %expert.5 = (bf16[64,2048]{1,0:T(8,128)(2,1)S(1)}, bf16[64,2048]{1,0:T(8,128)(2,1)S(1)}, bf16[64,2048]{1,0:T(8,128)(2,1)S(1)}, bf16[64,2048]{1,0:T(8,128)(2,1)S(1)}) custom-call(s32[1]{0:T(128)} %bitcast.own_ref, bf16[64,2176]{1,0:T(8,128)(2,1)S(1)} %collective-permute-done.9.refs_0_, bf16[64,2176]{1,0:T(8,128)(2,1)S(1)} %collective-permute-done.11.refs_1_, ...), custom_call_target="tpu_custom_call" | custom-call | flops 524288 | bytes 524288 | tf_op jit(solution)/shard_map/expert/pallas_call | solution.py:116
  24.5 3.2 %collective-permute-done.8.refs_1_ = bf16[64,2176]{1,0:T(8,128)(2,1)S(1)} collective-permute-done((bf16[64,2176]{1,0:T(8,128)(2,1)S(1)}, bf16[64,2176]{1,0:T(8,128)(2,1)S(1)}, u32[]{:S(2)}, u32[]{:S(2)}) %collective-permute-start.8) | collective-permute-done | bytes 278560 | tf_op jit(solution)/shard_map/ppermute | solution.py:241
  27.6 0.0 collective-permute-start.12
  27.6 1.6 %collective-permute-done.12.refs_0_ = bf16[64,2176]{1,0:T(8,128)(2,1)S(1)} collective-permute-done((bf16[64,2176]{1,0:T(8,128)(2,1)S(1)}, bf16[64,2176]{1,0:T(8,128)(2,1)S(1)}, u32[]{:S(2)}, u32[]{:S(2)}) %collective-permute-start.12) | collective-permute-done | bytes 278560 | tf_op jit(solution)/shard_map/ppermute | solution.py:247
  29.2 2.0 %expert.6 = (bf16[64,2048]{1,0:T(8,128)(2,1)S(1)}, bf16[64,2048]{1,0:T(8,128)(2,1)S(1)}) custom-call(s32[1]{0:T(128)} %bitcast.own_ref, bf16[64,2176]{1,0:T(8,128)(2,1)S(1)} %collective-permute-done.12.refs_0_, bf16[64,2176]{1,0:T(8,128)(2,1)S(1)} %collective-permute-done.8.refs_1_, bf16[1,2048,768]{2,1,0:T(8,128)(2,1)S(1)} %get-tuple-element.37.refs_4_.refs_2_, ...), custom_call_target="tpu_custom_call" | custom-call | flops 262144 | bytes 262144 | tf_op jit(solution)/shard_map/expert/pallas_call | solution.py:116
  31.2 0.2 collective-permute-start.13
  31.4 0.5 collective-permute-done.6.refs_1_
  31.9 0.5 collective-permute-start.7
  32.4 0.4 collective-permute-done.13
  32.8 0.1 add_convert_fusion.8
  32.9 1.4 %collective-permute-start.15 = (bf16[64,2048]{1,0:T(8,128)(2,1)S(1)}, bf16[64,2048]{1,0:T(8,128)(2,1)S(1)}, u32[]{:S(2)}, u32[]{:S(2)}) collective-permute-start(bf16[64,2048]{1,0:T(8,128)(2,1)S(1)} %add_convert_fusion.8), channel_id=1, source_target_pairs={{0,4},{1,3},{4,8},{5,1},{8,12},{9,5},{12,14},{13,9},{14,10},{15,13... | collective-permute-start | bytes 786440 | tf_op jit(solution)/shard_map/ppermute | solution.py:250
  34.3 2.7 %expert.7 = (bf16[64,2048]{1,0:T(8,128)(2,1)S(1)}, bf16[64,2048]{1,0:T(8,128)(2,1)S(1)}, bf16[64,2048]{1,0:T(8,128)(2,1)S(1)}, bf16[64,2048]{1,0:T(8,128)(2,1)S(1)}) custom-call(s32[1]{0:T(128)} %bitcast.own_ref, bf16[128,2176]{1,0:T(8,128)(2,1)S(1)} %collective-permute-done.7.refs_0_, bf16[128,2176]{1,0:T(8,128)(2,1)S(1)} %collective-permute-done.6.refs_1_, ...), custom_call_target="tpu_custom_call" | custom-call | flops 524288 | bytes 524288 | tf_op jit(solution)/shard_map/expert/pallas_call | solution.py:116
  37.0 0.1 collective-permute-start.14
  37.1 0.4 collective-permute-start.18
  37.6 0.1 collective-permute-start.22
  37.6 0.4 collective-permute-start.16
  38.1 1.2 %collective-permute-done.15 = bf16[64,2048]{1,0:T(8,128)(2,1)S(1)} collective-permute-done((bf16[64,2048]{1,0:T(8,128)(2,1)S(1)}, bf16[64,2048]{1,0:T(8,128)(2,1)S(1)}, u32[]{:S(2)}, u32[]{:S(2)}) %collective-permute-start.15) | collective-permute-done | bytes 262176 | tf_op jit(solution)/shard_map/ppermute | solution.py:250
  39.3 0.0 collective-permute-done.14
  39.3 0.1 add_convert_fusion.7
  39.4 1.8 %collective-permute-start.23 = (bf16[64,2048]{1,0:T(8,128)(2,1)S(1)}, bf16[64,2048]{1,0:T(8,128)(2,1)S(1)}, u32[]{:S(2)}, u32[]{:S(2)}) collective-permute-start(bf16[64,2048]{1,0:T(8,128)(2,1)S(1)} %add_convert_fusion.7), channel_id=1, source_target_pairs={{0,4},{1,3},{4,8},{5,1},{8,12},{9,5},{12,14},{13,9},{14,10},{15,13... | collective-permute-start | bytes 786440 | tf_op jit(solution)/shard_map/ppermute | solution.py:263
  41.2 0.0 collective-permute-done.16
  41.2 0.1 add_convert_fusion.6
  41.3 2.2 %collective-permute-start.19 = (bf16[64,2048]{1,0:T(8,128)(2,1)S(1)}, bf16[64,2048]{1,0:T(8,128)(2,1)S(1)}, u32[]{:S(2)}, u32[]{:S(2)}) collective-permute-start(bf16[64,2048]{1,0:T(8,128)(2,1)S(1)} %add_convert_fusion.6), channel_id=1, source_target_pairs={{0,4},{1,3},{4,8},{5,1},{8,12},{9,5},{12,14},{13,9},{14,10},{15,13... | collective-permute-start | bytes 786440 | tf_op jit(solution)/shard_map/ppermute | solution.py:263
  43.4 2.7 %expert.8 = (bf16[64,2048]{1,0:T(8,128)(2,1)S(1)}, bf16[64,2048]{1,0:T(8,128)(2,1)S(1)}, bf16[64,2048]{1,0:T(8,128)(2,1)S(1)}, bf16[64,2048]{1,0:T(8,128)(2,1)S(1)}) custom-call(s32[1]{0:T(128)} %bitcast.own_ref, bf16[64,2176]{1,0:T(8,128)(2,1)S(1)} %collective-permute-done.2.refs_0_, bf16[64,2176]{1,0:T(8,128)(2,1)S(1)} %collective-permute-done.10.refs_1_, ...), custom_call_target="tpu_custom_call" | custom-call | flops 524288 | bytes 524288 | tf_op jit(solution)/shard_map/expert/pallas_call | solution.py:116
  46.1 0.1 collective-permute-start.17
  46.2 0.5 collective-permute-start.24
  46.7 0.0 collective-permute-done.22
  46.7 0.1 add_convert_fusion.3
  46.8 1.2 %collective-permute-start.25 = (bf16[64,2048]{1,0:T(8,128)(2,1)S(1)}, bf16[64,2048]{1,0:T(8,128)(2,1)S(1)}, u32[]{:S(2)}, u32[]{:S(2)}) collective-permute-start(bf16[64,2048]{1,0:T(8,128)(2,1)S(1)} %add_convert_fusion.3), channel_id=1, source_target_pairs={{0,4},{1,3},{4,8},{5,1},{8,12},{9,5},{12,14},{13,9},{14,10},{15,13... | collective-permute-start | bytes 786440 | tf_op jit(solution)/shard_map/ppermute | solution.py:263
  48.0 0.0 collective-permute-done.18
  48.0 0.7 %collective-permute-done.19 = bf16[64,2048]{1,0:T(8,128)(2,1)S(1)} collective-permute-done((bf16[64,2048]{1,0:T(8,128)(2,1)S(1)}, bf16[64,2048]{1,0:T(8,128)(2,1)S(1)}, u32[]{:S(2)}, u32[]{:S(2)}) %collective-permute-start.19) | collective-permute-done | bytes 262176 | tf_op jit(solution)/shard_map/ppermute | solution.py:263
  48.7 0.1 add_convert_fusion.5
  48.8 1.8 %collective-permute-start.20 = (bf16[64,2048]{1,0:T(8,128)(2,1)S(1)}, bf16[64,2048]{1,0:T(8,128)(2,1)S(1)}, u32[]{:S(2)}, u32[]{:S(2)}) collective-permute-start(bf16[64,2048]{1,0:T(8,128)(2,1)S(1)} %add_convert_fusion.5), channel_id=1, source_target_pairs={{0,4},{1,3},{4,8},{5,1},{8,12},{9,5},{12,14},{13,9},{14,10},{15,13... | collective-permute-start | bytes 786440 | tf_op jit(solution)/shard_map/ppermute | solution.py:263
  50.5 2.1 %expert.9 = (bf16[64,2048]{1,0:T(8,128)(2,1)S(1)}, bf16[64,2048]{1,0:T(8,128)(2,1)S(1)}) custom-call(s32[1]{0:T(128)} %bitcast.own_ref, bf16[64,2176]{1,0:T(8,128)(2,1)S(1)} %copy-done, bf16[64,2176]{1,0:T(8,128)(2,1)S(1)} %collective-permute-done.1.refs_1_, bf16[1,2048,768]{2,1,0:T(8,128)(2,1)S(1)} %get-tuple-element.37.refs_4_.refs_2_, ...), custom_call_target="tpu_custom_call" | custom-call | flops 262144 | bytes 262144 | tf_op jit(solution)/shard_map/expert/pallas_call | solution.py:116
  52.6 0.6 collective-permute-done.25
  53.2 0.1 add_convert_fusion.2
  53.3 1.6 %collective-permute-start.26 = (bf16[64,2048]{1,0:T(8,128)(2,1)S(1)}, bf16[64,2048]{1,0:T(8,128)(2,1)S(1)}, u32[]{:S(2)}, u32[]{:S(2)}) collective-permute-start(bf16[64,2048]{1,0:T(8,128)(2,1)S(1)} %add_convert_fusion.2), channel_id=1, source_target_pairs={{0,4},{1,3},{4,8},{5,1},{8,12},{9,5},{12,14},{13,9},{14,10},{15,13... | collective-permute-start | bytes 786440 | tf_op jit(solution)/shard_map/ppermute | solution.py:263
  54.9 1.1 %collective-permute-done.20 = bf16[64,2048]{1,0:T(8,128)(2,1)S(1)} collective-permute-done((bf16[64,2048]{1,0:T(8,128)(2,1)S(1)}, bf16[64,2048]{1,0:T(8,128)(2,1)S(1)}, u32[]{:S(2)}, u32[]{:S(2)}) %collective-permute-start.20) | collective-permute-done | bytes 262176 | tf_op jit(solution)/shard_map/ppermute | solution.py:263
  56.0 0.1 add_convert_fusion.4
  56.1 1.2 %collective-permute-start.21 = (bf16[64,2048]{1,0:T(8,128)(2,1)S(1)}, bf16[64,2048]{1,0:T(8,128)(2,1)S(1)}, u32[]{:S(2)}, u32[]{:S(2)}) collective-permute-start(bf16[64,2048]{1,0:T(8,128)(2,1)S(1)} %add_convert_fusion.4), channel_id=1, source_target_pairs={{0,4},{1,3},{4,8},{5,1},{8,12},{9,5},{12,14},{13,9},{14,10},{15,13... | collective-permute-start | bytes 786440 | tf_op jit(solution)/shard_map/ppermute | solution.py:263
  57.3 2.5 %collective-permute-done.26 = bf16[64,2048]{1,0:T(8,128)(2,1)S(1)} collective-permute-done((bf16[64,2048]{1,0:T(8,128)(2,1)S(1)}, bf16[64,2048]{1,0:T(8,128)(2,1)S(1)}, u32[]{:S(2)}, u32[]{:S(2)}) %collective-permute-start.26) | collective-permute-done | bytes 262176 | tf_op jit(solution)/shard_map/ppermute | solution.py:263
  59.8 0.1 add_convert_fusion.1
  59.8 0.1 collective-permute-start.27
  59.9 2.7 %collective-permute-done.21 = bf16[64,2048]{1,0:T(8,128)(2,1)S(1)} collective-permute-done((bf16[64,2048]{1,0:T(8,128)(2,1)S(1)}, bf16[64,2048]{1,0:T(8,128)(2,1)S(1)}, u32[]{:S(2)}, u32[]{:S(2)}) %collective-permute-start.21) | collective-permute-done | bytes 262176 | tf_op jit(solution)/shard_map/ppermute | solution.py:263
  62.6 0.0 collective-permute-done.27
  62.6 0.8 %add_convert_fusion = bf16[64,2048]{1,0:T(8,128)(2,1)} fusion(bf16[64,2048]{1,0:T(8,128)(2,1)S(1)} %collective-permute-done.27, bf16[64,2048]{1,0:T(8,128)(2,1)S(1)} %get-tuple-element.60, bf16[64,2048]{1,0:T(8,128)(2,1)S(1)} %collective-permute-done.21), kind=kLoop, calls=%fused_computation.1 | loop fusion | flops 786432 | bytes 1048576 | tf_op jit(solution)/shard_map/convert_element_type | solution.py:210
  (12 shorter events, 0.1 us)
Async XLA Ops:
  1.7 3.2 %collective-permute-start.1 = (bf16[64,2176]{1,0:T(8,128)(2,1)}, bf16[64,2176]{1,0:T(8,128)(2,1)S(1)}, u32[]{:S(2)}, u32[]{:S(2)}) collective-permute-start(bf16[64,2176]{1,0:T(8,128)(2,1)} %pack.1.refs_0_), channel_id=1, source_target_pairs={{0,1},{1,0},{2,3},{3,2},{4,5},{5,4},{6,7},{7,6},{8,9},{9,8},{10,11... | collective-permute-start | bytes 835592 | tf_op jit(solution)/shard_map/ppermute | solution.py:227
  2.2 7.3 %collective-permute-start = (bf16[64,2176]{1,0:T(8,128)(2,1)}, bf16[64,2176]{1,0:T(8,128)(2,1)S(1)}, u32[]{:S(2)}, u32[]{:S(2)}) collective-permute-start(bf16[64,2176]{1,0:T(8,128)(2,1)} %pack.1.refs_0_), channel_id=1, source_target_pairs={{0,4},{1,3},{4,8},{5,1},{8,12},{9,5},{12,14},{13,9},{14,10},{15,13... | collective-permute-start | bytes 835592 | tf_op jit(solution)/shard_map/ppermute | solution.py:228
  4.9 7.6 %collective-permute-start.4 = (bf16[64,2176]{1,0:T(8,128)(2,1)S(1)}, bf16[64,2176]{1,0:T(8,128)(2,1)S(1)}, u32[]{:S(2)}, u32[]{:S(2)}) collective-permute-start(bf16[64,2176]{1,0:T(8,128)(2,1)S(1)} %collective-permute-done.1.refs_1_), channel_id=1, source_target_pairs={{0,4},{1,3},{4,8},{5,1},{8,12},{9,5},{12,14},{13,9},{14,10},{15,13... | collective-permute-start | bytes 835592 | tf_op jit(solution)/shard_map/ppermute | solution.py:228
  9.5 7.0 %collective-permute-start.3 = (bf16[64,2176]{1,0:T(8,128)(2,1)S(1)}, bf16[64,2176]{1,0:T(8,128)(2,1)S(1)}, u32[]{:S(2)}, u32[]{:S(2)}) collective-permute-start(bf16[64,2176]{1,0:T(8,128)(2,1)S(1)} %collective-permute-done.refs_2_), channel_id=1, source_target_pairs={{0,4},{1,3},{4,8},{5,1},{8,12},{9,5},{12,14},{13,9},{14,10},{15,13... | collective-permute-start | bytes 835592 | tf_op jit(solution)/shard_map/ppermute | solution.py:237
  12.5 7.2 %collective-permute-start.5 = (bf16[64,2176]{1,0:T(8,128)(2,1)S(1)}, bf16[64,2176]{1,0:T(8,128)(2,1)S(1)}, u32[]{:S(2)}, u32[]{:S(2)}) collective-permute-start(bf16[64,2176]{1,0:T(8,128)(2,1)S(1)} %collective-permute-done.4.refs_3_), channel_id=1, source_target_pairs={{0,4},{1,3},{4,8},{5,1},{8,12},{9,5},{12,14},{13,9},{14,10},{15,13... | collective-permute-start | bytes 835592 | tf_op jit(solution)/shard_map/ppermute | solution.py:237
  14.6 5.6 %collective-permute-start.2 = (bf16[64,2176]{1,0:T(8,128)(2,1)S(1)}, bf16[64,2176]{1,0:T(8,128)(2,1)S(1)}, u32[]{:S(2)}, u32[]{:S(2)}) collective-permute-start(bf16[64,2176]{1,0:T(8,128)(2,1)S(1)} %collective-permute-done.refs_2_), channel_id=1, source_target_pairs={{0,1},{1,0},{2,3},{3,2},{4,5},{5,4},{6,7},{7,6},{8,9},{9,8},{10,11... | collective-permute-start | bytes 835592 | tf_op jit(solution)/shard_map/ppermute | solution.py:240
  16.5 5.3 %collective-permute-start.9 = (bf16[64,2176]{1,0:T(8,128)(2,1)S(1)}, bf16[64,2176]{1,0:T(8,128)(2,1)S(1)}, u32[]{:S(2)}, u32[]{:S(2)}) collective-permute-start(bf16[64,2176]{1,0:T(8,128)(2,1)S(1)} %collective-permute-done.3.refs_2_), channel_id=1, source_target_pairs={{0,1},{1,0},{2,3},{3,2},{4,5},{5,4},{6,7},{7,6},{8,9},{9,8},{10,11... | collective-permute-start | bytes 835592 | tf_op jit(solution)/shard_map/ppermute | solution.py:240
  17.1 10.5 %collective-permute-start.8 = (bf16[64,2176]{1,0:T(8,128)(2,1)S(1)}, bf16[64,2176]{1,0:T(8,128)(2,1)S(1)}, u32[]{:S(2)}, u32[]{:S(2)}) collective-permute-start(bf16[64,2176]{1,0:T(8,128)(2,1)S(1)} %collective-permute-done.3.refs_2_), channel_id=1, source_target_pairs={{0,8},{1,7},{4,12},{5,3},{8,14},{9,1},{12,10},{13,5},{14,6},{15,9}... | collective-permute-start | bytes 835592 | tf_op jit(solution)/shard_map/ppermute | solution.py:241
  19.7 2.1 %collective-permute-start.10 = (bf16[64,2176]{1,0:T(8,128)(2,1)S(1)}, bf16[64,2176]{1,0:T(8,128)(2,1)S(1)}, u32[]{:S(2)}, u32[]{:S(2)}) collective-permute-start(bf16[64,2176]{1,0:T(8,128)(2,1)S(1)} %collective-permute-done.4.refs_3_), channel_id=1, source_target_pairs={{0,1},{1,0},{2,3},{3,2},{4,5},{5,4},{6,7},{7,6},{8,9},{9,8},{10,11... | collective-permute-start | bytes 835592 | tf_op jit(solution)/shard_map/ppermute | solution.py:240
  19.7 2.1 %collective-permute-start.11 = (bf16[64,2176]{1,0:T(8,128)(2,1)S(1)}, bf16[64,2176]{1,0:T(8,128)(2,1)S(1)}, u32[]{:S(2)}, u32[]{:S(2)}) collective-permute-start(bf16[64,2176]{1,0:T(8,128)(2,1)S(1)} %collective-permute-done.5.refs_3_), channel_id=1, source_target_pairs={{0,1},{1,0},{2,3},{3,2},{4,5},{5,4},{6,7},{7,6},{8,9},{9,8},{10,11... | collective-permute-start | bytes 835592 | tf_op jit(solution)/shard_map/ppermute | solution.py:240
  20.2 11.7 %collective-permute-start.6 = (bf16[128,2176]{1,0:T(8,128)(2,1)S(1)}, bf16[128,2176]{1,0:T(8,128)(2,1)S(1)}, u32[]{:S(2)}, u32[]{:S(2)}) collective-permute-start(bf16[128,2176]{1,0:T(8,128)(2,1)S(1)} %pad_maximum_fusion), channel_id=1, source_target_pairs={{0,4},{1,3},{4,8},{5,1},{8,12},{9,5},{12,14},{13,9},{14,10},{15,13... | collective-permute-start | bytes 1671176 | tf_op jit(solution)/shard_map/ppermute | solution.py:242
  27.6 1.6 %collective-permute-start.12 = (bf16[64,2176]{1,0:T(8,128)(2,1)S(1)}, bf16[64,2176]{1,0:T(8,128)(2,1)S(1)}, u32[]{:S(2)}, u32[]{:S(2)}) collective-permute-start(bf16[64,2176]{1,0:T(8,128)(2,1)S(1)} %collective-permute-done.8.refs_1_), channel_id=1, source_target_pairs={{0,1},{1,0},{2,3},{3,2},{4,5},{5,4},{6,7},{7,6},{8,9},{9,8},{10,11... | collective-permute-start | bytes 835592 | tf_op jit(solution)/shard_map/ppermute | solution.py:247
  31.2 1.6 %collective-permute-start.13 = (bf16[64,2048]{1,0:T(8,128)(2,1)S(1)}, bf16[64,2048]{1,0:T(8,128)(2,1)S(1)}, u32[]{:S(2)}, u32[]{:S(2)}) collective-permute-start(bf16[64,2048]{1,0:T(8,128)(2,1)S(1)} %get-tuple-element.46), channel_id=1, source_target_pairs={{0,1},{1,0},{2,3},{3,2},{4,5},{5,4},{6,7},{7,6},{8,9},{9,8},{10,11... | collective-permute-start | bytes 786440 | tf_op jit(solution)/shard_map/ppermute | solution.py:248
  31.9 2.4 %collective-permute-start.7 = (bf16[128,2176]{1,0:T(8,128)(2,1)S(1)}, bf16[128,2176]{1,0:T(8,128)(2,1)S(1)}, u32[]{:S(2)}, u32[]{:S(2)}) collective-permute-start(bf16[128,2176]{1,0:T(8,128)(2,1)S(1)} %collective-permute-done.6.refs_1_), channel_id=1, source_target_pairs={{0,1},{1,0},{2,3},{3,2},{4,5},{5,4},{6,7},{7,6},{8,9},{9,8},{10,11... | collective-permute-start | bytes 1671176 | tf_op jit(solution)/shard_map/ppermute | solution.py:249
  32.9 6.4 %collective-permute-start.15 = (bf16[64,2048]{1,0:T(8,128)(2,1)S(1)}, bf16[64,2048]{1,0:T(8,128)(2,1)S(1)}, u32[]{:S(2)}, u32[]{:S(2)}) collective-permute-start(bf16[64,2048]{1,0:T(8,128)(2,1)S(1)} %add_convert_fusion.8), channel_id=1, source_target_pairs={{0,4},{1,3},{4,8},{5,1},{8,12},{9,5},{12,14},{13,9},{14,10},{15,13... | collective-permute-start | bytes 786440 | tf_op jit(solution)/shard_map/ppermute | solution.py:250
  37.0 2.3 %collective-permute-start.14 = (bf16[64,2048]{1,0:T(8,128)(2,1)S(1)}, bf16[64,2048]{1,0:T(8,128)(2,1)S(1)}, u32[]{:S(2)}, u32[]{:S(2)}) collective-permute-start(bf16[64,2048]{1,0:T(8,128)(2,1)S(1)} %get-tuple-element.49), channel_id=1, source_target_pairs={{0,1},{1,0},{2,3},{3,2},{4,5},{5,4},{6,7},{7,6},{8,9},{9,8},{10,11... | collective-permute-start | bytes 786440 | tf_op jit(solution)/shard_map/ppermute | solution.py:243
  37.1 10.8 %collective-permute-start.18 = (bf16[64,2048]{1,0:T(8,128)(2,1)S(1)}, bf16[64,2048]{1,0:T(8,128)(2,1)S(1)}, u32[]{:S(2)}, u32[]{:S(2)}) collective-permute-start(bf16[64,2048]{1,0:T(8,128)(2,1)S(1)} %get-tuple-element.56), channel_id=1, source_target_pairs={{0,1},{1,0},{2,3},{3,2},{4,5},{5,4},{6,7},{7,6},{8,9},{9,8},{10,11... | collective-permute-start | bytes 786440 | tf_op jit(solution)/shard_map/ppermute | solution.py:243
  37.6 9.1 %collective-permute-start.22 = (bf16[64,2048]{1,0:T(8,128)(2,1)S(1)}, bf16[64,2048]{1,0:T(8,128)(2,1)S(1)}, u32[]{:S(2)}, u32[]{:S(2)}) collective-permute-start(bf16[64,2048]{1,0:T(8,128)(2,1)S(1)} %get-tuple-element.57), channel_id=1, source_target_pairs={{0,1},{1,0},{2,3},{3,2},{4,5},{5,4},{6,7},{7,6},{8,9},{9,8},{10,11... | collective-permute-start | bytes 786440 | tf_op jit(solution)/shard_map/ppermute | solution.py:243
  37.6 3.6 %collective-permute-start.16 = (bf16[64,2048]{1,0:T(8,128)(2,1)S(1)}, bf16[64,2048]{1,0:T(8,128)(2,1)S(1)}, u32[]{:S(2)}, u32[]{:S(2)}) collective-permute-start(bf16[64,2048]{1,0:T(8,128)(2,1)S(1)} %get-tuple-element.51), channel_id=1, source_target_pairs={{0,1},{1,0},{2,3},{3,2},{4,5},{5,4},{6,7},{7,6},{8,9},{9,8},{10,11... | collective-permute-start | bytes 786440 | tf_op jit(solution)/shard_map/ppermute | solution.py:243
  39.4 6.8 %collective-permute-start.23 = (bf16[64,2048]{1,0:T(8,128)(2,1)S(1)}, bf16[64,2048]{1,0:T(8,128)(2,1)S(1)}, u32[]{:S(2)}, u32[]{:S(2)}) collective-permute-start(bf16[64,2048]{1,0:T(8,128)(2,1)S(1)} %add_convert_fusion.7), channel_id=1, source_target_pairs={{0,4},{1,3},{4,8},{5,1},{8,12},{9,5},{12,14},{13,9},{14,10},{15,13... | collective-permute-start | bytes 786440 | tf_op jit(solution)/shard_map/ppermute | solution.py:263
  41.3 9.3 %copy-start = (bf16[64,2176]{1,0:T(8,128)(2,1)S(1)}, bf16[64,2176]{1,0:T(8,128)(2,1)}, u32[]{:S(2)}) copy-start(bf16[64,2176]{1,0:T(8,128)(2,1)} %pack.1.refs_0_) | copy-start | bytes 835588
  41.3 7.4 %collective-permute-start.19 = (bf16[64,2048]{1,0:T(8,128)(2,1)S(1)}, bf16[64,2048]{1,0:T(8,128)(2,1)S(1)}, u32[]{:S(2)}, u32[]{:S(2)}) collective-permute-start(bf16[64,2048]{1,0:T(8,128)(2,1)S(1)} %add_convert_fusion.6), channel_id=1, source_target_pairs={{0,4},{1,3},{4,8},{5,1},{8,12},{9,5},{12,14},{13,9},{14,10},{15,13... | collective-permute-start | bytes 786440 | tf_op jit(solution)/shard_map/ppermute | solution.py:263
  46.1 8.8 %collective-permute-start.17 = (bf16[64,2048]{1,0:T(8,128)(2,1)S(1)}, bf16[64,2048]{1,0:T(8,128)(2,1)S(1)}, u32[]{:S(2)}, u32[]{:S(2)}) collective-permute-start(bf16[64,2048]{1,0:T(8,128)(2,1)S(1)} %get-tuple-element.54), channel_id=1, source_target_pairs={{0,1},{1,0},{2,3},{3,2},{4,5},{5,4},{6,7},{7,6},{8,9},{9,8},{10,11... | collective-permute-start | bytes 786440 | tf_op jit(solution)/shard_map/ppermute | solution.py:243
  46.2 7.0 %collective-permute-start.24 = (bf16[64,2048]{1,0:T(8,128)(2,1)S(1)}, bf16[64,2048]{1,0:T(8,128)(2,1)S(1)}, u32[]{:S(2)}, u32[]{:S(2)}) collective-permute-start(bf16[64,2048]{1,0:T(8,128)(2,1)S(1)} %get-tuple-element.62), channel_id=1, source_target_pairs={{0,1},{1,0},{2,3},{3,2},{4,5},{5,4},{6,7},{7,6},{8,9},{9,8},{10,11... | collective-permute-start | bytes 786440 | tf_op jit(solution)/shard_map/ppermute | solution.py:243
  46.8 6.4 %collective-permute-start.25 = (bf16[64,2048]{1,0:T(8,128)(2,1)S(1)}, bf16[64,2048]{1,0:T(8,128)(2,1)S(1)}, u32[]{:S(2)}, u32[]{:S(2)}) collective-permute-start(bf16[64,2048]{1,0:T(8,128)(2,1)S(1)} %add_convert_fusion.3), channel_id=1, source_target_pairs={{0,4},{1,3},{4,8},{5,1},{8,12},{9,5},{12,14},{13,9},{14,10},{15,13... | collective-permute-start | bytes 786440 | tf_op jit(solution)/shard_map/ppermute | solution.py:263
  48.8 7.3 %collective-permute-start.20 = (bf16[64,2048]{1,0:T(8,128)(2,1)S(1)}, bf16[64,2048]{1,0:T(8,128)(2,1)S(1)}, u32[]{:S(2)}, u32[]{:S(2)}) collective-permute-start(bf16[64,2048]{1,0:T(8,128)(2,1)S(1)} %add_convert_fusion.5), channel_id=1, source_target_pairs={{0,4},{1,3},{4,8},{5,1},{8,12},{9,5},{12,14},{13,9},{14,10},{15,13... | collective-permute-start | bytes 786440 | tf_op jit(solution)/shard_map/ppermute | solution.py:263
  53.3 6.4 %collective-permute-start.26 = (bf16[64,2048]{1,0:T(8,128)(2,1)S(1)}, bf16[64,2048]{1,0:T(8,128)(2,1)S(1)}, u32[]{:S(2)}, u32[]{:S(2)}) collective-permute-start(bf16[64,2048]{1,0:T(8,128)(2,1)S(1)} %add_convert_fusion.2), channel_id=1, source_target_pairs={{0,4},{1,3},{4,8},{5,1},{8,12},{9,5},{12,14},{13,9},{14,10},{15,13... | collective-permute-start | bytes 786440 | tf_op jit(solution)/shard_map/ppermute | solution.py:263
  56.1 6.4 %collective-permute-start.21 = (bf16[64,2048]{1,0:T(8,128)(2,1)S(1)}, bf16[64,2048]{1,0:T(8,128)(2,1)S(1)}, u32[]{:S(2)}, u32[]{:S(2)}) collective-permute-start(bf16[64,2048]{1,0:T(8,128)(2,1)S(1)} %add_convert_fusion.4), channel_id=1, source_target_pairs={{0,4},{1,3},{4,8},{5,1},{8,12},{9,5},{12,14},{13,9},{14,10},{15,13... | collective-permute-start | bytes 786440 | tf_op jit(solution)/shard_map/ppermute | solution.py:263
  59.8 2.7 %collective-permute-start.27 = (bf16[64,2048]{1,0:T(8,128)(2,1)S(1)}, bf16[64,2048]{1,0:T(8,128)(2,1)S(1)}, u32[]{:S(2)}, u32[]{:S(2)}) collective-permute-start(bf16[64,2048]{1,0:T(8,128)(2,1)S(1)} %add_convert_fusion.1), channel_id=1, source_target_pairs={{0,1},{1,0},{2,3},{3,2},{4,5},{5,4},{6,7},{7,6},{8,9},{9,8},{10,11... | collective-permute-start | bytes 786440 | tf_op jit(solution)/shard_map/ppermute | solution.py:264

commit v11 on v10

--- a/solution.py
+++ b/solution.py
@@ -65,13 +65,13 @@
     return [(index, index ^ 1) for index in range(experts)]
 
 
-def ring_pairs(experts, places):
+def ring_pairs(experts, places, cross=0):
     order = ring_order(experts // 2)
     count = len(order)
     pairs = []
     for place, chip in enumerate(order):
-        pairs.append((2 * chip, 2 * order[(place + places) % count]))
-        pairs.append((2 * chip + 1, 2 * order[(place - places) % count] + 1))
+        pairs.append((2 * chip, 2 * order[(place + places) % count] + cross))
+        pairs.append((2 * chip + 1, 2 * order[(place - places) % count] + 1 - cross))
     return pairs
 
 
@@ -203,11 +203,11 @@
     )(*[pltpu.with_memory_space_constraint(array, pltpu.HBM) for array in (tokens, ids, scale)])
 
 
-def added(*terms):
+def added(*terms, kind=jnp.bfloat16):
     total = terms[0].astype(jnp.float32)
     for term in terms[1:]:
         total = total + term.astype(jnp.float32)
-    return total.astype(jnp.bfloat16)
+    return total.astype(kind)
 
 
 def after(value, *others):
@@ -220,6 +220,7 @@
     rounds = experts // 4
     swap = functools.partial(lax.ppermute, axis_name="expert", perm=swap_pairs(experts))
     ring = functools.partial(lax.ppermute, axis_name="expert", perm=ring_pairs(experts, 1))
+    home = functools.partial(lax.ppermute, axis_name="expert", perm=ring_pairs(experts, 1, 1))
     leap = functools.partial(lax.ppermute, axis_name="expert", perm=ring_pairs(experts, 2))
     own = lax.axis_index("expert").reshape(1)
 
@@ -244,9 +245,11 @@
     sums = {2: run(after(blocks[2][0], *blocks[1][:2]), *blocks[2][1:])}
     far = after(far, sums[2][0])
     sums[2] = turned(*sums[2])
-    keep, send = run(swap(far), far)
+    send, = run(far)
+    keep, = run(after(swap(far), send))
     lead, trail = [added(keep, swap(send))], []
-    sums[3] = turned(*run(after(swap(both), lead[0]), both))
+    sent = run(after(both, lead[0]))
+    sums[3] = turned(*run(after(swap(both), sent[0])), *sent)
     lead = [ring(lead[0])]
     for step in range(rounds - 1, 0, -1):
         if step == 2:
@@ -254,15 +257,17 @@
         if step == 1:
             lead = [after(lead[0], kept)]
         keep_trail, keep, send_trail, send = sums[step]
-        trail = [added(keep_trail, send_trail, *trail)]
+        if step == 3:
+            keep, lead = lax.optimization_barrier(added(keep, *lead, kind=jnp.float32)), []
         lead = [added(keep, send, *lead)]
+        trail = [added(after(keep_trail, lead[0]), send_trail, *trail)]
         if step == 3:
-            sums[1] = turned(*run(after(blocks[1][0], lead[0], trail[0]), *blocks[1][1:]))
+            sums[1] = turned(*run(after(blocks[1][0], trail[0]), *blocks[1][1:]))
         if step == 2:
-            kept, other = run(after(mine, lead[0]), sibling)
-        lead, trail = [ring(lead[0])], [ring(trail[0])]
-    last = swap(added(lead[0], other))
-    return added(trail[0], kept, last)
+            kept, other = run(after(mine, trail[0]), sibling)
+        lead, trail = [(ring if step > 1 else home)(lead[0])], [ring(trail[0])]
+    near = lax.optimization_barrier(added(lead[0], kept, swap(other), kind=jnp.float32))
+    return added(near, trail[0])
 
 
 def solution(mesh):

time: 63.5 us -> 64.1 us (level)
  waiting for transfers between devices: 15.4 us -> 10.3 us
  Pallas kernels: 18.5 us -> 22.2 us
  starting transfers between devices: 27.7 us -> 29.6 us
    pallas_call x5 -> x7, Pallas kernels: 12.1 us -> 15.8 us  [run_expert(): pl.pallas_call(functools.partial(expert_kernel, experts, len(blocks)), ou...]
    ppermute x9, waiting for transfers between devices: 9.14 us -> 6.11 us  [the longest x6 6.1 us: dense_body(): lead, trail = ([(ring if step > 1 else home)(lead[0])], [ring(trail[0])])]
    ppermute x9, starting transfers between devices: 10.2 us -> 11.5 us  [the longest x6 11.3 us: dense_body(): lead, trail = ([(ring if step > 1 else home)(lead[0])], [ring(trail[0])])]
    ppermute x1, waiting for transfers between devices: 1.25 us -> 0.01 us  [dense_body(): lead = [ring(lead[0])]]
    convert_element_type x9 -> x8, other arithmetic: 1.5 us -> 1.38 us  [added(): return total.astype(kind)]
  transfers between devices with their start and end apart: 28 -> 28, of which waited for: 12 -> 7; matrix products, arithmetic and copies ran while one was open for 1% -> 1% of each run, Pallas kernels for 26% -> 32%
where the time goes in v11:
time: 64.1 us; the launch traced here: 63.9 us
  starting transfers between devices  29.6 us (46%)
  Pallas kernels  22.2 us (35%)
  waiting for transfers between devices  10.3 us (16%)
  other arithmetic  1.56 us (2%)
    pallas_call x7, Pallas kernels, run_expert(): pl.pallas_call(functools.partial(expert_kernel, experts, len(blocks)), ou...  15.8 us
    ppermute x6, starting transfers between devices, dense_body(): lead, trail = ([(ring if step > 1 else home)(lead[0])], [ring(trail[0])])  11.3 us
    ppermute x6, waiting for transfers between devices, dense_body(): lead, trail = ([(ring if step > 1 else home)(lead[0])], [ring(trail[0])])  6.1 us
    pallas_call x2, Pallas kernels, load_weights(): pl.pallas_call(functools.partial(load_kernel, pieces), out_shape=[pltpu.V...  4.73 us
    ppermute x2, starting transfers between devices, dense_body(): first, second = (ring(mine), ring(sibling))  4.34 us
    ppermute x2, starting transfers between devices, dense_body(): first, second = (ring(first), ring(second))  4.21 us
    ppermute x1, waiting for transfers between devices, dense_body(): far = leap(first)  3.16 us
    ppermute x1, starting transfers between devices, dense_body(): far = leap(first)  2.59 us
  transfers between devices with their start and end apart: 28, of which 7 were waited for; matrix products, arithmetic and copies ran while one was open for 1% of the time, Pallas kernels for 32%

profile of v11, /device:TPU:0, one launch (start us, length us, event | category | flops | bytes accessed | tf_op | source)
XLA Modules:
  0.0 63.9 jit_solution(13482446456563855427)
XLA Ops:
  0.0 1.7 %pack.1.refs_0_ = bf16[64,2176]{1,0:T(8,128)(2,1)} custom-call(bf16[64,2048]{1,0:T(8,128)(2,1)} %tokens_ref, s32[8,64]{1,0:T(8,128)} %bitcast.3, f32[8,64]{1,0:T(8,128)} %bitcast.4), custom_call_target="tpu_custom_call" | custom-call | bytes 1024 | tf_op jit(solution)/shard_map/pack/pallas_call | solution.py:191
  1.7 0.5 collective-permute-start.1
  2.2 2.6 %collective-permute-start = (bf16[64,2176]{1,0:T(8,128)(2,1)}, bf16[64,2176]{1,0:T(8,128)(2,1)S(1)}, u32[]{:S(2)}, u32[]{:S(2)}) collective-permute-start(bf16[64,2176]{1,0:T(8,128)(2,1)} %pack.1.refs_0_), channel_id=1, source_target_pairs={{0,4},{1,3},{4,8},{5,1},{8,12},{9,5},{12,14},{13,9},{14,10},{15,13... | collective-permute-start | bytes 835592 | tf_op jit(solution)/shard_map/ppermute | solution.py:229
  4.9 0.0 collective-permute-done.1.refs_1_
  4.9 1.7 %collective-permute-start.4 = (bf16[64,2176]{1,0:T(8,128)(2,1)S(1)}, bf16[64,2176]{1,0:T(8,128)(2,1)S(1)}, u32[]{:S(2)}, u32[]{:S(2)}) collective-permute-start(bf16[64,2176]{1,0:T(8,128)(2,1)S(1)} %collective-permute-done.1.refs_1_), channel_id=1, source_target_pairs={{0,4},{1,3},{4,8},{5,1},{8,12},{9,5},{12,14},{13,9},{14,10},{15,13... | collective-permute-start | bytes 835592 | tf_op jit(solution)/shard_map/ppermute | solution.py:229
  6.6 2.9 %load.2 = (bf16[1,2048,768]{2,1,0:T(8,128)(2,1)S(1)}, bf16[1,2048,768]{2,1,0:T(8,128)(2,1)S(1)}) custom-call(bf16[1,2048,768]{2,1,0:T(8,128)(2,1)} %refs_0_, bf16[1,2048,768]{2,1,0:T(8,128)(2,1)} %refs_1_.1), custom_call_target="tpu_custom_call" | custom-call | bytes 1024 | tf_op jit(solution)/shard_map/load/pallas_call | solution.py:149
  9.4 0.1 collective-permute-done.refs_2_
  9.5 2.1 %collective-permute-start.3 = (bf16[64,2176]{1,0:T(8,128)(2,1)S(1)}, bf16[64,2176]{1,0:T(8,128)(2,1)S(1)}, u32[]{:S(2)}, u32[]{:S(2)}) collective-permute-start(bf16[64,2176]{1,0:T(8,128)(2,1)S(1)} %collective-permute-done.refs_2_), channel_id=1, source_target_pairs={{0,4},{1,3},{4,8},{5,1},{8,12},{9,5},{12,14},{13,9},{14,10},{15,13... | collective-permute-start | bytes 835592 | tf_op jit(solution)/shard_map/ppermute | solution.py:238
  11.6 0.9 %collective-permute-done.4.refs_3_ = bf16[64,2176]{1,0:T(8,128)(2,1)S(1)} collective-permute-done((bf16[64,2176]{1,0:T(8,128)(2,1)S(1)}, bf16[64,2176]{1,0:T(8,128)(2,1)S(1)}, u32[]{:S(2)}, u32[]{:S(2)}) %collective-permute-start.4) | collective-permute-done | bytes 278560 | tf_op jit(solution)/shard_map/ppermute | solution.py:229
  12.5 2.1 %collective-permute-start.5 = (bf16[64,2176]{1,0:T(8,128)(2,1)S(1)}, bf16[64,2176]{1,0:T(8,128)(2,1)S(1)}, u32[]{:S(2)}, u32[]{:S(2)}) collective-permute-start(bf16[64,2176]{1,0:T(8,128)(2,1)S(1)} %collective-permute-done.4.refs_3_), channel_id=1, source_target_pairs={{0,4},{1,3},{4,8},{5,1},{8,12},{9,5},{12,14},{13,9},{14,10},{15,13... | collective-permute-start | bytes 835592 | tf_op jit(solution)/shard_map/ppermute | solution.py:238
  14.6 0.0 collective-permute-start.2
  14.6 1.9 %load.3.refs_6_.refs_3_.refs_4_ = bf16[1,2048,768]{2,1,0:T(8,128)(2,1)S(1)} custom-call(bf16[1,2048,768]{2,1,0:T(8,128)(2,1)} %refs_0_.1), custom_call_target="tpu_custom_call" | custom-call | bytes 1024 | tf_op jit(solution)/shard_map/load/pallas_call | solution.py:149
  16.5 0.6 collective-permute-start.9
  17.1 2.6 %collective-permute-start.8 = (bf16[64,2176]{1,0:T(8,128)(2,1)S(1)}, bf16[64,2176]{1,0:T(8,128)(2,1)S(1)}, u32[]{:S(2)}, u32[]{:S(2)}) collective-permute-start(bf16[64,2176]{1,0:T(8,128)(2,1)S(1)} %collective-permute-done.3.refs_2_), channel_id=1, source_target_pairs={{0,8},{1,7},{4,12},{5,3},{8,14},{9,1},{12,10},{13,5},{14,6},{15,9}... | collective-permute-start | bytes 835592 | tf_op jit(solution)/shard_map/ppermute | solution.py:242
  19.7 0.0 collective-permute-done.5.refs_3_
  19.7 0.5 collective-permute-start.11
  20.2 0.0 collective-permute-done.2.refs_0_
  20.2 1.5 %collective-permute-start.6 = (bf16[128,2176]{1,0:T(8,128)(2,1)S(1)}, bf16[128,2176]{1,0:T(8,128)(2,1)S(1)}, u32[]{:S(2)}, u32[]{:S(2)}) collective-permute-start(bf16[128,2176]{1,0:T(8,128)(2,1)S(1)} %pad_maximum_fusion), channel_id=1, source_target_pairs={{0,4},{1,3},{4,8},{5,1},{8,12},{9,5},{12,14},{13,9},{14,10},{15,13... | collective-permute-start | bytes 1671176 | tf_op jit(solution)/shard_map/ppermute | solution.py:243
  21.8 2.7 %expert.7 = (bf16[64,2048]{1,0:T(8,128)(2,1)S(1)}, bf16[64,2048]{1,0:T(8,128)(2,1)S(1)}, bf16[64,2048]{1,0:T(8,128)(2,1)S(1)}, bf16[64,2048]{1,0:T(8,128)(2,1)S(1)}) custom-call(s32[1]{0:T(128)} %bitcast.own_ref, bf16[64,2176]{1,0:T(8,128)(2,1)S(1)} %collective-permute-done.9.refs_0_, bf16[64,2176]{1,0:T(8,128)(2,1)S(1)} %collective-permute-done.11.refs_1_, ...), custom_call_target="tpu_custom_call" | custom-call | flops 524288 | bytes 524288 | tf_op jit(solution)/shard_map/expert/pallas_call | solution.py:116
  24.5 3.2 %collective-permute-done.8.refs_0_ = bf16[64,2176]{1,0:T(8,128)(2,1)S(1)} collective-permute-done((bf16[64,2176]{1,0:T(8,128)(2,1)S(1)}, bf16[64,2176]{1,0:T(8,128)(2,1)S(1)}, u32[]{:S(2)}, u32[]{:S(2)}) %collective-permute-start.8) | collective-permute-done | bytes 278560 | tf_op jit(solution)/shard_map/ppermute | solution.py:242
  27.6 0.0 collective-permute-start.12
  27.6 2.2 %expert.8 = bf16[64,2048]{1,0:T(8,128)(2,1)S(1)} custom-call(s32[1]{0:T(128)} %bitcast.own_ref, bf16[64,2176]{1,0:T(8,128)(2,1)S(1)} %collective-permute-done.8.refs_0_, bf16[1,2048,768]{2,1,0:T(8,128)(2,1)S(1)} %get-tuple-element.40.refs_4_.refs_1_.refs_2_, bf16[1,2048,768]{2,1,0:T(8,128)(2,1)S(1)} %get-tuple-element.45.refs_5_.refs_2_.refs_3_, ...), custom_call_target="tpu_custom_call" | custom-call | flops 131072 | bytes 131072 | tf_op jit(solution)/shard_map/expert/pallas_call | solution.py:116
  29.8 0.6 collective-permute-start.13
  30.4 2.2 %expert.9 = bf16[64,2048]{1,0:T(8,128)(2,1)S(1)} custom-call(s32[1]{0:T(128)} %bitcast.own_ref, bf16[64,2176]{1,0:T(8,128)(2,1)S(1)} %collective-permute-done.12.refs_0_, bf16[1,2048,768]{2,1,0:T(8,128)(2,1)S(1)} %get-tuple-element.40.refs_4_.refs_1_.refs_2_, bf16[1,2048,768]{2,1,0:T(8,128)(2,1)S(1)} %get-tuple-element.45.refs_5_.refs_2_.refs_3_, ...), custom_call_target="tpu_custom_call" | custom-call | flops 131072 | bytes 131072 | tf_op jit(solution)/shard_map/expert/pallas_call | solution.py:116
  32.6 0.1 collective-permute-start.7
  32.7 0.0 collective-permute-done.13
  32.7 0.1 add_convert_fusion.7
  32.7 1.6 %collective-permute-start.14 = (bf16[64,2048]{1,0:T(8,128)(2,1)S(1)}, bf16[64,2048]{1,0:T(8,128)(2,1)S(1)}, u32[]{:S(2)}, u32[]{:S(2)}) collective-permute-start(bf16[64,2048]{1,0:T(8,128)(2,1)S(1)} %add_convert_fusion.7), channel_id=1, source_target_pairs={{0,4},{1,3},{4,8},{5,1},{8,12},{9,5},{12,14},{13,9},{14,10},{15,13... | collective-permute-start | bytes 786440 | tf_op jit(solution)/shard_map/ppermute | solution.py:253
  34.3 0.1 collective-permute-start.18
  34.4 0.4 collective-permute-start.21
  34.8 2.0 %expert.10 = (bf16[64,2048]{1,0:T(8,128)(2,1)S(1)}, bf16[64,2048]{1,0:T(8,128)(2,1)S(1)}) custom-call(s32[1]{0:T(128)} %bitcast.own_ref, bf16[128,2176]{1,0:T(8,128)(2,1)S(1)} %collective-permute-done.6.refs_0_, bf16[1,2048,768]{2,1,0:T(8,128)(2,1)S(1)} %get-tuple-element.40.refs_4_.refs_1_.refs_2_, ...), custom_call_target="tpu_custom_call" | custom-call | flops 262144 | bytes 262144 | tf_op jit(solution)/shard_map/expert/pallas_call | solution.py:116
  36.9 0.2 collective-permute-start.15
  37.0 0.0 collective-permute-done.7.refs_0_
  37.0 0.4 collective-permute-start.16
  37.5 2.0 %expert.11 = (bf16[64,2048]{1,0:T(8,128)(2,1)S(1)}, bf16[64,2048]{1,0:T(8,128)(2,1)S(1)}) custom-call(s32[1]{0:T(128)} %bitcast.own_ref, bf16[128,2176]{1,0:T(8,128)(2,1)S(1)} %collective-permute-done.7.refs_0_, bf16[1,2048,768]{2,1,0:T(8,128)(2,1)S(1)} %get-tuple-element.40.refs_4_.refs_1_.refs_2_, ...), custom_call_target="tpu_custom_call" | custom-call | flops 262144 | bytes 262144 | tf_op jit(solution)/shard_map/expert/pallas_call | solution.py:116
  39.5 0.1 convert_add_fusion.1
  39.6 0.0 collective-permute-done.15
  39.6 0.1 add_convert_fusion.6
  39.7 2.5 %collective-permute-start.19 = (bf16[64,2048]{1,0:T(8,128)(2,1)S(1)}, bf16[64,2048]{1,0:T(8,128)(2,1)S(1)}, u32[]{:S(2)}, u32[]{:S(2)}) collective-permute-start(bf16[64,2048]{1,0:T(8,128)(2,1)S(1)} %add_convert_fusion.6), channel_id=1, source_target_pairs={{0,4},{1,3},{4,8},{5,1},{8,12},{9,5},{12,14},{13,9},{14,10},{15,13... | collective-permute-start | bytes 786440 | tf_op jit(solution)/shard_map/ppermute | solution.py:268
  42.2 0.0 collective-permute-done.16
  42.2 0.1 add_convert_fusion.5
  42.3 1.2 %collective-permute-start.22 = (bf16[64,2048]{1,0:T(8,128)(2,1)S(1)}, bf16[64,2048]{1,0:T(8,128)(2,1)S(1)}, u32[]{:S(2)}, u32[]{:S(2)}) collective-permute-start(bf16[64,2048]{1,0:T(8,128)(2,1)S(1)} %add_convert_fusion.5), channel_id=1, source_target_pairs={{0,4},{1,3},{4,8},{5,1},{8,12},{9,5},{12,14},{13,9},{14,10},{15,13... | collective-permute-start | bytes 786440 | tf_op jit(solution)/shard_map/ppermute | solution.py:268
  43.5 2.7 %expert.12 = (bf16[64,2048]{1,0:T(8,128)(2,1)S(1)}, bf16[64,2048]{1,0:T(8,128)(2,1)S(1)}, bf16[64,2048]{1,0:T(8,128)(2,1)S(1)}, bf16[64,2048]{1,0:T(8,128)(2,1)S(1)}) custom-call(s32[1]{0:T(128)} %bitcast.own_ref, bf16[64,2176]{1,0:T(8,128)(2,1)S(1)} %collective-permute-done.2.refs_0_, bf16[64,2176]{1,0:T(8,128)(2,1)S(1)} %collective-permute-done.10.refs_1_, ...), custom_call_target="tpu_custom_call" | custom-call | flops 524288 | bytes 524288 | tf_op jit(solution)/shard_map/expert/pallas_call | solution.py:116
  46.1 0.1 collective-permute-start.17
  46.2 0.5 collective-permute-start.25
  46.7 0.0 collective-permute-done.18
  46.7 0.1 add_convert_fusion.4
  46.8 1.9 %collective-permute-start.20 = (bf16[64,2048]{1,0:T(8,128)(2,1)S(1)}, bf16[64,2048]{1,0:T(8,128)(2,1)S(1)}, u32[]{:S(2)}, u32[]{:S(2)}) collective-permute-start(bf16[64,2048]{1,0:T(8,128)(2,1)S(1)} %add_convert_fusion.4), channel_id=1, source_target_pairs={{0,4},{1,3},{4,8},{5,1},{8,12},{9,5},{12,14},{13,9},{14,10},{15,13... | collective-permute-start | bytes 786440 | tf_op jit(solution)/shard_map/ppermute | solution.py:268
  48.7 0.0 collective-permute-done.21
  48.7 0.2 collective-permute-done.22
  48.9 0.1 add_convert_fusion.3
  49.0 2.5 %collective-permute-start.26 = (bf16[64,2048]{1,0:T(8,128)(2,1)S(1)}, bf16[64,2048]{1,0:T(8,128)(2,1)S(1)}, u32[]{:S(2)}, u32[]{:S(2)}) collective-permute-start(bf16[64,2048]{1,0:T(8,128)(2,1)S(1)} %add_convert_fusion.3), channel_id=1, source_target_pairs={{0,4},{1,3},{4,8},{5,1},{8,12},{9,5},{12,14},{13,9},{14,10},{15,13... | collective-permute-start | bytes 786440 | tf_op jit(solution)/shard_map/ppermute | solution.py:268
  51.5 2.0 %expert.13 = (bf16[64,2048]{1,0:T(8,128)(2,1)S(1)}, bf16[64,2048]{1,0:T(8,128)(2,1)S(1)}) custom-call(s32[1]{0:T(128)} %bitcast.own_ref, bf16[64,2176]{1,0:T(8,128)(2,1)S(1)} %copy-done, bf16[64,2176]{1,0:T(8,128)(2,1)S(1)} %collective-permute-done.1.refs_1_, bf16[1,2048,768]{2,1,0:T(8,128)(2,1)S(1)} %get-tuple-element.40.refs_4_.refs_1_.refs_2_, ...), custom_call_target="tpu_custom_call" | custom-call | flops 262144 | bytes 262144 | tf_op jit(solution)/shard_map/expert/pallas_call | solution.py:116
  53.6 0.1 collective-permute-start.24
  53.6 0.0 collective-permute-done.20
  53.7 0.1 add_convert_fusion.2
  53.8 1.3 %collective-permute-start.23 = (bf16[64,2048]{1,0:T(8,128)(2,1)S(1)}, bf16[64,2048]{1,0:T(8,128)(2,1)S(1)}, u32[]{:S(2)}, u32[]{:S(2)}) collective-permute-start(bf16[64,2048]{1,0:T(8,128)(2,1)S(1)} %add_convert_fusion.2), channel_id=1, source_target_pairs={{0,5},{1,2},{4,9},{5,0},{8,13},{9,4},{12,15},{13,8},{14,11},{15,12... | collective-permute-start | bytes 786440 | tf_op jit(solution)/shard_map/ppermute | solution.py:268
  55.1 1.0 %collective-permute-done.26 = bf16[64,2048]{1,0:T(8,128)(2,1)S(1)} collective-permute-done((bf16[64,2048]{1,0:T(8,128)(2,1)S(1)}, bf16[64,2048]{1,0:T(8,128)(2,1)S(1)}, u32[]{:S(2)}, u32[]{:S(2)}) %collective-permute-start.26) | collective-permute-done | bytes 262176 | tf_op jit(solution)/shard_map/ppermute | solution.py:268
  56.1 0.1 add_convert_fusion.1
  56.2 1.9 %collective-permute-start.27 = (bf16[64,2048]{1,0:T(8,128)(2,1)S(1)}, bf16[64,2048]{1,0:T(8,128)(2,1)S(1)}, u32[]{:S(2)}, u32[]{:S(2)}) collective-permute-start(bf16[64,2048]{1,0:T(8,128)(2,1)S(1)} %add_convert_fusion.1), channel_id=1, source_target_pairs={{0,4},{1,3},{4,8},{5,1},{8,12},{9,5},{12,14},{13,9},{14,10},{15,13... | collective-permute-start | bytes 786440 | tf_op jit(solution)/shard_map/ppermute | solution.py:268
  58.1 1.6 %collective-permute-done.23 = bf16[64,2048]{1,0:T(8,128)(2,1)S(1)} collective-permute-done((bf16[64,2048]{1,0:T(8,128)(2,1)S(1)}, bf16[64,2048]{1,0:T(8,128)(2,1)S(1)}, u32[]{:S(2)}, u32[]{:S(2)}) %collective-permute-start.23) | collective-permute-done | bytes 262176 | tf_op jit(solution)/shard_map/ppermute | solution.py:268
  59.6 0.1 convert_add_fusion
  59.7 3.4 %collective-permute-done.27 = bf16[64,2048]{1,0:T(8,128)(2,1)S(1)} collective-permute-done((bf16[64,2048]{1,0:T(8,128)(2,1)S(1)}, bf16[64,2048]{1,0:T(8,128)(2,1)S(1)}, u32[]{:S(2)}, u32[]{:S(2)}) %collective-permute-start.27) | collective-permute-done | bytes 262176 | tf_op jit(solution)/shard_map/ppermute | solution.py:268
  63.1 0.8 %add_convert_fusion = bf16[64,2048]{1,0:T(8,128)(2,1)} fusion(f32[64,2048]{1,0:T(8,128)S(1)} %convert_add_fusion, bf16[64,2048]{1,0:T(8,128)(2,1)S(1)} %collective-permute-done.27), kind=kLoop, calls=%fused_computation.1 | loop fusion | flops 393216 | bytes 1048576 | tf_op jit(solution)/shard_map/convert_element_type | solution.py:210
  (15 shorter events, 0.1 us)
Async XLA Ops:
  1.7 3.2 %collective-permute-start.1 = (bf16[64,2176]{1,0:T(8,128)(2,1)}, bf16[64,2176]{1,0:T(8,128)(2,1)S(1)}, u32[]{:S(2)}, u32[]{:S(2)}) collective-permute-start(bf16[64,2176]{1,0:T(8,128)(2,1)} %pack.1.refs_0_), channel_id=1, source_target_pairs={{0,1},{1,0},{2,3},{3,2},{4,5},{5,4},{6,7},{7,6},{8,9},{9,8},{10,11... | collective-permute-start | bytes 835592 | tf_op jit(solution)/shard_map/ppermute | solution.py:228
  2.2 7.3 %collective-permute-start = (bf16[64,2176]{1,0:T(8,128)(2,1)}, bf16[64,2176]{1,0:T(8,128)(2,1)S(1)}, u32[]{:S(2)}, u32[]{:S(2)}) collective-permute-start(bf16[64,2176]{1,0:T(8,128)(2,1)} %pack.1.refs_0_), channel_id=1, source_target_pairs={{0,4},{1,3},{4,8},{5,1},{8,12},{9,5},{12,14},{13,9},{14,10},{15,13... | collective-permute-start | bytes 835592 | tf_op jit(solution)/shard_map/ppermute | solution.py:229
  4.9 7.6 %collective-permute-start.4 = (bf16[64,2176]{1,0:T(8,128)(2,1)S(1)}, bf16[64,2176]{1,0:T(8,128)(2,1)S(1)}, u32[]{:S(2)}, u32[]{:S(2)}) collective-permute-start(bf16[64,2176]{1,0:T(8,128)(2,1)S(1)} %collective-permute-done.1.refs_1_), channel_id=1, source_target_pairs={{0,4},{1,3},{4,8},{5,1},{8,12},{9,5},{12,14},{13,9},{14,10},{15,13... | collective-permute-start | bytes 835592 | tf_op jit(solution)/shard_map/ppermute | solution.py:229
  9.5 7.0 %collective-permute-start.3 = (bf16[64,2176]{1,0:T(8,128)(2,1)S(1)}, bf16[64,2176]{1,0:T(8,128)(2,1)S(1)}, u32[]{:S(2)}, u32[]{:S(2)}) collective-permute-start(bf16[64,2176]{1,0:T(8,128)(2,1)S(1)} %collective-permute-done.refs_2_), channel_id=1, source_target_pairs={{0,4},{1,3},{4,8},{5,1},{8,12},{9,5},{12,14},{13,9},{14,10},{15,13... | collective-permute-start | bytes 835592 | tf_op jit(solution)/shard_map/ppermute | solution.py:238
  12.5 7.2 %collective-permute-start.5 = (bf16[64,2176]{1,0:T(8,128)(2,1)S(1)}, bf16[64,2176]{1,0:T(8,128)(2,1)S(1)}, u32[]{:S(2)}, u32[]{:S(2)}) collective-permute-start(bf16[64,2176]{1,0:T(8,128)(2,1)S(1)} %collective-permute-done.4.refs_3_), channel_id=1, source_target_pairs={{0,4},{1,3},{4,8},{5,1},{8,12},{9,5},{12,14},{13,9},{14,10},{15,13... | collective-permute-start | bytes 835592 | tf_op jit(solution)/shard_map/ppermute | solution.py:238
  14.6 5.6 %collective-permute-start.2 = (bf16[64,2176]{1,0:T(8,128)(2,1)S(1)}, bf16[64,2176]{1,0:T(8,128)(2,1)S(1)}, u32[]{:S(2)}, u32[]{:S(2)}) collective-permute-start(bf16[64,2176]{1,0:T(8,128)(2,1)S(1)} %collective-permute-done.refs_2_), channel_id=1, source_target_pairs={{0,1},{1,0},{2,3},{3,2},{4,5},{5,4},{6,7},{7,6},{8,9},{9,8},{10,11... | collective-permute-start | bytes 835592 | tf_op jit(solution)/shard_map/ppermute | solution.py:241
  16.5 5.3 %collective-permute-start.9 = (bf16[64,2176]{1,0:T(8,128)(2,1)S(1)}, bf16[64,2176]{1,0:T(8,128)(2,1)S(1)}, u32[]{:S(2)}, u32[]{:S(2)}) collective-permute-start(bf16[64,2176]{1,0:T(8,128)(2,1)S(1)} %collective-permute-done.3.refs_2_), channel_id=1, source_target_pairs={{0,1},{1,0},{2,3},{3,2},{4,5},{5,4},{6,7},{7,6},{8,9},{9,8},{10,11... | collective-permute-start | bytes 835592 | tf_op jit(solution)/shard_map/ppermute | solution.py:241
  17.1 10.5 %collective-permute-start.8 = (bf16[64,2176]{1,0:T(8,128)(2,1)S(1)}, bf16[64,2176]{1,0:T(8,128)(2,1)S(1)}, u32[]{:S(2)}, u32[]{:S(2)}) collective-permute-start(bf16[64,2176]{1,0:T(8,128)(2,1)S(1)} %collective-permute-done.3.refs_2_), channel_id=1, source_target_pairs={{0,8},{1,7},{4,12},{5,3},{8,14},{9,1},{12,10},{13,5},{14,6},{15,9}... | collective-permute-start | bytes 835592 | tf_op jit(solution)/shard_map/ppermute | solution.py:242
  19.7 2.1 %collective-permute-start.10 = (bf16[64,2176]{1,0:T(8,128)(2,1)S(1)}, bf16[64,2176]{1,0:T(8,128)(2,1)S(1)}, u32[]{:S(2)}, u32[]{:S(2)}) collective-permute-start(bf16[64,2176]{1,0:T(8,128)(2,1)S(1)} %collective-permute-done.4.refs_3_), channel_id=1, source_target_pairs={{0,1},{1,0},{2,3},{3,2},{4,5},{5,4},{6,7},{7,6},{8,9},{9,8},{10,11... | collective-permute-start | bytes 835592 | tf_op jit(solution)/shard_map/ppermute | solution.py:241
  19.7 2.1 %collective-permute-start.11 = (bf16[64,2176]{1,0:T(8,128)(2,1)S(1)}, bf16[64,2176]{1,0:T(8,128)(2,1)S(1)}, u32[]{:S(2)}, u32[]{:S(2)}) collective-permute-start(bf16[64,2176]{1,0:T(8,128)(2,1)S(1)} %collective-permute-done.5.refs_3_), channel_id=1, source_target_pairs={{0,1},{1,0},{2,3},{3,2},{4,5},{5,4},{6,7},{7,6},{8,9},{9,8},{10,11... | collective-permute-start | bytes 835592 | tf_op jit(solution)/shard_map/ppermute | solution.py:241
  20.2 12.3 %collective-permute-start.6 = (bf16[128,2176]{1,0:T(8,128)(2,1)S(1)}, bf16[128,2176]{1,0:T(8,128)(2,1)S(1)}, u32[]{:S(2)}, u32[]{:S(2)}) collective-permute-start(bf16[128,2176]{1,0:T(8,128)(2,1)S(1)} %pad_maximum_fusion), channel_id=1, source_target_pairs={{0,4},{1,3},{4,8},{5,1},{8,12},{9,5},{12,14},{13,9},{14,10},{15,13... | collective-permute-start | bytes 1671176 | tf_op jit(solution)/shard_map/ppermute | solution.py:243
  27.6 2.8 %collective-permute-start.12 = (bf16[64,2176]{1,0:T(8,128)(2,1)S(1)}, bf16[64,2176]{1,0:T(8,128)(2,1)S(1)}, u32[]{:S(2)}, u32[]{:S(2)}) collective-permute-start(bf16[64,2176]{1,0:T(8,128)(2,1)S(1)} %collective-permute-done.8.refs_0_), channel_id=1, source_target_pairs={{0,1},{1,0},{2,3},{3,2},{4,5},{5,4},{6,7},{7,6},{8,9},{9,8},{10,11... | collective-permute-start | bytes 835592 | tf_op jit(solution)/shard_map/ppermute | solution.py:249
  29.8 2.9 %collective-permute-start.13 = (bf16[64,2048]{1,0:T(8,128)(2,1)S(1)}, bf16[64,2048]{1,0:T(8,128)(2,1)S(1)}, u32[]{:S(2)}, u32[]{:S(2)}) collective-permute-start(bf16[64,2048]{1,0:T(8,128)(2,1)S(1)} %expert.8), channel_id=1, source_target_pairs={{0,1},{1,0},{2,3},{3,2},{4,5},{5,4},{6,7},{7,6},{8,9},{9,8},{10,11... | collective-permute-start | bytes 786440 | tf_op jit(solution)/shard_map/ppermute | solution.py:250
  32.6 4.5 %collective-permute-start.7 = (bf16[128,2176]{1,0:T(8,128)(2,1)S(1)}, bf16[128,2176]{1,0:T(8,128)(2,1)S(1)}, u32[]{:S(2)}, u32[]{:S(2)}) collective-permute-start(bf16[128,2176]{1,0:T(8,128)(2,1)S(1)} %collective-permute-done.6.refs_0_), channel_id=1, source_target_pairs={{0,1},{1,0},{2,3},{3,2},{4,5},{5,4},{6,7},{7,6},{8,9},{9,8},{10,11... | collective-permute-start | bytes 1671176 | tf_op jit(solution)/shard_map/ppermute | solution.py:252
  32.7 6.8 %collective-permute-start.14 = (bf16[64,2048]{1,0:T(8,128)(2,1)S(1)}, bf16[64,2048]{1,0:T(8,128)(2,1)S(1)}, u32[]{:S(2)}, u32[]{:S(2)}) collective-permute-start(bf16[64,2048]{1,0:T(8,128)(2,1)S(1)} %add_convert_fusion.7), channel_id=1, source_target_pairs={{0,4},{1,3},{4,8},{5,1},{8,12},{9,5},{12,14},{13,9},{14,10},{15,13... | collective-permute-start | bytes 786440 | tf_op jit(solution)/shard_map/ppermute | solution.py:253
  34.3 12.4 %collective-permute-start.18 = (bf16[64,2048]{1,0:T(8,128)(2,1)S(1)}, bf16[64,2048]{1,0:T(8,128)(2,1)S(1)}, u32[]{:S(2)}, u32[]{:S(2)}) collective-permute-start(bf16[64,2048]{1,0:T(8,128)(2,1)S(1)} %get-tuple-element.59), channel_id=1, source_target_pairs={{0,1},{1,0},{2,3},{3,2},{4,5},{5,4},{6,7},{7,6},{8,9},{9,8},{10,11... | collective-permute-start | bytes 786440 | tf_op jit(solution)/shard_map/ppermute | solution.py:244
  34.4 14.3 %collective-permute-start.21 = (bf16[64,2048]{1,0:T(8,128)(2,1)S(1)}, bf16[64,2048]{1,0:T(8,128)(2,1)S(1)}, u32[]{:S(2)}, u32[]{:S(2)}) collective-permute-start(bf16[64,2048]{1,0:T(8,128)(2,1)S(1)} %get-tuple-element.64), channel_id=1, source_target_pairs={{0,1},{1,0},{2,3},{3,2},{4,5},{5,4},{6,7},{7,6},{8,9},{9,8},{10,11... | collective-permute-start | bytes 786440 | tf_op jit(solution)/shard_map/ppermute | solution.py:244
  36.9 2.7 %collective-permute-start.15 = (bf16[64,2048]{1,0:T(8,128)(2,1)S(1)}, bf16[64,2048]{1,0:T(8,128)(2,1)S(1)}, u32[]{:S(2)}, u32[]{:S(2)}) collective-permute-start(bf16[64,2048]{1,0:T(8,128)(2,1)S(1)} %get-tuple-element.50), channel_id=1, source_target_pairs={{0,1},{1,0},{2,3},{3,2},{4,5},{5,4},{6,7},{7,6},{8,9},{9,8},{10,11... | collective-permute-start | bytes 786440 | tf_op jit(solution)/shard_map/ppermute | solution.py:244
  37.0 5.1 %collective-permute-start.16 = (bf16[64,2048]{1,0:T(8,128)(2,1)S(1)}, bf16[64,2048]{1,0:T(8,128)(2,1)S(1)}, u32[]{:S(2)}, u32[]{:S(2)}) collective-permute-start(bf16[64,2048]{1,0:T(8,128)(2,1)S(1)} %get-tuple-element.55), channel_id=1, source_target_pairs={{0,1},{1,0},{2,3},{3,2},{4,5},{5,4},{6,7},{7,6},{8,9},{9,8},{10,11... | collective-permute-start | bytes 786440 | tf_op jit(solution)/shard_map/ppermute | solution.py:244
  39.7 6.6 %collective-permute-start.19 = (bf16[64,2048]{1,0:T(8,128)(2,1)S(1)}, bf16[64,2048]{1,0:T(8,128)(2,1)S(1)}, u32[]{:S(2)}, u32[]{:S(2)}) collective-permute-start(bf16[64,2048]{1,0:T(8,128)(2,1)S(1)} %add_convert_fusion.6), channel_id=1, source_target_pairs={{0,4},{1,3},{4,8},{5,1},{8,12},{9,5},{12,14},{13,9},{14,10},{15,13... | collective-permute-start | bytes 786440 | tf_op jit(solution)/shard_map/ppermute | solution.py:268
  42.2 9.3 %copy-start = (bf16[64,2176]{1,0:T(8,128)(2,1)S(1)}, bf16[64,2176]{1,0:T(8,128)(2,1)}, u32[]{:S(2)}) copy-start(bf16[64,2176]{1,0:T(8,128)(2,1)} %pack.1.refs_0_) | copy-start | bytes 835588
  42.3 6.6 %collective-permute-start.22 = (bf16[64,2048]{1,0:T(8,128)(2,1)S(1)}, bf16[64,2048]{1,0:T(8,128)(2,1)S(1)}, u32[]{:S(2)}, u32[]{:S(2)}) collective-permute-start(bf16[64,2048]{1,0:T(8,128)(2,1)S(1)} %add_convert_fusion.5), channel_id=1, source_target_pairs={{0,4},{1,3},{4,8},{5,1},{8,12},{9,5},{12,14},{13,9},{14,10},{15,13... | collective-permute-start | bytes 786440 | tf_op jit(solution)/shard_map/ppermute | solution.py:268
  46.1 7.5 %collective-permute-start.17 = (bf16[64,2048]{1,0:T(8,128)(2,1)S(1)}, bf16[64,2048]{1,0:T(8,128)(2,1)S(1)}, u32[]{:S(2)}, u32[]{:S(2)}) collective-permute-start(bf16[64,2048]{1,0:T(8,128)(2,1)S(1)} %get-tuple-element.58), channel_id=1, source_target_pairs={{0,1},{1,0},{2,3},{3,2},{4,5},{5,4},{6,7},{7,6},{8,9},{9,8},{10,11... | collective-permute-start | bytes 786440 | tf_op jit(solution)/shard_map/ppermute | solution.py:244
  46.2 8.9 %collective-permute-start.25 = (bf16[64,2048]{1,0:T(8,128)(2,1)S(1)}, bf16[64,2048]{1,0:T(8,128)(2,1)S(1)}, u32[]{:S(2)}, u32[]{:S(2)}) collective-permute-start(bf16[64,2048]{1,0:T(8,128)(2,1)S(1)} %get-tuple-element.70), channel_id=1, source_target_pairs={{0,1},{1,0},{2,3},{3,2},{4,5},{5,4},{6,7},{7,6},{8,9},{9,8},{10,11... | collective-permute-start | bytes 786440 | tf_op jit(solution)/shard_map/ppermute | solution.py:244
  46.8 6.8 %collective-permute-start.20 = (bf16[64,2048]{1,0:T(8,128)(2,1)S(1)}, bf16[64,2048]{1,0:T(8,128)(2,1)S(1)}, u32[]{:S(2)}, u32[]{:S(2)}) collective-permute-start(bf16[64,2048]{1,0:T(8,128)(2,1)S(1)} %add_convert_fusion.4), channel_id=1, source_target_pairs={{0,4},{1,3},{4,8},{5,1},{8,12},{9,5},{12,14},{13,9},{14,10},{15,13... | collective-permute-start | bytes 786440 | tf_op jit(solution)/shard_map/ppermute | solution.py:268
  49.0 7.1 %collective-permute-start.26 = (bf16[64,2048]{1,0:T(8,128)(2,1)S(1)}, bf16[64,2048]{1,0:T(8,128)(2,1)S(1)}, u32[]{:S(2)}, u32[]{:S(2)}) collective-permute-start(bf16[64,2048]{1,0:T(8,128)(2,1)S(1)} %add_convert_fusion.3), channel_id=1, source_target_pairs={{0,4},{1,3},{4,8},{5,1},{8,12},{9,5},{12,14},{13,9},{14,10},{15,13... | collective-permute-start | bytes 786440 | tf_op jit(solution)/shard_map/ppermute | solution.py:268
  53.6 4.5 %collective-permute-start.24 = (bf16[64,2048]{1,0:T(8,128)(2,1)S(1)}, bf16[64,2048]{1,0:T(8,128)(2,1)S(1)}, u32[]{:S(2)}, u32[]{:S(2)}) collective-permute-start(bf16[64,2048]{1,0:T(8,128)(2,1)S(1)} %get-tuple-element.68), channel_id=1, source_target_pairs={{0,1},{1,0},{2,3},{3,2},{4,5},{5,4},{6,7},{7,6},{8,9},{9,8},{10,11... | collective-permute-start | bytes 786440 | tf_op jit(solution)/shard_map/ppermute | solution.py:269
  53.8 5.9 %collective-permute-start.23 = (bf16[64,2048]{1,0:T(8,128)(2,1)S(1)}, bf16[64,2048]{1,0:T(8,128)(2,1)S(1)}, u32[]{:S(2)}, u32[]{:S(2)}) collective-permute-start(bf16[64,2048]{1,0:T(8,128)(2,1)S(1)} %add_convert_fusion.2), channel_id=1, source_target_pairs={{0,5},{1,2},{4,9},{5,0},{8,13},{9,4},{12,15},{13,8},{14,11},{15,12... | collective-permute-start | bytes 786440 | tf_op jit(solution)/shard_map/ppermute | solution.py:268
  56.2 6.9 %collective-permute-start.27 = (bf16[64,2048]{1,0:T(8,128)(2,1)S(1)}, bf16[64,2048]{1,0:T(8,128)(2,1)S(1)}, u32[]{:S(2)}, u32[]{:S(2)}) collective-permute-start(bf16[64,2048]{1,0:T(8,128)(2,1)S(1)} %add_convert_fusion.1), channel_id=1, source_target_pairs={{0,4},{1,3},{4,8},{5,1},{8,12},{9,5},{12,14},{13,9},{14,10},{15,13... | collective-permute-start | bytes 786440 | tf_op jit(solution)/shard_map/ppermute | solution.py:268

commit v12 on v11

--- a/solution.py
+++ b/solution.py
@@ -220,14 +220,15 @@
     rounds = experts // 4
     swap = functools.partial(lax.ppermute, axis_name="expert", perm=swap_pairs(experts))
     ring = functools.partial(lax.ppermute, axis_name="expert", perm=ring_pairs(experts, 1))
+    pass_on = functools.partial(lax.ppermute, axis_name="expert", perm=ring_pairs(experts, -1, 1))
     home = functools.partial(lax.ppermute, axis_name="expert", perm=ring_pairs(experts, 1, 1))
     leap = functools.partial(lax.ppermute, axis_name="expert", perm=ring_pairs(experts, 2))
     own = lax.axis_index("expert").reshape(1)
 
     mine = pack(after(tokens, own), expert_ids, router_weights, experts)
+    first, second = ring(mine), pass_on(mine)
+    gate_w, up_w = load_weights((after(w_gate, mine), w_up))
     sibling = swap(mine)
-    first, second = ring(mine), ring(sibling)
-    gate_w, up_w = load_weights((after(w_gate, sibling), w_up))
     first = after(first, gate_w)
     down_w, = load_weights((after(w_down, first),))
     weights = [gate_w, up_w, down_w]
@@ -237,33 +238,26 @@
         if step > 1:
             first, second = ring(first), ring(second)
         if step == 2:
-            first = after(first, down_w)
-        blocks[step] = (swap(first), swap(second), first, second)
+            first = after(first, down_w, sibling)
+        blocks[step] = (swap(after(first, second) if step == 2 else first), swap(second), first, second)
     far = leap(first)
     both = ring(jnp.concatenate([first, second], 0))
     turned = lambda keep, keep_trail, send, send_trail: (keep_trail, keep, swap(send_trail), swap(send))
     sums = {2: run(after(blocks[2][0], *blocks[1][:2]), *blocks[2][1:])}
-    far = after(far, sums[2][0])
-    sums[2] = turned(*sums[2])
-    send, = run(far)
-    keep, = run(after(swap(far), send))
+    sums[1] = run(after(blocks[1][0], sums[2][0]), *blocks[1][1:])
+    far = after(far, sums[1][0])
+    sums[2], sums[1] = turned(*sums[2]), turned(*sums[1])
+    keep, send = run(after(swap(far), *sums[2][2:]), far)
     lead, trail = [added(keep, swap(send))], []
-    sent = run(after(both, lead[0]))
-    sums[3] = turned(*run(after(swap(both), sent[0])), *sent)
+    sums[3] = turned(*run(after(swap(both), lead[0]), both))
     lead = [ring(lead[0])]
     for step in range(rounds - 1, 0, -1):
         if step == 2:
-            lead = [after(lead[0], sums[1][0])]
-        if step == 1:
             lead = [after(lead[0], kept)]
         keep_trail, keep, send_trail, send = sums[step]
-        if step == 3:
-            keep, lead = lax.optimization_barrier(added(keep, *lead, kind=jnp.float32)), []
         lead = [added(keep, send, *lead)]
         trail = [added(after(keep_trail, lead[0]), send_trail, *trail)]
         if step == 3:
-            sums[1] = turned(*run(after(blocks[1][0], trail[0]), *blocks[1][1:]))
-        if step == 2:
             kept, other = run(after(mine, trail[0]), sibling)
         lead, trail = [(ring if step > 1 else home)(lead[0])], [ring(trail[0])]
     near = lax.optimization_barrier(added(lead[0], kept, swap(other), kind=jnp.float32))

time: 64.1 us -> 66.6 us (1.039)
  waiting for transfers between devices: 10.3 us -> 21.6 us
  starting transfers between devices: 29.6 us -> 24.6 us
  Pallas kernels: 22.2 us -> 18.5 us
    ppermute x6, waiting for transfers between devices: 6.1 us -> 13.2 us  [dense_body(): lead, trail = ([(ring if step > 1 else home)(lead[0])], [ring(trail[0])])]
    ppermute x6, starting transfers between devices: 11.3 us -> 6.02 us  [dense_body(): lead, trail = ([(ring if step > 1 else home)(lead[0])], [ring(trail[0])])]
    pallas_call x7 -> x5, Pallas kernels: 15.8 us -> 12.1 us  [run_expert(): pl.pallas_call(functools.partial(expert_kernel, experts, len(blocks)), ou...]
    ppermute x1, waiting for transfers between devices: 3.16 us -> 0.01 us  [dense_body(): far = leap(first)]
    ppermute x2, waiting for transfers between devices: 0.01 us -> 2.56 us  [dense_body(): first, second = (ring(first), ring(second))]
    ppermute x3, waiting for transfers between devices: 0.01 us -> 1.35 us  [dense_body(): swap(send)]
    ppermute x1, waiting for transfers between devices: 0.01 us -> 1.3 us  [dense_body(): lead = [ring(lead[0])]]
    ppermute x1, waiting for transfers between devices: 0.01 us -> 1.02 us  [dense_body(): lead, trail = ([added(keep, swap(send))], [])]
  transfers between devices with their start and end apart: 28 -> 28, of which waited for: 7 -> 13; matrix products, arithmetic and copies ran while one was open for 1% -> 1% of each run, Pallas kernels for 32% -> 25%
where the time goes in v12:
time: 66.6 us; the launch traced here: 66.4 us
  starting transfers between devices  24.6 us (37%)
  waiting for transfers between devices  21.6 us (32%)
  Pallas kernels  18.5 us (28%)
  other arithmetic  1.53 us (2%)
    ppermute x6, waiting for transfers between devices, dense_body(): lead, trail = ([(ring if step > 1 else home)(lead[0])], [ring(trail[0])])  13.2 us
    pallas_call x5, Pallas kernels, run_expert(): pl.pallas_call(functools.partial(expert_kernel, experts, len(blocks)), ou...  12.1 us
    ppermute x6, starting transfers between devices, dense_body(): lead, trail = ([(ring if step > 1 else home)(lead[0])], [ring(trail[0])])  6.02 us
    pallas_call x2, Pallas kernels, load_weights(): pl.pallas_call(functools.partial(load_kernel, pieces), out_shape=[pltpu.V...  4.73 us
    ppermute x2, starting transfers between devices, dense_body(): first, second = (ring(first), ring(second))  3.95 us
    ppermute x2, starting transfers between devices, dense_body(): first, second = (ring(mine), pass_on(mine))  3.73 us
    ppermute x2, waiting for transfers between devices, dense_body(): first, second = (ring(first), ring(second))  2.56 us
    ppermute x1, starting transfers between devices, dense_body(): both = ring(jnp.concatenate([first, second], 0))  2.53 us
  transfers between devices with their start and end apart: 28, of which 13 were waited for; matrix products, arithmetic and copies ran while one was open for 1% of the time, Pallas kernels for 25%

profile of v12, /device:TPU:0, one launch (start us, length us, event | category | flops | bytes accessed | tf_op | source)
XLA Modules:
  0.0 66.4 jit_solution(6829852271667609417)
XLA Ops:
  0.0 1.7 %pack.1.refs_0_ = bf16[64,2176]{1,0:T(8,128)(2,1)} custom-call(bf16[64,2048]{1,0:T(8,128)(2,1)} %tokens_ref, s32[8,64]{1,0:T(8,128)} %bitcast.3, f32[8,64]{1,0:T(8,128)} %bitcast.4), custom_call_target="tpu_custom_call" | custom-call | bytes 1024 | tf_op jit(solution)/shard_map/pack/pallas_call | solution.py:191
  1.7 3.1 %collective-permute-start = (bf16[64,2176]{1,0:T(8,128)(2,1)}, bf16[64,2176]{1,0:T(8,128)(2,1)S(1)}, u32[]{:S(2)}, u32[]{:S(2)}) collective-permute-start(bf16[64,2176]{1,0:T(8,128)(2,1)} %pack.1.refs_0_), channel_id=1, source_target_pairs={{0,4},{1,3},{4,8},{5,1},{8,12},{9,5},{12,14},{13,9},{14,10},{15,13... | collective-permute-start | bytes 835592 | tf_op jit(solution)/shard_map/ppermute | solution.py:229
  4.8 0.7 collective-permute-start.4
  5.4 1.0 %collective-permute-start.3 = (bf16[64,2176]{1,0:T(8,128)(2,1)}, bf16[64,2176]{1,0:T(8,128)(2,1)S(1)}, u32[]{:S(2)}, u32[]{:S(2)}) collective-permute-start(bf16[64,2176]{1,0:T(8,128)(2,1)} %pack.1.refs_0_), channel_id=1, source_target_pairs={{0,1},{1,0},{2,3},{3,2},{4,5},{5,4},{6,7},{7,6},{8,9},{9,8},{10,11... | collective-permute-start | bytes 835592 | tf_op jit(solution)/shard_map/ppermute | solution.py:231
  6.5 2.9 %load.2 = (bf16[1,2048,768]{2,1,0:T(8,128)(2,1)S(1)}, bf16[1,2048,768]{2,1,0:T(8,128)(2,1)S(1)}) custom-call(bf16[1,2048,768]{2,1,0:T(8,128)(2,1)} %refs_0_, bf16[1,2048,768]{2,1,0:T(8,128)(2,1)} %refs_1_.1), custom_call_target="tpu_custom_call" | custom-call | bytes 1024 | tf_op jit(solution)/shard_map/load/pallas_call | solution.py:149
  9.3 1.8 %collective-permute-done.refs_2_ = bf16[64,2176]{1,0:T(8,128)(2,1)S(1)} collective-permute-done((bf16[64,2176]{1,0:T(8,128)(2,1)}, bf16[64,2176]{1,0:T(8,128)(2,1)S(1)}, u32[]{:S(2)}, u32[]{:S(2)}) %collective-permute-start) | collective-permute-done | bytes 278560 | tf_op jit(solution)/shard_map/ppermute | solution.py:229
  11.2 2.4 %collective-permute-start.2 = (bf16[64,2176]{1,0:T(8,128)(2,1)S(1)}, bf16[64,2176]{1,0:T(8,128)(2,1)S(1)}, u32[]{:S(2)}, u32[]{:S(2)}) collective-permute-start(bf16[64,2176]{1,0:T(8,128)(2,1)S(1)} %collective-permute-done.refs_2_), channel_id=1, source_target_pairs={{0,4},{1,3},{4,8},{5,1},{8,12},{9,5},{12,14},{13,9},{14,10},{15,13... | collective-permute-start | bytes 835592 | tf_op jit(solution)/shard_map/ppermute | solution.py:239
  13.5 1.6 %collective-permute-start.5 = (bf16[64,2176]{1,0:T(8,128)(2,1)S(1)}, bf16[64,2176]{1,0:T(8,128)(2,1)S(1)}, u32[]{:S(2)}, u32[]{:S(2)}) collective-permute-start(bf16[64,2176]{1,0:T(8,128)(2,1)S(1)} %collective-permute-done.4.refs_3_), channel_id=1, source_target_pairs={{0,4},{1,3},{4,8},{5,1},{8,12},{9,5},{12,14},{13,9},{14,10},{15,13... | collective-permute-start | bytes 835592 | tf_op jit(solution)/shard_map/ppermute | solution.py:239
  15.1 0.0 collective-permute-start.1
  15.1 1.9 %load.3.refs_6_.refs_4_ = bf16[1,2048,768]{2,1,0:T(8,128)(2,1)S(1)} custom-call(bf16[1,2048,768]{2,1,0:T(8,128)(2,1)} %refs_0_.1), custom_call_target="tpu_custom_call" | custom-call | bytes 1024 | tf_op jit(solution)/shard_map/load/pallas_call | solution.py:149
  17.0 0.6 collective-permute-start.7
  17.6 0.0 collective-permute-done.3.refs_1_
  17.6 1.4 %collective-permute-done.2.refs_2_ = bf16[64,2176]{1,0:T(8,128)(2,1)S(1)} collective-permute-done((bf16[64,2176]{1,0:T(8,128)(2,1)S(1)}, bf16[64,2176]{1,0:T(8,128)(2,1)S(1)}, u32[]{:S(2)}, u32[]{:S(2)}) %collective-permute-start.2) | collective-permute-done | bytes 278560 | tf_op jit(solution)/shard_map/ppermute | solution.py:239
  18.9 2.1 %collective-permute-start.13 = (bf16[64,2176]{1,0:T(8,128)(2,1)S(1)}, bf16[64,2176]{1,0:T(8,128)(2,1)S(1)}, u32[]{:S(2)}, u32[]{:S(2)}) collective-permute-start(bf16[64,2176]{1,0:T(8,128)(2,1)S(1)} %collective-permute-done.2.refs_2_), channel_id=1, source_target_pairs={{0,8},{1,7},{4,12},{5,3},{8,14},{9,1},{12,10},{13,5},{14,6},{15,9}... | collective-permute-start | bytes 835592 | tf_op jit(solution)/shard_map/ppermute | solution.py:243
  21.1 1.2 %collective-permute-done.5.refs_3_ = bf16[64,2176]{1,0:T(8,128)(2,1)S(1)} collective-permute-done((bf16[64,2176]{1,0:T(8,128)(2,1)S(1)}, bf16[64,2176]{1,0:T(8,128)(2,1)S(1)}, u32[]{:S(2)}, u32[]{:S(2)}) %collective-permute-start.5) | collective-permute-done | bytes 278560 | tf_op jit(solution)/shard_map/ppermute | solution.py:239
  22.3 0.0 collective-permute-start.6
  22.3 0.5 collective-permute-start.8
  22.8 0.0 collective-permute-done.7.refs_1_
  22.8 2.5 %collective-permute-start.11 = (bf16[128,2176]{1,0:T(8,128)(2,1)S(1)}, bf16[128,2176]{1,0:T(8,128)(2,1)S(1)}, u32[]{:S(2)}, u32[]{:S(2)}) collective-permute-start(bf16[128,2176]{1,0:T(8,128)(2,1)S(1)} %pad_maximum_fusion), channel_id=1, source_target_pairs={{0,4},{1,3},{4,8},{5,1},{8,12},{9,5},{12,14},{13,9},{14,10},{15,13... | collective-permute-start | bytes 1671176 | tf_op jit(solution)/shard_map/ppermute | solution.py:244
  25.4 0.0 collective-permute-done.6.refs_0_
  25.4 0.0 collective-permute-done.8.refs_1_
  25.4 2.7 %expert.5 = (bf16[64,2048]{1,0:T(8,128)(2,1)S(1)}, bf16[64,2048]{1,0:T(8,128)(2,1)S(1)}, bf16[64,2048]{1,0:T(8,128)(2,1)S(1)}, bf16[64,2048]{1,0:T(8,128)(2,1)S(1)}) custom-call(s32[1]{0:T(128)} %bitcast.own_ref, bf16[64,2176]{1,0:T(8,128)(2,1)S(1)} %collective-permute-done.6.refs_0_, bf16[64,2176]{1,0:T(8,128)(2,1)S(1)} %collective-permute-done.8.refs_1_, ...), custom_call_target="tpu_custom_call" | custom-call | flops 524288 | bytes 524288 | tf_op jit(solution)/shard_map/expert/pallas_call | solution.py:116
  28.1 2.7 %expert.6 = (bf16[64,2048]{1,0:T(8,128)(2,1)S(1)}, bf16[64,2048]{1,0:T(8,128)(2,1)S(1)}, bf16[64,2048]{1,0:T(8,128)(2,1)S(1)}, bf16[64,2048]{1,0:T(8,128)(2,1)S(1)}) custom-call(s32[1]{0:T(128)} %bitcast.own_ref, bf16[64,2176]{1,0:T(8,128)(2,1)S(1)} %collective-permute-done.1.refs_0_, bf16[64,2176]{1,0:T(8,128)(2,1)S(1)} %collective-permute-done.7.refs_1_, ...), custom_call_target="tpu_custom_call" | custom-call | flops 524288 | bytes 524288 | tf_op jit(solution)/shard_map/expert/pallas_call | solution.py:116
  30.7 0.0 collective-permute-done.13.refs_1_
  30.7 0.1 collective-permute-start.14
  30.8 0.5 collective-permute-start.10
  31.3 0.1 collective-permute-start.15
  31.4 1.3 %collective-permute-done.10 = bf16[64,2048]{1,0:T(8,128)(2,1)S(1)} collective-permute-done((bf16[64,2048]{1,0:T(8,128)(2,1)S(1)}, bf16[64,2048]{1,0:T(8,128)(2,1)S(1)}, u32[]{:S(2)}, u32[]{:S(2)}) %collective-permute-start.10) | collective-permute-done | bytes 262176 | tf_op jit(solution)/shard_map/ppermute | solution.py:245
  32.7 0.4 collective-permute-done.15
  33.1 0.0 collective-permute-done.14.refs_0_
  33.1 2.0 %expert.7 = (bf16[64,2048]{1,0:T(8,128)(2,1)S(1)}, bf16[64,2048]{1,0:T(8,128)(2,1)S(1)}) custom-call(s32[1]{0:T(128)} %bitcast.own_ref, bf16[64,2176]{1,0:T(8,128)(2,1)S(1)} %collective-permute-done.14.refs_0_, bf16[64,2176]{1,0:T(8,128)(2,1)S(1)} %collective-permute-done.13.refs_1_, bf16[1,2048,768]{2,1,0:T(8,128)(2,1)S(1)} %get-tuple-element.41.refs_4_.refs_2_, ...), custom_call_target="tpu_custom_call" | custom-call | flops 262144 | bytes 262144 | tf_op jit(solution)/shard_map/expert/pallas_call | solution.py:116
  35.2 0.2 collective-permute-start.16
  35.4 0.4 collective-permute-start.12
  35.7 1.0 %collective-permute-done.16 = bf16[64,2048]{1,0:T(8,128)(2,1)S(1)} collective-permute-done((bf16[64,2048]{1,0:T(8,128)(2,1)S(1)}, bf16[64,2048]{1,0:T(8,128)(2,1)S(1)}, u32[]{:S(2)}, u32[]{:S(2)}) %collective-permute-start.16) | collective-permute-done | bytes 262176 | tf_op jit(solution)/shard_map/ppermute | solution.py:251
  36.8 0.1 add_convert_fusion.7
  36.8 1.4 %collective-permute-start.18 = (bf16[64,2048]{1,0:T(8,128)(2,1)S(1)}, bf16[64,2048]{1,0:T(8,128)(2,1)S(1)}, u32[]{:S(2)}, u32[]{:S(2)}) collective-permute-start(bf16[64,2048]{1,0:T(8,128)(2,1)S(1)} %add_convert_fusion.7), channel_id=1, source_target_pairs={{0,4},{1,3},{4,8},{5,1},{8,12},{9,5},{12,14},{13,9},{14,10},{15,13... | collective-permute-start | bytes 786440 | tf_op jit(solution)/shard_map/ppermute | solution.py:253
  38.2 2.7 %expert.8 = (bf16[64,2048]{1,0:T(8,128)(2,1)S(1)}, bf16[64,2048]{1,0:T(8,128)(2,1)S(1)}, bf16[64,2048]{1,0:T(8,128)(2,1)S(1)}, bf16[64,2048]{1,0:T(8,128)(2,1)S(1)}) custom-call(s32[1]{0:T(128)} %bitcast.own_ref, bf16[128,2176]{1,0:T(8,128)(2,1)S(1)} %collective-permute-done.12.refs_0_, bf16[128,2176]{1,0:T(8,128)(2,1)S(1)} %collective-permute-done.11.refs_1_, ...), custom_call_target="tpu_custom_call" | custom-call | flops 524288 | bytes 524288 | tf_op jit(solution)/shard_map/expert/pallas_call | solution.py:116
  40.9 0.1 collective-permute-start.17
  41.0 0.5 collective-permute-start.9
  41.5 0.1 collective-permute-start.24
  41.5 0.4 collective-permute-start.20
  42.0 1.3 %collective-permute-done.18 = bf16[64,2048]{1,0:T(8,128)(2,1)S(1)} collective-permute-done((bf16[64,2048]{1,0:T(8,128)(2,1)S(1)}, bf16[64,2048]{1,0:T(8,128)(2,1)S(1)}, u32[]{:S(2)}, u32[]{:S(2)}) %collective-permute-start.18) | collective-permute-done | bytes 262176 | tf_op jit(solution)/shard_map/ppermute | solution.py:253
  43.3 0.1 add_convert_fusion.6
  43.4 1.4 %collective-permute-start.19 = (bf16[64,2048]{1,0:T(8,128)(2,1)S(1)}, bf16[64,2048]{1,0:T(8,128)(2,1)S(1)}, u32[]{:S(2)}, u32[]{:S(2)}) collective-permute-start(bf16[64,2048]{1,0:T(8,128)(2,1)S(1)} %add_convert_fusion.6), channel_id=1, source_target_pairs={{0,4},{1,3},{4,8},{5,1},{8,12},{9,5},{12,14},{13,9},{14,10},{15,13... | collective-permute-start | bytes 786440 | tf_op jit(solution)/shard_map/ppermute | solution.py:262
  44.8 0.1 add_convert_fusion.5
  44.8 0.4 collective-permute-start.25
  45.3 2.0 %expert.9 = (bf16[64,2048]{1,0:T(8,128)(2,1)S(1)}, bf16[64,2048]{1,0:T(8,128)(2,1)S(1)}) custom-call(s32[1]{0:T(128)} %bitcast.own_ref, bf16[64,2176]{1,0:T(8,128)(2,1)S(1)} %copy-done, bf16[64,2176]{1,0:T(8,128)(2,1)S(1)} %collective-permute-done.3.refs_1_, bf16[1,2048,768]{2,1,0:T(8,128)(2,1)S(1)} %get-tuple-element.41.refs_4_.refs_2_, ...), custom_call_target="tpu_custom_call" | custom-call | flops 262144 | bytes 262144 | tf_op jit(solution)/shard_map/expert/pallas_call | solution.py:116
  47.3 0.4 collective-permute-start.23
  47.7 2.1 %collective-permute-done.19 = bf16[64,2048]{1,0:T(8,128)(2,1)S(1)} collective-permute-done((bf16[64,2048]{1,0:T(8,128)(2,1)S(1)}, bf16[64,2048]{1,0:T(8,128)(2,1)S(1)}, u32[]{:S(2)}, u32[]{:S(2)}) %collective-permute-start.19) | collective-permute-done | bytes 262176 | tf_op jit(solution)/shard_map/ppermute | solution.py:262
  49.8 0.1 add_convert_fusion.4
  49.9 1.4 %collective-permute-start.21 = (bf16[64,2048]{1,0:T(8,128)(2,1)S(1)}, bf16[64,2048]{1,0:T(8,128)(2,1)S(1)}, u32[]{:S(2)}, u32[]{:S(2)}) collective-permute-start(bf16[64,2048]{1,0:T(8,128)(2,1)S(1)} %add_convert_fusion.4), channel_id=1, source_target_pairs={{0,4},{1,3},{4,8},{5,1},{8,12},{9,5},{12,14},{13,9},{14,10},{15,13... | collective-permute-start | bytes 786440 | tf_op jit(solution)/shard_map/ppermute | solution.py:262
  51.3 1.3 %collective-permute-done.25 = bf16[64,2048]{1,0:T(8,128)(2,1)S(1)} collective-permute-done((bf16[64,2048]{1,0:T(8,128)(2,1)S(1)}, bf16[64,2048]{1,0:T(8,128)(2,1)S(1)}, u32[]{:S(2)}, u32[]{:S(2)}) %collective-permute-start.25) | collective-permute-done | bytes 262176 | tf_op jit(solution)/shard_map/ppermute | solution.py:262
  52.6 0.1 add_convert_fusion.2
  52.7 1.4 %collective-permute-start.26 = (bf16[64,2048]{1,0:T(8,128)(2,1)S(1)}, bf16[64,2048]{1,0:T(8,128)(2,1)S(1)}, u32[]{:S(2)}, u32[]{:S(2)}) collective-permute-start(bf16[64,2048]{1,0:T(8,128)(2,1)S(1)} %add_convert_fusion.2), channel_id=1, source_target_pairs={{0,4},{1,3},{4,8},{5,1},{8,12},{9,5},{12,14},{13,9},{14,10},{15,13... | collective-permute-start | bytes 786440 | tf_op jit(solution)/shard_map/ppermute | solution.py:262
  54.1 2.2 %collective-permute-done.21 = bf16[64,2048]{1,0:T(8,128)(2,1)S(1)} collective-permute-done((bf16[64,2048]{1,0:T(8,128)(2,1)S(1)}, bf16[64,2048]{1,0:T(8,128)(2,1)S(1)}, u32[]{:S(2)}, u32[]{:S(2)}) %collective-permute-start.21) | collective-permute-done | bytes 262176 | tf_op jit(solution)/shard_map/ppermute | solution.py:262
  56.3 0.1 add_convert_fusion.3
  56.4 0.1 collective-permute-start.22
  56.5 2.6 %collective-permute-done.26 = bf16[64,2048]{1,0:T(8,128)(2,1)S(1)} collective-permute-done((bf16[64,2048]{1,0:T(8,128)(2,1)S(1)}, bf16[64,2048]{1,0:T(8,128)(2,1)S(1)}, u32[]{:S(2)}, u32[]{:S(2)}) %collective-permute-start.26) | collective-permute-done | bytes 262176 | tf_op jit(solution)/shard_map/ppermute | solution.py:262
  59.1 0.1 add_convert_fusion.1
  59.2 1.4 %collective-permute-start.27 = (bf16[64,2048]{1,0:T(8,128)(2,1)S(1)}, bf16[64,2048]{1,0:T(8,128)(2,1)S(1)}, u32[]{:S(2)}, u32[]{:S(2)}) collective-permute-start(bf16[64,2048]{1,0:T(8,128)(2,1)S(1)} %add_convert_fusion.1), channel_id=1, source_target_pairs={{0,4},{1,3},{4,8},{5,1},{8,12},{9,5},{12,14},{13,9},{14,10},{15,13... | collective-permute-start | bytes 786440 | tf_op jit(solution)/shard_map/ppermute | solution.py:262
  60.6 1.7 %collective-permute-done.22 = bf16[64,2048]{1,0:T(8,128)(2,1)S(1)} collective-permute-done((bf16[64,2048]{1,0:T(8,128)(2,1)S(1)}, bf16[64,2048]{1,0:T(8,128)(2,1)S(1)}, u32[]{:S(2)}, u32[]{:S(2)}) %collective-permute-start.22) | collective-permute-done | bytes 262176 | tf_op jit(solution)/shard_map/ppermute | solution.py:262
  62.3 0.1 convert_add_fusion
  62.4 3.3 %collective-permute-done.27 = bf16[64,2048]{1,0:T(8,128)(2,1)S(1)} collective-permute-done((bf16[64,2048]{1,0:T(8,128)(2,1)S(1)}, bf16[64,2048]{1,0:T(8,128)(2,1)S(1)}, u32[]{:S(2)}, u32[]{:S(2)}) %collective-permute-start.27) | collective-permute-done | bytes 262176 | tf_op jit(solution)/shard_map/ppermute | solution.py:262
  65.7 0.8 %add_convert_fusion = bf16[64,2048]{1,0:T(8,128)(2,1)} fusion(f32[64,2048]{1,0:T(8,128)S(1)} %convert_add_fusion, bf16[64,2048]{1,0:T(8,128)(2,1)S(1)} %collective-permute-done.27), kind=kLoop, calls=%fused_computation.1 | loop fusion | flops 393216 | bytes 1048576 | tf_op jit(solution)/shard_map/convert_element_type | solution.py:210
  (12 shorter events, 0.1 us)
Async XLA Ops:
  1.7 9.4 %collective-permute-start = (bf16[64,2176]{1,0:T(8,128)(2,1)}, bf16[64,2176]{1,0:T(8,128)(2,1)S(1)}, u32[]{:S(2)}, u32[]{:S(2)}) collective-permute-start(bf16[64,2176]{1,0:T(8,128)(2,1)} %pack.1.refs_0_), channel_id=1, source_target_pairs={{0,4},{1,3},{4,8},{5,1},{8,12},{9,5},{12,14},{13,9},{14,10},{15,13... | collective-permute-start | bytes 835592 | tf_op jit(solution)/shard_map/ppermute | solution.py:229
  4.8 8.7 %collective-permute-start.4 = (bf16[64,2176]{1,0:T(8,128)(2,1)}, bf16[64,2176]{1,0:T(8,128)(2,1)S(1)}, u32[]{:S(2)}, u32[]{:S(2)}) collective-permute-start(bf16[64,2176]{1,0:T(8,128)(2,1)} %pack.1.refs_0_), channel_id=1, source_target_pairs={{0,3},{1,4},{4,1},{5,8},{8,5},{9,12},{12,9},{13,14},{14,13},{15,10... | collective-permute-start | bytes 835592 | tf_op jit(solution)/shard_map/ppermute | solution.py:229
  5.4 12.1 %collective-permute-start.3 = (bf16[64,2176]{1,0:T(8,128)(2,1)}, bf16[64,2176]{1,0:T(8,128)(2,1)S(1)}, u32[]{:S(2)}, u32[]{:S(2)}) collective-permute-start(bf16[64,2176]{1,0:T(8,128)(2,1)} %pack.1.refs_0_), channel_id=1, source_target_pairs={{0,1},{1,0},{2,3},{3,2},{4,5},{5,4},{6,7},{7,6},{8,9},{9,8},{10,11... | collective-permute-start | bytes 835592 | tf_op jit(solution)/shard_map/ppermute | solution.py:231
  11.2 7.8 %collective-permute-start.2 = (bf16[64,2176]{1,0:T(8,128)(2,1)S(1)}, bf16[64,2176]{1,0:T(8,128)(2,1)S(1)}, u32[]{:S(2)}, u32[]{:S(2)}) collective-permute-start(bf16[64,2176]{1,0:T(8,128)(2,1)S(1)} %collective-permute-done.refs_2_), channel_id=1, source_target_pairs={{0,4},{1,3},{4,8},{5,1},{8,12},{9,5},{12,14},{13,9},{14,10},{15,13... | collective-permute-start | bytes 835592 | tf_op jit(solution)/shard_map/ppermute | solution.py:239
  13.5 8.7 %collective-permute-start.5 = (bf16[64,2176]{1,0:T(8,128)(2,1)S(1)}, bf16[64,2176]{1,0:T(8,128)(2,1)S(1)}, u32[]{:S(2)}, u32[]{:S(2)}) collective-permute-start(bf16[64,2176]{1,0:T(8,128)(2,1)S(1)} %collective-permute-done.4.refs_3_), channel_id=1, source_target_pairs={{0,4},{1,3},{4,8},{5,1},{8,12},{9,5},{12,14},{13,9},{14,10},{15,13... | collective-permute-start | bytes 835592 | tf_op jit(solution)/shard_map/ppermute | solution.py:239
  15.1 10.3 %collective-permute-start.1 = (bf16[64,2176]{1,0:T(8,128)(2,1)S(1)}, bf16[64,2176]{1,0:T(8,128)(2,1)S(1)}, u32[]{:S(2)}, u32[]{:S(2)}) collective-permute-start(bf16[64,2176]{1,0:T(8,128)(2,1)S(1)} %collective-permute-done.refs_2_), channel_id=1, source_target_pairs={{0,1},{1,0},{2,3},{3,2},{4,5},{5,4},{6,7},{7,6},{8,9},{9,8},{10,11... | collective-permute-start | bytes 835592 | tf_op jit(solution)/shard_map/ppermute | solution.py:242
  17.0 5.8 %collective-permute-start.7 = (bf16[64,2176]{1,0:T(8,128)(2,1)S(1)}, bf16[64,2176]{1,0:T(8,128)(2,1)S(1)}, u32[]{:S(2)}, u32[]{:S(2)}) collective-permute-start(bf16[64,2176]{1,0:T(8,128)(2,1)S(1)} %collective-permute-done.4.refs_3_), channel_id=1, source_target_pairs={{0,1},{1,0},{2,3},{3,2},{4,5},{5,4},{6,7},{7,6},{8,9},{9,8},{10,11... | collective-permute-start | bytes 835592 | tf_op jit(solution)/shard_map/ppermute | solution.py:242
  18.9 11.8 %collective-permute-start.13 = (bf16[64,2176]{1,0:T(8,128)(2,1)S(1)}, bf16[64,2176]{1,0:T(8,128)(2,1)S(1)}, u32[]{:S(2)}, u32[]{:S(2)}) collective-permute-start(bf16[64,2176]{1,0:T(8,128)(2,1)S(1)} %collective-permute-done.2.refs_2_), channel_id=1, source_target_pairs={{0,8},{1,7},{4,12},{5,3},{8,14},{9,1},{12,10},{13,5},{14,6},{15,9}... | collective-permute-start | bytes 835592 | tf_op jit(solution)/shard_map/ppermute | solution.py:243
  22.3 3.1 %collective-permute-start.6 = (bf16[64,2176]{1,0:T(8,128)(2,1)S(1)}, bf16[64,2176]{1,0:T(8,128)(2,1)S(1)}, u32[]{:S(2)}, u32[]{:S(2)}) collective-permute-start(bf16[64,2176]{1,0:T(8,128)(2,1)S(1)} %collective-permute-done.2.refs_2_), channel_id=1, source_target_pairs={{0,1},{1,0},{2,3},{3,2},{4,5},{5,4},{6,7},{7,6},{8,9},{9,8},{10,11... | collective-permute-start | bytes 835592 | tf_op jit(solution)/shard_map/ppermute | solution.py:242
  22.3 3.1 %collective-permute-start.8 = (bf16[64,2176]{1,0:T(8,128)(2,1)S(1)}, bf16[64,2176]{1,0:T(8,128)(2,1)S(1)}, u32[]{:S(2)}, u32[]{:S(2)}) collective-permute-start(bf16[64,2176]{1,0:T(8,128)(2,1)S(1)} %collective-permute-done.5.refs_3_), channel_id=1, source_target_pairs={{0,1},{1,0},{2,3},{3,2},{4,5},{5,4},{6,7},{7,6},{8,9},{9,8},{10,11... | collective-permute-start | bytes 835592 | tf_op jit(solution)/shard_map/ppermute | solution.py:242
  22.8 12.5 %collective-permute-start.11 = (bf16[128,2176]{1,0:T(8,128)(2,1)S(1)}, bf16[128,2176]{1,0:T(8,128)(2,1)S(1)}, u32[]{:S(2)}, u32[]{:S(2)}) collective-permute-start(bf16[128,2176]{1,0:T(8,128)(2,1)S(1)} %pad_maximum_fusion), channel_id=1, source_target_pairs={{0,4},{1,3},{4,8},{5,1},{8,12},{9,5},{12,14},{13,9},{14,10},{15,13... | collective-permute-start | bytes 1671176 | tf_op jit(solution)/shard_map/ppermute | solution.py:244
  30.7 2.4 %collective-permute-start.14 = (bf16[64,2176]{1,0:T(8,128)(2,1)S(1)}, bf16[64,2176]{1,0:T(8,128)(2,1)S(1)}, u32[]{:S(2)}, u32[]{:S(2)}) collective-permute-start(bf16[64,2176]{1,0:T(8,128)(2,1)S(1)} %collective-permute-done.13.refs_1_), channel_id=1, source_target_pairs={{0,1},{1,0},{2,3},{3,2},{4,5},{5,4},{6,7},{7,6},{8,9},{9,8},{10,11... | collective-permute-start | bytes 835592 | tf_op jit(solution)/shard_map/ppermute | solution.py:250
  30.8 1.9 %collective-permute-start.10 = (bf16[64,2048]{1,0:T(8,128)(2,1)S(1)}, bf16[64,2048]{1,0:T(8,128)(2,1)S(1)}, u32[]{:S(2)}, u32[]{:S(2)}) collective-permute-start(bf16[64,2048]{1,0:T(8,128)(2,1)S(1)} %get-tuple-element.52), channel_id=1, source_target_pairs={{0,1},{1,0},{2,3},{3,2},{4,5},{5,4},{6,7},{7,6},{8,9},{9,8},{10,11... | collective-permute-start | bytes 786440 | tf_op jit(solution)/shard_map/ppermute | solution.py:245
  31.3 1.8 %collective-permute-start.15 = (bf16[64,2048]{1,0:T(8,128)(2,1)S(1)}, bf16[64,2048]{1,0:T(8,128)(2,1)S(1)}, u32[]{:S(2)}, u32[]{:S(2)}) collective-permute-start(bf16[64,2048]{1,0:T(8,128)(2,1)S(1)} %get-tuple-element.54), channel_id=1, source_target_pairs={{0,1},{1,0},{2,3},{3,2},{4,5},{5,4},{6,7},{7,6},{8,9},{9,8},{10,11... | collective-permute-start | bytes 786440 | tf_op jit(solution)/shard_map/ppermute | solution.py:245
  35.2 1.6 %collective-permute-start.16 = (bf16[64,2048]{1,0:T(8,128)(2,1)S(1)}, bf16[64,2048]{1,0:T(8,128)(2,1)S(1)}, u32[]{:S(2)}, u32[]{:S(2)}) collective-permute-start(bf16[64,2048]{1,0:T(8,128)(2,1)S(1)} %get-tuple-element.57), channel_id=1, source_target_pairs={{0,1},{1,0},{2,3},{3,2},{4,5},{5,4},{6,7},{7,6},{8,9},{9,8},{10,11... | collective-permute-start | bytes 786440 | tf_op jit(solution)/shard_map/ppermute | solution.py:251
  35.4 2.9 %collective-permute-start.12 = (bf16[128,2176]{1,0:T(8,128)(2,1)S(1)}, bf16[128,2176]{1,0:T(8,128)(2,1)S(1)}, u32[]{:S(2)}, u32[]{:S(2)}) collective-permute-start(bf16[128,2176]{1,0:T(8,128)(2,1)S(1)} %collective-permute-done.11.refs_1_), channel_id=1, source_target_pairs={{0,1},{1,0},{2,3},{3,2},{4,5},{5,4},{6,7},{7,6},{8,9},{9,8},{10,11... | collective-permute-start | bytes 1671176 | tf_op jit(solution)/shard_map/ppermute | solution.py:252
  36.8 8.4 %copy-start = (bf16[64,2176]{1,0:T(8,128)(2,1)S(1)}, bf16[64,2176]{1,0:T(8,128)(2,1)}, u32[]{:S(2)}) copy-start(bf16[64,2176]{1,0:T(8,128)(2,1)} %pack.1.refs_0_) | copy-start | bytes 835588
  36.8 6.4 %collective-permute-start.18 = (bf16[64,2048]{1,0:T(8,128)(2,1)S(1)}, bf16[64,2048]{1,0:T(8,128)(2,1)S(1)}, u32[]{:S(2)}, u32[]{:S(2)}) collective-permute-start(bf16[64,2048]{1,0:T(8,128)(2,1)S(1)} %add_convert_fusion.7), channel_id=1, source_target_pairs={{0,4},{1,3},{4,8},{5,1},{8,12},{9,5},{12,14},{13,9},{14,10},{15,13... | collective-permute-start | bytes 786440 | tf_op jit(solution)/shard_map/ppermute | solution.py:253
  40.9 2.4 %collective-permute-start.17 = (bf16[64,2048]{1,0:T(8,128)(2,1)S(1)}, bf16[64,2048]{1,0:T(8,128)(2,1)S(1)}, u32[]{:S(2)}, u32[]{:S(2)}) collective-permute-start(bf16[64,2048]{1,0:T(8,128)(2,1)S(1)} %get-tuple-element.60), channel_id=1, source_target_pairs={{0,1},{1,0},{2,3},{3,2},{4,5},{5,4},{6,7},{7,6},{8,9},{9,8},{10,11... | collective-permute-start | bytes 786440 | tf_op jit(solution)/shard_map/ppermute | solution.py:245
  41.0 13.1 %collective-permute-start.9 = (bf16[64,2048]{1,0:T(8,128)(2,1)S(1)}, bf16[64,2048]{1,0:T(8,128)(2,1)S(1)}, u32[]{:S(2)}, u32[]{:S(2)}) collective-permute-start(bf16[64,2048]{1,0:T(8,128)(2,1)S(1)} %get-tuple-element.51), channel_id=1, source_target_pairs={{0,1},{1,0},{2,3},{3,2},{4,5},{5,4},{6,7},{7,6},{8,9},{9,8},{10,11... | collective-permute-start | bytes 786440 | tf_op jit(solution)/shard_map/ppermute | solution.py:245
  41.5 15.0 %collective-permute-start.24 = (bf16[64,2048]{1,0:T(8,128)(2,1)S(1)}, bf16[64,2048]{1,0:T(8,128)(2,1)S(1)}, u32[]{:S(2)}, u32[]{:S(2)}) collective-permute-start(bf16[64,2048]{1,0:T(8,128)(2,1)S(1)} %get-tuple-element.70), channel_id=1, source_target_pairs={{0,1},{1,0},{2,3},{3,2},{4,5},{5,4},{6,7},{7,6},{8,9},{9,8},{10,11... | collective-permute-start | bytes 786440 | tf_op jit(solution)/shard_map/ppermute | solution.py:245
  41.5 3.2 %collective-permute-start.20 = (bf16[64,2048]{1,0:T(8,128)(2,1)S(1)}, bf16[64,2048]{1,0:T(8,128)(2,1)S(1)}, u32[]{:S(2)}, u32[]{:S(2)}) collective-permute-start(bf16[64,2048]{1,0:T(8,128)(2,1)S(1)} %get-tuple-element.63), channel_id=1, source_target_pairs={{0,1},{1,0},{2,3},{3,2},{4,5},{5,4},{6,7},{7,6},{8,9},{9,8},{10,11... | collective-permute-start | bytes 786440 | tf_op jit(solution)/shard_map/ppermute | solution.py:245
  43.4 6.4 %collective-permute-start.19 = (bf16[64,2048]{1,0:T(8,128)(2,1)S(1)}, bf16[64,2048]{1,0:T(8,128)(2,1)S(1)}, u32[]{:S(2)}, u32[]{:S(2)}) collective-permute-start(bf16[64,2048]{1,0:T(8,128)(2,1)S(1)} %add_convert_fusion.6), channel_id=1, source_target_pairs={{0,4},{1,3},{4,8},{5,1},{8,12},{9,5},{12,14},{13,9},{14,10},{15,13... | collective-permute-start | bytes 786440 | tf_op jit(solution)/shard_map/ppermute | solution.py:262
  44.8 7.8 %collective-permute-start.25 = (bf16[64,2048]{1,0:T(8,128)(2,1)S(1)}, bf16[64,2048]{1,0:T(8,128)(2,1)S(1)}, u32[]{:S(2)}, u32[]{:S(2)}) collective-permute-start(bf16[64,2048]{1,0:T(8,128)(2,1)S(1)} %add_convert_fusion.5), channel_id=1, source_target_pairs={{0,4},{1,3},{4,8},{5,1},{8,12},{9,5},{12,14},{13,9},{14,10},{15,13... | collective-permute-start | bytes 786440 | tf_op jit(solution)/shard_map/ppermute | solution.py:262
  47.3 13.3 %collective-permute-start.23 = (bf16[64,2048]{1,0:T(8,128)(2,1)S(1)}, bf16[64,2048]{1,0:T(8,128)(2,1)S(1)}, u32[]{:S(2)}, u32[]{:S(2)}) collective-permute-start(bf16[64,2048]{1,0:T(8,128)(2,1)S(1)} %get-tuple-element.67), channel_id=1, source_target_pairs={{0,1},{1,0},{2,3},{3,2},{4,5},{5,4},{6,7},{7,6},{8,9},{9,8},{10,11... | collective-permute-start | bytes 786440 | tf_op jit(solution)/shard_map/ppermute | solution.py:263
  49.9 6.4 %collective-permute-start.21 = (bf16[64,2048]{1,0:T(8,128)(2,1)S(1)}, bf16[64,2048]{1,0:T(8,128)(2,1)S(1)}, u32[]{:S(2)}, u32[]{:S(2)}) collective-permute-start(bf16[64,2048]{1,0:T(8,128)(2,1)S(1)} %add_convert_fusion.4), channel_id=1, source_target_pairs={{0,4},{1,3},{4,8},{5,1},{8,12},{9,5},{12,14},{13,9},{14,10},{15,13... | collective-permute-start | bytes 786440 | tf_op jit(solution)/shard_map/ppermute | solution.py:262
  52.7 6.4 %collective-permute-start.26 = (bf16[64,2048]{1,0:T(8,128)(2,1)S(1)}, bf16[64,2048]{1,0:T(8,128)(2,1)S(1)}, u32[]{:S(2)}, u32[]{:S(2)}) collective-permute-start(bf16[64,2048]{1,0:T(8,128)(2,1)S(1)} %add_convert_fusion.2), channel_id=1, source_target_pairs={{0,4},{1,3},{4,8},{5,1},{8,12},{9,5},{12,14},{13,9},{14,10},{15,13... | collective-permute-start | bytes 786440 | tf_op jit(solution)/shard_map/ppermute | solution.py:262
  56.4 5.9 %collective-permute-start.22 = (bf16[64,2048]{1,0:T(8,128)(2,1)S(1)}, bf16[64,2048]{1,0:T(8,128)(2,1)S(1)}, u32[]{:S(2)}, u32[]{:S(2)}) collective-permute-start(bf16[64,2048]{1,0:T(8,128)(2,1)S(1)} %add_convert_fusion.3), channel_id=1, source_target_pairs={{0,5},{1,2},{4,9},{5,0},{8,13},{9,4},{12,15},{13,8},{14,11},{15,12... | collective-permute-start | bytes 786440 | tf_op jit(solution)/shard_map/ppermute | solution.py:262
  59.2 6.4 %collective-permute-start.27 = (bf16[64,2048]{1,0:T(8,128)(2,1)S(1)}, bf16[64,2048]{1,0:T(8,128)(2,1)S(1)}, u32[]{:S(2)}, u32[]{:S(2)}) collective-permute-start(bf16[64,2048]{1,0:T(8,128)(2,1)S(1)} %add_convert_fusion.1), channel_id=1, source_target_pairs={{0,4},{1,3},{4,8},{5,1},{8,12},{9,5},{12,14},{13,9},{14,10},{15,13... | collective-permute-start | bytes 786440 | tf_op jit(solution)/shard_map/ppermute | solution.py:262

commit v13 on v12

--- a/solution.py
+++ b/solution.py
@@ -220,15 +220,14 @@
     rounds = experts // 4
     swap = functools.partial(lax.ppermute, axis_name="expert", perm=swap_pairs(experts))
     ring = functools.partial(lax.ppermute, axis_name="expert", perm=ring_pairs(experts, 1))
-    pass_on = functools.partial(lax.ppermute, axis_name="expert", perm=ring_pairs(experts, -1, 1))
     home = functools.partial(lax.ppermute, axis_name="expert", perm=ring_pairs(experts, 1, 1))
     leap = functools.partial(lax.ppermute, axis_name="expert", perm=ring_pairs(experts, 2))
     own = lax.axis_index("expert").reshape(1)
 
     mine = pack(after(tokens, own), expert_ids, router_weights, experts)
-    first, second = ring(mine), pass_on(mine)
-    gate_w, up_w = load_weights((after(w_gate, mine), w_up))
     sibling = swap(mine)
+    first, second = ring(mine), ring(sibling)
+    gate_w, up_w = load_weights((after(w_gate, sibling), w_up))
     first = after(first, gate_w)
     down_w, = load_weights((after(w_down, first),))
     weights = [gate_w, up_w, down_w]
@@ -238,8 +237,8 @@
         if step > 1:
             first, second = ring(first), ring(second)
         if step == 2:
-            first = after(first, down_w, sibling)
-        blocks[step] = (swap(after(first, second) if step == 2 else first), swap(second), first, second)
+            first = after(first, down_w)
+        blocks[step] = (swap(first), swap(second), first, second)
     far = leap(first)
     both = ring(jnp.concatenate([first, second], 0))
     turned = lambda keep, keep_trail, send, send_trail: (keep_trail, keep, swap(send_trail), swap(send))

time: 66.6 us -> 62.7 us (0.941)
  waiting for transfers between devices: 21.6 us -> 15.8 us
  starting transfers between devices: 24.6 us -> 26.5 us
    ppermute x2, waiting for transfers between devices: 2.56 us -> 0.01 us  [dense_body(): first, second = (ring(first), ring(second))]
    ppermute x6, starting transfers between devices: 6.02 us -> 8.56 us  [dense_body(): lead, trail = ([(ring if step > 1 else home)(lead[0])], [ring(trail[0])])]
    ppermute x6, waiting for transfers between devices: 13.2 us -> 11 us  [dense_body(): lead, trail = ([(ring if step > 1 else home)(lead[0])], [ring(trail[0])])]
    ppermute x1, starting transfers between devices: 2.53 us -> 1.63 us  [dense_body(): both = ring(jnp.concatenate([first, second], 0))]
    ppermute x6, waiting for transfers between devices: 1.82 us -> 1.12 us  [the longest x2 0.96 us: dense_body(): first, second = (ring(mine), ring(sibling))]
  transfers between devices with their start and end apart: 28 -> 28, of which waited for: 13 -> 13; matrix products, arithmetic and copies ran while one was open for 1% -> 1% of each run, Pallas kernels for 25% -> 27%
where the time goes in v13:
time: 62.7 us; the launch traced here: 62.6 us
  starting transfers between devices  26.5 us (42%)
  Pallas kernels  18.5 us (30%)
  waiting for transfers between devices  15.8 us (25%)
  other arithmetic  1.53 us (2%)
    pallas_call x5, Pallas kernels, run_expert(): pl.pallas_call(functools.partial(expert_kernel, experts, len(blocks)), ou...  12.1 us
    ppermute x6, waiting for transfers between devices, dense_body(): lead, trail = ([(ring if step > 1 else home)(lead[0])], [ring(trail[0])])  11 us
    ppermute x6, starting transfers between devices, dense_body(): lead, trail = ([(ring if step > 1 else home)(lead[0])], [ring(trail[0])])  8.56 us
    pallas_call x2, Pallas kernels, load_weights(): pl.pallas_call(functools.partial(load_kernel, pieces), out_shape=[pltpu.V...  4.73 us
    ppermute x2, starting transfers between devices, dense_body(): first, second = (ring(mine), ring(sibling))  4.34 us
    ppermute x2, starting transfers between devices, dense_body(): first, second = (ring(first), ring(second))  4.21 us
    ppermute x1, starting transfers between devices, dense_body(): far = leap(first)  2.68 us
    pallas_call x1, Pallas kernels, pack(): pl.pallas_call(functools.partial(pack_kernel, experts), out_shape=jax.Sha...  1.7 us
  transfers between devices with their start and end apart: 28, of which 13 were waited for; matrix products, arithmetic and copies ran while one was open for 1% of the time, Pallas kernels for 27%

profile of v13, /device:TPU:0, one launch (start us, length us, event | category | flops | bytes accessed | tf_op | source)
XLA Modules:
  0.0 62.6 jit_solution(1568442338268532712)
XLA Ops:
  0.0 1.7 %pack.1.refs_0_ = bf16[64,2176]{1,0:T(8,128)(2,1)} custom-call(bf16[64,2048]{1,0:T(8,128)(2,1)} %tokens_ref, s32[8,64]{1,0:T(8,128)} %bitcast.3, f32[8,64]{1,0:T(8,128)} %bitcast.4), custom_call_target="tpu_custom_call" | custom-call | bytes 1024 | tf_op jit(solution)/shard_map/pack/pallas_call | solution.py:191
  1.7 0.5 collective-permute-start.1
  2.2 2.6 %collective-permute-start = (bf16[64,2176]{1,0:T(8,128)(2,1)}, bf16[64,2176]{1,0:T(8,128)(2,1)S(1)}, u32[]{:S(2)}, u32[]{:S(2)}) collective-permute-start(bf16[64,2176]{1,0:T(8,128)(2,1)} %pack.1.refs_0_), channel_id=1, source_target_pairs={{0,4},{1,3},{4,8},{5,1},{8,12},{9,5},{12,14},{13,9},{14,10},{15,13... | collective-permute-start | bytes 835592 | tf_op jit(solution)/shard_map/ppermute | solution.py:229
  4.9 1.7 %collective-permute-start.5 = (bf16[64,2176]{1,0:T(8,128)(2,1)S(1)}, bf16[64,2176]{1,0:T(8,128)(2,1)S(1)}, u32[]{:S(2)}, u32[]{:S(2)}) collective-permute-start(bf16[64,2176]{1,0:T(8,128)(2,1)S(1)} %collective-permute-done.1.refs_1_), channel_id=1, source_target_pairs={{0,4},{1,3},{4,8},{5,1},{8,12},{9,5},{12,14},{13,9},{14,10},{15,13... | collective-permute-start | bytes 835592 | tf_op jit(solution)/shard_map/ppermute | solution.py:229
  6.6 2.9 %load.2 = (bf16[1,2048,768]{2,1,0:T(8,128)(2,1)S(1)}, bf16[1,2048,768]{2,1,0:T(8,128)(2,1)S(1)}) custom-call(bf16[1,2048,768]{2,1,0:T(8,128)(2,1)} %refs_0_, bf16[1,2048,768]{2,1,0:T(8,128)(2,1)} %refs_1_.1), custom_call_target="tpu_custom_call" | custom-call | bytes 1024 | tf_op jit(solution)/shard_map/load/pallas_call | solution.py:149
  9.4 0.1 collective-permute-done.refs_2_
  9.5 2.1 %collective-permute-start.3 = (bf16[64,2176]{1,0:T(8,128)(2,1)S(1)}, bf16[64,2176]{1,0:T(8,128)(2,1)S(1)}, u32[]{:S(2)}, u32[]{:S(2)}) collective-permute-start(bf16[64,2176]{1,0:T(8,128)(2,1)S(1)} %collective-permute-done.refs_2_), channel_id=1, source_target_pairs={{0,4},{1,3},{4,8},{5,1},{8,12},{9,5},{12,14},{13,9},{14,10},{15,13... | collective-permute-start | bytes 835592 | tf_op jit(solution)/shard_map/ppermute | solution.py:238
  11.6 0.9 %collective-permute-done.5.refs_3_ = bf16[64,2176]{1,0:T(8,128)(2,1)S(1)} collective-permute-done((bf16[64,2176]{1,0:T(8,128)(2,1)S(1)}, bf16[64,2176]{1,0:T(8,128)(2,1)S(1)}, u32[]{:S(2)}, u32[]{:S(2)}) %collective-permute-start.5) | collective-permute-done | bytes 278560 | tf_op jit(solution)/shard_map/ppermute | solution.py:229
  12.5 2.1 %collective-permute-start.7 = (bf16[64,2176]{1,0:T(8,128)(2,1)S(1)}, bf16[64,2176]{1,0:T(8,128)(2,1)S(1)}, u32[]{:S(2)}, u32[]{:S(2)}) collective-permute-start(bf16[64,2176]{1,0:T(8,128)(2,1)S(1)} %collective-permute-done.5.refs_3_), channel_id=1, source_target_pairs={{0,4},{1,3},{4,8},{5,1},{8,12},{9,5},{12,14},{13,9},{14,10},{15,13... | collective-permute-start | bytes 835592 | tf_op jit(solution)/shard_map/ppermute | solution.py:238
  14.6 1.9 %load.3.refs_6_.refs_4_ = bf16[1,2048,768]{2,1,0:T(8,128)(2,1)S(1)} custom-call(bf16[1,2048,768]{2,1,0:T(8,128)(2,1)} %refs_0_.1), custom_call_target="tpu_custom_call" | custom-call | bytes 1024 | tf_op jit(solution)/shard_map/load/pallas_call | solution.py:149
  16.5 0.0 collective-permute-done.3.refs_2_
  16.5 2.7 %collective-permute-start.13 = (bf16[64,2176]{1,0:T(8,128)(2,1)S(1)}, bf16[64,2176]{1,0:T(8,128)(2,1)S(1)}, u32[]{:S(2)}, u32[]{:S(2)}) collective-permute-start(bf16[64,2176]{1,0:T(8,128)(2,1)S(1)} %collective-permute-done.3.refs_2_), channel_id=1, source_target_pairs={{0,8},{1,7},{4,12},{5,3},{8,14},{9,1},{12,10},{13,5},{14,6},{15,9}... | collective-permute-start | bytes 835592 | tf_op jit(solution)/shard_map/ppermute | solution.py:242
  19.2 0.0 collective-permute-start.4
  19.2 0.5 collective-permute-start.6
  19.7 0.0 collective-permute-start.8
  19.7 0.0 collective-permute-done.2.refs_0_
  19.8 1.6 %collective-permute-start.11 = (bf16[128,2176]{1,0:T(8,128)(2,1)S(1)}, bf16[128,2176]{1,0:T(8,128)(2,1)S(1)}, u32[]{:S(2)}, u32[]{:S(2)}) collective-permute-start(bf16[128,2176]{1,0:T(8,128)(2,1)S(1)} %pad_maximum_fusion), channel_id=1, source_target_pairs={{0,4},{1,3},{4,8},{5,1},{8,12},{9,5},{12,14},{13,9},{14,10},{15,13... | collective-permute-start | bytes 1671176 | tf_op jit(solution)/shard_map/ppermute | solution.py:243
  21.4 0.0 collective-permute-done.6.refs_1_
  21.4 0.1 collective-permute-done.8.refs_1_
  21.5 2.6 %expert.5 = (bf16[64,2048]{1,0:T(8,128)(2,1)S(1)}, bf16[64,2048]{1,0:T(8,128)(2,1)S(1)}, bf16[64,2048]{1,0:T(8,128)(2,1)S(1)}, bf16[64,2048]{1,0:T(8,128)(2,1)S(1)}) custom-call(s32[1]{0:T(128)} %bitcast.own_ref, bf16[64,2176]{1,0:T(8,128)(2,1)S(1)} %collective-permute-done.4.refs_0_, bf16[64,2176]{1,0:T(8,128)(2,1)S(1)} %collective-permute-done.8.refs_1_, ...), custom_call_target="tpu_custom_call" | custom-call | flops 524288 | bytes 524288 | tf_op jit(solution)/shard_map/expert/pallas_call | solution.py:116
  24.2 2.7 %expert.6 = (bf16[64,2048]{1,0:T(8,128)(2,1)S(1)}, bf16[64,2048]{1,0:T(8,128)(2,1)S(1)}, bf16[64,2048]{1,0:T(8,128)(2,1)S(1)}, bf16[64,2048]{1,0:T(8,128)(2,1)S(1)}) custom-call(s32[1]{0:T(128)} %bitcast.own_ref, bf16[64,2176]{1,0:T(8,128)(2,1)S(1)} %collective-permute-done.2.refs_0_, bf16[64,2176]{1,0:T(8,128)(2,1)S(1)} %collective-permute-done.6.refs_1_, ...), custom_call_target="tpu_custom_call" | custom-call | flops 524288 | bytes 524288 | tf_op jit(solution)/shard_map/expert/pallas_call | solution.py:116
  26.9 0.0 collective-permute-done.13.refs_1_
  26.9 0.2 collective-permute-start.14
  27.1 0.4 collective-permute-start.10
  27.4 0.1 collective-permute-start.15
  27.6 1.3 %collective-permute-done.10 = bf16[64,2048]{1,0:T(8,128)(2,1)S(1)} collective-permute-done((bf16[64,2048]{1,0:T(8,128)(2,1)S(1)}, bf16[64,2048]{1,0:T(8,128)(2,1)S(1)}, u32[]{:S(2)}, u32[]{:S(2)}) %collective-permute-start.10) | collective-permute-done | bytes 262176 | tf_op jit(solution)/shard_map/ppermute | solution.py:244
  28.9 0.4 collective-permute-done.15
  29.2 0.0 collective-permute-done.14.refs_0_
  29.2 2.0 %expert.7 = (bf16[64,2048]{1,0:T(8,128)(2,1)S(1)}, bf16[64,2048]{1,0:T(8,128)(2,1)S(1)}) custom-call(s32[1]{0:T(128)} %bitcast.own_ref, bf16[64,2176]{1,0:T(8,128)(2,1)S(1)} %collective-permute-done.14.refs_0_, bf16[64,2176]{1,0:T(8,128)(2,1)S(1)} %collective-permute-done.13.refs_1_, bf16[1,2048,768]{2,1,0:T(8,128)(2,1)S(1)} %get-tuple-element.40.refs_4_.refs_2_, ...), custom_call_target="tpu_custom_call" | custom-call | flops 262144 | bytes 262144 | tf_op jit(solution)/shard_map/expert/pallas_call | solution.py:116
  31.3 0.2 collective-permute-start.16
  31.5 0.0 collective-permute-done.11.refs_1_
  31.5 0.4 collective-permute-start.12
  31.9 1.0 %collective-permute-done.16 = bf16[64,2048]{1,0:T(8,128)(2,1)S(1)} collective-permute-done((bf16[64,2048]{1,0:T(8,128)(2,1)S(1)}, bf16[64,2048]{1,0:T(8,128)(2,1)S(1)}, u32[]{:S(2)}, u32[]{:S(2)}) %collective-permute-start.16) | collective-permute-done | bytes 262176 | tf_op jit(solution)/shard_map/ppermute | solution.py:250
  32.9 0.1 add_convert_fusion.7
  33.0 1.7 %collective-permute-start.18 = (bf16[64,2048]{1,0:T(8,128)(2,1)S(1)}, bf16[64,2048]{1,0:T(8,128)(2,1)S(1)}, u32[]{:S(2)}, u32[]{:S(2)}) collective-permute-start(bf16[64,2048]{1,0:T(8,128)(2,1)S(1)} %add_convert_fusion.7), channel_id=1, source_target_pairs={{0,4},{1,3},{4,8},{5,1},{8,12},{9,5},{12,14},{13,9},{14,10},{15,13... | collective-permute-start | bytes 786440 | tf_op jit(solution)/shard_map/ppermute | solution.py:252
  34.6 2.7 %expert.8 = (bf16[64,2048]{1,0:T(8,128)(2,1)S(1)}, bf16[64,2048]{1,0:T(8,128)(2,1)S(1)}, bf16[64,2048]{1,0:T(8,128)(2,1)S(1)}, bf16[64,2048]{1,0:T(8,128)(2,1)S(1)}) custom-call(s32[1]{0:T(128)} %bitcast.own_ref, bf16[128,2176]{1,0:T(8,128)(2,1)S(1)} %collective-permute-done.12.refs_0_, bf16[128,2176]{1,0:T(8,128)(2,1)S(1)} %collective-permute-done.11.refs_1_, ...), custom_call_target="tpu_custom_call" | custom-call | flops 524288 | bytes 524288 | tf_op jit(solution)/shard_map/expert/pallas_call | solution.py:116
  37.3 0.1 collective-permute-start.17
  37.4 0.5 collective-permute-start.9
  37.9 0.1 collective-permute-start.24
  38.0 0.4 collective-permute-start.20
  38.4 1.0 %collective-permute-done.18 = bf16[64,2048]{1,0:T(8,128)(2,1)S(1)} collective-permute-done((bf16[64,2048]{1,0:T(8,128)(2,1)S(1)}, bf16[64,2048]{1,0:T(8,128)(2,1)S(1)}, u32[]{:S(2)}, u32[]{:S(2)}) %collective-permute-start.18) | collective-permute-done | bytes 262176 | tf_op jit(solution)/shard_map/ppermute | solution.py:252
  39.4 0.0 collective-permute-done.17
  39.4 0.1 add_convert_fusion.6
  39.5 1.7 %collective-permute-start.19 = (bf16[64,2048]{1,0:T(8,128)(2,1)S(1)}, bf16[64,2048]{1,0:T(8,128)(2,1)S(1)}, u32[]{:S(2)}, u32[]{:S(2)}) collective-permute-start(bf16[64,2048]{1,0:T(8,128)(2,1)S(1)} %add_convert_fusion.6), channel_id=1, source_target_pairs={{0,4},{1,3},{4,8},{5,1},{8,12},{9,5},{12,14},{13,9},{14,10},{15,13... | collective-permute-start | bytes 786440 | tf_op jit(solution)/shard_map/ppermute | solution.py:261
  41.2 0.1 add_convert_fusion.5
  41.2 1.8 %collective-permute-start.25 = (bf16[64,2048]{1,0:T(8,128)(2,1)S(1)}, bf16[64,2048]{1,0:T(8,128)(2,1)S(1)}, u32[]{:S(2)}, u32[]{:S(2)}) collective-permute-start(bf16[64,2048]{1,0:T(8,128)(2,1)S(1)} %add_convert_fusion.5), channel_id=1, source_target_pairs={{0,4},{1,3},{4,8},{5,1},{8,12},{9,5},{12,14},{13,9},{14,10},{15,13... | collective-permute-start | bytes 786440 | tf_op jit(solution)/shard_map/ppermute | solution.py:261
  43.1 2.0 %expert.9 = (bf16[64,2048]{1,0:T(8,128)(2,1)S(1)}, bf16[64,2048]{1,0:T(8,128)(2,1)S(1)}) custom-call(s32[1]{0:T(128)} %bitcast.own_ref, bf16[64,2176]{1,0:T(8,128)(2,1)S(1)} %copy-done, bf16[64,2176]{1,0:T(8,128)(2,1)S(1)} %collective-permute-done.1.refs_1_, bf16[1,2048,768]{2,1,0:T(8,128)(2,1)S(1)} %get-tuple-element.40.refs_4_.refs_2_, ...), custom_call_target="tpu_custom_call" | custom-call | flops 262144 | bytes 262144 | tf_op jit(solution)/shard_map/expert/pallas_call | solution.py:116
  45.1 0.1 collective-permute-start.23
  45.2 0.7 %collective-permute-done.19 = bf16[64,2048]{1,0:T(8,128)(2,1)S(1)} collective-permute-done((bf16[64,2048]{1,0:T(8,128)(2,1)S(1)}, bf16[64,2048]{1,0:T(8,128)(2,1)S(1)}, u32[]{:S(2)}, u32[]{:S(2)}) %collective-permute-start.19) | collective-permute-done | bytes 262176 | tf_op jit(solution)/shard_map/ppermute | solution.py:261
  45.9 0.1 add_convert_fusion.4
  46.0 1.7 %collective-permute-start.21 = (bf16[64,2048]{1,0:T(8,128)(2,1)S(1)}, bf16[64,2048]{1,0:T(8,128)(2,1)S(1)}, u32[]{:S(2)}, u32[]{:S(2)}) collective-permute-start(bf16[64,2048]{1,0:T(8,128)(2,1)S(1)} %add_convert_fusion.4), channel_id=1, source_target_pairs={{0,4},{1,3},{4,8},{5,1},{8,12},{9,5},{12,14},{13,9},{14,10},{15,13... | collective-permute-start | bytes 786440 | tf_op jit(solution)/shard_map/ppermute | solution.py:261
  47.7 1.1 %collective-permute-done.25 = bf16[64,2048]{1,0:T(8,128)(2,1)S(1)} collective-permute-done((bf16[64,2048]{1,0:T(8,128)(2,1)S(1)}, bf16[64,2048]{1,0:T(8,128)(2,1)S(1)}, u32[]{:S(2)}, u32[]{:S(2)}) %collective-permute-start.25) | collective-permute-done | bytes 262176 | tf_op jit(solution)/shard_map/ppermute | solution.py:261
  48.7 0.1 add_convert_fusion.2
  48.9 1.7 %collective-permute-start.26 = (bf16[64,2048]{1,0:T(8,128)(2,1)S(1)}, bf16[64,2048]{1,0:T(8,128)(2,1)S(1)}, u32[]{:S(2)}, u32[]{:S(2)}) collective-permute-start(bf16[64,2048]{1,0:T(8,128)(2,1)S(1)} %add_convert_fusion.2), channel_id=1, source_target_pairs={{0,4},{1,3},{4,8},{5,1},{8,12},{9,5},{12,14},{13,9},{14,10},{15,13... | collective-permute-start | bytes 786440 | tf_op jit(solution)/shard_map/ppermute | solution.py:261
  50.5 2.0 %collective-permute-done.21 = bf16[64,2048]{1,0:T(8,128)(2,1)S(1)} collective-permute-done((bf16[64,2048]{1,0:T(8,128)(2,1)S(1)}, bf16[64,2048]{1,0:T(8,128)(2,1)S(1)}, u32[]{:S(2)}, u32[]{:S(2)}) %collective-permute-start.21) | collective-permute-done | bytes 262176 | tf_op jit(solution)/shard_map/ppermute | solution.py:261
  52.5 0.1 add_convert_fusion.3
  52.6 0.1 collective-permute-start.22
  52.7 2.6 %collective-permute-done.26 = bf16[64,2048]{1,0:T(8,128)(2,1)S(1)} collective-permute-done((bf16[64,2048]{1,0:T(8,128)(2,1)S(1)}, bf16[64,2048]{1,0:T(8,128)(2,1)S(1)}, u32[]{:S(2)}, u32[]{:S(2)}) %collective-permute-start.26) | collective-permute-done | bytes 262176 | tf_op jit(solution)/shard_map/ppermute | solution.py:261
  55.3 0.1 add_convert_fusion.1
  55.4 1.7 %collective-permute-start.27 = (bf16[64,2048]{1,0:T(8,128)(2,1)S(1)}, bf16[64,2048]{1,0:T(8,128)(2,1)S(1)}, u32[]{:S(2)}, u32[]{:S(2)}) collective-permute-start(bf16[64,2048]{1,0:T(8,128)(2,1)S(1)} %add_convert_fusion.1), channel_id=1, source_target_pairs={{0,4},{1,3},{4,8},{5,1},{8,12},{9,5},{12,14},{13,9},{14,10},{15,13... | collective-permute-start | bytes 786440 | tf_op jit(solution)/shard_map/ppermute | solution.py:261
  57.0 1.4 %collective-permute-done.22 = bf16[64,2048]{1,0:T(8,128)(2,1)S(1)} collective-permute-done((bf16[64,2048]{1,0:T(8,128)(2,1)S(1)}, bf16[64,2048]{1,0:T(8,128)(2,1)S(1)}, u32[]{:S(2)}, u32[]{:S(2)}) %collective-permute-start.22) | collective-permute-done | bytes 262176 | tf_op jit(solution)/shard_map/ppermute | solution.py:261
  58.4 0.1 convert_add_fusion
  58.5 3.3 %collective-permute-done.27 = bf16[64,2048]{1,0:T(8,128)(2,1)S(1)} collective-permute-done((bf16[64,2048]{1,0:T(8,128)(2,1)S(1)}, bf16[64,2048]{1,0:T(8,128)(2,1)S(1)}, u32[]{:S(2)}, u32[]{:S(2)}) %collective-permute-start.27) | collective-permute-done | bytes 262176 | tf_op jit(solution)/shard_map/ppermute | solution.py:261
  61.8 0.8 %add_convert_fusion = bf16[64,2048]{1,0:T(8,128)(2,1)} fusion(f32[64,2048]{1,0:T(8,128)S(1)} %convert_add_fusion, bf16[64,2048]{1,0:T(8,128)(2,1)S(1)} %collective-permute-done.27), kind=kLoop, calls=%fused_computation.1 | loop fusion | flops 393216 | bytes 1048576 | tf_op jit(solution)/shard_map/convert_element_type | solution.py:210
  (12 shorter events, 0.1 us)
Async XLA Ops:
  1.7 3.2 %collective-permute-start.1 = (bf16[64,2176]{1,0:T(8,128)(2,1)}, bf16[64,2176]{1,0:T(8,128)(2,1)S(1)}, u32[]{:S(2)}, u32[]{:S(2)}) collective-permute-start(bf16[64,2176]{1,0:T(8,128)(2,1)} %pack.1.refs_0_), channel_id=1, source_target_pairs={{0,1},{1,0},{2,3},{3,2},{4,5},{5,4},{6,7},{7,6},{8,9},{9,8},{10,11... | collective-permute-start | bytes 835592 | tf_op jit(solution)/shard_map/ppermute | solution.py:228
  2.2 7.3 %collective-permute-start = (bf16[64,2176]{1,0:T(8,128)(2,1)}, bf16[64,2176]{1,0:T(8,128)(2,1)S(1)}, u32[]{:S(2)}, u32[]{:S(2)}) collective-permute-start(bf16[64,2176]{1,0:T(8,128)(2,1)} %pack.1.refs_0_), channel_id=1, source_target_pairs={{0,4},{1,3},{4,8},{5,1},{8,12},{9,5},{12,14},{13,9},{14,10},{15,13... | collective-permute-start | bytes 835592 | tf_op jit(solution)/shard_map/ppermute | solution.py:229
  4.9 7.6 %collective-permute-start.5 = (bf16[64,2176]{1,0:T(8,128)(2,1)S(1)}, bf16[64,2176]{1,0:T(8,128)(2,1)S(1)}, u32[]{:S(2)}, u32[]{:S(2)}) collective-permute-start(bf16[64,2176]{1,0:T(8,128)(2,1)S(1)} %collective-permute-done.1.refs_1_), channel_id=1, source_target_pairs={{0,4},{1,3},{4,8},{5,1},{8,12},{9,5},{12,14},{13,9},{14,10},{15,13... | collective-permute-start | bytes 835592 | tf_op jit(solution)/shard_map/ppermute | solution.py:229
  9.5 7.0 %collective-permute-start.3 = (bf16[64,2176]{1,0:T(8,128)(2,1)S(1)}, bf16[64,2176]{1,0:T(8,128)(2,1)S(1)}, u32[]{:S(2)}, u32[]{:S(2)}) collective-permute-start(bf16[64,2176]{1,0:T(8,128)(2,1)S(1)} %collective-permute-done.refs_2_), channel_id=1, source_target_pairs={{0,4},{1,3},{4,8},{5,1},{8,12},{9,5},{12,14},{13,9},{14,10},{15,13... | collective-permute-start | bytes 835592 | tf_op jit(solution)/shard_map/ppermute | solution.py:238
  12.5 7.2 %collective-permute-start.7 = (bf16[64,2176]{1,0:T(8,128)(2,1)S(1)}, bf16[64,2176]{1,0:T(8,128)(2,1)S(1)}, u32[]{:S(2)}, u32[]{:S(2)}) collective-permute-start(bf16[64,2176]{1,0:T(8,128)(2,1)S(1)} %collective-permute-done.5.refs_3_), channel_id=1, source_target_pairs={{0,4},{1,3},{4,8},{5,1},{8,12},{9,5},{12,14},{13,9},{14,10},{15,13... | collective-permute-start | bytes 835592 | tf_op jit(solution)/shard_map/ppermute | solution.py:238
  14.6 5.1 %collective-permute-start.2 = (bf16[64,2176]{1,0:T(8,128)(2,1)S(1)}, bf16[64,2176]{1,0:T(8,128)(2,1)S(1)}, u32[]{:S(2)}, u32[]{:S(2)}) collective-permute-start(bf16[64,2176]{1,0:T(8,128)(2,1)S(1)} %collective-permute-done.refs_2_), channel_id=1, source_target_pairs={{0,1},{1,0},{2,3},{3,2},{4,5},{5,4},{6,7},{7,6},{8,9},{9,8},{10,11... | collective-permute-start | bytes 835592 | tf_op jit(solution)/shard_map/ppermute | solution.py:241
  16.5 10.4 %collective-permute-start.13 = (bf16[64,2176]{1,0:T(8,128)(2,1)S(1)}, bf16[64,2176]{1,0:T(8,128)(2,1)S(1)}, u32[]{:S(2)}, u32[]{:S(2)}) collective-permute-start(bf16[64,2176]{1,0:T(8,128)(2,1)S(1)} %collective-permute-done.3.refs_2_), channel_id=1, source_target_pairs={{0,8},{1,7},{4,12},{5,3},{8,14},{9,1},{12,10},{13,5},{14,6},{15,9}... | collective-permute-start | bytes 835592 | tf_op jit(solution)/shard_map/ppermute | solution.py:242
  19.2 2.2 %collective-permute-start.4 = (bf16[64,2176]{1,0:T(8,128)(2,1)S(1)}, bf16[64,2176]{1,0:T(8,128)(2,1)S(1)}, u32[]{:S(2)}, u32[]{:S(2)}) collective-permute-start(bf16[64,2176]{1,0:T(8,128)(2,1)S(1)} %collective-permute-done.3.refs_2_), channel_id=1, source_target_pairs={{0,1},{1,0},{2,3},{3,2},{4,5},{5,4},{6,7},{7,6},{8,9},{9,8},{10,11... | collective-permute-start | bytes 835592 | tf_op jit(solution)/shard_map/ppermute | solution.py:241
  19.2 2.2 %collective-permute-start.6 = (bf16[64,2176]{1,0:T(8,128)(2,1)S(1)}, bf16[64,2176]{1,0:T(8,128)(2,1)S(1)}, u32[]{:S(2)}, u32[]{:S(2)}) collective-permute-start(bf16[64,2176]{1,0:T(8,128)(2,1)S(1)} %collective-permute-done.5.refs_3_), channel_id=1, source_target_pairs={{0,1},{1,0},{2,3},{3,2},{4,5},{5,4},{6,7},{7,6},{8,9},{9,8},{10,11... | collective-permute-start | bytes 835592 | tf_op jit(solution)/shard_map/ppermute | solution.py:241
  19.7 1.8 %collective-permute-start.8 = (bf16[64,2176]{1,0:T(8,128)(2,1)S(1)}, bf16[64,2176]{1,0:T(8,128)(2,1)S(1)}, u32[]{:S(2)}, u32[]{:S(2)}) collective-permute-start(bf16[64,2176]{1,0:T(8,128)(2,1)S(1)} %collective-permute-done.7.refs_3_), channel_id=1, source_target_pairs={{0,1},{1,0},{2,3},{3,2},{4,5},{5,4},{6,7},{7,6},{8,9},{9,8},{10,11... | collective-permute-start | bytes 835592 | tf_op jit(solution)/shard_map/ppermute | solution.py:241
  19.8 11.8 %collective-permute-start.11 = (bf16[128,2176]{1,0:T(8,128)(2,1)S(1)}, bf16[128,2176]{1,0:T(8,128)(2,1)S(1)}, u32[]{:S(2)}, u32[]{:S(2)}) collective-permute-start(bf16[128,2176]{1,0:T(8,128)(2,1)S(1)} %pad_maximum_fusion), channel_id=1, source_target_pairs={{0,4},{1,3},{4,8},{5,1},{8,12},{9,5},{12,14},{13,9},{14,10},{15,13... | collective-permute-start | bytes 1671176 | tf_op jit(solution)/shard_map/ppermute | solution.py:243
  26.9 2.4 %collective-permute-start.14 = (bf16[64,2176]{1,0:T(8,128)(2,1)S(1)}, bf16[64,2176]{1,0:T(8,128)(2,1)S(1)}, u32[]{:S(2)}, u32[]{:S(2)}) collective-permute-start(bf16[64,2176]{1,0:T(8,128)(2,1)S(1)} %collective-permute-done.13.refs_1_), channel_id=1, source_target_pairs={{0,1},{1,0},{2,3},{3,2},{4,5},{5,4},{6,7},{7,6},{8,9},{9,8},{10,11... | collective-permute-start | bytes 835592 | tf_op jit(solution)/shard_map/ppermute | solution.py:249
  27.1 1.8 %collective-permute-start.10 = (bf16[64,2048]{1,0:T(8,128)(2,1)S(1)}, bf16[64,2048]{1,0:T(8,128)(2,1)S(1)}, u32[]{:S(2)}, u32[]{:S(2)}) collective-permute-start(bf16[64,2048]{1,0:T(8,128)(2,1)S(1)} %get-tuple-element.50), channel_id=1, source_target_pairs={{0,1},{1,0},{2,3},{3,2},{4,5},{5,4},{6,7},{7,6},{8,9},{9,8},{10,11... | collective-permute-start | bytes 786440 | tf_op jit(solution)/shard_map/ppermute | solution.py:244
  27.4 1.8 %collective-permute-start.15 = (bf16[64,2048]{1,0:T(8,128)(2,1)S(1)}, bf16[64,2048]{1,0:T(8,128)(2,1)S(1)}, u32[]{:S(2)}, u32[]{:S(2)}) collective-permute-start(bf16[64,2048]{1,0:T(8,128)(2,1)S(1)} %get-tuple-element.52), channel_id=1, source_target_pairs={{0,1},{1,0},{2,3},{3,2},{4,5},{5,4},{6,7},{7,6},{8,9},{9,8},{10,11... | collective-permute-start | bytes 786440 | tf_op jit(solution)/shard_map/ppermute | solution.py:244
  31.3 1.6 %collective-permute-start.16 = (bf16[64,2048]{1,0:T(8,128)(2,1)S(1)}, bf16[64,2048]{1,0:T(8,128)(2,1)S(1)}, u32[]{:S(2)}, u32[]{:S(2)}) collective-permute-start(bf16[64,2048]{1,0:T(8,128)(2,1)S(1)} %get-tuple-element.55), channel_id=1, source_target_pairs={{0,1},{1,0},{2,3},{3,2},{4,5},{5,4},{6,7},{7,6},{8,9},{9,8},{10,11... | collective-permute-start | bytes 786440 | tf_op jit(solution)/shard_map/ppermute | solution.py:250
  31.5 3.1 %collective-permute-start.12 = (bf16[128,2176]{1,0:T(8,128)(2,1)S(1)}, bf16[128,2176]{1,0:T(8,128)(2,1)S(1)}, u32[]{:S(2)}, u32[]{:S(2)}) collective-permute-start(bf16[128,2176]{1,0:T(8,128)(2,1)S(1)} %collective-permute-done.11.refs_1_), channel_id=1, source_target_pairs={{0,1},{1,0},{2,3},{3,2},{4,5},{5,4},{6,7},{7,6},{8,9},{9,8},{10,11... | collective-permute-start | bytes 1671176 | tf_op jit(solution)/shard_map/ppermute | solution.py:251
  33.0 10.1 %copy-start = (bf16[64,2176]{1,0:T(8,128)(2,1)S(1)}, bf16[64,2176]{1,0:T(8,128)(2,1)}, u32[]{:S(2)}) copy-start(bf16[64,2176]{1,0:T(8,128)(2,1)} %pack.1.refs_0_) | copy-start | bytes 835588
  33.0 6.4 %collective-permute-start.18 = (bf16[64,2048]{1,0:T(8,128)(2,1)S(1)}, bf16[64,2048]{1,0:T(8,128)(2,1)S(1)}, u32[]{:S(2)}, u32[]{:S(2)}) collective-permute-start(bf16[64,2048]{1,0:T(8,128)(2,1)S(1)} %add_convert_fusion.7), channel_id=1, source_target_pairs={{0,4},{1,3},{4,8},{5,1},{8,12},{9,5},{12,14},{13,9},{14,10},{15,13... | collective-permute-start | bytes 786440 | tf_op jit(solution)/shard_map/ppermute | solution.py:252
  37.3 2.1 %collective-permute-start.17 = (bf16[64,2048]{1,0:T(8,128)(2,1)S(1)}, bf16[64,2048]{1,0:T(8,128)(2,1)S(1)}, u32[]{:S(2)}, u32[]{:S(2)}) collective-permute-start(bf16[64,2048]{1,0:T(8,128)(2,1)S(1)} %get-tuple-element.58), channel_id=1, source_target_pairs={{0,1},{1,0},{2,3},{3,2},{4,5},{5,4},{6,7},{7,6},{8,9},{9,8},{10,11... | collective-permute-start | bytes 786440 | tf_op jit(solution)/shard_map/ppermute | solution.py:244
  37.4 13.1 %collective-permute-start.9 = (bf16[64,2048]{1,0:T(8,128)(2,1)S(1)}, bf16[64,2048]{1,0:T(8,128)(2,1)S(1)}, u32[]{:S(2)}, u32[]{:S(2)}) collective-permute-start(bf16[64,2048]{1,0:T(8,128)(2,1)S(1)} %get-tuple-element.49), channel_id=1, source_target_pairs={{0,1},{1,0},{2,3},{3,2},{4,5},{5,4},{6,7},{7,6},{8,9},{9,8},{10,11... | collective-permute-start | bytes 786440 | tf_op jit(solution)/shard_map/ppermute | solution.py:244
  37.9 14.8 %collective-permute-start.24 = (bf16[64,2048]{1,0:T(8,128)(2,1)S(1)}, bf16[64,2048]{1,0:T(8,128)(2,1)S(1)}, u32[]{:S(2)}, u32[]{:S(2)}) collective-permute-start(bf16[64,2048]{1,0:T(8,128)(2,1)S(1)} %get-tuple-element.68), channel_id=1, source_target_pairs={{0,1},{1,0},{2,3},{3,2},{4,5},{5,4},{6,7},{7,6},{8,9},{9,8},{10,11... | collective-permute-start | bytes 786440 | tf_op jit(solution)/shard_map/ppermute | solution.py:244
  38.0 3.2 %collective-permute-start.20 = (bf16[64,2048]{1,0:T(8,128)(2,1)S(1)}, bf16[64,2048]{1,0:T(8,128)(2,1)S(1)}, u32[]{:S(2)}, u32[]{:S(2)}) collective-permute-start(bf16[64,2048]{1,0:T(8,128)(2,1)S(1)} %get-tuple-element.61), channel_id=1, source_target_pairs={{0,1},{1,0},{2,3},{3,2},{4,5},{5,4},{6,7},{7,6},{8,9},{9,8},{10,11... | collective-permute-start | bytes 786440 | tf_op jit(solution)/shard_map/ppermute | solution.py:244
  39.5 6.4 %collective-permute-start.19 = (bf16[64,2048]{1,0:T(8,128)(2,1)S(1)}, bf16[64,2048]{1,0:T(8,128)(2,1)S(1)}, u32[]{:S(2)}, u32[]{:S(2)}) collective-permute-start(bf16[64,2048]{1,0:T(8,128)(2,1)S(1)} %add_convert_fusion.6), channel_id=1, source_target_pairs={{0,4},{1,3},{4,8},{5,1},{8,12},{9,5},{12,14},{13,9},{14,10},{15,13... | collective-permute-start | bytes 786440 | tf_op jit(solution)/shard_map/ppermute | solution.py:261
  41.2 7.5 %collective-permute-start.25 = (bf16[64,2048]{1,0:T(8,128)(2,1)S(1)}, bf16[64,2048]{1,0:T(8,128)(2,1)S(1)}, u32[]{:S(2)}, u32[]{:S(2)}) collective-permute-start(bf16[64,2048]{1,0:T(8,128)(2,1)S(1)} %add_convert_fusion.5), channel_id=1, source_target_pairs={{0,4},{1,3},{4,8},{5,1},{8,12},{9,5},{12,14},{13,9},{14,10},{15,13... | collective-permute-start | bytes 786440 | tf_op jit(solution)/shard_map/ppermute | solution.py:261
  45.1 11.9 %collective-permute-start.23 = (bf16[64,2048]{1,0:T(8,128)(2,1)S(1)}, bf16[64,2048]{1,0:T(8,128)(2,1)S(1)}, u32[]{:S(2)}, u32[]{:S(2)}) collective-permute-start(bf16[64,2048]{1,0:T(8,128)(2,1)S(1)} %get-tuple-element.65), channel_id=1, source_target_pairs={{0,1},{1,0},{2,3},{3,2},{4,5},{5,4},{6,7},{7,6},{8,9},{9,8},{10,11... | collective-permute-start | bytes 786440 | tf_op jit(solution)/shard_map/ppermute | solution.py:262
  46.0 6.4 %collective-permute-start.21 = (bf16[64,2048]{1,0:T(8,128)(2,1)S(1)}, bf16[64,2048]{1,0:T(8,128)(2,1)S(1)}, u32[]{:S(2)}, u32[]{:S(2)}) collective-permute-start(bf16[64,2048]{1,0:T(8,128)(2,1)S(1)} %add_convert_fusion.4), channel_id=1, source_target_pairs={{0,4},{1,3},{4,8},{5,1},{8,12},{9,5},{12,14},{13,9},{14,10},{15,13... | collective-permute-start | bytes 786440 | tf_op jit(solution)/shard_map/ppermute | solution.py:261
  48.9 6.4 %collective-permute-start.26 = (bf16[64,2048]{1,0:T(8,128)(2,1)S(1)}, bf16[64,2048]{1,0:T(8,128)(2,1)S(1)}, u32[]{:S(2)}, u32[]{:S(2)}) collective-permute-start(bf16[64,2048]{1,0:T(8,128)(2,1)S(1)} %add_convert_fusion.2), channel_id=1, source_target_pairs={{0,4},{1,3},{4,8},{5,1},{8,12},{9,5},{12,14},{13,9},{14,10},{15,13... | collective-permute-start | bytes 786440 | tf_op jit(solution)/shard_map/ppermute | solution.py:261
  52.6 5.9 %collective-permute-start.22 = (bf16[64,2048]{1,0:T(8,128)(2,1)S(1)}, bf16[64,2048]{1,0:T(8,128)(2,1)S(1)}, u32[]{:S(2)}, u32[]{:S(2)}) collective-permute-start(bf16[64,2048]{1,0:T(8,128)(2,1)S(1)} %add_convert_fusion.3), channel_id=1, source_target_pairs={{0,5},{1,2},{4,9},{5,0},{8,13},{9,4},{12,15},{13,8},{14,11},{15,12... | collective-permute-start | bytes 786440 | tf_op jit(solution)/shard_map/ppermute | solution.py:261
  55.4 6.4 %collective-permute-start.27 = (bf16[64,2048]{1,0:T(8,128)(2,1)S(1)}, bf16[64,2048]{1,0:T(8,128)(2,1)S(1)}, u32[]{:S(2)}, u32[]{:S(2)}) collective-permute-start(bf16[64,2048]{1,0:T(8,128)(2,1)S(1)} %add_convert_fusion.1), channel_id=1, source_target_pairs={{0,4},{1,3},{4,8},{5,1},{8,12},{9,5},{12,14},{13,9},{14,10},{15,13... | collective-permute-start | bytes 786440 | tf_op jit(solution)/shard_map/ppermute | solution.py:261

commit v14 on v13

--- a/solution.py
+++ b/solution.py
@@ -145,7 +145,7 @@
 
 
 def load_weights(weights):
-    pieces = math.gcd(weights[0].shape[1] // 16, 4)
+    pieces = math.gcd(weights[0].shape[1] // 16, 16)
     return pl.pallas_call(
         functools.partial(load_kernel, pieces),
         out_shape=[pltpu.VMEM(w.shape, w.dtype) for w in weights],
@@ -246,9 +246,9 @@
     sums[1] = run(after(blocks[1][0], sums[2][0]), *blocks[1][1:])
     far = after(far, sums[1][0])
     sums[2], sums[1] = turned(*sums[2]), turned(*sums[1])
-    keep, send = run(after(swap(far), *sums[2][2:]), far)
+    keep, send = run(swap(far), far)
     lead, trail = [added(keep, swap(send))], []
-    sums[3] = turned(*run(after(swap(both), lead[0]), both))
+    sums[3] = turned(*run(after(swap(both), lead[0], *sums[2][2:]), both))
     lead = [ring(lead[0])]
     for step in range(rounds - 1, 0, -1):
         if step == 2:

time: 62.7 us -> 62.6 us (level)
  waiting for transfers between devices: 15.8 us -> 12.7 us
  starting transfers between devices: 26.5 us -> 29.1 us
    ppermute x6, starting transfers between devices: 8.56 us -> 11.6 us  [dense_body(): lead, trail = ([(ring if step > 1 else home)(lead[0])], [ring(trail[0])])]
    ppermute x6, waiting for transfers between devices: 11 us -> 8.25 us  [dense_body(): lead, trail = ([(ring if step > 1 else home)(lead[0])], [ring(trail[0])])]
    ppermute x2, waiting for transfers between devices: 0.01 us -> 1.56 us  [the longest x1 1.56 us: dense_body(): keep, send = run(swap(far), far)]
    ppermute x3, waiting for transfers between devices: 1.29 us -> 0.01 us  [dense_body(): swap(send)]
  transfers between devices with their start and end apart: 28 -> 28, of which waited for: 13 -> 12; matrix products, arithmetic and copies ran while one was open for 1% -> 1% of each run, Pallas kernels for 27% -> 28%
where the time goes in v14:
time: 62.6 us; the launch traced here: 62.5 us
  starting transfers between devices  29.1 us (46%)
  Pallas kernels  19 us (30%)
  waiting for transfers between devices  12.7 us (20%)
  other arithmetic  1.53 us (2%)
    pallas_call x5, Pallas kernels, run_expert(): pl.pallas_call(functools.partial(expert_kernel, experts, len(blocks)), ou...  12.1 us
    ppermute x6, starting transfers between devices, dense_body(): lead, trail = ([(ring if step > 1 else home)(lead[0])], [ring(trail[0])])  11.6 us
    ppermute x6, waiting for transfers between devices, dense_body(): lead, trail = ([(ring if step > 1 else home)(lead[0])], [ring(trail[0])])  8.25 us
    pallas_call x2, Pallas kernels, load_weights(): pl.pallas_call(functools.partial(load_kernel, pieces), out_shape=[pltpu.V...  5.22 us
    ppermute x2, starting transfers between devices, dense_body(): first, second = (ring(mine), ring(sibling))  4.34 us
    ppermute x2, starting transfers between devices, dense_body(): first, second = (ring(first), ring(second))  3.99 us
    ppermute x1, starting transfers between devices, dense_body(): far = leap(first)  2.64 us
    ppermute x1, starting transfers between devices, dense_body(): lead = [ring(lead[0])]  1.97 us
  transfers between devices with their start and end apart: 28, of which 12 were waited for; matrix products, arithmetic and copies ran while one was open for 1% of the time, Pallas kernels for 28%

profile of v14, /device:TPU:0, one launch (start us, length us, event | category | flops | bytes accessed | tf_op | source)
XLA Modules:
  0.0 62.5 jit_solution(274097964519408700)
XLA Ops:
  0.0 1.7 %pack.1.refs_0_ = bf16[64,2176]{1,0:T(8,128)(2,1)} custom-call(bf16[64,2048]{1,0:T(8,128)(2,1)} %tokens_ref, s32[8,64]{1,0:T(8,128)} %bitcast.3, f32[8,64]{1,0:T(8,128)} %bitcast.4), custom_call_target="tpu_custom_call" | custom-call | bytes 1024 | tf_op jit(solution)/shard_map/pack/pallas_call | solution.py:191
  1.7 0.5 collective-permute-start.1
  2.2 2.6 %collective-permute-start = (bf16[64,2176]{1,0:T(8,128)(2,1)}, bf16[64,2176]{1,0:T(8,128)(2,1)S(1)}, u32[]{:S(2)}, u32[]{:S(2)}) collective-permute-start(bf16[64,2176]{1,0:T(8,128)(2,1)} %pack.1.refs_0_), channel_id=1, source_target_pairs={{0,4},{1,3},{4,8},{5,1},{8,12},{9,5},{12,14},{13,9},{14,10},{15,13... | collective-permute-start | bytes 835592 | tf_op jit(solution)/shard_map/ppermute | solution.py:229
  4.9 0.0 collective-permute-done.1.refs_1_
  4.9 1.7 %collective-permute-start.5 = (bf16[64,2176]{1,0:T(8,128)(2,1)S(1)}, bf16[64,2176]{1,0:T(8,128)(2,1)S(1)}, u32[]{:S(2)}, u32[]{:S(2)}) collective-permute-start(bf16[64,2176]{1,0:T(8,128)(2,1)S(1)} %collective-permute-done.1.refs_1_), channel_id=1, source_target_pairs={{0,4},{1,3},{4,8},{5,1},{8,12},{9,5},{12,14},{13,9},{14,10},{15,13... | collective-permute-start | bytes 835592 | tf_op jit(solution)/shard_map/ppermute | solution.py:229
  6.6 3.1 %load.2 = (bf16[1,2048,768]{2,1,0:T(8,128)(2,1)S(1)}, bf16[1,2048,768]{2,1,0:T(8,128)(2,1)S(1)}) custom-call(bf16[1,2048,768]{2,1,0:T(8,128)(2,1)} %refs_0_, bf16[1,2048,768]{2,1,0:T(8,128)(2,1)} %refs_1_.1), custom_call_target="tpu_custom_call" | custom-call | bytes 1024 | tf_op jit(solution)/shard_map/load/pallas_call | solution.py:149
  9.7 0.0 collective-permute-done.refs_2_
  9.7 1.9 %collective-permute-start.3 = (bf16[64,2176]{1,0:T(8,128)(2,1)S(1)}, bf16[64,2176]{1,0:T(8,128)(2,1)S(1)}, u32[]{:S(2)}, u32[]{:S(2)}) collective-permute-start(bf16[64,2176]{1,0:T(8,128)(2,1)S(1)} %collective-permute-done.refs_2_), channel_id=1, source_target_pairs={{0,4},{1,3},{4,8},{5,1},{8,12},{9,5},{12,14},{13,9},{14,10},{15,13... | collective-permute-start | bytes 835592 | tf_op jit(solution)/shard_map/ppermute | solution.py:238
  11.6 0.9 %collective-permute-done.5.refs_3_ = bf16[64,2176]{1,0:T(8,128)(2,1)S(1)} collective-permute-done((bf16[64,2176]{1,0:T(8,128)(2,1)S(1)}, bf16[64,2176]{1,0:T(8,128)(2,1)S(1)}, u32[]{:S(2)}, u32[]{:S(2)}) %collective-permute-start.5) | collective-permute-done | bytes 278560 | tf_op jit(solution)/shard_map/ppermute | solution.py:229
  12.5 2.1 %collective-permute-start.7 = (bf16[64,2176]{1,0:T(8,128)(2,1)S(1)}, bf16[64,2176]{1,0:T(8,128)(2,1)S(1)}, u32[]{:S(2)}, u32[]{:S(2)}) collective-permute-start(bf16[64,2176]{1,0:T(8,128)(2,1)S(1)} %collective-permute-done.5.refs_3_), channel_id=1, source_target_pairs={{0,4},{1,3},{4,8},{5,1},{8,12},{9,5},{12,14},{13,9},{14,10},{15,13... | collective-permute-start | bytes 835592 | tf_op jit(solution)/shard_map/ppermute | solution.py:238
  14.6 0.0 collective-permute-start.2
  14.6 2.1 %load.3.refs_6_.refs_4_ = bf16[1,2048,768]{2,1,0:T(8,128)(2,1)S(1)} custom-call(bf16[1,2048,768]{2,1,0:T(8,128)(2,1)} %refs_0_.1), custom_call_target="tpu_custom_call" | custom-call | bytes 1024 | tf_op jit(solution)/shard_map/load/pallas_call | solution.py:149
  16.7 0.0 collective-permute-done.3.refs_2_
  16.7 2.6 %collective-permute-start.13 = (bf16[64,2176]{1,0:T(8,128)(2,1)S(1)}, bf16[64,2176]{1,0:T(8,128)(2,1)S(1)}, u32[]{:S(2)}, u32[]{:S(2)}) collective-permute-start(bf16[64,2176]{1,0:T(8,128)(2,1)S(1)} %collective-permute-done.3.refs_2_), channel_id=1, source_target_pairs={{0,8},{1,7},{4,12},{5,3},{8,14},{9,1},{12,10},{13,5},{14,6},{15,9}... | collective-permute-start | bytes 835592 | tf_op jit(solution)/shard_map/ppermute | solution.py:242
  19.3 0.0 collective-permute-start.4
  19.3 0.5 collective-permute-start.6
  19.9 0.0 collective-permute-done.7.refs_3_
  19.9 0.0 collective-permute-start.8
  19.9 1.5 %collective-permute-start.11 = (bf16[128,2176]{1,0:T(8,128)(2,1)S(1)}, bf16[128,2176]{1,0:T(8,128)(2,1)S(1)}, u32[]{:S(2)}, u32[]{:S(2)}) collective-permute-start(bf16[128,2176]{1,0:T(8,128)(2,1)S(1)} %pad_maximum_fusion), channel_id=1, source_target_pairs={{0,4},{1,3},{4,8},{5,1},{8,12},{9,5},{12,14},{13,9},{14,10},{15,13... | collective-permute-start | bytes 1671176 | tf_op jit(solution)/shard_map/ppermute | solution.py:243
  21.5 0.0 collective-permute-done.6.refs_1_
  21.5 0.0 collective-permute-done.4.refs_0_
  21.5 0.2 collective-permute-done.8.refs_1_
  21.7 2.7 %expert.5 = (bf16[64,2048]{1,0:T(8,128)(2,1)S(1)}, bf16[64,2048]{1,0:T(8,128)(2,1)S(1)}, bf16[64,2048]{1,0:T(8,128)(2,1)S(1)}, bf16[64,2048]{1,0:T(8,128)(2,1)S(1)}) custom-call(s32[1]{0:T(128)} %bitcast.own_ref, bf16[64,2176]{1,0:T(8,128)(2,1)S(1)} %collective-permute-done.4.refs_0_, bf16[64,2176]{1,0:T(8,128)(2,1)S(1)} %collective-permute-done.8.refs_1_, ...), custom_call_target="tpu_custom_call" | custom-call | flops 524288 | bytes 524288 | tf_op jit(solution)/shard_map/expert/pallas_call | solution.py:116
  24.4 2.7 %expert.6 = (bf16[64,2048]{1,0:T(8,128)(2,1)S(1)}, bf16[64,2048]{1,0:T(8,128)(2,1)S(1)}, bf16[64,2048]{1,0:T(8,128)(2,1)S(1)}, bf16[64,2048]{1,0:T(8,128)(2,1)S(1)}) custom-call(s32[1]{0:T(128)} %bitcast.own_ref, bf16[64,2176]{1,0:T(8,128)(2,1)S(1)} %collective-permute-done.2.refs_0_, bf16[64,2176]{1,0:T(8,128)(2,1)S(1)} %collective-permute-done.6.refs_1_, ...), custom_call_target="tpu_custom_call" | custom-call | flops 524288 | bytes 524288 | tf_op jit(solution)/shard_map/expert/pallas_call | solution.py:116
  27.0 0.3 collective-permute-done.13.refs_1_
  27.3 1.6 %collective-permute-done.14.refs_0_ = bf16[64,2176]{1,0:T(8,128)(2,1)S(1)} collective-permute-done((bf16[64,2176]{1,0:T(8,128)(2,1)S(1)}, bf16[64,2176]{1,0:T(8,128)(2,1)S(1)}, u32[]{:S(2)}, u32[]{:S(2)}) %collective-permute-start.14) | collective-permute-done | bytes 278560 | tf_op jit(solution)/shard_map/ppermute | solution.py:249
  28.8 2.0 %expert.7 = (bf16[64,2048]{1,0:T(8,128)(2,1)S(1)}, bf16[64,2048]{1,0:T(8,128)(2,1)S(1)}) custom-call(s32[1]{0:T(128)} %bitcast.own_ref, bf16[64,2176]{1,0:T(8,128)(2,1)S(1)} %collective-permute-done.14.refs_0_, bf16[64,2176]{1,0:T(8,128)(2,1)S(1)} %collective-permute-done.13.refs_1_, bf16[1,2048,768]{2,1,0:T(8,128)(2,1)S(1)} %get-tuple-element.39.refs_4_.refs_2_, ...), custom_call_target="tpu_custom_call" | custom-call | flops 262144 | bytes 262144 | tf_op jit(solution)/shard_map/expert/pallas_call | solution.py:116
  30.9 0.2 collective-permute-start.15
  31.1 0.3 collective-permute-done.11.refs_1_
  31.4 0.1 collective-permute-start.12
  31.5 0.4 collective-permute-start.10
  31.9 0.1 collective-permute-start.16
  32.0 0.5 collective-permute-done.15
  32.5 0.1 add_convert_fusion.7
  32.6 2.0 %collective-permute-start.18 = (bf16[64,2048]{1,0:T(8,128)(2,1)S(1)}, bf16[64,2048]{1,0:T(8,128)(2,1)S(1)}, u32[]{:S(2)}, u32[]{:S(2)}) collective-permute-start(bf16[64,2048]{1,0:T(8,128)(2,1)S(1)} %add_convert_fusion.7), channel_id=1, source_target_pairs={{0,4},{1,3},{4,8},{5,1},{8,12},{9,5},{12,14},{13,9},{14,10},{15,13... | collective-permute-start | bytes 786440 | tf_op jit(solution)/shard_map/ppermute | solution.py:252
  34.5 0.0 collective-permute-done.16
  34.6 0.0 collective-permute-done.12.refs_0_
  34.6 2.7 %expert.8 = (bf16[64,2048]{1,0:T(8,128)(2,1)S(1)}, bf16[64,2048]{1,0:T(8,128)(2,1)S(1)}, bf16[64,2048]{1,0:T(8,128)(2,1)S(1)}, bf16[64,2048]{1,0:T(8,128)(2,1)S(1)}) custom-call(s32[1]{0:T(128)} %bitcast.own_ref, bf16[128,2176]{1,0:T(8,128)(2,1)S(1)} %collective-permute-done.12.refs_0_, bf16[128,2176]{1,0:T(8,128)(2,1)S(1)} %collective-permute-done.11.refs_1_, ...), custom_call_target="tpu_custom_call" | custom-call | flops 524288 | bytes 524288 | tf_op jit(solution)/shard_map/expert/pallas_call | solution.py:116
  37.2 0.1 collective-permute-start.17
  37.3 0.5 collective-permute-start.9
  37.8 0.1 collective-permute-start.24
  37.9 0.4 collective-permute-start.20
  38.3 0.7 %collective-permute-done.18 = bf16[64,2048]{1,0:T(8,128)(2,1)S(1)} collective-permute-done((bf16[64,2048]{1,0:T(8,128)(2,1)S(1)}, bf16[64,2048]{1,0:T(8,128)(2,1)S(1)}, u32[]{:S(2)}, u32[]{:S(2)}) %collective-permute-start.18) | collective-permute-done | bytes 262176 | tf_op jit(solution)/shard_map/ppermute | solution.py:252
  39.0 0.1 add_convert_fusion.6
  39.1 2.3 %collective-permute-start.19 = (bf16[64,2048]{1,0:T(8,128)(2,1)S(1)}, bf16[64,2048]{1,0:T(8,128)(2,1)S(1)}, u32[]{:S(2)}, u32[]{:S(2)}) collective-permute-start(bf16[64,2048]{1,0:T(8,128)(2,1)S(1)} %add_convert_fusion.6), channel_id=1, source_target_pairs={{0,4},{1,3},{4,8},{5,1},{8,12},{9,5},{12,14},{13,9},{14,10},{15,13... | collective-permute-start | bytes 786440 | tf_op jit(solution)/shard_map/ppermute | solution.py:261
  41.5 0.1 add_convert_fusion.5
  41.5 2.2 %collective-permute-start.25 = (bf16[64,2048]{1,0:T(8,128)(2,1)S(1)}, bf16[64,2048]{1,0:T(8,128)(2,1)S(1)}, u32[]{:S(2)}, u32[]{:S(2)}) collective-permute-start(bf16[64,2048]{1,0:T(8,128)(2,1)S(1)} %add_convert_fusion.5), channel_id=1, source_target_pairs={{0,4},{1,3},{4,8},{5,1},{8,12},{9,5},{12,14},{13,9},{14,10},{15,13... | collective-permute-start | bytes 786440 | tf_op jit(solution)/shard_map/ppermute | solution.py:261
  43.7 2.1 %expert.9 = (bf16[64,2048]{1,0:T(8,128)(2,1)S(1)}, bf16[64,2048]{1,0:T(8,128)(2,1)S(1)}) custom-call(s32[1]{0:T(128)} %bitcast.own_ref, bf16[64,2176]{1,0:T(8,128)(2,1)S(1)} %copy-done, bf16[64,2176]{1,0:T(8,128)(2,1)S(1)} %collective-permute-done.1.refs_1_, bf16[1,2048,768]{2,1,0:T(8,128)(2,1)S(1)} %get-tuple-element.39.refs_4_.refs_2_, ...), custom_call_target="tpu_custom_call" | custom-call | flops 262144 | bytes 262144 | tf_op jit(solution)/shard_map/expert/pallas_call | solution.py:116
  45.7 0.1 collective-permute-start.23
  45.8 0.1 add_convert_fusion.4
  45.9 2.0 %collective-permute-start.21 = (bf16[64,2048]{1,0:T(8,128)(2,1)S(1)}, bf16[64,2048]{1,0:T(8,128)(2,1)S(1)}, u32[]{:S(2)}, u32[]{:S(2)}) collective-permute-start(bf16[64,2048]{1,0:T(8,128)(2,1)S(1)} %add_convert_fusion.4), channel_id=1, source_target_pairs={{0,4},{1,3},{4,8},{5,1},{8,12},{9,5},{12,14},{13,9},{14,10},{15,13... | collective-permute-start | bytes 786440 | tf_op jit(solution)/shard_map/ppermute | solution.py:261
  48.0 0.4 collective-permute-done.25
  48.3 0.1 add_convert_fusion.2
  48.4 2.3 %collective-permute-start.26 = (bf16[64,2048]{1,0:T(8,128)(2,1)S(1)}, bf16[64,2048]{1,0:T(8,128)(2,1)S(1)}, u32[]{:S(2)}, u32[]{:S(2)}) collective-permute-start(bf16[64,2048]{1,0:T(8,128)(2,1)S(1)} %add_convert_fusion.2), channel_id=1, source_target_pairs={{0,4},{1,3},{4,8},{5,1},{8,12},{9,5},{12,14},{13,9},{14,10},{15,13... | collective-permute-start | bytes 786440 | tf_op jit(solution)/shard_map/ppermute | solution.py:261
  50.8 1.6 %collective-permute-done.21 = bf16[64,2048]{1,0:T(8,128)(2,1)S(1)} collective-permute-done((bf16[64,2048]{1,0:T(8,128)(2,1)S(1)}, bf16[64,2048]{1,0:T(8,128)(2,1)S(1)}, u32[]{:S(2)}, u32[]{:S(2)}) %collective-permute-start.21) | collective-permute-done | bytes 262176 | tf_op jit(solution)/shard_map/ppermute | solution.py:261
  52.4 0.1 add_convert_fusion.3
  52.5 0.7 %collective-permute-start.22 = (bf16[64,2048]{1,0:T(8,128)(2,1)S(1)}, bf16[64,2048]{1,0:T(8,128)(2,1)S(1)}, u32[]{:S(2)}, u32[]{:S(2)}) collective-permute-start(bf16[64,2048]{1,0:T(8,128)(2,1)S(1)} %add_convert_fusion.3), channel_id=1, source_target_pairs={{0,5},{1,2},{4,9},{5,0},{8,13},{9,4},{12,15},{13,8},{14,11},{15,12... | collective-permute-start | bytes 786440 | tf_op jit(solution)/shard_map/ppermute | solution.py:261
  53.2 2.0 %collective-permute-done.26 = bf16[64,2048]{1,0:T(8,128)(2,1)S(1)} collective-permute-done((bf16[64,2048]{1,0:T(8,128)(2,1)S(1)}, bf16[64,2048]{1,0:T(8,128)(2,1)S(1)}, u32[]{:S(2)}, u32[]{:S(2)}) %collective-permute-start.26) | collective-permute-done | bytes 262176 | tf_op jit(solution)/shard_map/ppermute | solution.py:261
  55.2 0.1 add_convert_fusion.1
  55.3 2.0 %collective-permute-start.27 = (bf16[64,2048]{1,0:T(8,128)(2,1)S(1)}, bf16[64,2048]{1,0:T(8,128)(2,1)S(1)}, u32[]{:S(2)}, u32[]{:S(2)}) collective-permute-start(bf16[64,2048]{1,0:T(8,128)(2,1)S(1)} %add_convert_fusion.1), channel_id=1, source_target_pairs={{0,4},{1,3},{4,8},{5,1},{8,12},{9,5},{12,14},{13,9},{14,10},{15,13... | collective-permute-start | bytes 786440 | tf_op jit(solution)/shard_map/ppermute | solution.py:261
  57.3 1.0 %collective-permute-done.22 = bf16[64,2048]{1,0:T(8,128)(2,1)S(1)} collective-permute-done((bf16[64,2048]{1,0:T(8,128)(2,1)S(1)}, bf16[64,2048]{1,0:T(8,128)(2,1)S(1)}, u32[]{:S(2)}, u32[]{:S(2)}) %collective-permute-start.22) | collective-permute-done | bytes 262176 | tf_op jit(solution)/shard_map/ppermute | solution.py:261
  58.3 0.1 convert_add_fusion
  58.4 3.3 %collective-permute-done.27 = bf16[64,2048]{1,0:T(8,128)(2,1)S(1)} collective-permute-done((bf16[64,2048]{1,0:T(8,128)(2,1)S(1)}, bf16[64,2048]{1,0:T(8,128)(2,1)S(1)}, u32[]{:S(2)}, u32[]{:S(2)}) %collective-permute-start.27) | collective-permute-done | bytes 262176 | tf_op jit(solution)/shard_map/ppermute | solution.py:261
  61.7 0.8 %add_convert_fusion = bf16[64,2048]{1,0:T(8,128)(2,1)} fusion(f32[64,2048]{1,0:T(8,128)S(1)} %convert_add_fusion, bf16[64,2048]{1,0:T(8,128)(2,1)S(1)} %collective-permute-done.27), kind=kLoop, calls=%fused_computation.1 | loop fusion | flops 393216 | bytes 1048576 | tf_op jit(solution)/shard_map/convert_element_type | solution.py:210
  (12 shorter events, 0.1 us)
Async XLA Ops:
  1.7 3.2 %collective-permute-start.1 = (bf16[64,2176]{1,0:T(8,128)(2,1)}, bf16[64,2176]{1,0:T(8,128)(2,1)S(1)}, u32[]{:S(2)}, u32[]{:S(2)}) collective-permute-start(bf16[64,2176]{1,0:T(8,128)(2,1)} %pack.1.refs_0_), channel_id=1, source_target_pairs={{0,1},{1,0},{2,3},{3,2},{4,5},{5,4},{6,7},{7,6},{8,9},{9,8},{10,11... | collective-permute-start | bytes 835592 | tf_op jit(solution)/shard_map/ppermute | solution.py:228
  2.2 7.5 %collective-permute-start = (bf16[64,2176]{1,0:T(8,128)(2,1)}, bf16[64,2176]{1,0:T(8,128)(2,1)S(1)}, u32[]{:S(2)}, u32[]{:S(2)}) collective-permute-start(bf16[64,2176]{1,0:T(8,128)(2,1)} %pack.1.refs_0_), channel_id=1, source_target_pairs={{0,4},{1,3},{4,8},{5,1},{8,12},{9,5},{12,14},{13,9},{14,10},{15,13... | collective-permute-start | bytes 835592 | tf_op jit(solution)/shard_map/ppermute | solution.py:229
  4.9 7.6 %collective-permute-start.5 = (bf16[64,2176]{1,0:T(8,128)(2,1)S(1)}, bf16[64,2176]{1,0:T(8,128)(2,1)S(1)}, u32[]{:S(2)}, u32[]{:S(2)}) collective-permute-start(bf16[64,2176]{1,0:T(8,128)(2,1)S(1)} %collective-permute-done.1.refs_1_), channel_id=1, source_target_pairs={{0,4},{1,3},{4,8},{5,1},{8,12},{9,5},{12,14},{13,9},{14,10},{15,13... | collective-permute-start | bytes 835592 | tf_op jit(solution)/shard_map/ppermute | solution.py:229
  9.7 7.0 %collective-permute-start.3 = (bf16[64,2176]{1,0:T(8,128)(2,1)S(1)}, bf16[64,2176]{1,0:T(8,128)(2,1)S(1)}, u32[]{:S(2)}, u32[]{:S(2)}) collective-permute-start(bf16[64,2176]{1,0:T(8,128)(2,1)S(1)} %collective-permute-done.refs_2_), channel_id=1, source_target_pairs={{0,4},{1,3},{4,8},{5,1},{8,12},{9,5},{12,14},{13,9},{14,10},{15,13... | collective-permute-start | bytes 835592 | tf_op jit(solution)/shard_map/ppermute | solution.py:238
  12.5 7.4 %collective-permute-start.7 = (bf16[64,2176]{1,0:T(8,128)(2,1)S(1)}, bf16[64,2176]{1,0:T(8,128)(2,1)S(1)}, u32[]{:S(2)}, u32[]{:S(2)}) collective-permute-start(bf16[64,2176]{1,0:T(8,128)(2,1)S(1)} %collective-permute-done.5.refs_3_), channel_id=1, source_target_pairs={{0,4},{1,3},{4,8},{5,1},{8,12},{9,5},{12,14},{13,9},{14,10},{15,13... | collective-permute-start | bytes 835592 | tf_op jit(solution)/shard_map/ppermute | solution.py:238
  14.6 5.3 %collective-permute-start.2 = (bf16[64,2176]{1,0:T(8,128)(2,1)S(1)}, bf16[64,2176]{1,0:T(8,128)(2,1)S(1)}, u32[]{:S(2)}, u32[]{:S(2)}) collective-permute-start(bf16[64,2176]{1,0:T(8,128)(2,1)S(1)} %collective-permute-done.refs_2_), channel_id=1, source_target_pairs={{0,1},{1,0},{2,3},{3,2},{4,5},{5,4},{6,7},{7,6},{8,9},{9,8},{10,11... | collective-permute-start | bytes 835592 | tf_op jit(solution)/shard_map/ppermute | solution.py:241
  16.7 10.6 %collective-permute-start.13 = (bf16[64,2176]{1,0:T(8,128)(2,1)S(1)}, bf16[64,2176]{1,0:T(8,128)(2,1)S(1)}, u32[]{:S(2)}, u32[]{:S(2)}) collective-permute-start(bf16[64,2176]{1,0:T(8,128)(2,1)S(1)} %collective-permute-done.3.refs_2_), channel_id=1, source_target_pairs={{0,8},{1,7},{4,12},{5,3},{8,14},{9,1},{12,10},{13,5},{14,6},{15,9}... | collective-permute-start | bytes 835592 | tf_op jit(solution)/shard_map/ppermute | solution.py:242
  19.3 2.1 %collective-permute-start.4 = (bf16[64,2176]{1,0:T(8,128)(2,1)S(1)}, bf16[64,2176]{1,0:T(8,128)(2,1)S(1)}, u32[]{:S(2)}, u32[]{:S(2)}) collective-permute-start(bf16[64,2176]{1,0:T(8,128)(2,1)S(1)} %collective-permute-done.3.refs_2_), channel_id=1, source_target_pairs={{0,1},{1,0},{2,3},{3,2},{4,5},{5,4},{6,7},{7,6},{8,9},{9,8},{10,11... | collective-permute-start | bytes 835592 | tf_op jit(solution)/shard_map/ppermute | solution.py:241
  19.3 2.1 %collective-permute-start.6 = (bf16[64,2176]{1,0:T(8,128)(2,1)S(1)}, bf16[64,2176]{1,0:T(8,128)(2,1)S(1)}, u32[]{:S(2)}, u32[]{:S(2)}) collective-permute-start(bf16[64,2176]{1,0:T(8,128)(2,1)S(1)} %collective-permute-done.5.refs_3_), channel_id=1, source_target_pairs={{0,1},{1,0},{2,3},{3,2},{4,5},{5,4},{6,7},{7,6},{8,9},{9,8},{10,11... | collective-permute-start | bytes 835592 | tf_op jit(solution)/shard_map/ppermute | solution.py:241
  19.9 1.8 %collective-permute-start.8 = (bf16[64,2176]{1,0:T(8,128)(2,1)S(1)}, bf16[64,2176]{1,0:T(8,128)(2,1)S(1)}, u32[]{:S(2)}, u32[]{:S(2)}) collective-permute-start(bf16[64,2176]{1,0:T(8,128)(2,1)S(1)} %collective-permute-done.7.refs_3_), channel_id=1, source_target_pairs={{0,1},{1,0},{2,3},{3,2},{4,5},{5,4},{6,7},{7,6},{8,9},{9,8},{10,11... | collective-permute-start | bytes 835592 | tf_op jit(solution)/shard_map/ppermute | solution.py:241
  19.9 11.5 %collective-permute-start.11 = (bf16[128,2176]{1,0:T(8,128)(2,1)S(1)}, bf16[128,2176]{1,0:T(8,128)(2,1)S(1)}, u32[]{:S(2)}, u32[]{:S(2)}) collective-permute-start(bf16[128,2176]{1,0:T(8,128)(2,1)S(1)} %pad_maximum_fusion), channel_id=1, source_target_pairs={{0,4},{1,3},{4,8},{5,1},{8,12},{9,5},{12,14},{13,9},{14,10},{15,13... | collective-permute-start | bytes 1671176 | tf_op jit(solution)/shard_map/ppermute | solution.py:243
  27.3 1.6 %collective-permute-start.14 = (bf16[64,2176]{1,0:T(8,128)(2,1)S(1)}, bf16[64,2176]{1,0:T(8,128)(2,1)S(1)}, u32[]{:S(2)}, u32[]{:S(2)}) collective-permute-start(bf16[64,2176]{1,0:T(8,128)(2,1)S(1)} %collective-permute-done.13.refs_1_), channel_id=1, source_target_pairs={{0,1},{1,0},{2,3},{3,2},{4,5},{5,4},{6,7},{7,6},{8,9},{9,8},{10,11... | collective-permute-start | bytes 835592 | tf_op jit(solution)/shard_map/ppermute | solution.py:249
  30.9 1.6 %collective-permute-start.15 = (bf16[64,2048]{1,0:T(8,128)(2,1)S(1)}, bf16[64,2048]{1,0:T(8,128)(2,1)S(1)}, u32[]{:S(2)}, u32[]{:S(2)}) collective-permute-start(bf16[64,2048]{1,0:T(8,128)(2,1)S(1)} %get-tuple-element.52), channel_id=1, source_target_pairs={{0,1},{1,0},{2,3},{3,2},{4,5},{5,4},{6,7},{7,6},{8,9},{9,8},{10,11... | collective-permute-start | bytes 786440 | tf_op jit(solution)/shard_map/ppermute | solution.py:250
  31.4 3.2 %collective-permute-start.12 = (bf16[128,2176]{1,0:T(8,128)(2,1)S(1)}, bf16[128,2176]{1,0:T(8,128)(2,1)S(1)}, u32[]{:S(2)}, u32[]{:S(2)}) collective-permute-start(bf16[128,2176]{1,0:T(8,128)(2,1)S(1)} %collective-permute-done.11.refs_1_), channel_id=1, source_target_pairs={{0,1},{1,0},{2,3},{3,2},{4,5},{5,4},{6,7},{7,6},{8,9},{9,8},{10,11... | collective-permute-start | bytes 1671176 | tf_op jit(solution)/shard_map/ppermute | solution.py:251
  31.5 3.0 %collective-permute-start.10 = (bf16[64,2048]{1,0:T(8,128)(2,1)S(1)}, bf16[64,2048]{1,0:T(8,128)(2,1)S(1)}, u32[]{:S(2)}, u32[]{:S(2)}) collective-permute-start(bf16[64,2048]{1,0:T(8,128)(2,1)S(1)} %get-tuple-element.49), channel_id=1, source_target_pairs={{0,1},{1,0},{2,3},{3,2},{4,5},{5,4},{6,7},{7,6},{8,9},{9,8},{10,11... | collective-permute-start | bytes 786440 | tf_op jit(solution)/shard_map/ppermute | solution.py:244
  31.9 2.6 %collective-permute-start.16 = (bf16[64,2048]{1,0:T(8,128)(2,1)S(1)}, bf16[64,2048]{1,0:T(8,128)(2,1)S(1)}, u32[]{:S(2)}, u32[]{:S(2)}) collective-permute-start(bf16[64,2048]{1,0:T(8,128)(2,1)S(1)} %get-tuple-element.53), channel_id=1, source_target_pairs={{0,1},{1,0},{2,3},{3,2},{4,5},{5,4},{6,7},{7,6},{8,9},{9,8},{10,11... | collective-permute-start | bytes 786440 | tf_op jit(solution)/shard_map/ppermute | solution.py:244
  32.6 11.1 %copy-start = (bf16[64,2176]{1,0:T(8,128)(2,1)S(1)}, bf16[64,2176]{1,0:T(8,128)(2,1)}, u32[]{:S(2)}) copy-start(bf16[64,2176]{1,0:T(8,128)(2,1)} %pack.1.refs_0_) | copy-start | bytes 835588
  32.6 6.4 %collective-permute-start.18 = (bf16[64,2048]{1,0:T(8,128)(2,1)S(1)}, bf16[64,2048]{1,0:T(8,128)(2,1)S(1)}, u32[]{:S(2)}, u32[]{:S(2)}) collective-permute-start(bf16[64,2048]{1,0:T(8,128)(2,1)S(1)} %add_convert_fusion.7), channel_id=1, source_target_pairs={{0,4},{1,3},{4,8},{5,1},{8,12},{9,5},{12,14},{13,9},{14,10},{15,13... | collective-permute-start | bytes 786440 | tf_op jit(solution)/shard_map/ppermute | solution.py:252
  37.2 1.8 %collective-permute-start.17 = (bf16[64,2048]{1,0:T(8,128)(2,1)S(1)}, bf16[64,2048]{1,0:T(8,128)(2,1)S(1)}, u32[]{:S(2)}, u32[]{:S(2)}) collective-permute-start(bf16[64,2048]{1,0:T(8,128)(2,1)S(1)} %get-tuple-element.56), channel_id=1, source_target_pairs={{0,1},{1,0},{2,3},{3,2},{4,5},{5,4},{6,7},{7,6},{8,9},{9,8},{10,11... | collective-permute-start | bytes 786440 | tf_op jit(solution)/shard_map/ppermute | solution.py:244
  37.3 13.5 %collective-permute-start.9 = (bf16[64,2048]{1,0:T(8,128)(2,1)S(1)}, bf16[64,2048]{1,0:T(8,128)(2,1)S(1)}, u32[]{:S(2)}, u32[]{:S(2)}) collective-permute-start(bf16[64,2048]{1,0:T(8,128)(2,1)S(1)} %get-tuple-element.48), channel_id=1, source_target_pairs={{0,1},{1,0},{2,3},{3,2},{4,5},{5,4},{6,7},{7,6},{8,9},{9,8},{10,11... | collective-permute-start | bytes 786440 | tf_op jit(solution)/shard_map/ppermute | solution.py:244
  37.8 15.4 %collective-permute-start.24 = (bf16[64,2048]{1,0:T(8,128)(2,1)S(1)}, bf16[64,2048]{1,0:T(8,128)(2,1)S(1)}, u32[]{:S(2)}, u32[]{:S(2)}) collective-permute-start(bf16[64,2048]{1,0:T(8,128)(2,1)S(1)} %get-tuple-element.66), channel_id=1, source_target_pairs={{0,1},{1,0},{2,3},{3,2},{4,5},{5,4},{6,7},{7,6},{8,9},{9,8},{10,11... | collective-permute-start | bytes 786440 | tf_op jit(solution)/shard_map/ppermute | solution.py:244
  37.9 3.6 %collective-permute-start.20 = (bf16[64,2048]{1,0:T(8,128)(2,1)S(1)}, bf16[64,2048]{1,0:T(8,128)(2,1)S(1)}, u32[]{:S(2)}, u32[]{:S(2)}) collective-permute-start(bf16[64,2048]{1,0:T(8,128)(2,1)S(1)} %get-tuple-element.59), channel_id=1, source_target_pairs={{0,1},{1,0},{2,3},{3,2},{4,5},{5,4},{6,7},{7,6},{8,9},{9,8},{10,11... | collective-permute-start | bytes 786440 | tf_op jit(solution)/shard_map/ppermute | solution.py:244
  39.1 6.7 %collective-permute-start.19 = (bf16[64,2048]{1,0:T(8,128)(2,1)S(1)}, bf16[64,2048]{1,0:T(8,128)(2,1)S(1)}, u32[]{:S(2)}, u32[]{:S(2)}) collective-permute-start(bf16[64,2048]{1,0:T(8,128)(2,1)S(1)} %add_convert_fusion.6), channel_id=1, source_target_pairs={{0,4},{1,3},{4,8},{5,1},{8,12},{9,5},{12,14},{13,9},{14,10},{15,13... | collective-permute-start | bytes 786440 | tf_op jit(solution)/shard_map/ppermute | solution.py:261
  41.5 6.8 %collective-permute-start.25 = (bf16[64,2048]{1,0:T(8,128)(2,1)S(1)}, bf16[64,2048]{1,0:T(8,128)(2,1)S(1)}, u32[]{:S(2)}, u32[]{:S(2)}) collective-permute-start(bf16[64,2048]{1,0:T(8,128)(2,1)S(1)} %add_convert_fusion.5), channel_id=1, source_target_pairs={{0,4},{1,3},{4,8},{5,1},{8,12},{9,5},{12,14},{13,9},{14,10},{15,13... | collective-permute-start | bytes 786440 | tf_op jit(solution)/shard_map/ppermute | solution.py:261
  45.7 11.6 %collective-permute-start.23 = (bf16[64,2048]{1,0:T(8,128)(2,1)S(1)}, bf16[64,2048]{1,0:T(8,128)(2,1)S(1)}, u32[]{:S(2)}, u32[]{:S(2)}) collective-permute-start(bf16[64,2048]{1,0:T(8,128)(2,1)S(1)} %get-tuple-element.63), channel_id=1, source_target_pairs={{0,1},{1,0},{2,3},{3,2},{4,5},{5,4},{6,7},{7,6},{8,9},{9,8},{10,11... | collective-permute-start | bytes 786440 | tf_op jit(solution)/shard_map/ppermute | solution.py:262
  45.9 6.4 %collective-permute-start.21 = (bf16[64,2048]{1,0:T(8,128)(2,1)S(1)}, bf16[64,2048]{1,0:T(8,128)(2,1)S(1)}, u32[]{:S(2)}, u32[]{:S(2)}) collective-permute-start(bf16[64,2048]{1,0:T(8,128)(2,1)S(1)} %add_convert_fusion.4), channel_id=1, source_target_pairs={{0,4},{1,3},{4,8},{5,1},{8,12},{9,5},{12,14},{13,9},{14,10},{15,13... | collective-permute-start | bytes 786440 | tf_op jit(solution)/shard_map/ppermute | solution.py:261
  48.4 6.7 %collective-permute-start.26 = (bf16[64,2048]{1,0:T(8,128)(2,1)S(1)}, bf16[64,2048]{1,0:T(8,128)(2,1)S(1)}, u32[]{:S(2)}, u32[]{:S(2)}) collective-permute-start(bf16[64,2048]{1,0:T(8,128)(2,1)S(1)} %add_convert_fusion.2), channel_id=1, source_target_pairs={{0,4},{1,3},{4,8},{5,1},{8,12},{9,5},{12,14},{13,9},{14,10},{15,13... | collective-permute-start | bytes 786440 | tf_op jit(solution)/shard_map/ppermute | solution.py:261
  52.5 5.9 %collective-permute-start.22 = (bf16[64,2048]{1,0:T(8,128)(2,1)S(1)}, bf16[64,2048]{1,0:T(8,128)(2,1)S(1)}, u32[]{:S(2)}, u32[]{:S(2)}) collective-permute-start(bf16[64,2048]{1,0:T(8,128)(2,1)S(1)} %add_convert_fusion.3), channel_id=1, source_target_pairs={{0,5},{1,2},{4,9},{5,0},{8,13},{9,4},{12,15},{13,8},{14,11},{15,12... | collective-permute-start | bytes 786440 | tf_op jit(solution)/shard_map/ppermute | solution.py:261
  55.3 6.4 %collective-permute-start.27 = (bf16[64,2048]{1,0:T(8,128)(2,1)S(1)}, bf16[64,2048]{1,0:T(8,128)(2,1)S(1)}, u32[]{:S(2)}, u32[]{:S(2)}) collective-permute-start(bf16[64,2048]{1,0:T(8,128)(2,1)S(1)} %add_convert_fusion.1), channel_id=1, source_target_pairs={{0,4},{1,3},{4,8},{5,1},{8,12},{9,5},{12,14},{13,9},{14,10},{15,13... | collective-permute-start | bytes 786440 | tf_op jit(solution)/shard_map/ppermute | solution.py:261

commit v15 on v14

--- a/solution.py
+++ b/solution.py
@@ -75,9 +75,22 @@
     return pairs
 
 
-def expert_kernel(experts, blocks, own_ref, *refs):
-    gate_ref, up_ref, down_ref, *outs = refs[blocks:-2]
-    rows_ref, hidden_ref = refs[-2:]
+def expert_kernel(experts, blocks, load, own_ref, *refs):
+    copies = []
+    if load:
+        gate_ref, up_ref, source, *outs, down_ref = refs[blocks:-3]
+        rows_ref, hidden_ref, done = refs[-3:]
+        depth = source.shape[1] // load
+        for piece in range(load):
+            part = pl.ds(piece * depth, depth)
+            copies.append(
+                pltpu.make_async_copy(source.at[:, part], down_ref.at[:, part], done.at[piece])
+            )
+    else:
+        gate_ref, up_ref, down_ref, *outs = refs[blocks:-2]
+        rows_ref, hidden_ref = refs[-2:]
+    for copy in copies:
+        copy.start()
     width, ff = gate_ref.shape[1:]
     each = outs[0].shape[0]
     at = 0
@@ -96,6 +109,8 @@
     own = own_ref[0]
     mine = (lane == own) | (lane == own + experts)
     weight = jnp.sum(jnp.where(mine, tail, 0.0), axis=1, keepdims=True)
+    for copy in copies:
+        copy.wait()
     step = math.gcd(width, 512)
     for at in range(0, width, step):
         part = slice(at, at + step)
@@ -108,23 +123,33 @@
             target[:, part] = out[number * each : (number + 1) * each]
 
 
-def run_expert(own, blocks, weights, experts, each):
+def run_expert(own, blocks, weights, experts, each, load=False):
     rows = sum(block.shape[0] for block in blocks)
     wide = blocks[0].shape[1]
     width, ff = weights[0].shape[1:]
     vmem = pl.BlockSpec(memory_space=pltpu.VMEM)
+    pieces = math.gcd(width // 16, 4) if load else 0
+    gate_w, up_w, down_w = weights
+    out_shape = [jax.ShapeDtypeStruct((each, width), jnp.bfloat16)] * (rows // each)
+    scratch = [pltpu.VMEM((rows, wide), jnp.bfloat16), pltpu.VMEM((rows, ff), jnp.bfloat16)]
+    place = vmem
+    if load:
+        out_shape.append(pltpu.VMEM(down_w.shape, down_w.dtype))
+        scratch.append(pltpu.SemaphoreType.DMA((pieces,)))
+        place = pl.BlockSpec(memory_space=pltpu.HBM)
+        down_w = pltpu.with_memory_space_constraint(down_w, pltpu.HBM)
     return pl.pallas_call(
-        functools.partial(expert_kernel, experts, len(blocks)),
-        out_shape=[jax.ShapeDtypeStruct((each, width), jnp.bfloat16)] * (rows // each),
-        in_specs=[pl.BlockSpec(memory_space=pltpu.SMEM)] + [vmem] * (len(blocks) + 3),
-        out_specs=[vmem] * (rows // each),
-        scratch_shapes=[pltpu.VMEM((rows, wide), jnp.bfloat16), pltpu.VMEM((rows, ff), jnp.bfloat16)],
+        functools.partial(expert_kernel, experts, len(blocks), pieces),
+        out_shape=out_shape,
+        in_specs=[pl.BlockSpec(memory_space=pltpu.SMEM)] + [vmem] * (len(blocks) + 2) + [place],
+        out_specs=[vmem] * len(out_shape),
+        scratch_shapes=scratch,
         compiler_params=pltpu.CompilerParams(vmem_limit_bytes=16 << 20),
         cost_estimate=pl.CostEstimate(
             flops=rows * width, bytes_accessed=rows * width, transcendentals=0
         ),
         name="expert",
-    )(own, *blocks, *weights)
+    )(own, *blocks, gate_w, up_w, down_w)
 
 
 def load_kernel(pieces, *refs):
@@ -145,7 +170,7 @@
 
 
 def load_weights(weights):
-    pieces = math.gcd(weights[0].shape[1] // 16, 16)
+    pieces = math.gcd(weights[0].shape[1] // 16, 4)
     return pl.pallas_call(
         functools.partial(load_kernel, pieces),
         out_shape=[pltpu.VMEM(w.shape, w.dtype) for w in weights],
@@ -229,20 +254,20 @@
     first, second = ring(mine), ring(sibling)
     gate_w, up_w = load_weights((after(w_gate, sibling), w_up))
     first = after(first, gate_w)
-    down_w, = load_weights((after(w_down, first),))
-    weights = [gate_w, up_w, down_w]
+    weights = [gate_w, up_w, w_down]
     run = lambda *blocks: run_expert(own, blocks, weights, experts, count)
     blocks = {}
     for step in range(1, rounds - 1):
         if step > 1:
             first, second = ring(first), ring(second)
-        if step == 2:
-            first = after(first, down_w)
         blocks[step] = (swap(first), swap(second), first, second)
     far = leap(first)
     both = ring(jnp.concatenate([first, second], 0))
     turned = lambda keep, keep_trail, send, send_trail: (keep_trail, keep, swap(send_trail), swap(send))
-    sums = {2: run(after(blocks[2][0], *blocks[1][:2]), *blocks[2][1:])}
+    blocks[2] = (after(blocks[2][0], *blocks[1][:2]), *blocks[2][1:])
+    *sums, down_w = run_expert(own, blocks[2], weights, experts, count, True)
+    weights = [gate_w, up_w, down_w]
+    sums = {2: sums}
     sums[1] = run(after(blocks[1][0], sums[2][0]), *blocks[1][1:])
     far = after(far, sums[1][0])
     sums[2], sums[1] = turned(*sums[2]), turned(*sums[1])

time: 62.6 us -> 62.9 us (level)
  waiting for transfers between devices: 12.7 us -> 15.3 us
  Pallas kernels: 19 us -> 17.8 us
  starting transfers between devices: 29.1 us -> 28 us
    ppermute x6, starting transfers between devices: 11.6 us -> 8.99 us  [dense_body(): lead, trail = ([(ring if step > 1 else home)(lead[0])], [ring(trail[0])])]
    pallas_call x2 -> x1, Pallas kernels: 5.22 us -> 2.86 us  [load_weights(): pl.pallas_call(functools.partial(load_kernel, pieces), out_shape=[pltpu.V...]
    ppermute x6, waiting for transfers between devices: 8.25 us -> 10.6 us  [dense_body(): lead, trail = ([(ring if step > 1 else home)(lead[0])], [ring(trail[0])])]
    pallas_call x5, Pallas kernels: 12.1 us -> 13.2 us  [run_expert(): pl.pallas_call(functools.partial(expert_kernel, experts, len(blocks), pie...]
    ppermute x2, waiting for transfers between devices: 0.01 us -> 0.95 us  [dense_body(): first, second = (ring(first), ring(second))]
  transfers between devices with their start and end apart: 28 -> 28, of which waited for: 12 -> 12; matrix products, arithmetic and copies ran while one was open for 1% -> 1% of each run, Pallas kernels for 28% -> 26%
where the time goes in v15:
time: 62.9 us; the launch traced here: 62.7 us
  starting transfers between devices  28 us (45%)
  Pallas kernels  17.8 us (28%)
  waiting for transfers between devices  15.3 us (24%)
  other arithmetic  1.51 us (2%)
    pallas_call x5, Pallas kernels, run_expert(): pl.pallas_call(functools.partial(expert_kernel, experts, len(blocks), pie...  13.2 us
    ppermute x6, waiting for transfers between devices, dense_body(): lead, trail = ([(ring if step > 1 else home)(lead[0])], [ring(trail[0])])  10.6 us
    ppermute x6, starting transfers between devices, dense_body(): lead, trail = ([(ring if step > 1 else home)(lead[0])], [ring(trail[0])])  8.99 us
    ppermute x2, starting transfers between devices, dense_body(): first, second = (ring(mine), ring(sibling))  4.34 us
    ppermute x2, starting transfers between devices, dense_body(): first, second = (ring(first), ring(second))  4.21 us
    ppermute x1, starting transfers between devices, dense_body(): far = leap(first)  3.12 us
    pallas_call x1, Pallas kernels, load_weights(): pl.pallas_call(functools.partial(load_kernel, pieces), out_shape=[pltpu.V...  2.86 us
    ppermute x1, starting transfers between devices, dense_body(): both = ring(jnp.concatenate([first, second], 0))  1.88 us
  transfers between devices with their start and end apart: 28, of which 12 were waited for; matrix products, arithmetic and copies ran while one was open for 1% of the time, Pallas kernels for 26%

profile of v15, /device:TPU:0, one launch (start us, length us, event | category | flops | bytes accessed | tf_op | source)
XLA Modules:
  0.0 62.7 jit_solution(17727193767574949441)
XLA Ops:
  0.0 1.7 %pack.1.refs_0_ = bf16[64,2176]{1,0:T(8,128)(2,1)} custom-call(bf16[64,2048]{1,0:T(8,128)(2,1)} %tokens_ref, s32[8,64]{1,0:T(8,128)} %bitcast.3, f32[8,64]{1,0:T(8,128)} %bitcast.4), custom_call_target="tpu_custom_call" | custom-call | bytes 1024 | tf_op jit(solution)/shard_map/pack/pallas_call | solution.py:216
  1.7 0.5 collective-permute-start.1
  2.2 2.6 %collective-permute-start = (bf16[64,2176]{1,0:T(8,128)(2,1)}, bf16[64,2176]{1,0:T(8,128)(2,1)S(1)}, u32[]{:S(2)}, u32[]{:S(2)}) collective-permute-start(bf16[64,2176]{1,0:T(8,128)(2,1)} %pack.1.refs_0_), channel_id=1, source_target_pairs={{0,4},{1,3},{4,8},{5,1},{8,12},{9,5},{12,14},{13,9},{14,10},{15,13... | collective-permute-start | bytes 835592 | tf_op jit(solution)/shard_map/ppermute | solution.py:254
  4.9 0.0 collective-permute-done.1.refs_1_
  4.9 1.7 %collective-permute-start.5 = (bf16[64,2176]{1,0:T(8,128)(2,1)S(1)}, bf16[64,2176]{1,0:T(8,128)(2,1)S(1)}, u32[]{:S(2)}, u32[]{:S(2)}) collective-permute-start(bf16[64,2176]{1,0:T(8,128)(2,1)S(1)} %collective-permute-done.1.refs_1_), channel_id=1, source_target_pairs={{0,4},{1,3},{4,8},{5,1},{8,12},{9,5},{12,14},{13,9},{14,10},{15,13... | collective-permute-start | bytes 835592 | tf_op jit(solution)/shard_map/ppermute | solution.py:254
  6.6 2.9 %load.1 = (bf16[1,2048,768]{2,1,0:T(8,128)(2,1)S(1)}, bf16[1,2048,768]{2,1,0:T(8,128)(2,1)S(1)}) custom-call(bf16[1,2048,768]{2,1,0:T(8,128)(2,1)} %refs_0_, bf16[1,2048,768]{2,1,0:T(8,128)(2,1)} %refs_1_.1), custom_call_target="tpu_custom_call" | custom-call | bytes 1024 | tf_op jit(solution)/shard_map/load/pallas_call | solution.py:174
  9.4 0.1 collective-permute-done.refs_2_
  9.5 2.1 %collective-permute-start.3 = (bf16[64,2176]{1,0:T(8,128)(2,1)S(1)}, bf16[64,2176]{1,0:T(8,128)(2,1)S(1)}, u32[]{:S(2)}, u32[]{:S(2)}) collective-permute-start(bf16[64,2176]{1,0:T(8,128)(2,1)S(1)} %collective-permute-done.refs_2_), channel_id=1, source_target_pairs={{0,4},{1,3},{4,8},{5,1},{8,12},{9,5},{12,14},{13,9},{14,10},{15,13... | collective-permute-start | bytes 835592 | tf_op jit(solution)/shard_map/ppermute | solution.py:262
  11.6 0.9 %collective-permute-done.5.refs_3_ = bf16[64,2176]{1,0:T(8,128)(2,1)S(1)} collective-permute-done((bf16[64,2176]{1,0:T(8,128)(2,1)S(1)}, bf16[64,2176]{1,0:T(8,128)(2,1)S(1)}, u32[]{:S(2)}, u32[]{:S(2)}) %collective-permute-start.5) | collective-permute-done | bytes 278560 | tf_op jit(solution)/shard_map/ppermute | solution.py:254
  12.5 2.1 %collective-permute-start.7 = (bf16[64,2176]{1,0:T(8,128)(2,1)S(1)}, bf16[64,2176]{1,0:T(8,128)(2,1)S(1)}, u32[]{:S(2)}, u32[]{:S(2)}) collective-permute-start(bf16[64,2176]{1,0:T(8,128)(2,1)S(1)} %collective-permute-done.5.refs_3_), channel_id=1, source_target_pairs={{0,4},{1,3},{4,8},{5,1},{8,12},{9,5},{12,14},{13,9},{14,10},{15,13... | collective-permute-start | bytes 835592 | tf_op jit(solution)/shard_map/ppermute | solution.py:262
  14.6 0.0 collective-permute-start.2
  14.6 0.5 collective-permute-start.6
  15.1 0.9 %collective-permute-done.3.refs_2_ = bf16[64,2176]{1,0:T(8,128)(2,1)S(1)} collective-permute-done((bf16[64,2176]{1,0:T(8,128)(2,1)S(1)}, bf16[64,2176]{1,0:T(8,128)(2,1)S(1)}, u32[]{:S(2)}, u32[]{:S(2)}) %collective-permute-start.3) | collective-permute-done | bytes 278560 | tf_op jit(solution)/shard_map/ppermute | solution.py:262
  16.1 0.0 collective-permute-start.4
  16.1 3.1 %collective-permute-start.13 = (bf16[64,2176]{1,0:T(8,128)(2,1)S(1)}, bf16[64,2176]{1,0:T(8,128)(2,1)S(1)}, u32[]{:S(2)}, u32[]{:S(2)}) collective-permute-start(bf16[64,2176]{1,0:T(8,128)(2,1)S(1)} %collective-permute-done.3.refs_2_), channel_id=1, source_target_pairs={{0,8},{1,7},{4,12},{5,3},{8,14},{9,1},{12,10},{13,5},{14,6},{15,9}... | collective-permute-start | bytes 835592 | tf_op jit(solution)/shard_map/ppermute | solution.py:264
  19.2 0.0 collective-permute-done.7.refs_3_
  19.2 0.1 collective-permute-start.8
  19.4 0.0 collective-permute-done.2.refs_0_
  19.4 1.9 %collective-permute-start.11 = (bf16[128,2176]{1,0:T(8,128)(2,1)S(1)}, bf16[128,2176]{1,0:T(8,128)(2,1)S(1)}, u32[]{:S(2)}, u32[]{:S(2)}) collective-permute-start(bf16[128,2176]{1,0:T(8,128)(2,1)S(1)} %pad_maximum_fusion), channel_id=1, source_target_pairs={{0,4},{1,3},{4,8},{5,1},{8,12},{9,5},{12,14},{13,9},{14,10},{15,13... | collective-permute-start | bytes 1671176 | tf_op jit(solution)/shard_map/ppermute | solution.py:265
  21.3 0.0 collective-permute-done.4.refs_0_
  21.3 0.0 collective-permute-done.6.refs_1_
  21.3 0.0 collective-permute-done.8.refs_1_
  21.3 3.9 %expert.5 = (bf16[64,2048]{1,0:T(8,128)(2,1)S(1)}, bf16[64,2048]{1,0:T(8,128)(2,1)S(1)}, bf16[64,2048]{1,0:T(8,128)(2,1)S(1)}, bf16[64,2048]{1,0:T(8,128)(2,1)S(1)}, bf16[1,2048,768]{2,1,0:T(8,128)(2,1)S(1)}) custom-call(s32[1]{0:T(128)} %bitcast.own_ref, bf16[64,2176]{1,0:T(8,128)(2,1)S(1)} %collective-permute-done.4.refs_0_, ...), custom_call_target="tpu_custom_call" | custom-call | flops 524288 | bytes 524288 | tf_op jit(solution)/shard_map/expert/pallas_call | solution.py:141
  25.1 2.6 %expert.6 = (bf16[64,2048]{1,0:T(8,128)(2,1)S(1)}, bf16[64,2048]{1,0:T(8,128)(2,1)S(1)}, bf16[64,2048]{1,0:T(8,128)(2,1)S(1)}, bf16[64,2048]{1,0:T(8,128)(2,1)S(1)}) custom-call(s32[1]{0:T(128)} %bitcast.own_ref, bf16[64,2176]{1,0:T(8,128)(2,1)S(1)} %collective-permute-done.2.refs_0_, bf16[64,2176]{1,0:T(8,128)(2,1)S(1)} %collective-permute-done.6.refs_1_, ...), custom_call_target="tpu_custom_call" | custom-call | flops 524288 | bytes 524288 | tf_op jit(solution)/shard_map/expert/pallas_call | solution.py:141
  27.8 0.2 collective-permute-start.14
  28.0 1.4 %collective-permute-done.14.refs_0_ = bf16[64,2176]{1,0:T(8,128)(2,1)S(1)} collective-permute-done((bf16[64,2176]{1,0:T(8,128)(2,1)S(1)}, bf16[64,2176]{1,0:T(8,128)(2,1)S(1)}, u32[]{:S(2)}, u32[]{:S(2)}) %collective-permute-start.14) | collective-permute-done | bytes 278560 | tf_op jit(solution)/shard_map/ppermute | solution.py:274
  29.4 2.0 %expert.7 = (bf16[64,2048]{1,0:T(8,128)(2,1)S(1)}, bf16[64,2048]{1,0:T(8,128)(2,1)S(1)}) custom-call(s32[1]{0:T(128)} %bitcast.own_ref, bf16[64,2176]{1,0:T(8,128)(2,1)S(1)} %collective-permute-done.14.refs_0_, bf16[64,2176]{1,0:T(8,128)(2,1)S(1)} %collective-permute-done.13.refs_1_, bf16[1,2048,768]{2,1,0:T(8,128)(2,1)S(1)} %get-tuple-element.38.refs_4_.refs_2_, ...), custom_call_target="tpu_custom_call" | custom-call | flops 262144 | bytes 262144 | tf_op jit(solution)/shard_map/expert/pallas_call | solution.py:141
  31.5 0.2 collective-permute-start.15
  31.7 0.0 collective-permute-done.11.refs_1_
  31.7 0.6 collective-permute-start.12
  32.3 0.0 collective-permute-start.10
  32.3 0.5 collective-permute-start.16
  32.8 0.3 collective-permute-done.15
  33.1 0.1 add_convert_fusion.7
  33.2 1.6 %collective-permute-start.18 = (bf16[64,2048]{1,0:T(8,128)(2,1)S(1)}, bf16[64,2048]{1,0:T(8,128)(2,1)S(1)}, u32[]{:S(2)}, u32[]{:S(2)}) collective-permute-start(bf16[64,2048]{1,0:T(8,128)(2,1)S(1)} %add_convert_fusion.7), channel_id=1, source_target_pairs={{0,4},{1,3},{4,8},{5,1},{8,12},{9,5},{12,14},{13,9},{14,10},{15,13... | collective-permute-start | bytes 786440 | tf_op jit(solution)/shard_map/ppermute | solution.py:277
  34.8 0.0 collective-permute-done.10
  34.8 2.6 %expert.8 = (bf16[64,2048]{1,0:T(8,128)(2,1)S(1)}, bf16[64,2048]{1,0:T(8,128)(2,1)S(1)}, bf16[64,2048]{1,0:T(8,128)(2,1)S(1)}, bf16[64,2048]{1,0:T(8,128)(2,1)S(1)}) custom-call(s32[1]{0:T(128)} %bitcast.own_ref, bf16[128,2176]{1,0:T(8,128)(2,1)S(1)} %collective-permute-done.12.refs_0_, bf16[128,2176]{1,0:T(8,128)(2,1)S(1)} %collective-permute-done.11.refs_1_, ...), custom_call_target="tpu_custom_call" | custom-call | flops 524288 | bytes 524288 | tf_op jit(solution)/shard_map/expert/pallas_call | solution.py:141
  37.5 0.3 collective-permute-start.17
  37.7 0.3 collective-permute-start.9
  38.0 0.2 collective-permute-start.24
  38.2 0.3 collective-permute-start.20
  38.5 1.0 %collective-permute-done.18 = bf16[64,2048]{1,0:T(8,128)(2,1)S(1)} collective-permute-done((bf16[64,2048]{1,0:T(8,128)(2,1)S(1)}, bf16[64,2048]{1,0:T(8,128)(2,1)S(1)}, u32[]{:S(2)}, u32[]{:S(2)}) %collective-permute-start.18) | collective-permute-done | bytes 262176 | tf_op jit(solution)/shard_map/ppermute | solution.py:277
  39.6 0.1 add_convert_fusion.6
  39.7 1.6 %collective-permute-start.19 = (bf16[64,2048]{1,0:T(8,128)(2,1)S(1)}, bf16[64,2048]{1,0:T(8,128)(2,1)S(1)}, u32[]{:S(2)}, u32[]{:S(2)}) collective-permute-start(bf16[64,2048]{1,0:T(8,128)(2,1)S(1)} %add_convert_fusion.6), channel_id=1, source_target_pairs={{0,4},{1,3},{4,8},{5,1},{8,12},{9,5},{12,14},{13,9},{14,10},{15,13... | collective-permute-start | bytes 786440 | tf_op jit(solution)/shard_map/ppermute | solution.py:286
  41.3 0.1 add_convert_fusion.5
  41.4 2.1 %collective-permute-start.25 = (bf16[64,2048]{1,0:T(8,128)(2,1)S(1)}, bf16[64,2048]{1,0:T(8,128)(2,1)S(1)}, u32[]{:S(2)}, u32[]{:S(2)}) collective-permute-start(bf16[64,2048]{1,0:T(8,128)(2,1)S(1)} %add_convert_fusion.5), channel_id=1, source_target_pairs={{0,4},{1,3},{4,8},{5,1},{8,12},{9,5},{12,14},{13,9},{14,10},{15,13... | collective-permute-start | bytes 786440 | tf_op jit(solution)/shard_map/ppermute | solution.py:286
  43.5 2.0 %expert.9 = (bf16[64,2048]{1,0:T(8,128)(2,1)S(1)}, bf16[64,2048]{1,0:T(8,128)(2,1)S(1)}) custom-call(s32[1]{0:T(128)} %bitcast.own_ref, bf16[64,2176]{1,0:T(8,128)(2,1)S(1)} %copy-done, bf16[64,2176]{1,0:T(8,128)(2,1)S(1)} %collective-permute-done.1.refs_1_, bf16[1,2048,768]{2,1,0:T(8,128)(2,1)S(1)} %get-tuple-element.38.refs_4_.refs_2_, ...), custom_call_target="tpu_custom_call" | custom-call | flops 262144 | bytes 262144 | tf_op jit(solution)/shard_map/expert/pallas_call | solution.py:141
  45.5 0.1 collective-permute-start.23
  45.6 0.5 collective-permute-done.19
  46.1 0.1 add_convert_fusion.4
  46.2 1.6 %collective-permute-start.21 = (bf16[64,2048]{1,0:T(8,128)(2,1)S(1)}, bf16[64,2048]{1,0:T(8,128)(2,1)S(1)}, u32[]{:S(2)}, u32[]{:S(2)}) collective-permute-start(bf16[64,2048]{1,0:T(8,128)(2,1)S(1)} %add_convert_fusion.4), channel_id=1, source_target_pairs={{0,4},{1,3},{4,8},{5,1},{8,12},{9,5},{12,14},{13,9},{14,10},{15,13... | collective-permute-start | bytes 786440 | tf_op jit(solution)/shard_map/ppermute | solution.py:286
  47.9 1.1 %collective-permute-done.25 = bf16[64,2048]{1,0:T(8,128)(2,1)S(1)} collective-permute-done((bf16[64,2048]{1,0:T(8,128)(2,1)S(1)}, bf16[64,2048]{1,0:T(8,128)(2,1)S(1)}, u32[]{:S(2)}, u32[]{:S(2)}) %collective-permute-start.25) | collective-permute-done | bytes 262176 | tf_op jit(solution)/shard_map/ppermute | solution.py:286
  48.9 0.1 add_convert_fusion.2
  49.0 1.6 %collective-permute-start.26 = (bf16[64,2048]{1,0:T(8,128)(2,1)S(1)}, bf16[64,2048]{1,0:T(8,128)(2,1)S(1)}, u32[]{:S(2)}, u32[]{:S(2)}) collective-permute-start(bf16[64,2048]{1,0:T(8,128)(2,1)S(1)} %add_convert_fusion.2), channel_id=1, source_target_pairs={{0,4},{1,3},{4,8},{5,1},{8,12},{9,5},{12,14},{13,9},{14,10},{15,13... | collective-permute-start | bytes 786440 | tf_op jit(solution)/shard_map/ppermute | solution.py:286
  50.7 2.0 %collective-permute-done.21 = bf16[64,2048]{1,0:T(8,128)(2,1)S(1)} collective-permute-done((bf16[64,2048]{1,0:T(8,128)(2,1)S(1)}, bf16[64,2048]{1,0:T(8,128)(2,1)S(1)}, u32[]{:S(2)}, u32[]{:S(2)}) %collective-permute-start.21) | collective-permute-done | bytes 262176 | tf_op jit(solution)/shard_map/ppermute | solution.py:286
  52.6 0.1 add_convert_fusion.3
  52.7 0.4 collective-permute-start.22
  53.1 2.3 %collective-permute-done.26 = bf16[64,2048]{1,0:T(8,128)(2,1)S(1)} collective-permute-done((bf16[64,2048]{1,0:T(8,128)(2,1)S(1)}, bf16[64,2048]{1,0:T(8,128)(2,1)S(1)}, u32[]{:S(2)}, u32[]{:S(2)}) %collective-permute-start.26) | collective-permute-done | bytes 262176 | tf_op jit(solution)/shard_map/ppermute | solution.py:286
  55.5 0.1 add_convert_fusion.1
  55.6 1.6 %collective-permute-start.27 = (bf16[64,2048]{1,0:T(8,128)(2,1)S(1)}, bf16[64,2048]{1,0:T(8,128)(2,1)S(1)}, u32[]{:S(2)}, u32[]{:S(2)}) collective-permute-start(bf16[64,2048]{1,0:T(8,128)(2,1)S(1)} %add_convert_fusion.1), channel_id=1, source_target_pairs={{0,4},{1,3},{4,8},{5,1},{8,12},{9,5},{12,14},{13,9},{14,10},{15,13... | collective-permute-start | bytes 786440 | tf_op jit(solution)/shard_map/ppermute | solution.py:286
  57.2 1.4 %collective-permute-done.22 = bf16[64,2048]{1,0:T(8,128)(2,1)S(1)} collective-permute-done((bf16[64,2048]{1,0:T(8,128)(2,1)S(1)}, bf16[64,2048]{1,0:T(8,128)(2,1)S(1)}, u32[]{:S(2)}, u32[]{:S(2)}) %collective-permute-start.22) | collective-permute-done | bytes 262176 | tf_op jit(solution)/shard_map/ppermute | solution.py:286
  58.6 0.1 convert_add_fusion
  58.7 3.3 %collective-permute-done.27 = bf16[64,2048]{1,0:T(8,128)(2,1)S(1)} collective-permute-done((bf16[64,2048]{1,0:T(8,128)(2,1)S(1)}, bf16[64,2048]{1,0:T(8,128)(2,1)S(1)}, u32[]{:S(2)}, u32[]{:S(2)}) %collective-permute-start.27) | collective-permute-done | bytes 262176 | tf_op jit(solution)/shard_map/ppermute | solution.py:286
  62.0 0.8 %add_convert_fusion = bf16[64,2048]{1,0:T(8,128)(2,1)} fusion(f32[64,2048]{1,0:T(8,128)S(1)} %convert_add_fusion, bf16[64,2048]{1,0:T(8,128)(2,1)S(1)} %collective-permute-done.27), kind=kLoop, calls=%fused_computation.1 | loop fusion | flops 393216 | bytes 1048576 | tf_op jit(solution)/shard_map/convert_element_type | solution.py:235
  (11 shorter events, 0.1 us)
Async XLA Ops:
  1.7 3.2 %collective-permute-start.1 = (bf16[64,2176]{1,0:T(8,128)(2,1)}, bf16[64,2176]{1,0:T(8,128)(2,1)S(1)}, u32[]{:S(2)}, u32[]{:S(2)}) collective-permute-start(bf16[64,2176]{1,0:T(8,128)(2,1)} %pack.1.refs_0_), channel_id=1, source_target_pairs={{0,1},{1,0},{2,3},{3,2},{4,5},{5,4},{6,7},{7,6},{8,9},{9,8},{10,11... | collective-permute-start | bytes 835592 | tf_op jit(solution)/shard_map/ppermute | solution.py:253
  2.2 7.3 %collective-permute-start = (bf16[64,2176]{1,0:T(8,128)(2,1)}, bf16[64,2176]{1,0:T(8,128)(2,1)S(1)}, u32[]{:S(2)}, u32[]{:S(2)}) collective-permute-start(bf16[64,2176]{1,0:T(8,128)(2,1)} %pack.1.refs_0_), channel_id=1, source_target_pairs={{0,4},{1,3},{4,8},{5,1},{8,12},{9,5},{12,14},{13,9},{14,10},{15,13... | collective-permute-start | bytes 835592 | tf_op jit(solution)/shard_map/ppermute | solution.py:254
  4.9 7.6 %collective-permute-start.5 = (bf16[64,2176]{1,0:T(8,128)(2,1)S(1)}, bf16[64,2176]{1,0:T(8,128)(2,1)S(1)}, u32[]{:S(2)}, u32[]{:S(2)}) collective-permute-start(bf16[64,2176]{1,0:T(8,128)(2,1)S(1)} %collective-permute-done.1.refs_1_), channel_id=1, source_target_pairs={{0,4},{1,3},{4,8},{5,1},{8,12},{9,5},{12,14},{13,9},{14,10},{15,13... | collective-permute-start | bytes 835592 | tf_op jit(solution)/shard_map/ppermute | solution.py:254
  9.5 6.5 %collective-permute-start.3 = (bf16[64,2176]{1,0:T(8,128)(2,1)S(1)}, bf16[64,2176]{1,0:T(8,128)(2,1)S(1)}, u32[]{:S(2)}, u32[]{:S(2)}) collective-permute-start(bf16[64,2176]{1,0:T(8,128)(2,1)S(1)} %collective-permute-done.refs_2_), channel_id=1, source_target_pairs={{0,4},{1,3},{4,8},{5,1},{8,12},{9,5},{12,14},{13,9},{14,10},{15,13... | collective-permute-start | bytes 835592 | tf_op jit(solution)/shard_map/ppermute | solution.py:262
  12.5 6.7 %collective-permute-start.7 = (bf16[64,2176]{1,0:T(8,128)(2,1)S(1)}, bf16[64,2176]{1,0:T(8,128)(2,1)S(1)}, u32[]{:S(2)}, u32[]{:S(2)}) collective-permute-start(bf16[64,2176]{1,0:T(8,128)(2,1)S(1)} %collective-permute-done.5.refs_3_), channel_id=1, source_target_pairs={{0,4},{1,3},{4,8},{5,1},{8,12},{9,5},{12,14},{13,9},{14,10},{15,13... | collective-permute-start | bytes 835592 | tf_op jit(solution)/shard_map/ppermute | solution.py:262
  14.6 4.8 %collective-permute-start.2 = (bf16[64,2176]{1,0:T(8,128)(2,1)S(1)}, bf16[64,2176]{1,0:T(8,128)(2,1)S(1)}, u32[]{:S(2)}, u32[]{:S(2)}) collective-permute-start(bf16[64,2176]{1,0:T(8,128)(2,1)S(1)} %collective-permute-done.refs_2_), channel_id=1, source_target_pairs={{0,1},{1,0},{2,3},{3,2},{4,5},{5,4},{6,7},{7,6},{8,9},{9,8},{10,11... | collective-permute-start | bytes 835592 | tf_op jit(solution)/shard_map/ppermute | solution.py:263
  14.6 6.7 %collective-permute-start.6 = (bf16[64,2176]{1,0:T(8,128)(2,1)S(1)}, bf16[64,2176]{1,0:T(8,128)(2,1)S(1)}, u32[]{:S(2)}, u32[]{:S(2)}) collective-permute-start(bf16[64,2176]{1,0:T(8,128)(2,1)S(1)} %collective-permute-done.5.refs_3_), channel_id=1, source_target_pairs={{0,1},{1,0},{2,3},{3,2},{4,5},{5,4},{6,7},{7,6},{8,9},{9,8},{10,11... | collective-permute-start | bytes 835592 | tf_op jit(solution)/shard_map/ppermute | solution.py:263
  16.1 5.2 %collective-permute-start.4 = (bf16[64,2176]{1,0:T(8,128)(2,1)S(1)}, bf16[64,2176]{1,0:T(8,128)(2,1)S(1)}, u32[]{:S(2)}, u32[]{:S(2)}) collective-permute-start(bf16[64,2176]{1,0:T(8,128)(2,1)S(1)} %collective-permute-done.3.refs_2_), channel_id=1, source_target_pairs={{0,1},{1,0},{2,3},{3,2},{4,5},{5,4},{6,7},{7,6},{8,9},{9,8},{10,11... | collective-permute-start | bytes 835592 | tf_op jit(solution)/shard_map/ppermute | solution.py:263
  16.1 11.7 %collective-permute-start.13 = (bf16[64,2176]{1,0:T(8,128)(2,1)S(1)}, bf16[64,2176]{1,0:T(8,128)(2,1)S(1)}, u32[]{:S(2)}, u32[]{:S(2)}) collective-permute-start(bf16[64,2176]{1,0:T(8,128)(2,1)S(1)} %collective-permute-done.3.refs_2_), channel_id=1, source_target_pairs={{0,8},{1,7},{4,12},{5,3},{8,14},{9,1},{12,10},{13,5},{14,6},{15,9}... | collective-permute-start | bytes 835592 | tf_op jit(solution)/shard_map/ppermute | solution.py:264
  19.2 2.1 %collective-permute-start.8 = (bf16[64,2176]{1,0:T(8,128)(2,1)S(1)}, bf16[64,2176]{1,0:T(8,128)(2,1)S(1)}, u32[]{:S(2)}, u32[]{:S(2)}) collective-permute-start(bf16[64,2176]{1,0:T(8,128)(2,1)S(1)} %collective-permute-done.7.refs_3_), channel_id=1, source_target_pairs={{0,1},{1,0},{2,3},{3,2},{4,5},{5,4},{6,7},{7,6},{8,9},{9,8},{10,11... | collective-permute-start | bytes 835592 | tf_op jit(solution)/shard_map/ppermute | solution.py:263
  19.4 12.3 %collective-permute-start.11 = (bf16[128,2176]{1,0:T(8,128)(2,1)S(1)}, bf16[128,2176]{1,0:T(8,128)(2,1)S(1)}, u32[]{:S(2)}, u32[]{:S(2)}) collective-permute-start(bf16[128,2176]{1,0:T(8,128)(2,1)S(1)} %pad_maximum_fusion), channel_id=1, source_target_pairs={{0,4},{1,3},{4,8},{5,1},{8,12},{9,5},{12,14},{13,9},{14,10},{15,13... | collective-permute-start | bytes 1671176 | tf_op jit(solution)/shard_map/ppermute | solution.py:265
  27.8 1.6 %collective-permute-start.14 = (bf16[64,2176]{1,0:T(8,128)(2,1)S(1)}, bf16[64,2176]{1,0:T(8,128)(2,1)S(1)}, u32[]{:S(2)}, u32[]{:S(2)}) collective-permute-start(bf16[64,2176]{1,0:T(8,128)(2,1)S(1)} %collective-permute-done.13.refs_1_), channel_id=1, source_target_pairs={{0,1},{1,0},{2,3},{3,2},{4,5},{5,4},{6,7},{7,6},{8,9},{9,8},{10,11... | collective-permute-start | bytes 835592 | tf_op jit(solution)/shard_map/ppermute | solution.py:274
  31.5 1.6 %collective-permute-start.15 = (bf16[64,2048]{1,0:T(8,128)(2,1)S(1)}, bf16[64,2048]{1,0:T(8,128)(2,1)S(1)}, u32[]{:S(2)}, u32[]{:S(2)}) collective-permute-start(bf16[64,2048]{1,0:T(8,128)(2,1)S(1)} %get-tuple-element.50), channel_id=1, source_target_pairs={{0,1},{1,0},{2,3},{3,2},{4,5},{5,4},{6,7},{7,6},{8,9},{9,8},{10,11... | collective-permute-start | bytes 786440 | tf_op jit(solution)/shard_map/ppermute | solution.py:275
  31.7 3.1 %collective-permute-start.12 = (bf16[128,2176]{1,0:T(8,128)(2,1)S(1)}, bf16[128,2176]{1,0:T(8,128)(2,1)S(1)}, u32[]{:S(2)}, u32[]{:S(2)}) collective-permute-start(bf16[128,2176]{1,0:T(8,128)(2,1)S(1)} %collective-permute-done.11.refs_1_), channel_id=1, source_target_pairs={{0,1},{1,0},{2,3},{3,2},{4,5},{5,4},{6,7},{7,6},{8,9},{9,8},{10,11... | collective-permute-start | bytes 1671176 | tf_op jit(solution)/shard_map/ppermute | solution.py:276
  32.3 2.5 %collective-permute-start.10 = (bf16[64,2048]{1,0:T(8,128)(2,1)S(1)}, bf16[64,2048]{1,0:T(8,128)(2,1)S(1)}, u32[]{:S(2)}, u32[]{:S(2)}) collective-permute-start(bf16[64,2048]{1,0:T(8,128)(2,1)S(1)} %get-tuple-element.47), channel_id=1, source_target_pairs={{0,1},{1,0},{2,3},{3,2},{4,5},{5,4},{6,7},{7,6},{8,9},{9,8},{10,11... | collective-permute-start | bytes 786440 | tf_op jit(solution)/shard_map/ppermute | solution.py:266
  32.3 2.5 %collective-permute-start.16 = (bf16[64,2048]{1,0:T(8,128)(2,1)S(1)}, bf16[64,2048]{1,0:T(8,128)(2,1)S(1)}, u32[]{:S(2)}, u32[]{:S(2)}) collective-permute-start(bf16[64,2048]{1,0:T(8,128)(2,1)S(1)} %get-tuple-element.51), channel_id=1, source_target_pairs={{0,1},{1,0},{2,3},{3,2},{4,5},{5,4},{6,7},{7,6},{8,9},{9,8},{10,11... | collective-permute-start | bytes 786440 | tf_op jit(solution)/shard_map/ppermute | solution.py:266
  33.2 10.3 %copy-start = (bf16[64,2176]{1,0:T(8,128)(2,1)S(1)}, bf16[64,2176]{1,0:T(8,128)(2,1)}, u32[]{:S(2)}) copy-start(bf16[64,2176]{1,0:T(8,128)(2,1)} %pack.1.refs_0_) | copy-start | bytes 835588
  33.2 6.4 %collective-permute-start.18 = (bf16[64,2048]{1,0:T(8,128)(2,1)S(1)}, bf16[64,2048]{1,0:T(8,128)(2,1)S(1)}, u32[]{:S(2)}, u32[]{:S(2)}) collective-permute-start(bf16[64,2048]{1,0:T(8,128)(2,1)S(1)} %add_convert_fusion.7), channel_id=1, source_target_pairs={{0,4},{1,3},{4,8},{5,1},{8,12},{9,5},{12,14},{13,9},{14,10},{15,13... | collective-permute-start | bytes 786440 | tf_op jit(solution)/shard_map/ppermute | solution.py:277
  37.5 2.1 %collective-permute-start.17 = (bf16[64,2048]{1,0:T(8,128)(2,1)S(1)}, bf16[64,2048]{1,0:T(8,128)(2,1)S(1)}, u32[]{:S(2)}, u32[]{:S(2)}) collective-permute-start(bf16[64,2048]{1,0:T(8,128)(2,1)S(1)} %get-tuple-element.54), channel_id=1, source_target_pairs={{0,1},{1,0},{2,3},{3,2},{4,5},{5,4},{6,7},{7,6},{8,9},{9,8},{10,11... | collective-permute-start | bytes 786440 | tf_op jit(solution)/shard_map/ppermute | solution.py:266
  37.7 12.9 %collective-permute-start.9 = (bf16[64,2048]{1,0:T(8,128)(2,1)S(1)}, bf16[64,2048]{1,0:T(8,128)(2,1)S(1)}, u32[]{:S(2)}, u32[]{:S(2)}) collective-permute-start(bf16[64,2048]{1,0:T(8,128)(2,1)S(1)} %get-tuple-element.46), channel_id=1, source_target_pairs={{0,1},{1,0},{2,3},{3,2},{4,5},{5,4},{6,7},{7,6},{8,9},{9,8},{10,11... | collective-permute-start | bytes 786440 | tf_op jit(solution)/shard_map/ppermute | solution.py:266
  38.0 15.1 %collective-permute-start.24 = (bf16[64,2048]{1,0:T(8,128)(2,1)S(1)}, bf16[64,2048]{1,0:T(8,128)(2,1)S(1)}, u32[]{:S(2)}, u32[]{:S(2)}) collective-permute-start(bf16[64,2048]{1,0:T(8,128)(2,1)S(1)} %get-tuple-element.64), channel_id=1, source_target_pairs={{0,1},{1,0},{2,3},{3,2},{4,5},{5,4},{6,7},{7,6},{8,9},{9,8},{10,11... | collective-permute-start | bytes 786440 | tf_op jit(solution)/shard_map/ppermute | solution.py:266
  38.2 3.1 %collective-permute-start.20 = (bf16[64,2048]{1,0:T(8,128)(2,1)S(1)}, bf16[64,2048]{1,0:T(8,128)(2,1)S(1)}, u32[]{:S(2)}, u32[]{:S(2)}) collective-permute-start(bf16[64,2048]{1,0:T(8,128)(2,1)S(1)} %get-tuple-element.57), channel_id=1, source_target_pairs={{0,1},{1,0},{2,3},{3,2},{4,5},{5,4},{6,7},{7,6},{8,9},{9,8},{10,11... | collective-permute-start | bytes 786440 | tf_op jit(solution)/shard_map/ppermute | solution.py:266
  39.7 6.4 %collective-permute-start.19 = (bf16[64,2048]{1,0:T(8,128)(2,1)S(1)}, bf16[64,2048]{1,0:T(8,128)(2,1)S(1)}, u32[]{:S(2)}, u32[]{:S(2)}) collective-permute-start(bf16[64,2048]{1,0:T(8,128)(2,1)S(1)} %add_convert_fusion.6), channel_id=1, source_target_pairs={{0,4},{1,3},{4,8},{5,1},{8,12},{9,5},{12,14},{13,9},{14,10},{15,13... | collective-permute-start | bytes 786440 | tf_op jit(solution)/shard_map/ppermute | solution.py:286
  41.4 7.5 %collective-permute-start.25 = (bf16[64,2048]{1,0:T(8,128)(2,1)S(1)}, bf16[64,2048]{1,0:T(8,128)(2,1)S(1)}, u32[]{:S(2)}, u32[]{:S(2)}) collective-permute-start(bf16[64,2048]{1,0:T(8,128)(2,1)S(1)} %add_convert_fusion.5), channel_id=1, source_target_pairs={{0,4},{1,3},{4,8},{5,1},{8,12},{9,5},{12,14},{13,9},{14,10},{15,13... | collective-permute-start | bytes 786440 | tf_op jit(solution)/shard_map/ppermute | solution.py:286
  45.5 11.7 %collective-permute-start.23 = (bf16[64,2048]{1,0:T(8,128)(2,1)S(1)}, bf16[64,2048]{1,0:T(8,128)(2,1)S(1)}, u32[]{:S(2)}, u32[]{:S(2)}) collective-permute-start(bf16[64,2048]{1,0:T(8,128)(2,1)S(1)} %get-tuple-element.61), channel_id=1, source_target_pairs={{0,1},{1,0},{2,3},{3,2},{4,5},{5,4},{6,7},{7,6},{8,9},{9,8},{10,11... | collective-permute-start | bytes 786440 | tf_op jit(solution)/shard_map/ppermute | solution.py:287
  46.2 6.4 %collective-permute-start.21 = (bf16[64,2048]{1,0:T(8,128)(2,1)S(1)}, bf16[64,2048]{1,0:T(8,128)(2,1)S(1)}, u32[]{:S(2)}, u32[]{:S(2)}) collective-permute-start(bf16[64,2048]{1,0:T(8,128)(2,1)S(1)} %add_convert_fusion.4), channel_id=1, source_target_pairs={{0,4},{1,3},{4,8},{5,1},{8,12},{9,5},{12,14},{13,9},{14,10},{15,13... | collective-permute-start | bytes 786440 | tf_op jit(solution)/shard_map/ppermute | solution.py:286
  49.0 6.4 %collective-permute-start.26 = (bf16[64,2048]{1,0:T(8,128)(2,1)S(1)}, bf16[64,2048]{1,0:T(8,128)(2,1)S(1)}, u32[]{:S(2)}, u32[]{:S(2)}) collective-permute-start(bf16[64,2048]{1,0:T(8,128)(2,1)S(1)} %add_convert_fusion.2), channel_id=1, source_target_pairs={{0,4},{1,3},{4,8},{5,1},{8,12},{9,5},{12,14},{13,9},{14,10},{15,13... | collective-permute-start | bytes 786440 | tf_op jit(solution)/shard_map/ppermute | solution.py:286
  52.7 5.9 %collective-permute-start.22 = (bf16[64,2048]{1,0:T(8,128)(2,1)S(1)}, bf16[64,2048]{1,0:T(8,128)(2,1)S(1)}, u32[]{:S(2)}, u32[]{:S(2)}) collective-permute-start(bf16[64,2048]{1,0:T(8,128)(2,1)S(1)} %add_convert_fusion.3), channel_id=1, source_target_pairs={{0,5},{1,2},{4,9},{5,0},{8,13},{9,4},{12,15},{13,8},{14,11},{15,12... | collective-permute-start | bytes 786440 | tf_op jit(solution)/shard_map/ppermute | solution.py:286
  55.6 6.4 %collective-permute-start.27 = (bf16[64,2048]{1,0:T(8,128)(2,1)S(1)}, bf16[64,2048]{1,0:T(8,128)(2,1)S(1)}, u32[]{:S(2)}, u32[]{:S(2)}) collective-permute-start(bf16[64,2048]{1,0:T(8,128)(2,1)S(1)} %add_convert_fusion.1), channel_id=1, source_target_pairs={{0,4},{1,3},{4,8},{5,1},{8,12},{9,5},{12,14},{13,9},{14,10},{15,13... | collective-permute-start | bytes 786440 | tf_op jit(solution)/shard_map/ppermute | solution.py:286

commit v16 on v15

--- a/solution.py
+++ b/solution.py
@@ -268,21 +268,22 @@
     *sums, down_w = run_expert(own, blocks[2], weights, experts, count, True)
     weights = [gate_w, up_w, down_w]
     sums = {2: sums}
-    sums[1] = run(after(blocks[1][0], sums[2][0]), *blocks[1][1:])
-    far = after(far, sums[1][0])
-    sums[2], sums[1] = turned(*sums[2]), turned(*sums[1])
+    far = after(far, sums[2][0])
+    sums[2] = turned(*sums[2])
     keep, send = run(swap(far), far)
     lead, trail = [added(keep, swap(send))], []
     sums[3] = turned(*run(after(swap(both), lead[0], *sums[2][2:]), both))
     lead = [ring(lead[0])]
     for step in range(rounds - 1, 0, -1):
         if step == 2:
-            lead = [after(lead[0], kept)]
+            lead = [after(lead[0], sums[1][0])]
         keep_trail, keep, send_trail, send = sums[step]
         lead = [added(keep, send, *lead)]
         trail = [added(after(keep_trail, lead[0]), send_trail, *trail)]
         if step == 3:
-            kept, other = run(after(mine, trail[0]), sibling)
+            sums[1] = turned(*run(after(blocks[1][0], trail[0]), *blocks[1][1:]))
+        if step == 1:
+            kept, other = run(after(mine, lead[0]), sibling)
         lead, trail = [(ring if step > 1 else home)(lead[0])], [ring(trail[0])]
     near = lax.optimization_barrier(added(lead[0], kept, swap(other), kind=jnp.float32))
     return added(near, trail[0])

time: 62.9 us -> 63.5 us (level)
  starting transfers between devices: 28 us -> 29.4 us
  waiting for transfers between devices: 15.3 us -> 14.5 us
    ppermute x6, waiting for transfers between devices: 10.6 us -> 7.57 us  [dense_body(): lead, trail = ([(ring if step > 1 else home)(lead[0])], [ring(trail[0])])]
    ppermute x1, waiting for transfers between devices: 0.01 us -> 1.54 us  [dense_body(): both = ring(jnp.concatenate([first, second], 0))]
    ppermute x1, waiting for transfers between devices: 0.01 us -> 0.96 us  [dense_body(): far = leap(first)]
    ppermute x6, starting transfers between devices: 8.99 us -> 9.63 us  [dense_body(): lead, trail = ([(ring if step > 1 else home)(lead[0])], [ring(trail[0])])]
  transfers between devices with their start and end apart: 28 -> 28, of which waited for: 12 -> 12; matrix products, arithmetic and copies ran while one was open for 1% -> 1% of each run, Pallas kernels for 26% -> 25%
where the time goes in v16:
time: 63.5 us; the launch traced here: 63.3 us
  starting transfers between devices  29.4 us (46%)
  Pallas kernels  17.8 us (28%)
  waiting for transfers between devices  14.5 us (23%)
  other arithmetic  1.51 us (2%)
    pallas_call x5, Pallas kernels, run_expert(): pl.pallas_call(functools.partial(expert_kernel, experts, len(blocks), pie...  13.2 us
    ppermute x6, starting transfers between devices, dense_body(): lead, trail = ([(ring if step > 1 else home)(lead[0])], [ring(trail[0])])  9.63 us
    ppermute x6, waiting for transfers between devices, dense_body(): lead, trail = ([(ring if step > 1 else home)(lead[0])], [ring(trail[0])])  7.57 us
    ppermute x2, starting transfers between devices, dense_body(): first, second = (ring(mine), ring(sibling))  4.34 us
    ppermute x2, starting transfers between devices, dense_body(): first, second = (ring(first), ring(second))  4.21 us
    ppermute x1, starting transfers between devices, dense_body(): far = leap(first)  3.12 us
    pallas_call x1, Pallas kernels, load_weights(): pl.pallas_call(functools.partial(load_kernel, pieces), out_shape=[pltpu.V...  2.86 us
    ppermute x1, starting transfers between devices, dense_body(): lead = [ring(lead[0])]  1.89 us
  transfers between devices with their start and end apart: 28, of which 12 were waited for; matrix products, arithmetic and copies ran while one was open for 1% of the time, Pallas kernels for 25%

profile of v16, /device:TPU:0, one launch (start us, length us, event | category | flops | bytes accessed | tf_op | source)
XLA Modules:
  0.0 63.3 jit_solution(3005345105298031559)
XLA Ops:
  0.0 1.7 %pack.1.refs_0_ = bf16[64,2176]{1,0:T(8,128)(2,1)} custom-call(bf16[64,2048]{1,0:T(8,128)(2,1)} %tokens_ref, s32[8,64]{1,0:T(8,128)} %bitcast.3, f32[8,64]{1,0:T(8,128)} %bitcast.4), custom_call_target="tpu_custom_call" | custom-call | bytes 1024 | tf_op jit(solution)/shard_map/pack/pallas_call | solution.py:216
  1.7 0.5 collective-permute-start.1
  2.2 2.6 %collective-permute-start = (bf16[64,2176]{1,0:T(8,128)(2,1)}, bf16[64,2176]{1,0:T(8,128)(2,1)S(1)}, u32[]{:S(2)}, u32[]{:S(2)}) collective-permute-start(bf16[64,2176]{1,0:T(8,128)(2,1)} %pack.1.refs_0_), channel_id=1, source_target_pairs={{0,4},{1,3},{4,8},{5,1},{8,12},{9,5},{12,14},{13,9},{14,10},{15,13... | collective-permute-start | bytes 835592 | tf_op jit(solution)/shard_map/ppermute | solution.py:254
  4.9 0.0 collective-permute-done.1.refs_1_
  4.9 1.7 %collective-permute-start.4 = (bf16[64,2176]{1,0:T(8,128)(2,1)S(1)}, bf16[64,2176]{1,0:T(8,128)(2,1)S(1)}, u32[]{:S(2)}, u32[]{:S(2)}) collective-permute-start(bf16[64,2176]{1,0:T(8,128)(2,1)S(1)} %collective-permute-done.1.refs_1_), channel_id=1, source_target_pairs={{0,4},{1,3},{4,8},{5,1},{8,12},{9,5},{12,14},{13,9},{14,10},{15,13... | collective-permute-start | bytes 835592 | tf_op jit(solution)/shard_map/ppermute | solution.py:254
  6.6 2.9 %load.1 = (bf16[1,2048,768]{2,1,0:T(8,128)(2,1)S(1)}, bf16[1,2048,768]{2,1,0:T(8,128)(2,1)S(1)}) custom-call(bf16[1,2048,768]{2,1,0:T(8,128)(2,1)} %refs_0_, bf16[1,2048,768]{2,1,0:T(8,128)(2,1)} %refs_1_.1), custom_call_target="tpu_custom_call" | custom-call | bytes 1024 | tf_op jit(solution)/shard_map/load/pallas_call | solution.py:174
  9.4 0.1 collective-permute-done.refs_2_
  9.5 2.1 %collective-permute-start.3 = (bf16[64,2176]{1,0:T(8,128)(2,1)S(1)}, bf16[64,2176]{1,0:T(8,128)(2,1)S(1)}, u32[]{:S(2)}, u32[]{:S(2)}) collective-permute-start(bf16[64,2176]{1,0:T(8,128)(2,1)S(1)} %collective-permute-done.refs_2_), channel_id=1, source_target_pairs={{0,4},{1,3},{4,8},{5,1},{8,12},{9,5},{12,14},{13,9},{14,10},{15,13... | collective-permute-start | bytes 835592 | tf_op jit(solution)/shard_map/ppermute | solution.py:262
  11.6 0.9 %collective-permute-done.4.refs_3_ = bf16[64,2176]{1,0:T(8,128)(2,1)S(1)} collective-permute-done((bf16[64,2176]{1,0:T(8,128)(2,1)S(1)}, bf16[64,2176]{1,0:T(8,128)(2,1)S(1)}, u32[]{:S(2)}, u32[]{:S(2)}) %collective-permute-start.4) | collective-permute-done | bytes 278560 | tf_op jit(solution)/shard_map/ppermute | solution.py:254
  12.5 2.1 %collective-permute-start.5 = (bf16[64,2176]{1,0:T(8,128)(2,1)S(1)}, bf16[64,2176]{1,0:T(8,128)(2,1)S(1)}, u32[]{:S(2)}, u32[]{:S(2)}) collective-permute-start(bf16[64,2176]{1,0:T(8,128)(2,1)S(1)} %collective-permute-done.4.refs_3_), channel_id=1, source_target_pairs={{0,4},{1,3},{4,8},{5,1},{8,12},{9,5},{12,14},{13,9},{14,10},{15,13... | collective-permute-start | bytes 835592 | tf_op jit(solution)/shard_map/ppermute | solution.py:262
  14.6 0.0 collective-permute-start.2
  14.6 0.5 collective-permute-start.10
  15.1 0.9 %collective-permute-done.3.refs_2_ = bf16[64,2176]{1,0:T(8,128)(2,1)S(1)} collective-permute-done((bf16[64,2176]{1,0:T(8,128)(2,1)S(1)}, bf16[64,2176]{1,0:T(8,128)(2,1)S(1)}, u32[]{:S(2)}, u32[]{:S(2)}) %collective-permute-start.3) | collective-permute-done | bytes 278560 | tf_op jit(solution)/shard_map/ppermute | solution.py:262
  16.1 0.0 collective-permute-start.9
  16.1 3.1 %collective-permute-start.8 = (bf16[64,2176]{1,0:T(8,128)(2,1)S(1)}, bf16[64,2176]{1,0:T(8,128)(2,1)S(1)}, u32[]{:S(2)}, u32[]{:S(2)}) collective-permute-start(bf16[64,2176]{1,0:T(8,128)(2,1)S(1)} %collective-permute-done.3.refs_2_), channel_id=1, source_target_pairs={{0,8},{1,7},{4,12},{5,3},{8,14},{9,1},{12,10},{13,5},{14,6},{15,9}... | collective-permute-start | bytes 835592 | tf_op jit(solution)/shard_map/ppermute | solution.py:264
  19.2 0.0 collective-permute-done.5.refs_3_
  19.2 0.1 collective-permute-start.11
  19.4 0.0 collective-permute-done.2.refs_0_
  19.4 1.9 %collective-permute-start.6 = (bf16[128,2176]{1,0:T(8,128)(2,1)S(1)}, bf16[128,2176]{1,0:T(8,128)(2,1)S(1)}, u32[]{:S(2)}, u32[]{:S(2)}) collective-permute-start(bf16[128,2176]{1,0:T(8,128)(2,1)S(1)} %pad_maximum_fusion), channel_id=1, source_target_pairs={{0,4},{1,3},{4,8},{5,1},{8,12},{9,5},{12,14},{13,9},{14,10},{15,13... | collective-permute-start | bytes 1671176 | tf_op jit(solution)/shard_map/ppermute | solution.py:265
  21.3 0.0 collective-permute-done.9.refs_0_
  21.3 0.0 collective-permute-done.10.refs_1_
  21.3 0.0 collective-permute-done.11.refs_1_
  21.3 3.9 %expert.5 = (bf16[64,2048]{1,0:T(8,128)(2,1)S(1)}, bf16[64,2048]{1,0:T(8,128)(2,1)S(1)}, bf16[64,2048]{1,0:T(8,128)(2,1)S(1)}, bf16[64,2048]{1,0:T(8,128)(2,1)S(1)}, bf16[1,2048,768]{2,1,0:T(8,128)(2,1)S(1)}) custom-call(s32[1]{0:T(128)} %bitcast.own_ref, bf16[64,2176]{1,0:T(8,128)(2,1)S(1)} %collective-permute-done.9.refs_0_, ...), custom_call_target="tpu_custom_call" | custom-call | flops 524288 | bytes 524288 | tf_op jit(solution)/shard_map/expert/pallas_call | solution.py:141
  25.1 1.0 %collective-permute-done.8.refs_1_ = bf16[64,2176]{1,0:T(8,128)(2,1)S(1)} collective-permute-done((bf16[64,2176]{1,0:T(8,128)(2,1)S(1)}, bf16[64,2176]{1,0:T(8,128)(2,1)S(1)}, u32[]{:S(2)}, u32[]{:S(2)}) %collective-permute-start.8) | collective-permute-done | bytes 278560 | tf_op jit(solution)/shard_map/ppermute | solution.py:264
  26.1 0.3 collective-permute-start.12
  26.4 1.2 %collective-permute-done.12.refs_0_ = bf16[64,2176]{1,0:T(8,128)(2,1)S(1)} collective-permute-done((bf16[64,2176]{1,0:T(8,128)(2,1)S(1)}, bf16[64,2176]{1,0:T(8,128)(2,1)S(1)}, u32[]{:S(2)}, u32[]{:S(2)}) %collective-permute-start.12) | collective-permute-done | bytes 278560 | tf_op jit(solution)/shard_map/ppermute | solution.py:273
  27.7 2.0 %expert.6 = (bf16[64,2048]{1,0:T(8,128)(2,1)S(1)}, bf16[64,2048]{1,0:T(8,128)(2,1)S(1)}) custom-call(s32[1]{0:T(128)} %bitcast.own_ref, bf16[64,2176]{1,0:T(8,128)(2,1)S(1)} %collective-permute-done.12.refs_0_, bf16[64,2176]{1,0:T(8,128)(2,1)S(1)} %collective-permute-done.8.refs_1_, bf16[1,2048,768]{2,1,0:T(8,128)(2,1)S(1)} %get-tuple-element.38.refs_4_.refs_2_, ...), custom_call_target="tpu_custom_call" | custom-call | flops 262144 | bytes 262144 | tf_op jit(solution)/shard_map/expert/pallas_call | solution.py:141
  29.7 0.4 collective-permute-start.13
  30.1 1.5 %collective-permute-done.6.refs_1_ = bf16[128,2176]{1,0:T(8,128)(2,1)S(1)} collective-permute-done((bf16[128,2176]{1,0:T(8,128)(2,1)S(1)}, bf16[128,2176]{1,0:T(8,128)(2,1)S(1)}, u32[]{:S(2)}, u32[]{:S(2)}) %collective-permute-start.6) | collective-permute-done | bytes 557088 | tf_op jit(solution)/shard_map/ppermute | solution.py:265
  31.7 0.6 %collective-permute-start.7 = (bf16[128,2176]{1,0:T(8,128)(2,1)S(1)}, bf16[128,2176]{1,0:T(8,128)(2,1)S(1)}, u32[]{:S(2)}, u32[]{:S(2)}) collective-permute-start(bf16[128,2176]{1,0:T(8,128)(2,1)S(1)} %collective-permute-done.6.refs_1_), channel_id=1, source_target_pairs={{0,1},{1,0},{2,3},{3,2},{4,5},{5,4},{6,7},{7,6},{8,9},{9,8},{10,11... | collective-permute-start | bytes 1671176 | tf_op jit(solution)/shard_map/ppermute | solution.py:275
  32.3 0.0 collective-permute-start.14
  32.3 0.5 collective-permute-start.15
  32.8 0.0 collective-permute-done.13
  32.8 0.1 add_convert_fusion.7
  32.9 1.9 %collective-permute-start.17 = (bf16[64,2048]{1,0:T(8,128)(2,1)S(1)}, bf16[64,2048]{1,0:T(8,128)(2,1)S(1)}, u32[]{:S(2)}, u32[]{:S(2)}) collective-permute-start(bf16[64,2048]{1,0:T(8,128)(2,1)S(1)} %add_convert_fusion.7), channel_id=1, source_target_pairs={{0,4},{1,3},{4,8},{5,1},{8,12},{9,5},{12,14},{13,9},{14,10},{15,13... | collective-permute-start | bytes 786440 | tf_op jit(solution)/shard_map/ppermute | solution.py:276
  34.8 0.0 collective-permute-done.14
  34.8 2.6 %expert.7 = (bf16[64,2048]{1,0:T(8,128)(2,1)S(1)}, bf16[64,2048]{1,0:T(8,128)(2,1)S(1)}, bf16[64,2048]{1,0:T(8,128)(2,1)S(1)}, bf16[64,2048]{1,0:T(8,128)(2,1)S(1)}) custom-call(s32[1]{0:T(128)} %bitcast.own_ref, bf16[128,2176]{1,0:T(8,128)(2,1)S(1)} %collective-permute-done.7.refs_0_, bf16[128,2176]{1,0:T(8,128)(2,1)S(1)} %collective-permute-done.6.refs_1_, ...), custom_call_target="tpu_custom_call" | custom-call | flops 524288 | bytes 524288 | tf_op jit(solution)/shard_map/expert/pallas_call | solution.py:141
  37.5 0.3 collective-permute-start.16
  37.7 0.3 collective-permute-start.18
  38.0 1.3 %collective-permute-done.17 = bf16[64,2048]{1,0:T(8,128)(2,1)S(1)} collective-permute-done((bf16[64,2048]{1,0:T(8,128)(2,1)S(1)}, bf16[64,2048]{1,0:T(8,128)(2,1)S(1)}, u32[]{:S(2)}, u32[]{:S(2)}) %collective-permute-start.17) | collective-permute-done | bytes 262176 | tf_op jit(solution)/shard_map/ppermute | solution.py:276
  39.3 0.1 add_convert_fusion.6
  39.4 1.9 %collective-permute-start.20 = (bf16[64,2048]{1,0:T(8,128)(2,1)S(1)}, bf16[64,2048]{1,0:T(8,128)(2,1)S(1)}, u32[]{:S(2)}, u32[]{:S(2)}) collective-permute-start(bf16[64,2048]{1,0:T(8,128)(2,1)S(1)} %add_convert_fusion.6), channel_id=1, source_target_pairs={{0,4},{1,3},{4,8},{5,1},{8,12},{9,5},{12,14},{13,9},{14,10},{15,13... | collective-permute-start | bytes 786440 | tf_op jit(solution)/shard_map/ppermute | solution.py:287
  41.3 0.1 add_convert_fusion.5
  41.4 2.1 %collective-permute-start.25 = (bf16[64,2048]{1,0:T(8,128)(2,1)S(1)}, bf16[64,2048]{1,0:T(8,128)(2,1)S(1)}, u32[]{:S(2)}, u32[]{:S(2)}) collective-permute-start(bf16[64,2048]{1,0:T(8,128)(2,1)S(1)} %add_convert_fusion.5), channel_id=1, source_target_pairs={{0,4},{1,3},{4,8},{5,1},{8,12},{9,5},{12,14},{13,9},{14,10},{15,13... | collective-permute-start | bytes 786440 | tf_op jit(solution)/shard_map/ppermute | solution.py:287
  43.5 2.6 %expert.8 = (bf16[64,2048]{1,0:T(8,128)(2,1)S(1)}, bf16[64,2048]{1,0:T(8,128)(2,1)S(1)}, bf16[64,2048]{1,0:T(8,128)(2,1)S(1)}, bf16[64,2048]{1,0:T(8,128)(2,1)S(1)}) custom-call(s32[1]{0:T(128)} %bitcast.own_ref, bf16[64,2176]{1,0:T(8,128)(2,1)S(1)} %collective-permute-done.2.refs_0_, bf16[64,2176]{1,0:T(8,128)(2,1)S(1)} %collective-permute-done.10.refs_1_, ...), custom_call_target="tpu_custom_call" | custom-call | flops 524288 | bytes 524288 | tf_op jit(solution)/shard_map/expert/pallas_call | solution.py:141
  46.1 0.1 collective-permute-start.19
  46.2 0.5 collective-permute-start.24
  46.7 0.1 add_convert_fusion.4
  46.8 1.6 %collective-permute-start.21 = (bf16[64,2048]{1,0:T(8,128)(2,1)S(1)}, bf16[64,2048]{1,0:T(8,128)(2,1)S(1)}, u32[]{:S(2)}, u32[]{:S(2)}) collective-permute-start(bf16[64,2048]{1,0:T(8,128)(2,1)S(1)} %add_convert_fusion.4), channel_id=1, source_target_pairs={{0,4},{1,3},{4,8},{5,1},{8,12},{9,5},{12,14},{13,9},{14,10},{15,13... | collective-permute-start | bytes 786440 | tf_op jit(solution)/shard_map/ppermute | solution.py:287
  48.4 0.2 collective-permute-done.25
  48.7 0.1 add_convert_fusion.2
  48.8 1.9 %collective-permute-start.26 = (bf16[64,2048]{1,0:T(8,128)(2,1)S(1)}, bf16[64,2048]{1,0:T(8,128)(2,1)S(1)}, u32[]{:S(2)}, u32[]{:S(2)}) collective-permute-start(bf16[64,2048]{1,0:T(8,128)(2,1)S(1)} %add_convert_fusion.2), channel_id=1, source_target_pairs={{0,4},{1,3},{4,8},{5,1},{8,12},{9,5},{12,14},{13,9},{14,10},{15,13... | collective-permute-start | bytes 786440 | tf_op jit(solution)/shard_map/ppermute | solution.py:287
  50.7 2.6 %collective-permute-done.21 = bf16[64,2048]{1,0:T(8,128)(2,1)S(1)} collective-permute-done((bf16[64,2048]{1,0:T(8,128)(2,1)S(1)}, bf16[64,2048]{1,0:T(8,128)(2,1)S(1)}, u32[]{:S(2)}, u32[]{:S(2)}) %collective-permute-start.21) | collective-permute-done | bytes 262176 | tf_op jit(solution)/shard_map/ppermute | solution.py:287
  53.2 0.1 add_convert_fusion.3
  53.4 0.5 collective-permute-start.22
  53.8 2.0 %expert.9 = (bf16[64,2048]{1,0:T(8,128)(2,1)S(1)}, bf16[64,2048]{1,0:T(8,128)(2,1)S(1)}) custom-call(s32[1]{0:T(128)} %bitcast.own_ref, bf16[64,2176]{1,0:T(8,128)(2,1)S(1)} %copy-done, bf16[64,2176]{1,0:T(8,128)(2,1)S(1)} %collective-permute-done.1.refs_1_, bf16[1,2048,768]{2,1,0:T(8,128)(2,1)S(1)} %get-tuple-element.38.refs_4_.refs_2_, ...), custom_call_target="tpu_custom_call" | custom-call | flops 262144 | bytes 262144 | tf_op jit(solution)/shard_map/expert/pallas_call | solution.py:141
  55.9 0.1 collective-permute-start.23
  56.0 0.1 collective-permute-done.26
  56.1 0.1 add_convert_fusion.1
  56.2 1.7 %collective-permute-start.27 = (bf16[64,2048]{1,0:T(8,128)(2,1)S(1)}, bf16[64,2048]{1,0:T(8,128)(2,1)S(1)}, u32[]{:S(2)}, u32[]{:S(2)}) collective-permute-start(bf16[64,2048]{1,0:T(8,128)(2,1)S(1)} %add_convert_fusion.1), channel_id=1, source_target_pairs={{0,4},{1,3},{4,8},{5,1},{8,12},{9,5},{12,14},{13,9},{14,10},{15,13... | collective-permute-start | bytes 786440 | tf_op jit(solution)/shard_map/ppermute | solution.py:287
  57.8 1.4 %collective-permute-done.22 = bf16[64,2048]{1,0:T(8,128)(2,1)S(1)} collective-permute-done((bf16[64,2048]{1,0:T(8,128)(2,1)S(1)}, bf16[64,2048]{1,0:T(8,128)(2,1)S(1)}, u32[]{:S(2)}, u32[]{:S(2)}) %collective-permute-start.22) | collective-permute-done | bytes 262176 | tf_op jit(solution)/shard_map/ppermute | solution.py:287
  59.2 0.1 convert_add_fusion
  59.3 3.3 %collective-permute-done.27 = bf16[64,2048]{1,0:T(8,128)(2,1)S(1)} collective-permute-done((bf16[64,2048]{1,0:T(8,128)(2,1)S(1)}, bf16[64,2048]{1,0:T(8,128)(2,1)S(1)}, u32[]{:S(2)}, u32[]{:S(2)}) %collective-permute-start.27) | collective-permute-done | bytes 262176 | tf_op jit(solution)/shard_map/ppermute | solution.py:287
  62.6 0.8 %add_convert_fusion = bf16[64,2048]{1,0:T(8,128)(2,1)} fusion(f32[64,2048]{1,0:T(8,128)S(1)} %convert_add_fusion, bf16[64,2048]{1,0:T(8,128)(2,1)S(1)} %collective-permute-done.27), kind=kLoop, calls=%fused_computation.1 | loop fusion | flops 393216 | bytes 1048576 | tf_op jit(solution)/shard_map/convert_element_type | solution.py:235
  (11 shorter events, 0.1 us)
Async XLA Ops:
  1.7 3.2 %collective-permute-start.1 = (bf16[64,2176]{1,0:T(8,128)(2,1)}, bf16[64,2176]{1,0:T(8,128)(2,1)S(1)}, u32[]{:S(2)}, u32[]{:S(2)}) collective-permute-start(bf16[64,2176]{1,0:T(8,128)(2,1)} %pack.1.refs_0_), channel_id=1, source_target_pairs={{0,1},{1,0},{2,3},{3,2},{4,5},{5,4},{6,7},{7,6},{8,9},{9,8},{10,11... | collective-permute-start | bytes 835592 | tf_op jit(solution)/shard_map/ppermute | solution.py:253
  2.2 7.3 %collective-permute-start = (bf16[64,2176]{1,0:T(8,128)(2,1)}, bf16[64,2176]{1,0:T(8,128)(2,1)S(1)}, u32[]{:S(2)}, u32[]{:S(2)}) collective-permute-start(bf16[64,2176]{1,0:T(8,128)(2,1)} %pack.1.refs_0_), channel_id=1, source_target_pairs={{0,4},{1,3},{4,8},{5,1},{8,12},{9,5},{12,14},{13,9},{14,10},{15,13... | collective-permute-start | bytes 835592 | tf_op jit(solution)/shard_map/ppermute | solution.py:254
  4.9 7.6 %collective-permute-start.4 = (bf16[64,2176]{1,0:T(8,128)(2,1)S(1)}, bf16[64,2176]{1,0:T(8,128)(2,1)S(1)}, u32[]{:S(2)}, u32[]{:S(2)}) collective-permute-start(bf16[64,2176]{1,0:T(8,128)(2,1)S(1)} %collective-permute-done.1.refs_1_), channel_id=1, source_target_pairs={{0,4},{1,3},{4,8},{5,1},{8,12},{9,5},{12,14},{13,9},{14,10},{15,13... | collective-permute-start | bytes 835592 | tf_op jit(solution)/shard_map/ppermute | solution.py:254
  9.5 6.5 %collective-permute-start.3 = (bf16[64,2176]{1,0:T(8,128)(2,1)S(1)}, bf16[64,2176]{1,0:T(8,128)(2,1)S(1)}, u32[]{:S(2)}, u32[]{:S(2)}) collective-permute-start(bf16[64,2176]{1,0:T(8,128)(2,1)S(1)} %collective-permute-done.refs_2_), channel_id=1, source_target_pairs={{0,4},{1,3},{4,8},{5,1},{8,12},{9,5},{12,14},{13,9},{14,10},{15,13... | collective-permute-start | bytes 835592 | tf_op jit(solution)/shard_map/ppermute | solution.py:262
  12.5 6.7 %collective-permute-start.5 = (bf16[64,2176]{1,0:T(8,128)(2,1)S(1)}, bf16[64,2176]{1,0:T(8,128)(2,1)S(1)}, u32[]{:S(2)}, u32[]{:S(2)}) collective-permute-start(bf16[64,2176]{1,0:T(8,128)(2,1)S(1)} %collective-permute-done.4.refs_3_), channel_id=1, source_target_pairs={{0,4},{1,3},{4,8},{5,1},{8,12},{9,5},{12,14},{13,9},{14,10},{15,13... | collective-permute-start | bytes 835592 | tf_op jit(solution)/shard_map/ppermute | solution.py:262
  14.6 4.8 %collective-permute-start.2 = (bf16[64,2176]{1,0:T(8,128)(2,1)S(1)}, bf16[64,2176]{1,0:T(8,128)(2,1)S(1)}, u32[]{:S(2)}, u32[]{:S(2)}) collective-permute-start(bf16[64,2176]{1,0:T(8,128)(2,1)S(1)} %collective-permute-done.refs_2_), channel_id=1, source_target_pairs={{0,1},{1,0},{2,3},{3,2},{4,5},{5,4},{6,7},{7,6},{8,9},{9,8},{10,11... | collective-permute-start | bytes 835592 | tf_op jit(solution)/shard_map/ppermute | solution.py:263
  14.6 6.7 %collective-permute-start.10 = (bf16[64,2176]{1,0:T(8,128)(2,1)S(1)}, bf16[64,2176]{1,0:T(8,128)(2,1)S(1)}, u32[]{:S(2)}, u32[]{:S(2)}) collective-permute-start(bf16[64,2176]{1,0:T(8,128)(2,1)S(1)} %collective-permute-done.4.refs_3_), channel_id=1, source_target_pairs={{0,1},{1,0},{2,3},{3,2},{4,5},{5,4},{6,7},{7,6},{8,9},{9,8},{10,11... | collective-permute-start | bytes 835592 | tf_op jit(solution)/shard_map/ppermute | solution.py:263
  16.1 5.2 %collective-permute-start.9 = (bf16[64,2176]{1,0:T(8,128)(2,1)S(1)}, bf16[64,2176]{1,0:T(8,128)(2,1)S(1)}, u32[]{:S(2)}, u32[]{:S(2)}) collective-permute-start(bf16[64,2176]{1,0:T(8,128)(2,1)S(1)} %collective-permute-done.3.refs_2_), channel_id=1, source_target_pairs={{0,1},{1,0},{2,3},{3,2},{4,5},{5,4},{6,7},{7,6},{8,9},{9,8},{10,11... | collective-permute-start | bytes 835592 | tf_op jit(solution)/shard_map/ppermute | solution.py:263
  16.1 10.0 %collective-permute-start.8 = (bf16[64,2176]{1,0:T(8,128)(2,1)S(1)}, bf16[64,2176]{1,0:T(8,128)(2,1)S(1)}, u32[]{:S(2)}, u32[]{:S(2)}) collective-permute-start(bf16[64,2176]{1,0:T(8,128)(2,1)S(1)} %collective-permute-done.3.refs_2_), channel_id=1, source_target_pairs={{0,8},{1,7},{4,12},{5,3},{8,14},{9,1},{12,10},{13,5},{14,6},{15,9}... | collective-permute-start | bytes 835592 | tf_op jit(solution)/shard_map/ppermute | solution.py:264
  19.2 2.1 %collective-permute-start.11 = (bf16[64,2176]{1,0:T(8,128)(2,1)S(1)}, bf16[64,2176]{1,0:T(8,128)(2,1)S(1)}, u32[]{:S(2)}, u32[]{:S(2)}) collective-permute-start(bf16[64,2176]{1,0:T(8,128)(2,1)S(1)} %collective-permute-done.5.refs_3_), channel_id=1, source_target_pairs={{0,1},{1,0},{2,3},{3,2},{4,5},{5,4},{6,7},{7,6},{8,9},{9,8},{10,11... | collective-permute-start | bytes 835592 | tf_op jit(solution)/shard_map/ppermute | solution.py:263
  19.4 12.3 %collective-permute-start.6 = (bf16[128,2176]{1,0:T(8,128)(2,1)S(1)}, bf16[128,2176]{1,0:T(8,128)(2,1)S(1)}, u32[]{:S(2)}, u32[]{:S(2)}) collective-permute-start(bf16[128,2176]{1,0:T(8,128)(2,1)S(1)} %pad_maximum_fusion), channel_id=1, source_target_pairs={{0,4},{1,3},{4,8},{5,1},{8,12},{9,5},{12,14},{13,9},{14,10},{15,13... | collective-permute-start | bytes 1671176 | tf_op jit(solution)/shard_map/ppermute | solution.py:265
  26.1 1.6 %collective-permute-start.12 = (bf16[64,2176]{1,0:T(8,128)(2,1)S(1)}, bf16[64,2176]{1,0:T(8,128)(2,1)S(1)}, u32[]{:S(2)}, u32[]{:S(2)}) collective-permute-start(bf16[64,2176]{1,0:T(8,128)(2,1)S(1)} %collective-permute-done.8.refs_1_), channel_id=1, source_target_pairs={{0,1},{1,0},{2,3},{3,2},{4,5},{5,4},{6,7},{7,6},{8,9},{9,8},{10,11... | collective-permute-start | bytes 835592 | tf_op jit(solution)/shard_map/ppermute | solution.py:273
  29.7 3.1 %collective-permute-start.13 = (bf16[64,2048]{1,0:T(8,128)(2,1)S(1)}, bf16[64,2048]{1,0:T(8,128)(2,1)S(1)}, u32[]{:S(2)}, u32[]{:S(2)}) collective-permute-start(bf16[64,2048]{1,0:T(8,128)(2,1)S(1)} %get-tuple-element.46), channel_id=1, source_target_pairs={{0,1},{1,0},{2,3},{3,2},{4,5},{5,4},{6,7},{7,6},{8,9},{9,8},{10,11... | collective-permute-start | bytes 786440 | tf_op jit(solution)/shard_map/ppermute | solution.py:274
  31.7 3.1 %collective-permute-start.7 = (bf16[128,2176]{1,0:T(8,128)(2,1)S(1)}, bf16[128,2176]{1,0:T(8,128)(2,1)S(1)}, u32[]{:S(2)}, u32[]{:S(2)}) collective-permute-start(bf16[128,2176]{1,0:T(8,128)(2,1)S(1)} %collective-permute-done.6.refs_1_), channel_id=1, source_target_pairs={{0,1},{1,0},{2,3},{3,2},{4,5},{5,4},{6,7},{7,6},{8,9},{9,8},{10,11... | collective-permute-start | bytes 1671176 | tf_op jit(solution)/shard_map/ppermute | solution.py:275
  32.3 2.5 %collective-permute-start.14 = (bf16[64,2048]{1,0:T(8,128)(2,1)S(1)}, bf16[64,2048]{1,0:T(8,128)(2,1)S(1)}, u32[]{:S(2)}, u32[]{:S(2)}) collective-permute-start(bf16[64,2048]{1,0:T(8,128)(2,1)S(1)} %get-tuple-element.47), channel_id=1, source_target_pairs={{0,1},{1,0},{2,3},{3,2},{4,5},{5,4},{6,7},{7,6},{8,9},{9,8},{10,11... | collective-permute-start | bytes 786440 | tf_op jit(solution)/shard_map/ppermute | solution.py:266
  32.3 2.5 %collective-permute-start.15 = (bf16[64,2048]{1,0:T(8,128)(2,1)S(1)}, bf16[64,2048]{1,0:T(8,128)(2,1)S(1)}, u32[]{:S(2)}, u32[]{:S(2)}) collective-permute-start(bf16[64,2048]{1,0:T(8,128)(2,1)S(1)} %get-tuple-element.48), channel_id=1, source_target_pairs={{0,1},{1,0},{2,3},{3,2},{4,5},{5,4},{6,7},{7,6},{8,9},{9,8},{10,11... | collective-permute-start | bytes 786440 | tf_op jit(solution)/shard_map/ppermute | solution.py:266
  32.9 6.4 %collective-permute-start.17 = (bf16[64,2048]{1,0:T(8,128)(2,1)S(1)}, bf16[64,2048]{1,0:T(8,128)(2,1)S(1)}, u32[]{:S(2)}, u32[]{:S(2)}) collective-permute-start(bf16[64,2048]{1,0:T(8,128)(2,1)S(1)} %add_convert_fusion.7), channel_id=1, source_target_pairs={{0,4},{1,3},{4,8},{5,1},{8,12},{9,5},{12,14},{13,9},{14,10},{15,13... | collective-permute-start | bytes 786440 | tf_op jit(solution)/shard_map/ppermute | solution.py:276
  37.5 1.9 %collective-permute-start.16 = (bf16[64,2048]{1,0:T(8,128)(2,1)S(1)}, bf16[64,2048]{1,0:T(8,128)(2,1)S(1)}, u32[]{:S(2)}, u32[]{:S(2)}) collective-permute-start(bf16[64,2048]{1,0:T(8,128)(2,1)S(1)} %get-tuple-element.52), channel_id=1, source_target_pairs={{0,1},{1,0},{2,3},{3,2},{4,5},{5,4},{6,7},{7,6},{8,9},{9,8},{10,11... | collective-permute-start | bytes 786440 | tf_op jit(solution)/shard_map/ppermute | solution.py:266
  37.7 3.6 %collective-permute-start.18 = (bf16[64,2048]{1,0:T(8,128)(2,1)S(1)}, bf16[64,2048]{1,0:T(8,128)(2,1)S(1)}, u32[]{:S(2)}, u32[]{:S(2)}) collective-permute-start(bf16[64,2048]{1,0:T(8,128)(2,1)S(1)} %get-tuple-element.54), channel_id=1, source_target_pairs={{0,1},{1,0},{2,3},{3,2},{4,5},{5,4},{6,7},{7,6},{8,9},{9,8},{10,11... | collective-permute-start | bytes 786440 | tf_op jit(solution)/shard_map/ppermute | solution.py:266
  39.4 7.3 %collective-permute-start.20 = (bf16[64,2048]{1,0:T(8,128)(2,1)S(1)}, bf16[64,2048]{1,0:T(8,128)(2,1)S(1)}, u32[]{:S(2)}, u32[]{:S(2)}) collective-permute-start(bf16[64,2048]{1,0:T(8,128)(2,1)S(1)} %add_convert_fusion.6), channel_id=1, source_target_pairs={{0,4},{1,3},{4,8},{5,1},{8,12},{9,5},{12,14},{13,9},{14,10},{15,13... | collective-permute-start | bytes 786440 | tf_op jit(solution)/shard_map/ppermute | solution.py:287
  41.4 7.3 %collective-permute-start.25 = (bf16[64,2048]{1,0:T(8,128)(2,1)S(1)}, bf16[64,2048]{1,0:T(8,128)(2,1)S(1)}, u32[]{:S(2)}, u32[]{:S(2)}) collective-permute-start(bf16[64,2048]{1,0:T(8,128)(2,1)S(1)} %add_convert_fusion.5), channel_id=1, source_target_pairs={{0,4},{1,3},{4,8},{5,1},{8,12},{9,5},{12,14},{13,9},{14,10},{15,13... | collective-permute-start | bytes 786440 | tf_op jit(solution)/shard_map/ppermute | solution.py:287
  46.1 7.7 %copy-start = (bf16[64,2176]{1,0:T(8,128)(2,1)S(1)}, bf16[64,2176]{1,0:T(8,128)(2,1)}, u32[]{:S(2)}) copy-start(bf16[64,2176]{1,0:T(8,128)(2,1)} %pack.1.refs_0_) | copy-start | bytes 835588
  46.1 4.5 %collective-permute-start.19 = (bf16[64,2048]{1,0:T(8,128)(2,1)S(1)}, bf16[64,2048]{1,0:T(8,128)(2,1)S(1)}, u32[]{:S(2)}, u32[]{:S(2)}) collective-permute-start(bf16[64,2048]{1,0:T(8,128)(2,1)S(1)} %get-tuple-element.57), channel_id=1, source_target_pairs={{0,1},{1,0},{2,3},{3,2},{4,5},{5,4},{6,7},{7,6},{8,9},{9,8},{10,11... | collective-permute-start | bytes 786440 | tf_op jit(solution)/shard_map/ppermute | solution.py:266
  46.2 9.7 %collective-permute-start.24 = (bf16[64,2048]{1,0:T(8,128)(2,1)S(1)}, bf16[64,2048]{1,0:T(8,128)(2,1)S(1)}, u32[]{:S(2)}, u32[]{:S(2)}) collective-permute-start(bf16[64,2048]{1,0:T(8,128)(2,1)S(1)} %get-tuple-element.64), channel_id=1, source_target_pairs={{0,1},{1,0},{2,3},{3,2},{4,5},{5,4},{6,7},{7,6},{8,9},{9,8},{10,11... | collective-permute-start | bytes 786440 | tf_op jit(solution)/shard_map/ppermute | solution.py:266
  46.8 6.4 %collective-permute-start.21 = (bf16[64,2048]{1,0:T(8,128)(2,1)S(1)}, bf16[64,2048]{1,0:T(8,128)(2,1)S(1)}, u32[]{:S(2)}, u32[]{:S(2)}) collective-permute-start(bf16[64,2048]{1,0:T(8,128)(2,1)S(1)} %add_convert_fusion.4), channel_id=1, source_target_pairs={{0,4},{1,3},{4,8},{5,1},{8,12},{9,5},{12,14},{13,9},{14,10},{15,13... | collective-permute-start | bytes 786440 | tf_op jit(solution)/shard_map/ppermute | solution.py:287
  48.8 7.3 %collective-permute-start.26 = (bf16[64,2048]{1,0:T(8,128)(2,1)S(1)}, bf16[64,2048]{1,0:T(8,128)(2,1)S(1)}, u32[]{:S(2)}, u32[]{:S(2)}) collective-permute-start(bf16[64,2048]{1,0:T(8,128)(2,1)S(1)} %add_convert_fusion.2), channel_id=1, source_target_pairs={{0,4},{1,3},{4,8},{5,1},{8,12},{9,5},{12,14},{13,9},{14,10},{15,13... | collective-permute-start | bytes 786440 | tf_op jit(solution)/shard_map/ppermute | solution.py:287
  53.4 5.9 %collective-permute-start.22 = (bf16[64,2048]{1,0:T(8,128)(2,1)S(1)}, bf16[64,2048]{1,0:T(8,128)(2,1)S(1)}, u32[]{:S(2)}, u32[]{:S(2)}) collective-permute-start(bf16[64,2048]{1,0:T(8,128)(2,1)S(1)} %add_convert_fusion.3), channel_id=1, source_target_pairs={{0,5},{1,2},{4,9},{5,0},{8,13},{9,4},{12,15},{13,8},{14,11},{15,12... | collective-permute-start | bytes 786440 | tf_op jit(solution)/shard_map/ppermute | solution.py:287
  55.9 2.0 %collective-permute-start.23 = (bf16[64,2048]{1,0:T(8,128)(2,1)S(1)}, bf16[64,2048]{1,0:T(8,128)(2,1)S(1)}, u32[]{:S(2)}, u32[]{:S(2)}) collective-permute-start(bf16[64,2048]{1,0:T(8,128)(2,1)S(1)} %get-tuple-element.62), channel_id=1, source_target_pairs={{0,1},{1,0},{2,3},{3,2},{4,5},{5,4},{6,7},{7,6},{8,9},{9,8},{10,11... | collective-permute-start | bytes 786440 | tf_op jit(solution)/shard_map/ppermute | solution.py:288
  56.2 6.4 %collective-permute-start.27 = (bf16[64,2048]{1,0:T(8,128)(2,1)S(1)}, bf16[64,2048]{1,0:T(8,128)(2,1)S(1)}, u32[]{:S(2)}, u32[]{:S(2)}) collective-permute-start(bf16[64,2048]{1,0:T(8,128)(2,1)S(1)} %add_convert_fusion.1), channel_id=1, source_target_pairs={{0,4},{1,3},{4,8},{5,1},{8,12},{9,5},{12,14},{13,9},{14,10},{15,13... | collective-permute-start | bytes 786440 | tf_op jit(solution)/shard_map/ppermute | solution.py:287

commit v17 on v14

--- a/solution.py
+++ b/solution.py
@@ -145,7 +145,7 @@
 
 
 def load_weights(weights):
-    pieces = math.gcd(weights[0].shape[1] // 16, 16)
+    pieces = math.gcd(weights[0].shape[1] // 16, 4)
     return pl.pallas_call(
         functools.partial(load_kernel, pieces),
         out_shape=[pltpu.VMEM(w.shape, w.dtype) for w in weights],

time: 62.6 us -> 62.5 us (level)
  starting transfers between devices: 29.1 us -> 30.4 us
  waiting for transfers between devices: 12.7 us -> 11.8 us
  transfers between devices with their start and end apart: 28 -> 28, of which waited for: 12 -> 13; matrix products, arithmetic and copies ran while one was open for 1% -> 1% of each run, Pallas kernels for 28% -> 27%
where the time goes in v17:
time: 62.5 us; the launch traced here: 62.4 us
  starting transfers between devices  30.4 us (49%)
  Pallas kernels  18.5 us (30%)
  waiting for transfers between devices  11.8 us (19%)
  other arithmetic  1.53 us (2%)
    ppermute x6, starting transfers between devices, dense_body(): lead, trail = ([(ring if step > 1 else home)(lead[0])], [ring(trail[0])])  12.1 us
    pallas_call x5, Pallas kernels, run_expert(): pl.pallas_call(functools.partial(expert_kernel, experts, len(blocks)), ou...  12 us
    ppermute x6, waiting for transfers between devices, dense_body(): lead, trail = ([(ring if step > 1 else home)(lead[0])], [ring(trail[0])])  7.96 us
    pallas_call x2, Pallas kernels, load_weights(): pl.pallas_call(functools.partial(load_kernel, pieces), out_shape=[pltpu.V...  4.73 us
    ppermute x2, starting transfers between devices, dense_body(): first, second = (ring(mine), ring(sibling))  4.34 us
    ppermute x2, starting transfers between devices, dense_body(): first, second = (ring(first), ring(second))  4.21 us
    ppermute x1, starting transfers between devices, dense_body(): far = leap(first)  2.68 us
    ppermute x1, starting transfers between devices, dense_body(): lead = [ring(lead[0])]  2.23 us
  transfers between devices with their start and end apart: 28, of which 13 were waited for; matrix products, arithmetic and copies ran while one was open for 1% of the time, Pallas kernels for 27%

profile of v17, /device:TPU:0, one launch (start us, length us, event | category | flops | bytes accessed | tf_op | source)
XLA Modules:
  0.0 62.4 jit_solution(2336697087565115718)
XLA Ops:
  0.0 1.7 %pack.1.refs_0_ = bf16[64,2176]{1,0:T(8,128)(2,1)} custom-call(bf16[64,2048]{1,0:T(8,128)(2,1)} %tokens_ref, s32[8,64]{1,0:T(8,128)} %bitcast.3, f32[8,64]{1,0:T(8,128)} %bitcast.4), custom_call_target="tpu_custom_call" | custom-call | bytes 1024 | tf_op jit(solution)/shard_map/pack/pallas_call | solution.py:191
  1.7 0.5 collective-permute-start.1
  2.2 2.6 %collective-permute-start = (bf16[64,2176]{1,0:T(8,128)(2,1)}, bf16[64,2176]{1,0:T(8,128)(2,1)S(1)}, u32[]{:S(2)}, u32[]{:S(2)}) collective-permute-start(bf16[64,2176]{1,0:T(8,128)(2,1)} %pack.1.refs_0_), channel_id=1, source_target_pairs={{0,4},{1,3},{4,8},{5,1},{8,12},{9,5},{12,14},{13,9},{14,10},{15,13... | collective-permute-start | bytes 835592 | tf_op jit(solution)/shard_map/ppermute | solution.py:229
  4.9 1.7 %collective-permute-start.5 = (bf16[64,2176]{1,0:T(8,128)(2,1)S(1)}, bf16[64,2176]{1,0:T(8,128)(2,1)S(1)}, u32[]{:S(2)}, u32[]{:S(2)}) collective-permute-start(bf16[64,2176]{1,0:T(8,128)(2,1)S(1)} %collective-permute-done.1.refs_1_), channel_id=1, source_target_pairs={{0,4},{1,3},{4,8},{5,1},{8,12},{9,5},{12,14},{13,9},{14,10},{15,13... | collective-permute-start | bytes 835592 | tf_op jit(solution)/shard_map/ppermute | solution.py:229
  6.6 2.9 %load.2 = (bf16[1,2048,768]{2,1,0:T(8,128)(2,1)S(1)}, bf16[1,2048,768]{2,1,0:T(8,128)(2,1)S(1)}) custom-call(bf16[1,2048,768]{2,1,0:T(8,128)(2,1)} %refs_0_, bf16[1,2048,768]{2,1,0:T(8,128)(2,1)} %refs_1_.1), custom_call_target="tpu_custom_call" | custom-call | bytes 1024 | tf_op jit(solution)/shard_map/load/pallas_call | solution.py:149
  9.4 0.1 collective-permute-done.refs_2_
  9.5 2.1 %collective-permute-start.3 = (bf16[64,2176]{1,0:T(8,128)(2,1)S(1)}, bf16[64,2176]{1,0:T(8,128)(2,1)S(1)}, u32[]{:S(2)}, u32[]{:S(2)}) collective-permute-start(bf16[64,2176]{1,0:T(8,128)(2,1)S(1)} %collective-permute-done.refs_2_), channel_id=1, source_target_pairs={{0,4},{1,3},{4,8},{5,1},{8,12},{9,5},{12,14},{13,9},{14,10},{15,13... | collective-permute-start | bytes 835592 | tf_op jit(solution)/shard_map/ppermute | solution.py:238
  11.6 0.9 %collective-permute-done.5.refs_3_ = bf16[64,2176]{1,0:T(8,128)(2,1)S(1)} collective-permute-done((bf16[64,2176]{1,0:T(8,128)(2,1)S(1)}, bf16[64,2176]{1,0:T(8,128)(2,1)S(1)}, u32[]{:S(2)}, u32[]{:S(2)}) %collective-permute-start.5) | collective-permute-done | bytes 278560 | tf_op jit(solution)/shard_map/ppermute | solution.py:229
  12.5 2.1 %collective-permute-start.7 = (bf16[64,2176]{1,0:T(8,128)(2,1)S(1)}, bf16[64,2176]{1,0:T(8,128)(2,1)S(1)}, u32[]{:S(2)}, u32[]{:S(2)}) collective-permute-start(bf16[64,2176]{1,0:T(8,128)(2,1)S(1)} %collective-permute-done.5.refs_3_), channel_id=1, source_target_pairs={{0,4},{1,3},{4,8},{5,1},{8,12},{9,5},{12,14},{13,9},{14,10},{15,13... | collective-permute-start | bytes 835592 | tf_op jit(solution)/shard_map/ppermute | solution.py:238
  14.6 0.0 collective-permute-start.2
  14.6 1.9 %load.3.refs_6_.refs_4_ = bf16[1,2048,768]{2,1,0:T(8,128)(2,1)S(1)} custom-call(bf16[1,2048,768]{2,1,0:T(8,128)(2,1)} %refs_0_.1), custom_call_target="tpu_custom_call" | custom-call | bytes 1024 | tf_op jit(solution)/shard_map/load/pallas_call | solution.py:149
  16.5 0.0 collective-permute-done.3.refs_2_
  16.5 2.7 %collective-permute-start.13 = (bf16[64,2176]{1,0:T(8,128)(2,1)S(1)}, bf16[64,2176]{1,0:T(8,128)(2,1)S(1)}, u32[]{:S(2)}, u32[]{:S(2)}) collective-permute-start(bf16[64,2176]{1,0:T(8,128)(2,1)S(1)} %collective-permute-done.3.refs_2_), channel_id=1, source_target_pairs={{0,8},{1,7},{4,12},{5,3},{8,14},{9,1},{12,10},{13,5},{14,6},{15,9}... | collective-permute-start | bytes 835592 | tf_op jit(solution)/shard_map/ppermute | solution.py:242
  19.2 0.5 collective-permute-start.6
  19.7 0.0 collective-permute-start.8
  19.7 0.0 collective-permute-done.2.refs_0_
  19.8 1.6 %collective-permute-start.11 = (bf16[128,2176]{1,0:T(8,128)(2,1)S(1)}, bf16[128,2176]{1,0:T(8,128)(2,1)S(1)}, u32[]{:S(2)}, u32[]{:S(2)}) collective-permute-start(bf16[128,2176]{1,0:T(8,128)(2,1)S(1)} %pad_maximum_fusion), channel_id=1, source_target_pairs={{0,4},{1,3},{4,8},{5,1},{8,12},{9,5},{12,14},{13,9},{14,10},{15,13... | collective-permute-start | bytes 1671176 | tf_op jit(solution)/shard_map/ppermute | solution.py:243
  21.4 0.1 collective-permute-done.8.refs_1_
  21.5 2.6 %expert.5 = (bf16[64,2048]{1,0:T(8,128)(2,1)S(1)}, bf16[64,2048]{1,0:T(8,128)(2,1)S(1)}, bf16[64,2048]{1,0:T(8,128)(2,1)S(1)}, bf16[64,2048]{1,0:T(8,128)(2,1)S(1)}) custom-call(s32[1]{0:T(128)} %bitcast.own_ref, bf16[64,2176]{1,0:T(8,128)(2,1)S(1)} %collective-permute-done.4.refs_0_, bf16[64,2176]{1,0:T(8,128)(2,1)S(1)} %collective-permute-done.8.refs_1_, ...), custom_call_target="tpu_custom_call" | custom-call | flops 524288 | bytes 524288 | tf_op jit(solution)/shard_map/expert/pallas_call | solution.py:116
  24.2 2.7 %expert.6 = (bf16[64,2048]{1,0:T(8,128)(2,1)S(1)}, bf16[64,2048]{1,0:T(8,128)(2,1)S(1)}, bf16[64,2048]{1,0:T(8,128)(2,1)S(1)}, bf16[64,2048]{1,0:T(8,128)(2,1)S(1)}) custom-call(s32[1]{0:T(128)} %bitcast.own_ref, bf16[64,2176]{1,0:T(8,128)(2,1)S(1)} %collective-permute-done.2.refs_0_, bf16[64,2176]{1,0:T(8,128)(2,1)S(1)} %collective-permute-done.6.refs_1_, ...), custom_call_target="tpu_custom_call" | custom-call | flops 524288 | bytes 524288 | tf_op jit(solution)/shard_map/expert/pallas_call | solution.py:116
  26.9 0.0 collective-permute-done.13.refs_1_
  26.9 0.2 collective-permute-start.14
  27.1 1.4 %collective-permute-done.14.refs_0_ = bf16[64,2176]{1,0:T(8,128)(2,1)S(1)} collective-permute-done((bf16[64,2176]{1,0:T(8,128)(2,1)S(1)}, bf16[64,2176]{1,0:T(8,128)(2,1)S(1)}, u32[]{:S(2)}, u32[]{:S(2)}) %collective-permute-start.14) | collective-permute-done | bytes 278560 | tf_op jit(solution)/shard_map/ppermute | solution.py:249
  28.5 2.0 %expert.7 = (bf16[64,2048]{1,0:T(8,128)(2,1)S(1)}, bf16[64,2048]{1,0:T(8,128)(2,1)S(1)}) custom-call(s32[1]{0:T(128)} %bitcast.own_ref, bf16[64,2176]{1,0:T(8,128)(2,1)S(1)} %collective-permute-done.14.refs_0_, bf16[64,2176]{1,0:T(8,128)(2,1)S(1)} %collective-permute-done.13.refs_1_, bf16[1,2048,768]{2,1,0:T(8,128)(2,1)S(1)} %get-tuple-element.39.refs_4_.refs_2_, ...), custom_call_target="tpu_custom_call" | custom-call | flops 262144 | bytes 262144 | tf_op jit(solution)/shard_map/expert/pallas_call | solution.py:116
  30.5 0.2 collective-permute-start.15
  30.8 0.3 collective-permute-done.11.refs_1_
  31.1 0.2 collective-permute-start.12
  31.3 0.3 collective-permute-start.10
  31.6 0.2 collective-permute-start.16
  31.8 0.4 collective-permute-done.15
  32.1 0.1 add_convert_fusion.7
  32.2 2.2 %collective-permute-start.18 = (bf16[64,2048]{1,0:T(8,128)(2,1)S(1)}, bf16[64,2048]{1,0:T(8,128)(2,1)S(1)}, u32[]{:S(2)}, u32[]{:S(2)}) collective-permute-start(bf16[64,2048]{1,0:T(8,128)(2,1)S(1)} %add_convert_fusion.7), channel_id=1, source_target_pairs={{0,4},{1,3},{4,8},{5,1},{8,12},{9,5},{12,14},{13,9},{14,10},{15,13... | collective-permute-start | bytes 786440 | tf_op jit(solution)/shard_map/ppermute | solution.py:252
  34.5 0.0 collective-permute-done.10
  34.5 0.0 collective-permute-done.16
  34.5 0.0 collective-permute-done.12.refs_0_
  34.5 2.7 %expert.8 = (bf16[64,2048]{1,0:T(8,128)(2,1)S(1)}, bf16[64,2048]{1,0:T(8,128)(2,1)S(1)}, bf16[64,2048]{1,0:T(8,128)(2,1)S(1)}, bf16[64,2048]{1,0:T(8,128)(2,1)S(1)}) custom-call(s32[1]{0:T(128)} %bitcast.own_ref, bf16[128,2176]{1,0:T(8,128)(2,1)S(1)} %collective-permute-done.12.refs_0_, bf16[128,2176]{1,0:T(8,128)(2,1)S(1)} %collective-permute-done.11.refs_1_, ...), custom_call_target="tpu_custom_call" | custom-call | flops 524288 | bytes 524288 | tf_op jit(solution)/shard_map/expert/pallas_call | solution.py:116
  37.1 0.1 collective-permute-start.17
  37.2 0.5 collective-permute-start.9
  37.7 0.1 collective-permute-start.24
  37.8 0.4 collective-permute-start.20
  38.2 0.4 collective-permute-done.18
  38.7 0.1 collective-permute-done.17
  38.7 0.1 add_convert_fusion.6
  38.8 2.5 %collective-permute-start.19 = (bf16[64,2048]{1,0:T(8,128)(2,1)S(1)}, bf16[64,2048]{1,0:T(8,128)(2,1)S(1)}, u32[]{:S(2)}, u32[]{:S(2)}) collective-permute-start(bf16[64,2048]{1,0:T(8,128)(2,1)S(1)} %add_convert_fusion.6), channel_id=1, source_target_pairs={{0,4},{1,3},{4,8},{5,1},{8,12},{9,5},{12,14},{13,9},{14,10},{15,13... | collective-permute-start | bytes 786440 | tf_op jit(solution)/shard_map/ppermute | solution.py:261
  41.4 0.0 collective-permute-done.20
  41.4 0.1 add_convert_fusion.5
  41.4 2.2 %collective-permute-start.25 = (bf16[64,2048]{1,0:T(8,128)(2,1)S(1)}, bf16[64,2048]{1,0:T(8,128)(2,1)S(1)}, u32[]{:S(2)}, u32[]{:S(2)}) collective-permute-start(bf16[64,2048]{1,0:T(8,128)(2,1)S(1)} %add_convert_fusion.5), channel_id=1, source_target_pairs={{0,4},{1,3},{4,8},{5,1},{8,12},{9,5},{12,14},{13,9},{14,10},{15,13... | collective-permute-start | bytes 786440 | tf_op jit(solution)/shard_map/ppermute | solution.py:261
  43.6 2.0 %expert.9 = (bf16[64,2048]{1,0:T(8,128)(2,1)S(1)}, bf16[64,2048]{1,0:T(8,128)(2,1)S(1)}) custom-call(s32[1]{0:T(128)} %bitcast.own_ref, bf16[64,2176]{1,0:T(8,128)(2,1)S(1)} %copy-done, bf16[64,2176]{1,0:T(8,128)(2,1)S(1)} %collective-permute-done.1.refs_1_, bf16[1,2048,768]{2,1,0:T(8,128)(2,1)S(1)} %get-tuple-element.39.refs_4_.refs_2_, ...), custom_call_target="tpu_custom_call" | custom-call | flops 262144 | bytes 262144 | tf_op jit(solution)/shard_map/expert/pallas_call | solution.py:116
  45.6 0.1 collective-permute-start.23
  45.7 0.1 add_convert_fusion.4
  45.8 2.0 %collective-permute-start.21 = (bf16[64,2048]{1,0:T(8,128)(2,1)S(1)}, bf16[64,2048]{1,0:T(8,128)(2,1)S(1)}, u32[]{:S(2)}, u32[]{:S(2)}) collective-permute-start(bf16[64,2048]{1,0:T(8,128)(2,1)S(1)} %add_convert_fusion.4), channel_id=1, source_target_pairs={{0,4},{1,3},{4,8},{5,1},{8,12},{9,5},{12,14},{13,9},{14,10},{15,13... | collective-permute-start | bytes 786440 | tf_op jit(solution)/shard_map/ppermute | solution.py:261
  47.9 0.2 collective-permute-done.25
  48.1 0.1 add_convert_fusion.2
  48.2 2.5 %collective-permute-start.26 = (bf16[64,2048]{1,0:T(8,128)(2,1)S(1)}, bf16[64,2048]{1,0:T(8,128)(2,1)S(1)}, u32[]{:S(2)}, u32[]{:S(2)}) collective-permute-start(bf16[64,2048]{1,0:T(8,128)(2,1)S(1)} %add_convert_fusion.2), channel_id=1, source_target_pairs={{0,4},{1,3},{4,8},{5,1},{8,12},{9,5},{12,14},{13,9},{14,10},{15,13... | collective-permute-start | bytes 786440 | tf_op jit(solution)/shard_map/ppermute | solution.py:261
  50.7 1.6 %collective-permute-done.21 = bf16[64,2048]{1,0:T(8,128)(2,1)S(1)} collective-permute-done((bf16[64,2048]{1,0:T(8,128)(2,1)S(1)}, bf16[64,2048]{1,0:T(8,128)(2,1)S(1)}, u32[]{:S(2)}, u32[]{:S(2)}) %collective-permute-start.21) | collective-permute-done | bytes 262176 | tf_op jit(solution)/shard_map/ppermute | solution.py:261
  52.3 0.1 add_convert_fusion.3
  52.4 0.8 %collective-permute-start.22 = (bf16[64,2048]{1,0:T(8,128)(2,1)S(1)}, bf16[64,2048]{1,0:T(8,128)(2,1)S(1)}, u32[]{:S(2)}, u32[]{:S(2)}) collective-permute-start(bf16[64,2048]{1,0:T(8,128)(2,1)S(1)} %add_convert_fusion.3), channel_id=1, source_target_pairs={{0,5},{1,2},{4,9},{5,0},{8,13},{9,4},{12,15},{13,8},{14,11},{15,12... | collective-permute-start | bytes 786440 | tf_op jit(solution)/shard_map/ppermute | solution.py:261
  53.1 1.9 %collective-permute-done.26 = bf16[64,2048]{1,0:T(8,128)(2,1)S(1)} collective-permute-done((bf16[64,2048]{1,0:T(8,128)(2,1)S(1)}, bf16[64,2048]{1,0:T(8,128)(2,1)S(1)}, u32[]{:S(2)}, u32[]{:S(2)}) %collective-permute-start.26) | collective-permute-done | bytes 262176 | tf_op jit(solution)/shard_map/ppermute | solution.py:261
  55.1 0.1 add_convert_fusion.1
  55.2 2.0 %collective-permute-start.27 = (bf16[64,2048]{1,0:T(8,128)(2,1)S(1)}, bf16[64,2048]{1,0:T(8,128)(2,1)S(1)}, u32[]{:S(2)}, u32[]{:S(2)}) collective-permute-start(bf16[64,2048]{1,0:T(8,128)(2,1)S(1)} %add_convert_fusion.1), channel_id=1, source_target_pairs={{0,4},{1,3},{4,8},{5,1},{8,12},{9,5},{12,14},{13,9},{14,10},{15,13... | collective-permute-start | bytes 786440 | tf_op jit(solution)/shard_map/ppermute | solution.py:261
  57.2 1.0 %collective-permute-done.22 = bf16[64,2048]{1,0:T(8,128)(2,1)S(1)} collective-permute-done((bf16[64,2048]{1,0:T(8,128)(2,1)S(1)}, bf16[64,2048]{1,0:T(8,128)(2,1)S(1)}, u32[]{:S(2)}, u32[]{:S(2)}) %collective-permute-start.22) | collective-permute-done | bytes 262176 | tf_op jit(solution)/shard_map/ppermute | solution.py:261
  58.2 0.1 convert_add_fusion
  58.3 3.3 %collective-permute-done.27 = bf16[64,2048]{1,0:T(8,128)(2,1)S(1)} collective-permute-done((bf16[64,2048]{1,0:T(8,128)(2,1)S(1)}, bf16[64,2048]{1,0:T(8,128)(2,1)S(1)}, u32[]{:S(2)}, u32[]{:S(2)}) %collective-permute-start.27) | collective-permute-done | bytes 262176 | tf_op jit(solution)/shard_map/ppermute | solution.py:261
  61.6 0.8 %add_convert_fusion = bf16[64,2048]{1,0:T(8,128)(2,1)} fusion(f32[64,2048]{1,0:T(8,128)S(1)} %convert_add_fusion, bf16[64,2048]{1,0:T(8,128)(2,1)S(1)} %collective-permute-done.27), kind=kLoop, calls=%fused_computation.1 | loop fusion | flops 393216 | bytes 1048576 | tf_op jit(solution)/shard_map/convert_element_type | solution.py:210
  (12 shorter events, 0.1 us)
Async XLA Ops:
  1.7 3.2 %collective-permute-start.1 = (bf16[64,2176]{1,0:T(8,128)(2,1)}, bf16[64,2176]{1,0:T(8,128)(2,1)S(1)}, u32[]{:S(2)}, u32[]{:S(2)}) collective-permute-start(bf16[64,2176]{1,0:T(8,128)(2,1)} %pack.1.refs_0_), channel_id=1, source_target_pairs={{0,1},{1,0},{2,3},{3,2},{4,5},{5,4},{6,7},{7,6},{8,9},{9,8},{10,11... | collective-permute-start | bytes 835592 | tf_op jit(solution)/shard_map/ppermute | solution.py:228
  2.2 7.3 %collective-permute-start = (bf16[64,2176]{1,0:T(8,128)(2,1)}, bf16[64,2176]{1,0:T(8,128)(2,1)S(1)}, u32[]{:S(2)}, u32[]{:S(2)}) collective-permute-start(bf16[64,2176]{1,0:T(8,128)(2,1)} %pack.1.refs_0_), channel_id=1, source_target_pairs={{0,4},{1,3},{4,8},{5,1},{8,12},{9,5},{12,14},{13,9},{14,10},{15,13... | collective-permute-start | bytes 835592 | tf_op jit(solution)/shard_map/ppermute | solution.py:229
  4.9 7.6 %collective-permute-start.5 = (bf16[64,2176]{1,0:T(8,128)(2,1)S(1)}, bf16[64,2176]{1,0:T(8,128)(2,1)S(1)}, u32[]{:S(2)}, u32[]{:S(2)}) collective-permute-start(bf16[64,2176]{1,0:T(8,128)(2,1)S(1)} %collective-permute-done.1.refs_1_), channel_id=1, source_target_pairs={{0,4},{1,3},{4,8},{5,1},{8,12},{9,5},{12,14},{13,9},{14,10},{15,13... | collective-permute-start | bytes 835592 | tf_op jit(solution)/shard_map/ppermute | solution.py:229
  9.5 7.0 %collective-permute-start.3 = (bf16[64,2176]{1,0:T(8,128)(2,1)S(1)}, bf16[64,2176]{1,0:T(8,128)(2,1)S(1)}, u32[]{:S(2)}, u32[]{:S(2)}) collective-permute-start(bf16[64,2176]{1,0:T(8,128)(2,1)S(1)} %collective-permute-done.refs_2_), channel_id=1, source_target_pairs={{0,4},{1,3},{4,8},{5,1},{8,12},{9,5},{12,14},{13,9},{14,10},{15,13... | collective-permute-start | bytes 835592 | tf_op jit(solution)/shard_map/ppermute | solution.py:238
  12.5 7.2 %collective-permute-start.7 = (bf16[64,2176]{1,0:T(8,128)(2,1)S(1)}, bf16[64,2176]{1,0:T(8,128)(2,1)S(1)}, u32[]{:S(2)}, u32[]{:S(2)}) collective-permute-start(bf16[64,2176]{1,0:T(8,128)(2,1)S(1)} %collective-permute-done.5.refs_3_), channel_id=1, source_target_pairs={{0,4},{1,3},{4,8},{5,1},{8,12},{9,5},{12,14},{13,9},{14,10},{15,13... | collective-permute-start | bytes 835592 | tf_op jit(solution)/shard_map/ppermute | solution.py:238
  14.6 5.1 %collective-permute-start.2 = (bf16[64,2176]{1,0:T(8,128)(2,1)S(1)}, bf16[64,2176]{1,0:T(8,128)(2,1)S(1)}, u32[]{:S(2)}, u32[]{:S(2)}) collective-permute-start(bf16[64,2176]{1,0:T(8,128)(2,1)S(1)} %collective-permute-done.refs_2_), channel_id=1, source_target_pairs={{0,1},{1,0},{2,3},{3,2},{4,5},{5,4},{6,7},{7,6},{8,9},{9,8},{10,11... | collective-permute-start | bytes 835592 | tf_op jit(solution)/shard_map/ppermute | solution.py:241
  16.5 10.4 %collective-permute-start.13 = (bf16[64,2176]{1,0:T(8,128)(2,1)S(1)}, bf16[64,2176]{1,0:T(8,128)(2,1)S(1)}, u32[]{:S(2)}, u32[]{:S(2)}) collective-permute-start(bf16[64,2176]{1,0:T(8,128)(2,1)S(1)} %collective-permute-done.3.refs_2_), channel_id=1, source_target_pairs={{0,8},{1,7},{4,12},{5,3},{8,14},{9,1},{12,10},{13,5},{14,6},{15,9}... | collective-permute-start | bytes 835592 | tf_op jit(solution)/shard_map/ppermute | solution.py:242
  19.2 2.2 %collective-permute-start.4 = (bf16[64,2176]{1,0:T(8,128)(2,1)S(1)}, bf16[64,2176]{1,0:T(8,128)(2,1)S(1)}, u32[]{:S(2)}, u32[]{:S(2)}) collective-permute-start(bf16[64,2176]{1,0:T(8,128)(2,1)S(1)} %collective-permute-done.3.refs_2_), channel_id=1, source_target_pairs={{0,1},{1,0},{2,3},{3,2},{4,5},{5,4},{6,7},{7,6},{8,9},{9,8},{10,11... | collective-permute-start | bytes 835592 | tf_op jit(solution)/shard_map/ppermute | solution.py:241
  19.2 2.2 %collective-permute-start.6 = (bf16[64,2176]{1,0:T(8,128)(2,1)S(1)}, bf16[64,2176]{1,0:T(8,128)(2,1)S(1)}, u32[]{:S(2)}, u32[]{:S(2)}) collective-permute-start(bf16[64,2176]{1,0:T(8,128)(2,1)S(1)} %collective-permute-done.5.refs_3_), channel_id=1, source_target_pairs={{0,1},{1,0},{2,3},{3,2},{4,5},{5,4},{6,7},{7,6},{8,9},{9,8},{10,11... | collective-permute-start | bytes 835592 | tf_op jit(solution)/shard_map/ppermute | solution.py:241
  19.7 1.8 %collective-permute-start.8 = (bf16[64,2176]{1,0:T(8,128)(2,1)S(1)}, bf16[64,2176]{1,0:T(8,128)(2,1)S(1)}, u32[]{:S(2)}, u32[]{:S(2)}) collective-permute-start(bf16[64,2176]{1,0:T(8,128)(2,1)S(1)} %collective-permute-done.7.refs_3_), channel_id=1, source_target_pairs={{0,1},{1,0},{2,3},{3,2},{4,5},{5,4},{6,7},{7,6},{8,9},{9,8},{10,11... | collective-permute-start | bytes 835592 | tf_op jit(solution)/shard_map/ppermute | solution.py:241
  19.8 11.3 %collective-permute-start.11 = (bf16[128,2176]{1,0:T(8,128)(2,1)S(1)}, bf16[128,2176]{1,0:T(8,128)(2,1)S(1)}, u32[]{:S(2)}, u32[]{:S(2)}) collective-permute-start(bf16[128,2176]{1,0:T(8,128)(2,1)S(1)} %pad_maximum_fusion), channel_id=1, source_target_pairs={{0,4},{1,3},{4,8},{5,1},{8,12},{9,5},{12,14},{13,9},{14,10},{15,13... | collective-permute-start | bytes 1671176 | tf_op jit(solution)/shard_map/ppermute | solution.py:243
  26.9 1.6 %collective-permute-start.14 = (bf16[64,2176]{1,0:T(8,128)(2,1)S(1)}, bf16[64,2176]{1,0:T(8,128)(2,1)S(1)}, u32[]{:S(2)}, u32[]{:S(2)}) collective-permute-start(bf16[64,2176]{1,0:T(8,128)(2,1)S(1)} %collective-permute-done.13.refs_1_), channel_id=1, source_target_pairs={{0,1},{1,0},{2,3},{3,2},{4,5},{5,4},{6,7},{7,6},{8,9},{9,8},{10,11... | collective-permute-start | bytes 835592 | tf_op jit(solution)/shard_map/ppermute | solution.py:249
  30.5 1.6 %collective-permute-start.15 = (bf16[64,2048]{1,0:T(8,128)(2,1)S(1)}, bf16[64,2048]{1,0:T(8,128)(2,1)S(1)}, u32[]{:S(2)}, u32[]{:S(2)}) collective-permute-start(bf16[64,2048]{1,0:T(8,128)(2,1)S(1)} %get-tuple-element.52), channel_id=1, source_target_pairs={{0,1},{1,0},{2,3},{3,2},{4,5},{5,4},{6,7},{7,6},{8,9},{9,8},{10,11... | collective-permute-start | bytes 786440 | tf_op jit(solution)/shard_map/ppermute | solution.py:250
  31.1 3.4 %collective-permute-start.12 = (bf16[128,2176]{1,0:T(8,128)(2,1)S(1)}, bf16[128,2176]{1,0:T(8,128)(2,1)S(1)}, u32[]{:S(2)}, u32[]{:S(2)}) collective-permute-start(bf16[128,2176]{1,0:T(8,128)(2,1)S(1)} %collective-permute-done.11.refs_1_), channel_id=1, source_target_pairs={{0,1},{1,0},{2,3},{3,2},{4,5},{5,4},{6,7},{7,6},{8,9},{9,8},{10,11... | collective-permute-start | bytes 1671176 | tf_op jit(solution)/shard_map/ppermute | solution.py:251
  31.3 3.2 %collective-permute-start.10 = (bf16[64,2048]{1,0:T(8,128)(2,1)S(1)}, bf16[64,2048]{1,0:T(8,128)(2,1)S(1)}, u32[]{:S(2)}, u32[]{:S(2)}) collective-permute-start(bf16[64,2048]{1,0:T(8,128)(2,1)S(1)} %get-tuple-element.49), channel_id=1, source_target_pairs={{0,1},{1,0},{2,3},{3,2},{4,5},{5,4},{6,7},{7,6},{8,9},{9,8},{10,11... | collective-permute-start | bytes 786440 | tf_op jit(solution)/shard_map/ppermute | solution.py:244
  31.6 2.9 %collective-permute-start.16 = (bf16[64,2048]{1,0:T(8,128)(2,1)S(1)}, bf16[64,2048]{1,0:T(8,128)(2,1)S(1)}, u32[]{:S(2)}, u32[]{:S(2)}) collective-permute-start(bf16[64,2048]{1,0:T(8,128)(2,1)S(1)} %get-tuple-element.53), channel_id=1, source_target_pairs={{0,1},{1,0},{2,3},{3,2},{4,5},{5,4},{6,7},{7,6},{8,9},{9,8},{10,11... | collective-permute-start | bytes 786440 | tf_op jit(solution)/shard_map/ppermute | solution.py:244
  32.2 11.4 %copy-start = (bf16[64,2176]{1,0:T(8,128)(2,1)S(1)}, bf16[64,2176]{1,0:T(8,128)(2,1)}, u32[]{:S(2)}) copy-start(bf16[64,2176]{1,0:T(8,128)(2,1)} %pack.1.refs_0_) | copy-start | bytes 835588
  32.2 6.4 %collective-permute-start.18 = (bf16[64,2048]{1,0:T(8,128)(2,1)S(1)}, bf16[64,2048]{1,0:T(8,128)(2,1)S(1)}, u32[]{:S(2)}, u32[]{:S(2)}) collective-permute-start(bf16[64,2048]{1,0:T(8,128)(2,1)S(1)} %add_convert_fusion.7), channel_id=1, source_target_pairs={{0,4},{1,3},{4,8},{5,1},{8,12},{9,5},{12,14},{13,9},{14,10},{15,13... | collective-permute-start | bytes 786440 | tf_op jit(solution)/shard_map/ppermute | solution.py:252
  37.1 1.6 %collective-permute-start.17 = (bf16[64,2048]{1,0:T(8,128)(2,1)S(1)}, bf16[64,2048]{1,0:T(8,128)(2,1)S(1)}, u32[]{:S(2)}, u32[]{:S(2)}) collective-permute-start(bf16[64,2048]{1,0:T(8,128)(2,1)S(1)} %get-tuple-element.56), channel_id=1, source_target_pairs={{0,1},{1,0},{2,3},{3,2},{4,5},{5,4},{6,7},{7,6},{8,9},{9,8},{10,11... | collective-permute-start | bytes 786440 | tf_op jit(solution)/shard_map/ppermute | solution.py:244
  37.2 13.5 %collective-permute-start.9 = (bf16[64,2048]{1,0:T(8,128)(2,1)S(1)}, bf16[64,2048]{1,0:T(8,128)(2,1)S(1)}, u32[]{:S(2)}, u32[]{:S(2)}) collective-permute-start(bf16[64,2048]{1,0:T(8,128)(2,1)S(1)} %get-tuple-element.48), channel_id=1, source_target_pairs={{0,1},{1,0},{2,3},{3,2},{4,5},{5,4},{6,7},{7,6},{8,9},{9,8},{10,11... | collective-permute-start | bytes 786440 | tf_op jit(solution)/shard_map/ppermute | solution.py:244
  37.7 15.4 %collective-permute-start.24 = (bf16[64,2048]{1,0:T(8,128)(2,1)S(1)}, bf16[64,2048]{1,0:T(8,128)(2,1)S(1)}, u32[]{:S(2)}, u32[]{:S(2)}) collective-permute-start(bf16[64,2048]{1,0:T(8,128)(2,1)S(1)} %get-tuple-element.66), channel_id=1, source_target_pairs={{0,1},{1,0},{2,3},{3,2},{4,5},{5,4},{6,7},{7,6},{8,9},{9,8},{10,11... | collective-permute-start | bytes 786440 | tf_op jit(solution)/shard_map/ppermute | solution.py:244
  37.8 3.6 %collective-permute-start.20 = (bf16[64,2048]{1,0:T(8,128)(2,1)S(1)}, bf16[64,2048]{1,0:T(8,128)(2,1)S(1)}, u32[]{:S(2)}, u32[]{:S(2)}) collective-permute-start(bf16[64,2048]{1,0:T(8,128)(2,1)S(1)} %get-tuple-element.59), channel_id=1, source_target_pairs={{0,1},{1,0},{2,3},{3,2},{4,5},{5,4},{6,7},{7,6},{8,9},{9,8},{10,11... | collective-permute-start | bytes 786440 | tf_op jit(solution)/shard_map/ppermute | solution.py:244
  38.8 6.9 %collective-permute-start.19 = (bf16[64,2048]{1,0:T(8,128)(2,1)S(1)}, bf16[64,2048]{1,0:T(8,128)(2,1)S(1)}, u32[]{:S(2)}, u32[]{:S(2)}) collective-permute-start(bf16[64,2048]{1,0:T(8,128)(2,1)S(1)} %add_convert_fusion.6), channel_id=1, source_target_pairs={{0,4},{1,3},{4,8},{5,1},{8,12},{9,5},{12,14},{13,9},{14,10},{15,13... | collective-permute-start | bytes 786440 | tf_op jit(solution)/shard_map/ppermute | solution.py:261
  41.4 6.6 %collective-permute-start.25 = (bf16[64,2048]{1,0:T(8,128)(2,1)S(1)}, bf16[64,2048]{1,0:T(8,128)(2,1)S(1)}, u32[]{:S(2)}, u32[]{:S(2)}) collective-permute-start(bf16[64,2048]{1,0:T(8,128)(2,1)S(1)} %add_convert_fusion.5), channel_id=1, source_target_pairs={{0,4},{1,3},{4,8},{5,1},{8,12},{9,5},{12,14},{13,9},{14,10},{15,13... | collective-permute-start | bytes 786440 | tf_op jit(solution)/shard_map/ppermute | solution.py:261
  45.6 11.6 %collective-permute-start.23 = (bf16[64,2048]{1,0:T(8,128)(2,1)S(1)}, bf16[64,2048]{1,0:T(8,128)(2,1)S(1)}, u32[]{:S(2)}, u32[]{:S(2)}) collective-permute-start(bf16[64,2048]{1,0:T(8,128)(2,1)S(1)} %get-tuple-element.63), channel_id=1, source_target_pairs={{0,1},{1,0},{2,3},{3,2},{4,5},{5,4},{6,7},{7,6},{8,9},{9,8},{10,11... | collective-permute-start | bytes 786440 | tf_op jit(solution)/shard_map/ppermute | solution.py:262
  45.8 6.4 %collective-permute-start.21 = (bf16[64,2048]{1,0:T(8,128)(2,1)S(1)}, bf16[64,2048]{1,0:T(8,128)(2,1)S(1)}, u32[]{:S(2)}, u32[]{:S(2)}) collective-permute-start(bf16[64,2048]{1,0:T(8,128)(2,1)S(1)} %add_convert_fusion.4), channel_id=1, source_target_pairs={{0,4},{1,3},{4,8},{5,1},{8,12},{9,5},{12,14},{13,9},{14,10},{15,13... | collective-permute-start | bytes 786440 | tf_op jit(solution)/shard_map/ppermute | solution.py:261
  48.2 6.9 %collective-permute-start.26 = (bf16[64,2048]{1,0:T(8,128)(2,1)S(1)}, bf16[64,2048]{1,0:T(8,128)(2,1)S(1)}, u32[]{:S(2)}, u32[]{:S(2)}) collective-permute-start(bf16[64,2048]{1,0:T(8,128)(2,1)S(1)} %add_convert_fusion.2), channel_id=1, source_target_pairs={{0,4},{1,3},{4,8},{5,1},{8,12},{9,5},{12,14},{13,9},{14,10},{15,13... | collective-permute-start | bytes 786440 | tf_op jit(solution)/shard_map/ppermute | solution.py:261
  52.4 5.9 %collective-permute-start.22 = (bf16[64,2048]{1,0:T(8,128)(2,1)S(1)}, bf16[64,2048]{1,0:T(8,128)(2,1)S(1)}, u32[]{:S(2)}, u32[]{:S(2)}) collective-permute-start(bf16[64,2048]{1,0:T(8,128)(2,1)S(1)} %add_convert_fusion.3), channel_id=1, source_target_pairs={{0,5},{1,2},{4,9},{5,0},{8,13},{9,4},{12,15},{13,8},{14,11},{15,12... | collective-permute-start | bytes 786440 | tf_op jit(solution)/shard_map/ppermute | solution.py:261
  55.2 6.4 %collective-permute-start.27 = (bf16[64,2048]{1,0:T(8,128)(2,1)S(1)}, bf16[64,2048]{1,0:T(8,128)(2,1)S(1)}, u32[]{:S(2)}, u32[]{:S(2)}) collective-permute-start(bf16[64,2048]{1,0:T(8,128)(2,1)S(1)} %add_convert_fusion.1), channel_id=1, source_target_pairs={{0,4},{1,3},{4,8},{5,1},{8,12},{9,5},{12,14},{13,9},{14,10},{15,13... | collective-permute-start | bytes 786440 | tf_op jit(solution)/shard_map/ppermute | solution.py:261

commit v18 on v17

--- a/solution.py
+++ b/solution.py
@@ -245,7 +245,7 @@
     sums = {2: run(after(blocks[2][0], *blocks[1][:2]), *blocks[2][1:])}
     sums[1] = run(after(blocks[1][0], sums[2][0]), *blocks[1][1:])
     far = after(far, sums[1][0])
-    sums[2], sums[1] = turned(*sums[2]), turned(*sums[1])
+    sums[2] = turned(*sums[2])
     keep, send = run(swap(far), far)
     lead, trail = [added(keep, swap(send))], []
     sums[3] = turned(*run(after(swap(both), lead[0], *sums[2][2:]), both))
@@ -258,6 +258,7 @@
         trail = [added(after(keep_trail, lead[0]), send_trail, *trail)]
         if step == 3:
             kept, other = run(after(mine, trail[0]), sibling)
+            sums[1] = turned(*sums[1][:2], *[after(sent, trail[0]) for sent in sums[1][2:]])
         lead, trail = [(ring if step > 1 else home)(lead[0])], [ring(trail[0])]
     near = lax.optimization_barrier(added(lead[0], kept, swap(other), kind=jnp.float32))
     return added(near, trail[0])

time: 62.5 us -> 63.1 us (level)
  waiting for transfers between devices: 11.8 us -> 13.4 us
  starting transfers between devices: 30.4 us -> 29.4 us
    ppermute x6, waiting for transfers between devices: 7.96 us -> 9.09 us  [dense_body(): lead, trail = ([(ring if step > 1 else home)(lead[0])], [ring(trail[0])])]
    ppermute x6, starting transfers between devices: 12.1 us -> 10.9 us  [dense_body(): lead, trail = ([(ring if step > 1 else home)(lead[0])], [ring(trail[0])])]
    ppermute x3, starting transfers between devices: 0.91 us -> 0.24 us  [dense_body(): swap(send)]
where the time goes in v18:
time: 63.1 us; the launch traced here: 62.9 us
  starting transfers between devices  29.4 us (47%)
  Pallas kernels  18.5 us (29%)
  waiting for transfers between devices  13.4 us (21%)
  other arithmetic  1.53 us (2%)
    pallas_call x5, Pallas kernels, run_expert(): pl.pallas_call(functools.partial(expert_kernel, experts, len(blocks)), ou...  12 us
    ppermute x6, starting transfers between devices, dense_body(): lead, trail = ([(ring if step > 1 else home)(lead[0])], [ring(trail[0])])  10.9 us
    ppermute x6, waiting for transfers between devices, dense_body(): lead, trail = ([(ring if step > 1 else home)(lead[0])], [ring(trail[0])])  9.09 us
    pallas_call x2, Pallas kernels, load_weights(): pl.pallas_call(functools.partial(load_kernel, pieces), out_shape=[pltpu.V...  4.73 us
    ppermute x2, starting transfers between devices, dense_body(): first, second = (ring(mine), ring(sibling))  4.34 us
    ppermute x2, starting transfers between devices, dense_body(): first, second = (ring(first), ring(second))  4.21 us
    ppermute x1, starting transfers between devices, dense_body(): far = leap(first)  2.68 us
    ppermute x1, starting transfers between devices, dense_body(): lead = [ring(lead[0])]  2.23 us
  transfers between devices with their start and end apart: 28, of which 13 were waited for; matrix products, arithmetic and copies ran while one was open for 1% of the time, Pallas kernels for 27%

profile of v18, /device:TPU:0, one launch (start us, length us, event | category | flops | bytes accessed | tf_op | source)
XLA Modules:
  0.0 62.9 jit_solution(13151530054784083480)
XLA Ops:
  0.0 1.7 %pack.1.refs_0_ = bf16[64,2176]{1,0:T(8,128)(2,1)} custom-call(bf16[64,2048]{1,0:T(8,128)(2,1)} %tokens_ref, s32[8,64]{1,0:T(8,128)} %bitcast.3, f32[8,64]{1,0:T(8,128)} %bitcast.4), custom_call_target="tpu_custom_call" | custom-call | bytes 1024 | tf_op jit(solution)/shard_map/pack/pallas_call | solution.py:191
  1.7 0.5 collective-permute-start.1
  2.2 2.6 %collective-permute-start = (bf16[64,2176]{1,0:T(8,128)(2,1)}, bf16[64,2176]{1,0:T(8,128)(2,1)S(1)}, u32[]{:S(2)}, u32[]{:S(2)}) collective-permute-start(bf16[64,2176]{1,0:T(8,128)(2,1)} %pack.1.refs_0_), channel_id=1, source_target_pairs={{0,4},{1,3},{4,8},{5,1},{8,12},{9,5},{12,14},{13,9},{14,10},{15,13... | collective-permute-start | bytes 835592 | tf_op jit(solution)/shard_map/ppermute | solution.py:229
  4.9 1.7 %collective-permute-start.5 = (bf16[64,2176]{1,0:T(8,128)(2,1)S(1)}, bf16[64,2176]{1,0:T(8,128)(2,1)S(1)}, u32[]{:S(2)}, u32[]{:S(2)}) collective-permute-start(bf16[64,2176]{1,0:T(8,128)(2,1)S(1)} %collective-permute-done.1.refs_1_), channel_id=1, source_target_pairs={{0,4},{1,3},{4,8},{5,1},{8,12},{9,5},{12,14},{13,9},{14,10},{15,13... | collective-permute-start | bytes 835592 | tf_op jit(solution)/shard_map/ppermute | solution.py:229
  6.6 2.9 %load.2 = (bf16[1,2048,768]{2,1,0:T(8,128)(2,1)S(1)}, bf16[1,2048,768]{2,1,0:T(8,128)(2,1)S(1)}) custom-call(bf16[1,2048,768]{2,1,0:T(8,128)(2,1)} %refs_0_, bf16[1,2048,768]{2,1,0:T(8,128)(2,1)} %refs_1_.1), custom_call_target="tpu_custom_call" | custom-call | bytes 1024 | tf_op jit(solution)/shard_map/load/pallas_call | solution.py:149
  9.4 0.1 collective-permute-done.refs_2_
  9.5 2.1 %collective-permute-start.3 = (bf16[64,2176]{1,0:T(8,128)(2,1)S(1)}, bf16[64,2176]{1,0:T(8,128)(2,1)S(1)}, u32[]{:S(2)}, u32[]{:S(2)}) collective-permute-start(bf16[64,2176]{1,0:T(8,128)(2,1)S(1)} %collective-permute-done.refs_2_), channel_id=1, source_target_pairs={{0,4},{1,3},{4,8},{5,1},{8,12},{9,5},{12,14},{13,9},{14,10},{15,13... | collective-permute-start | bytes 835592 | tf_op jit(solution)/shard_map/ppermute | solution.py:238
  11.6 0.9 %collective-permute-done.5.refs_3_ = bf16[64,2176]{1,0:T(8,128)(2,1)S(1)} collective-permute-done((bf16[64,2176]{1,0:T(8,128)(2,1)S(1)}, bf16[64,2176]{1,0:T(8,128)(2,1)S(1)}, u32[]{:S(2)}, u32[]{:S(2)}) %collective-permute-start.5) | collective-permute-done | bytes 278560 | tf_op jit(solution)/shard_map/ppermute | solution.py:229
  12.5 2.1 %collective-permute-start.7 = (bf16[64,2176]{1,0:T(8,128)(2,1)S(1)}, bf16[64,2176]{1,0:T(8,128)(2,1)S(1)}, u32[]{:S(2)}, u32[]{:S(2)}) collective-permute-start(bf16[64,2176]{1,0:T(8,128)(2,1)S(1)} %collective-permute-done.5.refs_3_), channel_id=1, source_target_pairs={{0,4},{1,3},{4,8},{5,1},{8,12},{9,5},{12,14},{13,9},{14,10},{15,13... | collective-permute-start | bytes 835592 | tf_op jit(solution)/shard_map/ppermute | solution.py:238
  14.6 1.9 %load.3.refs_6_.refs_4_ = bf16[1,2048,768]{2,1,0:T(8,128)(2,1)S(1)} custom-call(bf16[1,2048,768]{2,1,0:T(8,128)(2,1)} %refs_0_.1), custom_call_target="tpu_custom_call" | custom-call | bytes 1024 | tf_op jit(solution)/shard_map/load/pallas_call | solution.py:149
  16.5 0.0 collective-permute-done.3.refs_2_
  16.5 2.7 %collective-permute-start.11 = (bf16[64,2176]{1,0:T(8,128)(2,1)S(1)}, bf16[64,2176]{1,0:T(8,128)(2,1)S(1)}, u32[]{:S(2)}, u32[]{:S(2)}) collective-permute-start(bf16[64,2176]{1,0:T(8,128)(2,1)S(1)} %collective-permute-done.3.refs_2_), channel_id=1, source_target_pairs={{0,8},{1,7},{4,12},{5,3},{8,14},{9,1},{12,10},{13,5},{14,6},{15,9}... | collective-permute-start | bytes 835592 | tf_op jit(solution)/shard_map/ppermute | solution.py:242
  19.2 0.0 collective-permute-start.4
  19.2 0.5 collective-permute-start.6
  19.7 0.0 collective-permute-start.8
  19.7 0.0 collective-permute-done.2.refs_0_
  19.8 1.6 %collective-permute-start.9 = (bf16[128,2176]{1,0:T(8,128)(2,1)S(1)}, bf16[128,2176]{1,0:T(8,128)(2,1)S(1)}, u32[]{:S(2)}, u32[]{:S(2)}) collective-permute-start(bf16[128,2176]{1,0:T(8,128)(2,1)S(1)} %pad_maximum_fusion), channel_id=1, source_target_pairs={{0,4},{1,3},{4,8},{5,1},{8,12},{9,5},{12,14},{13,9},{14,10},{15,13... | collective-permute-start | bytes 1671176 | tf_op jit(solution)/shard_map/ppermute | solution.py:243
  21.4 0.0 collective-permute-done.6.refs_1_
  21.4 0.1 collective-permute-done.8.refs_1_
  21.5 2.6 %expert.5 = (bf16[64,2048]{1,0:T(8,128)(2,1)S(1)}, bf16[64,2048]{1,0:T(8,128)(2,1)S(1)}, bf16[64,2048]{1,0:T(8,128)(2,1)S(1)}, bf16[64,2048]{1,0:T(8,128)(2,1)S(1)}) custom-call(s32[1]{0:T(128)} %bitcast.own_ref, bf16[64,2176]{1,0:T(8,128)(2,1)S(1)} %collective-permute-done.4.refs_0_, bf16[64,2176]{1,0:T(8,128)(2,1)S(1)} %collective-permute-done.8.refs_1_, ...), custom_call_target="tpu_custom_call" | custom-call | flops 524288 | bytes 524288 | tf_op jit(solution)/shard_map/expert/pallas_call | solution.py:116
  24.2 2.7 %expert.6 = (bf16[64,2048]{1,0:T(8,128)(2,1)S(1)}, bf16[64,2048]{1,0:T(8,128)(2,1)S(1)}, bf16[64,2048]{1,0:T(8,128)(2,1)S(1)}, bf16[64,2048]{1,0:T(8,128)(2,1)S(1)}) custom-call(s32[1]{0:T(128)} %bitcast.own_ref, bf16[64,2176]{1,0:T(8,128)(2,1)S(1)} %collective-permute-done.2.refs_0_, bf16[64,2176]{1,0:T(8,128)(2,1)S(1)} %collective-permute-done.6.refs_1_, ...), custom_call_target="tpu_custom_call" | custom-call | flops 524288 | bytes 524288 | tf_op jit(solution)/shard_map/expert/pallas_call | solution.py:116
  26.9 0.0 collective-permute-done.11.refs_1_
  26.9 0.2 collective-permute-start.12
  27.1 1.4 %collective-permute-done.12.refs_0_ = bf16[64,2176]{1,0:T(8,128)(2,1)S(1)} collective-permute-done((bf16[64,2176]{1,0:T(8,128)(2,1)S(1)}, bf16[64,2176]{1,0:T(8,128)(2,1)S(1)}, u32[]{:S(2)}, u32[]{:S(2)}) %collective-permute-start.12) | collective-permute-done | bytes 278560 | tf_op jit(solution)/shard_map/ppermute | solution.py:249
  28.5 2.0 %expert.7 = (bf16[64,2048]{1,0:T(8,128)(2,1)S(1)}, bf16[64,2048]{1,0:T(8,128)(2,1)S(1)}) custom-call(s32[1]{0:T(128)} %bitcast.own_ref, bf16[64,2176]{1,0:T(8,128)(2,1)S(1)} %collective-permute-done.12.refs_0_, bf16[64,2176]{1,0:T(8,128)(2,1)S(1)} %collective-permute-done.11.refs_1_, bf16[1,2048,768]{2,1,0:T(8,128)(2,1)S(1)} %get-tuple-element.41.refs_4_.refs_2_, ...), custom_call_target="tpu_custom_call" | custom-call | flops 262144 | bytes 262144 | tf_op jit(solution)/shard_map/expert/pallas_call | solution.py:116
  30.5 0.2 collective-permute-start.13
  30.8 0.3 collective-permute-done.9.refs_1_
  31.1 0.2 collective-permute-start.10
  31.3 0.3 collective-permute-start.14
  31.6 0.2 collective-permute-start.15
  31.8 0.4 collective-permute-done.13
  32.1 0.1 add_convert_fusion.7
  32.2 2.2 %collective-permute-start.17 = (bf16[64,2048]{1,0:T(8,128)(2,1)S(1)}, bf16[64,2048]{1,0:T(8,128)(2,1)S(1)}, u32[]{:S(2)}, u32[]{:S(2)}) collective-permute-start(bf16[64,2048]{1,0:T(8,128)(2,1)S(1)} %add_convert_fusion.7), channel_id=1, source_target_pairs={{0,4},{1,3},{4,8},{5,1},{8,12},{9,5},{12,14},{13,9},{14,10},{15,13... | collective-permute-start | bytes 786440 | tf_op jit(solution)/shard_map/ppermute | solution.py:252
  34.5 0.0 collective-permute-done.14
  34.5 0.0 collective-permute-done.15
  34.5 0.0 collective-permute-done.10.refs_0_
  34.5 2.7 %expert.8 = (bf16[64,2048]{1,0:T(8,128)(2,1)S(1)}, bf16[64,2048]{1,0:T(8,128)(2,1)S(1)}, bf16[64,2048]{1,0:T(8,128)(2,1)S(1)}, bf16[64,2048]{1,0:T(8,128)(2,1)S(1)}) custom-call(s32[1]{0:T(128)} %bitcast.own_ref, bf16[128,2176]{1,0:T(8,128)(2,1)S(1)} %collective-permute-done.10.refs_0_, bf16[128,2176]{1,0:T(8,128)(2,1)S(1)} %collective-permute-done.9.refs_1_, ...), custom_call_target="tpu_custom_call" | custom-call | flops 524288 | bytes 524288 | tf_op jit(solution)/shard_map/expert/pallas_call | solution.py:116
  37.1 0.1 collective-permute-start.16
  37.2 0.5 collective-permute-start.18
  37.7 0.9 %collective-permute-done.17 = bf16[64,2048]{1,0:T(8,128)(2,1)S(1)} collective-permute-done((bf16[64,2048]{1,0:T(8,128)(2,1)S(1)}, bf16[64,2048]{1,0:T(8,128)(2,1)S(1)}, u32[]{:S(2)}, u32[]{:S(2)}) %collective-permute-start.17) | collective-permute-done | bytes 262176 | tf_op jit(solution)/shard_map/ppermute | solution.py:252
  38.7 0.1 collective-permute-done.16
  38.7 0.1 add_convert_fusion.6
  38.8 2.5 %collective-permute-start.20 = (bf16[64,2048]{1,0:T(8,128)(2,1)S(1)}, bf16[64,2048]{1,0:T(8,128)(2,1)S(1)}, u32[]{:S(2)}, u32[]{:S(2)}) collective-permute-start(bf16[64,2048]{1,0:T(8,128)(2,1)S(1)} %add_convert_fusion.6), channel_id=1, source_target_pairs={{0,4},{1,3},{4,8},{5,1},{8,12},{9,5},{12,14},{13,9},{14,10},{15,13... | collective-permute-start | bytes 786440 | tf_op jit(solution)/shard_map/ppermute | solution.py:262
  41.4 0.0 collective-permute-done.18
  41.4 0.1 add_convert_fusion.5
  41.4 2.2 %collective-permute-start.25 = (bf16[64,2048]{1,0:T(8,128)(2,1)S(1)}, bf16[64,2048]{1,0:T(8,128)(2,1)S(1)}, u32[]{:S(2)}, u32[]{:S(2)}) collective-permute-start(bf16[64,2048]{1,0:T(8,128)(2,1)S(1)} %add_convert_fusion.5), channel_id=1, source_target_pairs={{0,4},{1,3},{4,8},{5,1},{8,12},{9,5},{12,14},{13,9},{14,10},{15,13... | collective-permute-start | bytes 786440 | tf_op jit(solution)/shard_map/ppermute | solution.py:262
  43.6 2.0 %expert.9 = (bf16[64,2048]{1,0:T(8,128)(2,1)S(1)}, bf16[64,2048]{1,0:T(8,128)(2,1)S(1)}) custom-call(s32[1]{0:T(128)} %bitcast.own_ref, bf16[64,2176]{1,0:T(8,128)(2,1)S(1)} %copy-done, bf16[64,2176]{1,0:T(8,128)(2,1)S(1)} %collective-permute-done.1.refs_1_, bf16[1,2048,768]{2,1,0:T(8,128)(2,1)S(1)} %get-tuple-element.41.refs_4_.refs_2_, ...), custom_call_target="tpu_custom_call" | custom-call | flops 262144 | bytes 262144 | tf_op jit(solution)/shard_map/expert/pallas_call | solution.py:116
  45.7 0.6 collective-permute-start.23
  46.2 0.1 collective-permute-start.24
  46.3 0.1 add_convert_fusion.4
  46.4 1.5 %collective-permute-start.21 = (bf16[64,2048]{1,0:T(8,128)(2,1)S(1)}, bf16[64,2048]{1,0:T(8,128)(2,1)S(1)}, u32[]{:S(2)}, u32[]{:S(2)}) collective-permute-start(bf16[64,2048]{1,0:T(8,128)(2,1)S(1)} %add_convert_fusion.4), channel_id=1, source_target_pairs={{0,4},{1,3},{4,8},{5,1},{8,12},{9,5},{12,14},{13,9},{14,10},{15,13... | collective-permute-start | bytes 786440 | tf_op jit(solution)/shard_map/ppermute | solution.py:262
  47.9 0.1 collective-permute-done.25
  48.1 0.1 add_convert_fusion.2
  48.2 2.5 %collective-permute-start.26 = (bf16[64,2048]{1,0:T(8,128)(2,1)S(1)}, bf16[64,2048]{1,0:T(8,128)(2,1)S(1)}, u32[]{:S(2)}, u32[]{:S(2)}) collective-permute-start(bf16[64,2048]{1,0:T(8,128)(2,1)S(1)} %add_convert_fusion.2), channel_id=1, source_target_pairs={{0,4},{1,3},{4,8},{5,1},{8,12},{9,5},{12,14},{13,9},{14,10},{15,13... | collective-permute-start | bytes 786440 | tf_op jit(solution)/shard_map/ppermute | solution.py:262
  50.7 2.1 %collective-permute-done.21 = bf16[64,2048]{1,0:T(8,128)(2,1)S(1)} collective-permute-done((bf16[64,2048]{1,0:T(8,128)(2,1)S(1)}, bf16[64,2048]{1,0:T(8,128)(2,1)S(1)}, u32[]{:S(2)}, u32[]{:S(2)}) %collective-permute-start.21) | collective-permute-done | bytes 262176 | tf_op jit(solution)/shard_map/ppermute | solution.py:262
  52.8 0.1 add_convert_fusion.3
  52.9 0.7 %collective-permute-start.22 = (bf16[64,2048]{1,0:T(8,128)(2,1)S(1)}, bf16[64,2048]{1,0:T(8,128)(2,1)S(1)}, u32[]{:S(2)}, u32[]{:S(2)}) collective-permute-start(bf16[64,2048]{1,0:T(8,128)(2,1)S(1)} %add_convert_fusion.3), channel_id=1, source_target_pairs={{0,5},{1,2},{4,9},{5,0},{8,13},{9,4},{12,15},{13,8},{14,11},{15,12... | collective-permute-start | bytes 786440 | tf_op jit(solution)/shard_map/ppermute | solution.py:262
  53.6 2.0 %collective-permute-done.26 = bf16[64,2048]{1,0:T(8,128)(2,1)S(1)} collective-permute-done((bf16[64,2048]{1,0:T(8,128)(2,1)S(1)}, bf16[64,2048]{1,0:T(8,128)(2,1)S(1)}, u32[]{:S(2)}, u32[]{:S(2)}) %collective-permute-start.26) | collective-permute-done | bytes 262176 | tf_op jit(solution)/shard_map/ppermute | solution.py:262
  55.6 0.1 add_convert_fusion.1
  55.7 1.5 %collective-permute-start.27 = (bf16[64,2048]{1,0:T(8,128)(2,1)S(1)}, bf16[64,2048]{1,0:T(8,128)(2,1)S(1)}, u32[]{:S(2)}, u32[]{:S(2)}) collective-permute-start(bf16[64,2048]{1,0:T(8,128)(2,1)S(1)} %add_convert_fusion.1), channel_id=1, source_target_pairs={{0,4},{1,3},{4,8},{5,1},{8,12},{9,5},{12,14},{13,9},{14,10},{15,13... | collective-permute-start | bytes 786440 | tf_op jit(solution)/shard_map/ppermute | solution.py:262
  57.3 1.5 %collective-permute-done.22 = bf16[64,2048]{1,0:T(8,128)(2,1)S(1)} collective-permute-done((bf16[64,2048]{1,0:T(8,128)(2,1)S(1)}, bf16[64,2048]{1,0:T(8,128)(2,1)S(1)}, u32[]{:S(2)}, u32[]{:S(2)}) %collective-permute-start.22) | collective-permute-done | bytes 262176 | tf_op jit(solution)/shard_map/ppermute | solution.py:262
  58.8 0.1 convert_add_fusion
  58.9 3.3 %collective-permute-done.27 = bf16[64,2048]{1,0:T(8,128)(2,1)S(1)} collective-permute-done((bf16[64,2048]{1,0:T(8,128)(2,1)S(1)}, bf16[64,2048]{1,0:T(8,128)(2,1)S(1)}, u32[]{:S(2)}, u32[]{:S(2)}) %collective-permute-start.27) | collective-permute-done | bytes 262176 | tf_op jit(solution)/shard_map/ppermute | solution.py:262
  62.2 0.8 %add_convert_fusion = bf16[64,2048]{1,0:T(8,128)(2,1)} fusion(f32[64,2048]{1,0:T(8,128)S(1)} %convert_add_fusion, bf16[64,2048]{1,0:T(8,128)(2,1)S(1)} %collective-permute-done.27), kind=kLoop, calls=%fused_computation.1 | loop fusion | flops 393216 | bytes 1048576 | tf_op jit(solution)/shard_map/convert_element_type | solution.py:210
  (12 shorter events, 0.1 us)
Async XLA Ops:
  1.7 3.2 %collective-permute-start.1 = (bf16[64,2176]{1,0:T(8,128)(2,1)}, bf16[64,2176]{1,0:T(8,128)(2,1)S(1)}, u32[]{:S(2)}, u32[]{:S(2)}) collective-permute-start(bf16[64,2176]{1,0:T(8,128)(2,1)} %pack.1.refs_0_), channel_id=1, source_target_pairs={{0,1},{1,0},{2,3},{3,2},{4,5},{5,4},{6,7},{7,6},{8,9},{9,8},{10,11... | collective-permute-start | bytes 835592 | tf_op jit(solution)/shard_map/ppermute | solution.py:228
  2.2 7.3 %collective-permute-start = (bf16[64,2176]{1,0:T(8,128)(2,1)}, bf16[64,2176]{1,0:T(8,128)(2,1)S(1)}, u32[]{:S(2)}, u32[]{:S(2)}) collective-permute-start(bf16[64,2176]{1,0:T(8,128)(2,1)} %pack.1.refs_0_), channel_id=1, source_target_pairs={{0,4},{1,3},{4,8},{5,1},{8,12},{9,5},{12,14},{13,9},{14,10},{15,13... | collective-permute-start | bytes 835592 | tf_op jit(solution)/shard_map/ppermute | solution.py:229
  4.9 7.6 %collective-permute-start.5 = (bf16[64,2176]{1,0:T(8,128)(2,1)S(1)}, bf16[64,2176]{1,0:T(8,128)(2,1)S(1)}, u32[]{:S(2)}, u32[]{:S(2)}) collective-permute-start(bf16[64,2176]{1,0:T(8,128)(2,1)S(1)} %collective-permute-done.1.refs_1_), channel_id=1, source_target_pairs={{0,4},{1,3},{4,8},{5,1},{8,12},{9,5},{12,14},{13,9},{14,10},{15,13... | collective-permute-start | bytes 835592 | tf_op jit(solution)/shard_map/ppermute | solution.py:229
  9.5 7.0 %collective-permute-start.3 = (bf16[64,2176]{1,0:T(8,128)(2,1)S(1)}, bf16[64,2176]{1,0:T(8,128)(2,1)S(1)}, u32[]{:S(2)}, u32[]{:S(2)}) collective-permute-start(bf16[64,2176]{1,0:T(8,128)(2,1)S(1)} %collective-permute-done.refs_2_), channel_id=1, source_target_pairs={{0,4},{1,3},{4,8},{5,1},{8,12},{9,5},{12,14},{13,9},{14,10},{15,13... | collective-permute-start | bytes 835592 | tf_op jit(solution)/shard_map/ppermute | solution.py:238
  12.5 7.2 %collective-permute-start.7 = (bf16[64,2176]{1,0:T(8,128)(2,1)S(1)}, bf16[64,2176]{1,0:T(8,128)(2,1)S(1)}, u32[]{:S(2)}, u32[]{:S(2)}) collective-permute-start(bf16[64,2176]{1,0:T(8,128)(2,1)S(1)} %collective-permute-done.5.refs_3_), channel_id=1, source_target_pairs={{0,4},{1,3},{4,8},{5,1},{8,12},{9,5},{12,14},{13,9},{14,10},{15,13... | collective-permute-start | bytes 835592 | tf_op jit(solution)/shard_map/ppermute | solution.py:238
  14.6 5.1 %collective-permute-start.2 = (bf16[64,2176]{1,0:T(8,128)(2,1)S(1)}, bf16[64,2176]{1,0:T(8,128)(2,1)S(1)}, u32[]{:S(2)}, u32[]{:S(2)}) collective-permute-start(bf16[64,2176]{1,0:T(8,128)(2,1)S(1)} %collective-permute-done.refs_2_), channel_id=1, source_target_pairs={{0,1},{1,0},{2,3},{3,2},{4,5},{5,4},{6,7},{7,6},{8,9},{9,8},{10,11... | collective-permute-start | bytes 835592 | tf_op jit(solution)/shard_map/ppermute | solution.py:241
  16.5 10.4 %collective-permute-start.11 = (bf16[64,2176]{1,0:T(8,128)(2,1)S(1)}, bf16[64,2176]{1,0:T(8,128)(2,1)S(1)}, u32[]{:S(2)}, u32[]{:S(2)}) collective-permute-start(bf16[64,2176]{1,0:T(8,128)(2,1)S(1)} %collective-permute-done.3.refs_2_), channel_id=1, source_target_pairs={{0,8},{1,7},{4,12},{5,3},{8,14},{9,1},{12,10},{13,5},{14,6},{15,9}... | collective-permute-start | bytes 835592 | tf_op jit(solution)/shard_map/ppermute | solution.py:242
  19.2 2.2 %collective-permute-start.4 = (bf16[64,2176]{1,0:T(8,128)(2,1)S(1)}, bf16[64,2176]{1,0:T(8,128)(2,1)S(1)}, u32[]{:S(2)}, u32[]{:S(2)}) collective-permute-start(bf16[64,2176]{1,0:T(8,128)(2,1)S(1)} %collective-permute-done.3.refs_2_), channel_id=1, source_target_pairs={{0,1},{1,0},{2,3},{3,2},{4,5},{5,4},{6,7},{7,6},{8,9},{9,8},{10,11... | collective-permute-start | bytes 835592 | tf_op jit(solution)/shard_map/ppermute | solution.py:241
  19.2 2.2 %collective-permute-start.6 = (bf16[64,2176]{1,0:T(8,128)(2,1)S(1)}, bf16[64,2176]{1,0:T(8,128)(2,1)S(1)}, u32[]{:S(2)}, u32[]{:S(2)}) collective-permute-start(bf16[64,2176]{1,0:T(8,128)(2,1)S(1)} %collective-permute-done.5.refs_3_), channel_id=1, source_target_pairs={{0,1},{1,0},{2,3},{3,2},{4,5},{5,4},{6,7},{7,6},{8,9},{9,8},{10,11... | collective-permute-start | bytes 835592 | tf_op jit(solution)/shard_map/ppermute | solution.py:241
  19.7 1.8 %collective-permute-start.8 = (bf16[64,2176]{1,0:T(8,128)(2,1)S(1)}, bf16[64,2176]{1,0:T(8,128)(2,1)S(1)}, u32[]{:S(2)}, u32[]{:S(2)}) collective-permute-start(bf16[64,2176]{1,0:T(8,128)(2,1)S(1)} %collective-permute-done.7.refs_3_), channel_id=1, source_target_pairs={{0,1},{1,0},{2,3},{3,2},{4,5},{5,4},{6,7},{7,6},{8,9},{9,8},{10,11... | collective-permute-start | bytes 835592 | tf_op jit(solution)/shard_map/ppermute | solution.py:241
  19.8 11.3 %collective-permute-start.9 = (bf16[128,2176]{1,0:T(8,128)(2,1)S(1)}, bf16[128,2176]{1,0:T(8,128)(2,1)S(1)}, u32[]{:S(2)}, u32[]{:S(2)}) collective-permute-start(bf16[128,2176]{1,0:T(8,128)(2,1)S(1)} %pad_maximum_fusion), channel_id=1, source_target_pairs={{0,4},{1,3},{4,8},{5,1},{8,12},{9,5},{12,14},{13,9},{14,10},{15,13... | collective-permute-start | bytes 1671176 | tf_op jit(solution)/shard_map/ppermute | solution.py:243
  26.9 1.6 %collective-permute-start.12 = (bf16[64,2176]{1,0:T(8,128)(2,1)S(1)}, bf16[64,2176]{1,0:T(8,128)(2,1)S(1)}, u32[]{:S(2)}, u32[]{:S(2)}) collective-permute-start(bf16[64,2176]{1,0:T(8,128)(2,1)S(1)} %collective-permute-done.11.refs_1_), channel_id=1, source_target_pairs={{0,1},{1,0},{2,3},{3,2},{4,5},{5,4},{6,7},{7,6},{8,9},{9,8},{10,11... | collective-permute-start | bytes 835592 | tf_op jit(solution)/shard_map/ppermute | solution.py:249
  30.5 1.6 %collective-permute-start.13 = (bf16[64,2048]{1,0:T(8,128)(2,1)S(1)}, bf16[64,2048]{1,0:T(8,128)(2,1)S(1)}, u32[]{:S(2)}, u32[]{:S(2)}) collective-permute-start(bf16[64,2048]{1,0:T(8,128)(2,1)S(1)} %get-tuple-element.53), channel_id=1, source_target_pairs={{0,1},{1,0},{2,3},{3,2},{4,5},{5,4},{6,7},{7,6},{8,9},{9,8},{10,11... | collective-permute-start | bytes 786440 | tf_op jit(solution)/shard_map/ppermute | solution.py:250
  31.1 3.4 %collective-permute-start.10 = (bf16[128,2176]{1,0:T(8,128)(2,1)S(1)}, bf16[128,2176]{1,0:T(8,128)(2,1)S(1)}, u32[]{:S(2)}, u32[]{:S(2)}) collective-permute-start(bf16[128,2176]{1,0:T(8,128)(2,1)S(1)} %collective-permute-done.9.refs_1_), channel_id=1, source_target_pairs={{0,1},{1,0},{2,3},{3,2},{4,5},{5,4},{6,7},{7,6},{8,9},{9,8},{10,11... | collective-permute-start | bytes 1671176 | tf_op jit(solution)/shard_map/ppermute | solution.py:251
  31.3 3.2 %collective-permute-start.14 = (bf16[64,2048]{1,0:T(8,128)(2,1)S(1)}, bf16[64,2048]{1,0:T(8,128)(2,1)S(1)}, u32[]{:S(2)}, u32[]{:S(2)}) collective-permute-start(bf16[64,2048]{1,0:T(8,128)(2,1)S(1)} %get-tuple-element.54), channel_id=1, source_target_pairs={{0,1},{1,0},{2,3},{3,2},{4,5},{5,4},{6,7},{7,6},{8,9},{9,8},{10,11... | collective-permute-start | bytes 786440 | tf_op jit(solution)/shard_map/ppermute | solution.py:244
  31.6 2.9 %collective-permute-start.15 = (bf16[64,2048]{1,0:T(8,128)(2,1)S(1)}, bf16[64,2048]{1,0:T(8,128)(2,1)S(1)}, u32[]{:S(2)}, u32[]{:S(2)}) collective-permute-start(bf16[64,2048]{1,0:T(8,128)(2,1)S(1)} %get-tuple-element.55), channel_id=1, source_target_pairs={{0,1},{1,0},{2,3},{3,2},{4,5},{5,4},{6,7},{7,6},{8,9},{9,8},{10,11... | collective-permute-start | bytes 786440 | tf_op jit(solution)/shard_map/ppermute | solution.py:244
  32.2 11.4 %copy-start = (bf16[64,2176]{1,0:T(8,128)(2,1)S(1)}, bf16[64,2176]{1,0:T(8,128)(2,1)}, u32[]{:S(2)}) copy-start(bf16[64,2176]{1,0:T(8,128)(2,1)} %pack.1.refs_0_) | copy-start | bytes 835588
  32.2 6.4 %collective-permute-start.17 = (bf16[64,2048]{1,0:T(8,128)(2,1)S(1)}, bf16[64,2048]{1,0:T(8,128)(2,1)S(1)}, u32[]{:S(2)}, u32[]{:S(2)}) collective-permute-start(bf16[64,2048]{1,0:T(8,128)(2,1)S(1)} %add_convert_fusion.7), channel_id=1, source_target_pairs={{0,4},{1,3},{4,8},{5,1},{8,12},{9,5},{12,14},{13,9},{14,10},{15,13... | collective-permute-start | bytes 786440 | tf_op jit(solution)/shard_map/ppermute | solution.py:252
  37.1 1.6 %collective-permute-start.16 = (bf16[64,2048]{1,0:T(8,128)(2,1)S(1)}, bf16[64,2048]{1,0:T(8,128)(2,1)S(1)}, u32[]{:S(2)}, u32[]{:S(2)}) collective-permute-start(bf16[64,2048]{1,0:T(8,128)(2,1)S(1)} %get-tuple-element.59), channel_id=1, source_target_pairs={{0,1},{1,0},{2,3},{3,2},{4,5},{5,4},{6,7},{7,6},{8,9},{9,8},{10,11... | collective-permute-start | bytes 786440 | tf_op jit(solution)/shard_map/ppermute | solution.py:244
  37.2 4.2 %collective-permute-start.18 = (bf16[64,2048]{1,0:T(8,128)(2,1)S(1)}, bf16[64,2048]{1,0:T(8,128)(2,1)S(1)}, u32[]{:S(2)}, u32[]{:S(2)}) collective-permute-start(bf16[64,2048]{1,0:T(8,128)(2,1)S(1)} %get-tuple-element.61), channel_id=1, source_target_pairs={{0,1},{1,0},{2,3},{3,2},{4,5},{5,4},{6,7},{7,6},{8,9},{9,8},{10,11... | collective-permute-start | bytes 786440 | tf_op jit(solution)/shard_map/ppermute | solution.py:244
  38.8 7.5 %collective-permute-start.20 = (bf16[64,2048]{1,0:T(8,128)(2,1)S(1)}, bf16[64,2048]{1,0:T(8,128)(2,1)S(1)}, u32[]{:S(2)}, u32[]{:S(2)}) collective-permute-start(bf16[64,2048]{1,0:T(8,128)(2,1)S(1)} %add_convert_fusion.6), channel_id=1, source_target_pairs={{0,4},{1,3},{4,8},{5,1},{8,12},{9,5},{12,14},{13,9},{14,10},{15,13... | collective-permute-start | bytes 786440 | tf_op jit(solution)/shard_map/ppermute | solution.py:262
  41.4 6.6 %collective-permute-start.25 = (bf16[64,2048]{1,0:T(8,128)(2,1)S(1)}, bf16[64,2048]{1,0:T(8,128)(2,1)S(1)}, u32[]{:S(2)}, u32[]{:S(2)}) collective-permute-start(bf16[64,2048]{1,0:T(8,128)(2,1)S(1)} %add_convert_fusion.5), channel_id=1, source_target_pairs={{0,4},{1,3},{4,8},{5,1},{8,12},{9,5},{12,14},{13,9},{14,10},{15,13... | collective-permute-start | bytes 786440 | tf_op jit(solution)/shard_map/ppermute | solution.py:262
  43.6 7.1 %collective-permute-start.19 = (bf16[64,2048]{1,0:T(8,128)(2,1)S(1)}, bf16[64,2048]{1,0:T(8,128)(2,1)S(1)}, u32[]{:S(2)}, u32[]{:S(2)}) collective-permute-start(bf16[64,2048]{1,0:T(8,128)(2,1)S(1)} %get-tuple-element.62), channel_id=1, source_target_pairs={{0,1},{1,0},{2,3},{3,2},{4,5},{5,4},{6,7},{7,6},{8,9},{9,8},{10,11... | collective-permute-start | bytes 786440 | tf_op jit(solution)/shard_map/ppermute | solution.py:244
  45.7 11.6 %collective-permute-start.23 = (bf16[64,2048]{1,0:T(8,128)(2,1)S(1)}, bf16[64,2048]{1,0:T(8,128)(2,1)S(1)}, u32[]{:S(2)}, u32[]{:S(2)}) collective-permute-start(bf16[64,2048]{1,0:T(8,128)(2,1)S(1)} %get-tuple-element.66), channel_id=1, source_target_pairs={{0,1},{1,0},{2,3},{3,2},{4,5},{5,4},{6,7},{7,6},{8,9},{9,8},{10,11... | collective-permute-start | bytes 786440 | tf_op jit(solution)/shard_map/ppermute | solution.py:263
  46.2 7.4 %collective-permute-start.24 = (bf16[64,2048]{1,0:T(8,128)(2,1)S(1)}, bf16[64,2048]{1,0:T(8,128)(2,1)S(1)}, u32[]{:S(2)}, u32[]{:S(2)}) collective-permute-start(bf16[64,2048]{1,0:T(8,128)(2,1)S(1)} %get-tuple-element.70), channel_id=1, source_target_pairs={{0,1},{1,0},{2,3},{3,2},{4,5},{5,4},{6,7},{7,6},{8,9},{9,8},{10,11... | collective-permute-start | bytes 786440 | tf_op jit(solution)/shard_map/ppermute | solution.py:244
  46.4 6.4 %collective-permute-start.21 = (bf16[64,2048]{1,0:T(8,128)(2,1)S(1)}, bf16[64,2048]{1,0:T(8,128)(2,1)S(1)}, u32[]{:S(2)}, u32[]{:S(2)}) collective-permute-start(bf16[64,2048]{1,0:T(8,128)(2,1)S(1)} %add_convert_fusion.4), channel_id=1, source_target_pairs={{0,4},{1,3},{4,8},{5,1},{8,12},{9,5},{12,14},{13,9},{14,10},{15,13... | collective-permute-start | bytes 786440 | tf_op jit(solution)/shard_map/ppermute | solution.py:262
  48.2 7.5 %collective-permute-start.26 = (bf16[64,2048]{1,0:T(8,128)(2,1)S(1)}, bf16[64,2048]{1,0:T(8,128)(2,1)S(1)}, u32[]{:S(2)}, u32[]{:S(2)}) collective-permute-start(bf16[64,2048]{1,0:T(8,128)(2,1)S(1)} %add_convert_fusion.2), channel_id=1, source_target_pairs={{0,4},{1,3},{4,8},{5,1},{8,12},{9,5},{12,14},{13,9},{14,10},{15,13... | collective-permute-start | bytes 786440 | tf_op jit(solution)/shard_map/ppermute | solution.py:262
  52.9 5.9 %collective-permute-start.22 = (bf16[64,2048]{1,0:T(8,128)(2,1)S(1)}, bf16[64,2048]{1,0:T(8,128)(2,1)S(1)}, u32[]{:S(2)}, u32[]{:S(2)}) collective-permute-start(bf16[64,2048]{1,0:T(8,128)(2,1)S(1)} %add_convert_fusion.3), channel_id=1, source_target_pairs={{0,5},{1,2},{4,9},{5,0},{8,13},{9,4},{12,15},{13,8},{14,11},{15,12... | collective-permute-start | bytes 786440 | tf_op jit(solution)/shard_map/ppermute | solution.py:262
  55.7 6.4 %collective-permute-start.27 = (bf16[64,2048]{1,0:T(8,128)(2,1)S(1)}, bf16[64,2048]{1,0:T(8,128)(2,1)S(1)}, u32[]{:S(2)}, u32[]{:S(2)}) collective-permute-start(bf16[64,2048]{1,0:T(8,128)(2,1)S(1)} %add_convert_fusion.1), channel_id=1, source_target_pairs={{0,4},{1,3},{4,8},{5,1},{8,12},{9,5},{12,14},{13,9},{14,10},{15,13... | collective-permute-start | bytes 786440 | tf_op jit(solution)/shard_map/ppermute | solution.py:262
